TPU v7x, 32 devices: a whole 2x2x4 slice. The times are simulated.
32 devices in a mesh: groups: 2 (over y), leaf: 4 (over z), tensor: 2 (over x), sub: 2 (over core).
Axes of the slice: x: 2, y: 2, z: 4, core: 2. Of those that a mesh axis runs over, the one named last changes fastest.
Arguments:
- queries: bfloat16 [6144, 8192], P(('groups', 'leaf', 'sub'), 'tensor'), parts along dimension 0, may hold values from -6 to 6
- grad_out: bfloat16 [6144, 8192], P(('groups', 'leaf', 'sub'), 'tensor'), parts along dimension 0, may hold values from -12 to 12
- keys: bfloat16 [6144, 1024], P(('groups', 'leaf', 'sub'), 'tensor'), parts along dimension 0, may hold values from -6 to 6
- values: bfloat16 [6144, 1024], P(('groups', 'leaf', 'sub'), 'tensor'), parts along dimension 0, may hold values from -6 to 6
- log_norms: float32 [64, 6144], P('tensor', ('groups', 'leaf', 'sub')), parts along dimension 1, may hold values from 4 to 6
- row_deltas: float32 [64, 6144], P('tensor', ('groups', 'leaf', 'sub')), parts along dimension 1, may hold values from -12 to 12
- ancestors: int32 [16, 5], P(('groups', 'leaf', 'sub')), parts along dimension 0, may hold values from 0 to 23, as said below
- counts: int32 [16, 3], P(('groups', 'leaf', 'sub')), parts along dimension 0, may hold values from 16 to 128
- w_value: bfloat16 [5120, 1024], P('tensor'), may hold values from -0.078125 to 0.078125
Outputs:
- grad_queries: bfloat16 [6144, 8192], P(('groups', 'leaf', 'sub'), 'tensor'), parts along dimension 0
- grad_keys: bfloat16 [6144, 1024], P(('groups', 'leaf', 'sub'), 'tensor'), parts along dimension 0
- grad_values: bfloat16 [6144, 1024], P(('groups', 'leaf', 'sub'), 'tensor'), parts along dimension 0
- grad_input: bfloat16 [6144, 5120], P(('groups', 'leaf', 'sub'), 'tensor'), parts along dimension 0
There are 2 independent parts, one for each index of `groups`. A program takes and returns all parts, laid end to end along the dimension named above; an argument that names none is the same for every part. Nothing has to cross between parts.
Inputs may be any that keep to these rules, and one draw needn't show every extreme that they name: ancestors[d, j] is the page id (leaf times 3 plus slot) of leaf d's level-j page. For j < 3 the leaves whose level-j pages are the same page form exactly an aligned block of 8 >> j consecutive leaves, and that page is slot 0 of one leaf of the block; no slot 0 serves two blocks or levels. ancestors[d, 3] = d * 3 + 1 and ancestors[d, 4] = d * 3 + 2.
All inputs are finite; a program needn't handle non-finite values.
Results may differ from a plain program's by a relative error of at most 0.0061.
Values may be sent and summed in bfloat16 or wider, within the bound.
No kernel may reach another device: no remote copies, remote signals or barrier semaphores. Data moves between devices by JAX's collectives and lax.ppermute only.
A program may use at most 128 MiB of HBM per device.

v0:
```python
import math

import jax
import jax.numpy as jnp
from jax import lax
from jax.sharding import PartitionSpec as P

HD = 128
PAGE = 128
SLOTS = 3
INNER = 3
LEVELS = 5


def swapped(block, axis, distance):
    count = lax.axis_size(axis)
    route = []
    for low in range(count):
        high = low | 1 << distance
        if high != low and high < count:
            route += [(low, high), (high, low)]
    return lax.ppermute(block, axis, route)


def attend(query_rows, grad_rows, norm_rows, delta_rows, key_rows, value_rows, allowed):
    score_scale = 1.0 / math.sqrt(HD)
    scores = (
        jnp.einsum("rkgd,nkd->kgrn", query_rows, key_rows, preferred_element_type=jnp.float32)
        * score_scale
    )
    weights = jnp.where(allowed[None, None], jnp.exp(scores - norm_rows[..., None]), 0.0)
    grad_weights = jnp.einsum(
        "rkgd,nkd->kgrn", grad_rows, value_rows, preferred_element_type=jnp.float32
    )
    grad_scores = (weights * (grad_weights - delta_rows[..., None])).astype(jnp.bfloat16)
    weights_low = weights.astype(jnp.bfloat16)
    grad_value_part = jnp.einsum(
        "kgrn,rkgd->nkd", weights_low, grad_rows, preferred_element_type=jnp.float32
    )
    grad_key_part = (
        jnp.einsum("kgrn,rkgd->nkd", grad_scores, query_rows, preferred_element_type=jnp.float32)
        * score_scale
    )
    grad_query_part = (
        jnp.einsum("kgrn,nkd->rkgd", grad_scores, key_rows, preferred_element_type=jnp.float32)
        * score_scale
    )
    return (grad_query_part, grad_key_part, grad_value_part)


def spanning(leaves, bit_index):
    return len(
        [depth_index for depth_index in range(INNER) if 2 << bit_index <= leaves >> depth_index]
    )


def on_device(queries, grad_out, keys, values, log_norms, row_deltas, ancestors, counts, w_value):
    kv_local = keys.shape[1] // HD
    group_size = queries.shape[1] // keys.shape[1]
    width_local = kv_local * HD
    leaves = lax.axis_size(("leaf", "sub"))
    position = lax.axis_index(("leaf", "sub"))
    own_page = position * SLOTS
    path_ids = ancestors[0]
    page_counts = counts[0]
    level_ids = jnp.arange(INNER, dtype=jnp.int32)
    owned_levels = path_ids[:INNER] == own_page
    inner_level = jnp.sum(jnp.where(owned_levels, level_ids, 0))
    has_inner = jnp.any(owned_levels)
    key_pages = keys.reshape(SLOTS, PAGE, width_local)
    value_pages = values.reshape(SLOTS, PAGE, width_local)
    every_key, every_value, every_count = (
        lax.all_gather(key_pages[:1], ("leaf", "sub"), axis=0, tiled=True),
        lax.all_gather(value_pages[:1], ("leaf", "sub"), axis=0, tiled=True),
        lax.all_gather(page_counts[:1], ("leaf", "sub"), axis=0, tiled=True),
    )
    owners = path_ids[:INNER] // SLOTS
    inner_keys = every_key[owners]
    inner_values = every_value[owners]
    inner_counts = every_count[owners]
    path_keys = jnp.concatenate([inner_keys, key_pages[1:]]).reshape(LEVELS * PAGE, kv_local, HD)
    path_values = jnp.concatenate([inner_values, value_pages[1:]]).reshape(
        LEVELS * PAGE, kv_local, HD
    )
    path_counts = jnp.concatenate([inner_counts, page_counts[1:]])
    positions = jnp.arange(PAGE, dtype=jnp.int32)
    key_level = jnp.repeat(jnp.arange(LEVELS, dtype=jnp.int32), PAGE)
    key_pos = jnp.tile(positions, LEVELS)
    key_ok = key_pos < jnp.repeat(path_counts, PAGE)
    inner_rows = INNER * PAGE
    row_slot = jnp.repeat(jnp.arange(1, 3, dtype=jnp.int32), PAGE)
    row_pos = jnp.tile(positions, 2)
    row_level = INNER - 1 + row_slot
    row_ok = row_pos < jnp.repeat(page_counts[1:], PAGE)
    earlier = key_level[None, :] < row_level[:, None]
    same_page = (key_level[None, :] == row_level[:, None]) & (key_pos[None, :] <= row_pos[:, None])
    allowed_leaf = row_ok[:, None] & key_ok[None, :] & (earlier | same_page)
    grad_q_leaf, grad_k_leaf, grad_v_leaf = attend(
        queries[PAGE:].reshape(2 * PAGE, kv_local, group_size, HD),
        grad_out[PAGE:].reshape(2 * PAGE, kv_local, group_size, HD),
        log_norms[:, PAGE:].reshape(kv_local, group_size, 2 * PAGE),
        row_deltas[:, PAGE:].reshape(kv_local, group_size, 2 * PAGE),
        path_keys,
        path_values,
        allowed_leaf,
    )

    def inner_work():
        inner_key_level = key_level[:inner_rows]
        inner_key_pos = key_pos[:inner_rows]
        inner_earlier = inner_key_level[None, :] < inner_level
        inner_same = (inner_key_level[None, :] == inner_level) & (
            inner_key_pos[None, :] <= positions[:, None]
        )
        allowed_inner = (
            (positions < page_counts[0])[:, None]
            & key_ok[None, :inner_rows]
            & (inner_earlier | inner_same)
        )
        return attend(
            queries[:PAGE].reshape(PAGE, kv_local, group_size, HD),
            grad_out[:PAGE].reshape(PAGE, kv_local, group_size, HD),
            log_norms[:, :PAGE].reshape(kv_local, group_size, PAGE),
            row_deltas[:, :PAGE].reshape(kv_local, group_size, PAGE),
            path_keys[:inner_rows],
            path_values[:inner_rows],
            allowed_inner,
        )

    def inner_empty():
        return (
            jnp.zeros((PAGE, kv_local, group_size, HD), jnp.float32),
            jnp.zeros((inner_rows, kv_local, HD), jnp.float32),
            jnp.zeros((inner_rows, kv_local, HD), jnp.float32),
        )

    grad_q_inner, grad_k_inner, grad_v_inner = lax.cond(has_inner, inner_work, inner_empty)
    shared_keys = (grad_k_leaf[:inner_rows] + grad_k_inner).reshape(INNER, PAGE, width_local)
    shared_values = (grad_v_leaf[:inner_rows] + grad_v_inner).reshape(INNER, PAGE, width_local)
    for bit_index in range(leaves.bit_length() - 1):
        active = spanning(leaves, bit_index)
        far_keys, far_values = swapped(
            (shared_keys[:active], shared_values[:active]), ("leaf", "sub"), bit_index
        )
        shared_keys = jnp.concatenate([shared_keys[:active] + far_keys, shared_keys[active:]])
        shared_values = jnp.concatenate(
            [shared_values[:active] + far_values, shared_values[active:]]
        )
    own_keys = jnp.where(has_inner, shared_keys[inner_level], 0.0)
    own_values = jnp.where(has_inner, shared_values[inner_level], 0.0)
    grad_keys = (
        jnp.concatenate([own_keys[None], grad_k_leaf[inner_rows:].reshape(2, PAGE, width_local)])
        .reshape(SLOTS * PAGE, width_local)
        .astype(jnp.bfloat16)
    )
    grad_values = (
        jnp.concatenate([own_values[None], grad_v_leaf[inner_rows:].reshape(2, PAGE, width_local)])
        .reshape(SLOTS * PAGE, width_local)
        .astype(jnp.bfloat16)
    )
    grad_queries = (
        jnp.concatenate([grad_q_inner, grad_q_leaf])
        .reshape(SLOTS * PAGE, queries.shape[1])
        .astype(jnp.bfloat16)
    )
    grad_input = lax.dot_general(
        lax.all_gather(grad_values, "tensor", axis=1, tiled=True),
        w_value,
        (((1,), (1,)), ((), ())),
        preferred_element_type=jnp.float32,
    ).astype(jnp.bfloat16)
    return (grad_queries, grad_keys, grad_values, grad_input)


def solution(mesh):
    placed = (
        P(("groups", "leaf", "sub"), "tensor"),
        P(("groups", "leaf", "sub"), "tensor"),
        P(("groups", "leaf", "sub"), "tensor"),
        P(("groups", "leaf", "sub"), "tensor"),
        P("tensor", ("groups", "leaf", "sub")),
        P("tensor", ("groups", "leaf", "sub")),
        P(("groups", "leaf", "sub"), None),
        P(("groups", "leaf", "sub"), None),
        P("tensor", None),
    )
    return jax.shard_map(
        on_device,
        mesh=mesh,
        in_specs=placed,
        out_specs=(
            P(("groups", "leaf", "sub"), "tensor"),
            P(("groups", "leaf", "sub"), "tensor"),
            P(("groups", "leaf", "sub"), "tensor"),
            P(("groups", "leaf", "sub"), "tensor"),
        ),
        check_vma=False,
    )
```

profile of v0, /device:TPU:0, one launch (start us, length us, event | category | flops | bytes accessed | tf_op | source)
XLA Modules:
  0.0 211.0 jit_solution(9123053149655026333)
XLA Ops:
  7.2 1.6 slice.134
  8.9 1.6 slice.138
  10.5 0.7 fusion.43
  11.1 1.2 dynamic-slice
  12.4 1.3 bitcast_dynamic-update-slice_fusion
  13.7 1.4 compare_reduce_fusion
  15.1 10.6 %all-reduce = s32[8]{0:T(128)S(1)} all-reduce(s32[8]{0:T(128)S(1)} %bitcast_dynamic-update-slice_fusion), channel_id=2, replica_groups=mesh['groups'=2,'leaf'=4,'tensor'=2,'sub'=2] {'leaf','sub'}, use_global_device_ids=true, to_apply=%add | all-reduce | flops 8 | bytes 64 | tf_op jit(solution)/shard_map/all_gather | solution.py:75
  25.7 1.7 slice.140
  28.1 3.1 %slice.142 = bf16[256,4096]{1,0:T(8,128)(2,1)} slice(bf16[384,4096]{1,0:T(8,128)(2,1)} %param.11), slice={[128:384], [0:4096]} | slice | bytes 4194304 | tf_op jit(solution)/shard_map/slice | solution.py:99
  31.2 3.3 %copy.70 = bf16[256,4096]{0,1:T(8,128)(2,1)S(1)} copy(bf16[256,4096]{1,0:T(8,128)(2,1)} %slice.142) | data formatting | bytes 4194304
  34.6 3.2 %slice.144 = bf16[256,4096]{1,0:T(8,128)(2,1)} slice(bf16[384,4096]{1,0:T(8,128)(2,1)} %param.12), slice={[128:384], [0:4096]} | slice | bytes 4194304 | tf_op jit(solution)/shard_map/slice | solution.py:100
  37.8 4.1 %copy.71 = bf16[256,4096]{0,1:T(8,128)(2,1)} copy(bf16[256,4096]{1,0:T(8,128)(2,1)} %slice.144) | data formatting | bytes 4194304
  41.8 0.6 gather_fusion
  42.6 0.7 fusion.42
  44.1 1.0 or_and_fusion.1
  45.1 1.8 gather_fusion.1
  46.9 12.0 %all-gather.8.cloned.1.call-done = bf16[1024,512]{1,0:T(8,128)(2,1)} async-done(((bf16[128,512]{1,0:T(8,128)(2,1)}), bf16[1024,512]{1,0:T(8,128)(2,1)}) %all-gather.8.cloned.1.call-update) | async-done | bytes 1048592 | tf_op jit(solution)/shard_map/all_gather | solution.py:74
  59.0 2.5 %gather_fusion.2 = bf16[3,128,512]{2,1,0:T(8,128)(2,1)} fusion(bf16[8,128,512]{2,1,0:T(8,128)(2,1)} %bitcast.176, s32[1024]{0:T(1024)S(1)} %pad_clamp_fusion), kind=kCustom, calls=%fused_computation.2 | custom fusion | bytes 786444 | tf_op jit(solution)/shard_map/gather | solution.py:79
  61.8 1.1 pad_maximum_fusion.2
  62.9 1.0 reshape.384
  63.9 0.9 copy.56
  64.8 8.6 %fusion.46 = f32[4,640,256,8]{2,1,3,0:T(8,128)} fusion(bf16[640,4,128,1]{0,2,3,1:T(8,128)(2,1)S(1)} %copy.56, bf16[256,4,8,128]{0,3,2,1:T(8,128)(2,1)S(1)} %bitcast.159), kind=kOutput, calls=%fused_computation.99 | convolution fusion | flops 1342177280 | bytes 23724032 | tf_op jit(solution)/shard_map/rkgd,nkd->kgrn/dot_general | solution.py:28
  73.4 12.1 %fusion.26 = f32[640,4,128]{2,0,1:T(8,128)} fusion(bf16[256,4,8,128]{0,3,2,1:T(8,128)(2,1)} %bitcast.166, f32[4,640,256,8]{2,1,3,0:T(8,128)} %fusion.46, f32[4,8,256]{2,1,0:T(8,128)} %get-tuple-element.91, pred[256,640]{0,1:T(8,128)(4,1)} %or_and_fusion.1), kind=kOutput, calls=%fused_computation.43 | convolution fusion | flops 1363148800 | bytes 24576000 | tf_op jit(solution)/shard_map/kgrn,rkgd->nkd/dot_general | solution.py:37
  85.5 13.2 %fusion.18 = bf16[4,8,256,640]{2,3,1,0:T(8,128)(2,1)} fusion(f32[4,640,256,8]{2,1,3,0:T(8,128)} %fusion.46, f32[4,8,256]{2,1,0:T(8,128)S(1)} %get-tuple-element.90, f32[4,8,256]{2,1,0:T(8,128)} %get-tuple-element.91, pred[256,640]{0,1:T(8,128)(4,1)} %or_and_fusion.1, bf16[256,4,8,128]{0,3,2,1:T(8,128)(2,1)} %bitcast.167, ...), kind=kOutput, calls=%fused_computation.32 | convolution fusion | flops 1373634560 | bytes 34439168 | tf_op jit(solution)/shard_map/rkgd,nkd->kgrn/dot_general | solution.py:32
  98.7 7.9 %fusion.30 = f32[640,4,128]{2,0,1:T(8,128)} fusion(bf16[4,8,256,640]{2,3,1,0:T(8,128)(2,1)} %fusion.18, bf16[256,4,8,128]{0,3,2,1:T(8,128)(2,1)S(1)} %bitcast.160), kind=kOutput, calls=%fused_computation.46 | convolution fusion | flops 1342504960 | bytes 13893632 | tf_op jit(solution)/shard_map/kgrn,rkgd->nkd/dot_general | solution.py:41
  106.6 27.6 %conditional.1 = (f32[384,4,128]{2,0,1:T(8,128)}, f32[384,4,128]{2,0,1:T(8,128)}, bf16[128,4,8,128]{0,3,2,1:T(8,128)(2,1)}) conditional(s32[]{:T(128)} %convert_element_type.30, () %tuple.16, (s32[1,3]{1,0:T(1,128)S(1)}, s32[128]{0:T(128)S(1)}, s32[5]{0:T(128)S(1)}, s32[640]{0:T(1024)S(1)}, s32[640]{0:T(1024)S(1)}, /*index=5*/s32[640]{0:T(1024)S(1)}, ...), branch_computations={%region_2.3_spmd, %region_3.4_spmd} | conditional | flops 2030487040 | bytes 85474064 | solution.py:137
  107.6 0.6 slice_bitcast_fusion.5
  108.5 2.2 %copy.23 = bf16[640,4,128]{2,0,1:T(8,128)(2,1)} copy(bf16[640,4,128]{2,1,0:T(4,128)(2,1)} %copy-done.3) | data formatting | bytes 1310720 | tf_op jit(solution)/shard_map
  110.7 2.0 copy.25
  112.7 4.6 %copy.26 = bf16[384,4096]{0,1:T(8,128)(2,1)} copy(bf16[384,4096]{1,0:T(8,128)(2,1)} %get-tuple-element.75) | data formatting | bytes 6291456 | tf_op jit(solution)/shard_map
  117.3 2.3 %slice.167 = bf16[128,4096]{0,1:T(8,128)(2,1)} slice(bf16[384,4096]{0,1:T(8,128)(2,1)} %copy.26), slice={[0:128], [0:4096]} | slice | bytes 2097152 | tf_op jit(solution)/shard_map/cond/branch_1_fun/slice | solution.py:122
  119.6 2.8 %copy.24 = bf16[384,4096]{0,1:T(8,128)(2,1)} copy(bf16[384,4096]{1,0:T(8,128)(2,1)S(1)} %copy-done) | data formatting | bytes 6291456 | tf_op jit(solution)/shard_map
  122.4 1.4 slice.165
  123.8 2.0 fusion.14
  125.8 2.0 fusion.9
  127.8 2.0 fusion.1
  129.8 1.9 fusion.13
  131.6 1.2 fusion.8
  132.8 1.3 copy.69
  134.2 1.6 slice_add_fusion
  136.2 1.2 reshape.391
  137.7 1.2 slice_add_fusion.1
  141.9 1.5 add.79
  143.5 0.9 slice.174
  144.4 1.7 collective-permute-start.4
  146.2 0.9 slice.169
  147.6 5.8 %fusion.25 = bf16[256,4,8,128]{0,3,2,1:T(8,128)(2,1)S(1)} fusion(bf16[640,4,128,1]{0,2,3,1:T(8,128)(2,1)S(1)} %copy-done.2, bf16[4,8,256,640]{2,3,1,0:T(8,128)(2,1)} %fusion.18), kind=kOutput, calls=%fused_computation.42 | convolution fusion | flops 1344274432 | bytes 13238272 | tf_op jit(solution)/shard_map/kgrn,nkd->rkgd/dot_general | solution.py:45
  153.4 0.7 slice.202
  154.2 1.1 slice.201
  155.2 1.8 pad_maximum_fusion
  157.0 2.9 %copy.42 = bf16[384,4096]{1,0:T(8,128)(2,1)} copy(bf16[384,4096]{0,1:T(8,128)(2,1)S(1)} %bitcast.161) | data formatting | bytes 6291456
  159.9 1.2 copy.38
  161.5 1.0 slice.176
  162.4 1.0 slice.171
  163.4 1.3 slice_add_fusion.4
  164.7 1.8 collective-permute-start.5
  166.5 6.7 %collective-permute-done.1 = f32[2,128,512]{2,1,0:T(8,128)} collective-permute-done((f32[2,128,512]{2,1,0:T(8,128)}, f32[2,128,512]{2,1,0:T(8,128)}, u32[]{:S(2)}, u32[]{:S(2)}) %collective-permute-start.1) | collective-permute-done | bytes 524320 | tf_op jit(solution)/shard_map/ppermute | solution.py:22
  173.3 1.3 slice_add_fusion.5
  175.0 11.2 %collective-permute-done.5 = f32[1,128,512]{2,1,0:T(8,128)S(1)} collective-permute-done((f32[1,128,512]{2,1,0:T(8,128)S(1)}, f32[1,128,512]{2,1,0:T(8,128)S(1)}, u32[]{:S(2)}, u32[]{:S(2)}) %collective-permute-start.5) | collective-permute-done | bytes 262176 | tf_op jit(solution)/shard_map/ppermute | solution.py:22
  186.2 0.8 fusion.34
  187.0 9.5 %all_gather.15 = bf16[384,1024]{1,0:T(8,128)(2,1)S(1)} all-gather(bf16[384,512]{1,0:T(8,128)(2,1)S(1)} %bitcast.168), channel_id=1, replica_groups=mesh['groups'=2,'leaf'=4,'tensor'=2,'sub'=2] {'tensor'}, dimensions={1}, use_global_device_ids=true | all-gather | bytes 1179648 | tf_op jit(solution)/shard_map/all_gather | solution.py:167
  196.6 0.8 fusion.37
  197.4 0.8 pad_maximum_fusion.3
  198.2 6.0 %convolution_convert_fusion = bf16[384,2560]{1,0:T(8,128)(2,1)} fusion(bf16[384,1024]{1,0:T(8,128)(2,1)S(1)} %all_gather.15, bf16[2560,1024]{1,0:T(8,128)(2,1)} %param.19), kind=kOutput, calls=%fused_computation.39 | convolution fusion | flops 2014248960 | bytes 7995392 | tf_op jit(solution)/shard_map/dot_general | solution.py:166
  (90 shorter events, 5.9 us)
Async XLA Ops:
  7.2 38.0 %all-gather.6.cloned.1.call-start = ((), (), s32[]{:S(2)}) async-start(), calls=%async_computation | async-start | bytes 1179648 | tf_op jit(solution)/shard_map/all_gather | solution.py:73
  8.8 50.2 %all-gather.8.cloned.1.call-start = ((), (), s32[]{:S(2)}) async-start(), calls=%async_computation.1 | async-start | bytes 1179648 | tf_op jit(solution)/shard_map/all_gather | solution.py:74
  34.5 8.0 %copy-start.20 = (s32[1,3]{1,0:T(1,128)S(1)}, s32[1,3]{1,0:T(1,128)}, u32[]{:S(2)}) copy-start(s32[1,3]{1,0:T(1,128)} %param.18) | copy-start | bytes 40
  34.5 8.1 %copy-start.19 = (s32[1,5]{1,0:T(1,128)S(1)}, s32[1,5]{1,0:T(1,128)}, u32[]{:S(2)}) copy-start(s32[1,5]{1,0:T(1,128)} %param.17) | copy-start | bytes 64
  34.5 9.0 %copy-start.13 = (f32[32,384]{1,0:T(8,128)S(1)}, f32[32,384]{1,0:T(8,128)}, u32[]{:S(2)}) copy-start(f32[32,384]{1,0:T(8,128)} %param.16) | copy-start | bytes 147460
  34.6 9.0 %copy-start.14 = (f32[32,384]{1,0:T(8,128)S(1)}, f32[32,384]{1,0:T(8,128)}, u32[]{:S(2)}) copy-start(f32[32,384]{1,0:T(8,128)} %param.15) | copy-start | bytes 147460
  34.6 27.0 %slice-start = ((bf16[384,512]{1,0:T(8,128)(2,1)}), bf16[256,512]{1,0:T(8,128)(2,1)S(1)}, s32[]{:S(2)}) async-start(bf16[384,512]{1,0:T(8,128)(2,1)} %param.13), calls=%async_computation.2 | async-start | bytes 524288 | tf_op jit(solution)/shard_map/slice | solution.py:81
  42.6 0.7 copy-start.17
  64.8 8.6 %copy-start.1 = (bf16[640,4,128,1]{0,2,3,1:T(8,128)(2,1)}, bf16[640,4,128,1]{0,2,3,1:T(8,128)(2,1)S(1)}, u32[]{:S(2)}) copy-start(bf16[640,4,128,1]{0,2,3,1:T(8,128)(2,1)S(1)} %copy.56) | copy-start | bytes 1966084
  73.4 12.1 %copy-start.7 = (bf16[640,4,128]{2,1,0:T(4,128)(2,1)S(1)}, bf16[640,4,128]{2,1,0:T(4,128)(2,1)}, u32[]{:S(2)}) copy-start(bf16[640,4,128]{2,1,0:T(4,128)(2,1)} %reshape.384) | copy-start | bytes 1966084
  98.7 7.9 %copy-start.18 = (s32[5]{0:T(128)S(1)}, s32[5]{0:T(128)}, u32[]{:S(2)}) copy-start(s32[5]{0:T(128)} %copy-done.17) | copy-start | bytes 64
  98.7 7.9 %copy-start.21 = (s32[1,3]{1,0:T(1,128)S(1)}, s32[1,3]{1,0:T(1,128)}, u32[]{:S(2)}) copy-start(s32[1,3]{1,0:T(1,128)} %param.18) | copy-start | bytes 40
  106.8 1.4 copy-start.3
  106.8 1.4 copy-start.8
  108.5 11.1 %copy-start = (bf16[384,4096]{1,0:T(8,128)(2,1)S(1)}, bf16[384,4096]{1,0:T(8,128)(2,1)}, u32[]{:S(2)}) copy-start(bf16[384,4096]{1,0:T(8,128)(2,1)} %get-tuple-element.72) | copy-start | bytes 9437188 | tf_op jit(solution)/shard_map/cond
  122.4 3.4 %copy-start.11 = (bf16[128,4096]{0,1:T(8,128)(2,1)S(1)}, bf16[128,4096]{0,1:T(8,128)(2,1)}, u32[]{:S(2)}) copy-start(bf16[128,4096]{0,1:T(8,128)(2,1)} %slice.167) | copy-start | bytes 3145732 | tf_op jit(solution)/shard_map/cond
  122.4 3.4 %copy-start.16 = (f32[4,8,128]{2,1,0:T(8,128)S(1)}, f32[4,8,128]{2,1,0:T(8,128)}, u32[]{:S(2)}) copy-start(f32[4,8,128]{2,1,0:T(8,128)} %get-tuple-element.83) | copy-start | bytes 49156 | tf_op jit(solution)/shard_map/cond
  125.7 2.0 copy-start.12
  125.8 2.0 copy-start.15
  127.8 3.9 %copy-start.9 = (bf16[640,4,128]{2,0,1:T(8,128)(2,1)S(1)}, bf16[640,4,128]{2,0,1:T(8,128)(2,1)}, u32[]{:S(2)}) copy-start(bf16[640,4,128]{2,0,1:T(8,128)(2,1)} %copy.23) | copy-start | bytes 1966084 | tf_op jit(solution)/shard_map/cond
  134.2 3.5 %copy-start.6 = (f32[640,4,128]{2,0,1:T(8,128)S(1)}, f32[640,4,128]{2,0,1:T(8,128)}, u32[]{:S(2)}) copy-start(f32[640,4,128]{2,0,1:T(8,128)} %fusion.30) | copy-start | bytes 3932164
  137.5 4.5 %collective-permute-start.3 = (f32[3,128,512]{2,1,0:T(8,128)}, f32[3,128,512]{2,1,0:T(8,128)}, u32[]{:S(2)}, u32[]{:S(2)}) collective-permute-start(f32[3,128,512]{2,1,0:T(8,128)} %reshape.391), channel_id=1, source_target_pairs={{0,1},{1,0},{4,5},{5,4},{8,9},{9,8},{12,13},{13,12},{2,3},{3,2},{6... | collective-permute-start | bytes 2359304 | tf_op jit(solution)/shard_map/ppermute | solution.py:22
  138.9 8.7 %copy-start.2 = (bf16[640,4,128,1]{0,2,3,1:T(8,128)(2,1)S(1)}, bf16[640,4,128,1]{0,2,3,1:T(8,128)(2,1)}, u32[]{:S(2)}) copy-start(bf16[640,4,128,1]{0,2,3,1:T(8,128)(2,1)} %copy-done.1) | copy-start | bytes 1966084
  139.7 6.3 %collective-permute-start = (f32[3,128,512]{2,1,0:T(8,128)S(1)}, f32[3,128,512]{2,1,0:T(8,128)S(1)}, u32[]{:S(2)}, u32[]{:S(2)}) collective-permute-start(f32[3,128,512]{2,1,0:T(8,128)S(1)} %reshape.389), channel_id=1, source_target_pairs={{0,1},{1,0},{4,5},{5,4},{8,9},{9,8},{12,13},{13,12},{2,3},{3,2},{6... | collective-permute-start | bytes 2359304 | tf_op jit(solution)/shard_map/ppermute | solution.py:22
  143.5 2.6 %copy-start.5 = (f32[3,128,512]{2,1,0:T(8,128)}, f32[3,128,512]{2,1,0:T(8,128)S(1)}, u32[]{:S(2)}) copy-start(f32[3,128,512]{2,1,0:T(8,128)S(1)} %add.79) | copy-start | bytes 2359300
  144.4 19.0 %collective-permute-start.4 = (f32[2,128,512]{2,1,0:T(8,128)}, f32[2,128,512]{2,1,0:T(8,128)}, u32[]{:S(2)}, u32[]{:S(2)}) collective-permute-start(f32[2,128,512]{2,1,0:T(8,128)} %slice.174), channel_id=1, source_target_pairs={{0,4},{4,0},{1,5},{5,1},{8,12},{12,8},{9,13},{13,9},{2,6},{6,2},{3... | collective-permute-start | bytes 1572872 | tf_op jit(solution)/shard_map/ppermute | solution.py:22
  146.2 1.1 copy-start.4
  147.3 26.0 %collective-permute-start.1 = (f32[2,128,512]{2,1,0:T(8,128)}, f32[2,128,512]{2,1,0:T(8,128)}, u32[]{:S(2)}, u32[]{:S(2)}) collective-permute-start(f32[2,128,512]{2,1,0:T(8,128)} %slice.169), channel_id=1, source_target_pairs={{0,4},{4,0},{1,5},{5,1},{8,12},{12,8},{9,13},{13,9},{2,6},{6,2},{3... | collective-permute-start | bytes 1572872 | tf_op jit(solution)/shard_map/ppermute | solution.py:22
  164.7 21.4 %collective-permute-start.5 = (f32[1,128,512]{2,1,0:T(8,128)S(1)}, f32[1,128,512]{2,1,0:T(8,128)S(1)}, u32[]{:S(2)}, u32[]{:S(2)}) collective-permute-start(f32[1,128,512]{2,1,0:T(8,128)S(1)} %slice.175), channel_id=1, source_target_pairs={{0,8},{8,0},{1,9},{9,1},{4,12},{12,4},{5,13},{13,5},{2,10},{10,2},... | collective-permute-start | bytes 786440 | tf_op jit(solution)/shard_map/ppermute | solution.py:22
  174.6 22.0 %collective-permute-start.2 = (f32[1,128,512]{2,1,0:T(8,128)S(1)}, f32[1,128,512]{2,1,0:T(8,128)S(1)}, u32[]{:S(2)}, u32[]{:S(2)}) collective-permute-start(f32[1,128,512]{2,1,0:T(8,128)S(1)} %slice.170), channel_id=1, source_target_pairs={{0,8},{8,0},{1,9},{9,1},{4,12},{12,4},{5,13},{13,5},{2,10},{10,2},... | collective-permute-start | bytes 786440 | tf_op jit(solution)/shard_map/ppermute | solution.py:22
  187.0 17.1 %copy-start.10 = (bf16[3,128,512]{2,1,0:T(8,128)(2,1)}, bf16[3,128,512]{2,1,0:T(8,128)(2,1)S(1)}, u32[]{:S(2)}) copy-start(bf16[3,128,512]{2,1,0:T(8,128)(2,1)S(1)} %pad_maximum_fusion.4) | copy-start | bytes 1179652
Sparse Core Ops, SparseCore 0:
  10.2 24.8 all-gather.5
  37.3 21.6 all-gather.7
where the time goes:
time: 212 us; the launch traced here: 211 us
  matrix products  62.6 us (30%)
  local copies, waits for them, and re-layouts  58.8 us (28%)
  waiting for transfers between devices  30 us (14%)
  blocking collectives  20.1 us (9%)
  other arithmetic  17.4 us (8%)
  between operations  16.9 us (8%)
  starting transfers between devices  4.84 us (2%)
    ppermute x6, waiting for transfers between devices, swapped(): return lax.ppermute(block, axis, route)  17.9 us
    dot_general x2, matrix products, attend(): jnp.einsum('rkgd,nkd->kgrn', grad_rows, value_rows, preferred_element_typ...  15.1 us
    dot_general x2, matrix products, attend(): jnp.einsum('kgrn,rkgd->nkd', weights_low, grad_rows, preferred_element_ty...  14.1 us
    unnamed x34, local copies, waits for them, and re-layouts  13 us
    all_gather x1, waiting for transfers between devices, on_device(): lax.all_gather(value_pages[:1], ('leaf', 'sub'), axis=0, tiled=True)  12 us
    another operation x4, local copies, waits for them, and re-layouts  11.6 us
    all_gather x1, blocking collectives, on_device(): lax.all_gather(page_counts[:1], ('leaf', 'sub'), axis=0, tiled=True)  10.6 us
    dot_general x2, matrix products, attend(): jnp.einsum('rkgd,nkd->kgrn', query_rows, key_rows, preferred_element_type...  10.6 us
  transfers between devices with their start and end apart: 8, of which 3 were waited for; matrix products, arithmetic and copies ran while one was open for 24% of the time, Pallas kernels for 0%

commit v1 on v0

v1 whole, which is shorter than its diff:
```python
import functools
import math

import jax
import jax.numpy as jnp
from jax import lax
from jax.experimental import pallas as pl
from jax.experimental.pallas import tpu as pltpu
from jax.sharding import PartitionSpec as P

HD = 128
PAGE = 128
SLOTS = 3
INNER = 3
LOG2E = math.log2(math.e)
SCALE = 1.0 / math.sqrt(HD)
BF16 = jnp.bfloat16
F32 = jnp.float32
I32 = jnp.int32
VMEM_LIMIT = 40 << 20
SMALL_LIMIT = 16 << 20


def params(limit=VMEM_LIMIT):
    return pltpu.CompilerParams(vmem_limit_bytes=limit)


def dot_t(left, right):
    return lax.dot_general(left, right, (((1,), (1,)), ((), ())), preferred_element_type=F32)


def dot_n(left, right):
    return lax.dot_general(left, right, (((1,), (0,)), ((), ())), preferred_element_type=F32)


def dot_rows(left, right):
    return lax.dot_general(left, right, (((0,), (0,)), ((), ())), preferred_element_type=F32)


class Path:
    def __init__(self, ids_ref):
        self.pages = [ids_ref[j] for j in range(INNER)]
        self.own = ids_ref[INNER] - 1
        self.leaf = self.own // SLOTS
        self.core = lax.rem(self.leaf, 2)
        self.owns = [self.pages[j] == self.own for j in range(INNER)]
        self.has_inner = self.owns[0] | self.owns[1] | self.owns[2]

    def owner(self, level):
        return self.pages[level] // SLOTS

    def same(self, level, shift):
        return (self.owner(level) >> shift) == (self.leaf >> shift)


def row_ok(count, rows, width):
    return lax.broadcasted_iota(I32, (rows, width), 0) < count


def whole(shape):
    return pl.BlockSpec(shape, lambda *_: (0,) * len(shape))


def small(body, ids, counts, arrays, outs, aliases=None):
    return pl.pallas_call(
        body,
        out_shape=tuple(jax.ShapeDtypeStruct(s, d) for s, d in outs),
        grid_spec=pltpu.PrefetchScalarGridSpec(
            num_scalar_prefetch=2,
            grid=(1,),
            in_specs=[whole(a.shape) for a in arrays],
            out_specs=tuple(whole(s) for s, _ in outs),
        ),
        compiler_params=params(SMALL_LIMIT),
    )(ids, counts, *arrays)


def probabilities(q, g, k, v, norm, delta, keep):
    p = jnp.exp2(dot_t(q, k) * (SCALE * LOG2E) - norm)
    if keep is not None:
        p = jnp.where(keep, p, 0.0)
    ds = p * (dot_t(g, v) - delta)
    return p.astype(BF16), ds.astype(BF16)


def own_pages_kernel(group, ids, counts, q, g, k, v, norms, deltas, l2_own, l2_far, *refs):
    dq, dk, dv, dv12, own0, send2 = refs[-7:-1]
    acc = refs[-1]
    path = Path(ids)
    n0 = jnp.where(path.has_inner, counts[0], 0)
    ok = [row_ok(n, PAGE, HD) for n in (n0, counts[1], counts[2])]
    ok3 = jnp.concatenate(ok, axis=0)
    zero = jnp.zeros((), BF16)
    kk = jnp.where(ok3, k[...], zero)
    vv = jnp.where(ok3, v[...], zero)
    mine = path.owns[2]
    k2 = jnp.where(mine, l2_own[0], l2_far[0])
    v2 = jnp.where(mine, l2_own[1], l2_far[1])
    k0, v0 = kk[:PAGE], vv[:PAGE]
    k3 = jnp.concatenate([kk[PAGE:], k2], axis=0)
    v3 = jnp.concatenate([vv[PAGE:], v2], axis=0)
    keep0 = lax.broadcasted_iota(I32, (PAGE, PAGE), 1) <= lax.broadcasted_iota(
        I32, (PAGE, PAGE), 0
    )
    col = lax.broadcasted_iota(I32, (2 * PAGE, 3 * PAGE), 1)
    row = lax.broadcasted_iota(I32, (2 * PAGE, 3 * PAGE), 0)
    keep3 = (col <= row) | (col >= 2 * PAGE)
    norm_t = (norms[...] * LOG2E).T
    delta_t = deltas[...].T
    acc[...] = jnp.zeros_like(acc)
    for h in range(group):
        lanes = slice(h * HD, (h + 1) * HD)
        qh = jnp.where(ok3, q[:, lanes], zero)
        gh = jnp.where(ok3, g[:, lanes], zero)
        norm, delta = norm_t[:, h : h + 1], delta_t[:, h : h + 1]
        p, ds = probabilities(
            qh[:PAGE], gh[:PAGE], k0, v0, norm[:PAGE], delta[:PAGE], keep0
        )
        dq[:PAGE, lanes] = dot_n(ds, k0)
        acc[0, :, :PAGE] += dot_rows(qh[:PAGE], ds)
        acc[1, :, :PAGE] += dot_rows(gh[:PAGE], p)
        p, ds = probabilities(
            qh[PAGE:], gh[PAGE:], k3, v3, norm[PAGE:], delta[PAGE:], keep3
        )
        dq[PAGE:, lanes] = dot_n(ds, k3)
        acc[0, :, PAGE:] += dot_rows(qh[PAGE:], ds)
        acc[1, :, PAGE:] += dot_rows(gh[PAGE:], p)
    grad_k = acc[0].T * SCALE
    grad_v = acc[1].T
    ok12 = ok3[PAGE:]
    dk[:PAGE] = jnp.zeros((PAGE, HD), BF16)
    dv[:PAGE] = jnp.zeros((PAGE, HD), BF16)
    dk[PAGE:] = jnp.where(ok12, grad_k[PAGE : 3 * PAGE], 0.0).astype(BF16)
    low = jnp.where(ok12, grad_v[PAGE : 3 * PAGE], 0.0).astype(BF16)
    dv[PAGE:] = low
    dv12[...] = low
    own0[0] = grad_k[:PAGE] + jnp.where(mine, grad_k[3 * PAGE :], 0.0)
    own0[1] = grad_v[:PAGE] + jnp.where(mine, grad_v[3 * PAGE :], 0.0)
    send2[0] = grad_k[3 * PAGE :].astype(BF16)
    send2[1] = grad_v[3 * PAGE :].astype(BF16)


def shared_pages_kernel(group, ids, counts, q, g, norms, deltas, mine, far, prev, *refs):
    dq, keep_out, send_out = refs[-4:-1]
    acc = refs[-1]
    path = Path(ids)
    n0 = jnp.where(path.has_inner, counts[0], 0)
    ok3 = jnp.concatenate([row_ok(n, PAGE, HD) for n in (n0, counts[1], counts[2])], axis=0)
    zero = jnp.zeros((), BF16)
    first = path.core == 0
    near = jnp.concatenate([mine[0], mine[1]], axis=0)
    away = jnp.concatenate([far[0], far[1]], axis=0)
    kk = jnp.where(first, near, away)
    vv = jnp.where(first, away, near)
    col = lax.broadcasted_iota(I32, (PAGE, 2 * PAGE), 1)
    limit = jnp.where(path.owns[2], 2 * PAGE, jnp.where(path.owns[1], PAGE, 0))
    keep0 = col < limit
    norm_t = (norms[...] * LOG2E).T
    delta_t = deltas[...].T
    acc[...] = jnp.zeros_like(acc)
    for h in range(group):
        lanes = slice(h * HD, (h + 1) * HD)
        qh = jnp.where(ok3, q[:, lanes], zero)
        gh = jnp.where(ok3, g[:, lanes], zero)
        norm, delta = norm_t[:, h : h + 1], delta_t[:, h : h + 1]
        for rows, keep in ((slice(0, PAGE), keep0), (slice(PAGE, 3 * PAGE), None)):
            p, ds = probabilities(qh[rows], gh[rows], kk, vv, norm[rows], delta[rows], keep)
            total = (prev[rows, lanes] + dot_n(ds, kk)) * SCALE
            dq[rows, lanes] = jnp.where(ok3[rows], total, 0.0).astype(BF16)
            acc[0] += dot_rows(qh[rows], ds)
            acc[1] += dot_rows(gh[rows], p)
    grad_k = acc[0].T * SCALE
    grad_v = acc[1].T
    kept = jnp.where(first, grad_k, grad_v)
    sent = jnp.where(first, grad_v, grad_k).astype(BF16)
    for j in range(2):
        keep_out[j] = kept[j * PAGE : (j + 1) * PAGE]
        send_out[j] = sent[j * PAGE : (j + 1) * PAGE]


def cost(rows, keys, kv, group):
    return pl.CostEstimate(
        flops=10 * rows * keys * HD * kv * group,
        bytes_accessed=kv * group * HD * SLOTS * PAGE * 8,
        transcendentals=rows * keys * kv * group,
    )


def own_pages(start, count, group, ids, counts, q, g, k, v, norms, deltas, l2_own, l2_far, carry):
    rows = SLOTS * PAGE
    width = k.shape[1]
    wide = group * HD
    part = count * HD
    at = lambda i, *_: (0, start + i)
    col = lambda i, *_: (0, i)
    page = pl.BlockSpec((2, PAGE, HD), lambda i, *_: (0, 0, start + i))
    here = pl.BlockSpec((2, PAGE, HD), lambda i, *_: (0, 0, i))
    vec = pl.BlockSpec((group, rows), lambda i, *_: (start + i, 0))
    args = [q, g, k, v, norms, deltas, l2_own, l2_far]
    in_specs = [
        pl.BlockSpec((rows, wide), at),
        pl.BlockSpec((rows, wide), at),
        pl.BlockSpec((rows, HD), at),
        pl.BlockSpec((rows, HD), at),
        vec,
        vec,
        page,
        page,
    ]
    aliases = {}
    if carry is not None:
        aliases = {2 + len(args): 1, 3 + len(args): 2}
        args += list(carry)
        in_specs += [pl.BlockSpec(memory_space=pl.ANY)] * 2
    return pl.pallas_call(
        functools.partial(own_pages_kernel, group),
        out_shape=(
            jax.ShapeDtypeStruct((rows, count * wide), F32),
            jax.ShapeDtypeStruct((rows, width), BF16),
            jax.ShapeDtypeStruct((rows, width), BF16),
            jax.ShapeDtypeStruct((2 * PAGE, part), BF16),
            jax.ShapeDtypeStruct((2, PAGE, part), F32),
            jax.ShapeDtypeStruct((2, PAGE, part), BF16),
        ),
        grid_spec=pltpu.PrefetchScalarGridSpec(
            num_scalar_prefetch=2,
            grid=(count,),
            in_specs=in_specs,
            out_specs=(
                pl.BlockSpec((rows, wide), col),
                pl.BlockSpec((rows, HD), at),
                pl.BlockSpec((rows, HD), at),
                pl.BlockSpec((2 * PAGE, HD), col),
                here,
                here,
            ),
            scratch_shapes=[pltpu.VMEM((2, HD, 4 * PAGE), F32)],
        ),
        input_output_aliases=aliases,
        compiler_params=params(),
        cost_estimate=cost(2 * PAGE, 4 * PAGE, count, group),
    )(ids, counts, *args)


def shared_pages(start, count, group, ids, counts, q, g, norms, deltas, mine, far, prev, carry):
    rows = SLOTS * PAGE
    wide = group * HD
    part = count * HD
    at = lambda i, *_: (0, start + i)
    page = pl.BlockSpec((2, PAGE, HD), lambda i, *_: (0, 0, start + i))
    here = pl.BlockSpec((2, PAGE, HD), lambda i, *_: (0, 0, i))
    vec = pl.BlockSpec((group, rows), lambda i, *_: (start + i, 0))
    args = [q, g, norms, deltas, mine, far, prev]
    in_specs = [
        pl.BlockSpec((rows, wide), at),
        pl.BlockSpec((rows, wide), at),
        vec,
        vec,
        page,
        page,
        pl.BlockSpec((rows, wide), lambda i, *_: (0, i)),
    ]
    aliases = {}
    if carry is not None:
        aliases = {2 + len(args): 0}
        args.append(carry)
        in_specs.append(pl.BlockSpec(memory_space=pl.ANY))
    return pl.pallas_call(
        functools.partial(shared_pages_kernel, group),
        out_shape=(
            jax.ShapeDtypeStruct(q.shape, BF16),
            jax.ShapeDtypeStruct((2, PAGE, part), F32),
            jax.ShapeDtypeStruct((2, PAGE, part), BF16),
        ),
        grid_spec=pltpu.PrefetchScalarGridSpec(
            num_scalar_prefetch=2,
            grid=(count,),
            in_specs=in_specs,
            out_specs=(pl.BlockSpec((rows, wide), at), here, here),
            scratch_shapes=[pltpu.VMEM((2, HD, 2 * PAGE), F32)],
        ),
        input_output_aliases=aliases,
        compiler_params=params(),
        cost_estimate=cost(3 * PAGE, 2 * PAGE, count, group),
    )(ids, counts, *args)


def input_grad(parts, first, w, rows, carry):
    total = SLOTS * PAGE
    out_cols, depth = w.shape
    tile = next(t for t in (640, 512, 320, 128, out_cols) if out_cols % t == 0)
    lead = total - rows if carry is None else 0

    def body(flag, *refs):
        w_ref, out = refs[len(parts)], refs[-1]
        if len(parts) == 1:
            product = dot_t(refs[0][...], w_ref[...])
        else:
            mine, other = refs[0][...], refs[1][...]
            lead_half = flag[0] == 0
            half = depth // 2
            product = dot_t(jnp.where(lead_half, mine, other), w_ref[:, :half])
            product += dot_t(jnp.where(lead_half, other, mine), w_ref[:, half:])
        if lead:
            out[:lead] = jnp.zeros((lead, tile), BF16)
        out[lead:] = product.astype(BF16)

    args = [*parts, w]
    in_specs = [whole(a.shape) for a in parts] + [
        pl.BlockSpec((tile, depth), lambda i, *_: (i, 0))
    ]
    aliases = {}
    if carry is not None:
        aliases = {1 + len(args): 0}
        args.append(carry)
        in_specs.append(pl.BlockSpec(memory_space=pl.ANY))
    return pl.pallas_call(
        body,
        out_shape=jax.ShapeDtypeStruct((total, out_cols), BF16),
        grid_spec=pltpu.PrefetchScalarGridSpec(
            num_scalar_prefetch=1,
            grid=(out_cols // tile,),
            in_specs=in_specs,
            out_specs=pl.BlockSpec((rows + lead, tile), lambda i, *_: (0, i)),
        ),
        input_output_aliases=aliases,
        compiler_params=params(),
        cost_estimate=pl.CostEstimate(
            flops=2 * rows * depth * out_cols,
            bytes_accessed=2 * (depth * out_cols + rows * out_cols),
            transcendentals=0,
        ),
    )(first, *args)


def flipped(block, axis, bit):
    count = lax.axis_size(axis)
    return lax.ppermute(block, axis, [(i, i ^ bit) for i in range(count) if i ^ bit < count])


def spanning(leaves, bit_index):
    return len([j for j in range(INNER) if 2 << bit_index <= leaves >> j])


def gather_small_tree(ids, counts, own, width):
    page = ((PAGE, width), BF16)
    from_core = flipped(own, "sub", 1)

    def choose_chip(ids_ref, _, own_ref, far_ref, out):
        path = Path(ids_ref)
        for kind in range(2):
            for mine in (False, True):

                @pl.when((path.core == kind) & (path.owns[2] != mine))
                def _copy(kind=kind, mine=mine):
                    out[...] = (own_ref if mine else far_ref)[kind]

    (chip,) = small(choose_chip, ids, counts, [own, from_core], [page])
    from_pair = flipped(chip, "leaf", 1)

    def choose_pair(ids_ref, _, near_ref, far_ref, out):
        path = Path(ids_ref)
        out[...] = jnp.where(path.same(0, 1), near_ref[...], far_ref[...])

    (pair,) = small(choose_pair, ids, counts, [chip, from_pair], [page])
    from_half = flipped(pair, "leaf", 2)

    def choose_all(ids_ref, _, chip_ref, pair_far, pair_ref, half_far, out):
        path = Path(ids_ref)
        out[0] = jnp.where(path.same(0, 2), pair_ref[...], half_far[...])
        out[1] = jnp.where(path.same(1, 1), chip_ref[...], pair_far[...])

    (mine,) = small(
        choose_all,
        ids,
        counts,
        [chip, from_pair, pair, from_half],
        [((2, PAGE, width), BF16)],
    )
    return from_core, mine, flipped(mine, "sub", 1)


def reduce_small_tree(ids, counts, kept, sent):
    width = kept.shape[-1]
    two = (2, PAGE, width)
    far = flipped(sent, "sub", 1)

    def add_low(_, __, near, away, total, low):
        value = near[...] + away[...].astype(F32)
        total[...] = value
        low[...] = value.astype(BF16)

    total, low = small(add_low, ids, counts, [kept, far], [(two, F32), (two, BF16)])
    far = flipped(low, "leaf", 1)

    def add_pair(_, __, near, away, total, low):
        value = near[...] + away[...].astype(F32)
        total[...] = value
        low[...] = value[0].astype(BF16)

    total, low = small(
        add_pair, ids, counts, [total, far], [(two, F32), ((PAGE, width), BF16)]
    )
    far = flipped(low, "leaf", 2)

    def pick(ids_ref, _, near, away, out):
        path = Path(ids_ref)
        root = near[0] + away[...].astype(F32)
        out[...] = jnp.where(path.same(0, 1), root, near[1]).astype(BF16)

    (mine,) = small(pick, ids, counts, [total, far], [((PAGE, width), BF16)])
    return mine, flipped(mine, "sub", 1)


def finish_small_tree(ids, counts, own0, far2, mine, far, dk, dv):
    width = dk.shape[1]
    pieces = len(own0)

    def body(ids_ref, counts_ref, *refs):
        dk_out, dv_out, dv0_out = refs[-3:]
        path = Path(ids_ref)
        n0 = jnp.where(path.has_inner, counts_ref[0], 0)
        leads = path.core == 0
        for i in range(pieces):
            own_r, far2_r, mine_r, far_r = refs[4 * i : 4 * i + 4]
            part = own_r.shape[-1]
            cols = slice(i * part, (i + 1) * part)
            ok = row_ok(n0, PAGE, part)
            near, away = mine_r[...], far_r[...]
            k_in = jnp.where(path.owns[2], far2_r[0], jnp.where(leads, near, away))
            v_in = jnp.where(path.owns[2], far2_r[1], jnp.where(leads, away, near))
            dk_out[:, cols] = jnp.where(ok, own_r[0] + k_in.astype(F32), 0.0).astype(BF16)
            low = jnp.where(ok, own_r[1] + v_in.astype(F32), 0.0).astype(BF16)
            dv_out[:, cols] = low
            dv0_out[:, cols] = low

    args = [a for group in zip(own0, far2, mine, far) for a in group]
    return pl.pallas_call(
        body,
        out_shape=(
            jax.ShapeDtypeStruct(dk.shape, BF16),
            jax.ShapeDtypeStruct(dv.shape, BF16),
            jax.ShapeDtypeStruct((PAGE, width), BF16),
        ),
        grid_spec=pltpu.PrefetchScalarGridSpec(
            num_scalar_prefetch=2,
            grid=(1,),
            in_specs=[whole(a.shape) for a in args] + [pl.BlockSpec(memory_space=pl.ANY)] * 2,
            out_specs=(whole((PAGE, width)),) * 3,
        ),
        input_output_aliases={2 + len(args): 0, 3 + len(args): 1},
        compiler_params=params(SMALL_LIMIT),
    )(ids, counts, *args, dk, dv)


def gather_tree(ids, counts, own, width):
    leaves = lax.axis_size(("leaf", "sub"))
    owned = ids[:INNER] == ids[INNER] - 1
    pages = jnp.where(owned[:, None, None, None], own[None], jnp.zeros((), BF16))
    for bit in range(leaves.bit_length() - 1):
        active = spanning(leaves, bit)
        far = flipped(pages[:active], ("leaf", "sub"), 1 << bit)
        pages = jnp.concatenate([pages[:active] + far, pages[active:]])
    return pages


def reduce_tree(ids, parts):
    leaves = lax.axis_size(("leaf", "sub"))
    for bit in range(leaves.bit_length() - 1):
        active = spanning(leaves, bit)
        far = flipped(parts[:active], ("leaf", "sub"), 1 << bit)
        parts = jnp.concatenate([parts[:active] + far, parts[active:]])
    owned = ids[:INNER] == ids[INNER] - 1
    return jnp.sum(jnp.where(owned[:, None, None, None], parts, 0.0), axis=0)


def on_device(queries, grad_out, keys, values, log_norms, row_deltas, ancestors, counts, w_value):
    width = keys.shape[1]
    kv = width // HD
    group = queries.shape[1] // width
    leaves = lax.axis_size(("leaf", "sub"))
    ids = ancestors[0]
    rows_of = counts[0]
    pieces = 2 if kv % 2 == 0 else 1
    per = kv // pieces
    fast = leaves == 8 and lax.axis_size("sub") == 2

    def own_page(_, counts_ref, k_ref, v_ref, out):
        ok = row_ok(counts_ref[0], PAGE, width)
        out[0] = jnp.where(ok, k_ref[...], jnp.zeros((), BF16))
        out[1] = jnp.where(ok, v_ref[...], jnp.zeros((), BF16))

    own = pl.pallas_call(
        own_page,
        out_shape=jax.ShapeDtypeStruct((2, PAGE, width), BF16),
        grid_spec=pltpu.PrefetchScalarGridSpec(
            num_scalar_prefetch=2,
            grid=(1,),
            in_specs=[whole((PAGE, width))] * 2,
            out_specs=whole((2, PAGE, width)),
        ),
        compiler_params=params(SMALL_LIMIT),
    )(ids, rows_of, keys, values)
    if fast:
        l2_far, mine, theirs = gather_small_tree(ids, rows_of, own, width)
        l2_own = own
    else:
        pages = gather_tree(ids, rows_of, own, width)
        l2_own = l2_far = pages[2]
        first = lax.axis_index("sub") == 0
        mine = jnp.where(first, pages[:2, 0], pages[:2, 1])
        theirs = jnp.where(first, pages[:2, 1], pages[:2, 0])

    own_out, dk, dv = [], None, None
    for i in range(pieces):
        carry = None if dk is None else (dk, dv)
        dq, dk, dv, dv12, own0, send2 = own_pages(
            i * per, per, group, ids, rows_of, queries, grad_out, keys, values,
            log_norms, row_deltas, l2_own, l2_far, carry,
        )
        own_out.append((dq, dv12, own0, send2))

    grad_queries, shared_out = None, []
    for i in range(pieces):
        grad_queries, kept, sent = shared_pages(
            i * per, per, group, ids, rows_of, queries, grad_out, log_norms, row_deltas,
            mine, theirs, own_out[i][0], grad_queries,
        )
        shared_out.append((kept, sent))

    if fast:
        far2 = [flipped(o[3], "sub", 1) for o in own_out]
        reduced = [reduce_small_tree(ids, rows_of, *s) for s in shared_out]
        grad_keys, grad_values, dv0 = finish_small_tree(
            ids, rows_of, [o[2] for o in own_out], far2,
            [r[0] for r in reduced], [r[1] for r in reduced], dk, dv,
        )
    else:
        first = lax.axis_index("sub") == 0
        zero = jnp.zeros((), BF16)
        own0, gained = [], []
        for o, (kept, sent) in zip(own_out, shared_out):
            sent = sent.astype(F32)
            upper = jnp.stack([jnp.where(first, kept, sent), jnp.where(first, sent, kept)], axis=1)
            low = o[3].astype(F32)
            gained.append(reduce_tree(ids, jnp.concatenate([upper, low[None]])))
            owns2 = ids[2] == ids[INNER] - 1
            own0.append(o[2] - jnp.where(owns2, low, 0.0))
        total = jnp.concatenate(gained, axis=-1) + jnp.concatenate(own0, axis=-1)
        has = jnp.any(ids[:INNER] == ids[INNER] - 1)
        ok = (jnp.arange(PAGE) < jnp.where(has, rows_of[0], 0))[:, None]
        total = jnp.where(ok, total, 0.0).astype(BF16)
        grad_keys = lax.dynamic_update_slice(dk, total[0], (0, 0))
        grad_values = lax.dynamic_update_slice(dv, total[1], (0, 0))
        dv0 = total[1]

    dv12 = jnp.concatenate([o[1] for o in own_out], axis=1)
    tensor = lax.axis_size("tensor")
    side = lax.axis_index("tensor").astype(I32).reshape(1)
    if tensor == 2:
        spread = lambda part: [part, flipped(part, "tensor", 1)]
    else:
        spread = lambda part: [lax.all_gather(part, "tensor", axis=1, tiled=True)]
    grad_input = input_grad(spread(dv12), side, w_value, 2 * PAGE, None)
    grad_input = input_grad(spread(dv0), side, w_value, PAGE, grad_input)
    return (grad_queries, grad_keys, grad_values, grad_input)


def solution(mesh):
    placed = (
        P(("groups", "leaf", "sub"), "tensor"),
        P(("groups", "leaf", "sub"), "tensor"),
        P(("groups", "leaf", "sub"), "tensor"),
        P(("groups", "leaf", "sub"), "tensor"),
        P("tensor", ("groups", "leaf", "sub")),
        P("tensor", ("groups", "leaf", "sub")),
        P(("groups", "leaf", "sub"), None),
        P(("groups", "leaf", "sub"), None),
        P("tensor", None),
    )
    return jax.shard_map(
        on_device,
        mesh=mesh,
        in_specs=placed,
        out_specs=(
            P(("groups", "leaf", "sub"), "tensor"),
            P(("groups", "leaf", "sub"), "tensor"),
            P(("groups", "leaf", "sub"), "tensor"),
            P(("groups", "leaf", "sub"), "tensor"),
        ),
        check_vma=False,
    )
```

time: 212 us -> 104 us (0.49)
  matrix products: 62.6 us -> 0 us
  Pallas kernels: 0 us -> 55.2 us
  local copies, waits for them, and re-layouts: 58.8 us -> 14.5 us
  blocking collectives: 20.1 us -> 0 us
  other arithmetic: 17.4 us -> 0.01 us
  between operations: 16.9 us -> 0.83 us
  waiting for transfers between devices: 30 us -> 17.3 us
  starting transfers between devices: 4.84 us -> 16 us
    dot_general x11 -> x0, matrix products: 62.6 us -> none  [the longest x2 15.1 us: attend(): jnp.einsum('rkgd,nkd->kgrn', grad_rows, value_rows, preferred_element_typ...]
    pallas_call x0 -> x17, Pallas kernels: none -> 55.2 us  [the longest x2 21.6 us: own_pages(): pl.pallas_call(functools.partial(own_pages_kernel, group), out_shape=(jax...]
    slice x22 -> x0, local copies, waits for them, and re-layouts: 21.9 us -> none  [the longest x1 3.18 us: on_device(): grad_out[PAGE:].reshape(2 * PAGE, kv_local, group_size, HD)]
    all_gather x2 -> x0, blocking collectives: 20.1 us -> none  [the longest x1 10.6 us: on_device(): lax.all_gather(page_counts[:1], ('leaf', 'sub'), axis=0, tiled=True)]
    all_gather x2 -> x0, waiting for transfers between devices: 12 us -> none  [the longest x1 12 us: on_device(): lax.all_gather(value_pages[:1], ('leaf', 'sub'), axis=0, tiled=True)]
    another operation x5 -> x0, local copies, waits for them, and re-layouts: 11.7 us -> none
    ppermute x6 -> x16, starting transfers between devices: 4.76 us -> 16 us  [flipped(): lax.ppermute(block, axis, [(i, i ^ bit) for i in range(count) if i ^ bit...]
    add x9 -> x0, other arithmetic: 7.06 us -> none  [the longest x3 2.83 us: on_device(): shared_values[:active] + far_values]
  transfers between devices with their start and end apart: 8 -> 16, of which waited for: 3 -> 8; matrix products, arithmetic and copies ran while one was open for 24% -> 0% of each run, Pallas kernels for 0% -> 38%
where the time goes in v1:
time: 104 us
  Pallas kernels  55.2 us (53%)
  waiting for transfers between devices  17.3 us (17%)
  starting transfers between devices  16 us (15%)
  local copies, waits for them, and re-layouts  14.5 us (14%)
    pallas_call x2, Pallas kernels, own_pages(): pl.pallas_call(functools.partial(own_pages_kernel, group), out_shape=(jax...  21.6 us
    pallas_call x2, Pallas kernels, shared_pages(): pl.pallas_call(functools.partial(shared_pages_kernel, group), out_shape=(...  20.3 us
    ppermute x16, waiting for transfers between devices, flipped(): lax.ppermute(block, axis, [(i, i ^ bit) for i in range(count) if i ^ bit...  17.3 us
    ppermute x16, starting transfers between devices, flipped(): lax.ppermute(block, axis, [(i, i ^ bit) for i in range(count) if i ^ bit...  16 us
    unnamed x35, local copies, waits for them, and re-layouts  14.5 us
    pallas_call x2, Pallas kernels, input_grad(): pl.pallas_call(body, out_shape=jax.ShapeDtypeStruct((total, out_cols), BF...  6.36 us
    pallas_call x9, Pallas kernels, small(): pl.pallas_call(body, out_shape=tuple((jax.ShapeDtypeStruct(s, d) for s, d...  5.15 us
  transfers between devices with their start and end apart: 16, of which 8 were waited for; matrix products, arithmetic and copies ran while one was open for 0% of the time, Pallas kernels for 38%

profile of v1, /device:TPU:0, one launch (start us, length us, event | category | flops | bytes accessed | tf_op | source)
XLA Modules:
  0.0 103.8 jit_solution(3452053258554913212)
XLA Ops:
  0.6 0.0 copy-start.5
  0.6 1.0 copy-done.5
  1.6 1.0 copy-done.7
  2.6 0.7 copy-done.11
  3.3 0.7 copy-done.13
  3.9 0.6 shard_map.120.own_ref.l2_own
  4.5 0.5 collective-permute-start
  5.0 1.2 %collective-permute-done.far_ref.l2_far = bf16[2,128,512]{2,1,0:T(8,128)(2,1)S(1)} collective-permute-done((bf16[2,128,512]{2,1,0:T(8,128)(2,1)S(1)}, bf16[2,128,512]{2,1,0:T(8,128)(2,1)S(1)}, u32[]{:S(2)}, u32[]{:S(2)}) %collective-permute-start) | collective-permute-done | bytes 262176 | tf_op jit(solution)/shard_map/ppermute | solution.py:338
  6.2 0.6 shard_map.121.near_ref.chip_ref
  6.8 3.0 %collective-permute-start.1 = (bf16[128,512]{1,0:T(8,128)(2,1)S(1)}, bf16[128,512]{1,0:T(8,128)(2,1)S(1)}, u32[]{:S(2)}, u32[]{:S(2)}) collective-permute-start(bf16[128,512]{1,0:T(8,128)(2,1)S(1)} %shard_map.121.near_ref.chip_ref), channel_id=1, source_target_pairs={{0,4},{4,0},{8,12},{12,8},{1,5},{5,1},{9,13},{13,9},{2,6},{6,2},{1... | collective-permute-start | bytes 393224 | tf_op jit(solution)/shard_map/ppermute | solution.py:338
  9.8 3.8 %collective-permute-done.1.far_ref.pair_far = bf16[128,512]{1,0:T(8,128)(2,1)S(1)} collective-permute-done((bf16[128,512]{1,0:T(8,128)(2,1)S(1)}, bf16[128,512]{1,0:T(8,128)(2,1)S(1)}, u32[]{:S(2)}, u32[]{:S(2)}) %collective-permute-start.1) | collective-permute-done | bytes 131104 | tf_op jit(solution)/shard_map/ppermute | solution.py:338
  13.6 0.6 shard_map.122.pair_ref
  14.2 2.8 %collective-permute-start.2 = (bf16[128,512]{1,0:T(8,128)(2,1)S(1)}, bf16[128,512]{1,0:T(8,128)(2,1)S(1)}, u32[]{:S(2)}, u32[]{:S(2)}) collective-permute-start(bf16[128,512]{1,0:T(8,128)(2,1)S(1)} %shard_map.122.pair_ref), channel_id=1, source_target_pairs={{0,8},{4,12},{8,0},{12,4},{1,9},{5,13},{9,1},{13,5},{2,10},{6,14},... | collective-permute-start | bytes 393224 | tf_op jit(solution)/shard_map/ppermute | solution.py:338
  17.0 6.0 %collective-permute-done.2.half_far = bf16[128,512]{1,0:T(8,128)(2,1)S(1)} collective-permute-done((bf16[128,512]{1,0:T(8,128)(2,1)S(1)}, bf16[128,512]{1,0:T(8,128)(2,1)S(1)}, u32[]{:S(2)}, u32[]{:S(2)}) %collective-permute-start.2) | collective-permute-done | bytes 131104 | tf_op jit(solution)/shard_map/ppermute | solution.py:338
  23.0 0.6 shard_map.123.mine
  23.6 0.1 collective-permute-start.3
  23.6 0.0 copy-start.1
  23.6 1.9 %copy-done.1 = bf16[384,4096]{1,0:T(8,128)(2,1)S(1)} copy-done((bf16[384,4096]{1,0:T(8,128)(2,1)S(1)}, bf16[384,4096]{1,0:T(8,128)(2,1)}, u32[]{:S(2)}) %copy-start.1) | copy-done | bytes 3145752
  25.5 1.9 %copy-done.3 = bf16[384,4096]{1,0:T(8,128)(2,1)S(1)} copy-done((bf16[384,4096]{1,0:T(8,128)(2,1)S(1)}, bf16[384,4096]{1,0:T(8,128)(2,1)}, u32[]{:S(2)}) %copy-start.3) | copy-done | bytes 3145752
  27.4 1.0 copy-done.6
  28.4 1.0 copy-done.8
  29.4 0.8 copy-done.9
  30.2 0.8 copy-done.10
  31.0 0.7 copy-done.12
  31.7 0.7 copy-done.14
  32.3 10.8 %shard_map.124 = (f32[384,2048]{1,0:T(8,128)S(1)}, bf16[384,512]{1,0:T(8,128)(2,1)}, bf16[384,512]{1,0:T(8,128)(2,1)}, bf16[256,256]{1,0:T(8,128)(2,1)S(1)}, f32...) custom-call(s32[5]{0:T(128)S(1)} %bitcast.9, s32[3]{0:T(128)S(1)} %bitcast.24, bf16[384,4096]{1,0:T(8,128)(2,1)S(1)} %copy-done.1, ...), custom_call_target="tpu_custom_call" | custom-call | flops 2684354560 | bytes 6291456 | tf_op jit(solution)/shard_map/pallas_call | solution.py:215
  43.1 10.8 %shard_map.125 = (f32[384,2048]{1,0:T(8,128)S(1)}, bf16[384,512]{1,0:T(8,128)(2,1)}, bf16[384,512]{1,0:T(8,128)(2,1)}, bf16[256,256]{1,0:T(8,128)(2,1)S(1)}, f32...) custom-call(s32[5]{0:T(128)S(1)} %bitcast.10, ...), custom_call_target="tpu_custom_call", output_to_operand_aliasing={{1}: (10, {}), {2}: (11, {})} | custom-call | flops 2684354560 | bytes 6291456 | tf_op jit(solution)/shard_map/pallas_call | solution.py:215
  53.9 0.0 collective-permute-done.3.far
  53.9 10.0 %shard_map.126 = (bf16[384,4096]{1,0:T(8,128)(2,1)}, f32[2,128,256]{2,1,0:T(8,128)S(1)}, bf16[2,128,256]{2,1,0:T(8,128)(2,1)S(1)}) custom-call(s32[5]{0:T(128)S(1)} %bitcast.11, s32[3]{0:T(128)S(1)} %bitcast.26, bf16[384,4096]{1,0:T(8,128)(2,1)S(1)} %copy-done.2, bf16[384,4096]{1,0:T(8,128)(2,1)S(1)} %copy-done.4, f32[32,384]{1,0:T(8,128)S(1)} %copy-done.9, ...), custom_call_target="tpu_custom_call" | custom-call | flops 2013265920 | bytes 6291456 | tf_op jit(solution)/shard_map/pallas_call | solution.py:268
  63.9 0.5 collective-permute-start.5
  64.4 10.3 %shard_map.127 = (bf16[384,4096]{1,0:T(8,128)(2,1)}, f32[2,128,256]{2,1,0:T(8,128)S(1)}, bf16[2,128,256]{2,1,0:T(8,128)(2,1)S(1)}) custom-call(s32[5]{0:T(128)S(1)} %bitcast.12, s32[3]{0:T(128)S(1)} %bitcast.27, bf16[384,4096]{1,0:T(8,128)(2,1)S(1)} %copy-done.2, bf16[384,4096]{1,0:T(8,128)(2,1)S(1)} %copy-done.4, ...), custom_call_target="tpu_custom_call", output_to_operand_aliasing={{0}: (9, {})} | custom-call | flops 2013265920 | bytes 6291456 | tf_op jit(solution)/shard_map/pallas_call | solution.py:268
  74.7 0.0 collective-permute-start.10
  74.7 0.0 collective-permute-done.5.away
  74.7 0.6 shard_map.128
  75.3 0.6 collective-permute-start.6
  75.9 0.1 collective-permute-done.10.away
  76.0 0.6 shard_map.131
  76.6 1.4 %collective-permute-start.11 = (bf16[2,128,256]{2,1,0:T(8,128)(2,1)S(1)}, bf16[2,128,256]{2,1,0:T(8,128)(2,1)S(1)}, u32[]{:S(2)}, u32[]{:S(2)}) collective-permute-start(bf16[2,128,256]{2,1,0:T(8,128)(2,1)S(1)} %get-tuple-element.52), channel_id=1, source_target_pairs={{0,4},{4,0},{8,12},{12,8},{1,5},{5,1},{9,13},{13,9},{2,6},{6,2},{1... | collective-permute-start | bytes 393224 | tf_op jit(solution)/shard_map/ppermute | solution.py:338
  78.0 1.4 %collective-permute-start.15 = (bf16[256,512]{1,0:T(8,128)(2,1)S(1)}, bf16[256,512]{1,0:T(8,128)(2,1)S(1)}, u32[]{:S(2)}, u32[]{:S(2)}) collective-permute-start(bf16[256,512]{1,0:T(8,128)(2,1)S(1)} %constant_dynamic-update-slice_fusion.refs_0_), channel_id=1, source_target_pairs={{0,2},{2,0},{1,3},{3,1},{4,6},{6,4},{5,7},{7,5},{8,10},{10,8},{9,1... | collective-permute-start | bytes 786440 | tf_op jit(solution)/shard_map/ppermute | solution.py:338
  79.4 0.0 collective-permute-start.4
  79.4 2.2 %collective-permute-done.6.away = bf16[2,128,256]{2,1,0:T(8,128)(2,1)S(1)} collective-permute-done((bf16[2,128,256]{2,1,0:T(8,128)(2,1)S(1)}, bf16[2,128,256]{2,1,0:T(8,128)(2,1)S(1)}, u32[]{:S(2)}, u32[]{:S(2)}) %collective-permute-start.6) | collective-permute-done | bytes 131104 | tf_op jit(solution)/shard_map/ppermute | solution.py:338
  81.6 0.6 shard_map.129
  82.2 2.0 %collective-permute-start.7 = (bf16[128,256]{1,0:T(8,128)(2,1)S(1)}, bf16[128,256]{1,0:T(8,128)(2,1)S(1)}, u32[]{:S(2)}, u32[]{:S(2)}) collective-permute-start(bf16[128,256]{1,0:T(8,128)(2,1)S(1)} %get-tuple-element.46), channel_id=1, source_target_pairs={{0,8},{4,12},{8,0},{12,4},{1,9},{5,13},{9,1},{13,5},{2,10},{6,14},... | collective-permute-start | bytes 196616 | tf_op jit(solution)/shard_map/ppermute | solution.py:338
  84.2 0.0 collective-permute-done.11.away
  84.2 0.6 shard_map.132
  84.8 2.0 %collective-permute-start.12 = (bf16[128,256]{1,0:T(8,128)(2,1)S(1)}, bf16[128,256]{1,0:T(8,128)(2,1)S(1)}, u32[]{:S(2)}, u32[]{:S(2)}) collective-permute-start(bf16[128,256]{1,0:T(8,128)(2,1)S(1)} %get-tuple-element.54), channel_id=1, source_target_pairs={{0,8},{4,12},{8,0},{12,4},{1,9},{5,13},{9,1},{13,5},{2,10},{6,14},... | collective-permute-start | bytes 196616 | tf_op jit(solution)/shard_map/ppermute | solution.py:338
  86.8 0.0 collective-permute-start.9
  86.8 1.5 %collective-permute-done.7.away = bf16[128,256]{1,0:T(8,128)(2,1)S(1)} collective-permute-done((bf16[128,256]{1,0:T(8,128)(2,1)S(1)}, bf16[128,256]{1,0:T(8,128)(2,1)S(1)}, u32[]{:S(2)}, u32[]{:S(2)}) %collective-permute-start.7) | collective-permute-done | bytes 65568 | tf_op jit(solution)/shard_map/ppermute | solution.py:338
  88.3 0.6 shard_map.130.refs_2_
  88.9 0.1 collective-permute-start.8
  89.0 1.3 %collective-permute-done.12.away = bf16[128,256]{1,0:T(8,128)(2,1)S(1)} collective-permute-done((bf16[128,256]{1,0:T(8,128)(2,1)S(1)}, bf16[128,256]{1,0:T(8,128)(2,1)S(1)}, u32[]{:S(2)}, u32[]{:S(2)}) %collective-permute-start.12) | collective-permute-done | bytes 65568 | tf_op jit(solution)/shard_map/ppermute | solution.py:338
  90.3 0.6 shard_map.133.refs_6_
  90.8 0.1 collective-permute-start.13
  90.9 0.0 collective-permute-done.4.refs_1_
  90.9 0.0 collective-permute-done.9.refs_5_
  90.9 0.0 collective-permute-done.8.refs_3_
  90.9 1.2 %collective-permute-done.13.refs_7_ = bf16[128,256]{1,0:T(8,128)(2,1)S(1)} collective-permute-done((bf16[128,256]{1,0:T(8,128)(2,1)S(1)}, bf16[128,256]{1,0:T(8,128)(2,1)S(1)}, u32[]{:S(2)}, u32[]{:S(2)}) %collective-permute-start.13) | collective-permute-done | bytes 65568 | tf_op jit(solution)/shard_map/ppermute | solution.py:338
  92.2 1.3 %shard_map.134 = (bf16[384,512]{1,0:T(8,128)(2,1)}, bf16[384,512]{1,0:T(8,128)(2,1)}, bf16[128,512]{1,0:T(8,128)(2,1)S(1)}) custom-call(s32[5]{0:T(128)S(1)} %bitcast.19, s32[3]{0:T(128)S(1)} %bitcast.34, f32[2,128,256]{2,1,0:T(8,128)S(1)} %get-tuple-element.39.refs_0_, ...), custom_call_target="tpu_custom_call", output_to_operand_aliasing={{0}: (10, {}), {1}: (11, {})} | custom-call | tf_op jit(solution)/shard_map/pallas_call | solution.py:438
  93.5 1.4 %collective-permute-start.14 = (bf16[128,512]{1,0:T(8,128)(2,1)S(1)}, bf16[128,512]{1,0:T(8,128)(2,1)S(1)}, u32[]{:S(2)}, u32[]{:S(2)}) collective-permute-start(bf16[128,512]{1,0:T(8,128)(2,1)S(1)} %get-tuple-element.59.refs_0_), channel_id=1, source_target_pairs={{0,2},{2,0},{1,3},{3,1},{4,6},{6,4},{5,7},{7,5},{8,10},{10,8},{9,1... | collective-permute-start | bytes 393224 | tf_op jit(solution)/shard_map/ppermute | solution.py:338
  94.9 0.0 collective-permute-done.15.refs_1_
  94.9 2.5 %copy-done = bf16[2560,1024]{1,0:T(8,128)(2,1)S(1)} copy-done((bf16[2560,1024]{1,0:T(8,128)(2,1)S(1)}, bf16[2560,1024]{1,0:T(8,128)(2,1)}, u32[]{:S(2)}) %copy-start) | copy-done | bytes 5242904
  97.4 3.4 %shard_map.135.refs_3_ = bf16[384,2560]{1,0:T(8,128)(2,1)} custom-call(s32[1]{0:T(128)} %bitcast.2.flag, bf16[256,512]{1,0:T(8,128)(2,1)S(1)} %constant_dynamic-update-slice_fusion.refs_0_, bf16[256,512]{1,0:T(8,128)(2,1)S(1)} %collective-permute-done.15.refs_1_, bf16[2560,1024]{1,0:T(8,128)(2,1)S(1)} %copy-done), custom_call_target="tpu_custom_call" | custom-call | flops 1342177280 | bytes 6553600 | tf_op jit(solution)/shard_map/pallas_call | solution.py:317
  100.8 0.0 collective-permute-done.14.refs_1_
  100.8 3.0 %shard_map.136 = bf16[384,2560]{1,0:T(8,128)(2,1)} custom-call(s32[1]{0:T(128)} %bitcast.2.flag, bf16[128,512]{1,0:T(8,128)(2,1)S(1)} %get-tuple-element.59.refs_0_, bf16[128,512]{1,0:T(8,128)(2,1)S(1)} %collective-permute-done.14.refs_1_, bf16[2560,1024]{1,0:T(8,128)(2,1)S(1)} %bitcast.4, ...), custom_call_target="tpu_custom_call", output_to_operand_aliasing={{}: (4, {})} | custom-call | flops 671088640 | bytes 5898240 | tf_op jit(solution)/shard_map/pallas_call | solution.py:317
  (22 shorter events, 0.1 us)
Async XLA Ops:
  0.6 1.0 copy-start.5
  1.6 1.0 copy-start.7
  2.6 0.7 copy-start.11
  3.3 0.7 copy-start.13
  4.5 1.7 %collective-permute-start = (bf16[2,128,512]{2,1,0:T(8,128)(2,1)S(1)}, bf16[2,128,512]{2,1,0:T(8,128)(2,1)S(1)}, u32[]{:S(2)}, u32[]{:S(2)}) collective-permute-start(bf16[2,128,512]{2,1,0:T(8,128)(2,1)S(1)} %shard_map.120.own_ref.l2_own), channel_id=1, source_target_pairs={{0,1},{1,0},{2,3},{3,2},{4,5},{5,4},{6,7},{7,6},{8,9},{9,8},{10,11... | collective-permute-start | bytes 786440 | tf_op jit(solution)/shard_map/ppermute | solution.py:338
  6.8 6.8 %collective-permute-start.1 = (bf16[128,512]{1,0:T(8,128)(2,1)S(1)}, bf16[128,512]{1,0:T(8,128)(2,1)S(1)}, u32[]{:S(2)}, u32[]{:S(2)}) collective-permute-start(bf16[128,512]{1,0:T(8,128)(2,1)S(1)} %shard_map.121.near_ref.chip_ref), channel_id=1, source_target_pairs={{0,4},{4,0},{8,12},{12,8},{1,5},{5,1},{9,13},{13,9},{2,6},{6,2},{1... | collective-permute-start | bytes 393224 | tf_op jit(solution)/shard_map/ppermute | solution.py:338
  14.2 8.8 %collective-permute-start.2 = (bf16[128,512]{1,0:T(8,128)(2,1)S(1)}, bf16[128,512]{1,0:T(8,128)(2,1)S(1)}, u32[]{:S(2)}, u32[]{:S(2)}) collective-permute-start(bf16[128,512]{1,0:T(8,128)(2,1)S(1)} %shard_map.122.pair_ref), channel_id=1, source_target_pairs={{0,8},{4,12},{8,0},{12,4},{1,9},{5,13},{9,1},{13,5},{2,10},{6,14},... | collective-permute-start | bytes 393224 | tf_op jit(solution)/shard_map/ppermute | solution.py:338
  23.6 30.3 %collective-permute-start.3 = (bf16[2,128,512]{2,1,0:T(8,128)(2,1)S(1)}, bf16[2,128,512]{2,1,0:T(8,128)(2,1)S(1)}, u32[]{:S(2)}, u32[]{:S(2)}) collective-permute-start(bf16[2,128,512]{2,1,0:T(8,128)(2,1)S(1)} %shard_map.123.mine), channel_id=1, source_target_pairs={{0,1},{1,0},{2,3},{3,2},{4,5},{5,4},{6,7},{7,6},{8,9},{9,8},{10,11... | collective-permute-start | bytes 786440 | tf_op jit(solution)/shard_map/ppermute | solution.py:338
  23.6 1.9 %copy-start.1 = (bf16[384,4096]{1,0:T(8,128)(2,1)S(1)}, bf16[384,4096]{1,0:T(8,128)(2,1)}, u32[]{:S(2)}) copy-start(bf16[384,4096]{1,0:T(8,128)(2,1)} %q.7) | copy-start | bytes 9437188
  25.5 1.9 %copy-start.3 = (bf16[384,4096]{1,0:T(8,128)(2,1)S(1)}, bf16[384,4096]{1,0:T(8,128)(2,1)}, u32[]{:S(2)}) copy-start(bf16[384,4096]{1,0:T(8,128)(2,1)} %g.7) | copy-start | bytes 9437188
  27.4 1.0 copy-start.6
  28.4 1.0 copy-start.8
  29.4 0.8 copy-start.9
  30.2 0.8 copy-start.10
  31.0 0.7 copy-start.12
  31.7 0.7 copy-start.14
  43.1 10.8 %copy-start.2 = (bf16[384,4096]{1,0:T(8,128)(2,1)S(1)}, bf16[384,4096]{1,0:T(8,128)(2,1)}, u32[]{:S(2)}) copy-start(bf16[384,4096]{1,0:T(8,128)(2,1)} %q.7) | copy-start | bytes 9437188
  43.1 10.8 %copy-start.4 = (bf16[384,4096]{1,0:T(8,128)(2,1)S(1)}, bf16[384,4096]{1,0:T(8,128)(2,1)}, u32[]{:S(2)}) copy-start(bf16[384,4096]{1,0:T(8,128)(2,1)} %g.7) | copy-start | bytes 9437188
  63.9 10.8 %collective-permute-start.5 = (bf16[2,128,256]{2,1,0:T(8,128)(2,1)S(1)}, bf16[2,128,256]{2,1,0:T(8,128)(2,1)S(1)}, u32[]{:S(2)}, u32[]{:S(2)}) collective-permute-start(bf16[2,128,256]{2,1,0:T(8,128)(2,1)S(1)} %get-tuple-element.42), channel_id=1, source_target_pairs={{0,1},{1,0},{2,3},{3,2},{4,5},{5,4},{6,7},{7,6},{8,9},{9,8},{10,11... | collective-permute-start | bytes 393224 | tf_op jit(solution)/shard_map/ppermute | solution.py:338
  74.7 1.3 %collective-permute-start.10 = (bf16[2,128,256]{2,1,0:T(8,128)(2,1)S(1)}, bf16[2,128,256]{2,1,0:T(8,128)(2,1)S(1)}, u32[]{:S(2)}, u32[]{:S(2)}) collective-permute-start(bf16[2,128,256]{2,1,0:T(8,128)(2,1)S(1)} %get-tuple-element.50), channel_id=1, source_target_pairs={{0,1},{1,0},{2,3},{3,2},{4,5},{5,4},{6,7},{7,6},{8,9},{9,8},{10,11... | collective-permute-start | bytes 393224 | tf_op jit(solution)/shard_map/ppermute | solution.py:338
  75.3 6.4 %collective-permute-start.6 = (bf16[2,128,256]{2,1,0:T(8,128)(2,1)S(1)}, bf16[2,128,256]{2,1,0:T(8,128)(2,1)S(1)}, u32[]{:S(2)}, u32[]{:S(2)}) collective-permute-start(bf16[2,128,256]{2,1,0:T(8,128)(2,1)S(1)} %get-tuple-element.44), channel_id=1, source_target_pairs={{0,4},{4,0},{8,12},{12,8},{1,5},{5,1},{9,13},{13,9},{2,6},{6,2},{1... | collective-permute-start | bytes 393224 | tf_op jit(solution)/shard_map/ppermute | solution.py:338
  76.6 7.6 %collective-permute-start.11 = (bf16[2,128,256]{2,1,0:T(8,128)(2,1)S(1)}, bf16[2,128,256]{2,1,0:T(8,128)(2,1)S(1)}, u32[]{:S(2)}, u32[]{:S(2)}) collective-permute-start(bf16[2,128,256]{2,1,0:T(8,128)(2,1)S(1)} %get-tuple-element.52), channel_id=1, source_target_pairs={{0,4},{4,0},{8,12},{12,8},{1,5},{5,1},{9,13},{13,9},{2,6},{6,2},{1... | collective-permute-start | bytes 393224 | tf_op jit(solution)/shard_map/ppermute | solution.py:338
  78.0 16.9 %collective-permute-start.15 = (bf16[256,512]{1,0:T(8,128)(2,1)S(1)}, bf16[256,512]{1,0:T(8,128)(2,1)S(1)}, u32[]{:S(2)}, u32[]{:S(2)}) collective-permute-start(bf16[256,512]{1,0:T(8,128)(2,1)S(1)} %constant_dynamic-update-slice_fusion.refs_0_), channel_id=1, source_target_pairs={{0,2},{2,0},{1,3},{3,1},{4,6},{6,4},{5,7},{7,5},{8,10},{10,8},{9,1... | collective-permute-start | bytes 786440 | tf_op jit(solution)/shard_map/ppermute | solution.py:338
  79.4 11.5 %collective-permute-start.4 = (bf16[2,128,256]{2,1,0:T(8,128)(2,1)S(1)}, bf16[2,128,256]{2,1,0:T(8,128)(2,1)S(1)}, u32[]{:S(2)}, u32[]{:S(2)}) collective-permute-start(bf16[2,128,256]{2,1,0:T(8,128)(2,1)S(1)} %get-tuple-element.40), channel_id=1, source_target_pairs={{0,1},{1,0},{2,3},{3,2},{4,5},{5,4},{6,7},{7,6},{8,9},{9,8},{10,11... | collective-permute-start | bytes 393224 | tf_op jit(solution)/shard_map/ppermute | solution.py:338
  82.2 6.1 %collective-permute-start.7 = (bf16[128,256]{1,0:T(8,128)(2,1)S(1)}, bf16[128,256]{1,0:T(8,128)(2,1)S(1)}, u32[]{:S(2)}, u32[]{:S(2)}) collective-permute-start(bf16[128,256]{1,0:T(8,128)(2,1)S(1)} %get-tuple-element.46), channel_id=1, source_target_pairs={{0,8},{4,12},{8,0},{12,4},{1,9},{5,13},{9,1},{13,5},{2,10},{6,14},... | collective-permute-start | bytes 196616 | tf_op jit(solution)/shard_map/ppermute | solution.py:338
  84.8 5.4 %collective-permute-start.12 = (bf16[128,256]{1,0:T(8,128)(2,1)S(1)}, bf16[128,256]{1,0:T(8,128)(2,1)S(1)}, u32[]{:S(2)}, u32[]{:S(2)}) collective-permute-start(bf16[128,256]{1,0:T(8,128)(2,1)S(1)} %get-tuple-element.54), channel_id=1, source_target_pairs={{0,8},{4,12},{8,0},{12,4},{1,9},{5,13},{9,1},{13,5},{2,10},{6,14},... | collective-permute-start | bytes 196616 | tf_op jit(solution)/shard_map/ppermute | solution.py:338
  86.8 4.1 %collective-permute-start.9 = (bf16[2,128,256]{2,1,0:T(8,128)(2,1)S(1)}, bf16[2,128,256]{2,1,0:T(8,128)(2,1)S(1)}, u32[]{:S(2)}, u32[]{:S(2)}) collective-permute-start(bf16[2,128,256]{2,1,0:T(8,128)(2,1)S(1)} %get-tuple-element.48), channel_id=1, source_target_pairs={{0,1},{1,0},{2,3},{3,2},{4,5},{5,4},{6,7},{7,6},{8,9},{9,8},{10,11... | collective-permute-start | bytes 393224 | tf_op jit(solution)/shard_map/ppermute | solution.py:338
  88.3 12.4 %slice-start = ((s8[5242880]{0:T(1024)(128)(4,1)}), s8[1048576]{0:T(1024)(128)(4,1)S(1)}, s32[]{:S(2)}) async-start(s8[5242880]{0:T(1024)(128)(4,1)} %bitcast.3), calls=%async_computation | async-start | bytes 2097152
  88.9 2.0 %collective-permute-start.8 = (bf16[128,256]{1,0:T(8,128)(2,1)S(1)}, bf16[128,256]{1,0:T(8,128)(2,1)S(1)}, u32[]{:S(2)}, u32[]{:S(2)}) collective-permute-start(bf16[128,256]{1,0:T(8,128)(2,1)S(1)} %shard_map.130.refs_2_), channel_id=1, source_target_pairs={{0,1},{1,0},{2,3},{3,2},{4,5},{5,4},{6,7},{7,6},{8,9},{9,8},{10,11... | collective-permute-start | bytes 196616 | tf_op jit(solution)/shard_map/ppermute | solution.py:338
  90.8 1.3 %collective-permute-start.13 = (bf16[128,256]{1,0:T(8,128)(2,1)S(1)}, bf16[128,256]{1,0:T(8,128)(2,1)S(1)}, u32[]{:S(2)}, u32[]{:S(2)}) collective-permute-start(bf16[128,256]{1,0:T(8,128)(2,1)S(1)} %shard_map.133.refs_6_), channel_id=1, source_target_pairs={{0,1},{1,0},{2,3},{3,2},{4,5},{5,4},{6,7},{7,6},{8,9},{9,8},{10,11... | collective-permute-start | bytes 196616 | tf_op jit(solution)/shard_map/ppermute | solution.py:338
  93.5 7.3 %collective-permute-start.14 = (bf16[128,512]{1,0:T(8,128)(2,1)S(1)}, bf16[128,512]{1,0:T(8,128)(2,1)S(1)}, u32[]{:S(2)}, u32[]{:S(2)}) collective-permute-start(bf16[128,512]{1,0:T(8,128)(2,1)S(1)} %get-tuple-element.59.refs_0_), channel_id=1, source_target_pairs={{0,2},{2,0},{1,3},{3,1},{4,6},{6,4},{5,7},{7,5},{8,10},{10,8},{9,1... | collective-permute-start | bytes 393224 | tf_op jit(solution)/shard_map/ppermute | solution.py:338
  94.9 2.5 %copy-start = (bf16[2560,1024]{1,0:T(8,128)(2,1)S(1)}, bf16[2560,1024]{1,0:T(8,128)(2,1)}, u32[]{:S(2)}) copy-start(bf16[2560,1024]{1,0:T(8,128)(2,1)} %refs_2_.3) | copy-start | bytes 15728644
  97.4 3.4 %slice-start.1 = ((s8[5242880]{0:T(1024)(128)(4,1)}), s8[4194304]{0:T(1024)(128)(4,1)S(1)}, s32[]{:S(2)}) async-start(s8[5242880]{0:T(1024)(128)(4,1)} %bitcast.3), calls=%async_computation.1 | async-start | bytes 8388608

commit v2 on v1

v2 whole, which is shorter than its diff:
```python
import functools
import math

import jax
import jax.numpy as jnp
from jax import lax
from jax.experimental import pallas as pl
from jax.experimental.pallas import tpu as pltpu
from jax.sharding import PartitionSpec as P

HD = 128
PAGE = 128
SLOTS = 3
INNER = 3
LOG2E = math.log2(math.e)
SCALE = 1.0 / math.sqrt(HD)
BF16 = jnp.bfloat16
F32 = jnp.float32
I32 = jnp.int32
VMEM_LIMIT = 40 << 20
SMALL_LIMIT = 16 << 20


def params(limit=VMEM_LIMIT):
    return pltpu.CompilerParams(vmem_limit_bytes=limit)


def dot_t(left, right):
    return lax.dot_general(left, right, (((1,), (1,)), ((), ())), preferred_element_type=F32)


def dot_n(left, right):
    return lax.dot_general(left, right, (((1,), (0,)), ((), ())), preferred_element_type=F32)


def dot_rows(left, right):
    return lax.dot_general(left, right, (((0,), (0,)), ((), ())), preferred_element_type=F32)


class Path:
    def __init__(self, ids_ref):
        self.pages = [ids_ref[j] for j in range(INNER)]
        self.own = ids_ref[INNER] - 1
        self.leaf = self.own // SLOTS
        self.core = lax.rem(self.leaf, 2)
        self.owns = [self.pages[j] == self.own for j in range(INNER)]
        self.has_inner = self.owns[0] | self.owns[1] | self.owns[2]

    def owner(self, level):
        return self.pages[level] // SLOTS

    def same(self, level, shift):
        return (self.owner(level) >> shift) == (self.leaf >> shift)


def row_ok(count, rows, width):
    return lax.broadcasted_iota(I32, (rows, width), 0) < count


def whole(shape):
    return pl.BlockSpec(shape, lambda *_: (0,) * len(shape))


def small(body, ids, counts, arrays, outs, after=()):
    taken = 2 + len(arrays)

    def kernel(*refs):
        body(*refs[:taken], *refs[taken + len(after) :])

    return pl.pallas_call(
        kernel,
        out_shape=tuple(jax.ShapeDtypeStruct(s, d) for s, d in outs),
        grid_spec=pltpu.PrefetchScalarGridSpec(
            num_scalar_prefetch=2,
            grid=(1,),
            in_specs=[whole(a.shape) for a in arrays]
            + [pl.BlockSpec(memory_space=pl.ANY)] * len(after),
            out_specs=tuple(whole(s) for s, _ in outs),
        ),
        compiler_params=params(SMALL_LIMIT),
    )(ids, counts, *arrays, *after)


def turned(keys, queries, values, grads, norm, delta, keep):
    p = jnp.exp2(dot_t(keys, queries) * (SCALE * LOG2E) - norm)
    if keep is not None:
        p = jnp.where(keep, p, 0.0)
    ds = p * (dot_t(values, grads) - delta)
    return p.astype(BF16), ds.astype(BF16)


def stacked(ref, rows, pair):
    return jnp.concatenate([ref[rows, h * HD : (h + 1) * HD] for h in pair], axis=0)


def prepare_rows(path, counts, norms, deltas, norm_s, delta_s):
    steps, heads, _ = norm_s.shape
    lane = lax.broadcasted_iota(I32, norms.shape, 1)
    n0 = jnp.where(path.has_inner, counts[0], 0)
    slot, pos = lane // PAGE, lane % PAGE
    limit = jnp.where(slot == 0, n0, jnp.where(slot == 1, counts[1], counts[2]))
    norm = jnp.where(pos < limit, norms[...] * LOG2E, 1e30)
    for s in range(steps):
        norm_s[s] = norm[s * heads : (s + 1) * heads]
        delta_s[s] = deltas[s * heads : (s + 1) * heads]


def finish_queries(dq, prev, rows, heads, parts):
    size = rows.stop - rows.start
    for n, h in enumerate(heads):
        part = parts[:, n * size : (n + 1) * size]
        down = slice(h * HD, (h + 1) * HD)
        if prev is not None:
            part = part + prev[down, rows]
        if dq.dtype == F32:
            dq[down, rows] = part
        else:
            dq[rows, down] = (part.T * SCALE).astype(BF16)


def own_pages_kernel(heads, second, ids, counts, q, g, k, v, norms, deltas, l2_own, l2_far, *refs):
    prev = refs[0] if second else None
    dq, dk, dv, dv12, own0, send2 = refs[-14:-8]
    k0_s, v0_s, k3_s, v3_s, turn_s, acc, norm_s, delta_s = refs[-8:]
    path = Path(ids)
    mine = path.owns[2]
    step = pl.program_id(1)

    @pl.when(step == 0)
    def _start():
        n0 = jnp.where(path.has_inner, counts[0], 0)
        zero = jnp.zeros((), BF16)
        for slot, n in enumerate((n0, counts[1], counts[2])):
            rows = slice(slot * PAGE, (slot + 1) * PAGE)
            ok = row_ok(n, PAGE, HD)
            kk = jnp.where(ok, k[rows], zero)
            vv = jnp.where(ok, v[rows], zero)
            if slot == 0:
                k0_s[...] = kk
                v0_s[...] = vv
                turn_s[:, 3 * PAGE :] = kk.T
            else:
                at = slice((slot - 1) * PAGE, slot * PAGE)
                k3_s[at] = kk
                v3_s[at] = vv
                turn_s[:, at] = kk.T
        k2 = jnp.where(mine, l2_own[0], l2_far[0])
        k3_s[2 * PAGE :] = k2
        v3_s[2 * PAGE :] = jnp.where(mine, l2_own[1], l2_far[1])
        turn_s[:, 2 * PAGE : 3 * PAGE] = k2.T
        acc[...] = jnp.zeros_like(acc)
        prepare_rows(path, counts, norms, deltas, norm_s, delta_s)

    key = lax.broadcasted_iota(I32, (PAGE, 2 * PAGE), 0)
    row = lax.broadcasted_iota(I32, (PAGE, 2 * PAGE), 1)
    keep0 = key <= row % PAGE
    key = lax.broadcasted_iota(I32, (3 * PAGE, 4 * PAGE), 0)
    row = lax.broadcasted_iota(I32, (3 * PAGE, 4 * PAGE), 1) % (2 * PAGE)
    keep3 = (key <= row) | (key >= 2 * PAGE)
    top, rest = slice(0, PAGE), slice(PAGE, 3 * PAGE)
    for first in range(0, heads, 2):
        pair = (first, first + 1)

        def vectors(ref, rows):
            return jnp.concatenate(
                [ref[step, h : h + 1, rows] for h in pair], axis=1
            )

        for rows, keep, ks, vs, kt, at in (
            (top, keep0, k0_s, v0_s, slice(3 * PAGE, 4 * PAGE), slice(0, PAGE)),
            (rest, keep3, k3_s, v3_s, slice(0, 3 * PAGE), slice(PAGE, 4 * PAGE)),
        ):
            qq, gg = stacked(q, rows, pair), stacked(g, rows, pair)
            p, ds = turned(
                ks[...], qq, vs[...], gg, vectors(norm_s, rows), vectors(delta_s, rows), keep
            )
            acc[0, at] += dot_n(ds, qq)
            acc[1, at] += dot_n(p, gg)
            finish_queries(dq, prev, rows, pair, dot_n(turn_s[:, kt], ds))

    @pl.when(step == pl.num_programs(1) - 1)
    def _end():
        dk[:PAGE] = jnp.zeros((PAGE, HD), BF16)
        dv[:PAGE] = jnp.zeros((PAGE, HD), BF16)
        for slot in (1, 2):
            ok = row_ok(counts[slot], PAGE, HD)
            rows = slice(slot * PAGE, (slot + 1) * PAGE)
            dk[rows] = jnp.where(ok, acc[0, rows] * SCALE, 0.0).astype(BF16)
            low = jnp.where(ok, acc[1, rows], 0.0).astype(BF16)
            dv[rows] = low
            dv12[(slot - 1) * PAGE : slot * PAGE] = low
        k2, v2 = acc[0, 3 * PAGE :] * SCALE, acc[1, 3 * PAGE :]
        own0[0] = acc[0, :PAGE] * SCALE + jnp.where(mine, k2, 0.0)
        own0[1] = acc[1, :PAGE] + jnp.where(mine, v2, 0.0)
        send2[0] = k2.astype(BF16)
        send2[1] = v2.astype(BF16)


def shared_pages_kernel(heads, second, ids, counts, q, g, norms, deltas, mine, far, *refs):
    prev = refs[0] if second else None
    dq, keep_out, send_out = refs[-9:-6]
    k_s, v_s, turn_s, acc, norm_s, delta_s = refs[-6:]
    path = Path(ids)
    leads = path.core == 0
    step = pl.program_id(1)

    @pl.when(step == 0)
    def _start():
        for j in range(2):
            at = slice(j * PAGE, (j + 1) * PAGE)
            near, away = mine[j], far[j]
            kk = jnp.where(leads, near, away)
            k_s[at] = kk
            turn_s[:, at] = kk.T
            v_s[at] = jnp.where(leads, away, near)
        acc[...] = jnp.zeros_like(acc)
        prepare_rows(path, counts, norms, deltas, norm_s, delta_s)

    limit = jnp.where(path.owns[2], 2 * PAGE, jnp.where(path.owns[1], PAGE, 0))
    key = lax.broadcasted_iota(I32, (2 * PAGE, 3 * PAGE), 0)
    row = lax.broadcasted_iota(I32, (2 * PAGE, 3 * PAGE), 1)
    keep = (key < limit) | (row >= PAGE)
    keep = jnp.concatenate([keep, keep], axis=1)
    rows = slice(0, 3 * PAGE)
    for first in range(0, heads, 2):
        pair = (first, first + 1)

        def vectors(ref):
            return jnp.concatenate([ref[step, h : h + 1, :] for h in pair], axis=1)

        qq, gg = stacked(q, rows, pair), stacked(g, rows, pair)
        p, ds = turned(k_s[...], qq, v_s[...], gg, vectors(norm_s), vectors(delta_s), keep)
        acc[0] += dot_n(ds, qq)
        acc[1] += dot_n(p, gg)
        finish_queries(dq, prev, rows, pair, dot_n(turn_s[...], ds))

    @pl.when(step == pl.num_programs(1) - 1)
    def _end():
        for j in range(2):
            at = slice(j * PAGE, (j + 1) * PAGE)
            grad_k, grad_v = acc[0, at] * SCALE, acc[1, at]
            keep_out[j] = jnp.where(leads, grad_k, grad_v)
            send_out[j] = jnp.where(leads, grad_v, grad_k).astype(BF16)


def cost(rows, keys, group):
    return pl.CostEstimate(
        flops=40 * rows * keys * HD * group,
        bytes_accessed=group * HD * SLOTS * PAGE * 8,
        transcendentals=rows * keys * group,
    )


def steps_of(group):
    return 2 if group % 4 == 0 else 1


def query_out(queries, group, kv, second, steps):
    rows = SLOTS * PAGE
    heads = group // steps
    if second:
        shape = jax.ShapeDtypeStruct(queries.shape, BF16)
        return shape, pl.BlockSpec((rows, heads * HD), lambda i, s, *_: (0, kv * steps + s))
    shape = jax.ShapeDtypeStruct((group * HD, rows), F32)
    return shape, pl.BlockSpec((heads * HD, rows), lambda i, s, *_: (s, 0))


def head_kernel(body, kv, group, ids, counts, q, g, rest, rest_specs, prev, queries, carries,
                outs, out_specs, scratch, estimate, after):
    rows = SLOTS * PAGE
    steps = steps_of(group)
    heads = group // steps
    second = prev is not None
    block = pl.BlockSpec((rows, heads * HD), lambda i, s, *_: (0, kv * steps + s))
    args = [q, g, *rest]
    in_specs = [block, block, *rest_specs]
    if second:
        args.append(prev)
        in_specs.append(pl.BlockSpec((heads * HD, rows), lambda i, s, *_: (s, 0)))
    aliases = {}
    for out, array in carries.items():
        if array is not None:
            aliases[2 + len(args)] = out
            args.append(array)
            in_specs.append(pl.BlockSpec(memory_space=pl.ANY))
    for array in after:
        args.append(array)
        in_specs.append(pl.BlockSpec(memory_space=pl.ANY))
    dq_shape, dq_spec = query_out(q, group, kv, second, steps)
    return pl.pallas_call(
        functools.partial(body, heads, second),
        out_shape=(dq_shape, *outs),
        grid_spec=pltpu.PrefetchScalarGridSpec(
            num_scalar_prefetch=2,
            grid=(1, steps),
            in_specs=in_specs,
            out_specs=(dq_spec, *out_specs),
            scratch_shapes=[
                *scratch,
                pltpu.VMEM((steps, heads, rows), F32),
                pltpu.VMEM((steps, heads, rows), F32),
            ],
        ),
        input_output_aliases=aliases,
        compiler_params=params(),
        cost_estimate=estimate,
    )(ids, counts, *args)


def own_pages(kv, group, ids, counts, q, g, k, v, norms, deltas, l2_own, l2_far, prev, grad_q,
              grad_kv, after):
    rows = SLOTS * PAGE
    col = lambda *_: (0, kv)
    page = pl.BlockSpec((2, PAGE, HD), lambda *_: (0, 0, kv))
    vec = pl.BlockSpec((group, rows), lambda *_: (kv, 0))
    one = pl.BlockSpec((rows, HD), col)
    full = jax.ShapeDtypeStruct(k.shape, BF16)
    return head_kernel(
        own_pages_kernel, kv, group, ids, counts, q, g,
        [k, v, norms, deltas, l2_own, l2_far], [one, one, vec, vec, page, page],
        prev, q, {0: grad_q, 1: grad_kv[0], 2: grad_kv[1]},
        (
            full,
            full,
            jax.ShapeDtypeStruct((2 * PAGE, HD), BF16),
            jax.ShapeDtypeStruct((2, PAGE, HD), F32),
            jax.ShapeDtypeStruct((2, PAGE, HD), BF16),
        ),
        (one, one, whole((2 * PAGE, HD)), whole((2, PAGE, HD)), whole((2, PAGE, HD))),
        [
            pltpu.VMEM((PAGE, HD), BF16),
            pltpu.VMEM((PAGE, HD), BF16),
            pltpu.VMEM((3 * PAGE, HD), BF16),
            pltpu.VMEM((3 * PAGE, HD), BF16),
            pltpu.VMEM((HD, 4 * PAGE), BF16),
            pltpu.VMEM((2, 4 * PAGE, HD), F32),
        ],
        cost(2 * PAGE, 4 * PAGE, group), after,
    )


def shared_pages(kv, group, ids, counts, q, g, norms, deltas, mine, far, prev, grad_q, after):
    rows = SLOTS * PAGE
    page = pl.BlockSpec((2, PAGE, HD), lambda *_: (0, 0, kv))
    vec = pl.BlockSpec((group, rows), lambda *_: (kv, 0))
    return head_kernel(
        shared_pages_kernel, kv, group, ids, counts, q, g,
        [norms, deltas, mine, far], [vec, vec, page, page],
        prev, q, {0: grad_q},
        (
            jax.ShapeDtypeStruct((2, PAGE, HD), F32),
            jax.ShapeDtypeStruct((2, PAGE, HD), BF16),
        ),
        (whole((2, PAGE, HD)), whole((2, PAGE, HD))),
        [
            pltpu.VMEM((2 * PAGE, HD), BF16),
            pltpu.VMEM((2 * PAGE, HD), BF16),
            pltpu.VMEM((HD, 2 * PAGE), BF16),
            pltpu.VMEM((2, 2 * PAGE, HD), F32),
        ],
        cost(3 * PAGE, 2 * PAGE, group), after,
    )


def input_grad(near, far, side, w, rows, carry):
    total = SLOTS * PAGE
    out_cols, depth = w.shape
    tile = next(t for t in (640, 512, 320, 128, out_cols) if out_cols % t == 0)
    lead = total - rows if carry is None else 0
    count = len(near)

    def body(flag, *refs):
        w_ref, out = refs[2 * count if far else count], refs[-1]
        mine = jnp.concatenate([r[...] for r in refs[:count]], axis=1)
        if far:
            other = jnp.concatenate([r[...] for r in refs[count : 2 * count]], axis=1)
            leads = flag[0] == 0
            half = depth // 2
            product = dot_t(jnp.where(leads, mine, other), w_ref[:, :half])
            product += dot_t(jnp.where(leads, other, mine), w_ref[:, half:])
        else:
            product = dot_t(mine, w_ref[...])
        if lead:
            out[:lead] = jnp.zeros((lead, tile), BF16)
        out[lead:] = product.astype(BF16)

    args = [*near, *(far or []), w]
    in_specs = [whole(a.shape) for a in args[:-1]]
    in_specs.append(pl.BlockSpec((tile, depth), lambda i, *_: (i, 0)))
    aliases = {}
    if carry is not None:
        aliases = {1 + len(args): 0}
        args.append(carry)
        in_specs.append(pl.BlockSpec(memory_space=pl.ANY))
    return pl.pallas_call(
        body,
        out_shape=jax.ShapeDtypeStruct((total, out_cols), BF16),
        grid_spec=pltpu.PrefetchScalarGridSpec(
            num_scalar_prefetch=1,
            grid=(out_cols // tile,),
            in_specs=in_specs,
            out_specs=pl.BlockSpec((rows + lead, tile), lambda i, *_: (0, i)),
        ),
        input_output_aliases=aliases,
        compiler_params=params(),
        cost_estimate=pl.CostEstimate(
            flops=4 * rows * depth * out_cols,
            bytes_accessed=2 * (depth * out_cols + rows * out_cols),
            transcendentals=0,
        ),
    )(side, *args)


def flipped(block, axis, bit):
    count = lax.axis_size(axis)
    return lax.ppermute(block, axis, [(i, i ^ bit) for i in range(count) if i ^ bit < count])


def spanning(leaves, bit_index):
    return len([j for j in range(INNER) if 2 << bit_index <= leaves >> j])


def gather_small_tree(ids, counts, own, width, meanwhile):
    page = ((PAGE, width), BF16)
    from_core = flipped(own, "sub", 1)

    def choose_chip(ids_ref, _, own_ref, far_ref, out):
        path = Path(ids_ref)
        for kind in range(2):
            for mine in (False, True):

                @pl.when((path.core == kind) & (path.owns[2] != mine))
                def _copy(kind=kind, mine=mine):
                    out[...] = (own_ref if mine else far_ref)[kind]

    (chip,) = small(choose_chip, ids, counts, [own, from_core], [page])
    from_pair = flipped(chip, "leaf", 1)

    def choose_pair(ids_ref, _, near_ref, far_ref, out):
        path = Path(ids_ref)
        out[...] = jnp.where(path.same(0, 1), near_ref[...], far_ref[...])

    after = meanwhile(from_core, chip)
    (pair,) = small(choose_pair, ids, counts, [chip, from_pair], [page], after)
    from_half = flipped(pair, "leaf", 2)

    def choose_all(ids_ref, _, chip_ref, pair_far, pair_ref, half_far, out):
        path = Path(ids_ref)
        out[0] = jnp.where(path.same(0, 2), pair_ref[...], half_far[...])
        out[1] = jnp.where(path.same(1, 1), chip_ref[...], pair_far[...])

    after = meanwhile(from_core, pair)
    (mine,) = small(
        choose_all,
        ids,
        counts,
        [chip, from_pair, pair, from_half],
        [((2, PAGE, width), BF16)],
        after,
    )
    theirs = flipped(mine, "sub", 1)
    return from_core, mine, theirs


def reduce_small_tree(ids, counts, kept, sent):
    count = len(kept)
    part = kept[0].shape[-1]
    width = part * count
    two = (2, PAGE, width)
    far = [flipped(s, "sub", 1) for s in sent]

    def add_low(_, __, *refs):
        total, low = refs[-2:]
        for i in range(count):
            cols = slice(i * part, (i + 1) * part)
            value = refs[i][...] + refs[count + i][...].astype(F32)
            total[:, :, cols] = value
            low[:, :, cols] = value.astype(BF16)

    total, low = small(add_low, ids, counts, [*kept, *far], [(two, F32), (two, BF16)])
    far = flipped(low, "leaf", 1)

    def add_pair(_, __, near, away, total, low):
        value = near[...] + away[...].astype(F32)
        total[...] = value
        low[...] = value[0].astype(BF16)

    total, low = small(
        add_pair, ids, counts, [total, far], [(two, F32), ((PAGE, width), BF16)]
    )
    far = flipped(low, "leaf", 2)

    def pick(ids_ref, _, near, away, out):
        path = Path(ids_ref)
        root = near[0] + away[...].astype(F32)
        out[...] = jnp.where(path.same(0, 1), root, near[1]).astype(BF16)

    (mine,) = small(pick, ids, counts, [total, far], [((PAGE, width), BF16)])
    return mine, flipped(mine, "sub", 1)


def finish_small_tree(ids, counts, own0, far2, mine, far, dk, dv):
    width = dk.shape[1]
    heads, groups = len(own0), len(mine)
    part = width // groups

    def body(ids_ref, counts_ref, *refs):
        own_r, far2_r = refs[:heads], refs[heads : 2 * heads]
        mine_r = refs[2 * heads : 2 * heads + groups]
        far_r = refs[2 * heads + groups : 2 * (heads + groups)]
        dk_out, dv_out, dv0_out = refs[-3:]
        path = Path(ids_ref)
        n0 = jnp.where(path.has_inner, counts_ref[0], 0)
        leads = path.core == 0
        ok = row_ok(n0, PAGE, HD)
        for i in range(heads):
            cols = slice(i * HD, (i + 1) * HD)
            n, at = divmod(i * HD, part)
            near, away = mine_r[n][:, at : at + HD], far_r[n][:, at : at + HD]
            k_in = jnp.where(path.owns[2], far2_r[i][0], jnp.where(leads, near, away))
            v_in = jnp.where(path.owns[2], far2_r[i][1], jnp.where(leads, away, near))
            dk_out[:, cols] = jnp.where(ok, own_r[i][0] + k_in.astype(F32), 0.0).astype(BF16)
            low = jnp.where(ok, own_r[i][1] + v_in.astype(F32), 0.0).astype(BF16)
            dv_out[:, cols] = low
            dv0_out[:, cols] = low

    args = [*own0, *far2, *mine, *far]
    return pl.pallas_call(
        body,
        out_shape=(
            jax.ShapeDtypeStruct(dk.shape, BF16),
            jax.ShapeDtypeStruct(dv.shape, BF16),
            jax.ShapeDtypeStruct((PAGE, width), BF16),
        ),
        grid_spec=pltpu.PrefetchScalarGridSpec(
            num_scalar_prefetch=2,
            grid=(1,),
            in_specs=[whole(a.shape) for a in args] + [pl.BlockSpec(memory_space=pl.ANY)] * 2,
            out_specs=(whole((PAGE, width)),) * 3,
        ),
        input_output_aliases={2 + len(args): 0, 3 + len(args): 1},
        compiler_params=params(SMALL_LIMIT),
    )(ids, counts, *args, dk, dv)


def gather_tree(ids, counts, own, width):
    leaves = lax.axis_size(("leaf", "sub"))
    owned = ids[:INNER] == ids[INNER] - 1
    pages = jnp.where(owned[:, None, None, None], own[None], jnp.zeros((), BF16))
    for bit in range(leaves.bit_length() - 1):
        active = spanning(leaves, bit)
        far = flipped(pages[:active], ("leaf", "sub"), 1 << bit)
        pages = jnp.concatenate([pages[:active] + far, pages[active:]])
    return pages


def reduce_tree(ids, parts):
    leaves = lax.axis_size(("leaf", "sub"))
    for bit in range(leaves.bit_length() - 1):
        active = spanning(leaves, bit)
        far = flipped(parts[:active], ("leaf", "sub"), 1 << bit)
        parts = jnp.concatenate([parts[:active] + far, parts[active:]])
    owned = ids[:INNER] == ids[INNER] - 1
    return jnp.sum(jnp.where(owned[:, None, None, None], parts, 0.0), axis=0)


def on_device(queries, grad_out, keys, values, log_norms, row_deltas, ancestors, counts, w_value):
    width = keys.shape[1]
    kv = width // HD
    group = queries.shape[1] // width
    leaves = lax.axis_size(("leaf", "sub"))
    ids = ancestors[0]
    rows_of = counts[0]
    fast = leaves == 8 and lax.axis_size("sub") == 2
    queries, grad_out, keys, values, log_norms, row_deltas, w_value = (
        pltpu.with_memory_space_constraint(a, pltpu.HBM)
        for a in (queries, grad_out, keys, values, log_norms, row_deltas, w_value)
    )

    def own_page(_, counts_ref, k_ref, v_ref, out):
        ok = row_ok(counts_ref[0], PAGE, width)
        out[0] = jnp.where(ok, k_ref[...], jnp.zeros((), BF16))
        out[1] = jnp.where(ok, v_ref[...], jnp.zeros((), BF16))

    own = pl.pallas_call(
        own_page,
        out_shape=jax.ShapeDtypeStruct((2, PAGE, width), BF16),
        grid_spec=pltpu.PrefetchScalarGridSpec(
            num_scalar_prefetch=2,
            grid=(1,),
            in_specs=[whole((PAGE, width))] * 2,
            out_specs=whole((2, PAGE, width)),
        ),
        compiler_params=params(SMALL_LIMIT),
    )(ids, rows_of, keys, values)

    state = {"gq": None, "kv": (None, None), "l2": (own, own)}
    own_out, shared_out, turned_q = {}, {}, {}

    def run_own(i, after=()):
        prev = turned_q.get(i)
        dq, dk, dv, *rest = own_pages(
            i, group, ids, rows_of, queries, grad_out, keys, values, log_norms, row_deltas,
            *state["l2"], prev, None if prev is None else state["gq"], state["kv"], after,
        )
        state["kv"] = (dk, dv)
        if prev is None:
            turned_q[i] = dq
        else:
            state["gq"] = dq
        own_out[i] = rest

    def run_shared(i, after=()):
        prev = turned_q.get(i)
        dq, *rest = shared_pages(
            i, group, ids, rows_of, queries, grad_out, log_norms, row_deltas, *state["shared"],
            prev, None if prev is None else state["gq"], after,
        )
        if prev is None:
            turned_q[i] = dq
        else:
            state["gq"] = dq
        shared_out[i] = rest

    last = kv - 1 if fast and kv > 1 else kv
    if fast:
        todo = list(range(last))
        quota = [1, len(todo) - 1]

        def meanwhile(from_core, token):
            state["l2"] = (own, from_core)
            done = ()
            for _ in range(quota.pop(0)):
                run_own(todo[0], (token,))
                done = (own_out[todo.pop(0)][1],)
            return done

        _, mine, theirs = gather_small_tree(ids, rows_of, own, width, meanwhile)
    else:
        pages = gather_tree(ids, rows_of, own, width)
        state["l2"] = (pages[2], pages[2])
        first = lax.axis_index("sub") == 0
        mine = jnp.where(first, pages[:2, 0], pages[:2, 1])
        theirs = jnp.where(first, pages[:2, 1], pages[:2, 0])
        for i in range(last):
            run_own(i)
    state["shared"] = (mine, theirs)
    for i in range(kv):
        run_shared(i)
    for i in range(last, kv):
        run_own(i, (shared_out[kv - 1][0],))

    if fast:
        far2 = [flipped(own_out[i][2], "sub", 1) for i in range(kv)]
        cuts = [range(0, kv // 2), range(kv // 2, kv)] if kv > 1 else [range(kv)]
        reduced = [
            reduce_small_tree(
                ids, rows_of, [shared_out[i][0] for i in cut], [shared_out[i][1] for i in cut]
            )
            for cut in cuts
        ]
        grad_keys, grad_values, dv0 = finish_small_tree(
            ids, rows_of, [own_out[i][1] for i in range(kv)], far2,
            [r[0] for r in reduced], [r[1] for r in reduced], *state["kv"],
        )
    else:
        first = lax.axis_index("sub") == 0
        own0, gained = [], []
        for i in range(kv):
            kept, sent = shared_out[i]
            sent = sent.astype(F32)
            upper = jnp.stack([jnp.where(first, kept, sent), jnp.where(first, sent, kept)], axis=1)
            low = own_out[i][2].astype(F32)
            gained.append(reduce_tree(ids, jnp.concatenate([upper, low[None]])))
            owns2 = ids[2] == ids[INNER] - 1
            own0.append(own_out[i][1] - jnp.where(owns2, low, 0.0))
        total = jnp.concatenate(gained, axis=-1) + jnp.concatenate(own0, axis=-1)
        has = jnp.any(ids[:INNER] == ids[INNER] - 1)
        ok = (jnp.arange(PAGE) < jnp.where(has, rows_of[0], 0))[:, None]
        total = jnp.where(ok, total, 0.0).astype(BF16)
        grad_keys = lax.dynamic_update_slice(state["kv"][0], total[0], (0, 0))
        grad_values = lax.dynamic_update_slice(state["kv"][1], total[1], (0, 0))
        dv0 = total[1]

    dv12 = [own_out[i][0] for i in range(kv)]
    side = lax.axis_index("tensor").astype(I32).reshape(1)
    if lax.axis_size("tensor") == 2:
        spread = lambda parts: (parts, [flipped(p, "tensor", 1) for p in parts])
    else:
        spread = lambda parts: (
            [lax.all_gather(jnp.concatenate(parts, axis=1), "tensor", axis=1, tiled=True)],
            None,
        )
    grad_input = input_grad(*spread(dv12), side, w_value, 2 * PAGE, None)
    grad_input = input_grad(*spread([dv0]), side, w_value, PAGE, grad_input)
    return (state["gq"], grad_keys, grad_values, grad_input)


def solution(mesh):
    placed = (
        P(("groups", "leaf", "sub"), "tensor"),
        P(("groups", "leaf", "sub"), "tensor"),
        P(("groups", "leaf", "sub"), "tensor"),
        P(("groups", "leaf", "sub"), "tensor"),
        P("tensor", ("groups", "leaf", "sub")),
        P("tensor", ("groups", "leaf", "sub")),
        P(("groups", "leaf", "sub"), None),
        P(("groups", "leaf", "sub"), None),
        P("tensor", None),
    )
    return jax.shard_map(
        on_device,
        mesh=mesh,
        in_specs=placed,
        out_specs=(
            P(("groups", "leaf", "sub"), "tensor"),
            P(("groups", "leaf", "sub"), "tensor"),
            P(("groups", "leaf", "sub"), "tensor"),
            P(("groups", "leaf", "sub"), "tensor"),
        ),
        check_vma=False,
    )
```

time: 104 us -> 93.7 us (0.901)
  local copies, waits for them, and re-layouts: 14.5 us -> 2.62 us
  waiting for transfers between devices: 17.3 us -> 9.8 us
  Pallas kernels: 55.2 us -> 61.9 us
  starting transfers between devices: 16 us -> 18.1 us
    unnamed x35 -> x12, local copies, waits for them, and re-layouts: 14.5 us -> 2.62 us
    ppermute x16 -> x23, waiting for transfers between devices: 17.3 us -> 9.8 us  [flipped(): lax.ppermute(block, axis, [(i, i ^ bit) for i in range(count) if i ^ bit...]
    pallas_call x2, Pallas kernels: 6.36 us -> 10.7 us  [input_grad(): pl.pallas_call(body, out_shape=jax.ShapeDtypeStruct((total, out_cols), BF...]
    ppermute x16 -> x23, starting transfers between devices: 16 us -> 18.1 us  [flipped(): lax.ppermute(block, axis, [(i, i ^ bit) for i in range(count) if i ^ bit...]
    pallas_call x13 -> x17, Pallas kernels: 47 us -> 48.3 us  [the longest x8 43.1 us: head_kernel(): pl.pallas_call(functools.partial(body, heads, second), out_shape=(dq_shap...]
  transfers between devices with their start and end apart: 16 -> 23, of which waited for: 8 -> 7; matrix products, arithmetic and copies ran while one was open for 0% -> 0% of each run, Pallas kernels for 38% -> 41%
where the time goes in v2:
time: 93.7 us; the launch traced here: 93.2 us
  Pallas kernels  61.9 us (66%)
  starting transfers between devices  18.1 us (19%)
  waiting for transfers between devices  9.8 us (10%)
  local copies, waits for them, and re-layouts  2.62 us (3%)
    pallas_call x8, Pallas kernels, head_kernel(): pl.pallas_call(functools.partial(body, heads, second), out_shape=(dq_shap...  43.1 us
    ppermute x23, starting transfers between devices, flipped(): lax.ppermute(block, axis, [(i, i ^ bit) for i in range(count) if i ^ bit...  18.1 us
    pallas_call x2, Pallas kernels, input_grad(): pl.pallas_call(body, out_shape=jax.ShapeDtypeStruct((total, out_cols), BF...  10.7 us
    ppermute x23, waiting for transfers between devices, flipped(): lax.ppermute(block, axis, [(i, i ^ bit) for i in range(count) if i ^ bit...  9.8 us
    pallas_call x9, Pallas kernels, small(): pl.pallas_call(kernel, out_shape=tuple((jax.ShapeDtypeStruct(s, d) for s,...  5.16 us
    unnamed x12, local copies, waits for them, and re-layouts  2.62 us
  transfers between devices with their start and end apart: 23, of which 7 were waited for; matrix products, arithmetic and copies ran while one was open for 0% of the time, Pallas kernels for 41%

profile of v2, /device:TPU:0, one launch (start us, length us, event | category | flops | bytes accessed | tf_op | source)
XLA Modules:
  0.0 93.2 jit_solution(11497031932842967633)
XLA Ops:
  0.6 0.0 copy-start
  0.6 0.6 copy-done
  1.3 0.7 copy-done.3
  1.9 1.5 %shard_map.120.refs_2_.l2_own = bf16[2,128,512]{2,1,0:T(8,128)(2,1)S(1)} custom-call(s32[5]{0:T(128)S(1)} %bitcast.3, s32[3]{0:T(128)S(1)} %bitcast.22, bf16[384,512]{1,0:T(8,128)(2,1)} %k.7, bf16[384,512]{1,0:T(8,128)(2,1)} %v.7), custom_call_target="tpu_custom_call" | custom-call | tf_op jit(solution)/shard_map/pallas_call | solution.py:585
  3.5 0.5 collective-permute-start
  4.0 1.2 %collective-permute-done.refs_3_.l2_far = bf16[2,128,512]{2,1,0:T(8,128)(2,1)S(1)} collective-permute-done((bf16[2,128,512]{2,1,0:T(8,128)(2,1)S(1)}, bf16[2,128,512]{2,1,0:T(8,128)(2,1)S(1)}, u32[]{:S(2)}, u32[]{:S(2)}) %collective-permute-start) | collective-permute-done | bytes 262176 | tf_op jit(solution)/shard_map/ppermute | solution.py:416
  5.2 0.6 shard_map.121.refs_0_.refs_2_
  5.8 3.0 %collective-permute-start.1 = (bf16[128,512]{1,0:T(8,128)(2,1)S(1)}, bf16[128,512]{1,0:T(8,128)(2,1)S(1)}, u32[]{:S(2)}, u32[]{:S(2)}) collective-permute-start(bf16[128,512]{1,0:T(8,128)(2,1)S(1)} %shard_map.121.refs_0_.refs_2_), channel_id=1, source_target_pairs={{0,4},{4,0},{8,12},{12,8},{1,5},{5,1},{9,13},{13,9},{2,6},{6,2},{1... | collective-permute-start | bytes 393224 | tf_op jit(solution)/shard_map/ppermute | solution.py:416
  8.8 0.7 copy-done.1
  9.4 0.7 copy-done.4
  10.1 5.7 %shard_map.122 = (f32[1024,384]{1,0:T(8,128)S(1)}, bf16[384,512]{1,0:T(8,128)(2,1)}, bf16[384,512]{1,0:T(8,128)(2,1)}, bf16[256,128]{1,0:T(8,128)(2,1)S(1)}, f32...) custom-call(s32[5]{0:T(128)S(1)} %bitcast.5, s32[3]{0:T(128)S(1)} %bitcast.24, bf16[384,4096]{1,0:T(8,128)(2,1)} %q.15, ...), custom_call_target="tpu_custom_call" | custom-call | flops 5368709120 | bytes 3145728 | tf_op jit(solution)/shard_map/pallas_call | solution.py:290
  15.8 0.6 shard_map.123.refs_2_.refs_4_
  16.4 2.7 %collective-permute-start.2 = (bf16[128,512]{1,0:T(8,128)(2,1)S(1)}, bf16[128,512]{1,0:T(8,128)(2,1)S(1)}, u32[]{:S(2)}, u32[]{:S(2)}) collective-permute-start(bf16[128,512]{1,0:T(8,128)(2,1)S(1)} %shard_map.123.refs_2_.refs_4_), channel_id=1, source_target_pairs={{0,8},{4,12},{8,0},{12,4},{1,9},{5,13},{9,1},{13,5},{2,10},{6,14},... | collective-permute-start | bytes 393224 | tf_op jit(solution)/shard_map/ppermute | solution.py:416
  19.0 5.8 %shard_map.124 = (f32[1024,384]{1,0:T(8,128)S(1)}, bf16[384,512]{1,0:T(8,128)(2,1)}, bf16[384,512]{1,0:T(8,128)(2,1)}, bf16[256,128]{1,0:T(8,128)(2,1)S(1)}, f32...) custom-call(s32[5]{0:T(128)S(1)} %bitcast.7, ...), custom_call_target="tpu_custom_call", output_to_operand_aliasing={{1}: (10, {}), {2}: (11, {})} | custom-call | flops 5368709120 | bytes 3145728 | tf_op jit(solution)/shard_map/pallas_call | solution.py:290
  24.8 5.7 %shard_map.125 = (f32[1024,384]{1,0:T(8,128)S(1)}, bf16[384,512]{1,0:T(8,128)(2,1)}, bf16[384,512]{1,0:T(8,128)(2,1)}, bf16[256,128]{1,0:T(8,128)(2,1)S(1)}, f32...) custom-call(s32[5]{0:T(128)S(1)} %bitcast.8, ...), custom_call_target="tpu_custom_call", output_to_operand_aliasing={{1}: (10, {}), {2}: (11, {})} | custom-call | flops 5368709120 | bytes 3145728 | tf_op jit(solution)/shard_map/pallas_call | solution.py:290
  30.6 0.6 shard_map.126.mine
  31.1 0.1 collective-permute-start.3
  31.2 1.5 %collective-permute-done.3.far = bf16[2,128,512]{2,1,0:T(8,128)(2,1)S(1)} collective-permute-done((bf16[2,128,512]{2,1,0:T(8,128)(2,1)S(1)}, bf16[2,128,512]{2,1,0:T(8,128)(2,1)S(1)}, u32[]{:S(2)}, u32[]{:S(2)}) %collective-permute-start.3) | collective-permute-done | bytes 262176 | tf_op jit(solution)/shard_map/ppermute | solution.py:416
  32.7 5.1 %shard_map.128 = (bf16[384,4096]{1,0:T(8,128)(2,1)}, f32[2,128,128]{2,1,0:T(8,128)S(1)}, bf16[2,128,128]{2,1,0:T(8,128)(2,1)S(1)}) custom-call(s32[5]{0:T(128)S(1)} %bitcast.10, s32[3]{0:T(128)S(1)} %bitcast.29, bf16[384,4096]{1,0:T(8,128)(2,1)} %q.15, bf16[384,4096]{1,0:T(8,128)(2,1)} %g.15, f32[32,384]{1,0:T(8,128)} %norms.15, f32[32,384]{1,0:T(8,128)} %deltas.15, ...), custom_call_target="tpu_custom_call" | custom-call | flops 4026531840 | bytes 3145728 | tf_op jit(solution)/shard_map/pallas_call | solution.py:290
  37.9 5.2 %shard_map.129 = (bf16[384,4096]{1,0:T(8,128)(2,1)}, f32[2,128,128]{2,1,0:T(8,128)S(1)}, bf16[2,128,128]{2,1,0:T(8,128)(2,1)S(1)}) custom-call(s32[5]{0:T(128)S(1)} %bitcast.11, s32[3]{0:T(128)S(1)} %bitcast.30, bf16[384,4096]{1,0:T(8,128)(2,1)} %q.15, bf16[384,4096]{1,0:T(8,128)(2,1)} %g.15, f32[32,384]{1,0:T(8,128)} %norms.15, ...), custom_call_target="tpu_custom_call", output_to_operand_aliasing={{0}: (9, {})} | custom-call | flops 4026531840 | bytes 3145728 | tf_op jit(solution)/shard_map/pallas_call | solution.py:290
  43.1 5.1 %shard_map.130 = (bf16[384,4096]{1,0:T(8,128)(2,1)}, f32[2,128,128]{2,1,0:T(8,128)S(1)}, bf16[2,128,128]{2,1,0:T(8,128)(2,1)S(1)}) custom-call(s32[5]{0:T(128)S(1)} %bitcast.12, s32[3]{0:T(128)S(1)} %bitcast.31, bf16[384,4096]{1,0:T(8,128)(2,1)} %q.15, bf16[384,4096]{1,0:T(8,128)(2,1)} %g.15, f32[32,384]{1,0:T(8,128)} %norms.15, ...), custom_call_target="tpu_custom_call", output_to_operand_aliasing={{0}: (9, {})} | custom-call | flops 4026531840 | bytes 3145728 | tf_op jit(solution)/shard_map/pallas_call | solution.py:290
  48.2 0.1 collective-permute-start.12
  48.3 4.2 %shard_map.127 = (f32[1024,384]{1,0:T(8,128)S(1)}, f32[2,128,128]{2,1,0:T(8,128)S(1)}, bf16[2,128,128]{2,1,0:T(8,128)(2,1)S(1)}) custom-call(s32[5]{0:T(128)S(1)} %bitcast.13, s32[3]{0:T(128)S(1)} %bitcast.32, bf16[384,4096]{1,0:T(8,128)(2,1)} %q.15, bf16[384,4096]{1,0:T(8,128)(2,1)} %g.15, f32[32,384]{1,0:T(8,128)} %norms.15, f32[32,384]{1,0:T(8,128)} %deltas.15, ...), custom_call_target="tpu_custom_call" | custom-call | flops 4026531840 | bytes 3145728 | tf_op jit(solution)/shard_map/pallas_call | solution.py:290
  52.5 0.4 collective-permute-start.13
  53.0 0.1 collective-permute-start.9
  53.1 0.4 collective-permute-start.8
  53.5 0.0 collective-permute-done.12.refs_4_
  53.5 0.4 collective-permute-done.13.refs_5_
  53.9 0.6 shard_map.135
  54.5 0.5 collective-permute-start.14
  55.0 0.0 collective-permute-done.9.refs_5_
  55.0 0.0 collective-permute-done.8.refs_4_
  55.0 0.6 shard_map.132
  55.6 1.6 %collective-permute-start.10 = (bf16[2,128,256]{2,1,0:T(8,128)(2,1)S(1)}, bf16[2,128,256]{2,1,0:T(8,128)(2,1)S(1)}, u32[]{:S(2)}, u32[]{:S(2)}) collective-permute-start(bf16[2,128,256]{2,1,0:T(8,128)(2,1)S(1)} %get-tuple-element.79), channel_id=1, source_target_pairs={{0,4},{4,0},{8,12},{12,8},{1,5},{5,1},{9,13},{13,9},{2,6},{6,2},{1... | collective-permute-start | bytes 393224 | tf_op jit(solution)/shard_map/ppermute | solution.py:416
  57.2 0.0 collective-permute-start.4
  57.2 0.5 collective-permute-start.6
  57.7 3.1 %collective-permute-done.14.refs_3_ = bf16[2,128,256]{2,1,0:T(8,128)(2,1)S(1)} collective-permute-done((bf16[2,128,256]{2,1,0:T(8,128)(2,1)S(1)}, bf16[2,128,256]{2,1,0:T(8,128)(2,1)S(1)}, u32[]{:S(2)}, u32[]{:S(2)}) %collective-permute-start.14) | collective-permute-done | bytes 131104 | tf_op jit(solution)/shard_map/ppermute | solution.py:416
  60.8 0.6 shard_map.136
  61.4 0.4 collective-permute-start.15
  61.8 1.3 %collective-permute-done.10.refs_3_ = bf16[2,128,256]{2,1,0:T(8,128)(2,1)S(1)} collective-permute-done((bf16[2,128,256]{2,1,0:T(8,128)(2,1)S(1)}, bf16[2,128,256]{2,1,0:T(8,128)(2,1)S(1)}, u32[]{:S(2)}, u32[]{:S(2)}) %collective-permute-start.10) | collective-permute-done | bytes 131104 | tf_op jit(solution)/shard_map/ppermute | solution.py:416
  63.1 0.6 shard_map.133
  63.7 1.4 %collective-permute-start.11 = (bf16[128,256]{1,0:T(8,128)(2,1)S(1)}, bf16[128,256]{1,0:T(8,128)(2,1)S(1)}, u32[]{:S(2)}, u32[]{:S(2)}) collective-permute-start(bf16[128,256]{1,0:T(8,128)(2,1)S(1)} %get-tuple-element.81), channel_id=1, source_target_pairs={{0,8},{4,12},{8,0},{12,4},{1,9},{5,13},{9,1},{13,5},{2,10},{6,14},... | collective-permute-start | bytes 196616 | tf_op jit(solution)/shard_map/ppermute | solution.py:416
  65.1 6.2 %shard_map.131 = (bf16[384,4096]{1,0:T(8,128)(2,1)}, bf16[384,512]{1,0:T(8,128)(2,1)}, bf16[384,512]{1,0:T(8,128)(2,1)}, bf16[256,128]{1,0:T(8,128)(2,1)S(1)}, f...) custom-call(s32[5]{0:T(128)S(1)} %bitcast.18, ...), custom_call_target="tpu_custom_call", output_to_operand_aliasing={{0}: (11, {}), {1}: (12, {}), {2}: (13, {})} | custom-call | flops 5368709120 | bytes 3145728 | tf_op jit(solution)/shard_map/pallas_call | solution.py:290
  71.3 0.0 collective-permute-done.15.refs_3_
  71.3 0.1 collective-permute-start.7
  71.4 0.6 shard_map.137.refs_9_
  71.9 0.6 collective-permute-start.17
  72.5 0.6 shard_map.134.refs_8_
  73.1 0.0 collective-permute-done.4.refs_4_
  73.1 0.1 collective-permute-start.16
  73.2 0.0 collective-permute-done.6.refs_6_
  73.2 1.5 %collective-permute-start.19 = (bf16[256,128]{1,0:T(8,128)(2,1)S(1)}, bf16[256,128]{1,0:T(8,128)(2,1)S(1)}, u32[]{:S(2)}, u32[]{:S(2)}) collective-permute-start(bf16[256,128]{1,0:T(8,128)(2,1)S(1)} %get-tuple-element.94.refs_0_), channel_id=1, source_target_pairs={{0,2},{2,0},{1,3},{3,1},{4,6},{6,4},{5,7},{7,5},{8,10},{10,8},{9,1... | collective-permute-start | bytes 196616 | tf_op jit(solution)/shard_map/ppermute | solution.py:416
  74.7 0.0 collective-permute-done.5.refs_5_
  74.7 0.5 collective-permute-start.21
  75.3 1.5 %collective-permute-start.20 = (bf16[256,128]{1,0:T(8,128)(2,1)S(1)}, bf16[256,128]{1,0:T(8,128)(2,1)S(1)}, u32[]{:S(2)}, u32[]{:S(2)}) collective-permute-start(bf16[256,128]{1,0:T(8,128)(2,1)S(1)} %get-tuple-element.95.refs_1_), channel_id=1, source_target_pairs={{0,2},{2,0},{1,3},{3,1},{4,6},{6,4},{5,7},{7,5},{8,10},{10,8},{9,1... | collective-permute-start | bytes 196616 | tf_op jit(solution)/shard_map/ppermute | solution.py:416
  76.8 0.5 collective-permute-start.22
  77.3 0.0 collective-permute-done.16.refs_10_
  77.3 1.4 %shard_map.138 = (bf16[384,512]{1,0:T(8,128)(2,1)}, bf16[384,512]{1,0:T(8,128)(2,1)}, bf16[128,512]{1,0:T(8,128)(2,1)S(1)}) custom-call(s32[5]{0:T(128)S(1)} %bitcast.21, s32[3]{0:T(128)S(1)} %bitcast.40, f32[2,128,128]{2,1,0:T(8,128)S(1)} %get-tuple-element.51.refs_4_.refs_0_, ...), custom_call_target="tpu_custom_call", output_to_operand_aliasing={{0}: (14, {}), {1}: (15, {})} | custom-call | tf_op jit(solution)/shard_map/pallas_call | solution.py:528
  78.7 1.5 %collective-permute-start.18 = (bf16[128,512]{1,0:T(8,128)(2,1)S(1)}, bf16[128,512]{1,0:T(8,128)(2,1)S(1)}, u32[]{:S(2)}, u32[]{:S(2)}) collective-permute-start(bf16[128,512]{1,0:T(8,128)(2,1)S(1)} %get-tuple-element.93.refs_0_), channel_id=1, source_target_pairs={{0,2},{2,0},{1,3},{3,1},{4,6},{6,4},{5,7},{7,5},{8,10},{10,8},{9,1... | collective-permute-start | bytes 393224 | tf_op jit(solution)/shard_map/ppermute | solution.py:416
  80.2 0.0 collective-permute-done.19.refs_4_
  80.2 0.9 collective-permute-done.20.refs_5_
  81.1 1.4 %collective-permute-done.22.refs_7_ = bf16[256,128]{1,0:T(8,128)(2,1)S(1)} collective-permute-done((bf16[256,128]{1,0:T(8,128)(2,1)S(1)}, bf16[256,128]{1,0:T(8,128)(2,1)S(1)}, u32[]{:S(2)}, u32[]{:S(2)}) %collective-permute-start.22) | collective-permute-done | bytes 65568 | tf_op jit(solution)/shard_map/ppermute | solution.py:416
  82.5 5.5 %shard_map.139.refs_3_ = bf16[384,2560]{1,0:T(8,128)(2,1)} custom-call(s32[1]{0:T(128)} %bitcast.2.flag, bf16[256,128]{1,0:T(8,128)(2,1)S(1)} %get-tuple-element.94.refs_0_, bf16[256,128]{1,0:T(8,128)(2,1)S(1)} %get-tuple-element.95.refs_1_, bf16[256,128]{1,0:T(8,128)(2,1)S(1)} %get-tuple-element.96.refs_2_, bf16[256,128]{1,0:T(8,128)(2,1)S(1)} %get-tuple-element.97.refs_3_, ...), custom_call_target="tpu_custom_call" | custom-call | flops 2684354560 | bytes 6553600 | tf_op jit(solution)/shard_map/pallas_call | solution.py:395
  88.0 5.1 %shard_map.140 = bf16[384,2560]{1,0:T(8,128)(2,1)} custom-call(s32[1]{0:T(128)} %bitcast.2.flag, bf16[128,512]{1,0:T(8,128)(2,1)S(1)} %get-tuple-element.93.refs_0_, bf16[128,512]{1,0:T(8,128)(2,1)S(1)} %collective-permute-done.18.refs_1_, bf16[2560,1024]{1,0:T(8,128)(2,1)} %refs_2_.1, ...), custom_call_target="tpu_custom_call", output_to_operand_aliasing={{}: (4, {})} | custom-call | flops 1342177280 | bytes 5898240 | tf_op jit(solution)/shard_map/pallas_call | solution.py:395
  (15 shorter events, 0.0 us)
Async XLA Ops:
  0.6 0.7 copy-start
  1.3 0.7 copy-start.3
  3.5 1.7 %collective-permute-start = (bf16[2,128,512]{2,1,0:T(8,128)(2,1)S(1)}, bf16[2,128,512]{2,1,0:T(8,128)(2,1)S(1)}, u32[]{:S(2)}, u32[]{:S(2)}) collective-permute-start(bf16[2,128,512]{2,1,0:T(8,128)(2,1)S(1)} %shard_map.120.refs_2_.l2_own), channel_id=1, source_target_pairs={{0,1},{1,0},{2,3},{3,2},{4,5},{5,4},{6,7},{7,6},{8,9},{9,8},{10,11... | collective-permute-start | bytes 786440 | tf_op jit(solution)/shard_map/ppermute | solution.py:416
  5.8 10.1 %collective-permute-start.1 = (bf16[128,512]{1,0:T(8,128)(2,1)S(1)}, bf16[128,512]{1,0:T(8,128)(2,1)S(1)}, u32[]{:S(2)}, u32[]{:S(2)}) collective-permute-start(bf16[128,512]{1,0:T(8,128)(2,1)S(1)} %shard_map.121.refs_0_.refs_2_), channel_id=1, source_target_pairs={{0,4},{4,0},{8,12},{12,8},{1,5},{5,1},{9,13},{13,9},{2,6},{6,2},{1... | collective-permute-start | bytes 393224 | tf_op jit(solution)/shard_map/ppermute | solution.py:416
  8.8 0.7 copy-start.1
  9.4 0.7 copy-start.4
  16.4 14.2 %collective-permute-start.2 = (bf16[128,512]{1,0:T(8,128)(2,1)S(1)}, bf16[128,512]{1,0:T(8,128)(2,1)S(1)}, u32[]{:S(2)}, u32[]{:S(2)}) collective-permute-start(bf16[128,512]{1,0:T(8,128)(2,1)S(1)} %shard_map.123.refs_2_.refs_4_), channel_id=1, source_target_pairs={{0,8},{4,12},{8,0},{12,4},{1,9},{5,13},{9,1},{13,5},{2,10},{6,14},... | collective-permute-start | bytes 393224 | tf_op jit(solution)/shard_map/ppermute | solution.py:416
  31.1 1.6 %collective-permute-start.3 = (bf16[2,128,512]{2,1,0:T(8,128)(2,1)S(1)}, bf16[2,128,512]{2,1,0:T(8,128)(2,1)S(1)}, u32[]{:S(2)}, u32[]{:S(2)}) collective-permute-start(bf16[2,128,512]{2,1,0:T(8,128)(2,1)S(1)} %shard_map.126.mine), channel_id=1, source_target_pairs={{0,1},{1,0},{2,3},{3,2},{4,5},{5,4},{6,7},{7,6},{8,9},{9,8},{10,11... | collective-permute-start | bytes 786440 | tf_op jit(solution)/shard_map/ppermute | solution.py:416
  48.2 5.3 %collective-permute-start.12 = (bf16[2,128,128]{2,1,0:T(8,128)(2,1)S(1)}, bf16[2,128,128]{2,1,0:T(8,128)(2,1)S(1)}, u32[]{:S(2)}, u32[]{:S(2)}) collective-permute-start(bf16[2,128,128]{2,1,0:T(8,128)(2,1)S(1)} %get-tuple-element.83), channel_id=1, source_target_pairs={{0,1},{1,0},{2,3},{3,2},{4,5},{5,4},{6,7},{7,6},{8,9},{9,8},{10,11... | collective-permute-start | bytes 196616 | tf_op jit(solution)/shard_map/ppermute | solution.py:416
  52.5 1.3 %collective-permute-start.13 = (bf16[2,128,128]{2,1,0:T(8,128)(2,1)S(1)}, bf16[2,128,128]{2,1,0:T(8,128)(2,1)S(1)}, u32[]{:S(2)}, u32[]{:S(2)}) collective-permute-start(bf16[2,128,128]{2,1,0:T(8,128)(2,1)S(1)} %get-tuple-element.84), channel_id=1, source_target_pairs={{0,1},{1,0},{2,3},{3,2},{4,5},{5,4},{6,7},{7,6},{8,9},{9,8},{10,11... | collective-permute-start | bytes 196616 | tf_op jit(solution)/shard_map/ppermute | solution.py:416
  53.0 2.0 %collective-permute-start.9 = (bf16[2,128,128]{2,1,0:T(8,128)(2,1)S(1)}, bf16[2,128,128]{2,1,0:T(8,128)(2,1)S(1)}, u32[]{:S(2)}, u32[]{:S(2)}) collective-permute-start(bf16[2,128,128]{2,1,0:T(8,128)(2,1)S(1)} %get-tuple-element.77), channel_id=1, source_target_pairs={{0,1},{1,0},{2,3},{3,2},{4,5},{5,4},{6,7},{7,6},{8,9},{9,8},{10,11... | collective-permute-start | bytes 196616 | tf_op jit(solution)/shard_map/ppermute | solution.py:416
  53.1 1.9 %collective-permute-start.8 = (bf16[2,128,128]{2,1,0:T(8,128)(2,1)S(1)}, bf16[2,128,128]{2,1,0:T(8,128)(2,1)S(1)}, u32[]{:S(2)}, u32[]{:S(2)}) collective-permute-start(bf16[2,128,128]{2,1,0:T(8,128)(2,1)S(1)} %get-tuple-element.76), channel_id=1, source_target_pairs={{0,1},{1,0},{2,3},{3,2},{4,5},{5,4},{6,7},{7,6},{8,9},{9,8},{10,11... | collective-permute-start | bytes 196616 | tf_op jit(solution)/shard_map/ppermute | solution.py:416
  54.5 6.4 %collective-permute-start.14 = (bf16[2,128,256]{2,1,0:T(8,128)(2,1)S(1)}, bf16[2,128,256]{2,1,0:T(8,128)(2,1)S(1)}, u32[]{:S(2)}, u32[]{:S(2)}) collective-permute-start(bf16[2,128,256]{2,1,0:T(8,128)(2,1)S(1)} %get-tuple-element.86), channel_id=1, source_target_pairs={{0,4},{4,0},{8,12},{12,8},{1,5},{5,1},{9,13},{13,9},{2,6},{6,2},{1... | collective-permute-start | bytes 393224 | tf_op jit(solution)/shard_map/ppermute | solution.py:416
  55.6 7.5 %collective-permute-start.10 = (bf16[2,128,256]{2,1,0:T(8,128)(2,1)S(1)}, bf16[2,128,256]{2,1,0:T(8,128)(2,1)S(1)}, u32[]{:S(2)}, u32[]{:S(2)}) collective-permute-start(bf16[2,128,256]{2,1,0:T(8,128)(2,1)S(1)} %get-tuple-element.79), channel_id=1, source_target_pairs={{0,4},{4,0},{8,12},{12,8},{1,5},{5,1},{9,13},{13,9},{2,6},{6,2},{1... | collective-permute-start | bytes 393224 | tf_op jit(solution)/shard_map/ppermute | solution.py:416
  57.2 15.9 %collective-permute-start.4 = (bf16[2,128,128]{2,1,0:T(8,128)(2,1)S(1)}, bf16[2,128,128]{2,1,0:T(8,128)(2,1)S(1)}, u32[]{:S(2)}, u32[]{:S(2)}) collective-permute-start(bf16[2,128,128]{2,1,0:T(8,128)(2,1)S(1)} %get-tuple-element.70), channel_id=1, source_target_pairs={{0,1},{1,0},{2,3},{3,2},{4,5},{5,4},{6,7},{7,6},{8,9},{9,8},{10,11... | collective-permute-start | bytes 196616 | tf_op jit(solution)/shard_map/ppermute | solution.py:416
  57.2 16.0 %collective-permute-start.6 = (bf16[2,128,128]{2,1,0:T(8,128)(2,1)S(1)}, bf16[2,128,128]{2,1,0:T(8,128)(2,1)S(1)}, u32[]{:S(2)}, u32[]{:S(2)}) collective-permute-start(bf16[2,128,128]{2,1,0:T(8,128)(2,1)S(1)} %get-tuple-element.72), channel_id=1, source_target_pairs={{0,1},{1,0},{2,3},{3,2},{4,5},{5,4},{6,7},{7,6},{8,9},{9,8},{10,11... | collective-permute-start | bytes 196616 | tf_op jit(solution)/shard_map/ppermute | solution.py:416
  57.7 17.0 %collective-permute-start.5 = (bf16[2,128,128]{2,1,0:T(8,128)(2,1)S(1)}, bf16[2,128,128]{2,1,0:T(8,128)(2,1)S(1)}, u32[]{:S(2)}, u32[]{:S(2)}) collective-permute-start(bf16[2,128,128]{2,1,0:T(8,128)(2,1)S(1)} %get-tuple-element.71), channel_id=1, source_target_pairs={{0,1},{1,0},{2,3},{3,2},{4,5},{5,4},{6,7},{7,6},{8,9},{9,8},{10,11... | collective-permute-start | bytes 196616 | tf_op jit(solution)/shard_map/ppermute | solution.py:416
  61.4 9.9 %collective-permute-start.15 = (bf16[128,256]{1,0:T(8,128)(2,1)S(1)}, bf16[128,256]{1,0:T(8,128)(2,1)S(1)}, u32[]{:S(2)}, u32[]{:S(2)}) collective-permute-start(bf16[128,256]{1,0:T(8,128)(2,1)S(1)} %get-tuple-element.88), channel_id=1, source_target_pairs={{0,8},{4,12},{8,0},{12,4},{1,9},{5,13},{9,1},{13,5},{2,10},{6,14},... | collective-permute-start | bytes 196616 | tf_op jit(solution)/shard_map/ppermute | solution.py:416
  63.7 8.3 %collective-permute-start.11 = (bf16[128,256]{1,0:T(8,128)(2,1)S(1)}, bf16[128,256]{1,0:T(8,128)(2,1)S(1)}, u32[]{:S(2)}, u32[]{:S(2)}) collective-permute-start(bf16[128,256]{1,0:T(8,128)(2,1)S(1)} %get-tuple-element.81), channel_id=1, source_target_pairs={{0,8},{4,12},{8,0},{12,4},{1,9},{5,13},{9,1},{13,5},{2,10},{6,14},... | collective-permute-start | bytes 196616 | tf_op jit(solution)/shard_map/ppermute | solution.py:416
  65.1 12.3 %copy-start.2 = (s32[1,5]{1,0:T(1,128)S(1)}, s32[1,5]{1,0:T(1,128)}, u32[]{:S(2)}) copy-start(s32[1,5]{1,0:T(1,128)} %param.15) | copy-start | bytes 64
  65.1 12.3 %copy-start.5 = (s32[1,3]{1,0:T(1,128)S(1)}, s32[1,3]{1,0:T(1,128)}, u32[]{:S(2)}) copy-start(s32[1,3]{1,0:T(1,128)} %param.16) | copy-start | bytes 40
  71.3 4.0 %collective-permute-start.7 = (bf16[2,128,128]{2,1,0:T(8,128)(2,1)S(1)}, bf16[2,128,128]{2,1,0:T(8,128)(2,1)S(1)}, u32[]{:S(2)}, u32[]{:S(2)}) collective-permute-start(bf16[2,128,128]{2,1,0:T(8,128)(2,1)S(1)} %get-tuple-element.73), channel_id=1, source_target_pairs={{0,1},{1,0},{2,3},{3,2},{4,5},{5,4},{6,7},{7,6},{8,9},{9,8},{10,11... | collective-permute-start | bytes 196616 | tf_op jit(solution)/shard_map/ppermute | solution.py:416
  71.9 4.8 %collective-permute-start.17 = (bf16[128,256]{1,0:T(8,128)(2,1)S(1)}, bf16[128,256]{1,0:T(8,128)(2,1)S(1)}, u32[]{:S(2)}, u32[]{:S(2)}) collective-permute-start(bf16[128,256]{1,0:T(8,128)(2,1)S(1)} %shard_map.137.refs_9_), channel_id=1, source_target_pairs={{0,1},{1,0},{2,3},{3,2},{4,5},{5,4},{6,7},{7,6},{8,9},{9,8},{10,11... | collective-permute-start | bytes 196616 | tf_op jit(solution)/shard_map/ppermute | solution.py:416
  73.1 4.2 %collective-permute-start.16 = (bf16[128,256]{1,0:T(8,128)(2,1)S(1)}, bf16[128,256]{1,0:T(8,128)(2,1)S(1)}, u32[]{:S(2)}, u32[]{:S(2)}) collective-permute-start(bf16[128,256]{1,0:T(8,128)(2,1)S(1)} %shard_map.134.refs_8_), channel_id=1, source_target_pairs={{0,1},{1,0},{2,3},{3,2},{4,5},{5,4},{6,7},{7,6},{8,9},{9,8},{10,11... | collective-permute-start | bytes 196616 | tf_op jit(solution)/shard_map/ppermute | solution.py:416
  73.2 7.0 %collective-permute-start.19 = (bf16[256,128]{1,0:T(8,128)(2,1)S(1)}, bf16[256,128]{1,0:T(8,128)(2,1)S(1)}, u32[]{:S(2)}, u32[]{:S(2)}) collective-permute-start(bf16[256,128]{1,0:T(8,128)(2,1)S(1)} %get-tuple-element.94.refs_0_), channel_id=1, source_target_pairs={{0,2},{2,0},{1,3},{3,1},{4,6},{6,4},{5,7},{7,5},{8,10},{10,8},{9,1... | collective-permute-start | bytes 196616 | tf_op jit(solution)/shard_map/ppermute | solution.py:416
  74.7 5.5 %collective-permute-start.21 = (bf16[256,128]{1,0:T(8,128)(2,1)S(1)}, bf16[256,128]{1,0:T(8,128)(2,1)S(1)}, u32[]{:S(2)}, u32[]{:S(2)}) collective-permute-start(bf16[256,128]{1,0:T(8,128)(2,1)S(1)} %get-tuple-element.96.refs_2_), channel_id=1, source_target_pairs={{0,2},{2,0},{1,3},{3,1},{4,6},{6,4},{5,7},{7,5},{8,10},{10,8},{9,1... | collective-permute-start | bytes 196616 | tf_op jit(solution)/shard_map/ppermute | solution.py:416
  75.3 5.8 %collective-permute-start.20 = (bf16[256,128]{1,0:T(8,128)(2,1)S(1)}, bf16[256,128]{1,0:T(8,128)(2,1)S(1)}, u32[]{:S(2)}, u32[]{:S(2)}) collective-permute-start(bf16[256,128]{1,0:T(8,128)(2,1)S(1)} %get-tuple-element.95.refs_1_), channel_id=1, source_target_pairs={{0,2},{2,0},{1,3},{3,1},{4,6},{6,4},{5,7},{7,5},{8,10},{10,8},{9,1... | collective-permute-start | bytes 196616 | tf_op jit(solution)/shard_map/ppermute | solution.py:416
  76.8 5.7 %collective-permute-start.22 = (bf16[256,128]{1,0:T(8,128)(2,1)S(1)}, bf16[256,128]{1,0:T(8,128)(2,1)S(1)}, u32[]{:S(2)}, u32[]{:S(2)}) collective-permute-start(bf16[256,128]{1,0:T(8,128)(2,1)S(1)} %get-tuple-element.97.refs_3_), channel_id=1, source_target_pairs={{0,2},{2,0},{1,3},{3,1},{4,6},{6,4},{5,7},{7,5},{8,10},{10,8},{9,1... | collective-permute-start | bytes 196616 | tf_op jit(solution)/shard_map/ppermute | solution.py:416
  78.7 9.3 %collective-permute-start.18 = (bf16[128,512]{1,0:T(8,128)(2,1)S(1)}, bf16[128,512]{1,0:T(8,128)(2,1)S(1)}, u32[]{:S(2)}, u32[]{:S(2)}) collective-permute-start(bf16[128,512]{1,0:T(8,128)(2,1)S(1)} %get-tuple-element.93.refs_0_), channel_id=1, source_target_pairs={{0,2},{2,0},{1,3},{3,1},{4,6},{6,4},{5,7},{7,5},{8,10},{10,8},{9,1... | collective-permute-start | bytes 393224 | tf_op jit(solution)/shard_map/ppermute | solution.py:416

commit v3 on v0

v3 whole, which is shorter than its diff:
```python
import functools
import math

import jax
import jax.numpy as jnp
from jax import lax
from jax.experimental import pallas as pl
from jax.experimental.pallas import tpu as pltpu
from jax.sharding import PartitionSpec as P

HD = 128
PAGE = 128
SLOTS = 3
INNER = 3
ROWS = SLOTS * PAGE
LOG2E = math.log2(math.e)
SCALE = 1.0 / math.sqrt(HD)
BF16 = jnp.bfloat16
F32 = jnp.float32
I32 = jnp.int32
VMEM_LIMIT = 24 << 20
BLOCKED = 1e30


def dot_t(left, right):
    return lax.dot_general(left, right, (((1,), (1,)), ((), ())), preferred_element_type=F32)


def dot_n(left, right):
    return lax.dot_general(left, right, (((1,), (0,)), ((), ())), preferred_element_type=F32)


class Path:
    def __init__(self, ids_ref):
        self.pages = [ids_ref[j] for j in range(INNER)]
        self.own = ids_ref[INNER] - 1
        self.leaf = self.own // SLOTS
        self.core = lax.rem(self.leaf, 2)
        self.owns = [self.pages[j] == self.own for j in range(INNER)]
        self.has_inner = self.owns[0] | self.owns[1] | self.owns[2]

    def owner(self, level):
        return self.pages[level] // SLOTS

    def same(self, level, shift):
        return (self.owner(level) >> shift) == (self.leaf >> shift)

    def counts(self, counts_ref):
        return jnp.where(self.has_inner, counts_ref[0], 0), counts_ref[1], counts_ref[2]


def row_ok(count, rows, width):
    return lax.broadcasted_iota(I32, (rows, width), 0) < count


def kernel_call(body, ids, counts, near, far, outs, scratch=(), aliases=None, after=(), cost=None):
    smem = pl.BlockSpec(memory_space=pltpu.SMEM)
    vmem = pl.BlockSpec(memory_space=pltpu.VMEM)
    hbm = pl.BlockSpec(memory_space=pl.ANY)
    near = [pltpu.with_memory_space_constraint(a, pltpu.VMEM) for a in near]
    first = 2
    place = {("near", i): first + i for i in range(len(near))}
    place |= {("far", i): first + len(near) + i for i in range(len(far))}
    used = first + len(near) + len(far)

    def kernel(*refs):
        body(*refs[:used], *refs[used + len(after) :])

    return pl.pallas_call(
        kernel,
        out_shape=tuple(
            pltpu.VMEM(s, d) if inside else jax.ShapeDtypeStruct(s, d) for s, d, inside in outs
        ),
        in_specs=[smem] * 2 + [vmem] * len(near) + [hbm] * (len(far) + len(after)),
        out_specs=tuple(vmem if inside else hbm for _, _, inside in outs),
        scratch_shapes=list(scratch),
        input_output_aliases={place[k]: v for k, v in (aliases or {}).items()},
        compiler_params=pltpu.CompilerParams(vmem_limit_bytes=VMEM_LIMIT),
        cost_estimate=cost,
    )(ids, counts, *near, *far, *after)


def load_all(ids, counts, queries, grads, keys, values, norms, deltas, after=()):
    arrays = [queries, grads, keys, values, norms, deltas]
    cuts = []
    for n, a in enumerate(arrays):
        pieces = 4 if a.shape[1] >= 4096 else 1
        step = a.shape[1] // pieces
        cuts += [(n, i * step, step) for i in range(pieces)]

    def body(ids_ref, counts_ref, *refs):
        src, dst, sem = refs[: len(arrays)], refs[len(arrays) : 2 * len(arrays)], refs[-1]
        copies = [
            pltpu.make_async_copy(
                src[n].at[:, start : start + size], dst[n].at[:, start : start + size], sem.at[i]
            )
            for i, (n, start, size) in enumerate(cuts)
        ]
        for c in copies:
            c.start()
        for c in copies:
            c.wait()
        norm = dst[4]
        lane = lax.broadcasted_iota(I32, norm.shape, 1)
        n0, n1, n2 = Path(ids_ref).counts(counts_ref)
        limit = jnp.where(lane < PAGE, n0, jnp.where(lane < 2 * PAGE, n1, n2))
        norm[...] = jnp.where(lane % PAGE < limit, norm[...] * (1.0 / SCALE), BLOCKED)

    return kernel_call(
        body, ids, counts, [], arrays, [(a.shape, a.dtype, True) for a in arrays],
        [pltpu.SemaphoreType.DMA((len(cuts),))], after=after,
    )


def row_terms(rows):
    high = rows.astype(BF16).astype(F32)
    rest = rows - high
    middle = rest.astype(BF16).astype(F32)
    parts = [high, middle, rest - middle]
    spare = HD - 3 * rows.shape[0]
    parts.append(jnp.zeros((spare, rows.shape[1]), F32))
    return jnp.concatenate(parts, axis=0).T.astype(BF16)


class Head:
    def __init__(self, kv, group, q, g, norms, deltas, en, ed):
        self.kv, self.group, self.q, self.g, self.en, self.ed = kv, group, q, g, en, ed
        self.heads = min(4, group)
        heads = slice(kv * group, (kv + 1) * group)
        en[...] = row_terms(norms[heads, :])
        ed[...] = row_terms(deltas[heads, :])

    def lanes(self, part, j):
        at = self.kv * self.group * HD + part * (self.heads * HD) + j * HD
        return pl.ds(pl.multiple_of(at, HD), HD)

    def stacked(self, ref, part, slot):
        rows = slice(slot * PAGE, (slot + 1) * PAGE)
        return jnp.concatenate(
            [ref[rows, self.lanes(part, j)] for j in range(self.heads)], axis=0
        )

    def deep(self, stacked, terms, part, slot):
        rows = slice(slot * PAGE, (slot + 1) * PAGE)
        column = lax.broadcasted_iota(I32, (1, HD), 1) % self.group
        extra = [
            terms[rows] * (column == part * self.heads + j).astype(F32).astype(BF16)
            for j in range(self.heads)
        ]
        return jnp.concatenate([stacked, jnp.concatenate(extra, axis=0)], axis=1)

    def scores(self, part, slot, qs, gs, k_deep, v_deep, keep):
        p = keep(jnp.exp2(dot_n(self.deep(qs, self.en, part, slot), k_deep) * (SCALE * LOG2E)))
        ds = p * dot_n(self.deep(gs, self.ed, part, slot), v_deep)
        return p.astype(BF16), ds.astype(BF16)

    def turned_at(self, part, slot):
        wide = self.heads * PAGE
        parts = self.group // self.heads
        at = ((self.kv * parts + part) * SLOTS + slot) * wide
        return pl.ds(pl.multiple_of(at, wide), wide)

    def put_queries(self, part, slot, rows_by_head, dq, prev, stage):
        rows = slice(slot * PAGE, (slot + 1) * PAGE)
        for j in range(self.heads):
            value = rows_by_head[j * PAGE : (j + 1) * PAGE]
            if stage is None:
                dq[rows, self.lanes(part, j)] = value
            else:
                if prev is not None:
                    value = value + prev[rows, self.lanes(part, j)]
                stage[rows, j * HD : (j + 1) * HD] = (value * SCALE).astype(BF16)


def set_keys(deep, upright, at, page):
    where = slice(at * PAGE, (at + 1) * PAGE)
    deep[:HD, where] = page.T
    if upright is not None:
        upright[where] = page


def run_heads(kvs, group, finish, one_part, stage, sem, gq):
    parts = group // min(4, group)
    wide = min(4, group) * HD
    copies = []
    for n, kv in enumerate(kvs):
        setup, part_body, end = one_part(n, kv)
        setup()

        def step(part, _, n=n, kv=kv, part_body=part_body):
            slot = n * parts + part
            done = finish[n]
            part_body(part, stage.at[slot] if done else None)
            if done:
                at = pl.multiple_of((kv * parts + part) * wide, wide)
                pltpu.make_async_copy(
                    stage.at[slot], gq.at[:, pl.ds(at, wide)], sem.at[slot]
                ).start()
            return 0

        lax.fori_loop(0, parts, step, 0)
        end()
        if finish[n]:
            copies += [(n * parts + p, (kv * parts + p) * wide) for p in range(parts)]
    for slot, at in copies:
        pltpu.make_async_copy(
            stage.at[slot], gq.at[:, at : at + wide], sem.at[slot]
        ).wait()


def cost(blocks, heads):
    return pl.CostEstimate(
        flops=40 * blocks * PAGE * PAGE * HD * heads,
        bytes_accessed=4 * heads * HD * ROWS,
        transcendentals=blocks * PAGE * PAGE * heads,
    )


def attend(own, kvs, group, ids, counts, loaded, pages, state, w=None, after=()):
    q, g, k, v, norms, deltas = loaded
    count = len(kvs)
    parts = group // min(4, group)
    width = count * HD
    finish = [kv in state["done"] for kv in kvs]
    fresh = [kv not in state["done"] for kv in kvs]
    kv_total = k.shape[1] // HD
    names = ["dq", "qt", "gt", "gq"]
    full = {
        "dq": (q.shape, F32, True),
        "qt": ((HD, kv_total * group * ROWS), BF16, True),
        "gt": ((HD, kv_total * group * ROWS), BF16, True),
        "gq": (q.shape, BF16, False),
    }
    if not any(finish):
        names.remove("gq")
    near = [q, g, norms, deltas, *pages]
    if own:
        near += [k, v]
    far, aliases, outs = [], {}, []
    for name in names:
        outs.append(full[name])
        array = state.get(name)
        if array is None:
            continue
        if full[name][2]:
            aliases["near", len(near)] = len(outs) - 1
            near.append(array)
        else:
            aliases["far", len(far)] = len(outs) - 1
            far.append(array)
    if own:
        outs += [
            ((2 * PAGE, width), BF16, True),
            ((2 * PAGE, width), BF16, True),
            ((2, PAGE, width), F32, True),
            ((2, PAGE, width), BF16, True),
        ]
        keys_in = 4
    else:
        outs += [((2, PAGE, width), F32, True), ((2, PAGE, width), BF16, True)]
        keys_in = 2
    if w is not None:
        far.append(w)
        outs.append((w.shape, w.dtype, True))
    scratch = [
        pltpu.VMEM((2 * HD, keys_in * PAGE), BF16),
        pltpu.VMEM((2 * HD, keys_in * PAGE), BF16),
        pltpu.VMEM((keys_in * PAGE, HD), BF16),
        pltpu.VMEM((2, HD, keys_in * PAGE), F32),
        pltpu.VMEM((ROWS, HD), BF16),
        pltpu.VMEM((ROWS, HD), BF16),
        pltpu.VMEM((count * parts, ROWS, min(4, group) * HD), BF16),
        pltpu.SemaphoreType.DMA((count * parts + 1,)),
    ]

    def body(ids_ref, counts_ref, q, g, norms, deltas, *refs):
        k_deep, v_deep, k_up, acc, en, ed, stage, sem = refs[-8:]
        out_refs = refs[-8 - len(outs) : -8]
        held = dict(zip(names, out_refs))
        results = out_refs[len(names) :]
        path = Path(ids_ref)
        if w is not None:
            w_copy = pltpu.make_async_copy(
                refs[-8 - len(outs) - 1], results[-1], sem.at[count * parts]
            )
            w_copy.start()
        k_deep[HD:] = jnp.full((HD, keys_in * PAGE), -1.0, BF16)
        v_deep[HD:] = jnp.full((HD, keys_in * PAGE), -1.0, BF16)
        tall = min(4, group) * PAGE
        tri = lax.broadcasted_iota(I32, (tall, PAGE), 1) <= (
            lax.broadcasted_iota(I32, (tall, PAGE), 0) % PAGE
        )
        cols = lambda a, b: slice(a * PAGE, b * PAGE)

        def one_part(n, kv):
            head = Head(kv, group, q, g, norms, deltas, en, ed)
            lane = slice(kv * HD, (kv + 1) * HD)
            here = slice(n * HD, (n + 1) * HD)

            def setup_own():
                l2_own, l2_far, k, v = refs[:4]
                zero = jnp.zeros((), BF16)
                for slot, (at, c) in enumerate(zip((3, 0, 2), path.counts(counts_ref))):
                    ok = row_ok(c, PAGE, HD)
                    set_keys(k_deep, k_up, at, jnp.where(ok, k[cols(slot, slot + 1), lane], zero))
                    set_keys(v_deep, None, at, jnp.where(ok, v[cols(slot, slot + 1), lane], zero))
                mine = path.owns[2]
                set_keys(k_deep, k_up, 1, jnp.where(mine, l2_own[0, :, lane], l2_far[0, :, lane]))
                set_keys(v_deep, None, 1, jnp.where(mine, l2_own[1, :, lane], l2_far[1, :, lane]))
                acc[...] = jnp.zeros_like(acc)

            def setup_shared():
                mine, theirs = refs[:2]
                leads = path.core == 0
                for j in range(2):
                    near_page, far_page = mine[j, :, lane], theirs[j, :, lane]
                    set_keys(k_deep, k_up, j, jnp.where(leads, near_page, far_page))
                    set_keys(v_deep, None, j, jnp.where(leads, far_page, near_page))
                acc[...] = jnp.zeros_like(acc)

            def keep_own(slot):
                def keep(p):
                    masked = jnp.where(tri, p[:, :PAGE] if slot != 2 else p[:, 2 * PAGE :], 0.0)
                    if slot == 0:
                        return masked
                    if slot == 1:
                        return jnp.concatenate([masked, p[:, PAGE:]], axis=1)
                    return jnp.concatenate([p[:, : 2 * PAGE], masked], axis=1)

                return keep

            limit = jnp.where(path.owns[2], 2 * PAGE, jnp.where(path.owns[1], PAGE, 0))

            def keep_shared(slot):
                if slot:
                    return lambda p: p
                column = lax.broadcasted_iota(I32, (tall, 2 * PAGE), 1)
                return lambda p: jnp.where(column < limit, p, 0.0)

            spans = {0: cols(3, 4), 1: cols(0, 2), 2: cols(0, 3)} if own else dict.fromkeys(
                range(SLOTS), cols(0, 2)
            )

            def part_body(part, stage_ref):
                for slot in range(SLOTS):
                    span = spans[slot]
                    qs, gs = head.stacked(q, part, slot), head.stacked(g, part, slot)
                    keep = (keep_own if own else keep_shared)(slot)
                    p, ds = head.scores(
                        part, slot, qs, gs, k_deep[:, span], v_deep[:, span], keep
                    )
                    turn = head.turned_at(part, slot)
                    if fresh[n]:
                        qt, gt = qs.T, gs.T
                        held["qt"][:, turn] = qt
                        held["gt"][:, turn] = gt
                    else:
                        qt, gt = held["qt"][:, turn], held["gt"][:, turn]
                    acc[0, :, span] += dot_n(qt, ds)
                    acc[1, :, span] += dot_n(gt, p)
                    head.put_queries(
                        part, slot, dot_n(ds, k_up[span]), held["dq"],
                        None if fresh[n] else held["dq"], stage_ref,
                    )

            def end_own():
                dk12, dv12, own0, send2 = results[:4]
                grad = [acc[0].T * SCALE, acc[1].T]
                for at, c, to in ((0, counts_ref[1], 0), (2, counts_ref[2], 1)):
                    ok = row_ok(c, PAGE, HD)
                    for kind, out in ((0, dk12), (1, dv12)):
                        out[cols(to, to + 1), here] = jnp.where(
                            ok, grad[kind][cols(at, at + 1)], 0.0
                        ).astype(BF16)
                for kind in range(2):
                    level2 = grad[kind][cols(1, 2)]
                    own0[kind, :, here] = grad[kind][cols(3, 4)] + jnp.where(
                        path.owns[2], level2, 0.0
                    )
                    send2[kind, :, here] = level2.astype(BF16)

            def end_shared():
                kept, sent = results[:2]
                leads = path.core == 0
                grad_k, grad_v = acc[0].T * SCALE, acc[1].T
                for j in range(2):
                    a, b = grad_k[cols(j, j + 1)], grad_v[cols(j, j + 1)]
                    kept[j, :, here] = jnp.where(leads, a, b)
                    sent[j, :, here] = jnp.where(leads, b, a).astype(BF16)

            if own:
                return setup_own, part_body, end_own
            return setup_shared, part_body, end_shared

        run_heads(kvs, group, finish, one_part, stage, sem, held.get("gq"))
        if w is not None:
            w_copy.wait()

    made = kernel_call(
        body, ids, counts, near, far, outs, scratch, aliases, after,
        cost(6, group * count),
    )
    for name, array in zip(names, made):
        state[name] = array
    state["done"] = state["done"] | set(kvs)
    return made[len(names) :]


def input_grad(ids, counts, near, far, side, w, rows, carry):
    out_cols, depth = w.shape
    tile = next(t for t in (640, 512, 320, 128, out_cols) if out_cols % t == 0)
    top = 0 if rows == PAGE else PAGE
    count = len(near)
    steps = out_cols // tile
    pieces = [*near, *(far or [])]

    def body(_, counts_ref, w_ref, *refs):
        flag, out, stage, sem = refs[-4:]
        mine = jnp.concatenate([r[...] for r in refs[:count]], axis=1)
        if far:
            other = jnp.concatenate([r[...] for r in refs[count : 2 * count]], axis=1)
            leads = flag[0] == 0
            left = jnp.where(leads, mine, other)
            right = jnp.where(leads, other, mine)
            mine = jnp.concatenate([left, right], axis=1)
        copies = []
        for i in range(steps):
            at = slice(i * tile, (i + 1) * tile)
            stage[i] = dot_t(mine, w_ref[at]).astype(BF16)
            copies.append(
                pltpu.make_async_copy(stage.at[i], out.at[top : top + rows, at], sem.at[i])
            )
            copies[-1].start()
        for c in copies:
            c.wait()

    used = 1 + len(pieces)
    vmem = pl.BlockSpec(memory_space=pltpu.VMEM)
    smem = pl.BlockSpec(memory_space=pltpu.SMEM)
    hbm = pl.BlockSpec(memory_space=pl.ANY)
    more = [] if carry is None else [carry]

    def kernel(ids_ref, counts_ref, *refs):
        body(ids_ref, counts_ref, *refs[:used], refs[used], *refs[used + 1 + len(more) :])

    return pl.pallas_call(
        kernel,
        out_shape=jax.ShapeDtypeStruct((ROWS, out_cols), BF16),
        in_specs=[smem] * 2 + [vmem] * used + [smem] + [hbm] * len(more),
        out_specs=hbm,
        scratch_shapes=[
            pltpu.VMEM((steps, rows, tile), BF16),
            pltpu.SemaphoreType.DMA((steps,)),
        ],
        input_output_aliases={} if carry is None else {2 + used + 1: 0},
        compiler_params=pltpu.CompilerParams(vmem_limit_bytes=VMEM_LIMIT),
        cost_estimate=pl.CostEstimate(
            flops=4 * rows * depth * out_cols,
            bytes_accessed=2 * (depth * out_cols + rows * out_cols),
            transcendentals=0,
        ),
    )(
        ids, counts, pltpu.with_memory_space_constraint(w, pltpu.VMEM), *pieces, side, *more
    )


def flipped(block, axis, bit):
    count = lax.axis_size(axis)
    return lax.ppermute(block, axis, [(i, i ^ bit) for i in range(count) if i ^ bit < count])


def spanning(leaves, bit_index):
    return len([j for j in range(INNER) if 2 << bit_index <= leaves >> j])


def own_shared_page(ids, counts, keys, values):
    width = keys.shape[1]

    def body(_, counts_ref, k_ref, v_ref, out, held, sem):
        copies = [
            pltpu.make_async_copy(ref.at[:PAGE], held.at[i], sem.at[i])
            for i, ref in enumerate((k_ref, v_ref))
        ]
        for c in copies:
            c.start()
        for c in copies:
            c.wait()
        ok = row_ok(counts_ref[0], PAGE, width)
        for i in range(2):
            out[i] = jnp.where(ok, held[i], jnp.zeros((), BF16))

    (own,) = kernel_call(
        body, ids, counts, [], [keys, values], [((2, PAGE, width), BF16, True)],
        [pltpu.VMEM((2, PAGE, width), BF16), pltpu.SemaphoreType.DMA((2,))],
    )
    return own


def gather_small_tree(ids, counts, own, width, beside_pair, beside_half):
    page = ((PAGE, width), BF16, True)
    from_core = flipped(own, "sub", 1)

    def choose_chip(ids_ref, _, own_ref, far_ref, out):
        path = Path(ids_ref)
        for kind in range(2):
            for mine in (False, True):

                @pl.when((path.core == kind) & (path.owns[2] != mine))
                def _copy(kind=kind, mine=mine):
                    out[...] = (own_ref if mine else far_ref)[kind]

    (chip,) = kernel_call(choose_chip, ids, counts, [own, from_core], [], [page])
    from_pair = flipped(chip, "leaf", 1)

    def choose_pair(ids_ref, _, near_ref, far_ref, out):
        path = Path(ids_ref)
        out[...] = jnp.where(path.same(0, 1), near_ref[...], far_ref[...])

    after = beside_pair(from_core, chip)
    (pair,) = kernel_call(choose_pair, ids, counts, [chip, from_pair], [], [page], after=after)
    from_half = flipped(pair, "leaf", 2)

    def choose_all(ids_ref, _, chip_ref, pair_far, pair_ref, half_far, out):
        path = Path(ids_ref)
        out[0] = jnp.where(path.same(0, 2), pair_ref[...], half_far[...])
        out[1] = jnp.where(path.same(1, 1), chip_ref[...], pair_far[...])

    after = beside_half(pair)
    (mine,) = kernel_call(
        choose_all, ids, counts, [chip, from_pair, pair, from_half], [],
        [((2, PAGE, width), BF16, True)], after=after,
    )
    return mine, flipped(mine, "sub", 1)


class Reduction:
    def __init__(self, ids, counts, kept, sent):
        self.ids, self.counts, self.kept = ids, counts, kept
        self.width = kept.shape[-1]
        self.far = flipped(sent, "sub", 1)

    def call(self, body, near, outs, after):
        return kernel_call(body, self.ids, self.counts, near, [], outs, after=after)

    def over_cores(self, after=()):
        def body(_, __, near, away, total, low):
            value = near[...] + away[...].astype(F32)
            total[...] = value
            low[...] = value.astype(BF16)

        two = (2, PAGE, self.width)
        self.total, low = self.call(
            body, [self.kept, self.far], [(two, F32, True), (two, BF16, True)], after
        )
        self.far = flipped(low, "leaf", 1)
        return low

    def over_pair(self, after=()):
        def body(_, __, near, away, total, low):
            value = near[...] + away[...].astype(F32)
            total[...] = value
            low[...] = value[0].astype(BF16)

        two = (2, PAGE, self.width)
        self.total, low = self.call(
            body, [self.total, self.far], [(two, F32, True), ((PAGE, self.width), BF16, True)],
            after,
        )
        self.far = flipped(low, "leaf", 2)
        return low

    def over_half(self, after=()):
        def body(ids_ref, _, near, away, out):
            path = Path(ids_ref)
            root = near[0] + away[...].astype(F32)
            out[...] = jnp.where(path.same(0, 1), root, near[1]).astype(BF16)

        (self.mine,) = self.call(
            body, [self.total, self.far], [((PAGE, self.width), BF16, True)], after
        )
        self.far = flipped(self.mine, "sub", 1)
        return self.mine


def place_own_pages(ids, counts, parts):
    width = sum(k.shape[1] for k, _ in parts)
    near = [k for k, _ in parts] + [v for _, v in parts]

    def body(_, __, *refs):
        outs, held, sem = refs[-4:-2], refs[-2], refs[-1]
        copies = []
        for kind in range(2):
            at = 0
            for r in refs[kind * len(parts) : (kind + 1) * len(parts)]:
                held[kind, :, at : at + r.shape[1]] = r[...]
                at += r.shape[1]
            copies.append(
                pltpu.make_async_copy(held.at[kind], outs[kind].at[PAGE:], sem.at[kind])
            )
            copies[-1].start()
        for c in copies:
            c.wait()

    full = ((ROWS, width), BF16, False)
    return kernel_call(
        body, ids, counts, near, [], [full, full],
        [pltpu.VMEM((2, 2 * PAGE, width), BF16), pltpu.SemaphoreType.DMA((2,))],
    )


def finish_small_tree(ids, counts, own0, far2, mine, far, dk, dv):
    width = dk.shape[1]

    def columns(refs, at):
        for r in refs:
            if at < r.shape[-1]:
                return r, slice(at, at + HD)
            at -= r.shape[-1]

    def body(ids_ref, counts_ref, *refs):
        groups, start = [], 0
        for arrays in (own0, far2, mine, far):
            groups.append(refs[start : start + len(arrays)])
            start += len(arrays)
        dk_out, dv_out, dv0_out, held, sem = refs[-5:]
        path = Path(ids_ref)
        leads = path.core == 0
        ok = row_ok(path.counts(counts_ref)[0], PAGE, HD)
        for at in range(0, width, HD):
            own_r, c = columns(groups[0], at)
            base = [own_r[0, :, c], own_r[1, :, c]]
            low_r, c = columns(groups[1], at)
            low = [low_r[0, :, c], low_r[1, :, c]]
            near_r, c = columns(groups[2], at)
            far_r, _ = columns(groups[3], at)
            near, away = near_r[:, c], far_r[:, c]
            gained = [jnp.where(leads, near, away), jnp.where(leads, away, near)]
            for kind in range(2):
                more = jnp.where(path.owns[2], low[kind], gained[kind]).astype(F32)
                total = jnp.where(ok, base[kind] + more, 0.0).astype(BF16)
                held[kind, :, at : at + HD] = total
                if kind:
                    dv0_out[:, at : at + HD] = total
        copies = [
            pltpu.make_async_copy(held.at[i], out.at[:PAGE], sem.at[i])
            for i, out in enumerate((dk_out, dv_out))
        ]
        for c in copies:
            c.start()
        for c in copies:
            c.wait()

    full = ((ROWS, width), BF16, False)
    return kernel_call(
        body, ids, counts, [*own0, *far2, *mine, *far], [dk, dv],
        [full, full, ((PAGE, width), BF16, True)],
        [pltpu.VMEM((2, PAGE, width), BF16), pltpu.SemaphoreType.DMA((2,))],
        aliases={("far", 0): 0, ("far", 1): 1},
    )


def gather_tree(ids, own):
    leaves = lax.axis_size(("leaf", "sub"))
    owned = ids[:INNER] == ids[INNER] - 1
    pages = jnp.where(owned[:, None, None, None], own[None], jnp.zeros((), BF16))
    for bit in range(leaves.bit_length() - 1):
        active = spanning(leaves, bit)
        far = flipped(pages[:active], ("leaf", "sub"), 1 << bit)
        pages = jnp.concatenate([pages[:active] + far, pages[active:]])
    return pages


def reduce_tree(ids, parts):
    leaves = lax.axis_size(("leaf", "sub"))
    for bit in range(leaves.bit_length() - 1):
        active = spanning(leaves, bit)
        far = flipped(parts[:active], ("leaf", "sub"), 1 << bit)
        parts = jnp.concatenate([parts[:active] + far, parts[active:]])
    owned = ids[:INNER] == ids[INNER] - 1
    return jnp.sum(jnp.where(owned[:, None, None, None], parts, 0.0), axis=0)


def on_device(queries, grad_out, keys, values, log_norms, row_deltas, ancestors, counts, w_value):
    width = keys.shape[1]
    kv = width // HD
    group = queries.shape[1] // width
    leaves = lax.axis_size(("leaf", "sub"))
    hbm = lambda a: pltpu.with_memory_space_constraint(a, pltpu.HBM)
    ids = hbm(ancestors[0])
    rows_of = hbm(counts[0])
    side = lax.axis_index("tensor").astype(I32).reshape(1)
    two_sides = lax.axis_size("tensor") == 2
    queries, grad_out, keys, values, log_norms, row_deltas, w_value = map(
        hbm, (queries, grad_out, keys, values, log_norms, row_deltas, w_value)
    )
    state = {"done": frozenset()}
    loaded = []
    outcome = {}

    def load(after=()):
        loaded.extend(
            load_all(
                ids, rows_of, queries, grad_out, keys, values, log_norms, row_deltas, after
            )
        )

    def own_pages(kvs, pages, after=()):
        outcome["own", kvs] = attend(
            True, kvs, group, ids, rows_of, loaded, pages, state, after=after
        )
        return outcome["own", kvs]

    def shared_pages(kvs, pages, after=(), w=None):
        outcome["shared", kvs] = attend(
            False, kvs, group, ids, rows_of, loaded, pages, state, w, after
        )
        return outcome["shared", kvs]

    def spread(part):
        if two_sides:
            return flipped(part, "tensor", 1)
        return lax.all_gather(part, "tensor", axis=1, tiled=True)

    own = own_shared_page(ids, rows_of, keys, values)
    if leaves == 8 and lax.axis_size("sub") == 2 and kv == 4 and two_sides:
        level2 = []

        def beside_pair(from_core, chip):
            load((chip,))
            level2.extend((own, from_core))
            return (own_pages((0,), level2)[3],)

        def beside_half(pair):
            return (own_pages((1, 2), level2, (pair,))[3],)

        mine, theirs = gather_small_tree(ids, rows_of, own, width, beside_pair, beside_half)
        shared = (mine, theirs)
        first = [(0,), (1, 2)]
        far_v = [spread(outcome["own", c][1]) for c in first]
        far2 = [flipped(outcome["own", c][3], "sub", 1) for c in first]
        kept, sent, w_near = shared_pages((0, 1), shared, w=w_value)
        lead = Reduction(ids, rows_of, kept, sent)
        kept, sent = shared_pages((2, 3), shared, (*far_v, *far2))
        tail = Reduction(ids, rows_of, kept, sent)
        lead.over_cores((kept,))
        low = tail.over_cores()
        last = own_pages((3,), level2, (low,))
        far_v.append(spread(last[1]))
        far2.append(flipped(last[3], "sub", 1))
        lead.over_pair((last[3],))
        low = tail.over_pair((last[3],))
        cuts = [*first, (3,)]
        dk, dv = place_own_pages(
            ids, rows_of, [outcome["own", c][:2] for c in cuts]
        )
        lead.over_half()
        tail.over_half()
        grad_keys, grad_values, dv0 = finish_small_tree(
            ids, rows_of, [outcome["own", c][2] for c in cuts], far2,
            [lead.mine, tail.mine], [lead.far, tail.far], dk, dv,
        )
        near_v = [outcome["own", c][1] for c in cuts]
        far0 = spread(dv0)
        grad_input = input_grad(ids, rows_of, near_v, far_v, side, w_near, 2 * PAGE, None)
        grad_input = input_grad(ids, rows_of, [dv0], [far0], side, w_near, PAGE, grad_input)
        return (state["gq"], grad_keys, grad_values, grad_input)

    kvs = tuple(range(kv))
    first = lax.axis_index("sub") == 0
    path_ids = ancestors[0]
    pages = gather_tree(path_ids, own)
    load()
    dk12, dv12, own0, send2 = own_pages(kvs, (pages[2], pages[2]))
    kept, sent, w_near = shared_pages(
        kvs,
        (
            jnp.where(first, pages[:2, 0], pages[:2, 1]),
            jnp.where(first, pages[:2, 1], pages[:2, 0]),
        ),
        w=w_value,
    )
    sent = sent.astype(F32)
    upper = jnp.stack([jnp.where(first, kept, sent), jnp.where(first, sent, kept)], axis=1)
    low = send2.astype(F32)
    total = reduce_tree(path_ids, jnp.concatenate([upper, low[None]]))
    total += own0 - jnp.where(path_ids[2] == path_ids[INNER] - 1, low, 0.0)
    has = jnp.any(path_ids[:INNER] == path_ids[INNER] - 1)
    ok = (jnp.arange(PAGE) < jnp.where(has, counts[0, 0], 0))[:, None]
    total = jnp.where(ok, total, 0.0).astype(BF16)
    dk, dv = place_own_pages(ids, rows_of, [(dk12, dv12)])
    grad_keys = lax.dynamic_update_slice(dk, total[0], (0, 0))
    grad_values = lax.dynamic_update_slice(dv, total[1], (0, 0))
    if two_sides:
        pair = lambda part: ([part], [spread(part)])
    else:
        pair = lambda part: ([spread(part)], None)
    grad_input = input_grad(ids, rows_of, *pair(dv12), side, w_near, 2 * PAGE, None)
    grad_input = input_grad(ids, rows_of, *pair(total[1]), side, w_near, PAGE, grad_input)
    return (state["gq"], grad_keys, grad_values, grad_input)


def solution(mesh):
    placed = (
        P(("groups", "leaf", "sub"), "tensor"),
        P(("groups", "leaf", "sub"), "tensor"),
        P(("groups", "leaf", "sub"), "tensor"),
        P(("groups", "leaf", "sub"), "tensor"),
        P("tensor", ("groups", "leaf", "sub")),
        P("tensor", ("groups", "leaf", "sub")),
        P(("groups", "leaf", "sub"), None),
        P(("groups", "leaf", "sub"), None),
        P("tensor", None),
    )
    return jax.shard_map(
        on_device,
        mesh=mesh,
        in_specs=placed,
        out_specs=(
            P(("groups", "leaf", "sub"), "tensor"),
            P(("groups", "leaf", "sub"), "tensor"),
            P(("groups", "leaf", "sub"), "tensor"),
            P(("groups", "leaf", "sub"), "tensor"),
        ),
        check_vma=False,
    )
```

time: 212 us -> 83.9 us (0.40)
  matrix products: 62.6 us -> 0 us
  Pallas kernels: 0 us -> 54 us
  local copies, waits for them, and re-layouts: 58.8 us -> 4.82 us
  waiting for transfers between devices: 30 us -> 6.29 us
  blocking collectives: 20.1 us -> 0 us
  other arithmetic: 17.4 us -> 0.01 us
  between operations: 16.9 us -> 1.08 us
  starting transfers between devices: 4.84 us -> 17.3 us
    dot_general x11 -> x0, matrix products: 62.6 us -> none  [the longest x2 15.1 us: attend(): jnp.einsum('rkgd,nkd->kgrn', grad_rows, value_rows, preferred_element_typ...]
    pallas_call x0 -> x20, Pallas kernels: none -> 54 us  [the longest x18 47.4 us: kernel_call(): pl.pallas_call(kernel, out_shape=tuple((pltpu.VMEM(s, d) if inside else j...]
    slice x22 -> x0, local copies, waits for them, and re-layouts: 21.9 us -> none  [the longest x1 3.18 us: on_device(): grad_out[PAGE:].reshape(2 * PAGE, kv_local, group_size, HD)]
    all_gather x2 -> x0, blocking collectives: 20.1 us -> none  [the longest x1 10.6 us: on_device(): lax.all_gather(page_counts[:1], ('leaf', 'sub'), axis=0, tiled=True)]
    ppermute x6 -> x19, starting transfers between devices: 4.76 us -> 17.3 us  [flipped(): lax.ppermute(block, axis, [(i, i ^ bit) for i in range(count) if i ^ bit...]
    all_gather x2 -> x0, waiting for transfers between devices: 12 us -> none  [the longest x1 12 us: on_device(): lax.all_gather(value_pages[:1], ('leaf', 'sub'), axis=0, tiled=True)]
    another operation x5 -> x0, local copies, waits for them, and re-layouts: 11.7 us -> none
    ppermute x6 -> x19, waiting for transfers between devices: 17.9 us -> 6.29 us  [flipped(): lax.ppermute(block, axis, [(i, i ^ bit) for i in range(count) if i ^ bit...]
  transfers between devices with their start and end apart: 8 -> 19, of which waited for: 3 -> 3; matrix products, arithmetic and copies ran while one was open for 24% -> 0% of each run, Pallas kernels for 0% -> 48%
where the time goes in v3:
time: 83.9 us; the launch traced here: 83.4 us
  Pallas kernels  54 us (64%)
  starting transfers between devices  17.3 us (21%)
  waiting for transfers between devices  6.29 us (7%)
  local copies, waits for them, and re-layouts  4.82 us (6%)
  between operations  1.08 us (1%)
    pallas_call x18, Pallas kernels, kernel_call(): pl.pallas_call(kernel, out_shape=tuple((pltpu.VMEM(s, d) if inside else j...  47.4 us
    ppermute x19, starting transfers between devices, flipped(): lax.ppermute(block, axis, [(i, i ^ bit) for i in range(count) if i ^ bit...  17.3 us
    pallas_call x2, Pallas kernels, input_grad(): pl.pallas_call(kernel, out_shape=jax.ShapeDtypeStruct((ROWS, out_cols), B...  6.51 us
    ppermute x19, waiting for transfers between devices, flipped(): lax.ppermute(block, axis, [(i, i ^ bit) for i in range(count) if i ^ bit...  6.29 us
    unnamed x8, local copies, waits for them, and re-layouts  4.82 us
  transfers between devices with their start and end apart: 19, of which 3 were waited for; matrix products, arithmetic and copies ran while one was open for 0% of the time, Pallas kernels for 48%

profile of v3, /device:TPU:0, one launch (start us, length us, event | category | flops | bytes accessed | tf_op | source)
XLA Modules:
  0.0 83.4 jit_solution(17268775069649827993)
XLA Ops:
  0.6 1.7 %shard_map.120.refs_2_.refs_6_ = bf16[2,128,512]{2,1,0:T(8,128)(2,1)S(1)} custom-call(s32[5]{0:T(128)} %bitcast.5, s32[3]{0:T(128)} %bitcast.25, bf16[384,512]{1,0:T(8,128)(2,1)} %refs_4_.1, bf16[384,512]{1,0:T(8,128)(2,1)} %refs_5_.1), custom_call_target="tpu_custom_call" | custom-call | tf_op jit(solution)/shard_map/pallas_call | solution.py:69
  2.3 0.5 collective-permute-start
  2.8 1.2 %collective-permute-done.refs_3_.refs_7_ = bf16[2,128,512]{2,1,0:T(8,128)(2,1)S(1)} collective-permute-done((bf16[2,128,512]{2,1,0:T(8,128)(2,1)S(1)}, bf16[2,128,512]{2,1,0:T(8,128)(2,1)S(1)}, u32[]{:S(2)}, u32[]{:S(2)}) %collective-permute-start) | collective-permute-done | bytes 262176 | tf_op jit(solution)/shard_map/ppermute | solution.py:469
  4.0 0.7 shard_map.121.refs_8_.refs_2_
  4.7 3.0 %collective-permute-start.1 = (bf16[128,512]{1,0:T(8,128)(2,1)S(1)}, bf16[128,512]{1,0:T(8,128)(2,1)S(1)}, u32[]{:S(2)}, u32[]{:S(2)}) collective-permute-start(bf16[128,512]{1,0:T(8,128)(2,1)S(1)} %shard_map.121.refs_8_.refs_2_), channel_id=1, source_target_pairs={{0,4},{4,0},{8,12},{12,8},{1,5},{5,1},{9,13},{13,9},{2,6},{6,2},{1... | collective-permute-start | bytes 393224 | tf_op jit(solution)/shard_map/ppermute | solution.py:469
  7.7 3.8 %shard_map.122 = (bf16[384,4096]{1,0:T(8,128)(2,1)S(1)}, bf16[384,4096]{1,0:T(8,128)(2,1)S(1)}, bf16[384,512]{1,0:T(8,128)(2,1)S(1)}, bf16[384,512]{1,0:T(8,128)...) custom-call(s32[5]{0:T(128)} %bitcast.7, s32[3]{0:T(128)} %bitcast.27, bf16[384,4096]{1,0:T(8,128)(2,1)} %refs_2_.3, ...), custom_call_target="tpu_custom_call" | custom-call | tf_op jit(solution)/shard_map/pallas_call | solution.py:69
  11.5 4.5 %shard_map.123 = (f32[384,4096]{1,0:T(8,128)S(1)}, bf16[128,12288]{1,0:T(8,128)(2,1)S(1)}, bf16[128,12288]{1,0:T(8,128)(2,1)S(1)}, bf16[256,128]{1,0:T(8,128)(2,...) custom-call(s32[5]{0:T(128)} %bitcast.8, s32[3]{0:T(128)} %bitcast.28, ...), custom_call_target="tpu_custom_call" | custom-call | flops 4026531840 | bytes 1572864 | tf_op jit(solution)/shard_map/pallas_call | solution.py:69
  16.1 0.0 collective-permute-done.1.refs_3_
  16.1 0.7 shard_map.124.refs_13_.refs_4_
  16.8 2.6 %collective-permute-start.2 = (bf16[128,512]{1,0:T(8,128)(2,1)S(1)}, bf16[128,512]{1,0:T(8,128)(2,1)S(1)}, u32[]{:S(2)}, u32[]{:S(2)}) collective-permute-start(bf16[128,512]{1,0:T(8,128)(2,1)S(1)} %shard_map.124.refs_13_.refs_4_), channel_id=1, source_target_pairs={{0,8},{4,12},{8,0},{12,4},{1,9},{5,13},{9,1},{13,5},{2,10},{6,14},... | collective-permute-start | bytes 393224 | tf_op jit(solution)/shard_map/ppermute | solution.py:469
  19.4 8.2 %shard_map.125 = (f32[384,4096]{1,0:T(8,128)S(1)}, bf16[128,12288]{1,0:T(8,128)(2,1)S(1)}, bf16[128,12288]{1,0:T(8,128)(2,1)S(1)}, bf16[256,256]{1,0:T(8,128)(2,...) custom-call(s32[5]{0:T(128)} %bitcast.10, ...), custom_call_target="tpu_custom_call", output_to_operand_aliasing={{0}: (10, {}), {1}: (11, {}), {2}: (12, {})} | custom-call | flops 8053063680 | bytes 3145728 | tf_op jit(solution)/shard_map/pallas_call | solution.py:69
  27.6 0.0 collective-permute-done.2.refs_5_
  27.6 0.7 shard_map.126.refs_6_
  28.3 0.1 collective-permute-start.3
  28.4 0.5 collective-permute-start.6
  28.9 1.5 %collective-permute-start.4 = (bf16[256,128]{1,0:T(8,128)(2,1)S(1)}, bf16[256,128]{1,0:T(8,128)(2,1)S(1)}, u32[]{:S(2)}, u32[]{:S(2)}) collective-permute-start(bf16[256,128]{1,0:T(8,128)(2,1)S(1)} %get-tuple-element.73.refs_5_.refs_1_), channel_id=1, source_target_pairs={{0,2},{2,0},{1,3},{3,1},{4,6},{6,4},{5,7},{7,5},{8,10},{10,8},{9,1... | collective-permute-start | bytes 196616 | tf_op jit(solution)/shard_map/ppermute | solution.py:469
  30.4 0.0 collective-permute-start.7
  30.4 0.5 collective-permute-start.5
  30.9 0.0 collective-permute-done.3.refs_7_
  31.0 7.6 %shard_map.127 = (f32[384,4096]{1,0:T(8,128)S(1)}, bf16[128,12288]{1,0:T(8,128)(2,1)S(1)}, bf16[128,12288]{1,0:T(8,128)(2,1)S(1)}, bf16[384,4096]{1,0:T(8,128)(2...) custom-call(s32[5]{0:T(128)} %bitcast.12, ...), custom_call_target="tpu_custom_call", output_to_operand_aliasing={{0}: (8, {}), {1}: (9, {}), {2}: (10, {})} | custom-call | flops 8053063680 | bytes 3145728 | tf_op jit(solution)/shard_map/pallas_call | solution.py:69
  38.6 0.0 copy-start
  38.6 2.3 %copy-done = bf16[2560,1024]{1,0:T(8,128)(2,1)} copy-done((bf16[2560,1024]{1,0:T(8,128)(2,1)}, bf16[2560,1024]{1,0:T(8,128)(2,1)S(1)}, u32[]{:S(2)}) %copy-start) | copy-done | bytes 5242904
  40.9 0.0 collective-permute-done.6.refs_14_.refs_5_
  40.9 0.0 collective-permute-done.4.refs_12_.refs_4_
  40.9 0.0 collective-permute-done.7.refs_15_.refs_6_
  40.9 0.0 collective-permute-done.5.refs_13_.refs_5_
  40.9 7.1 %shard_map.128 = (f32[384,4096]{1,0:T(8,128)S(1)}, bf16[128,12288]{1,0:T(8,128)(2,1)S(1)}, bf16[128,12288]{1,0:T(8,128)(2,1)S(1)}, bf16[384,4096]{1,0:T(8,128)(2...) custom-call(s32[5]{0:T(128)} %bitcast.13, ...), custom_call_target="tpu_custom_call", output_to_operand_aliasing={{0}: (8, {}), {1}: (9, {}), {2}: (10, {}), {3}: (11, {})} | custom-call | flops 8053063680 | bytes 3145728 | tf_op jit(solution)/shard_map/pallas_call | solution.py:69
  48.0 0.3 collective-permute-start.8
  48.3 0.3 collective-permute-start.10
  48.6 0.8 %collective-permute-done.8.refs_3_ = bf16[2,128,256]{2,1,0:T(8,128)(2,1)S(1)} collective-permute-done((bf16[2,128,256]{2,1,0:T(8,128)(2,1)S(1)}, bf16[2,128,256]{2,1,0:T(8,128)(2,1)S(1)}, u32[]{:S(2)}, u32[]{:S(2)}) %collective-permute-start.8) | collective-permute-done | bytes 131104 | tf_op jit(solution)/shard_map/ppermute | solution.py:469
  49.5 0.7 shard_map.129
  50.2 0.5 collective-permute-start.13
  50.7 0.0 collective-permute-done.10.refs_3_
  50.7 0.7 shard_map.131
  51.4 1.6 %collective-permute-start.11 = (bf16[2,128,256]{2,1,0:T(8,128)(2,1)S(1)}, bf16[2,128,256]{2,1,0:T(8,128)(2,1)S(1)}, u32[]{:S(2)}, u32[]{:S(2)}) collective-permute-start(bf16[2,128,256]{2,1,0:T(8,128)(2,1)S(1)} %get-tuple-element.90), channel_id=1, source_target_pairs={{0,4},{4,0},{8,12},{12,8},{1,5},{5,1},{9,13},{13,9},{2,6},{6,2},{1... | collective-permute-start | bytes 393224 | tf_op jit(solution)/shard_map/ppermute | solution.py:469
  53.0 5.0 %shard_map.130 = (f32[384,4096]{1,0:T(8,128)S(1)}, bf16[128,12288]{1,0:T(8,128)(2,1)S(1)}, bf16[128,12288]{1,0:T(8,128)(2,1)S(1)}, bf16[384,4096]{1,0:T(8,128)(2...) custom-call(s32[5]{0:T(128)} %bitcast.16, ...), custom_call_target="tpu_custom_call", output_to_operand_aliasing={{0}: (10, {}), {1}: (11, {}), {2}: (12, {}), {3}: (13, {})} | custom-call | flops 4026531840 | bytes 1572864 | tf_op jit(solution)/shard_map/pallas_call | solution.py:69
  58.1 0.0 collective-permute-done.13.refs_3_
  58.1 0.7 shard_map.134
  58.8 0.4 collective-permute-start.14
  59.2 0.0 collective-permute-done.11.refs_3_
  59.2 0.7 shard_map.132
  59.9 2.6 %collective-permute-start.12 = (bf16[128,256]{1,0:T(8,128)(2,1)S(1)}, bf16[128,256]{1,0:T(8,128)(2,1)S(1)}, u32[]{:S(2)}, u32[]{:S(2)}) collective-permute-start(bf16[128,256]{1,0:T(8,128)(2,1)S(1)} %get-tuple-element.92), channel_id=1, source_target_pairs={{0,8},{4,12},{8,0},{12,4},{1,9},{5,13},{9,1},{13,5},{2,10},{6,14},... | collective-permute-start | bytes 196616 | tf_op jit(solution)/shard_map/ppermute | solution.py:469
  62.6 0.0 collective-permute-start.9
  62.6 4.2 %collective-permute-done.14.refs_3_ = bf16[128,256]{1,0:T(8,128)(2,1)S(1)} collective-permute-done((bf16[128,256]{1,0:T(8,128)(2,1)S(1)}, bf16[128,256]{1,0:T(8,128)(2,1)S(1)}, u32[]{:S(2)}, u32[]{:S(2)}) %collective-permute-start.14) | collective-permute-done | bytes 65568 | tf_op jit(solution)/shard_map/ppermute | solution.py:469
  66.8 0.7 shard_map.135.refs_9_
  67.5 0.1 collective-permute-start.16
  67.6 0.0 collective-permute-done.12.refs_3_
  67.6 0.0 slice-start
  67.6 0.8 shard_map.133.refs_8_
  68.5 0.5 collective-permute-start.15
  69.0 1.5 %collective-permute-start.18 = (bf16[256,128]{1,0:T(8,128)(2,1)S(1)}, bf16[256,128]{1,0:T(8,128)(2,1)S(1)}, u32[]{:S(2)}, u32[]{:S(2)}) collective-permute-start(bf16[256,128]{1,0:T(8,128)(2,1)S(1)} %get-tuple-element.99.refs_7_.refs_3_), channel_id=1, source_target_pairs={{0,2},{2,0},{1,3},{3,1},{4,6},{6,4},{5,7},{7,5},{8,10},{10,8},{9,1... | collective-permute-start | bytes 196616 | tf_op jit(solution)/shard_map/ppermute | solution.py:469
  70.5 1.5 %shard_map.136 = (bf16[384,512]{1,0:T(8,128)(2,1)}, bf16[384,512]{1,0:T(8,128)(2,1)}) custom-call(s32[5]{0:T(128)} %bitcast.21, s32[3]{0:T(128)} %bitcast.41, bf16[256,128]{1,0:T(8,128)(2,1)S(1)} %get-tuple-element.96.refs_2_, bf16[256,256]{1,0:T(8,128)(2,1)S(1)} %get-tuple-element.97.refs_3_, bf16[256,128]{1,0:T(8,128)(2,1)S(1)} %get-tuple-element.98.refs_4_, ...), custom_call_target="tpu_custom_call" | custom-call | tf_op jit(solution)/shard_map/pallas_call | solution.py:69
  72.0 0.0 collective-permute-done.9.refs_7_
  72.0 0.0 collective-permute-done.16.refs_11_
  72.1 0.0 collective-permute-done.15.refs_10_
  72.1 1.5 %shard_map.137 = (bf16[384,512]{1,0:T(8,128)(2,1)}, bf16[384,512]{1,0:T(8,128)(2,1)}, bf16[128,512]{1,0:T(8,128)(2,1)S(1)}) custom-call(s32[5]{0:T(128)} %bitcast.22, s32[3]{0:T(128)} %bitcast.42, f32[2,128,128]{2,1,0:T(8,128)S(1)} %get-tuple-element.83.refs_2_, ...), custom_call_target="tpu_custom_call", output_to_operand_aliasing={{0}: (12, {}), {1}: (13, {})} | custom-call | tf_op jit(solution)/shard_map/pallas_call | solution.py:69
  73.6 0.6 collective-permute-start.17
  74.2 0.0 collective-permute-done.18.refs_6_
  74.2 2.5 %copy-done.1 = bf16[2560,1024]{1,0:T(8,128)(2,1)S(1)} copy-done((bf16[2560,1024]{1,0:T(8,128)(2,1)S(1)}, bf16[2560,1024]{1,0:T(8,128)(2,1)}, u32[]{:S(2)}) %copy-start.1) | copy-done | bytes 5242904
  76.7 3.4 %shard_map.138.refs_4_ = bf16[384,2560]{1,0:T(8,128)(2,1)} custom-call(s32[5]{0:T(128)} %bitcast.23, s32[3]{0:T(128)} %bitcast.43, bf16[2560,1024]{1,0:T(8,128)(2,1)S(1)} %copy-done.1, bf16[256,128]{1,0:T(8,128)(2,1)S(1)} %get-tuple-element.73.refs_5_.refs_1_, bf16[256,256]{1,0:T(8,128)(2,1)S(1)} %get-tuple-element.74.refs_6_.refs_2_, ...), custom_call_target="tpu_custom_call" | custom-call | flops 2684354560 | bytes 6553600 | tf_op jit(solution)/shard_map/pallas_call | solution.py:446
  80.1 0.0 collective-permute-done.17.refs_2_
  80.1 0.0 slice-done
  80.1 0.0 slice-done.1
  80.1 3.1 %shard_map.139 = bf16[384,2560]{1,0:T(8,128)(2,1)} custom-call(s32[5]{0:T(128)} %bitcast.24, s32[3]{0:T(128)} %bitcast.44, bf16[2560,1024]{1,0:T(8,128)(2,1)S(1)} %bitcast.4, bf16[128,512]{1,0:T(8,128)(2,1)S(1)} %get-tuple-element.105.refs_1_, bf16[128,512]{1,0:T(8,128)(2,1)S(1)} %collective-permute-done.17.refs_2_, ...), custom_call_target="tpu_custom_call", output_to_operand_aliasing={{}: (6, {})} | custom-call | flops 1342177280 | bytes 5898240 | tf_op jit(solution)/shard_map/pallas_call | solution.py:446
  (3 shorter events, 0.0 us)
Async XLA Ops:
  2.3 1.7 %collective-permute-start = (bf16[2,128,512]{2,1,0:T(8,128)(2,1)S(1)}, bf16[2,128,512]{2,1,0:T(8,128)(2,1)S(1)}, u32[]{:S(2)}, u32[]{:S(2)}) collective-permute-start(bf16[2,128,512]{2,1,0:T(8,128)(2,1)S(1)} %shard_map.120.refs_2_.refs_6_), channel_id=1, source_target_pairs={{0,1},{1,0},{2,3},{3,2},{4,5},{5,4},{6,7},{7,6},{8,9},{9,8},{10,11... | collective-permute-start | bytes 786440 | tf_op jit(solution)/shard_map/ppermute | solution.py:469
  4.7 11.3 %collective-permute-start.1 = (bf16[128,512]{1,0:T(8,128)(2,1)S(1)}, bf16[128,512]{1,0:T(8,128)(2,1)S(1)}, u32[]{:S(2)}, u32[]{:S(2)}) collective-permute-start(bf16[128,512]{1,0:T(8,128)(2,1)S(1)} %shard_map.121.refs_8_.refs_2_), channel_id=1, source_target_pairs={{0,4},{4,0},{8,12},{12,8},{1,5},{5,1},{9,13},{13,9},{2,6},{6,2},{1... | collective-permute-start | bytes 393224 | tf_op jit(solution)/shard_map/ppermute | solution.py:469
  16.8 10.8 %collective-permute-start.2 = (bf16[128,512]{1,0:T(8,128)(2,1)S(1)}, bf16[128,512]{1,0:T(8,128)(2,1)S(1)}, u32[]{:S(2)}, u32[]{:S(2)}) collective-permute-start(bf16[128,512]{1,0:T(8,128)(2,1)S(1)} %shard_map.124.refs_13_.refs_4_), channel_id=1, source_target_pairs={{0,8},{4,12},{8,0},{12,4},{1,9},{5,13},{9,1},{13,5},{2,10},{6,14},... | collective-permute-start | bytes 393224 | tf_op jit(solution)/shard_map/ppermute | solution.py:469
  28.3 2.6 %collective-permute-start.3 = (bf16[2,128,512]{2,1,0:T(8,128)(2,1)S(1)}, bf16[2,128,512]{2,1,0:T(8,128)(2,1)S(1)}, u32[]{:S(2)}, u32[]{:S(2)}) collective-permute-start(bf16[2,128,512]{2,1,0:T(8,128)(2,1)S(1)} %shard_map.126.refs_6_), channel_id=1, source_target_pairs={{0,1},{1,0},{2,3},{3,2},{4,5},{5,4},{6,7},{7,6},{8,9},{9,8},{10,11... | collective-permute-start | bytes 786440 | tf_op jit(solution)/shard_map/ppermute | solution.py:469
  28.4 12.5 %collective-permute-start.6 = (bf16[2,128,128]{2,1,0:T(8,128)(2,1)S(1)}, bf16[2,128,128]{2,1,0:T(8,128)(2,1)S(1)}, u32[]{:S(2)}, u32[]{:S(2)}) collective-permute-start(bf16[2,128,128]{2,1,0:T(8,128)(2,1)S(1)} %get-tuple-element.61.refs_4_), channel_id=1, source_target_pairs={{0,1},{1,0},{2,3},{3,2},{4,5},{5,4},{6,7},{7,6},{8,9},{9,8},{10,11... | collective-permute-start | bytes 196616 | tf_op jit(solution)/shard_map/ppermute | solution.py:469
  28.9 12.0 %collective-permute-start.4 = (bf16[256,128]{1,0:T(8,128)(2,1)S(1)}, bf16[256,128]{1,0:T(8,128)(2,1)S(1)}, u32[]{:S(2)}, u32[]{:S(2)}) collective-permute-start(bf16[256,128]{1,0:T(8,128)(2,1)S(1)} %get-tuple-element.73.refs_5_.refs_1_), channel_id=1, source_target_pairs={{0,2},{2,0},{1,3},{3,1},{4,6},{6,4},{5,7},{7,5},{8,10},{10,8},{9,1... | collective-permute-start | bytes 196616 | tf_op jit(solution)/shard_map/ppermute | solution.py:469
  30.4 10.5 %collective-permute-start.7 = (bf16[2,128,256]{2,1,0:T(8,128)(2,1)S(1)}, bf16[2,128,256]{2,1,0:T(8,128)(2,1)S(1)}, u32[]{:S(2)}, u32[]{:S(2)}) collective-permute-start(bf16[2,128,256]{2,1,0:T(8,128)(2,1)S(1)} %get-tuple-element.65.refs_6_), channel_id=1, source_target_pairs={{0,1},{1,0},{2,3},{3,2},{4,5},{5,4},{6,7},{7,6},{8,9},{9,8},{10,11... | collective-permute-start | bytes 393224 | tf_op jit(solution)/shard_map/ppermute | solution.py:469
  30.4 10.5 %collective-permute-start.5 = (bf16[256,256]{1,0:T(8,128)(2,1)S(1)}, bf16[256,256]{1,0:T(8,128)(2,1)S(1)}, u32[]{:S(2)}, u32[]{:S(2)}) collective-permute-start(bf16[256,256]{1,0:T(8,128)(2,1)S(1)} %get-tuple-element.74.refs_6_.refs_2_), channel_id=1, source_target_pairs={{0,2},{2,0},{1,3},{3,1},{4,6},{6,4},{5,7},{7,5},{8,10},{10,8},{9,1... | collective-permute-start | bytes 393224 | tf_op jit(solution)/shard_map/ppermute | solution.py:469
  38.6 2.3 %copy-start = (bf16[2560,1024]{1,0:T(8,128)(2,1)}, bf16[2560,1024]{1,0:T(8,128)(2,1)S(1)}, u32[]{:S(2)}) copy-start(bf16[2560,1024]{1,0:T(8,128)(2,1)S(1)} %get-tuple-element.104.refs_0_) | copy-start | bytes 15728644
  48.0 1.4 %collective-permute-start.8 = (bf16[2,128,256]{2,1,0:T(8,128)(2,1)S(1)}, bf16[2,128,256]{2,1,0:T(8,128)(2,1)S(1)}, u32[]{:S(2)}, u32[]{:S(2)}) collective-permute-start(bf16[2,128,256]{2,1,0:T(8,128)(2,1)S(1)} %get-tuple-element.80), channel_id=1, source_target_pairs={{0,1},{1,0},{2,3},{3,2},{4,5},{5,4},{6,7},{7,6},{8,9},{9,8},{10,11... | collective-permute-start | bytes 393224 | tf_op jit(solution)/shard_map/ppermute | solution.py:469
  48.3 2.4 %collective-permute-start.10 = (bf16[2,128,256]{2,1,0:T(8,128)(2,1)S(1)}, bf16[2,128,256]{2,1,0:T(8,128)(2,1)S(1)}, u32[]{:S(2)}, u32[]{:S(2)}) collective-permute-start(bf16[2,128,256]{2,1,0:T(8,128)(2,1)S(1)} %get-tuple-element.88), channel_id=1, source_target_pairs={{0,1},{1,0},{2,3},{3,2},{4,5},{5,4},{6,7},{7,6},{8,9},{9,8},{10,11... | collective-permute-start | bytes 393224 | tf_op jit(solution)/shard_map/ppermute | solution.py:469
  50.2 7.9 %collective-permute-start.13 = (bf16[2,128,256]{2,1,0:T(8,128)(2,1)S(1)}, bf16[2,128,256]{2,1,0:T(8,128)(2,1)S(1)}, u32[]{:S(2)}, u32[]{:S(2)}) collective-permute-start(bf16[2,128,256]{2,1,0:T(8,128)(2,1)S(1)} %get-tuple-element.81.refs_14_), channel_id=1, source_target_pairs={{0,4},{4,0},{8,12},{12,8},{1,5},{5,1},{9,13},{13,9},{2,6},{6,2},{1... | collective-permute-start | bytes 393224 | tf_op jit(solution)/shard_map/ppermute | solution.py:469
  51.4 7.8 %collective-permute-start.11 = (bf16[2,128,256]{2,1,0:T(8,128)(2,1)S(1)}, bf16[2,128,256]{2,1,0:T(8,128)(2,1)S(1)}, u32[]{:S(2)}, u32[]{:S(2)}) collective-permute-start(bf16[2,128,256]{2,1,0:T(8,128)(2,1)S(1)} %get-tuple-element.90), channel_id=1, source_target_pairs={{0,4},{4,0},{8,12},{12,8},{1,5},{5,1},{9,13},{13,9},{2,6},{6,2},{1... | collective-permute-start | bytes 393224 | tf_op jit(solution)/shard_map/ppermute | solution.py:469
  58.8 8.0 %collective-permute-start.14 = (bf16[128,256]{1,0:T(8,128)(2,1)S(1)}, bf16[128,256]{1,0:T(8,128)(2,1)S(1)}, u32[]{:S(2)}, u32[]{:S(2)}) collective-permute-start(bf16[128,256]{1,0:T(8,128)(2,1)S(1)} %get-tuple-element.95), channel_id=1, source_target_pairs={{0,8},{4,12},{8,0},{12,4},{1,9},{5,13},{9,1},{13,5},{2,10},{6,14},... | collective-permute-start | bytes 196616 | tf_op jit(solution)/shard_map/ppermute | solution.py:469
  59.9 7.7 %collective-permute-start.12 = (bf16[128,256]{1,0:T(8,128)(2,1)S(1)}, bf16[128,256]{1,0:T(8,128)(2,1)S(1)}, u32[]{:S(2)}, u32[]{:S(2)}) collective-permute-start(bf16[128,256]{1,0:T(8,128)(2,1)S(1)} %get-tuple-element.92), channel_id=1, source_target_pairs={{0,8},{4,12},{8,0},{12,4},{1,9},{5,13},{9,1},{13,5},{2,10},{6,14},... | collective-permute-start | bytes 196616 | tf_op jit(solution)/shard_map/ppermute | solution.py:469
  62.6 9.4 %collective-permute-start.9 = (bf16[2,128,128]{2,1,0:T(8,128)(2,1)S(1)}, bf16[2,128,128]{2,1,0:T(8,128)(2,1)S(1)}, u32[]{:S(2)}, u32[]{:S(2)}) collective-permute-start(bf16[2,128,128]{2,1,0:T(8,128)(2,1)S(1)} %get-tuple-element.86.refs_4_), channel_id=1, source_target_pairs={{0,1},{1,0},{2,3},{3,2},{4,5},{5,4},{6,7},{7,6},{8,9},{9,8},{10,11... | collective-permute-start | bytes 196616 | tf_op jit(solution)/shard_map/ppermute | solution.py:469
  67.5 4.5 %collective-permute-start.16 = (bf16[128,256]{1,0:T(8,128)(2,1)S(1)}, bf16[128,256]{1,0:T(8,128)(2,1)S(1)}, u32[]{:S(2)}, u32[]{:S(2)}) collective-permute-start(bf16[128,256]{1,0:T(8,128)(2,1)S(1)} %shard_map.135.refs_9_), channel_id=1, source_target_pairs={{0,1},{1,0},{2,3},{3,2},{4,5},{5,4},{6,7},{7,6},{8,9},{9,8},{10,11... | collective-permute-start | bytes 196616 | tf_op jit(solution)/shard_map/ppermute | solution.py:469
  67.6 12.5 %slice-start = ((s8[5242880]{0:T(1024)(128)(4,1)}), s8[1048576]{0:T(1024)(128)(4,1)S(1)}, s32[]{:S(2)}) async-start(s8[5242880]{0:T(1024)(128)(4,1)} %bitcast.3), calls=%async_computation | async-start | bytes 2097152
  68.5 3.6 %collective-permute-start.15 = (bf16[128,256]{1,0:T(8,128)(2,1)S(1)}, bf16[128,256]{1,0:T(8,128)(2,1)S(1)}, u32[]{:S(2)}, u32[]{:S(2)}) collective-permute-start(bf16[128,256]{1,0:T(8,128)(2,1)S(1)} %shard_map.133.refs_8_), channel_id=1, source_target_pairs={{0,1},{1,0},{2,3},{3,2},{4,5},{5,4},{6,7},{7,6},{8,9},{9,8},{10,11... | collective-permute-start | bytes 196616 | tf_op jit(solution)/shard_map/ppermute | solution.py:469
  69.0 5.2 %collective-permute-start.18 = (bf16[256,128]{1,0:T(8,128)(2,1)S(1)}, bf16[256,128]{1,0:T(8,128)(2,1)S(1)}, u32[]{:S(2)}, u32[]{:S(2)}) collective-permute-start(bf16[256,128]{1,0:T(8,128)(2,1)S(1)} %get-tuple-element.99.refs_7_.refs_3_), channel_id=1, source_target_pairs={{0,2},{2,0},{1,3},{3,1},{4,6},{6,4},{5,7},{7,5},{8,10},{10,8},{9,1... | collective-permute-start | bytes 196616 | tf_op jit(solution)/shard_map/ppermute | solution.py:469
  73.6 6.5 %collective-permute-start.17 = (bf16[128,512]{1,0:T(8,128)(2,1)S(1)}, bf16[128,512]{1,0:T(8,128)(2,1)S(1)}, u32[]{:S(2)}, u32[]{:S(2)}) collective-permute-start(bf16[128,512]{1,0:T(8,128)(2,1)S(1)} %get-tuple-element.105.refs_1_), channel_id=1, source_target_pairs={{0,2},{2,0},{1,3},{3,1},{4,6},{6,4},{5,7},{7,5},{8,10},{10,8},{9,1... | collective-permute-start | bytes 393224 | tf_op jit(solution)/shard_map/ppermute | solution.py:469
  74.2 2.5 %copy-start.1 = (bf16[2560,1024]{1,0:T(8,128)(2,1)S(1)}, bf16[2560,1024]{1,0:T(8,128)(2,1)}, u32[]{:S(2)}) copy-start(bf16[2560,1024]{1,0:T(8,128)(2,1)} %copy-done) | copy-start | bytes 15728644
  76.7 3.4 %slice-start.1 = ((s8[5242880]{0:T(1024)(128)(4,1)}), s8[4194304]{0:T(1024)(128)(4,1)S(1)}, s32[]{:S(2)}) async-start(s8[5242880]{0:T(1024)(128)(4,1)} %bitcast.3), calls=%async_computation.1 | async-start | bytes 8388608

commit v4 on v0

v4 whole, which is shorter than its diff:
```python
import math

import jax
import jax.numpy as jnp
from jax import lax
from jax.experimental import pallas as pl
from jax.experimental.pallas import tpu as pltpu
from jax.sharding import PartitionSpec as P

HD = 128
PAGE = 128
SLOTS = 3
INNER = 3
ROWS = SLOTS * PAGE
LOG2E = math.log2(math.e)
SCALE = 1.0 / math.sqrt(HD)
BF16 = jnp.bfloat16
F32 = jnp.float32
I32 = jnp.int32
LARGE = 16 << 20
SMALL = 6 << 20
BLOCKED = 1e30


def dot_t(left, right):
    return lax.dot_general(left, right, (((1,), (1,)), ((), ())), preferred_element_type=F32)


def dot_n(left, right):
    return lax.dot_general(left, right, (((1,), (0,)), ((), ())), preferred_element_type=F32)


FACTS = 16
N0, N1, N2, OWNS2, LIMIT, LEADS, ROOT_IN_PAIR, ROOT_IN_HALF, NEXT_IN_CHIP = range(9)


def write_facts(facts, ids, counts):
    own = ids[INNER] - 1
    leaf = own // SLOTS
    owns = [ids[j] == own for j in range(INNER)]
    same = lambda level, shift: ((ids[level] // SLOTS) >> shift) == (leaf >> shift)
    number = lambda flag: jnp.where(flag, 1, 0)
    facts[N0] = jnp.where(owns[0] | owns[1] | owns[2], counts[0], 0)
    facts[N1] = counts[1]
    facts[N2] = counts[2]
    facts[OWNS2] = number(owns[2])
    facts[LIMIT] = jnp.where(owns[2], 2 * PAGE, jnp.where(owns[1], PAGE, 0))
    facts[LEADS] = number(lax.rem(leaf, 2) == 0)
    facts[ROOT_IN_PAIR] = number(same(0, 1))
    facts[ROOT_IN_HALF] = number(same(0, 2))
    facts[NEXT_IN_CHIP] = number(same(1, 1))
    for i in range(NEXT_IN_CHIP + 1, FACTS):
        facts[i] = 0


def row_ok(count, rows, width):
    return lax.broadcasted_iota(I32, (rows, width), 0) < count


def kernel_call(body, facts, near, far, outs, scratch=(), aliases=None, after=(), cost=None,
                limit=SMALL):
    smem = pl.BlockSpec(memory_space=pltpu.SMEM)
    vmem = pl.BlockSpec(memory_space=pltpu.VMEM)
    hbm = pl.BlockSpec(memory_space=pl.ANY)
    near = [pltpu.with_memory_space_constraint(a, pltpu.VMEM) for a in near]
    place = {("near", i): 1 + i for i in range(len(near))}
    place |= {("far", i): 1 + len(near) + i for i in range(len(far))}
    used = 1 + len(near) + len(far)

    def kernel(*refs):
        body(*refs[:used], *refs[used + len(after) :])

    return pl.pallas_call(
        kernel,
        out_shape=tuple(
            pltpu.VMEM(s, d) if inside else jax.ShapeDtypeStruct(s, d) for s, d, inside in outs
        ),
        in_specs=[smem] + [vmem] * len(near) + [hbm] * (len(far) + len(after)),
        out_specs=tuple(vmem if inside else hbm for _, _, inside in outs),
        scratch_shapes=list(scratch),
        input_output_aliases={place[k]: v for k, v in (aliases or {}).items()},
        compiler_params=pltpu.CompilerParams(vmem_limit_bytes=limit),
        cost_estimate=cost,
    )(pltpu.with_memory_space_constraint(facts, pltpu.SMEM), *near, *far, *after)


def start(ids, counts, keys, values):
    width = keys.shape[1]

    def body(ids_ref, counts_ref, k_ref, v_ref, facts, out, held, sem):
        copies = [
            pltpu.make_async_copy(ref.at[:PAGE], held.at[i], sem.at[i])
            for i, ref in enumerate((k_ref, v_ref))
        ]
        for c in copies:
            c.start()
        write_facts(facts, ids_ref, counts_ref)
        for c in copies:
            c.wait()
        ok = row_ok(counts_ref[0], PAGE, width)
        for i in range(2):
            out[i] = jnp.where(ok, held[i], jnp.zeros((), BF16))

    smem = pl.BlockSpec(memory_space=pltpu.SMEM)
    hbm = pl.BlockSpec(memory_space=pl.ANY)
    return pl.pallas_call(
        body,
        out_shape=(pltpu.SMEM((FACTS,), I32), pltpu.VMEM((2, PAGE, width), BF16)),
        in_specs=[smem, smem, hbm, hbm],
        out_specs=(smem, pl.BlockSpec(memory_space=pltpu.VMEM)),
        scratch_shapes=[pltpu.VMEM((2, PAGE, width), BF16), pltpu.SemaphoreType.DMA((2,))],
        compiler_params=pltpu.CompilerParams(vmem_limit_bytes=SMALL),
    )(ids, counts, keys, values)


def row_terms(rows):
    high = rows.astype(BF16).astype(F32)
    rest = rows - high
    middle = rest.astype(BF16).astype(F32)
    parts = [high, middle, rest - middle]
    spare = HD - 3 * rows.shape[0]
    parts.append(jnp.zeros((spare, rows.shape[1]), F32))
    return jnp.concatenate(parts, axis=0).T.astype(BF16)


class Head:
    def __init__(self, kv, group, q, g, norms, deltas, en, ed):
        self.kv, self.group, self.q, self.g, self.en, self.ed = kv, group, q, g, en, ed
        self.heads = min(4, group)
        self.parts = group // self.heads
        self.tall = self.heads * PAGE
        heads = slice(kv * group, (kv + 1) * group)
        en[...] = row_terms(norms[heads, :])
        ed[...] = row_terms(deltas[heads, :])

    def lanes(self, part, j):
        at = self.kv * self.group * HD + part * (self.heads * HD) + j * HD
        return pl.ds(pl.multiple_of(at, HD), HD)

    def stacked(self, ref, part, slots):
        return jnp.concatenate(
            [
                ref[slot * PAGE : (slot + 1) * PAGE, self.lanes(part, j)]
                for slot in slots
                for j in range(self.heads)
            ],
            axis=0,
        )

    def deep(self, stacked, terms, part, slots):
        column = lax.broadcasted_iota(I32, (1, HD), 1) % self.group
        picks = [
            (column == part * self.heads + j).astype(F32).astype(BF16)
            for j in range(self.heads)
        ]
        extra = [
            terms[slot * PAGE : (slot + 1) * PAGE] * pick for slot in slots for pick in picks
        ]
        return jnp.concatenate([stacked, jnp.concatenate(extra, axis=0)], axis=1)

    def turned_at(self, part, slot, count):
        at = ((self.kv * self.parts + part) * SLOTS + slot) * self.tall
        return pl.ds(pl.multiple_of(at, self.tall), self.tall * count)

    def put_queries(self, part, slot, rows_by_head, dq, add, stage):
        rows = slice(slot * PAGE, (slot + 1) * PAGE)
        for j in range(self.heads):
            value = rows_by_head[j * PAGE : (j + 1) * PAGE]
            if stage is None:
                dq[rows, self.lanes(part, j)] = value
            else:
                if add:
                    value = value + dq[rows, self.lanes(part, j)]
                stage[rows, j * HD : (j + 1) * HD] = (value * SCALE).astype(BF16)


def set_keys(deep, upright, at, page):
    where = slice(at * PAGE, (at + 1) * PAGE)
    deep[:HD, where] = page.T
    if upright is not None:
        upright[where] = page


def weigh(scores, grads, keep):
    p = keep(jnp.exp2(scores * (SCALE * LOG2E)))
    return p.astype(BF16), (p * grads).astype(BF16)


def attend(own, kvs, group, facts, inputs, pages, state, w=None, prior=(), ride=None, after=()):
    loading = "loaded" not in state
    q, g, k, v, norms, deltas = inputs if loading else state["loaded"]
    count = len(kvs)
    parts = group // min(4, group)
    tall = min(4, group) * PAGE
    wide = min(4, group) * HD
    width = count * HD
    base = prior[0].shape[1] if prior else 0
    kv_total = k.shape[1] // HD
    fresh = [kv not in state["done"] for kv in kvs]
    names = ["dq", "qt", "gt"] + ([] if all(fresh) else ["gq"])
    turned = ((HD, kv_total * group * ROWS), BF16, True)
    full = {"dq": (q.shape, F32, True), "qt": turned, "gt": turned, "gq": (q.shape, BF16, False)}

    near, far, aliases, outs = [], [], {}, []
    at_near, at_far = {}, {}

    def add_near(name, array):
        at_near[name] = len(near)
        near.append(array)

    def add_far(name, array):
        at_far[name] = len(far)
        far.append(array)

    for name in names:
        outs.append(full[name])
        if name in state:
            if full[name][2]:
                add_near(name, state[name])
                aliases["near", at_near[name]] = len(outs) - 1
            else:
                add_far(name, state[name])
                aliases["far", at_far[name]] = len(outs) - 1
    at_results = len(outs)
    if own:
        outs += [
            ((2 * PAGE, base + width), BF16, True),
            ((2 * PAGE, base + width), BF16, True),
            ((2, PAGE, base + width), F32, True),
            ((2, PAGE, base + width), BF16, True),
        ]
    else:
        outs += [
            ((2, PAGE, width), F32, True),
            ((2 if ride is None else 4, PAGE, width), BF16, True),
        ]
    at_loaded = len(outs)
    in_names = ["q", "g", "k", "v", "norms", "deltas"]
    in_arrays = [q, g, k, v, norms, deltas]
    for name, array in zip(in_names, in_arrays):
        if loading:
            add_far(name, array)
            outs.append((array.shape, array.dtype, True))
        else:
            add_near(name, array)
    at_w = len(outs)
    if w is not None:
        add_far("w", w)
        outs.append((w.shape, w.dtype, True))
    for i, page in enumerate(pages):
        add_near(("page", i), page)
    for i, array in enumerate(prior):
        add_near(("prior", i), array)
    if ride is not None:
        add_near("ride", ride[0])
    key_pages = 4 if own else 2
    scratch = [
        pltpu.VMEM((2 * HD, key_pages * PAGE), BF16),
        pltpu.VMEM((2 * HD, key_pages * PAGE), BF16),
        pltpu.VMEM((key_pages * PAGE, HD), BF16),
        pltpu.VMEM((2, HD, key_pages * PAGE), F32),
        pltpu.VMEM((ROWS, HD), BF16),
        pltpu.VMEM((ROWS, HD), BF16),
        pltpu.VMEM((count * parts, ROWS, wide), BF16),
        pltpu.SemaphoreType.DMA((count * parts,)),
        pltpu.SemaphoreType.DMA((2 * kv_total + 5,)),
    ]
    cols = lambda a, b: slice(a * PAGE, b * PAGE)

    def body(facts, *refs):
        ins, out_refs = refs[: len(near) + len(far)], refs[len(near) + len(far) : -len(scratch)]
        k_deep, v_deep, k_up, acc, en, ed, stage, sem, load_sem = refs[-len(scratch) :]
        near_ref = lambda name: ins[at_near[name]]
        far_ref = lambda name: ins[len(near) + at_far[name]]
        held = dict(zip(names, out_refs))
        results = out_refs[at_results:at_loaded]
        copies = {}
        if loading:
            into = dict(zip(in_names, out_refs[at_loaded:at_w]))

            def load(key, name, columns=None):
                src, dst = far_ref(name), into[name]
                if columns is not None:
                    src, dst = src.at[:, columns], dst.at[:, columns]
                copies[key] = pltpu.make_async_copy(src, dst, load_sem.at[len(copies)])
                copies[key].start()

            for name in in_names[2:]:
                load(name, name)
            for kv in range(kv_total):
                at = slice(kv * group * HD, (kv + 1) * group * HD)
                load(("q", kv), "q", at)
                load(("g", kv), "g", at)
        else:
            into = {name: near_ref(name) for name in in_names}
        if w is not None:
            w_copy = pltpu.make_async_copy(
                far_ref("w"), out_refs[at_w], load_sem.at[2 * kv_total + 4]
            )
            w_copy.start()
        q, g, k, v, norms, deltas = (into[name] for name in in_names)

        def arrived(*keys):
            for key in keys:
                if key in copies:
                    copies.pop(key).wait()

        k_deep[HD:] = jnp.full((HD, key_pages * PAGE), -1.0, BF16)
        v_deep[HD:] = jnp.full((HD, key_pages * PAGE), -1.0, BF16)
        for out, i in zip(results, range(len(prior))):
            out[..., :base] = near_ref(("prior", i))[...]
        if ride is not None:
            results[1][2:] = near_ref("ride")[:, :, ride[1] : ride[1] + width]
        owns2, leads = facts[OWNS2] == 1, facts[LEADS] == 1
        if loading:
            arrived("norms", "deltas", "k", "v")
            lane = lax.broadcasted_iota(I32, norms.shape, 1)
            limit = jnp.where(
                lane < PAGE, facts[N0], jnp.where(lane < 2 * PAGE, facts[N1], facts[N2])
            )
            norms[...] = jnp.where(lane % PAGE < limit, norms[...] * (1.0 / SCALE), BLOCKED)
        lower = lambda rows: lax.broadcasted_iota(I32, (rows, PAGE), 1) <= (
            lax.broadcasted_iota(I32, (rows, PAGE), 0) % PAGE
        )

        def set_pages(n, kv):
            lane = slice(kv * HD, (kv + 1) * HD)
            first, second = (near_ref(("page", i)) for i in range(2))
            if own:
                zero = jnp.zeros((), BF16)
                for slot, (at, c) in enumerate(((3, N0), (0, N1), (2, N2))):
                    ok = row_ok(facts[c], PAGE, HD)
                    rows = cols(slot, slot + 1)
                    set_keys(k_deep, k_up, at, jnp.where(ok, k[rows, lane], zero))
                    set_keys(v_deep, None, at, jnp.where(ok, v[rows, lane], zero))
                level2 = [jnp.where(owns2, first[i, :, lane], second[i, :, lane]) for i in (0, 1)]
                set_keys(k_deep, k_up, 1, level2[0])
                set_keys(v_deep, None, 1, level2[1])
            else:
                for j in range(2):
                    mine, theirs = first[j, :, lane], second[j, :, lane]
                    set_keys(k_deep, k_up, j, jnp.where(leads, mine, theirs))
                    set_keys(v_deep, None, j, jnp.where(leads, theirs, mine))
            acc[...] = jnp.zeros_like(acc)

        def turned_rows(head, part, is_fresh, qs, gs, order):
            if is_fresh:
                for name, rows in (("qt", qs), ("gt", gs)):
                    for i, slot in enumerate(order):
                        held[name][:, head.turned_at(part, slot, 1)] = rows[
                            i * tall : (i + 1) * tall
                        ].T
            return lambda name, slot, slots: held[name][:, head.turned_at(part, slot, slots)]

        def own_part(head, part, n, stage_ref):
            order = (1, 2, 0)
            qs, gs = head.stacked(q, part, order), head.stacked(g, part, order)
            qd, gd = head.deep(qs, en, part, order), head.deep(gs, ed, part, order)
            turn = turned_rows(head, part, fresh[n], qs, gs, order)
            low = lower(tall)

            def keep_first(p):
                masked = jnp.where(low, p[:tall, :PAGE], 0.0)
                return jnp.concatenate(
                    [jnp.concatenate([masked, p[:tall, PAGE:]], axis=1), p[tall:]], axis=0
                )

            pa, da = weigh(
                dot_n(qd[: 2 * tall], k_deep[:, : 2 * PAGE]),
                dot_n(gd[: 2 * tall], v_deep[:, : 2 * PAGE]),
                keep_first,
            )
            both = lambda x: jnp.concatenate([x[:tall, :PAGE], x[tall:, PAGE:]], axis=0)
            low2 = lower(2 * tall)
            pb, db = weigh(
                both(dot_n(qd[tall:], k_deep[:, 2 * PAGE :])),
                both(dot_n(gd[tall:], v_deep[:, 2 * PAGE :])),
                lambda p: jnp.where(low2, p, 0.0),
            )
            for i, (name, a, b) in enumerate((("qt", da, db), ("gt", pa, pb))):
                acc[i, :, : 2 * PAGE] += dot_n(turn(name, 1, 2), a)
                acc[i, :, cols(2, 3)] += dot_n(turn(name, 2, 1), b[:tall])
                acc[i, :, cols(3, 4)] += dot_n(turn(name, 0, 1), b[tall:])
            first = dot_n(da, k_up[: 2 * PAGE])
            put = lambda slot, rows: head.put_queries(
                part, slot, rows, held["dq"], not fresh[n], stage_ref
            )
            put(1, first[:tall])
            put(2, first[tall:] + dot_n(db[:tall], k_up[cols(2, 3)]))
            put(0, dot_n(db[tall:], k_up[cols(3, 4)]))

        def shared_part(head, part, n, stage_ref):
            order = (0, 1, 2)
            qs, gs = head.stacked(q, part, order), head.stacked(g, part, order)
            qd, gd = head.deep(qs, en, part, order), head.deep(gs, ed, part, order)
            turn = turned_rows(head, part, fresh[n], qs, gs, order)
            column = lax.broadcasted_iota(I32, (tall, 2 * PAGE), 1)
            seen = column < facts[LIMIT]

            def keep(p):
                return jnp.concatenate([jnp.where(seen, p[:tall], 0.0), p[tall:]], axis=0)

            p, ds = weigh(dot_n(qd, k_deep[...]), dot_n(gd, v_deep[...]), keep)
            acc[0] += dot_n(turn("qt", 0, SLOTS), ds)
            acc[1] += dot_n(turn("gt", 0, SLOTS), p)
            dq = dot_n(ds, k_up[...])
            for slot in range(SLOTS):
                head.put_queries(
                    part, slot, dq[slot * tall : (slot + 1) * tall], held["dq"], not fresh[n],
                    stage_ref,
                )

        def put_own(n):
            dk12, dv12, own0, send2 = results
            here = slice(base + n * HD, base + (n + 1) * HD)
            grad = [acc[0].T * SCALE, acc[1].T]
            for at, c, to in ((0, N1, 0), (2, N2, 1)):
                ok = row_ok(facts[c], PAGE, HD)
                for kind, out in ((0, dk12), (1, dv12)):
                    out[cols(to, to + 1), here] = jnp.where(
                        ok, grad[kind][cols(at, at + 1)], 0.0
                    ).astype(BF16)
            for kind in range(2):
                level2 = grad[kind][cols(1, 2)]
                own0[kind, :, here] = grad[kind][cols(3, 4)] + jnp.where(owns2, level2, 0.0)
                send2[kind, :, here] = level2.astype(BF16)

        def put_shared(n):
            kept, sent = results
            here = slice(n * HD, (n + 1) * HD)
            grad_k, grad_v = acc[0].T * SCALE, acc[1].T
            for j in range(2):
                a, b = grad_k[cols(j, j + 1)], grad_v[cols(j, j + 1)]
                kept[j, :, here] = jnp.where(leads, a, b)
                sent[j, :, here] = jnp.where(leads, b, a).astype(BF16)

        sends = []
        for n, kv in enumerate(kvs):
            arrived(("q", kv), ("g", kv))
            head = Head(kv, group, q, g, norms, deltas, en, ed)
            set_pages(n, kv)

            def step(part, _, n=n, kv=kv, head=head):
                slot = n * parts + part
                (own_part if own else shared_part)(
                    head, part, n, None if fresh[n] else stage.at[slot]
                )
                if not fresh[n]:
                    at = pl.multiple_of((kv * parts + part) * wide, wide)
                    pltpu.make_async_copy(
                        stage.at[slot], held["gq"].at[:, pl.ds(at, wide)], sem.at[slot]
                    ).start()
                return 0

            lax.fori_loop(0, parts, step, 0)
            (put_own if own else put_shared)(n)
            if not fresh[n]:
                sends += [(n * parts + p, (kv * parts + p) * wide) for p in range(parts)]
        for slot, at in sends:
            pltpu.make_async_copy(
                stage.at[slot], held["gq"].at[:, at : at + wide], sem.at[slot]
            ).wait()
        arrived(*list(copies))
        if w is not None:
            w_copy.wait()

    made = kernel_call(
        body, facts, near, far, outs, scratch, aliases, after,
        pl.CostEstimate(
            flops=240 * PAGE * PAGE * HD * group * count,
            bytes_accessed=4 * group * count * HD * ROWS,
            transcendentals=6 * PAGE * PAGE * group * count,
        ),
        LARGE,
    )
    for name, array in zip(names, made):
        state[name] = array
    state["done"] = state["done"] | set(kvs)
    if loading:
        state["loaded"] = made[at_loaded:at_w]
    results = list(made[at_results:at_loaded])
    return results + ([made[at_w]] if w is not None else [])


def input_grad(facts, near, far, side, w, rows, grads, carry):
    out_cols, depth = w.shape
    tile = next(t for t in (640, 512, 320, 128, out_cols) if out_cols % t == 0)
    top = 0 if rows == PAGE else PAGE
    steps = out_cols // tile
    width = sum(a.shape[1] for a in grads[0])
    arrays = [w, *near, *(far or []), *grads[0], *grads[1]]
    count = len(grads[0])

    def body(facts, flag, w_ref, *refs):
        near_r, refs = refs[: len(near)], refs[len(near) :]
        far_r, refs = refs[: len(far or [])], refs[len(far or []) :]
        grad_r = refs[: 2 * count]
        out, dk, dv, made, stage, sem = refs[-6:]
        made[...] = jnp.zeros_like(made)
        copies = []
        for dst, pieces in ((dk, grad_r[:count]), (dv, grad_r[count:])):
            at = 0
            for src in pieces:
                here = dst.at[top : top + rows, at : at + src.shape[1]]
                copies.append(pltpu.make_async_copy(src, here, sem.at[steps + len(copies)]))
                copies[-1].start()
                at += src.shape[1]
        full = jnp.concatenate([r[...] for r in near_r], axis=1)
        if far:
            other = jnp.concatenate([r[...] for r in far_r], axis=1)
            leads = flag[0] == 0
            full = jnp.concatenate(
                [jnp.where(leads, full, other), jnp.where(leads, other, full)], axis=1
            )
        for i in range(steps):
            at = slice(i * tile, (i + 1) * tile)
            stage[i] = dot_t(w_ref[at], full).T.astype(BF16)
            copies.append(
                pltpu.make_async_copy(stage.at[i], out.at[top : top + rows, at], sem.at[i])
            )
            copies[-1].start()
        for c in copies:
            c.wait()

    smem = pl.BlockSpec(memory_space=pltpu.SMEM)
    hbm = pl.BlockSpec(memory_space=pl.ANY)
    arrays = [pltpu.with_memory_space_constraint(a, pltpu.VMEM) for a in arrays]
    carry = list(carry or [])
    kept = jax.ShapeDtypeStruct((ROWS, width), BF16)
    return pl.pallas_call(
        body,
        out_shape=(
            jax.ShapeDtypeStruct((ROWS, out_cols), BF16), kept, kept, pltpu.VMEM((8, HD), F32)
        ),
        in_specs=[smem] * 2
        + [pl.BlockSpec(memory_space=pltpu.VMEM)] * len(arrays)
        + [hbm] * len(carry),
        out_specs=(hbm, hbm, hbm, pl.BlockSpec(memory_space=pltpu.VMEM)),
        scratch_shapes=[
            pltpu.VMEM((steps, rows, tile), BF16),
            pltpu.SemaphoreType.DMA((steps + 2 * count,)),
        ],
        input_output_aliases={2 + len(arrays) + i: i for i in range(len(carry))},
        compiler_params=pltpu.CompilerParams(vmem_limit_bytes=LARGE),
        cost_estimate=pl.CostEstimate(
            flops=4 * rows * depth * out_cols,
            bytes_accessed=2 * rows * out_cols,
            transcendentals=0,
        ),
    )(pltpu.with_memory_space_constraint(facts, pltpu.SMEM), side, *arrays, *carry)


def flipped(block, axis, bit):
    count = lax.axis_size(axis)
    return lax.ppermute(block, axis, [(i, i ^ bit) for i in range(count) if i ^ bit < count])


def spanning(leaves, bit_index):
    return len([j for j in range(INNER) if 2 << bit_index <= leaves >> j])


def gather_small_tree(facts, own, beside_pair, beside_half):
    two = (own.shape, BF16, True)
    page = (own.shape[1:], BF16, True)
    from_core = flipped(own, "sub", 1)

    def choose_chip(facts, own_ref, far_ref, out):
        for kind in range(2):
            for mine in range(2):

                @pl.when((facts[LEADS] != kind) & (facts[OWNS2] != mine))
                def _copy(kind=kind, mine=mine):
                    out[...] = (own_ref if mine else far_ref)[kind]

    (chip,) = kernel_call(choose_chip, facts, [own, from_core], [], [page])
    from_pair = flipped(chip, "leaf", 1)

    def choose_pair(facts, near_ref, far_ref, out):
        out[...] = jnp.where(facts[ROOT_IN_PAIR] == 1, near_ref[...], far_ref[...])

    after = beside_pair(from_core, chip)
    (pair,) = kernel_call(choose_pair, facts, [chip, from_pair], [], [page], after=after)
    from_half = flipped(pair, "leaf", 2)

    def choose_all(facts, chip_ref, pair_far, pair_ref, half_far, out):
        out[0] = jnp.where(facts[ROOT_IN_HALF] == 1, pair_ref[...], half_far[...])
        out[1] = jnp.where(facts[NEXT_IN_CHIP] == 1, chip_ref[...], pair_far[...])

    after = beside_half(pair)
    (mine,) = kernel_call(
        choose_all, facts, [chip, from_pair, pair, from_half], [], [two], after=after
    )
    return mine, flipped(mine, "sub", 1)


class Reduction:
    def __init__(self, facts, kept, sent):
        self.facts, self.kept = facts, kept
        self.width = sum(k.shape[-1] for k in kept)
        self.first_far = [flipped(s, "sub", 1) for s in sent]

    def call(self, body, near, outs, after):
        return kernel_call(body, self.facts, near, [], outs, after=after)

    def over_cores(self, after=()):
        count = len(self.kept)

        def body(_, *refs):
            total, low = refs[-2:]
            at = 0
            for near, away in zip(refs[:count], refs[count : 2 * count]):
                here = slice(at, at + near.shape[-1])
                at += near.shape[-1]
                value = near[...] + away[:2].astype(F32)
                total[:, :, here] = value
                low[:, :, here] = value.astype(BF16)

        two = (2, PAGE, self.width)
        self.total, low = self.call(
            body, [*self.kept, *self.first_far], [(two, F32, True), (two, BF16, True)], after
        )
        self.far = flipped(low, "leaf", 1)
        return low

    def over_pair(self, after=()):
        def body(_, near, away, total, low):
            value = near[...] + away[...].astype(F32)
            total[...] = value
            low[...] = value[0].astype(BF16)

        two = (2, PAGE, self.width)
        self.total, low = self.call(
            body, [self.total, self.far], [(two, F32, True), ((PAGE, self.width), BF16, True)],
            after,
        )
        self.far = flipped(low, "leaf", 2)
        return low

    def over_half(self, passenger=None, after=()):
        more = [] if passenger is None else [passenger]

        def body(facts, near, away, *refs):
            out = refs[-1]
            root = near[0] + away[...].astype(F32)
            out[0] = jnp.where(facts[ROOT_IN_PAIR] == 1, root, near[1]).astype(BF16)
            if more:
                half = refs[0].shape[-1]
                out[1, :, :half] = refs[0][0]
                out[1, :, half:] = refs[0][1]

        shape = (1 + len(more), PAGE, self.width)
        (self.mine,) = self.call(
            body, [self.total, self.far, *more], [(shape, BF16, True)], after
        )
        self.last_far = flipped(self.mine, "sub", 1)


def finish_small_tree(facts, own0, lead, tail):
    width = sum(a.shape[-1] for a in own0)
    half = width // 2
    near = [*own0, lead.mine, lead.last_far, tail.mine, tail.last_far, lead.first_far[0],
            tail.first_far[0]]

    def body(facts, own_r, own_last, lead_near, lead_far, tail_near, tail_far, lead2, tail2, dk, dv):
        owns2, leads = facts[OWNS2] == 1, facts[LEADS] == 1
        ok = row_ok(facts[N0], PAGE, HD)
        for at in range(0, width, HD):
            c = slice(at % half, at % half + HD)
            first = at < half
            near = (lead_near if first else tail_near)[0, :, c]
            away = (lead_far if first else tail_far)[0, :, c]
            gained = [jnp.where(leads, near, away), jnp.where(leads, away, near)]
            for kind, out in enumerate((dk, dv)):
                if first:
                    level2 = lead2[2 + kind, :, c]
                elif at + HD < width:
                    level2 = tail2[2 + kind, :, c]
                else:
                    level2 = tail_far[1, :, kind * HD : (kind + 1) * HD]
                more = jnp.where(owns2, level2, gained[kind]).astype(F32)
                if at + HD < width:
                    mine = own_r[kind, :, at : at + HD]
                else:
                    mine = own_last[kind]
                out[:, at : at + HD] = jnp.where(ok, mine + more, 0.0).astype(BF16)

    page = ((PAGE, width), BF16, True)
    return kernel_call(body, facts, near, [], [page, page])


def gather_tree(ids, own):
    leaves = lax.axis_size(("leaf", "sub"))
    owned = ids[:INNER] == ids[INNER] - 1
    pages = jnp.where(owned[:, None, None, None], own[None], jnp.zeros((), BF16))
    for bit in range(leaves.bit_length() - 1):
        active = spanning(leaves, bit)
        far = flipped(pages[:active], ("leaf", "sub"), 1 << bit)
        pages = jnp.concatenate([pages[:active] + far, pages[active:]])
    return pages


def reduce_tree(ids, parts):
    leaves = lax.axis_size(("leaf", "sub"))
    for bit in range(leaves.bit_length() - 1):
        active = spanning(leaves, bit)
        far = flipped(parts[:active], ("leaf", "sub"), 1 << bit)
        parts = jnp.concatenate([parts[:active] + far, parts[active:]])
    owned = ids[:INNER] == ids[INNER] - 1
    return jnp.sum(jnp.where(owned[:, None, None, None], parts, 0.0), axis=0)


def on_device(queries, grad_out, keys, values, log_norms, row_deltas, ancestors, counts, w_value):
    kv = keys.shape[1] // HD
    group = queries.shape[1] // keys.shape[1]
    leaves = lax.axis_size(("leaf", "sub"))
    hbm = lambda a: pltpu.with_memory_space_constraint(a, pltpu.HBM)
    side = lax.axis_index("tensor").astype(I32).reshape(1)
    two_sides = lax.axis_size("tensor") == 2
    inputs = [hbm(a) for a in (queries, grad_out, keys, values, log_norms, row_deltas)]
    facts, own = start(hbm(ancestors[0]), hbm(counts[0]), *inputs[2:4])
    state = {"done": frozenset()}

    def own_pages(kvs, pages, prior=(), after=()):
        return attend(
            True, kvs, group, facts, inputs, pages, state, prior=prior, after=after
        )

    def shared_pages(kvs, pages, w=None, ride=None, after=()):
        return attend(False, kvs, group, facts, inputs, pages, state, w, ride=ride, after=after)

    def spread(part):
        if two_sides:
            return flipped(part, "tensor", 1)
        return lax.all_gather(part, "tensor", axis=1, tiled=True)

    if leaves == 8 and lax.axis_size("sub") == 2 and kv == 4 and two_sides:
        level2, results = [], []

        def beside_pair(from_core, chip):
            level2.extend((own, from_core))
            results.append(own_pages((0,), level2, after=(chip,)))
            return (results[-1][3],)

        def beside_half(pair):
            results.append(own_pages((1, 2), level2, results[-1], (pair,)))
            return (results[-1][3],)

        shared = gather_small_tree(facts, own, beside_pair, beside_half)
        _, dv12, _, send2 = results[-1]
        far_v = [spread(dv12)]
        kept, sent, w_near = shared_pages((0, 1), shared, hbm(w_value), (send2, 0))
        lead = Reduction(facts, [kept], [sent])
        kept, sent = shared_pages((2,), shared, ride=(send2, 2 * HD), after=far_v)
        low = lead.over_cores((kept,))
        last_kept, last_sent = shared_pages((3,), shared, after=(low,))
        tail = Reduction(facts, [kept, last_kept], [sent, last_sent])
        low = lead.over_pair((last_kept,))
        last = own_pages((3,), level2, after=(low, tail.over_cores()))
        far_v.append(spread(last[1]))
        low = tail.over_pair((last[3],))
        lead.over_half(after=(low,))
        near_v = [dv12, last[1]]
        both = list(zip(results[-1], last))
        *grads, made = input_grad(facts, near_v, far_v, side, w_near, 2 * PAGE, both[:2], None)
        tail.over_half(last[3], (made,))
        dk0, dv0 = finish_small_tree(facts, both[2], lead, tail)
        grad_input, grad_keys, grad_values, _ = input_grad(
            facts, [dv0], [spread(dv0)], side, w_near, PAGE, ([dk0], [dv0]), grads
        )
        return (state["gq"], grad_keys, grad_values, grad_input)

    kvs = tuple(range(kv))
    first = lax.axis_index("sub") == 0
    path_ids = ancestors[0]
    pages = gather_tree(path_ids, own)
    dk12, dv12, own0, send2 = own_pages(kvs, (pages[2], pages[2]))
    kept, sent, w_near = shared_pages(
        kvs,
        (
            jnp.where(first, pages[:2, 0], pages[:2, 1]),
            jnp.where(first, pages[:2, 1], pages[:2, 0]),
        ),
        hbm(w_value),
    )
    sent = sent.astype(F32)
    upper = jnp.stack([jnp.where(first, kept, sent), jnp.where(first, sent, kept)], axis=1)
    low = send2.astype(F32)
    total = reduce_tree(path_ids, jnp.concatenate([upper, low[None]]))
    total += own0 - jnp.where(path_ids[2] == path_ids[INNER] - 1, low, 0.0)
    has = jnp.any(path_ids[:INNER] == path_ids[INNER] - 1)
    ok = (jnp.arange(PAGE) < jnp.where(has, counts[0, 0], 0))[:, None]
    dk0, dv0 = jnp.where(ok, total, 0.0).astype(BF16)
    if two_sides:
        pair = lambda part: ([part], [spread(part)])
    else:
        pair = lambda part: ([spread(part)], None)
    *grads, _ = input_grad(facts, *pair(dv12), side, w_near, 2 * PAGE, ([dk12], [dv12]), None)
    grad_input, grad_keys, grad_values, _ = input_grad(
        facts, *pair(dv0), side, w_near, PAGE, ([dk0], [dv0]), grads
    )
    return (state["gq"], grad_keys, grad_values, grad_input)


def solution(mesh):
    placed = (
        P(("groups", "leaf", "sub"), "tensor"),
        P(("groups", "leaf", "sub"), "tensor"),
        P(("groups", "leaf", "sub"), "tensor"),
        P(("groups", "leaf", "sub"), "tensor"),
        P("tensor", ("groups", "leaf", "sub")),
        P("tensor", ("groups", "leaf", "sub")),
        P(("groups", "leaf", "sub"), None),
        P(("groups", "leaf", "sub"), None),
        P("tensor", None),
    )
    return jax.shard_map(
        on_device,
        mesh=mesh,
        in_specs=placed,
        out_specs=(
            P(("groups", "leaf", "sub"), "tensor"),
            P(("groups", "leaf", "sub"), "tensor"),
            P(("groups", "leaf", "sub"), "tensor"),
            P(("groups", "leaf", "sub"), "tensor"),
        ),
        check_vma=False,
    )
```

time: 212 us -> 67.9 us (0.32)
  matrix products: 62.6 us -> 0 us
  local copies, waits for them, and re-layouts: 58.8 us -> 4.98 us
  Pallas kernels: 0 us -> 36.1 us
  waiting for transfers between devices: 30 us -> 9.13 us
  blocking collectives: 20.1 us -> 0 us
  other arithmetic: 17.4 us -> 0 us
  between operations: 16.9 us -> 1 us
  starting transfers between devices: 4.84 us -> 16.5 us
    dot_general x11 -> x0, matrix products: 62.6 us -> none  [the longest x2 15.1 us: attend(): jnp.einsum('rkgd,nkd->kgrn', grad_rows, value_rows, preferred_element_typ...]
    pallas_call x0 -> x19, Pallas kernels: none -> 36.1 us  [the longest x16 28.9 us: kernel_call(): pl.pallas_call(kernel, out_shape=tuple((pltpu.VMEM(s, d) if inside else j...]
    slice x22 -> x0, local copies, waits for them, and re-layouts: 21.9 us -> none  [the longest x1 3.18 us: on_device(): grad_out[PAGE:].reshape(2 * PAGE, kv_local, group_size, HD)]
    all_gather x2 -> x0, blocking collectives: 20.1 us -> none  [the longest x1 10.6 us: on_device(): lax.all_gather(page_counts[:1], ('leaf', 'sub'), axis=0, tiled=True)]
    all_gather x2 -> x0, waiting for transfers between devices: 12 us -> none  [the longest x1 12 us: on_device(): lax.all_gather(value_pages[:1], ('leaf', 'sub'), axis=0, tiled=True)]
    ppermute x6 -> x16, starting transfers between devices: 4.76 us -> 16.5 us  [flipped(): lax.ppermute(block, axis, [(i, i ^ bit) for i in range(count) if i ^ bit...]
    another operation x5 -> x0, local copies, waits for them, and re-layouts: 11.7 us -> none
    ppermute x6 -> x16, waiting for transfers between devices: 17.9 us -> 9.13 us  [flipped(): lax.ppermute(block, axis, [(i, i ^ bit) for i in range(count) if i ^ bit...]
  transfers between devices with their start and end apart: 8 -> 16, of which waited for: 3 -> 5; matrix products, arithmetic and copies ran while one was open for 24% -> 0% of each run, Pallas kernels for 0% -> 46%
where the time goes in v4:
time: 67.9 us; the launch traced here: 67.7 us
  Pallas kernels  36.1 us (53%)
  starting transfers between devices  16.5 us (24%)
  waiting for transfers between devices  9.13 us (13%)
  local copies, waits for them, and re-layouts  4.98 us (7%)
  between operations  1 us (1%)
    pallas_call x16, Pallas kernels, kernel_call(): pl.pallas_call(kernel, out_shape=tuple((pltpu.VMEM(s, d) if inside else j...  28.9 us
    ppermute x16, starting transfers between devices, flipped(): lax.ppermute(block, axis, [(i, i ^ bit) for i in range(count) if i ^ bit...  16.5 us
    ppermute x16, waiting for transfers between devices, flipped(): lax.ppermute(block, axis, [(i, i ^ bit) for i in range(count) if i ^ bit...  9.13 us
    pallas_call x2, Pallas kernels, input_grad(): pl.pallas_call(body, out_shape=(jax.ShapeDtypeStruct((ROWS, out_cols), BF...  5.48 us
    unnamed x6, local copies, waits for them, and re-layouts  4.98 us
    pallas_call x1, Pallas kernels, start(): pl.pallas_call(body, out_shape=(pltpu.SMEM((FACTS,), I32), pltpu.VMEM((2,...  1.68 us
  transfers between devices with their start and end apart: 16, of which 5 were waited for; matrix products, arithmetic and copies ran while one was open for 0% of the time, Pallas kernels for 46%

profile of v4, /device:TPU:0, one launch (start us, length us, event | category | flops | bytes accessed | tf_op | source)
XLA Modules:
  0.0 67.7 jit_solution(252644844061626056)
XLA Ops:
  0.6 1.7 %shard_map.120 = (s32[16]{0:T(128)S(4)}, bf16[2,128,512]{2,1,0:T(8,128)(2,1)S(1)}) custom-call(s32[5]{0:T(128)} %bitcast.3, s32[3]{0:T(128)} %bitcast.4, bf16[384,512]{1,0:T(8,128)(2,1)} %refs_5_.1, bf16[384,512]{1,0:T(8,128)(2,1)} %refs_6_.1), custom_call_target="tpu_custom_call" | custom-call | tf_op jit(solution)/shard_map/pallas_call | solution.py:106
  2.3 0.5 collective-permute-start
  2.8 1.2 %collective-permute-done.refs_2_.refs_11_ = bf16[2,128,512]{2,1,0:T(8,128)(2,1)S(1)} collective-permute-done((bf16[2,128,512]{2,1,0:T(8,128)(2,1)S(1)}, bf16[2,128,512]{2,1,0:T(8,128)(2,1)S(1)}, u32[]{:S(2)}, u32[]{:S(2)}) %collective-permute-start) | collective-permute-done | bytes 262176 | tf_op jit(solution)/shard_map/ppermute | solution.py:555
  4.0 3.0 %collective-permute-start.1 = (bf16[128,512]{1,0:T(8,128)(2,1)S(1)}, bf16[128,512]{1,0:T(8,128)(2,1)S(1)}, u32[]{:S(2)}, u32[]{:S(2)}) collective-permute-start(bf16[128,512]{1,0:T(8,128)(2,1)S(1)} %shard_map.121.refs_9_.refs_1_), channel_id=1, source_target_pairs={{0,4},{4,0},{8,12},{12,8},{1,5},{5,1},{9,13},{13,9},{2,6},{6,2},{1... | collective-permute-start | bytes 393224 | tf_op jit(solution)/shard_map/ppermute | solution.py:555
  7.0 4.9 %shard_map.122 = (f32[384,4096]{1,0:T(8,128)S(1)}, bf16[128,12288]{1,0:T(8,128)(2,1)S(1)}, bf16[128,12288]{1,0:T(8,128)(2,1)S(1)}, bf16[256,128]{1,0:T(8,128)(2,...) custom-call(s32[16]{0:T(128)S(4)} %get-tuple-element.66.refs_0_.fact, ...), custom_call_target="tpu_custom_call" | custom-call | flops 4026531840 | bytes 1572864 | tf_op jit(solution)/shard_map/pallas_call | solution.py:73
  11.9 0.0 collective-permute-done.1.refs_2_
  12.0 2.6 %collective-permute-start.2 = (bf16[128,512]{1,0:T(8,128)(2,1)S(1)}, bf16[128,512]{1,0:T(8,128)(2,1)S(1)}, u32[]{:S(2)}, u32[]{:S(2)}) collective-permute-start(bf16[128,512]{1,0:T(8,128)(2,1)S(1)} %shard_map.123.refs_16_.refs_3_), channel_id=1, source_target_pairs={{0,8},{4,12},{8,0},{12,4},{1,9},{5,13},{9,1},{13,5},{2,10},{6,14},... | collective-permute-start | bytes 393224 | tf_op jit(solution)/shard_map/ppermute | solution.py:555
  14.6 6.3 %shard_map.124 = (f32[384,4096]{1,0:T(8,128)S(1)}, bf16[128,12288]{1,0:T(8,128)(2,1)S(1)}, bf16[128,12288]{1,0:T(8,128)(2,1)S(1)}, bf16[256,384]{1,0:T(8,128)(2,...) custom-call(s32[16]{0:T(128)S(4)} %get-tuple-element.66.refs_0_.fact, ...), custom_call_target="tpu_custom_call", output_to_operand_aliasing={{0}: (1, {}), {1}: (2, {}), {2}: (3, {})} | custom-call | flops 8053063680 | bytes 3145728 | tf_op jit(solution)/shard_map/pallas_call | solution.py:73
  20.9 0.0 collective-permute-done.2.refs_4_
  20.9 0.1 collective-permute-start.3
  21.0 1.6 %collective-permute-start.4 = (bf16[256,384]{1,0:T(8,128)(2,1)S(1)}, bf16[256,384]{1,0:T(8,128)(2,1)S(1)}, u32[]{:S(2)}, u32[]{:S(2)}) collective-permute-start(bf16[256,384]{1,0:T(8,128)(2,1)S(1)} %get-tuple-element.89.refs_0_.refs_6_), channel_id=1, source_target_pairs={{0,2},{2,0},{1,3},{3,1},{4,6},{6,4},{5,7},{7,5},{8,10},{10,8},{9,1... | collective-permute-start | bytes 589832 | tf_op jit(solution)/shard_map/ppermute | solution.py:555
  22.6 0.0 collective-permute-done.3.refs_11_
  22.6 6.7 %shard_map.126 = (f32[384,4096]{1,0:T(8,128)S(1)}, bf16[128,12288]{1,0:T(8,128)(2,1)S(1)}, bf16[128,12288]{1,0:T(8,128)(2,1)S(1)}, bf16[384,4096]{1,0:T(8,128)(2...) custom-call(s32[16]{0:T(128)S(4)} %get-tuple-element.66.refs_0_.fact, ...), custom_call_target="tpu_custom_call", output_to_operand_aliasing={{0}: (1, {}), {1}: (2, {}), {2}: (3, {})} | custom-call | flops 8053063680 | bytes 3145728 | tf_op jit(solution)/shard_map/pallas_call | solution.py:73
  29.3 0.0 copy-start
  29.3 0.2 collective-permute-start.5
  29.6 0.0 collective-permute-done.4.refs_14_.refs_2_
  29.6 3.8 %shard_map.127 = (f32[384,4096]{1,0:T(8,128)S(1)}, bf16[128,12288]{1,0:T(8,128)(2,1)S(1)}, bf16[128,12288]{1,0:T(8,128)(2,1)S(1)}, bf16[384,4096]{1,0:T(8,128)(2...) custom-call(s32[16]{0:T(128)S(4)} %get-tuple-element.66.refs_0_.fact, ...), custom_call_target="tpu_custom_call", output_to_operand_aliasing={{0}: (1, {}), {1}: (2, {}), {2}: (3, {}), {3}: (13, {})} | custom-call | flops 4026531840 | bytes 1572864 | tf_op jit(solution)/shard_map/pallas_call | solution.py:73
  33.3 0.0 copy-done
  33.4 0.4 collective-permute-start.7
  33.8 0.0 collective-permute-done.5.refs_2_.refs_7_
  33.8 0.7 %collective-permute-start.6 = (bf16[2,128,256]{2,1,0:T(8,128)(2,1)S(1)}, bf16[2,128,256]{2,1,0:T(8,128)(2,1)S(1)}, u32[]{:S(2)}, u32[]{:S(2)}) collective-permute-start(bf16[2,128,256]{2,1,0:T(8,128)(2,1)S(1)} %get-tuple-element.96.refs_12_), channel_id=1, source_target_pairs={{0,4},{4,0},{8,12},{12,8},{1,5},{5,1},{9,13},{13,9},{2,6},{6,2},{1... | collective-permute-start | bytes 393224 | tf_op jit(solution)/shard_map/ppermute | solution.py:555
  34.5 3.2 %shard_map.129 = (f32[384,4096]{1,0:T(8,128)S(1)}, bf16[128,12288]{1,0:T(8,128)(2,1)S(1)}, bf16[128,12288]{1,0:T(8,128)(2,1)S(1)}, f32[2,128,128]{2,1,0:T(8,128)S(1)}, bf16[2,128,128]{2,1,0:T(8,128)(2,1)S(1)}) custom-call(s32[16]{0:T(128)S(4)} %get-tuple-element.66.refs_0_.facts, ...), custom_call_target="tpu_custom_call", output_to_operand_aliasing={{0}: (1, {}), {1}: (2, {}), {2}: (3, {})} | custom-call | flops 4026531840 | bytes 1572864 | tf_op jit(solution)/shard_map/pallas_call | solution.py:73
  37.7 0.1 collective-permute-start.8
  37.7 0.0 collective-permute-done.7.refs_3_.refs_8_
  37.8 1.2 %collective-permute-done.8.refs_4_ = bf16[2,128,128]{2,1,0:T(8,128)(2,1)S(1)} collective-permute-done((bf16[2,128,128]{2,1,0:T(8,128)(2,1)S(1)}, bf16[2,128,128]{2,1,0:T(8,128)(2,1)S(1)}, u32[]{:S(2)}, u32[]{:S(2)}) %collective-permute-start.8) | collective-permute-done | bytes 65568 | tf_op jit(solution)/shard_map/ppermute | solution.py:555
  39.0 1.5 %collective-permute-start.10 = (bf16[2,128,256]{2,1,0:T(8,128)(2,1)S(1)}, bf16[2,128,256]{2,1,0:T(8,128)(2,1)S(1)}, u32[]{:S(2)}, u32[]{:S(2)}) collective-permute-start(bf16[2,128,256]{2,1,0:T(8,128)(2,1)S(1)} %get-tuple-element.106.refs_14_), channel_id=1, source_target_pairs={{0,4},{4,0},{8,12},{12,8},{1,5},{5,1},{9,13},{13,9},{2,6},{6,2},{1... | collective-permute-start | bytes 393224 | tf_op jit(solution)/shard_map/ppermute | solution.py:555
  40.5 0.0 collective-permute-done.6.refs_2_
  40.5 3.8 %shard_map.132 = (f32[384,4096]{1,0:T(8,128)S(1)}, bf16[128,12288]{1,0:T(8,128)(2,1)S(1)}, bf16[128,12288]{1,0:T(8,128)(2,1)S(1)}, bf16[384,4096]{1,0:T(8,128)(2...) custom-call(s32[16]{0:T(128)S(4)} %get-tuple-element.66.refs_0_.fact, ...), custom_call_target="tpu_custom_call", output_to_operand_aliasing={{0}: (1, {}), {1}: (2, {}), {2}: (3, {}), {3}: (12, {})} | custom-call | flops 4026531840 | bytes 1572864 | tf_op jit(solution)/shard_map/pallas_call | solution.py:73
  44.3 1.5 %collective-permute-start.13 = (bf16[256,128]{1,0:T(8,128)(2,1)S(1)}, bf16[256,128]{1,0:T(8,128)(2,1)S(1)}, u32[]{:S(2)}, u32[]{:S(2)}) collective-permute-start(bf16[256,128]{1,0:T(8,128)(2,1)S(1)} %get-tuple-element.116.refs_1_.refs_7_), channel_id=1, source_target_pairs={{0,2},{2,0},{1,3},{3,1},{4,6},{6,4},{5,7},{7,5},{8,10},{10,8},{9,1... | collective-permute-start | bytes 196616 | tf_op jit(solution)/shard_map/ppermute | solution.py:555
  45.8 1.1 %collective-permute-start.9 = (bf16[128,256]{1,0:T(8,128)(2,1)S(1)}, bf16[128,256]{1,0:T(8,128)(2,1)S(1)}, u32[]{:S(2)}, u32[]{:S(2)}) collective-permute-start(bf16[128,256]{1,0:T(8,128)(2,1)S(1)} %get-tuple-element.103.refs_13_), channel_id=1, source_target_pairs={{0,8},{4,12},{8,0},{12,4},{1,9},{5,13},{9,1},{13,5},{2,10},{6,14},... | collective-permute-start | bytes 196616 | tf_op jit(solution)/shard_map/ppermute | solution.py:555
  46.9 0.0 collective-permute-done.10.refs_2_
  47.0 1.9 %collective-permute-start.12 = (bf16[128,256]{1,0:T(8,128)(2,1)S(1)}, bf16[128,256]{1,0:T(8,128)(2,1)S(1)}, u32[]{:S(2)}, u32[]{:S(2)}) collective-permute-start(bf16[128,256]{1,0:T(8,128)(2,1)S(1)} %get-tuple-element.114.refs_3_), channel_id=1, source_target_pairs={{0,8},{4,12},{8,0},{12,4},{1,9},{5,13},{9,1},{13,5},{2,10},{6,14},... | collective-permute-start | bytes 196616 | tf_op jit(solution)/shard_map/ppermute | solution.py:555
  48.8 0.0 collective-permute-done.13.refs_3_
  48.8 0.0 copy-start.1
  48.9 2.5 %copy-done.1 = bf16[2560,1024]{1,0:T(8,128)(2,1)S(1)} copy-done((bf16[2560,1024]{1,0:T(8,128)(2,1)S(1)}, bf16[2560,1024]{1,0:T(8,128)(2,1)}, u32[]{:S(2)}) %copy-start.1) | copy-done | bytes 5242904
  51.3 2.5 %shard_map.135 = (bf16[384,2560]{1,0:T(8,128)(2,1)}, bf16[384,512]{1,0:T(8,128)(2,1)}, bf16[384,512]{1,0:T(8,128)(2,1)}, f32[8,128]{1,0:T(8,128)S(1)}) custom-call(s32[16]{0:T(128)S(4)} %get-tuple-element.66.refs_0_.facts, s32[1]{0:T(128)} %bitcast.2.flag, bf16[2560,1024]{1,0:T(8,128)(2,1)S(1)} %copy-done.1, ...), custom_call_target="tpu_custom_call" | custom-call | flops 2684354560 | bytes 1310720 | tf_op jit(solution)/shard_map/pallas_call | solution.py:530
  53.9 0.7 collective-permute-done.12.refs_2_
  54.6 0.1 collective-permute-start.14
  54.6 0.0 collective-permute-done.9.refs_2_
  54.7 0.5 collective-permute-start.11
  55.2 0.9 %collective-permute-done.11.refs_4_ = bf16[1,128,256]{2,1,0:T(8,128)(2,1)S(1)} collective-permute-done((bf16[1,128,256]{2,1,0:T(8,128)(2,1)S(1)}, bf16[1,128,256]{2,1,0:T(8,128)(2,1)S(1)}, u32[]{:S(2)}, u32[]{:S(2)}) %collective-permute-start.11) | collective-permute-done | bytes 65568 | tf_op jit(solution)/shard_map/ppermute | solution.py:555
  56.1 0.0 collective-permute-done.14.refs_6_
  56.1 0.1 shard_map.137
  56.3 0.7 collective-permute-start.15
  56.9 5.2 %collective-permute-done.15.refs_1_ = bf16[128,512]{1,0:T(8,128)(2,1)S(1)} collective-permute-done((bf16[128,512]{1,0:T(8,128)(2,1)S(1)}, bf16[128,512]{1,0:T(8,128)(2,1)S(1)}, u32[]{:S(2)}, u32[]{:S(2)}) %collective-permute-start.15) | collective-permute-done | bytes 131104 | tf_op jit(solution)/shard_map/ppermute | solution.py:555
  62.1 0.0 copy-start.2
  62.1 2.5 %copy-done.2 = bf16[2560,1024]{1,0:T(8,128)(2,1)S(1)} copy-done((bf16[2560,1024]{1,0:T(8,128)(2,1)S(1)}, bf16[2560,1024]{1,0:T(8,128)(2,1)}, u32[]{:S(2)}) %copy-start.2) | copy-done | bytes 5242904
  64.6 3.0 %shard_map.138 = (bf16[384,2560]{1,0:T(8,128)(2,1)}, bf16[384,512]{1,0:T(8,128)(2,1)}, bf16[384,512]{1,0:T(8,128)(2,1)}, f32[8,128]{1,0:T(8,128)}) custom-call(s32[16]{0:T(128)S(4)} %get-tuple-element.66.refs_0_.facts, s32[1]{0:T(128)} %bitcast.2.flag, bf16[2560,1024]{1,0:T(8,128)(2,1)S(1)} %copy-done.2, ...), custom_call_target="tpu_custom_call", output_to_operand_aliasing={{0}: (7, {}), {1}: (8, {}), {2}: (9, {})} | custom-call | flops 1342177280 | bytes 655360 | tf_op jit(solution)/shard_map/pallas_call | solution.py:530
  (9 shorter events, 0.3 us)
Async XLA Ops:
  2.3 1.7 %collective-permute-start = (bf16[2,128,512]{2,1,0:T(8,128)(2,1)S(1)}, bf16[2,128,512]{2,1,0:T(8,128)(2,1)S(1)}, u32[]{:S(2)}, u32[]{:S(2)}) collective-permute-start(bf16[2,128,512]{2,1,0:T(8,128)(2,1)S(1)} %get-tuple-element.67.refs_1_.refs_10_), channel_id=1, source_target_pairs={{0,1},{1,0},{2,3},{3,2},{4,5},{5,4},{6,7},{7,6},{8,9},{9,8},{10,11... | collective-permute-start | bytes 786440 | tf_op jit(solution)/shard_map/ppermute | solution.py:555
  4.0 7.9 %collective-permute-start.1 = (bf16[128,512]{1,0:T(8,128)(2,1)S(1)}, bf16[128,512]{1,0:T(8,128)(2,1)S(1)}, u32[]{:S(2)}, u32[]{:S(2)}) collective-permute-start(bf16[128,512]{1,0:T(8,128)(2,1)S(1)} %shard_map.121.refs_9_.refs_1_), channel_id=1, source_target_pairs={{0,4},{4,0},{8,12},{12,8},{1,5},{5,1},{9,13},{13,9},{2,6},{6,2},{1... | collective-permute-start | bytes 393224 | tf_op jit(solution)/shard_map/ppermute | solution.py:555
  12.0 8.9 %collective-permute-start.2 = (bf16[128,512]{1,0:T(8,128)(2,1)S(1)}, bf16[128,512]{1,0:T(8,128)(2,1)S(1)}, u32[]{:S(2)}, u32[]{:S(2)}) collective-permute-start(bf16[128,512]{1,0:T(8,128)(2,1)S(1)} %shard_map.123.refs_16_.refs_3_), channel_id=1, source_target_pairs={{0,8},{4,12},{8,0},{12,4},{1,9},{5,13},{9,1},{13,5},{2,10},{6,14},... | collective-permute-start | bytes 393224 | tf_op jit(solution)/shard_map/ppermute | solution.py:555
  20.9 1.6 %collective-permute-start.3 = (bf16[2,128,512]{2,1,0:T(8,128)(2,1)S(1)}, bf16[2,128,512]{2,1,0:T(8,128)(2,1)S(1)}, u32[]{:S(2)}, u32[]{:S(2)}) collective-permute-start(bf16[2,128,512]{2,1,0:T(8,128)(2,1)S(1)} %shard_map.125.refs_10_), channel_id=1, source_target_pairs={{0,1},{1,0},{2,3},{3,2},{4,5},{5,4},{6,7},{7,6},{8,9},{9,8},{10,11... | collective-permute-start | bytes 786440 | tf_op jit(solution)/shard_map/ppermute | solution.py:555
  21.0 8.6 %collective-permute-start.4 = (bf16[256,384]{1,0:T(8,128)(2,1)S(1)}, bf16[256,384]{1,0:T(8,128)(2,1)S(1)}, u32[]{:S(2)}, u32[]{:S(2)}) collective-permute-start(bf16[256,384]{1,0:T(8,128)(2,1)S(1)} %get-tuple-element.89.refs_0_.refs_6_), channel_id=1, source_target_pairs={{0,2},{2,0},{1,3},{3,1},{4,6},{6,4},{5,7},{7,5},{8,10},{10,8},{9,1... | collective-permute-start | bytes 589832 | tf_op jit(solution)/shard_map/ppermute | solution.py:555
  29.3 4.0 %copy-start = (bf16[2560,1024]{1,0:T(8,128)(2,1)}, bf16[2560,1024]{1,0:T(8,128)(2,1)S(1)}, u32[]{:S(2)}) copy-start(bf16[2560,1024]{1,0:T(8,128)(2,1)S(1)} %get-tuple-element.108.w_ref) | copy-start | bytes 15728644
  29.3 4.4 %collective-permute-start.5 = (bf16[4,128,256]{2,1,0:T(8,128)(2,1)S(1)}, bf16[4,128,256]{2,1,0:T(8,128)(2,1)S(1)}, u32[]{:S(2)}, u32[]{:S(2)}) collective-permute-start(bf16[4,128,256]{2,1,0:T(8,128)(2,1)S(1)} %get-tuple-element.94), channel_id=1, source_target_pairs={{0,1},{1,0},{2,3},{3,2},{4,5},{5,4},{6,7},{7,6},{8,9},{9,8},{10,11... | collective-permute-start | bytes 786440 | tf_op jit(solution)/shard_map/ppermute | solution.py:555
  33.4 4.4 %collective-permute-start.7 = (bf16[4,128,128]{2,1,0:T(8,128)(2,1)S(1)}, bf16[4,128,128]{2,1,0:T(8,128)(2,1)S(1)}, u32[]{:S(2)}, u32[]{:S(2)}) collective-permute-start(bf16[4,128,128]{2,1,0:T(8,128)(2,1)S(1)} %get-tuple-element.104), channel_id=1, source_target_pairs={{0,1},{1,0},{2,3},{3,2},{4,5},{5,4},{6,7},{7,6},{8,9},{9,8},{10,11... | collective-permute-start | bytes 393224 | tf_op jit(solution)/shard_map/ppermute | solution.py:555
  33.8 6.7 %collective-permute-start.6 = (bf16[2,128,256]{2,1,0:T(8,128)(2,1)S(1)}, bf16[2,128,256]{2,1,0:T(8,128)(2,1)S(1)}, u32[]{:S(2)}, u32[]{:S(2)}) collective-permute-start(bf16[2,128,256]{2,1,0:T(8,128)(2,1)S(1)} %get-tuple-element.96.refs_12_), channel_id=1, source_target_pairs={{0,4},{4,0},{8,12},{12,8},{1,5},{5,1},{9,13},{13,9},{2,6},{6,2},{1... | collective-permute-start | bytes 393224 | tf_op jit(solution)/shard_map/ppermute | solution.py:555
  37.7 1.3 %collective-permute-start.8 = (bf16[2,128,128]{2,1,0:T(8,128)(2,1)S(1)}, bf16[2,128,128]{2,1,0:T(8,128)(2,1)S(1)}, u32[]{:S(2)}, u32[]{:S(2)}) collective-permute-start(bf16[2,128,128]{2,1,0:T(8,128)(2,1)S(1)} %get-tuple-element.105), channel_id=1, source_target_pairs={{0,1},{1,0},{2,3},{3,2},{4,5},{5,4},{6,7},{7,6},{8,9},{9,8},{10,11... | collective-permute-start | bytes 196616 | tf_op jit(solution)/shard_map/ppermute | solution.py:555
  39.0 7.9 %collective-permute-start.10 = (bf16[2,128,256]{2,1,0:T(8,128)(2,1)S(1)}, bf16[2,128,256]{2,1,0:T(8,128)(2,1)S(1)}, u32[]{:S(2)}, u32[]{:S(2)}) collective-permute-start(bf16[2,128,256]{2,1,0:T(8,128)(2,1)S(1)} %get-tuple-element.106.refs_14_), channel_id=1, source_target_pairs={{0,4},{4,0},{8,12},{12,8},{1,5},{5,1},{9,13},{13,9},{2,6},{6,2},{1... | collective-permute-start | bytes 393224 | tf_op jit(solution)/shard_map/ppermute | solution.py:555
  44.3 4.5 %collective-permute-start.13 = (bf16[256,128]{1,0:T(8,128)(2,1)S(1)}, bf16[256,128]{1,0:T(8,128)(2,1)S(1)}, u32[]{:S(2)}, u32[]{:S(2)}) collective-permute-start(bf16[256,128]{1,0:T(8,128)(2,1)S(1)} %get-tuple-element.116.refs_1_.refs_7_), channel_id=1, source_target_pairs={{0,2},{2,0},{1,3},{3,1},{4,6},{6,4},{5,7},{7,5},{8,10},{10,8},{9,1... | collective-permute-start | bytes 196616 | tf_op jit(solution)/shard_map/ppermute | solution.py:555
  45.8 8.8 %collective-permute-start.9 = (bf16[128,256]{1,0:T(8,128)(2,1)S(1)}, bf16[128,256]{1,0:T(8,128)(2,1)S(1)}, u32[]{:S(2)}, u32[]{:S(2)}) collective-permute-start(bf16[128,256]{1,0:T(8,128)(2,1)S(1)} %get-tuple-element.103.refs_13_), channel_id=1, source_target_pairs={{0,8},{4,12},{8,0},{12,4},{1,9},{5,13},{9,1},{13,5},{2,10},{6,14},... | collective-permute-start | bytes 196616 | tf_op jit(solution)/shard_map/ppermute | solution.py:555
  47.0 7.5 %collective-permute-start.12 = (bf16[128,256]{1,0:T(8,128)(2,1)S(1)}, bf16[128,256]{1,0:T(8,128)(2,1)S(1)}, u32[]{:S(2)}, u32[]{:S(2)}) collective-permute-start(bf16[128,256]{1,0:T(8,128)(2,1)S(1)} %get-tuple-element.114.refs_3_), channel_id=1, source_target_pairs={{0,8},{4,12},{8,0},{12,4},{1,9},{5,13},{9,1},{13,5},{2,10},{6,14},... | collective-permute-start | bytes 196616 | tf_op jit(solution)/shard_map/ppermute | solution.py:555
  48.8 2.5 %copy-start.1 = (bf16[2560,1024]{1,0:T(8,128)(2,1)S(1)}, bf16[2560,1024]{1,0:T(8,128)(2,1)}, u32[]{:S(2)}) copy-start(bf16[2560,1024]{1,0:T(8,128)(2,1)} %copy-done) | copy-start | bytes 15728644
  54.6 1.6 %collective-permute-start.14 = (bf16[2,128,256]{2,1,0:T(8,128)(2,1)S(1)}, bf16[2,128,256]{2,1,0:T(8,128)(2,1)S(1)}, u32[]{:S(2)}, u32[]{:S(2)}) collective-permute-start(bf16[2,128,256]{2,1,0:T(8,128)(2,1)S(1)} %shard_map.136.refs_5_), channel_id=1, source_target_pairs={{0,1},{1,0},{2,3},{3,2},{4,5},{5,4},{6,7},{7,6},{8,9},{9,8},{10,11... | collective-permute-start | bytes 393224 | tf_op jit(solution)/shard_map/ppermute | solution.py:555
  54.7 1.5 %collective-permute-start.11 = (bf16[1,128,256]{2,1,0:T(8,128)(2,1)S(1)}, bf16[1,128,256]{2,1,0:T(8,128)(2,1)S(1)}, u32[]{:S(2)}, u32[]{:S(2)}) collective-permute-start(bf16[1,128,256]{2,1,0:T(8,128)(2,1)S(1)} %shard_map.134.refs_3_), channel_id=1, source_target_pairs={{0,1},{1,0},{2,3},{3,2},{4,5},{5,4},{6,7},{7,6},{8,9},{9,8},{10,11... | collective-permute-start | bytes 196616 | tf_op jit(solution)/shard_map/ppermute | solution.py:555
  56.3 5.8 %collective-permute-start.15 = (bf16[128,512]{1,0:T(8,128)(2,1)S(1)}, bf16[128,512]{1,0:T(8,128)(2,1)S(1)}, u32[]{:S(2)}, u32[]{:S(2)}) collective-permute-start(bf16[128,512]{1,0:T(8,128)(2,1)S(1)} %get-tuple-element.120.refs_0_.refs_3_), channel_id=1, source_target_pairs={{0,2},{2,0},{1,3},{3,1},{4,6},{6,4},{5,7},{7,5},{8,10},{10,8},{9,1... | collective-permute-start | bytes 393224 | tf_op jit(solution)/shard_map/ppermute | solution.py:555
  62.1 2.5 %copy-start.2 = (bf16[2560,1024]{1,0:T(8,128)(2,1)S(1)}, bf16[2560,1024]{1,0:T(8,128)(2,1)}, u32[]{:S(2)}) copy-start(bf16[2560,1024]{1,0:T(8,128)(2,1)} %copy-done) | copy-start | bytes 15728644

commit v5 on v4

--- a/solution.py
+++ b/solution.py
@@ -17,8 +17,9 @@
 BF16 = jnp.bfloat16
 F32 = jnp.float32
 I32 = jnp.int32
-LARGE = 16 << 20
-SMALL = 6 << 20
+LARGE = 10 << 20
+SMALL = 4 << 20
+SLIGHT = pl.CostEstimate(flops=1000, bytes_accessed=1000, transcendentals=0)
 BLOCKED = 1e30
 
 
@@ -80,7 +81,7 @@
         scratch_shapes=list(scratch),
         input_output_aliases={place[k]: v for k, v in (aliases or {}).items()},
         compiler_params=pltpu.CompilerParams(vmem_limit_bytes=limit),
-        cost_estimate=cost,
+        cost_estimate=cost or SLIGHT,
     )(pltpu.with_memory_space_constraint(facts, pltpu.SMEM), *near, *far, *after)
 
 
@@ -186,7 +187,8 @@
     return p.astype(BF16), (p * grads).astype(BF16)
 
 
-def attend(own, kvs, group, facts, inputs, pages, state, w=None, prior=(), ride=None, after=()):
+def attend(own, kvs, group, facts, inputs, pages, state, w=None, prior=(), ride=None, after=(),
+           load=240):
     loading = "loaded" not in state
     q, g, k, v, norms, deltas = inputs if loading else state["loaded"]
     count = len(kvs)
@@ -452,7 +454,8 @@
                     ).start()
                 return 0
 
-            lax.fori_loop(0, parts, step, 0)
+            for part in range(parts):
+                step(part, 0)
             (put_own if own else put_shared)(n)
             if not fresh[n]:
                 sends += [(n * parts + p, (kv * parts + p) * wide) for p in range(parts)]
@@ -467,9 +470,7 @@
     made = kernel_call(
         body, facts, near, far, outs, scratch, aliases, after,
         pl.CostEstimate(
-            flops=240 * PAGE * PAGE * HD * group * count,
-            bytes_accessed=4 * group * count * HD * ROWS,
-            transcendentals=6 * PAGE * PAGE * group * count,
+            flops=load * PAGE * PAGE * HD * group * count, bytes_accessed=1000, transcendentals=0
         ),
         LARGE,
     )
@@ -482,18 +483,21 @@
     return results + ([made[at_w]] if w is not None else [])
 
 
-def input_grad(facts, near, far, side, w, rows, grads, carry):
+def input_grad(facts, side, w, rows, own=None, far=None, begun=None, grads=None, carry=None):
     out_cols, depth = w.shape
     tile = next(t for t in (640, 512, 320, 128, out_cols) if out_cols % t == 0)
     top = 0 if rows == PAGE else PAGE
     steps = out_cols // tile
     width = sum(a.shape[1] for a in grads[0])
-    arrays = [w, *near, *(far or []), *grads[0], *grads[1]]
+    own, far = list(own or []), list(far or [])
+    extra = [] if begun is None else [begun]
+    arrays = [w, *own, *far, *extra, *grads[0], *grads[1]]
     count = len(grads[0])
 
     def body(facts, flag, w_ref, *refs):
-        near_r, refs = refs[: len(near)], refs[len(near) :]
-        far_r, refs = refs[: len(far or [])], refs[len(far or []) :]
+        own_r, refs = refs[: len(own)], refs[len(own) :]
+        far_r, refs = refs[: len(far)], refs[len(far) :]
+        begun_r, refs = refs[: len(extra)], refs[len(extra) :]
         grad_r = refs[: 2 * count]
         out, dk, dv, made, stage, sem = refs[-6:]
         made[...] = jnp.zeros_like(made)
@@ -505,16 +509,24 @@
                 copies.append(pltpu.make_async_copy(src, here, sem.at[steps + len(copies)]))
                 copies[-1].start()
                 at += src.shape[1]
-        full = jnp.concatenate([r[...] for r in near_r], axis=1)
-        if far:
-            other = jnp.concatenate([r[...] for r in far_r], axis=1)
-            leads = flag[0] == 0
-            full = jnp.concatenate(
-                [jnp.where(leads, full, other), jnp.where(leads, other, full)], axis=1
+        columns = lambda rs: jnp.concatenate([r[...] for r in rs], axis=1) if rs else None
+        mine, other = columns(own_r), columns(far_r)
+        half = depth // 2
+        where = slice(None)
+        if far and own:
+            lead = flag[0] == 0
+            mine = jnp.concatenate(
+                [jnp.where(lead, mine, other), jnp.where(lead, other, mine)], axis=1
             )
+        elif far:
+            mine = other
+            where = pl.ds(pl.multiple_of((1 - flag[0]) * half, half), half)
         for i in range(steps):
             at = slice(i * tile, (i + 1) * tile)
-            stage[i] = dot_t(w_ref[at], full).T.astype(BF16)
+            product = dot_t(w_ref[at, where], mine)
+            if extra:
+                product += begun_r[0][at]
+            stage[i] = product.T.astype(BF16)
             copies.append(
                 pltpu.make_async_copy(stage.at[i], out.at[top : top + rows, at], sem.at[i])
             )
@@ -523,6 +535,7 @@
             c.wait()
 
     smem = pl.BlockSpec(memory_space=pltpu.SMEM)
+    vmem = pl.BlockSpec(memory_space=pltpu.VMEM)
     hbm = pl.BlockSpec(memory_space=pl.ANY)
     arrays = [pltpu.with_memory_space_constraint(a, pltpu.VMEM) for a in arrays]
     carry = list(carry or [])
@@ -532,22 +545,42 @@
         out_shape=(
             jax.ShapeDtypeStruct((ROWS, out_cols), BF16), kept, kept, pltpu.VMEM((8, HD), F32)
         ),
-        in_specs=[smem] * 2
-        + [pl.BlockSpec(memory_space=pltpu.VMEM)] * len(arrays)
-        + [hbm] * len(carry),
-        out_specs=(hbm, hbm, hbm, pl.BlockSpec(memory_space=pltpu.VMEM)),
+        in_specs=[smem] * 2 + [vmem] * len(arrays) + [hbm] * len(carry),
+        out_specs=(hbm, hbm, hbm, vmem),
         scratch_shapes=[
             pltpu.VMEM((steps, rows, tile), BF16),
             pltpu.SemaphoreType.DMA((steps + 2 * count,)),
         ],
         input_output_aliases={2 + len(arrays) + i: i for i in range(len(carry))},
         compiler_params=pltpu.CompilerParams(vmem_limit_bytes=LARGE),
+        cost_estimate=SLIGHT,
+    )(pltpu.with_memory_space_constraint(facts, pltpu.SMEM), side, *arrays, *carry)
+
+
+def begin_input_grad(facts, side, w, own):
+    out_cols, depth = w.shape
+    tile = next(t for t in (640, 512, 320, 128, out_cols) if out_cols % t == 0)
+    half = depth // 2
+
+    def body(facts, side_r, w_ref, own_r, out):
+        where = pl.ds(pl.multiple_of(side_r[0] * half, half), half)
+        for i in range(out_cols // tile):
+            at = slice(i * tile, (i + 1) * tile)
+            out[at] = dot_t(w_ref[at, where], own_r[...])
+
+    smem = pl.BlockSpec(memory_space=pltpu.SMEM)
+    vmem = pl.BlockSpec(memory_space=pltpu.VMEM)
+    arrays = [pltpu.with_memory_space_constraint(a, pltpu.VMEM) for a in (w, own)]
+    return pl.pallas_call(
+        body,
+        out_shape=pltpu.VMEM((out_cols, own.shape[0]), F32),
+        in_specs=[smem, smem, vmem, vmem],
+        out_specs=vmem,
+        compiler_params=pltpu.CompilerParams(vmem_limit_bytes=LARGE),
         cost_estimate=pl.CostEstimate(
-            flops=4 * rows * depth * out_cols,
-            bytes_accessed=2 * rows * out_cols,
-            transcendentals=0,
+            flops=own.shape[0] * depth * out_cols, bytes_accessed=1000, transcendentals=0
         ),
-    )(pltpu.with_memory_space_constraint(facts, pltpu.SMEM), side, *arrays, *carry)
+    )(pltpu.with_memory_space_constraint(facts, pltpu.SMEM), side, *arrays)
 
 
 def flipped(block, axis, bit):
@@ -622,70 +655,71 @@
         self.far = flipped(low, "leaf", 1)
         return low
 
-    def over_pair(self, after=()):
-        def body(_, near, away, total, low):
+
+def over_pair(facts, pieces, handed=()):
+    count = len(pieces)
+    width = sum(r.width for r in pieces)
+
+    def body(_, *refs):
+        ins, handed_in = refs[: 2 * count], refs[2 * count : 2 * count + len(handed)]
+        total, low = refs[2 * count + len(handed) :][:2]
+        at = 0
+        for near, away in zip(ins[:count], ins[count:]):
+            here = slice(at, at + near.shape[-1])
+            at += near.shape[-1]
             value = near[...] + away[...].astype(F32)
-            total[...] = value
-            low[...] = value[0].astype(BF16)
-
-        two = (2, PAGE, self.width)
-        self.total, low = self.call(
-            body, [self.total, self.far], [(two, F32, True), ((PAGE, self.width), BF16, True)],
-            after,
-        )
-        self.far = flipped(low, "leaf", 2)
-        return low
-
-    def over_half(self, passenger=None, after=()):
-        more = [] if passenger is None else [passenger]
-
-        def body(facts, near, away, *refs):
-            out = refs[-1]
-            root = near[0] + away[...].astype(F32)
-            out[0] = jnp.where(facts[ROOT_IN_PAIR] == 1, root, near[1]).astype(BF16)
-            if more:
-                half = refs[0].shape[-1]
-                out[1, :, :half] = refs[0][0]
-                out[1, :, half:] = refs[0][1]
-
-        shape = (1 + len(more), PAGE, self.width)
-        (self.mine,) = self.call(
-            body, [self.total, self.far, *more], [(shape, BF16, True)], after
-        )
-        self.last_far = flipped(self.mine, "sub", 1)
-
-
-def finish_small_tree(facts, own0, lead, tail):
+            total[:, :, here] = value
+            low[:, here] = value[0].astype(BF16)
+        for src, dst in zip(handed_in, refs[2 * count + len(handed) + 2 :]):
+            dst[...] = src[...]
+
+    outs = [((2, PAGE, width), F32, True), ((PAGE, width), BF16, True)]
+    outs += [(a.shape, a.dtype, True) for a in handed]
+    near = [r.total for r in pieces] + [r.far for r in pieces] + list(handed)
+    total, low, *passed = kernel_call(body, facts, near, [], outs)
+    return total, flipped(low, "leaf", 2), passed
+
+
+def over_half(facts, total, far, passenger, after=()):
+    width = total.shape[-1]
+    more = passenger.shape[-1]
+
+    def body(facts, near, away, extra, out):
+        root = near[0] + away[...].astype(F32)
+        out[:, :width] = jnp.where(facts[ROOT_IN_PAIR] == 1, root, near[1]).astype(BF16)
+        for kind in range(2):
+            out[:, width + kind * more : width + (kind + 1) * more] = extra[kind]
+
+    outs = [((PAGE, width + 2 * more), BF16, True)]
+    (mine,) = kernel_call(body, facts, [total, far, passenger], [], outs, after=after)
+    return mine, flipped(mine, "sub", 1)
+
+
+def finish_small_tree(facts, own0, mine, far, lead2, tail2):
     width = sum(a.shape[-1] for a in own0)
     half = width // 2
-    near = [*own0, lead.mine, lead.last_far, tail.mine, tail.last_far, lead.first_far[0],
-            tail.first_far[0]]
-
-    def body(facts, own_r, own_last, lead_near, lead_far, tail_near, tail_far, lead2, tail2, dk, dv):
+
+    def body(facts, own_r, own_last, mine_r, far_r, lead_r, tail_r, dk, dv):
         owns2, leads = facts[OWNS2] == 1, facts[LEADS] == 1
         ok = row_ok(facts[N0], PAGE, HD)
         for at in range(0, width, HD):
-            c = slice(at % half, at % half + HD)
-            first = at < half
-            near = (lead_near if first else tail_near)[0, :, c]
-            away = (lead_far if first else tail_far)[0, :, c]
+            c = slice(at, at + HD)
+            last = at + HD == width
+            near, away = mine_r[:, c], far_r[:, c]
             gained = [jnp.where(leads, near, away), jnp.where(leads, away, near)]
             for kind, out in enumerate((dk, dv)):
-                if first:
-                    level2 = lead2[2 + kind, :, c]
-                elif at + HD < width:
-                    level2 = tail2[2 + kind, :, c]
+                if last:
+                    level2 = far_r[:, width + kind * HD : width + (kind + 1) * HD]
+                elif at < half:
+                    level2 = lead_r[2 + kind, :, c]
                 else:
-                    level2 = tail_far[1, :, kind * HD : (kind + 1) * HD]
+                    level2 = tail_r[2 + kind, :, at - half : at - half + HD]
                 more = jnp.where(owns2, level2, gained[kind]).astype(F32)
-                if at + HD < width:
-                    mine = own_r[kind, :, at : at + HD]
-                else:
-                    mine = own_last[kind]
-                out[:, at : at + HD] = jnp.where(ok, mine + more, 0.0).astype(BF16)
+                base = own_last[kind] if last else own_r[kind, :, c]
+                out[:, c] = jnp.where(ok, base + more, 0.0).astype(BF16)
 
     page = ((PAGE, width), BF16, True)
-    return kernel_call(body, facts, near, [], [page, page])
+    return kernel_call(body, facts, [*own0, mine, far, lead2, tail2], [], [page, page])
 
 
 def gather_tree(ids, own):
@@ -720,13 +754,13 @@
     facts, own = start(hbm(ancestors[0]), hbm(counts[0]), *inputs[2:4])
     state = {"done": frozenset()}
 
-    def own_pages(kvs, pages, prior=(), after=()):
+    def own_pages(kvs, pages, prior=(), after=(), w=None, load=240):
         return attend(
-            True, kvs, group, facts, inputs, pages, state, prior=prior, after=after
+            True, kvs, group, facts, inputs, pages, state, w, prior, after=after, load=load
         )
 
-    def shared_pages(kvs, pages, w=None, ride=None, after=()):
-        return attend(False, kvs, group, facts, inputs, pages, state, w, ride=ride, after=after)
+    def shared_pages(kvs, pages, ride=None, after=()):
+        return attend(False, kvs, group, facts, inputs, pages, state, ride=ride, after=after)
 
     def spread(part):
         if two_sides:
@@ -748,24 +782,30 @@
         shared = gather_small_tree(facts, own, beside_pair, beside_half)
         _, dv12, _, send2 = results[-1]
         far_v = [spread(dv12)]
-        kept, sent, w_near = shared_pages((0, 1), shared, hbm(w_value), (send2, 0))
+        kept, sent = shared_pages((0, 1), shared, (send2, 0))
         lead = Reduction(facts, [kept], [sent])
         kept, sent = shared_pages((2,), shared, ride=(send2, 2 * HD), after=far_v)
         low = lead.over_cores((kept,))
         last_kept, last_sent = shared_pages((3,), shared, after=(low,))
         tail = Reduction(facts, [kept, last_kept], [sent, last_sent])
-        low = lead.over_pair((last_kept,))
-        last = own_pages((3,), level2, after=(low, tail.over_cores()))
+        *last, w_near = own_pages(
+            (3,), level2, after=(tail.over_cores((lead.far,)),), w=hbm(w_value)
+        )
+        total, from_half, (last[1],) = over_pair(facts, [lead, tail], [last[1]])
         far_v.append(spread(last[1]))
-        low = tail.over_pair((last[3],))
-        lead.over_half(after=(low,))
         near_v = [dv12, last[1]]
         both = list(zip(results[-1], last))
-        *grads, made = input_grad(facts, near_v, far_v, side, w_near, 2 * PAGE, both[:2], None)
-        tail.over_half(last[3], (made,))
-        dk0, dv0 = finish_small_tree(facts, both[2], lead, tail)
+        *grads, made = input_grad(
+            facts, side, w_near, 2 * PAGE, near_v, far_v, grads=both[:2]
+        )
+        dk0, dv0 = finish_small_tree(
+            facts, both[2], *over_half(facts, total, from_half, last[3], (made,)),
+            lead.first_far[0], tail.first_far[0],
+        )
+        far_v = [spread(dv0)]
+        begun = begin_input_grad(facts, side, w_near, dv0)
         grad_input, grad_keys, grad_values, _ = input_grad(
-            facts, [dv0], [spread(dv0)], side, w_near, PAGE, ([dk0], [dv0]), grads
+            facts, side, w_near, PAGE, far=far_v, begun=begun, grads=([dk0], [dv0]), carry=grads
         )
         return (state["gq"], grad_keys, grad_values, grad_input)
 
@@ -773,14 +813,13 @@
     first = lax.axis_index("sub") == 0
     path_ids = ancestors[0]
     pages = gather_tree(path_ids, own)
-    dk12, dv12, own0, send2 = own_pages(kvs, (pages[2], pages[2]))
-    kept, sent, w_near = shared_pages(
+    dk12, dv12, own0, send2, w_near = own_pages(kvs, (pages[2], pages[2]), w=hbm(w_value))
+    kept, sent = shared_pages(
         kvs,
         (
             jnp.where(first, pages[:2, 0], pages[:2, 1]),
             jnp.where(first, pages[:2, 1], pages[:2, 0]),
         ),
-        hbm(w_value),
     )
     sent = sent.astype(F32)
     upper = jnp.stack([jnp.where(first, kept, sent), jnp.where(first, sent, kept)], axis=1)
@@ -794,9 +833,11 @@
         pair = lambda part: ([part], [spread(part)])
     else:
         pair = lambda part: ([spread(part)], None)
-    *grads, _ = input_grad(facts, *pair(dv12), side, w_near, 2 * PAGE, ([dk12], [dv12]), None)
+    *grads, _ = input_grad(
+        facts, side, w_near, 2 * PAGE, *pair(dv12), grads=([dk12], [dv12])
+    )
     grad_input, grad_keys, grad_values, _ = input_grad(
-        facts, *pair(dv0), side, w_near, PAGE, ([dk0], [dv0]), grads
+        facts, side, w_near, PAGE, *pair(dv0), grads=([dk0], [dv0]), carry=grads
     )
     return (state["gq"], grad_keys, grad_values, grad_input)
 

time: 67.9 us -> 67 us (0.987)
  waiting for transfers between devices: 9.13 us -> 14 us
  Pallas kernels: 36.1 us -> 31.8 us
  starting transfers between devices: 16.5 us -> 15.2 us
    ppermute x16 -> x14, waiting for transfers between devices: 9.13 us -> 14 us  [flipped(): lax.ppermute(block, axis, [(i, i ^ bit) for i in range(count) if i ^ bit...]
    pallas_call x16 -> x14, Pallas kernels: 28.9 us -> 24.4 us  [kernel_call(): pl.pallas_call(kernel, out_shape=tuple((pltpu.VMEM(s, d) if inside else j...]
    ppermute x16 -> x14, starting transfers between devices: 16.5 us -> 15.2 us  [flipped(): lax.ppermute(block, axis, [(i, i ^ bit) for i in range(count) if i ^ bit...]
    pallas_call x0 -> x1, Pallas kernels: none -> 0.83 us  [begin_input_grad(): pl.pallas_call(body, out_shape=pltpu.VMEM((out_cols, own.shape[0]), F32),...]
  transfers between devices with their start and end apart: 16 -> 14, of which waited for: 5 -> 8; matrix products, arithmetic and copies ran while one was open for 0% -> 0% of each run, Pallas kernels for 46% -> 41%
where the time goes in v5:
time: 67 us; the launch traced here: 66.8 us
  Pallas kernels  31.8 us (47%)
  starting transfers between devices  15.2 us (23%)
  waiting for transfers between devices  14 us (21%)
  local copies, waits for them, and re-layouts  4.81 us (7%)
  between operations  0.99 us (1%)
    pallas_call x14, Pallas kernels, kernel_call(): pl.pallas_call(kernel, out_shape=tuple((pltpu.VMEM(s, d) if inside else j...  24.4 us
    ppermute x14, starting transfers between devices, flipped(): lax.ppermute(block, axis, [(i, i ^ bit) for i in range(count) if i ^ bit...  15.2 us
    ppermute x14, waiting for transfers between devices, flipped(): lax.ppermute(block, axis, [(i, i ^ bit) for i in range(count) if i ^ bit...  14 us
    pallas_call x2, Pallas kernels, input_grad(): pl.pallas_call(body, out_shape=(jax.ShapeDtypeStruct((ROWS, out_cols), BF...  4.85 us
    unnamed x6, local copies, waits for them, and re-layouts  4.81 us
    pallas_call x1, Pallas kernels, start(): pl.pallas_call(body, out_shape=(pltpu.SMEM((FACTS,), I32), pltpu.VMEM((2,...  1.68 us
  transfers between devices with their start and end apart: 14, of which 8 were waited for; matrix products, arithmetic and copies ran while one was open for 0% of the time, Pallas kernels for 41%

profile of v5, /device:TPU:0, one launch (start us, length us, event | category | flops | bytes accessed | tf_op | source)
XLA Modules:
  0.0 66.8 jit_solution(1514692645466436275)
XLA Ops:
  0.6 1.7 %shard_map.120 = (s32[16]{0:T(128)S(4)}, bf16[2,128,512]{2,1,0:T(8,128)(2,1)S(1)}) custom-call(s32[5]{0:T(128)} %bitcast.3, s32[3]{0:T(128)} %bitcast.4, bf16[384,512]{1,0:T(8,128)(2,1)} %refs_5_.1, bf16[384,512]{1,0:T(8,128)(2,1)} %refs_6_.1), custom_call_target="tpu_custom_call" | custom-call | tf_op jit(solution)/shard_map/pallas_call | solution.py:107
  2.3 0.5 collective-permute-start
  2.8 1.2 %collective-permute-done.refs_2_.refs_11_ = bf16[2,128,512]{2,1,0:T(8,128)(2,1)S(1)} collective-permute-done((bf16[2,128,512]{2,1,0:T(8,128)(2,1)S(1)}, bf16[2,128,512]{2,1,0:T(8,128)(2,1)S(1)}, u32[]{:S(2)}, u32[]{:S(2)}) %collective-permute-start) | collective-permute-done | bytes 262176 | tf_op jit(solution)/shard_map/ppermute | solution.py:588
  4.0 3.0 %collective-permute-start.1 = (bf16[128,512]{1,0:T(8,128)(2,1)S(1)}, bf16[128,512]{1,0:T(8,128)(2,1)S(1)}, u32[]{:S(2)}, u32[]{:S(2)}) collective-permute-start(bf16[128,512]{1,0:T(8,128)(2,1)S(1)} %shard_map.121.refs_9_.refs_1_), channel_id=1, source_target_pairs={{0,4},{4,0},{8,12},{12,8},{1,5},{5,1},{9,13},{13,9},{2,6},{6,2},{1... | collective-permute-start | bytes 393224 | tf_op jit(solution)/shard_map/ppermute | solution.py:588
  7.1 4.3 %shard_map.122 = (f32[384,4096]{1,0:T(8,128)S(1)}, bf16[128,12288]{1,0:T(8,128)(2,1)S(1)}, bf16[128,12288]{1,0:T(8,128)(2,1)S(1)}, bf16[256,128]{1,0:T(8,128)(2,...) custom-call(s32[16]{0:T(128)S(4)} %get-tuple-element.65.refs_0_.fact, ...), custom_call_target="tpu_custom_call" | custom-call | flops 4026531840 | bytes 1000 | tf_op jit(solution)/shard_map/pallas_call | solution.py:74
  11.4 0.0 collective-permute-done.1.refs_2_
  11.4 2.6 %collective-permute-start.2 = (bf16[128,512]{1,0:T(8,128)(2,1)S(1)}, bf16[128,512]{1,0:T(8,128)(2,1)S(1)}, u32[]{:S(2)}, u32[]{:S(2)}) collective-permute-start(bf16[128,512]{1,0:T(8,128)(2,1)S(1)} %shard_map.123.refs_16_.refs_3_), channel_id=1, source_target_pairs={{0,8},{4,12},{8,0},{12,4},{1,9},{5,13},{9,1},{13,5},{2,10},{6,14},... | collective-permute-start | bytes 393224 | tf_op jit(solution)/shard_map/ppermute | solution.py:588
  14.0 4.9 %shard_map.124 = (f32[384,4096]{1,0:T(8,128)S(1)}, bf16[128,12288]{1,0:T(8,128)(2,1)S(1)}, bf16[128,12288]{1,0:T(8,128)(2,1)S(1)}, bf16[256,384]{1,0:T(8,128)(2,...) custom-call(s32[16]{0:T(128)S(4)} %get-tuple-element.65.refs_0_.fact, ...), custom_call_target="tpu_custom_call", output_to_operand_aliasing={{0}: (1, {}), {1}: (2, {}), {2}: (3, {})} | custom-call | flops 8053063680 | bytes 1000 | tf_op jit(solution)/shard_map/pallas_call | solution.py:74
  18.9 1.5 %collective-permute-done.2.refs_4_ = bf16[128,512]{1,0:T(8,128)(2,1)S(1)} collective-permute-done((bf16[128,512]{1,0:T(8,128)(2,1)S(1)}, bf16[128,512]{1,0:T(8,128)(2,1)S(1)}, u32[]{:S(2)}, u32[]{:S(2)}) %collective-permute-start.2) | collective-permute-done | bytes 131104 | tf_op jit(solution)/shard_map/ppermute | solution.py:588
  20.4 0.1 collective-permute-start.3
  20.5 1.6 %collective-permute-start.4 = (bf16[256,384]{1,0:T(8,128)(2,1)S(1)}, bf16[256,384]{1,0:T(8,128)(2,1)S(1)}, u32[]{:S(2)}, u32[]{:S(2)}) collective-permute-start(bf16[256,384]{1,0:T(8,128)(2,1)S(1)} %get-tuple-element.88.refs_0_.refs_6_), channel_id=1, source_target_pairs={{0,2},{2,0},{1,3},{3,1},{4,6},{6,4},{5,7},{7,5},{8,10},{10,8},{9,1... | collective-permute-start | bytes 589832 | tf_op jit(solution)/shard_map/ppermute | solution.py:588
  22.1 0.0 collective-permute-done.3.refs_11_
  22.1 4.6 %shard_map.126 = (f32[384,4096]{1,0:T(8,128)S(1)}, bf16[128,12288]{1,0:T(8,128)(2,1)S(1)}, bf16[128,12288]{1,0:T(8,128)(2,1)S(1)}, bf16[384,4096]{1,0:T(8,128)(2...) custom-call(s32[16]{0:T(128)S(4)} %get-tuple-element.65.refs_0_.fact, ...), custom_call_target="tpu_custom_call", output_to_operand_aliasing={{0}: (1, {}), {1}: (2, {}), {2}: (3, {})} | custom-call | flops 8053063680 | bytes 1000 | tf_op jit(solution)/shard_map/pallas_call | solution.py:74
  26.7 0.2 collective-permute-start.5
  26.9 0.9 %collective-permute-done.4.refs_14_.refs_2_ = bf16[256,384]{1,0:T(8,128)(2,1)S(1)} collective-permute-done((bf16[256,384]{1,0:T(8,128)(2,1)S(1)}, bf16[256,384]{1,0:T(8,128)(2,1)S(1)}, u32[]{:S(2)}, u32[]{:S(2)}) %collective-permute-start.4) | collective-permute-done | bytes 196640 | tf_op jit(solution)/shard_map/ppermute | solution.py:588
  27.8 3.1 %shard_map.127 = (f32[384,4096]{1,0:T(8,128)S(1)}, bf16[128,12288]{1,0:T(8,128)(2,1)S(1)}, bf16[128,12288]{1,0:T(8,128)(2,1)S(1)}, bf16[384,4096]{1,0:T(8,128)(2...) custom-call(s32[16]{0:T(128)S(4)} %get-tuple-element.65.refs_0_.fact, ...), custom_call_target="tpu_custom_call", output_to_operand_aliasing={{0}: (1, {}), {1}: (2, {}), {2}: (3, {}), {3}: (13, {})} | custom-call | flops 4026531840 | bytes 1000 | tf_op jit(solution)/shard_map/pallas_call | solution.py:74
  30.9 0.1 collective-permute-start.6
  31.0 0.0 collective-permute-done.5.refs_2_.refs_5_
  31.1 0.1 collective-permute-start.8
  31.1 2.2 %shard_map.129 = (f32[384,4096]{1,0:T(8,128)S(1)}, bf16[128,12288]{1,0:T(8,128)(2,1)S(1)}, bf16[128,12288]{1,0:T(8,128)(2,1)S(1)}, f32[2,128,128]{2,1,0:T(8,128)S(1)}, bf16[2,128,128]{2,1,0:T(8,128)(2,1)S(1)}) custom-call(s32[16]{0:T(128)S(4)} %get-tuple-element.65.refs_0_.facts, ...), custom_call_target="tpu_custom_call", output_to_operand_aliasing={{0}: (1, {}), {1}: (2, {}), {2}: (3, {})} | custom-call | flops 4026531840 | bytes 1000 | tf_op jit(solution)/shard_map/pallas_call | solution.py:74
  33.4 0.5 collective-permute-start.7
  33.9 0.0 collective-permute-done.6.refs_3_.refs_6_
  33.9 0.9 %collective-permute-done.7.refs_4_ = bf16[2,128,128]{2,1,0:T(8,128)(2,1)S(1)} collective-permute-done((bf16[2,128,128]{2,1,0:T(8,128)(2,1)S(1)}, bf16[2,128,128]{2,1,0:T(8,128)(2,1)S(1)}, u32[]{:S(2)}, u32[]{:S(2)}) %collective-permute-start.7) | collective-permute-done | bytes 65568 | tf_op jit(solution)/shard_map/ppermute | solution.py:588
  34.8 2.2 %collective-permute-done.8.refs_5_.refs_3_ = bf16[2,128,256]{2,1,0:T(8,128)(2,1)S(1)} collective-permute-done((bf16[2,128,256]{2,1,0:T(8,128)(2,1)S(1)}, bf16[2,128,256]{2,1,0:T(8,128)(2,1)S(1)}, u32[]{:S(2)}, u32[]{:S(2)}) %collective-permute-start.8) | collective-permute-done | bytes 131104 | tf_op jit(solution)/shard_map/ppermute | solution.py:588
  37.1 0.4 collective-permute-start.9
  37.4 4.9 %shard_map.131 = (f32[384,4096]{1,0:T(8,128)S(1)}, bf16[128,12288]{1,0:T(8,128)(2,1)S(1)}, bf16[128,12288]{1,0:T(8,128)(2,1)S(1)}, bf16[384,4096]{1,0:T(8,128)(2...) custom-call(s32[16]{0:T(128)S(4)} %get-tuple-element.65.refs_0_.fact, ...), custom_call_target="tpu_custom_call", output_to_operand_aliasing={{0}: (1, {}), {1}: (2, {}), {2}: (3, {}), {3}: (12, {})} | custom-call | flops 4026531840 | bytes 1000 | tf_op jit(solution)/shard_map/pallas_call | solution.py:74
  42.3 0.0 copy-start
  42.3 2.3 %copy-done = bf16[2560,1024]{1,0:T(8,128)(2,1)} copy-done((bf16[2560,1024]{1,0:T(8,128)(2,1)}, bf16[2560,1024]{1,0:T(8,128)(2,1)S(1)}, u32[]{:S(2)}) %copy-start) | copy-done | bytes 5242904
  44.6 0.0 collective-permute-done.9.refs_4_
  44.6 0.1 shard_map.132
  44.7 3.0 %collective-permute-start.10 = (bf16[128,512]{1,0:T(8,128)(2,1)S(1)}, bf16[128,512]{1,0:T(8,128)(2,1)S(1)}, u32[]{:S(2)}, u32[]{:S(2)}) collective-permute-start(bf16[128,512]{1,0:T(8,128)(2,1)S(1)} %get-tuple-element.112), channel_id=1, source_target_pairs={{0,8},{4,12},{8,0},{12,4},{1,9},{5,13},{9,1},{13,5},{2,10},{6,14},... | collective-permute-start | bytes 393224 | tf_op jit(solution)/shard_map/ppermute | solution.py:588
  47.7 1.5 %collective-permute-start.11 = (bf16[256,128]{1,0:T(8,128)(2,1)S(1)}, bf16[256,128]{1,0:T(8,128)(2,1)S(1)}, u32[]{:S(2)}, u32[]{:S(2)}) collective-permute-start(bf16[256,128]{1,0:T(8,128)(2,1)S(1)} %get-tuple-element.114.refs_1_.refs_7_), channel_id=1, source_target_pairs={{0,2},{2,0},{1,3},{3,1},{4,6},{6,4},{5,7},{7,5},{8,10},{10,8},{9,1... | collective-permute-start | bytes 196616 | tf_op jit(solution)/shard_map/ppermute | solution.py:588
  49.2 2.8 %collective-permute-done.11.refs_3_ = bf16[256,128]{1,0:T(8,128)(2,1)S(1)} collective-permute-done((bf16[256,128]{1,0:T(8,128)(2,1)S(1)}, bf16[256,128]{1,0:T(8,128)(2,1)S(1)}, u32[]{:S(2)}, u32[]{:S(2)}) %collective-permute-start.11) | collective-permute-done | bytes 65568 | tf_op jit(solution)/shard_map/ppermute | solution.py:588
  52.0 0.0 copy-start.1
  52.0 2.5 %copy-done.1 = bf16[2560,1024]{1,0:T(8,128)(2,1)S(1)} copy-done((bf16[2560,1024]{1,0:T(8,128)(2,1)S(1)}, bf16[2560,1024]{1,0:T(8,128)(2,1)}, u32[]{:S(2)}) %copy-start.1) | copy-done | bytes 5242904
  54.5 0.0 copy-start.2
  54.5 2.6 %shard_map.133 = (bf16[384,2560]{1,0:T(8,128)(2,1)}, bf16[384,512]{1,0:T(8,128)(2,1)}, bf16[384,512]{1,0:T(8,128)(2,1)}, f32[8,128]{1,0:T(8,128)S(1)}) custom-call(s32[16]{0:T(128)S(4)} %get-tuple-element.65.refs_0_.facts, s32[1]{0:T(128)} %bitcast.2.flag.side_r, bf16[2560,1024]{1,0:T(8,128)(2,1)S(1)} %copy-done.1, ...), custom_call_target="tpu_custom_call" | custom-call | flops 1000 | bytes 1000 | tf_op jit(solution)/shard_map/pallas_call | solution.py:543
  57.0 0.0 collective-permute-done.10.refs_2_
  57.1 0.1 collective-permute-start.12
  57.2 1.4 %collective-permute-done.12.refs_4_ = bf16[128,768]{1,0:T(8,128)(2,1)S(1)} collective-permute-done((bf16[128,768]{1,0:T(8,128)(2,1)S(1)}, bf16[128,768]{1,0:T(8,128)(2,1)S(1)}, u32[]{:S(2)}, u32[]{:S(2)}) %collective-permute-start.12) | collective-permute-done | bytes 196640 | tf_op jit(solution)/shard_map/ppermute | solution.py:588
  58.6 0.1 shard_map.135
  58.7 1.6 %collective-permute-start.13 = (bf16[128,512]{1,0:T(8,128)(2,1)S(1)}, bf16[128,512]{1,0:T(8,128)(2,1)S(1)}, u32[]{:S(2)}, u32[]{:S(2)}) collective-permute-start(bf16[128,512]{1,0:T(8,128)(2,1)S(1)} %get-tuple-element.118.own_r.refs_3_), channel_id=1, source_target_pairs={{0,2},{2,0},{1,3},{3,1},{4,6},{6,4},{5,7},{7,5},{8,10},{10,8},{9,1... | collective-permute-start | bytes 393224 | tf_op jit(solution)/shard_map/ppermute | solution.py:588
  60.3 0.0 copy-done.2
  60.3 0.8 %shard_map.136.refs_1_ = f32[2560,128]{1,0:T(8,128)S(1)} custom-call(s32[16]{0:T(128)S(4)} %get-tuple-element.65.refs_0_.facts, s32[1]{0:T(128)} %bitcast.2.flag.side_r, bf16[2560,1024]{1,0:T(8,128)(2,1)S(1)} %copy-done.2, bf16[128,512]{1,0:T(8,128)(2,1)S(1)} %get-tuple-element.118.own_r.refs_3_), custom_call_target="tpu_custom_call" | custom-call | flops 335544320 | bytes 1000 | tf_op jit(solution)/shard_map/pallas_call | solution.py:574
  61.1 3.2 %collective-permute-done.13.refs_0_ = bf16[128,512]{1,0:T(8,128)(2,1)S(1)} collective-permute-done((bf16[128,512]{1,0:T(8,128)(2,1)S(1)}, bf16[128,512]{1,0:T(8,128)(2,1)S(1)}, u32[]{:S(2)}, u32[]{:S(2)}) %collective-permute-start.13) | collective-permute-done | bytes 131104 | tf_op jit(solution)/shard_map/ppermute | solution.py:588
  64.3 2.3 %shard_map.137 = (bf16[384,2560]{1,0:T(8,128)(2,1)}, bf16[384,512]{1,0:T(8,128)(2,1)}, bf16[384,512]{1,0:T(8,128)(2,1)}, f32[8,128]{1,0:T(8,128)}) custom-call(s32[16]{0:T(128)S(4)} %get-tuple-element.65.refs_0_.facts, s32[1]{0:T(128)} %bitcast.2.flag.side_r, ...), custom_call_target="tpu_custom_call", output_to_operand_aliasing={{0}: (7, {}), {1}: (8, {}), {2}: (9, {})} | custom-call | flops 1000 | bytes 1000 | tf_op jit(solution)/shard_map/pallas_call | solution.py:543
  (6 shorter events, 0.2 us)
Async XLA Ops:
  2.3 1.7 %collective-permute-start = (bf16[2,128,512]{2,1,0:T(8,128)(2,1)S(1)}, bf16[2,128,512]{2,1,0:T(8,128)(2,1)S(1)}, u32[]{:S(2)}, u32[]{:S(2)}) collective-permute-start(bf16[2,128,512]{2,1,0:T(8,128)(2,1)S(1)} %get-tuple-element.66.refs_1_.refs_10_), channel_id=1, source_target_pairs={{0,1},{1,0},{2,3},{3,2},{4,5},{5,4},{6,7},{7,6},{8,9},{9,8},{10,11... | collective-permute-start | bytes 786440 | tf_op jit(solution)/shard_map/ppermute | solution.py:588
  4.0 7.3 %collective-permute-start.1 = (bf16[128,512]{1,0:T(8,128)(2,1)S(1)}, bf16[128,512]{1,0:T(8,128)(2,1)S(1)}, u32[]{:S(2)}, u32[]{:S(2)}) collective-permute-start(bf16[128,512]{1,0:T(8,128)(2,1)S(1)} %shard_map.121.refs_9_.refs_1_), channel_id=1, source_target_pairs={{0,4},{4,0},{8,12},{12,8},{1,5},{5,1},{9,13},{13,9},{2,6},{6,2},{1... | collective-permute-start | bytes 393224 | tf_op jit(solution)/shard_map/ppermute | solution.py:588
  11.4 9.0 %collective-permute-start.2 = (bf16[128,512]{1,0:T(8,128)(2,1)S(1)}, bf16[128,512]{1,0:T(8,128)(2,1)S(1)}, u32[]{:S(2)}, u32[]{:S(2)}) collective-permute-start(bf16[128,512]{1,0:T(8,128)(2,1)S(1)} %shard_map.123.refs_16_.refs_3_), channel_id=1, source_target_pairs={{0,8},{4,12},{8,0},{12,4},{1,9},{5,13},{9,1},{13,5},{2,10},{6,14},... | collective-permute-start | bytes 393224 | tf_op jit(solution)/shard_map/ppermute | solution.py:588
  20.4 1.6 %collective-permute-start.3 = (bf16[2,128,512]{2,1,0:T(8,128)(2,1)S(1)}, bf16[2,128,512]{2,1,0:T(8,128)(2,1)S(1)}, u32[]{:S(2)}, u32[]{:S(2)}) collective-permute-start(bf16[2,128,512]{2,1,0:T(8,128)(2,1)S(1)} %shard_map.125.refs_10_), channel_id=1, source_target_pairs={{0,1},{1,0},{2,3},{3,2},{4,5},{5,4},{6,7},{7,6},{8,9},{9,8},{10,11... | collective-permute-start | bytes 786440 | tf_op jit(solution)/shard_map/ppermute | solution.py:588
  20.5 7.3 %collective-permute-start.4 = (bf16[256,384]{1,0:T(8,128)(2,1)S(1)}, bf16[256,384]{1,0:T(8,128)(2,1)S(1)}, u32[]{:S(2)}, u32[]{:S(2)}) collective-permute-start(bf16[256,384]{1,0:T(8,128)(2,1)S(1)} %get-tuple-element.88.refs_0_.refs_6_), channel_id=1, source_target_pairs={{0,2},{2,0},{1,3},{3,1},{4,6},{6,4},{5,7},{7,5},{8,10},{10,8},{9,1... | collective-permute-start | bytes 589832 | tf_op jit(solution)/shard_map/ppermute | solution.py:588
  26.7 4.3 %collective-permute-start.5 = (bf16[4,128,256]{2,1,0:T(8,128)(2,1)S(1)}, bf16[4,128,256]{2,1,0:T(8,128)(2,1)S(1)}, u32[]{:S(2)}, u32[]{:S(2)}) collective-permute-start(bf16[4,128,256]{2,1,0:T(8,128)(2,1)S(1)} %get-tuple-element.93), channel_id=1, source_target_pairs={{0,1},{1,0},{2,3},{3,2},{4,5},{5,4},{6,7},{7,6},{8,9},{9,8},{10,11... | collective-permute-start | bytes 786440 | tf_op jit(solution)/shard_map/ppermute | solution.py:588
  30.9 3.0 %collective-permute-start.6 = (bf16[4,128,128]{2,1,0:T(8,128)(2,1)S(1)}, bf16[4,128,128]{2,1,0:T(8,128)(2,1)S(1)}, u32[]{:S(2)}, u32[]{:S(2)}) collective-permute-start(bf16[4,128,128]{2,1,0:T(8,128)(2,1)S(1)} %get-tuple-element.101), channel_id=1, source_target_pairs={{0,1},{1,0},{2,3},{3,2},{4,5},{5,4},{6,7},{7,6},{8,9},{9,8},{10,11... | collective-permute-start | bytes 393224 | tf_op jit(solution)/shard_map/ppermute | solution.py:588
  31.1 6.0 %collective-permute-start.8 = (bf16[2,128,256]{2,1,0:T(8,128)(2,1)S(1)}, bf16[2,128,256]{2,1,0:T(8,128)(2,1)S(1)}, u32[]{:S(2)}, u32[]{:S(2)}) collective-permute-start(bf16[2,128,256]{2,1,0:T(8,128)(2,1)S(1)} %get-tuple-element.95.refs_12_), channel_id=1, source_target_pairs={{0,4},{4,0},{8,12},{12,8},{1,5},{5,1},{9,13},{13,9},{2,6},{6,2},{1... | collective-permute-start | bytes 393224 | tf_op jit(solution)/shard_map/ppermute | solution.py:588
  33.4 1.5 %collective-permute-start.7 = (bf16[2,128,128]{2,1,0:T(8,128)(2,1)S(1)}, bf16[2,128,128]{2,1,0:T(8,128)(2,1)S(1)}, u32[]{:S(2)}, u32[]{:S(2)}) collective-permute-start(bf16[2,128,128]{2,1,0:T(8,128)(2,1)S(1)} %get-tuple-element.102), channel_id=1, source_target_pairs={{0,1},{1,0},{2,3},{3,2},{4,5},{5,4},{6,7},{7,6},{8,9},{9,8},{10,11... | collective-permute-start | bytes 196616 | tf_op jit(solution)/shard_map/ppermute | solution.py:588
  37.1 7.6 %collective-permute-start.9 = (bf16[2,128,256]{2,1,0:T(8,128)(2,1)S(1)}, bf16[2,128,256]{2,1,0:T(8,128)(2,1)S(1)}, u32[]{:S(2)}, u32[]{:S(2)}) collective-permute-start(bf16[2,128,256]{2,1,0:T(8,128)(2,1)S(1)} %get-tuple-element.103.refs_14_), channel_id=1, source_target_pairs={{0,4},{4,0},{8,12},{12,8},{1,5},{5,1},{9,13},{13,9},{2,6},{6,2},{1... | collective-permute-start | bytes 393224 | tf_op jit(solution)/shard_map/ppermute | solution.py:588
  42.3 2.3 %copy-start = (bf16[2560,1024]{1,0:T(8,128)(2,1)}, bf16[2560,1024]{1,0:T(8,128)(2,1)S(1)}, u32[]{:S(2)}) copy-start(bf16[2560,1024]{1,0:T(8,128)(2,1)S(1)} %get-tuple-element.105.w_ref) | copy-start | bytes 15728644
  44.7 12.4 %collective-permute-start.10 = (bf16[128,512]{1,0:T(8,128)(2,1)S(1)}, bf16[128,512]{1,0:T(8,128)(2,1)S(1)}, u32[]{:S(2)}, u32[]{:S(2)}) collective-permute-start(bf16[128,512]{1,0:T(8,128)(2,1)S(1)} %get-tuple-element.112), channel_id=1, source_target_pairs={{0,8},{4,12},{8,0},{12,4},{1,9},{5,13},{9,1},{13,5},{2,10},{6,14},... | collective-permute-start | bytes 393224 | tf_op jit(solution)/shard_map/ppermute | solution.py:588
  47.7 4.3 %collective-permute-start.11 = (bf16[256,128]{1,0:T(8,128)(2,1)S(1)}, bf16[256,128]{1,0:T(8,128)(2,1)S(1)}, u32[]{:S(2)}, u32[]{:S(2)}) collective-permute-start(bf16[256,128]{1,0:T(8,128)(2,1)S(1)} %get-tuple-element.114.refs_1_.refs_7_), channel_id=1, source_target_pairs={{0,2},{2,0},{1,3},{3,1},{4,6},{6,4},{5,7},{7,5},{8,10},{10,8},{9,1... | collective-permute-start | bytes 196616 | tf_op jit(solution)/shard_map/ppermute | solution.py:588
  52.0 2.5 %copy-start.1 = (bf16[2560,1024]{1,0:T(8,128)(2,1)S(1)}, bf16[2560,1024]{1,0:T(8,128)(2,1)}, u32[]{:S(2)}) copy-start(bf16[2560,1024]{1,0:T(8,128)(2,1)} %copy-done) | copy-start | bytes 15728644
  54.5 5.8 %copy-start.2 = (bf16[2560,1024]{1,0:T(8,128)(2,1)S(1)}, bf16[2560,1024]{1,0:T(8,128)(2,1)}, u32[]{:S(2)}) copy-start(bf16[2560,1024]{1,0:T(8,128)(2,1)} %copy-done) | copy-start | bytes 15728644
  57.1 1.5 %collective-permute-start.12 = (bf16[128,768]{1,0:T(8,128)(2,1)S(1)}, bf16[128,768]{1,0:T(8,128)(2,1)S(1)}, u32[]{:S(2)}, u32[]{:S(2)}) collective-permute-start(bf16[128,768]{1,0:T(8,128)(2,1)S(1)} %shard_map.134.refs_3_), channel_id=1, source_target_pairs={{0,1},{1,0},{2,3},{3,2},{4,5},{5,4},{6,7},{7,6},{8,9},{9,8},{10,11... | collective-permute-start | bytes 589832 | tf_op jit(solution)/shard_map/ppermute | solution.py:588
  58.7 5.6 %collective-permute-start.13 = (bf16[128,512]{1,0:T(8,128)(2,1)S(1)}, bf16[128,512]{1,0:T(8,128)(2,1)S(1)}, u32[]{:S(2)}, u32[]{:S(2)}) collective-permute-start(bf16[128,512]{1,0:T(8,128)(2,1)S(1)} %get-tuple-element.118.own_r.refs_3_), channel_id=1, source_target_pairs={{0,2},{2,0},{1,3},{3,1},{4,6},{6,4},{5,7},{7,5},{8,10},{10,8},{9,1... | collective-permute-start | bytes 393224 | tf_op jit(solution)/shard_map/ppermute | solution.py:588

commit v6 on v5

--- a/solution.py
+++ b/solution.py
@@ -32,23 +32,24 @@
 
 
 FACTS = 16
-N0, N1, N2, OWNS2, LIMIT, LEADS, ROOT_IN_PAIR, ROOT_IN_HALF, NEXT_IN_CHIP = range(9)
+N0, N1, N2, OWNS2, LIMIT, LEADS, ROOT_IN_CHIP, ROOT_IN_PAIR, NEXT_IN_CHIP = range(9)
 
 
 def write_facts(facts, ids, counts):
-    own = ids[INNER] - 1
+    page = [ids[0, j] for j in range(INNER + 1)]
+    own = page[INNER] - 1
     leaf = own // SLOTS
-    owns = [ids[j] == own for j in range(INNER)]
-    same = lambda level, shift: ((ids[level] // SLOTS) >> shift) == (leaf >> shift)
+    owns = [page[j] == own for j in range(INNER)]
+    same = lambda level, shift: ((page[level] // SLOTS) >> shift) == (leaf >> shift)
     number = lambda flag: jnp.where(flag, 1, 0)
-    facts[N0] = jnp.where(owns[0] | owns[1] | owns[2], counts[0], 0)
-    facts[N1] = counts[1]
-    facts[N2] = counts[2]
+    facts[N0] = jnp.where(owns[0] | owns[1] | owns[2], counts[0, 0], 0)
+    facts[N1] = counts[0, 1]
+    facts[N2] = counts[0, 2]
     facts[OWNS2] = number(owns[2])
     facts[LIMIT] = jnp.where(owns[2], 2 * PAGE, jnp.where(owns[1], PAGE, 0))
     facts[LEADS] = number(lax.rem(leaf, 2) == 0)
-    facts[ROOT_IN_PAIR] = number(same(0, 1))
-    facts[ROOT_IN_HALF] = number(same(0, 2))
+    facts[ROOT_IN_CHIP] = number(same(0, 1))
+    facts[ROOT_IN_PAIR] = number(same(0, 2))
     facts[NEXT_IN_CHIP] = number(same(1, 1))
     for i in range(NEXT_IN_CHIP + 1, FACTS):
         facts[i] = 0
@@ -88,18 +89,26 @@
 def start(ids, counts, keys, values):
     width = keys.shape[1]
 
-    def body(ids_ref, counts_ref, k_ref, v_ref, facts, out, held, sem):
+    def body(ids_ref, counts_ref, k_ref, v_ref, facts, out, held, ids_s, counts_s, sem):
         copies = [
-            pltpu.make_async_copy(ref.at[:PAGE], held.at[i], sem.at[i])
-            for i, ref in enumerate((k_ref, v_ref))
+            pltpu.make_async_copy(src, dst, sem.at[i])
+            for i, (src, dst) in enumerate(
+                (
+                    (ids_ref, ids_s),
+                    (counts_ref, counts_s),
+                    (k_ref.at[:PAGE], held.at[0]),
+                    (v_ref.at[:PAGE], held.at[1]),
+                )
+            )
         ]
         for c in copies:
             c.start()
-        write_facts(facts, ids_ref, counts_ref)
-        for c in copies:
-            c.wait()
-        ok = row_ok(counts_ref[0], PAGE, width)
+        copies[0].wait()
+        copies[1].wait()
+        write_facts(facts, ids_s, counts_s)
+        ok = row_ok(counts_s[0, 0], PAGE, width)
         for i in range(2):
+            copies[2 + i].wait()
             out[i] = jnp.where(ok, held[i], jnp.zeros((), BF16))
 
     smem = pl.BlockSpec(memory_space=pltpu.SMEM)
@@ -107,9 +116,14 @@
     return pl.pallas_call(
         body,
         out_shape=(pltpu.SMEM((FACTS,), I32), pltpu.VMEM((2, PAGE, width), BF16)),
-        in_specs=[smem, smem, hbm, hbm],
+        in_specs=[hbm] * 4,
         out_specs=(smem, pl.BlockSpec(memory_space=pltpu.VMEM)),
-        scratch_shapes=[pltpu.VMEM((2, PAGE, width), BF16), pltpu.SemaphoreType.DMA((2,))],
+        scratch_shapes=[
+            pltpu.VMEM((2, PAGE, width), BF16),
+            pltpu.SMEM(ids.shape, I32),
+            pltpu.SMEM(counts.shape, I32),
+            pltpu.SemaphoreType.DMA((4,)),
+        ],
         compiler_params=pltpu.CompilerParams(vmem_limit_bytes=SMALL),
     )(ids, counts, keys, values)
 
@@ -187,8 +201,7 @@
     return p.astype(BF16), (p * grads).astype(BF16)
 
 
-def attend(own, kvs, group, facts, inputs, pages, state, w=None, prior=(), ride=None, after=(),
-           load=240):
+def attend(own, kvs, group, facts, inputs, pages, state, prior=(), after=()):
     loading = "loaded" not in state
     q, g, k, v, norms, deltas = inputs if loading else state["loaded"]
     count = len(kvs)
@@ -234,7 +247,7 @@
     else:
         outs += [
             ((2, PAGE, width), F32, True),
-            ((2 if ride is None else 4, PAGE, width), BF16, True),
+            ((2, PAGE, width), BF16, True),
         ]
     at_loaded = len(outs)
     in_names = ["q", "g", "k", "v", "norms", "deltas"]
@@ -245,16 +258,11 @@
             outs.append((array.shape, array.dtype, True))
         else:
             add_near(name, array)
-    at_w = len(outs)
-    if w is not None:
-        add_far("w", w)
-        outs.append((w.shape, w.dtype, True))
+    at_end = len(outs)
     for i, page in enumerate(pages):
         add_near(("page", i), page)
     for i, array in enumerate(prior):
         add_near(("prior", i), array)
-    if ride is not None:
-        add_near("ride", ride[0])
     key_pages = 4 if own else 2
     scratch = [
         pltpu.VMEM((2 * HD, key_pages * PAGE), BF16),
@@ -265,7 +273,7 @@
         pltpu.VMEM((ROWS, HD), BF16),
         pltpu.VMEM((count * parts, ROWS, wide), BF16),
         pltpu.SemaphoreType.DMA((count * parts,)),
-        pltpu.SemaphoreType.DMA((2 * kv_total + 5,)),
+        pltpu.SemaphoreType.DMA((2 * kv_total + 4,)),
     ]
     cols = lambda a, b: slice(a * PAGE, b * PAGE)
 
@@ -278,7 +286,7 @@
         results = out_refs[at_results:at_loaded]
         copies = {}
         if loading:
-            into = dict(zip(in_names, out_refs[at_loaded:at_w]))
+            into = dict(zip(in_names, out_refs[at_loaded:at_end]))
 
             def load(key, name, columns=None):
                 src, dst = far_ref(name), into[name]
@@ -295,11 +303,6 @@
                 load(("g", kv), "g", at)
         else:
             into = {name: near_ref(name) for name in in_names}
-        if w is not None:
-            w_copy = pltpu.make_async_copy(
-                far_ref("w"), out_refs[at_w], load_sem.at[2 * kv_total + 4]
-            )
-            w_copy.start()
         q, g, k, v, norms, deltas = (into[name] for name in in_names)
 
         def arrived(*keys):
@@ -311,8 +314,6 @@
         v_deep[HD:] = jnp.full((HD, key_pages * PAGE), -1.0, BF16)
         for out, i in zip(results, range(len(prior))):
             out[..., :base] = near_ref(("prior", i))[...]
-        if ride is not None:
-            results[1][2:] = near_ref("ride")[:, :, ride[1] : ride[1] + width]
         owns2, leads = facts[OWNS2] == 1, facts[LEADS] == 1
         if loading:
             arrived("norms", "deltas", "k", "v")
@@ -464,13 +465,11 @@
                 stage.at[slot], held["gq"].at[:, at : at + wide], sem.at[slot]
             ).wait()
         arrived(*list(copies))
-        if w is not None:
-            w_copy.wait()
 
     made = kernel_call(
         body, facts, near, far, outs, scratch, aliases, after,
         pl.CostEstimate(
-            flops=load * PAGE * PAGE * HD * group * count, bytes_accessed=1000, transcendentals=0
+            flops=240 * PAGE * PAGE * HD * group * count, bytes_accessed=1000, transcendentals=0
         ),
         LARGE,
     )
@@ -478,55 +477,48 @@
         state[name] = array
     state["done"] = state["done"] | set(kvs)
     if loading:
-        state["loaded"] = made[at_loaded:at_w]
-    results = list(made[at_results:at_loaded])
-    return results + ([made[at_w]] if w is not None else [])
-
-
-def input_grad(facts, side, w, rows, own=None, far=None, begun=None, grads=None, carry=None):
+        state["loaded"] = made[at_loaded:at_end]
+    return list(made[at_results:at_loaded])
+
+
+def width_tiles(w):
+    tile = next(t for t in (512, 640, 320, 128, w.shape[0]) if w.shape[0] % t == 0)
+    return [slice(i, i + tile) for i in range(0, w.shape[0], tile)]
+
+
+def input_grad(facts, side, w, rows, own, far, grads, carry=None):
     out_cols, depth = w.shape
-    tile = next(t for t in (640, 512, 320, 128, out_cols) if out_cols % t == 0)
+    tiles = width_tiles(w)
     top = 0 if rows == PAGE else PAGE
-    steps = out_cols // tile
+    steps = len(tiles)
     width = sum(a.shape[1] for a in grads[0])
-    own, far = list(own or []), list(far or [])
-    extra = [] if begun is None else [begun]
-    arrays = [w, *own, *far, *extra, *grads[0], *grads[1]]
+    arrays = [*own, *far, *grads[0], *grads[1]]
     count = len(grads[0])
-
-    def body(facts, flag, w_ref, *refs):
+    carry = list(carry or [])
+
+    def body(facts, flag, *refs):
         own_r, refs = refs[: len(own)], refs[len(own) :]
         far_r, refs = refs[: len(far)], refs[len(far) :]
-        begun_r, refs = refs[: len(extra)], refs[len(extra) :]
-        grad_r = refs[: 2 * count]
-        out, dk, dv, made, stage, sem = refs[-6:]
+        grad_r, w_ref = refs[: 2 * count], refs[2 * count]
+        out, dk, dv, made, w_near, stage, w_sem, sem = refs[-8:]
+        loads = [
+            pltpu.make_async_copy(w_ref.at[at], w_near.at[at], w_sem.at[i])
+            for i, at in enumerate(tiles)
+        ]
+        for c in loads:
+            c.start()
         made[...] = jnp.zeros_like(made)
-        copies = []
-        for dst, pieces in ((dk, grad_r[:count]), (dv, grad_r[count:])):
-            at = 0
-            for src in pieces:
-                here = dst.at[top : top + rows, at : at + src.shape[1]]
-                copies.append(pltpu.make_async_copy(src, here, sem.at[steps + len(copies)]))
-                copies[-1].start()
-                at += src.shape[1]
-        columns = lambda rs: jnp.concatenate([r[...] for r in rs], axis=1) if rs else None
-        mine, other = columns(own_r), columns(far_r)
-        half = depth // 2
-        where = slice(None)
-        if far and own:
-            lead = flag[0] == 0
-            mine = jnp.concatenate(
-                [jnp.where(lead, mine, other), jnp.where(lead, other, mine)], axis=1
+        columns = lambda rs: jnp.concatenate([r[...] for r in rs], axis=1)
+        full = columns(own_r)
+        if far:
+            other, leads = columns(far_r), flag[0] == 0
+            full = jnp.concatenate(
+                [jnp.where(leads, full, other), jnp.where(leads, other, full)], axis=1
             )
-        elif far:
-            mine = other
-            where = pl.ds(pl.multiple_of((1 - flag[0]) * half, half), half)
-        for i in range(steps):
-            at = slice(i * tile, (i + 1) * tile)
-            product = dot_t(w_ref[at, where], mine)
-            if extra:
-                product += begun_r[0][at]
-            stage[i] = product.T.astype(BF16)
+        copies = put_rows(grad_r, dk, dv, top, rows, sem, steps)
+        for i, at in enumerate(tiles):
+            loads[i].wait()
+            stage[i] = dot_t(w_near[at], full).astype(BF16).T
             copies.append(
                 pltpu.make_async_copy(stage.at[i], out.at[top : top + rows, at], sem.at[i])
             )
@@ -538,49 +530,102 @@
     vmem = pl.BlockSpec(memory_space=pltpu.VMEM)
     hbm = pl.BlockSpec(memory_space=pl.ANY)
     arrays = [pltpu.with_memory_space_constraint(a, pltpu.VMEM) for a in arrays]
-    carry = list(carry or [])
     kept = jax.ShapeDtypeStruct((ROWS, width), BF16)
     return pl.pallas_call(
         body,
         out_shape=(
             jax.ShapeDtypeStruct((ROWS, out_cols), BF16), kept, kept, pltpu.VMEM((8, HD), F32)
         ),
-        in_specs=[smem] * 2 + [vmem] * len(arrays) + [hbm] * len(carry),
+        in_specs=[smem] * 2 + [vmem] * len(arrays) + [hbm] * (1 + len(carry)),
         out_specs=(hbm, hbm, hbm, vmem),
         scratch_shapes=[
-            pltpu.VMEM((steps, rows, tile), BF16),
+            pltpu.VMEM(w.shape, BF16),
+            pltpu.VMEM((steps, rows, out_cols // steps), BF16),
+            pltpu.SemaphoreType.DMA((steps,)),
             pltpu.SemaphoreType.DMA((steps + 2 * count,)),
         ],
-        input_output_aliases={2 + len(arrays) + i: i for i in range(len(carry))},
+        input_output_aliases={3 + len(arrays) + i: i for i in range(len(carry))},
         compiler_params=pltpu.CompilerParams(vmem_limit_bytes=LARGE),
         cost_estimate=SLIGHT,
-    )(pltpu.with_memory_space_constraint(facts, pltpu.SMEM), side, *arrays, *carry)
+    )(pltpu.with_memory_space_constraint(facts, pltpu.SMEM), side, *arrays, w, *carry)
+
+
+def put_rows(pieces, dk, dv, top, rows, sem, first):
+    copies = []
+    count = len(pieces) // 2
+    for dst, mine in ((dk, pieces[:count]), (dv, pieces[count:])):
+        at = 0
+        for src in mine:
+            here = dst.at[top : top + rows, at : at + src.shape[1]]
+            copies.append(pltpu.make_async_copy(src, here, sem.at[first + len(copies)]))
+            copies[-1].start()
+            at += src.shape[1]
+    return copies
 
 
 def begin_input_grad(facts, side, w, own):
     out_cols, depth = w.shape
-    tile = next(t for t in (640, 512, 320, 128, out_cols) if out_cols % t == 0)
+    tiles = width_tiles(w)
     half = depth // 2
 
-    def body(facts, side_r, w_ref, own_r, out):
-        where = pl.ds(pl.multiple_of(side_r[0] * half, half), half)
-        for i in range(out_cols // tile):
-            at = slice(i * tile, (i + 1) * tile)
-            out[at] = dot_t(w_ref[at, where], own_r[...])
+    def body(facts, flag, own_r, w_ref, out, w_far, w_near, sem):
+        place = lambda which: pl.ds(pl.multiple_of(which * half, half), half)
+        loads = [
+            pltpu.make_async_copy(w_ref.at[at, place(flag[0])], w_near.at[at], sem.at[i])
+            for i, at in enumerate(tiles)
+        ]
+        rest = pltpu.make_async_copy(w_ref.at[:, place(1 - flag[0])], w_far, sem.at[len(tiles)])
+        for c in [*loads, rest]:
+            c.start()
+        for i, at in enumerate(tiles):
+            loads[i].wait()
+            out[at] = dot_t(w_near[at], own_r[...])
+        rest.wait()
 
     smem = pl.BlockSpec(memory_space=pltpu.SMEM)
     vmem = pl.BlockSpec(memory_space=pltpu.VMEM)
-    arrays = [pltpu.with_memory_space_constraint(a, pltpu.VMEM) for a in (w, own)]
     return pl.pallas_call(
         body,
-        out_shape=pltpu.VMEM((out_cols, own.shape[0]), F32),
-        in_specs=[smem, smem, vmem, vmem],
-        out_specs=vmem,
+        out_shape=(pltpu.VMEM((out_cols, own.shape[0]), F32), pltpu.VMEM((out_cols, half), BF16)),
+        in_specs=[smem, smem, vmem, pl.BlockSpec(memory_space=pl.ANY)],
+        out_specs=(vmem, vmem),
+        scratch_shapes=[
+            pltpu.VMEM((out_cols, half), BF16), pltpu.SemaphoreType.DMA((len(tiles) + 1,))
+        ],
         compiler_params=pltpu.CompilerParams(vmem_limit_bytes=LARGE),
         cost_estimate=pl.CostEstimate(
             flops=own.shape[0] * depth * out_cols, bytes_accessed=1000, transcendentals=0
         ),
-    )(pltpu.with_memory_space_constraint(facts, pltpu.SMEM), side, *arrays)
+    )(
+        pltpu.with_memory_space_constraint(facts, pltpu.SMEM), side,
+        pltpu.with_memory_space_constraint(own, pltpu.VMEM), w,
+    )
+
+
+def end_input_grad(facts, far, begun, w_far, grads, carry):
+    tiles = width_tiles(w_far)
+    steps = len(tiles)
+    rows = far.shape[0]
+
+    def body(facts, far_r, begun_r, w_r, *refs):
+        out, dk, dv, stage, sem = refs[-5:]
+        copies = put_rows(refs[:2], dk, dv, 0, rows, sem, steps)
+        for i, at in enumerate(tiles):
+            stage[i] = (dot_t(w_r[at], far_r[...]) + begun_r[at]).astype(BF16).T
+            copies.append(pltpu.make_async_copy(stage.at[i], out.at[:rows, at], sem.at[i]))
+            copies[-1].start()
+        for c in copies:
+            c.wait()
+
+    return kernel_call(
+        body, facts, [far, begun, w_far, *grads], carry,
+        [(a.shape, a.dtype, False) for a in carry],
+        [
+            pltpu.VMEM((steps, rows, w_far.shape[0] // steps), BF16),
+            pltpu.SemaphoreType.DMA((steps + 2,)),
+        ],
+        {("far", i): i for i in range(len(carry))},
+    )
 
 
 def flipped(block, axis, bit):
@@ -609,14 +654,14 @@
     from_pair = flipped(chip, "leaf", 1)
 
     def choose_pair(facts, near_ref, far_ref, out):
-        out[...] = jnp.where(facts[ROOT_IN_PAIR] == 1, near_ref[...], far_ref[...])
+        out[...] = jnp.where(facts[ROOT_IN_CHIP] == 1, near_ref[...], far_ref[...])
 
     after = beside_pair(from_core, chip)
     (pair,) = kernel_call(choose_pair, facts, [chip, from_pair], [], [page], after=after)
     from_half = flipped(pair, "leaf", 2)
 
     def choose_all(facts, chip_ref, pair_far, pair_ref, half_far, out):
-        out[0] = jnp.where(facts[ROOT_IN_HALF] == 1, pair_ref[...], half_far[...])
+        out[0] = jnp.where(facts[ROOT_IN_PAIR] == 1, pair_ref[...], half_far[...])
         out[1] = jnp.where(facts[NEXT_IN_CHIP] == 1, chip_ref[...], pair_far[...])
 
     after = beside_half(pair)
@@ -626,67 +671,46 @@
     return mine, flipped(mine, "sub", 1)
 
 
-class Reduction:
-    def __init__(self, facts, kept, sent):
-        self.facts, self.kept = facts, kept
-        self.width = sum(k.shape[-1] for k in kept)
-        self.first_far = [flipped(s, "sub", 1) for s in sent]
-
-    def call(self, body, near, outs, after):
-        return kernel_call(body, self.facts, near, [], outs, after=after)
-
-    def over_cores(self, after=()):
-        count = len(self.kept)
-
-        def body(_, *refs):
-            total, low = refs[-2:]
-            at = 0
-            for near, away in zip(refs[:count], refs[count : 2 * count]):
-                here = slice(at, at + near.shape[-1])
-                at += near.shape[-1]
-                value = near[...] + away[:2].astype(F32)
-                total[:, :, here] = value
-                low[:, :, here] = value.astype(BF16)
-
-        two = (2, PAGE, self.width)
-        self.total, low = self.call(
-            body, [*self.kept, *self.first_far], [(two, F32, True), (two, BF16, True)], after
-        )
-        self.far = flipped(low, "leaf", 1)
-        return low
-
-
-def over_pair(facts, pieces, handed=()):
-    count = len(pieces)
-    width = sum(r.width for r in pieces)
-
-    def body(_, *refs):
-        ins, handed_in = refs[: 2 * count], refs[2 * count : 2 * count + len(handed)]
-        total, low = refs[2 * count + len(handed) :][:2]
-        at = 0
-        for near, away in zip(ins[:count], ins[count:]):
-            here = slice(at, at + near.shape[-1])
-            at += near.shape[-1]
-            value = near[...] + away[...].astype(F32)
-            total[:, :, here] = value
-            low[:, here] = value[0].astype(BF16)
-        for src, dst in zip(handed_in, refs[2 * count + len(handed) + 2 :]):
-            dst[...] = src[...]
-
-    outs = [((2, PAGE, width), F32, True), ((PAGE, width), BF16, True)]
-    outs += [(a.shape, a.dtype, True) for a in handed]
-    near = [r.total for r in pieces] + [r.far for r in pieces] + list(handed)
-    total, low, *passed = kernel_call(body, facts, near, [], outs)
-    return total, flipped(low, "leaf", 2), passed
-
-
-def over_half(facts, total, far, passenger, after=()):
+def over_cores(facts, kept, sent):
+    width = kept.shape[-1]
+
+    def body(_, near, away, total, root, next_one):
+        for j, low in enumerate((root, next_one)):
+            value = near[j] + away[j].astype(F32)
+            total[j] = value
+            low[...] = value.astype(BF16)
+
+    page = ((PAGE, width), BF16, True)
+    total, root, next_one = kernel_call(
+        body, facts, [kept, flipped(sent, "sub", 1)], [],
+        [((2, PAGE, width), F32, True), page, page],
+    )
+    return total, root, flipped(root, "leaf", 2), flipped(next_one, "leaf", 1)
+
+
+def over_halves(facts, total, root_far, next_far, after):
+    width = total.shape[-1]
+
+    def body(_, near, root_r, next_r, out, low):
+        root = near[0] + root_r[...].astype(F32)
+        out[0] = root
+        low[...] = root.astype(BF16)
+        out[1] = near[1] + next_r[...].astype(F32)
+
+    total, low = kernel_call(
+        body, facts, [total, root_far, next_far], [],
+        [((2, PAGE, width), F32, True), ((PAGE, width), BF16, True)], after=after,
+    )
+    return total, flipped(low, "leaf", 1)
+
+
+def over_chips(facts, total, far, passenger, after=()):
     width = total.shape[-1]
     more = passenger.shape[-1]
 
     def body(facts, near, away, extra, out):
         root = near[0] + away[...].astype(F32)
-        out[:, :width] = jnp.where(facts[ROOT_IN_PAIR] == 1, root, near[1]).astype(BF16)
+        out[:, :width] = jnp.where(facts[ROOT_IN_CHIP] == 1, root, near[1]).astype(BF16)
         for kind in range(2):
             out[:, width + kind * more : width + (kind + 1) * more] = extra[kind]
 
@@ -695,11 +719,10 @@
     return mine, flipped(mine, "sub", 1)
 
 
-def finish_small_tree(facts, own0, mine, far, lead2, tail2):
+def finish_small_tree(facts, own0, mine, far, level2_far):
     width = sum(a.shape[-1] for a in own0)
-    half = width // 2
-
-    def body(facts, own_r, own_last, mine_r, far_r, lead_r, tail_r, dk, dv):
+
+    def body(facts, own_r, own_last, mine_r, far_r, low_r, dk, dv):
         owns2, leads = facts[OWNS2] == 1, facts[LEADS] == 1
         ok = row_ok(facts[N0], PAGE, HD)
         for at in range(0, width, HD):
@@ -710,16 +733,14 @@
             for kind, out in enumerate((dk, dv)):
                 if last:
                     level2 = far_r[:, width + kind * HD : width + (kind + 1) * HD]
-                elif at < half:
-                    level2 = lead_r[2 + kind, :, c]
                 else:
-                    level2 = tail_r[2 + kind, :, at - half : at - half + HD]
+                    level2 = low_r[kind, :, c]
                 more = jnp.where(owns2, level2, gained[kind]).astype(F32)
                 base = own_last[kind] if last else own_r[kind, :, c]
                 out[:, c] = jnp.where(ok, base + more, 0.0).astype(BF16)
 
     page = ((PAGE, width), BF16, True)
-    return kernel_call(body, facts, [*own0, mine, far, lead2, tail2], [], [page, page])
+    return kernel_call(body, facts, [*own0, mine, far, level2_far], [], [page, page])
 
 
 def gather_tree(ids, own):
@@ -751,69 +772,56 @@
     side = lax.axis_index("tensor").astype(I32).reshape(1)
     two_sides = lax.axis_size("tensor") == 2
     inputs = [hbm(a) for a in (queries, grad_out, keys, values, log_norms, row_deltas)]
-    facts, own = start(hbm(ancestors[0]), hbm(counts[0]), *inputs[2:4])
+    facts, own = start(hbm(ancestors), hbm(counts), *inputs[2:4])
     state = {"done": frozenset()}
 
-    def own_pages(kvs, pages, prior=(), after=(), w=None, load=240):
-        return attend(
-            True, kvs, group, facts, inputs, pages, state, w, prior, after=after, load=load
-        )
-
-    def shared_pages(kvs, pages, ride=None, after=()):
-        return attend(False, kvs, group, facts, inputs, pages, state, ride=ride, after=after)
+    def own_pages(kvs, pages, prior=(), after=()):
+        return attend(True, kvs, group, facts, inputs, pages, state, prior, after)
+
+    def shared_pages(kvs, pages, after=()):
+        return attend(False, kvs, group, facts, inputs, pages, state, after=after)
 
     def spread(part):
         if two_sides:
             return flipped(part, "tensor", 1)
         return lax.all_gather(part, "tensor", axis=1, tiled=True)
 
-    if leaves == 8 and lax.axis_size("sub") == 2 and kv == 4 and two_sides:
+    kvs = tuple(range(kv))
+    w = hbm(w_value)
+    if leaves == 8 and lax.axis_size("sub") == 2 and kv >= 3 and two_sides:
         level2, results = [], []
 
         def beside_pair(from_core, chip):
             level2.extend((own, from_core))
-            results.append(own_pages((0,), level2, after=(chip,)))
+            results.append(own_pages(kvs[:1], level2, after=(chip,)))
             return (results[-1][3],)
 
         def beside_half(pair):
-            results.append(own_pages((1, 2), level2, results[-1], (pair,)))
+            results.append(own_pages(kvs[1:-1], level2, results[-1], (pair,)))
             return (results[-1][3],)
 
         shared = gather_small_tree(facts, own, beside_pair, beside_half)
-        _, dv12, _, send2 = results[-1]
-        far_v = [spread(dv12)]
-        kept, sent = shared_pages((0, 1), shared, (send2, 0))
-        lead = Reduction(facts, [kept], [sent])
-        kept, sent = shared_pages((2,), shared, ride=(send2, 2 * HD), after=far_v)
-        low = lead.over_cores((kept,))
-        last_kept, last_sent = shared_pages((3,), shared, after=(low,))
-        tail = Reduction(facts, [kept, last_kept], [sent, last_sent])
-        *last, w_near = own_pages(
-            (3,), level2, after=(tail.over_cores((lead.far,)),), w=hbm(w_value)
-        )
-        total, from_half, (last[1],) = over_pair(facts, [lead, tail], [last[1]])
+        most = results[-1]
+        far_v = [spread(most[1])]
+        level2_far = flipped(most[3], "sub", 1)
+        kept, sent = shared_pages(kvs, shared)
+        total, root, root_far, next_far = over_cores(facts, kept, sent)
+        last = own_pages(kvs[-1:], level2, after=(root, far_v[0], level2_far))
         far_v.append(spread(last[1]))
-        near_v = [dv12, last[1]]
-        both = list(zip(results[-1], last))
-        *grads, made = input_grad(
-            facts, side, w_near, 2 * PAGE, near_v, far_v, grads=both[:2]
-        )
-        dk0, dv0 = finish_small_tree(
-            facts, both[2], *over_half(facts, total, from_half, last[3], (made,)),
-            lead.first_far[0], tail.first_far[0],
-        )
-        far_v = [spread(dv0)]
-        begun = begin_input_grad(facts, side, w_near, dv0)
-        grad_input, grad_keys, grad_values, _ = input_grad(
-            facts, side, w_near, PAGE, far=far_v, begun=begun, grads=([dk0], [dv0]), carry=grads
-        )
-        return (state["gq"], grad_keys, grad_values, grad_input)
-
-    kvs = tuple(range(kv))
+        total, far = over_halves(facts, total, root_far, next_far, (last[3],))
+        both = list(zip(most, last))
+        *grads, made = input_grad(facts, side, w, 2 * PAGE, both[1], far_v, both[:2])
+        mine, far = over_chips(facts, total, far, last[3], (made,))
+        dk0, dv0 = finish_small_tree(facts, both[2], mine, far, level2_far)
+        far_v = spread(dv0)
+        begun, w_far = begin_input_grad(facts, side, w, dv0)
+        grads = end_input_grad(facts, far_v, begun, w_far, [dk0, dv0], grads)
+        return (state["gq"], grads[1], grads[2], grads[0])
+
     first = lax.axis_index("sub") == 0
     path_ids = ancestors[0]
     pages = gather_tree(path_ids, own)
-    dk12, dv12, own0, send2, w_near = own_pages(kvs, (pages[2], pages[2]), w=hbm(w_value))
+    dk12, dv12, own0, send2 = own_pages(kvs, (pages[2], pages[2]))
     kept, sent = shared_pages(
         kvs,
         (
@@ -832,14 +840,10 @@
     if two_sides:
         pair = lambda part: ([part], [spread(part)])
     else:
-        pair = lambda part: ([spread(part)], None)
-    *grads, _ = input_grad(
-        facts, side, w_near, 2 * PAGE, *pair(dv12), grads=([dk12], [dv12])
-    )
-    grad_input, grad_keys, grad_values, _ = input_grad(
-        facts, side, w_near, PAGE, *pair(dv0), grads=([dk0], [dv0]), carry=grads
-    )
-    return (state["gq"], grad_keys, grad_values, grad_input)
+        pair = lambda part: ([spread(part)], [])
+    *grads, _ = input_grad(facts, side, w, 2 * PAGE, *pair(dv12), ([dk12], [dv12]))
+    grads = input_grad(facts, side, w, PAGE, *pair(dv0), ([dk0], [dv0]), grads)
+    return (state["gq"], grads[1], grads[2], grads[0])
 
 
 def solution(mesh):

time: 67 us -> 60.3 us (0.90)
  local copies, waits for them, and re-layouts: 4.81 us -> 0 us
  starting transfers between devices: 15.2 us -> 13.6 us
    unnamed x6 -> x0, local copies, waits for them, and re-layouts: 4.81 us -> none
    pallas_call x1, Pallas kernels: 0.83 us -> 3.09 us  [begin_input_grad(): pl.pallas_call(body, out_shape=(pltpu.VMEM((out_cols, own.shape[0]), F32)...]
    pallas_call x14 -> x12, Pallas kernels: 24.4 us -> 22.2 us  [kernel_call(): pl.pallas_call(kernel, out_shape=tuple((pltpu.VMEM(s, d) if inside else j...]
    ppermute x14 -> x13, starting transfers between devices: 15.2 us -> 13.6 us  [flipped(): lax.ppermute(block, axis, [(i, i ^ bit) for i in range(count) if i ^ bit...]
    pallas_call x2 -> x1, Pallas kernels: 4.85 us -> 5.87 us  [input_grad(): pl.pallas_call(body, out_shape=(jax.ShapeDtypeStruct((ROWS, out_cols), BF...]
    ppermute x14 -> x13, waiting for transfers between devices: 14 us -> 13.4 us  [flipped(): lax.ppermute(block, axis, [(i, i ^ bit) for i in range(count) if i ^ bit...]
  transfers between devices with their start and end apart: 14 -> 13, of which waited for: 8 -> 9; matrix products, arithmetic and copies ran while one was open for 0% -> 0% of each run, Pallas kernels for 41% -> 36%
where the time goes in v6:
time: 60.3 us; the launch traced here: 60.2 us
  Pallas kernels  32.2 us (53%)
  starting transfers between devices  13.6 us (23%)
  waiting for transfers between devices  13.4 us (22%)
  between operations  0.94 us (2%)
    pallas_call x12, Pallas kernels, kernel_call(): pl.pallas_call(kernel, out_shape=tuple((pltpu.VMEM(s, d) if inside else j...  22.2 us
    ppermute x13, starting transfers between devices, flipped(): lax.ppermute(block, axis, [(i, i ^ bit) for i in range(count) if i ^ bit...  13.6 us
    ppermute x13, waiting for transfers between devices, flipped(): lax.ppermute(block, axis, [(i, i ^ bit) for i in range(count) if i ^ bit...  13.4 us
    pallas_call x1, Pallas kernels, input_grad(): pl.pallas_call(body, out_shape=(jax.ShapeDtypeStruct((ROWS, out_cols), BF...  5.87 us
    pallas_call x1, Pallas kernels, begin_input_grad(): pl.pallas_call(body, out_shape=(pltpu.VMEM((out_cols, own.shape[0]), F32)...  3.09 us
  transfers between devices with their start and end apart: 13, of which 9 were waited for; matrix products, arithmetic and copies ran while one was open for 0% of the time, Pallas kernels for 36%

profile of v6, /device:TPU:0, one launch (start us, length us, event | category | flops | bytes accessed | tf_op | source)
XLA Modules:
  0.0 60.2 jit_solution(17781025231990847207)
XLA Ops:
  0.6 1.0 %shard_map.120 = (s32[16]{0:T(128)S(4)}, bf16[2,128,512]{2,1,0:T(8,128)(2,1)S(1)}) custom-call(s32[1,5]{1,0:T(1,128)} %ids_ref.1, s32[1,3]{1,0:T(1,128)} %counts_ref.1, bf16[384,512]{1,0:T(8,128)(2,1)} %refs_5_.1, bf16[384,512]{1,0:T(8,128)(2,1)} %refs_6_.1), custom_call_target="tpu_custom_call" | custom-call | tf_op jit(solution)/shard_map/pallas_call | solution.py:116
  1.7 0.5 collective-permute-start
  2.2 1.2 %collective-permute-done.refs_2_.refs_11_ = bf16[2,128,512]{2,1,0:T(8,128)(2,1)S(1)} collective-permute-done((bf16[2,128,512]{2,1,0:T(8,128)(2,1)S(1)}, bf16[2,128,512]{2,1,0:T(8,128)(2,1)S(1)}, u32[]{:S(2)}, u32[]{:S(2)}) %collective-permute-start) | collective-permute-done | bytes 262176 | tf_op jit(solution)/shard_map/ppermute | solution.py:633
  3.4 3.0 %collective-permute-start.1 = (bf16[128,512]{1,0:T(8,128)(2,1)S(1)}, bf16[128,512]{1,0:T(8,128)(2,1)S(1)}, u32[]{:S(2)}, u32[]{:S(2)}) collective-permute-start(bf16[128,512]{1,0:T(8,128)(2,1)S(1)} %shard_map.121.refs_9_.refs_1_), channel_id=1, source_target_pairs={{0,4},{4,0},{8,12},{12,8},{1,5},{5,1},{9,13},{13,9},{2,6},{6,2},{1... | collective-permute-start | bytes 393224 | tf_op jit(solution)/shard_map/ppermute | solution.py:633
  6.4 4.3 %shard_map.122 = (f32[384,4096]{1,0:T(8,128)S(1)}, bf16[128,12288]{1,0:T(8,128)(2,1)S(1)}, bf16[128,12288]{1,0:T(8,128)(2,1)S(1)}, bf16[256,128]{1,0:T(8,128)(2,...) custom-call(s32[16]{0:T(128)S(4)} %get-tuple-element.53.refs_0_.fact, ...), custom_call_target="tpu_custom_call" | custom-call | flops 4026531840 | bytes 1000 | tf_op jit(solution)/shard_map/pallas_call | solution.py:75
  10.7 0.0 collective-permute-done.1.refs_2_
  10.7 2.6 %collective-permute-start.2 = (bf16[128,512]{1,0:T(8,128)(2,1)S(1)}, bf16[128,512]{1,0:T(8,128)(2,1)S(1)}, u32[]{:S(2)}, u32[]{:S(2)}) collective-permute-start(bf16[128,512]{1,0:T(8,128)(2,1)S(1)} %shard_map.123.refs_16_.refs_3_), channel_id=1, source_target_pairs={{0,8},{4,12},{8,0},{12,4},{1,9},{5,13},{9,1},{13,5},{2,10},{6,14},... | collective-permute-start | bytes 393224 | tf_op jit(solution)/shard_map/ppermute | solution.py:633
  13.4 4.9 %shard_map.124 = (f32[384,4096]{1,0:T(8,128)S(1)}, bf16[128,12288]{1,0:T(8,128)(2,1)S(1)}, bf16[128,12288]{1,0:T(8,128)(2,1)S(1)}, bf16[256,384]{1,0:T(8,128)(2,...) custom-call(s32[16]{0:T(128)S(4)} %get-tuple-element.53.refs_0_.fact, ...), custom_call_target="tpu_custom_call", output_to_operand_aliasing={{0}: (1, {}), {1}: (2, {}), {2}: (3, {})} | custom-call | flops 8053063680 | bytes 1000 | tf_op jit(solution)/shard_map/pallas_call | solution.py:75
  18.3 1.5 %collective-permute-done.2.refs_4_ = bf16[128,512]{1,0:T(8,128)(2,1)S(1)} collective-permute-done((bf16[128,512]{1,0:T(8,128)(2,1)S(1)}, bf16[128,512]{1,0:T(8,128)(2,1)S(1)}, u32[]{:S(2)}, u32[]{:S(2)}) %collective-permute-start.2) | collective-permute-done | bytes 131104 | tf_op jit(solution)/shard_map/ppermute | solution.py:633
  19.8 0.1 collective-permute-start.3
  19.8 1.5 %collective-permute-done.3.refs_11_ = bf16[2,128,512]{2,1,0:T(8,128)(2,1)S(1)} collective-permute-done((bf16[2,128,512]{2,1,0:T(8,128)(2,1)S(1)}, bf16[2,128,512]{2,1,0:T(8,128)(2,1)S(1)}, u32[]{:S(2)}, u32[]{:S(2)}) %collective-permute-start.3) | collective-permute-done | bytes 262176 | tf_op jit(solution)/shard_map/ppermute | solution.py:633
  21.4 7.7 %shard_map.126 = (f32[384,4096]{1,0:T(8,128)S(1)}, bf16[128,12288]{1,0:T(8,128)(2,1)S(1)}, bf16[128,12288]{1,0:T(8,128)(2,1)S(1)}, bf16[384,4096]{1,0:T(8,128)(2...) custom-call(s32[16]{0:T(128)S(4)} %get-tuple-element.53.refs_0_.fact, ...), custom_call_target="tpu_custom_call", output_to_operand_aliasing={{0}: (1, {}), {1}: (2, {}), {2}: (3, {})} | custom-call | flops 16106127360 | bytes 1000 | tf_op jit(solution)/shard_map/pallas_call | solution.py:75
  29.0 0.2 collective-permute-start.4
  29.2 1.5 %collective-permute-start.5 = (bf16[256,384]{1,0:T(8,128)(2,1)S(1)}, bf16[256,384]{1,0:T(8,128)(2,1)S(1)}, u32[]{:S(2)}, u32[]{:S(2)}) collective-permute-start(bf16[256,384]{1,0:T(8,128)(2,1)S(1)} %get-tuple-element.79.refs_0_.refs_6_), channel_id=1, source_target_pairs={{0,2},{2,0},{1,3},{3,1},{4,6},{6,4},{5,7},{7,5},{8,10},{10,8},{9,1... | collective-permute-start | bytes 589832 | tf_op jit(solution)/shard_map/ppermute | solution.py:633
  30.8 0.1 collective-permute-start.6
  30.8 0.0 collective-permute-done.4.refs_2_
  30.8 0.1 shard_map.127
  30.9 0.1 collective-permute-start.7
  31.0 3.3 %collective-permute-start.8 = (bf16[128,512]{1,0:T(8,128)(2,1)S(1)}, bf16[128,512]{1,0:T(8,128)(2,1)S(1)}, u32[]{:S(2)}, u32[]{:S(2)}) collective-permute-start(bf16[128,512]{1,0:T(8,128)(2,1)S(1)} %get-tuple-element.84), channel_id=1, source_target_pairs={{0,4},{4,0},{8,12},{12,8},{1,5},{5,1},{9,13},{13,9},{2,6},{6,2},{1... | collective-permute-start | bytes 393224 | tf_op jit(solution)/shard_map/ppermute | solution.py:633
  34.2 2.2 %collective-permute-done.5.refs_14_.refs_2_ = bf16[256,384]{1,0:T(8,128)(2,1)S(1)} collective-permute-done((bf16[256,384]{1,0:T(8,128)(2,1)S(1)}, bf16[256,384]{1,0:T(8,128)(2,1)S(1)}, u32[]{:S(2)}, u32[]{:S(2)}) %collective-permute-start.5) | collective-permute-done | bytes 196640 | tf_op jit(solution)/shard_map/ppermute | solution.py:633
  36.4 0.0 collective-permute-done.6.refs_15_.refs_5_
  36.4 3.4 %shard_map.128 = (f32[384,4096]{1,0:T(8,128)S(1)}, bf16[128,12288]{1,0:T(8,128)(2,1)S(1)}, bf16[128,12288]{1,0:T(8,128)(2,1)S(1)}, bf16[384,4096]{1,0:T(8,128)(2...) custom-call(s32[16]{0:T(128)S(4)} %get-tuple-element.53.refs_0_.fact, ...), custom_call_target="tpu_custom_call", output_to_operand_aliasing={{0}: (1, {}), {1}: (2, {}), {2}: (3, {}), {3}: (12, {})} | custom-call | flops 4026531840 | bytes 1000 | tf_op jit(solution)/shard_map/pallas_call | solution.py:75
  39.8 0.8 %collective-permute-done.7.refs_2_ = bf16[128,512]{1,0:T(8,128)(2,1)S(1)} collective-permute-done((bf16[128,512]{1,0:T(8,128)(2,1)S(1)}, bf16[128,512]{1,0:T(8,128)(2,1)S(1)}, u32[]{:S(2)}, u32[]{:S(2)}) %collective-permute-start.7) | collective-permute-done | bytes 131104 | tf_op jit(solution)/shard_map/ppermute | solution.py:633
  40.6 0.1 collective-permute-done.8.refs_3_
  40.7 0.1 shard_map.129
  40.8 0.1 collective-permute-start.9
  40.9 1.0 %collective-permute-start.10 = (bf16[256,128]{1,0:T(8,128)(2,1)S(1)}, bf16[256,128]{1,0:T(8,128)(2,1)S(1)}, u32[]{:S(2)}, u32[]{:S(2)}) collective-permute-start(bf16[256,128]{1,0:T(8,128)(2,1)S(1)} %get-tuple-element.88.refs_1_.refs_7_), channel_id=1, source_target_pairs={{0,2},{2,0},{1,3},{3,1},{4,6},{6,4},{5,7},{7,5},{8,10},{10,8},{9,1... | collective-permute-start | bytes 196616 | tf_op jit(solution)/shard_map/ppermute | solution.py:633
  41.9 3.3 %collective-permute-done.10.refs_3_ = bf16[256,128]{1,0:T(8,128)(2,1)S(1)} collective-permute-done((bf16[256,128]{1,0:T(8,128)(2,1)S(1)}, bf16[256,128]{1,0:T(8,128)(2,1)S(1)}, u32[]{:S(2)}, u32[]{:S(2)}) %collective-permute-start.10) | collective-permute-done | bytes 65568 | tf_op jit(solution)/shard_map/ppermute | solution.py:633
  45.2 5.9 %shard_map.130 = (bf16[384,2560]{1,0:T(8,128)(2,1)}, bf16[384,512]{1,0:T(8,128)(2,1)}, bf16[384,512]{1,0:T(8,128)(2,1)}, f32[8,128]{1,0:T(8,128)S(1)}) custom-call(s32[16]{0:T(128)S(4)} %get-tuple-element.53.refs_0_.facts, s32[1]{0:T(128)} %bitcast.flag, bf16[256,384]{1,0:T(8,128)(2,1)S(1)} %get-tuple-element.79.refs_0_.refs_6_, ...), custom_call_target="tpu_custom_call" | custom-call | flops 1000 | bytes 1000 | tf_op jit(solution)/shard_map/pallas_call | solution.py:534
  51.1 0.0 collective-permute-done.9.refs_2_
  51.1 0.1 collective-permute-start.11
  51.2 1.4 %collective-permute-done.11.refs_4_ = bf16[128,768]{1,0:T(8,128)(2,1)S(1)} collective-permute-done((bf16[128,768]{1,0:T(8,128)(2,1)S(1)}, bf16[128,768]{1,0:T(8,128)(2,1)S(1)}, u32[]{:S(2)}, u32[]{:S(2)}) %collective-permute-start.11) | collective-permute-done | bytes 196640 | tf_op jit(solution)/shard_map/ppermute | solution.py:633
  52.6 0.1 shard_map.132
  52.8 1.1 %collective-permute-start.12 = (bf16[128,512]{1,0:T(8,128)(2,1)S(1)}, bf16[128,512]{1,0:T(8,128)(2,1)S(1)}, u32[]{:S(2)}, u32[]{:S(2)}) collective-permute-start(bf16[128,512]{1,0:T(8,128)(2,1)S(1)} %get-tuple-element.92.own_r.refs_5_), channel_id=1, source_target_pairs={{0,2},{2,0},{1,3},{3,1},{4,6},{6,4},{5,7},{7,5},{8,10},{10,8},{9,1... | collective-permute-start | bytes 393224 | tf_op jit(solution)/shard_map/ppermute | solution.py:633
  53.8 3.1 %shard_map.133 = (f32[2560,128]{1,0:T(8,128)S(1)}, bf16[2560,512]{1,0:T(8,128)(2,1)S(1)}) custom-call(s32[16]{0:T(128)S(4)} %get-tuple-element.53.refs_0_.facts, s32[1]{0:T(128)} %bitcast.flag, bf16[128,512]{1,0:T(8,128)(2,1)S(1)} %get-tuple-element.92.own_r.refs_5_, bf16[2560,1024]{1,0:T(8,128)(2,1)} %w_ref.1), custom_call_target="tpu_custom_call" | custom-call | flops 335544320 | bytes 1000 | tf_op jit(solution)/shard_map/pallas_call | solution.py:587
  56.9 1.5 %collective-permute-done.12.refs_1_ = bf16[128,512]{1,0:T(8,128)(2,1)S(1)} collective-permute-done((bf16[128,512]{1,0:T(8,128)(2,1)S(1)}, bf16[128,512]{1,0:T(8,128)(2,1)S(1)}, u32[]{:S(2)}, u32[]{:S(2)}) %collective-permute-start.12) | collective-permute-done | bytes 131104 | tf_op jit(solution)/shard_map/ppermute | solution.py:633
  58.4 1.7 %shard_map.134 = (bf16[384,2560]{1,0:T(8,128)(2,1)}, bf16[384,512]{1,0:T(8,128)(2,1)}, bf16[384,512]{1,0:T(8,128)(2,1)}) custom-call(s32[16]{0:T(128)S(4)} %get-tuple-element.53.refs_0_.facts, bf16[128,512]{1,0:T(8,128)(2,1)S(1)} %collective-permute-done.12.refs_1_, ...), custom_call_target="tpu_custom_call", output_to_operand_aliasing={{0}: (6, {}), {1}: (7, {}), {2}: (8, {})} | custom-call | flops 1000 | bytes 1000 | tf_op jit(solution)/shard_map/pallas_call | solution.py:75
  (4 shorter events, 0.1 us)
Async XLA Ops:
  1.7 1.7 %collective-permute-start = (bf16[2,128,512]{2,1,0:T(8,128)(2,1)S(1)}, bf16[2,128,512]{2,1,0:T(8,128)(2,1)S(1)}, u32[]{:S(2)}, u32[]{:S(2)}) collective-permute-start(bf16[2,128,512]{2,1,0:T(8,128)(2,1)S(1)} %get-tuple-element.54.refs_1_.refs_10_), channel_id=1, source_target_pairs={{0,1},{1,0},{2,3},{3,2},{4,5},{5,4},{6,7},{7,6},{8,9},{9,8},{10,11... | collective-permute-start | bytes 786440 | tf_op jit(solution)/shard_map/ppermute | solution.py:633
  3.4 7.3 %collective-permute-start.1 = (bf16[128,512]{1,0:T(8,128)(2,1)S(1)}, bf16[128,512]{1,0:T(8,128)(2,1)S(1)}, u32[]{:S(2)}, u32[]{:S(2)}) collective-permute-start(bf16[128,512]{1,0:T(8,128)(2,1)S(1)} %shard_map.121.refs_9_.refs_1_), channel_id=1, source_target_pairs={{0,4},{4,0},{8,12},{12,8},{1,5},{5,1},{9,13},{13,9},{2,6},{6,2},{1... | collective-permute-start | bytes 393224 | tf_op jit(solution)/shard_map/ppermute | solution.py:633
  10.7 9.0 %collective-permute-start.2 = (bf16[128,512]{1,0:T(8,128)(2,1)S(1)}, bf16[128,512]{1,0:T(8,128)(2,1)S(1)}, u32[]{:S(2)}, u32[]{:S(2)}) collective-permute-start(bf16[128,512]{1,0:T(8,128)(2,1)S(1)} %shard_map.123.refs_16_.refs_3_), channel_id=1, source_target_pairs={{0,8},{4,12},{8,0},{12,4},{1,9},{5,13},{9,1},{13,5},{2,10},{6,14},... | collective-permute-start | bytes 393224 | tf_op jit(solution)/shard_map/ppermute | solution.py:633
  19.8 1.6 %collective-permute-start.3 = (bf16[2,128,512]{2,1,0:T(8,128)(2,1)S(1)}, bf16[2,128,512]{2,1,0:T(8,128)(2,1)S(1)}, u32[]{:S(2)}, u32[]{:S(2)}) collective-permute-start(bf16[2,128,512]{2,1,0:T(8,128)(2,1)S(1)} %shard_map.125.refs_10_), channel_id=1, source_target_pairs={{0,1},{1,0},{2,3},{3,2},{4,5},{5,4},{6,7},{7,6},{8,9},{9,8},{10,11... | collective-permute-start | bytes 786440 | tf_op jit(solution)/shard_map/ppermute | solution.py:633
  29.0 1.8 %collective-permute-start.4 = (bf16[2,128,512]{2,1,0:T(8,128)(2,1)S(1)}, bf16[2,128,512]{2,1,0:T(8,128)(2,1)S(1)}, u32[]{:S(2)}, u32[]{:S(2)}) collective-permute-start(bf16[2,128,512]{2,1,0:T(8,128)(2,1)S(1)} %get-tuple-element.77), channel_id=1, source_target_pairs={{0,1},{1,0},{2,3},{3,2},{4,5},{5,4},{6,7},{7,6},{8,9},{9,8},{10,11... | collective-permute-start | bytes 786440 | tf_op jit(solution)/shard_map/ppermute | solution.py:633
  29.2 7.2 %collective-permute-start.5 = (bf16[256,384]{1,0:T(8,128)(2,1)S(1)}, bf16[256,384]{1,0:T(8,128)(2,1)S(1)}, u32[]{:S(2)}, u32[]{:S(2)}) collective-permute-start(bf16[256,384]{1,0:T(8,128)(2,1)S(1)} %get-tuple-element.79.refs_0_.refs_6_), channel_id=1, source_target_pairs={{0,2},{2,0},{1,3},{3,1},{4,6},{6,4},{5,7},{7,5},{8,10},{10,8},{9,1... | collective-permute-start | bytes 589832 | tf_op jit(solution)/shard_map/ppermute | solution.py:633
  30.8 5.7 %collective-permute-start.6 = (bf16[2,128,384]{2,1,0:T(8,128)(2,1)S(1)}, bf16[2,128,384]{2,1,0:T(8,128)(2,1)S(1)}, u32[]{:S(2)}, u32[]{:S(2)}) collective-permute-start(bf16[2,128,384]{2,1,0:T(8,128)(2,1)S(1)} %get-tuple-element.71.refs_5_), channel_id=1, source_target_pairs={{0,1},{1,0},{2,3},{3,2},{4,5},{5,4},{6,7},{7,6},{8,9},{9,8},{10,11... | collective-permute-start | bytes 589832 | tf_op jit(solution)/shard_map/ppermute | solution.py:633
  30.9 9.7 %collective-permute-start.7 = (bf16[128,512]{1,0:T(8,128)(2,1)S(1)}, bf16[128,512]{1,0:T(8,128)(2,1)S(1)}, u32[]{:S(2)}, u32[]{:S(2)}) collective-permute-start(bf16[128,512]{1,0:T(8,128)(2,1)S(1)} %get-tuple-element.78.refs_13_), channel_id=1, source_target_pairs={{0,8},{4,12},{8,0},{12,4},{1,9},{5,13},{9,1},{13,5},{2,10},{6,14},... | collective-permute-start | bytes 393224 | tf_op jit(solution)/shard_map/ppermute | solution.py:633
  31.0 9.7 %collective-permute-start.8 = (bf16[128,512]{1,0:T(8,128)(2,1)S(1)}, bf16[128,512]{1,0:T(8,128)(2,1)S(1)}, u32[]{:S(2)}, u32[]{:S(2)}) collective-permute-start(bf16[128,512]{1,0:T(8,128)(2,1)S(1)} %get-tuple-element.84), channel_id=1, source_target_pairs={{0,4},{4,0},{8,12},{12,8},{1,5},{5,1},{9,13},{13,9},{2,6},{6,2},{1... | collective-permute-start | bytes 393224 | tf_op jit(solution)/shard_map/ppermute | solution.py:633
  40.8 10.3 %collective-permute-start.9 = (bf16[128,512]{1,0:T(8,128)(2,1)S(1)}, bf16[128,512]{1,0:T(8,128)(2,1)S(1)}, u32[]{:S(2)}, u32[]{:S(2)}) collective-permute-start(bf16[128,512]{1,0:T(8,128)(2,1)S(1)} %get-tuple-element.87), channel_id=1, source_target_pairs={{0,4},{4,0},{8,12},{12,8},{1,5},{5,1},{9,13},{13,9},{2,6},{6,2},{1... | collective-permute-start | bytes 393224 | tf_op jit(solution)/shard_map/ppermute | solution.py:633
  40.9 4.3 %collective-permute-start.10 = (bf16[256,128]{1,0:T(8,128)(2,1)S(1)}, bf16[256,128]{1,0:T(8,128)(2,1)S(1)}, u32[]{:S(2)}, u32[]{:S(2)}) collective-permute-start(bf16[256,128]{1,0:T(8,128)(2,1)S(1)} %get-tuple-element.88.refs_1_.refs_7_), channel_id=1, source_target_pairs={{0,2},{2,0},{1,3},{3,1},{4,6},{6,4},{5,7},{7,5},{8,10},{10,8},{9,1... | collective-permute-start | bytes 196616 | tf_op jit(solution)/shard_map/ppermute | solution.py:633
  51.1 1.5 %collective-permute-start.11 = (bf16[128,768]{1,0:T(8,128)(2,1)S(1)}, bf16[128,768]{1,0:T(8,128)(2,1)S(1)}, u32[]{:S(2)}, u32[]{:S(2)}) collective-permute-start(bf16[128,768]{1,0:T(8,128)(2,1)S(1)} %shard_map.131.refs_3_), channel_id=1, source_target_pairs={{0,1},{1,0},{2,3},{3,2},{4,5},{5,4},{6,7},{7,6},{8,9},{9,8},{10,11... | collective-permute-start | bytes 589832 | tf_op jit(solution)/shard_map/ppermute | solution.py:633
  52.8 5.6 %collective-permute-start.12 = (bf16[128,512]{1,0:T(8,128)(2,1)S(1)}, bf16[128,512]{1,0:T(8,128)(2,1)S(1)}, u32[]{:S(2)}, u32[]{:S(2)}) collective-permute-start(bf16[128,512]{1,0:T(8,128)(2,1)S(1)} %get-tuple-element.92.own_r.refs_5_), channel_id=1, source_target_pairs={{0,2},{2,0},{1,3},{3,1},{4,6},{6,4},{5,7},{7,5},{8,10},{10,8},{9,1... | collective-permute-start | bytes 393224 | tf_op jit(solution)/shard_map/ppermute | solution.py:633

commit v7 on v6

--- a/solution.py
+++ b/solution.py
@@ -60,30 +60,32 @@
 
 
 def kernel_call(body, facts, near, far, outs, scratch=(), aliases=None, after=(), cost=None,
-                limit=SMALL):
+                limit=SMALL, hold=()):
     smem = pl.BlockSpec(memory_space=pltpu.SMEM)
     vmem = pl.BlockSpec(memory_space=pltpu.VMEM)
     hbm = pl.BlockSpec(memory_space=pl.ANY)
     near = [pltpu.with_memory_space_constraint(a, pltpu.VMEM) for a in near]
+    hold = [pltpu.with_memory_space_constraint(a, pltpu.VMEM) for a in hold]
     place = {("near", i): 1 + i for i in range(len(near))}
     place |= {("far", i): 1 + len(near) + i for i in range(len(far))}
     used = 1 + len(near) + len(far)
 
     def kernel(*refs):
-        body(*refs[:used], *refs[used + len(after) :])
+        body(*refs[:used], *refs[used + len(hold) + len(after) :])
 
     return pl.pallas_call(
         kernel,
         out_shape=tuple(
             pltpu.VMEM(s, d) if inside else jax.ShapeDtypeStruct(s, d) for s, d, inside in outs
         ),
-        in_specs=[smem] + [vmem] * len(near) + [hbm] * (len(far) + len(after)),
+        in_specs=[smem] + [vmem] * len(near) + [hbm] * len(far) + [vmem] * len(hold)
+        + [hbm] * len(after),
         out_specs=tuple(vmem if inside else hbm for _, _, inside in outs),
         scratch_shapes=list(scratch),
         input_output_aliases={place[k]: v for k, v in (aliases or {}).items()},
         compiler_params=pltpu.CompilerParams(vmem_limit_bytes=limit),
         cost_estimate=cost or SLIGHT,
-    )(pltpu.with_memory_space_constraint(facts, pltpu.SMEM), *near, *far, *after)
+    )(pltpu.with_memory_space_constraint(facts, pltpu.SMEM), *near, *far, *hold, *after)
 
 
 def start(ids, counts, keys, values):
@@ -201,7 +203,8 @@
     return p.astype(BF16), (p * grads).astype(BF16)
 
 
-def attend(own, kvs, group, facts, inputs, pages, state, prior=(), after=()):
+def attend(own, kvs, group, facts, inputs, pages, state, prior=(), after=(), w=None,
+           hold=()):
     loading = "loaded" not in state
     q, g, k, v, norms, deltas = inputs if loading else state["loaded"]
     count = len(kvs)
@@ -259,6 +262,9 @@
         else:
             add_near(name, array)
     at_end = len(outs)
+    if w is not None:
+        add_far("w", w)
+        outs.append((w.shape, w.dtype, True))
     for i, page in enumerate(pages):
         add_near(("page", i), page)
     for i, array in enumerate(prior):
@@ -273,7 +279,7 @@
         pltpu.VMEM((ROWS, HD), BF16),
         pltpu.VMEM((count * parts, ROWS, wide), BF16),
         pltpu.SemaphoreType.DMA((count * parts,)),
-        pltpu.SemaphoreType.DMA((2 * kv_total + 4,)),
+        pltpu.SemaphoreType.DMA((2 * kv_total + 5,)),
     ]
     cols = lambda a, b: slice(a * PAGE, b * PAGE)
 
@@ -303,6 +309,11 @@
                 load(("g", kv), "g", at)
         else:
             into = {name: near_ref(name) for name in in_names}
+        if w is not None:
+            w_copy = pltpu.make_async_copy(
+                far_ref("w"), out_refs[at_end], load_sem.at[2 * kv_total + 4]
+            )
+            w_copy.start()
         q, g, k, v, norms, deltas = (into[name] for name in in_names)
 
         def arrived(*keys):
@@ -465,6 +476,8 @@
                 stage.at[slot], held["gq"].at[:, at : at + wide], sem.at[slot]
             ).wait()
         arrived(*list(copies))
+        if w is not None:
+            w_copy.wait()
 
     made = kernel_call(
         body, facts, near, far, outs, scratch, aliases, after,
@@ -472,13 +485,14 @@
             flops=240 * PAGE * PAGE * HD * group * count, bytes_accessed=1000, transcendentals=0
         ),
         LARGE,
+        hold,
     )
     for name, array in zip(names, made):
         state[name] = array
     state["done"] = state["done"] | set(kvs)
     if loading:
         state["loaded"] = made[at_loaded:at_end]
-    return list(made[at_results:at_loaded])
+    return list(made[at_results:at_loaded]) + list(made[at_end:])
 
 
 def width_tiles(w):
@@ -563,69 +577,86 @@
     return copies
 
 
-def begin_input_grad(facts, side, w, own):
+def begin_input_grad(facts, side, w, own, after=()):
     out_cols, depth = w.shape
-    tiles = width_tiles(w)
     half = depth // 2
-
-    def body(facts, flag, own_r, w_ref, out, w_far, w_near, sem):
-        place = lambda which: pl.ds(pl.multiple_of(which * half, half), half)
-        loads = [
-            pltpu.make_async_copy(w_ref.at[at, place(flag[0])], w_near.at[at], sem.at[i])
-            for i, at in enumerate(tiles)
-        ]
-        rest = pltpu.make_async_copy(w_ref.at[:, place(1 - flag[0])], w_far, sem.at[len(tiles)])
-        for c in [*loads, rest]:
-            c.start()
-        for i, at in enumerate(tiles):
-            loads[i].wait()
-            out[at] = dot_t(w_near[at], own_r[...])
-        rest.wait()
+    rows = own[0].shape[0]
+    count = len(own)
+
+    def body(facts, flag, w_ref, *refs):
+        mine, out = jnp.concatenate([r[...] for r in refs[:count]], axis=1), refs[-1]
+        where = pl.ds(pl.multiple_of(flag[0] * half, half), half)
+        for at in width_tiles(w):
+            out[at] = dot_t(w_ref[at, where], mine)
 
     smem = pl.BlockSpec(memory_space=pltpu.SMEM)
     vmem = pl.BlockSpec(memory_space=pltpu.VMEM)
+    near = [pltpu.with_memory_space_constraint(a, pltpu.VMEM) for a in (w, *own)]
+
+    def kernel(*refs):
+        body(*refs[: 3 + count], refs[-1])
+
     return pl.pallas_call(
-        body,
-        out_shape=(pltpu.VMEM((out_cols, own.shape[0]), F32), pltpu.VMEM((out_cols, half), BF16)),
-        in_specs=[smem, smem, vmem, pl.BlockSpec(memory_space=pl.ANY)],
-        out_specs=(vmem, vmem),
-        scratch_shapes=[
-            pltpu.VMEM((out_cols, half), BF16), pltpu.SemaphoreType.DMA((len(tiles) + 1,))
-        ],
+        kernel,
+        out_shape=pltpu.VMEM((out_cols, rows), F32),
+        in_specs=[smem, smem] + [vmem] * len(near) + [pl.BlockSpec(memory_space=pl.ANY)] * len(after),
+        out_specs=vmem,
         compiler_params=pltpu.CompilerParams(vmem_limit_bytes=LARGE),
-        cost_estimate=pl.CostEstimate(
-            flops=own.shape[0] * depth * out_cols, bytes_accessed=1000, transcendentals=0
-        ),
-    )(
-        pltpu.with_memory_space_constraint(facts, pltpu.SMEM), side,
-        pltpu.with_memory_space_constraint(own, pltpu.VMEM), w,
-    )
-
-
-def end_input_grad(facts, far, begun, w_far, grads, carry):
-    tiles = width_tiles(w_far)
+        cost_estimate=SLIGHT,
+    )(pltpu.with_memory_space_constraint(facts, pltpu.SMEM), side, *near, *after)
+
+
+def end_input_grad(facts, side, w, far, begun, grads, carry=None, after=()):
+    tiles = width_tiles(w)
+    out_cols, depth = w.shape
+    half = depth // 2
     steps = len(tiles)
-    rows = far.shape[0]
-
-    def body(facts, far_r, begun_r, w_r, *refs):
-        out, dk, dv, stage, sem = refs[-5:]
-        copies = put_rows(refs[:2], dk, dv, 0, rows, sem, steps)
+    rows = far[0].shape[0]
+    top = 0 if rows == PAGE else PAGE
+    width = sum(a.shape[1] for a in grads[0])
+    near = [w, begun, *far, *grads[0], *grads[1]]
+    carry = list(carry or [])
+
+    def body(facts, flag, w_r, begun_r, *refs):
+        far_r, grad_r = refs[: len(far)], refs[len(far) : len(near) - 2]
+        out, dk, dv, made, stage, sem = refs[-6:]
+        made[...] = jnp.zeros_like(made)
+        copies = put_rows(grad_r, dk, dv, top, rows, sem, steps)
+        other = jnp.concatenate([r[...] for r in far_r], axis=1)
+        where = pl.ds(pl.multiple_of((1 - flag[0]) * half, half), half)
         for i, at in enumerate(tiles):
-            stage[i] = (dot_t(w_r[at], far_r[...]) + begun_r[at]).astype(BF16).T
-            copies.append(pltpu.make_async_copy(stage.at[i], out.at[:rows, at], sem.at[i]))
+            stage[i] = (dot_t(w_r[at, where], other) + begun_r[at]).astype(BF16).T
+            copies.append(
+                pltpu.make_async_copy(stage.at[i], out.at[top : top + rows, at], sem.at[i])
+            )
             copies[-1].start()
         for c in copies:
             c.wait()
 
-    return kernel_call(
-        body, facts, [far, begun, w_far, *grads], carry,
-        [(a.shape, a.dtype, False) for a in carry],
-        [
-            pltpu.VMEM((steps, rows, w_far.shape[0] // steps), BF16),
-            pltpu.SemaphoreType.DMA((steps + 2,)),
+    smem = pl.BlockSpec(memory_space=pltpu.SMEM)
+    vmem = pl.BlockSpec(memory_space=pltpu.VMEM)
+    hbm = pl.BlockSpec(memory_space=pl.ANY)
+    near = [pltpu.with_memory_space_constraint(a, pltpu.VMEM) for a in near]
+    kept = jax.ShapeDtypeStruct((ROWS, width), BF16)
+
+    def kernel(*refs):
+        body(*refs[: 2 + len(near)], *refs[2 + len(near) + len(carry) + len(after) :])
+
+    return pl.pallas_call(
+        kernel,
+        out_shape=(
+            jax.ShapeDtypeStruct((ROWS, out_cols), BF16), kept, kept, pltpu.VMEM((8, HD), F32)
+        ),
+        in_specs=[smem, smem] + [vmem] * len(near) + [hbm] * (len(carry) + len(after)),
+        out_specs=(hbm, hbm, hbm, vmem),
+        scratch_shapes=[
+            pltpu.VMEM((steps, rows, out_cols // steps), BF16),
+            pltpu.SemaphoreType.DMA((steps + 2 * len(grads[0]),)),
         ],
-        {("far", i): i for i in range(len(carry))},
-    )
+        input_output_aliases={2 + len(near) + i: i for i in range(len(carry))},
+        compiler_params=pltpu.CompilerParams(vmem_limit_bytes=LARGE),
+        cost_estimate=SLIGHT,
+    )(pltpu.with_memory_space_constraint(facts, pltpu.SMEM), side, *near, *carry, *after)
 
 
 def flipped(block, axis, bit):
@@ -671,7 +702,7 @@
     return mine, flipped(mine, "sub", 1)
 
 
-def over_cores(facts, kept, sent):
+def over_cores(facts, kept, sent, hold):
     width = kept.shape[-1]
 
     def body(_, near, away, total, root, next_one):
@@ -683,12 +714,12 @@
     page = ((PAGE, width), BF16, True)
     total, root, next_one = kernel_call(
         body, facts, [kept, flipped(sent, "sub", 1)], [],
-        [((2, PAGE, width), F32, True), page, page],
+        [((2, PAGE, width), F32, True), page, page], hold=hold,
     )
     return total, root, flipped(root, "leaf", 2), flipped(next_one, "leaf", 1)
 
 
-def over_halves(facts, total, root_far, next_far, after):
+def over_halves(facts, total, root_far, next_far, after, hold):
     width = total.shape[-1]
 
     def body(_, near, root_r, next_r, out, low):
@@ -700,11 +731,12 @@
     total, low = kernel_call(
         body, facts, [total, root_far, next_far], [],
         [((2, PAGE, width), F32, True), ((PAGE, width), BF16, True)], after=after,
+        hold=hold,
     )
-    return total, flipped(low, "leaf", 1)
-
-
-def over_chips(facts, total, far, passenger, after=()):
+    return total, low, flipped(low, "leaf", 1)
+
+
+def over_chips(facts, total, far, passenger, after, hold):
     width = total.shape[-1]
     more = passenger.shape[-1]
 
@@ -715,11 +747,13 @@
             out[:, width + kind * more : width + (kind + 1) * more] = extra[kind]
 
     outs = [((PAGE, width + 2 * more), BF16, True)]
-    (mine,) = kernel_call(body, facts, [total, far, passenger], [], outs, after=after)
+    (mine,) = kernel_call(
+        body, facts, [total, far, passenger], [], outs, after=after, hold=hold
+    )
     return mine, flipped(mine, "sub", 1)
 
 
-def finish_small_tree(facts, own0, mine, far, level2_far):
+def finish_small_tree(facts, own0, mine, far, level2_far, hold):
     width = sum(a.shape[-1] for a in own0)
 
     def body(facts, own_r, own_last, mine_r, far_r, low_r, dk, dv):
@@ -740,7 +774,9 @@
                 out[:, c] = jnp.where(ok, base + more, 0.0).astype(BF16)
 
     page = ((PAGE, width), BF16, True)
-    return kernel_call(body, facts, [*own0, mine, far, level2_far], [], [page, page])
+    return kernel_call(
+        body, facts, [*own0, mine, far, level2_far], [], [page, page], hold=hold
+    )
 
 
 def gather_tree(ids, own):
@@ -775,11 +811,11 @@
     facts, own = start(hbm(ancestors), hbm(counts), *inputs[2:4])
     state = {"done": frozenset()}
 
-    def own_pages(kvs, pages, prior=(), after=()):
-        return attend(True, kvs, group, facts, inputs, pages, state, prior, after)
-
-    def shared_pages(kvs, pages, after=()):
-        return attend(False, kvs, group, facts, inputs, pages, state, after=after)
+    def own_pages(kvs, pages, prior=(), after=(), hold=()):
+        return attend(True, kvs, group, facts, inputs, pages, state, prior, after, hold=hold)
+
+    def shared_pages(kvs, pages, after=(), w=None):
+        return attend(False, kvs, group, facts, inputs, pages, state, after=after, w=w)
 
     def spread(part):
         if two_sides:
@@ -804,18 +840,20 @@
         most = results[-1]
         far_v = [spread(most[1])]
         level2_far = flipped(most[3], "sub", 1)
-        kept, sent = shared_pages(kvs, shared)
-        total, root, root_far, next_far = over_cores(facts, kept, sent)
-        last = own_pages(kvs[-1:], level2, after=(root, far_v[0], level2_far))
+        kept, sent, w_near = shared_pages(kvs, shared, w=w)
+        hold = (w_near,)
+        total, root, root_far, next_far = over_cores(facts, kept, sent, hold)
+        last = own_pages(kvs[-1:], level2, after=(root,), hold=hold)
+        both = list(zip(most, last))
+        begun = begin_input_grad(facts, side, w_near, both[1], (far_v[0], level2_far))
         far_v.append(spread(last[1]))
-        total, far = over_halves(facts, total, root_far, next_far, (last[3],))
-        both = list(zip(most, last))
-        *grads, made = input_grad(facts, side, w, 2 * PAGE, both[1], far_v, both[:2])
-        mine, far = over_chips(facts, total, far, last[3], (made,))
-        dk0, dv0 = finish_small_tree(facts, both[2], mine, far, level2_far)
+        total, low, far = over_halves(facts, total, root_far, next_far, (begun,), hold)
+        *grads, made = end_input_grad(facts, side, w_near, far_v, begun, both[:2], after=(low,))
+        mine, far = over_chips(facts, total, far, last[3], (made,), hold)
+        dk0, dv0 = finish_small_tree(facts, both[2], mine, far, level2_far, hold)
         far_v = spread(dv0)
-        begun, w_far = begin_input_grad(facts, side, w, dv0)
-        grads = end_input_grad(facts, far_v, begun, w_far, [dk0, dv0], grads)
+        begun = begin_input_grad(facts, side, w_near, [dv0])
+        grads = end_input_grad(facts, side, w_near, [far_v], begun, ([dk0], [dv0]), grads)
         return (state["gq"], grads[1], grads[2], grads[0])
 
     first = lax.axis_index("sub") == 0

time: 60.3 us -> 79.3 us (1.32)
  local copies, waits for them, and re-layouts: 0 us -> 22.1 us
  Pallas kernels: 32.2 us -> 29.4 us
  waiting for transfers between devices: 13.4 us -> 11.8 us
  starting transfers between devices: 13.6 us -> 14.5 us
    unnamed x0 -> x52, local copies, waits for them, and re-layouts: none -> 22.1 us
    pallas_call x2 -> x4, Pallas kernels: 8.96 us -> 5.89 us  [the longest x2 4.19 us: end_input_grad(): pl.pallas_call(kernel, out_shape=(jax.ShapeDtypeStruct((ROWS, out_cols),...]
    ppermute x13, waiting for transfers between devices: 13.4 us -> 11.8 us  [flipped(): lax.ppermute(block, axis, [(i, i ^ bit) for i in range(count) if i ^ bit...]
    ppermute x13, starting transfers between devices: 13.6 us -> 14.5 us  [flipped(): lax.ppermute(block, axis, [(i, i ^ bit) for i in range(count) if i ^ bit...]
    pallas_call x12 -> x11, Pallas kernels: 22.2 us -> 22.5 us  [kernel_call(): pl.pallas_call(kernel, out_shape=tuple((pltpu.VMEM(s, d) if inside else j...]
  transfers between devices with their start and end apart: 13 -> 13, of which waited for: 9 -> 6; matrix products, arithmetic and copies ran while one was open for 0% -> 0% of each run, Pallas kernels for 36% -> 22%
where the time goes in v7:
time: 79.3 us; the launch traced here: 78.9 us
  Pallas kernels  29.4 us (37%)
  local copies, waits for them, and re-layouts  22.1 us (28%)
  starting transfers between devices  14.5 us (18%)
  waiting for transfers between devices  11.8 us (15%)
  between operations  1.12 us (1%)
    pallas_call x11, Pallas kernels, kernel_call(): pl.pallas_call(kernel, out_shape=tuple((pltpu.VMEM(s, d) if inside else j...  22.5 us
    unnamed x52, local copies, waits for them, and re-layouts  22.1 us
    ppermute x13, starting transfers between devices, flipped(): lax.ppermute(block, axis, [(i, i ^ bit) for i in range(count) if i ^ bit...  14.5 us
    ppermute x13, waiting for transfers between devices, flipped(): lax.ppermute(block, axis, [(i, i ^ bit) for i in range(count) if i ^ bit...  11.8 us
    pallas_call x2, Pallas kernels, end_input_grad(): pl.pallas_call(kernel, out_shape=(jax.ShapeDtypeStruct((ROWS, out_cols),...  4.19 us
    pallas_call x2, Pallas kernels, begin_input_grad(): pl.pallas_call(kernel, out_shape=pltpu.VMEM((out_cols, rows), F32), in_sp...  1.7 us
  transfers between devices with their start and end apart: 13, of which 6 were waited for; matrix products, arithmetic and copies ran while one was open for 0% of the time, Pallas kernels for 22%

profile of v7, /device:TPU:0, one launch (start us, length us, event | category | flops | bytes accessed | tf_op | source)
XLA Modules:
  0.0 78.9 jit_solution(14674311449055134967)
XLA Ops:
  0.6 1.0 %shard_map.120 = (s32[16]{0:T(128)S(4)}, bf16[2,128,512]{2,1,0:T(8,128)(2,1)S(1)}) custom-call(s32[1,5]{1,0:T(1,128)} %ids_ref.1, s32[1,3]{1,0:T(1,128)} %counts_ref.1, bf16[384,512]{1,0:T(8,128)(2,1)} %refs_5_.1, bf16[384,512]{1,0:T(8,128)(2,1)} %refs_6_.1), custom_call_target="tpu_custom_call" | custom-call | tf_op jit(solution)/shard_map/pallas_call | solution.py:118
  1.7 0.5 collective-permute-start
  2.2 1.2 %collective-permute-done.refs_2_.refs_11_ = bf16[2,128,512]{2,1,0:T(8,128)(2,1)S(1)} collective-permute-done((bf16[2,128,512]{2,1,0:T(8,128)(2,1)S(1)}, bf16[2,128,512]{2,1,0:T(8,128)(2,1)S(1)}, u32[]{:S(2)}, u32[]{:S(2)}) %collective-permute-start) | collective-permute-done | bytes 262176 | tf_op jit(solution)/shard_map/ppermute | solution.py:664
  3.4 3.0 %collective-permute-start.1 = (bf16[128,512]{1,0:T(8,128)(2,1)S(1)}, bf16[128,512]{1,0:T(8,128)(2,1)S(1)}, u32[]{:S(2)}, u32[]{:S(2)}) collective-permute-start(bf16[128,512]{1,0:T(8,128)(2,1)S(1)} %shard_map.121.refs_9_.refs_1_), channel_id=1, source_target_pairs={{0,4},{4,0},{8,12},{12,8},{1,5},{5,1},{9,13},{13,9},{2,6},{6,2},{1... | collective-permute-start | bytes 393224 | tf_op jit(solution)/shard_map/ppermute | solution.py:664
  6.4 4.3 %shard_map.122 = (f32[384,4096]{1,0:T(8,128)S(1)}, bf16[128,12288]{1,0:T(8,128)(2,1)S(1)}, bf16[128,12288]{1,0:T(8,128)(2,1)S(1)}, bf16[256,128]{1,0:T(8,128)(2,...) custom-call(s32[16]{0:T(128)S(4)} %get-tuple-element.52.refs_0_, ...), custom_call_target="tpu_custom_call" | custom-call | flops 4026531840 | bytes 1000 | tf_op jit(solution)/shard_map/pallas_call | solution.py:76
  10.7 0.0 copy-start.5
  10.7 0.0 copy-start.17
  10.7 0.0 copy-start.19
  10.7 0.0 collective-permute-done.1.refs_2_
  10.8 2.6 %collective-permute-start.2 = (bf16[128,512]{1,0:T(8,128)(2,1)S(1)}, bf16[128,512]{1,0:T(8,128)(2,1)S(1)}, u32[]{:S(2)}, u32[]{:S(2)}) collective-permute-start(bf16[128,512]{1,0:T(8,128)(2,1)S(1)} %shard_map.123.refs_16_.refs_3_), channel_id=1, source_target_pairs={{0,8},{4,12},{8,0},{12,4},{1,9},{5,13},{9,1},{13,5},{2,10},{6,14},... | collective-permute-start | bytes 393224 | tf_op jit(solution)/shard_map/ppermute | solution.py:664
  13.4 0.0 copy-done.11
  13.4 4.9 %shard_map.124 = (f32[384,4096]{1,0:T(8,128)S(1)}, bf16[128,12288]{1,0:T(8,128)(2,1)S(1)}, bf16[128,12288]{1,0:T(8,128)(2,1)S(1)}, bf16[256,384]{1,0:T(8,128)(2,...) custom-call(s32[16]{0:T(128)S(4)} %get-tuple-element.52.refs_0_, ...), custom_call_target="tpu_custom_call", output_to_operand_aliasing={{0}: (1, {}), {1}: (2, {}), {2}: (3, {})} | custom-call | flops 8053063680 | bytes 1000 | tf_op jit(solution)/shard_map/pallas_call | solution.py:76
  18.3 0.0 copy-start.13
  18.3 0.0 copy-start.21
  18.3 0.0 copy-start.23
  18.3 0.0 copy-start.24
  18.3 1.4 %collective-permute-done.2.refs_4_ = bf16[128,512]{1,0:T(8,128)(2,1)S(1)} collective-permute-done((bf16[128,512]{1,0:T(8,128)(2,1)S(1)}, bf16[128,512]{1,0:T(8,128)(2,1)S(1)}, u32[]{:S(2)}, u32[]{:S(2)}) %collective-permute-start.2) | collective-permute-done | bytes 131104 | tf_op jit(solution)/shard_map/ppermute | solution.py:664
  19.8 0.1 collective-permute-start.3
  19.9 1.5 %collective-permute-done.3.refs_11_ = bf16[2,128,512]{2,1,0:T(8,128)(2,1)S(1)} collective-permute-done((bf16[2,128,512]{2,1,0:T(8,128)(2,1)S(1)}, bf16[2,128,512]{2,1,0:T(8,128)(2,1)S(1)}, u32[]{:S(2)}, u32[]{:S(2)}) %collective-permute-start.3) | collective-permute-done | bytes 262176 | tf_op jit(solution)/shard_map/ppermute | solution.py:664
  21.4 0.0 copy-done.13
  21.4 0.0 copy-done.21
  21.4 0.0 copy-done.23
  21.4 0.0 copy-done.24
  21.4 8.4 %shard_map.126 = (f32[384,4096]{1,0:T(8,128)S(1)}, bf16[128,12288]{1,0:T(8,128)(2,1)S(1)}, bf16[128,12288]{1,0:T(8,128)(2,1)S(1)}, bf16[384,4096]{1,0:T(8,128)(2...) custom-call(s32[16]{0:T(128)S(4)} %get-tuple-element.52.refs_0_, ...), custom_call_target="tpu_custom_call", output_to_operand_aliasing={{0}: (1, {}), {1}: (2, {}), {2}: (3, {})} | custom-call | flops 16106127360 | bytes 1000 | tf_op jit(solution)/shard_map/pallas_call | solution.py:76
  29.9 2.3 %copy-done = bf16[2560,1024]{1,0:T(8,128)(2,1)} copy-done((bf16[2560,1024]{1,0:T(8,128)(2,1)}, bf16[2560,1024]{1,0:T(8,128)(2,1)S(1)}, u32[]{:S(2)}) %copy-start) | copy-done | bytes 5242904
  32.2 2.7 %copy-done.3 = f32[384,4096]{1,0:T(8,128)} copy-done((f32[384,4096]{1,0:T(8,128)}, f32[384,4096]{1,0:T(8,128)S(1)}, u32[]{:S(2)}) %copy-start.3) | copy-done | bytes 6291480
  34.9 1.7 %copy-done.7 = bf16[128,12288]{1,0:T(8,128)(2,1)} copy-done((bf16[128,12288]{1,0:T(8,128)(2,1)}, bf16[128,12288]{1,0:T(8,128)(2,1)S(1)}, u32[]{:S(2)}) %copy-start.7) | copy-done | bytes 3145752
  36.5 1.6 %copy-done.9 = bf16[128,12288]{1,0:T(8,128)(2,1)} copy-done((bf16[128,12288]{1,0:T(8,128)(2,1)}, bf16[128,12288]{1,0:T(8,128)(2,1)S(1)}, u32[]{:S(2)}) %copy-start.9) | copy-done | bytes 3145752
  38.2 0.8 %copy-done.15 = f32[2,128,512]{2,1,0:T(8,128)} copy-done((f32[2,128,512]{2,1,0:T(8,128)}, f32[2,128,512]{2,1,0:T(8,128)S(1)}, u32[]{:S(2)}) %copy-start.15) | copy-done | bytes 524312
  39.0 0.1 collective-permute-start.4
  39.1 0.4 collective-permute-start.8
  39.5 1.5 %collective-permute-start.7 = (bf16[256,384]{1,0:T(8,128)(2,1)}, bf16[256,384]{1,0:T(8,128)(2,1)S(1)}, u32[]{:S(2)}, u32[]{:S(2)}) collective-permute-start(bf16[256,384]{1,0:T(8,128)(2,1)} %copy-done.13), channel_id=1, source_target_pairs={{0,2},{2,0},{1,3},{3,1},{4,6},{6,4},{5,7},{7,5},{8,10},{10,8},{9,1... | collective-permute-start | bytes 589832 | tf_op jit(solution)/shard_map/ppermute | solution.py:664
  41.0 0.0 collective-permute-done.4.refs_2_
  41.0 2.5 %copy-done.1 = bf16[2560,1024]{1,0:T(8,128)(2,1)S(1)} copy-done((bf16[2560,1024]{1,0:T(8,128)(2,1)S(1)}, bf16[2560,1024]{1,0:T(8,128)(2,1)}, u32[]{:S(2)}) %copy-start.1) | copy-done | bytes 5242904
  43.5 1.0 %copy-done.16 = f32[2,128,512]{2,1,0:T(8,128)S(1)} copy-done((f32[2,128,512]{2,1,0:T(8,128)S(1)}, f32[2,128,512]{2,1,0:T(8,128)}, u32[]{:S(2)}) %copy-start.16) | copy-done | bytes 524312
  44.5 1.2 %shard_map.127 = (f32[2,128,512]{2,1,0:T(8,128)S(1)}, bf16[128,512]{1,0:T(8,128)(2,1)S(1)}, bf16[128,512]{1,0:T(8,128)(2,1)S(1)}) custom-call(s32[16]{0:T(128)S(4)} %get-tuple-element.52.refs_0_, f32[2,128,512]{2,1,0:T(8,128)S(1)} %copy-done.16, bf16[2,128,512]{2,1,0:T(8,128)(2,1)} %collective-permute-done.4.refs_2_, bf16[2560,1024]{1,0:T(8,128)(2,1)S(1)} %copy-done.1), custom_call_target="tpu_custom_call" | custom-call | flops 1000 | bytes 1000 | tf_op jit(solution)/shard_map/pallas_call | solution.py:76
  45.7 0.1 collective-permute-start.5
  45.8 3.2 %collective-permute-start.6 = (bf16[128,512]{1,0:T(8,128)(2,1)S(1)}, bf16[128,512]{1,0:T(8,128)(2,1)S(1)}, u32[]{:S(2)}, u32[]{:S(2)}) collective-permute-start(bf16[128,512]{1,0:T(8,128)(2,1)S(1)} %get-tuple-element.83), channel_id=1, source_target_pairs={{0,4},{4,0},{8,12},{12,8},{1,5},{5,1},{9,13},{13,9},{2,6},{6,2},{1... | collective-permute-start | bytes 393224 | tf_op jit(solution)/shard_map/ppermute | solution.py:664
  49.0 0.0 copy-done.2
  49.0 0.0 copy-done.18
  49.0 2.8 %copy-done.4 = f32[384,4096]{1,0:T(8,128)S(1)} copy-done((f32[384,4096]{1,0:T(8,128)S(1)}, f32[384,4096]{1,0:T(8,128)}, u32[]{:S(2)}) %copy-start.4) | copy-done | bytes 6291480
  51.8 1.9 %copy-done.6 = bf16[384,4096]{1,0:T(8,128)(2,1)S(1)} copy-done((bf16[384,4096]{1,0:T(8,128)(2,1)S(1)}, bf16[384,4096]{1,0:T(8,128)(2,1)}, u32[]{:S(2)}) %copy-start.6) | copy-done | bytes 3145752
  53.7 1.9 %copy-done.8 = bf16[128,12288]{1,0:T(8,128)(2,1)S(1)} copy-done((bf16[128,12288]{1,0:T(8,128)(2,1)S(1)}, bf16[128,12288]{1,0:T(8,128)(2,1)}, u32[]{:S(2)}) %copy-start.8) | copy-done | bytes 3145752
  55.6 1.9 %copy-done.10 = bf16[128,12288]{1,0:T(8,128)(2,1)S(1)} copy-done((bf16[128,12288]{1,0:T(8,128)(2,1)S(1)}, bf16[128,12288]{1,0:T(8,128)(2,1)}, u32[]{:S(2)}) %copy-start.10) | copy-done | bytes 3145752
  57.4 1.0 %copy-done.20 = bf16[384,512]{1,0:T(8,128)(2,1)S(1)} copy-done((bf16[384,512]{1,0:T(8,128)(2,1)S(1)}, bf16[384,512]{1,0:T(8,128)(2,1)}, u32[]{:S(2)}) %copy-start.20) | copy-done | bytes 393240
  58.4 3.4 %shard_map.128 = (f32[384,4096]{1,0:T(8,128)S(1)}, bf16[128,12288]{1,0:T(8,128)(2,1)S(1)}, bf16[128,12288]{1,0:T(8,128)(2,1)S(1)}, bf16[384,4096]{1,0:T(8,128)(2...) custom-call(s32[16]{0:T(128)S(4)} %get-tuple-element.52.refs_0_, ...), custom_call_target="tpu_custom_call", output_to_operand_aliasing={{0}: (1, {}), {1}: (2, {}), {2}: (3, {}), {3}: (12, {})} | custom-call | flops 4026531840 | bytes 1000 | tf_op jit(solution)/shard_map/pallas_call | solution.py:76
  61.8 0.0 collective-permute-done.7.refs_5_.refs_4_
  61.8 0.0 collective-permute-done.8.refs_6_.refs_5_
  61.9 0.9 %shard_map.129.refs_5_.refs_3_ = f32[2560,256]{1,0:T(8,128)S(1)} custom-call(s32[16]{0:T(128)S(4)} %get-tuple-element.52.refs_0_, s32[1]{0:T(128)} %bitcast.refs_1_, bf16[2560,1024]{1,0:T(8,128)(2,1)S(1)} %copy-done.2, bf16[256,384]{1,0:T(8,128)(2,1)S(1)} %copy-done.14, bf16[256,128]{1,0:T(8,128)(2,1)S(1)} %get-tuple-element.85.refs_4_.refs_9_, ...), custom_call_target="tpu_custom_call" | custom-call | flops 1000 | bytes 1000 | tf_op jit(solution)/shard_map/pallas_call | solution.py:599
  62.7 0.0 collective-permute-done.5.refs_2_
  62.8 0.0 collective-permute-done.6.refs_3_
  62.8 0.1 shard_map.130
  62.8 0.1 collective-permute-start.9
  62.9 1.4 %collective-permute-start.10 = (bf16[256,128]{1,0:T(8,128)(2,1)S(1)}, bf16[256,128]{1,0:T(8,128)(2,1)S(1)}, u32[]{:S(2)}, u32[]{:S(2)}) collective-permute-start(bf16[256,128]{1,0:T(8,128)(2,1)S(1)} %get-tuple-element.85.refs_4_.refs_9_), channel_id=1, source_target_pairs={{0,2},{2,0},{1,3},{3,1},{4,6},{6,4},{5,7},{7,5},{8,10},{10,8},{9,1... | collective-permute-start | bytes 196616 | tf_op jit(solution)/shard_map/ppermute | solution.py:664
  64.4 2.9 %collective-permute-done.10.refs_5_ = bf16[256,128]{1,0:T(8,128)(2,1)S(1)} collective-permute-done((bf16[256,128]{1,0:T(8,128)(2,1)S(1)}, bf16[256,128]{1,0:T(8,128)(2,1)S(1)}, u32[]{:S(2)}, u32[]{:S(2)}) %collective-permute-start.10) | collective-permute-done | bytes 65568 | tf_op jit(solution)/shard_map/ppermute | solution.py:664
  67.3 1.9 %shard_map.131 = (bf16[384,2560]{1,0:T(8,128)(2,1)}, bf16[384,512]{1,0:T(8,128)(2,1)}, bf16[384,512]{1,0:T(8,128)(2,1)}, f32[8,128]{1,0:T(8,128)S(1)}) custom-call(s32[16]{0:T(128)S(4)} %get-tuple-element.52.refs_0_, s32[1]{0:T(128)} %bitcast.refs_1_, bf16[2560,1024]{1,0:T(8,128)(2,1)S(1)} %copy-done.2, f32[2560,256]{1,0:T(8,128)S(1)} %shard_map.129.refs_5_.refs_3_, ...), custom_call_target="tpu_custom_call" | custom-call | flops 1000 | bytes 1000 | tf_op jit(solution)/shard_map/pallas_call | solution.py:645
  69.2 0.0 collective-permute-done.9.refs_2_
  69.3 0.1 collective-permute-start.11
  69.3 1.4 %collective-permute-done.11.refs_4_ = bf16[128,768]{1,0:T(8,128)(2,1)S(1)} collective-permute-done((bf16[128,768]{1,0:T(8,128)(2,1)S(1)}, bf16[128,768]{1,0:T(8,128)(2,1)S(1)}, u32[]{:S(2)}, u32[]{:S(2)}) %collective-permute-start.11) | collective-permute-done | bytes 196640 | tf_op jit(solution)/shard_map/ppermute | solution.py:664
  70.8 0.1 shard_map.133
  70.9 1.4 %collective-permute-start.12 = (bf16[128,512]{1,0:T(8,128)(2,1)S(1)}, bf16[128,512]{1,0:T(8,128)(2,1)S(1)}, u32[]{:S(2)}, u32[]{:S(2)}) collective-permute-start(bf16[128,512]{1,0:T(8,128)(2,1)S(1)} %get-tuple-element.92.refs_3_.refs_6_), channel_id=1, source_target_pairs={{0,2},{2,0},{1,3},{3,1},{4,6},{6,4},{5,7},{7,5},{8,10},{10,8},{9,1... | collective-permute-start | bytes 393224 | tf_op jit(solution)/shard_map/ppermute | solution.py:664
  72.3 0.8 %shard_map.134.refs_3_ = f32[2560,128]{1,0:T(8,128)S(1)} custom-call(s32[16]{0:T(128)S(4)} %get-tuple-element.52.refs_0_, s32[1]{0:T(128)} %bitcast.refs_1_, bf16[2560,1024]{1,0:T(8,128)(2,1)S(1)} %copy-done.2, bf16[128,512]{1,0:T(8,128)(2,1)S(1)} %get-tuple-element.92.refs_3_.refs_6_), custom_call_target="tpu_custom_call" | custom-call | flops 1000 | bytes 1000 | tf_op jit(solution)/shard_map/pallas_call | solution.py:599
  73.1 3.4 %collective-permute-done.12.refs_4_ = bf16[128,512]{1,0:T(8,128)(2,1)S(1)} collective-permute-done((bf16[128,512]{1,0:T(8,128)(2,1)S(1)}, bf16[128,512]{1,0:T(8,128)(2,1)S(1)}, u32[]{:S(2)}, u32[]{:S(2)}) %collective-permute-start.12) | collective-permute-done | bytes 131104 | tf_op jit(solution)/shard_map/ppermute | solution.py:664
  76.5 2.3 %shard_map.135 = (bf16[384,2560]{1,0:T(8,128)(2,1)}, bf16[384,512]{1,0:T(8,128)(2,1)}, bf16[384,512]{1,0:T(8,128)(2,1)}, f32[8,128]{1,0:T(8,128)}) custom-call(s32[16]{0:T(128)S(4)} %get-tuple-element.52.refs_0_, s32[1]{0:T(128)} %bitcast.refs_1_, bf16[2560,1024]{1,0:T(8,128)(2,1)S(1)} %copy-done.2, ...), custom_call_target="tpu_custom_call", output_to_operand_aliasing={{0}: (7, {}), {1}: (8, {}), {2}: (9, {})} | custom-call | flops 1000 | bytes 1000 | tf_op jit(solution)/shard_map/pallas_call | solution.py:645
  (30 shorter events, 0.2 us)
Async XLA Ops:
  1.7 1.7 %collective-permute-start = (bf16[2,128,512]{2,1,0:T(8,128)(2,1)S(1)}, bf16[2,128,512]{2,1,0:T(8,128)(2,1)S(1)}, u32[]{:S(2)}, u32[]{:S(2)}) collective-permute-start(bf16[2,128,512]{2,1,0:T(8,128)(2,1)S(1)} %get-tuple-element.53.refs_1_.refs_10_), channel_id=1, source_target_pairs={{0,1},{1,0},{2,3},{3,2},{4,5},{5,4},{6,7},{7,6},{8,9},{9,8},{10,11... | collective-permute-start | bytes 786440 | tf_op jit(solution)/shard_map/ppermute | solution.py:664
  3.3 10.1 %copy-start.11 = (bf16[2,128,512]{2,1,0:T(8,128)(2,1)}, bf16[2,128,512]{2,1,0:T(8,128)(2,1)S(1)}, u32[]{:S(2)}) copy-start(bf16[2,128,512]{2,1,0:T(8,128)(2,1)S(1)} %collective-permute-done.refs_2_.refs_11_) | copy-start | bytes 786436
  3.4 7.4 %collective-permute-start.1 = (bf16[128,512]{1,0:T(8,128)(2,1)S(1)}, bf16[128,512]{1,0:T(8,128)(2,1)S(1)}, u32[]{:S(2)}, u32[]{:S(2)}) collective-permute-start(bf16[128,512]{1,0:T(8,128)(2,1)S(1)} %shard_map.121.refs_9_.refs_1_), channel_id=1, source_target_pairs={{0,4},{4,0},{8,12},{12,8},{1,5},{5,1},{9,13},{13,9},{2,6},{6,2},{1... | collective-permute-start | bytes 393224 | tf_op jit(solution)/shard_map/ppermute | solution.py:664
  10.7 10.7 %copy-start.5 = (bf16[384,4096]{1,0:T(8,128)(2,1)}, bf16[384,4096]{1,0:T(8,128)(2,1)S(1)}, u32[]{:S(2)}) copy-start(bf16[384,4096]{1,0:T(8,128)(2,1)S(1)} %get-tuple-element.58.refs_5_) | copy-start | bytes 9437188
  10.7 10.7 %copy-start.17 = (bf16[384,512]{1,0:T(8,128)(2,1)}, bf16[384,512]{1,0:T(8,128)(2,1)S(1)}, u32[]{:S(2)}) copy-start(bf16[384,512]{1,0:T(8,128)(2,1)S(1)} %get-tuple-element.59.refs_6_) | copy-start | bytes 1179652
  10.7 10.7 %copy-start.19 = (bf16[384,512]{1,0:T(8,128)(2,1)}, bf16[384,512]{1,0:T(8,128)(2,1)S(1)}, u32[]{:S(2)}) copy-start(bf16[384,512]{1,0:T(8,128)(2,1)S(1)} %get-tuple-element.60.refs_7_) | copy-start | bytes 1179652
  10.8 9.0 %collective-permute-start.2 = (bf16[128,512]{1,0:T(8,128)(2,1)S(1)}, bf16[128,512]{1,0:T(8,128)(2,1)S(1)}, u32[]{:S(2)}, u32[]{:S(2)}) collective-permute-start(bf16[128,512]{1,0:T(8,128)(2,1)S(1)} %shard_map.123.refs_16_.refs_3_), channel_id=1, source_target_pairs={{0,8},{4,12},{8,0},{12,4},{1,9},{5,13},{9,1},{13,5},{2,10},{6,14},... | collective-permute-start | bytes 393224 | tf_op jit(solution)/shard_map/ppermute | solution.py:664
  18.3 3.1 %copy-start.13 = (bf16[256,384]{1,0:T(8,128)(2,1)}, bf16[256,384]{1,0:T(8,128)(2,1)S(1)}, u32[]{:S(2)}) copy-start(bf16[256,384]{1,0:T(8,128)(2,1)S(1)} %get-tuple-element.84.refs_3_.refs_8_) | copy-start | bytes 589828
  18.3 3.1 %copy-start.21 = (f32[2,128,384]{2,1,0:T(8,128)}, f32[2,128,384]{2,1,0:T(8,128)S(1)}, u32[]{:S(2)}) copy-start(f32[2,128,384]{2,1,0:T(8,128)S(1)} %get-tuple-element.80.refs_1_) | copy-start | bytes 1179652
  18.3 3.1 %copy-start.23 = (bf16[2,128,384]{2,1,0:T(8,128)(2,1)}, bf16[2,128,384]{2,1,0:T(8,128)(2,1)S(1)}, u32[]{:S(2)}) copy-start(bf16[2,128,384]{2,1,0:T(8,128)(2,1)S(1)} %get-tuple-element.70.refs_5_) | copy-start | bytes 589828
  18.3 3.1 %copy-start.24 = (bf16[256,384]{1,0:T(8,128)(2,1)}, bf16[256,384]{1,0:T(8,128)(2,1)S(1)}, u32[]{:S(2)}) copy-start(bf16[256,384]{1,0:T(8,128)(2,1)S(1)} %get-tuple-element.89.refs_6_) | copy-start | bytes 589828
  19.8 1.6 %collective-permute-start.3 = (bf16[2,128,512]{2,1,0:T(8,128)(2,1)S(1)}, bf16[2,128,512]{2,1,0:T(8,128)(2,1)S(1)}, u32[]{:S(2)}, u32[]{:S(2)}) collective-permute-start(bf16[2,128,512]{2,1,0:T(8,128)(2,1)S(1)} %shard_map.125.refs_10_), channel_id=1, source_target_pairs={{0,1},{1,0},{2,3},{3,2},{4,5},{5,4},{6,7},{7,6},{8,9},{9,8},{10,11... | collective-permute-start | bytes 786440 | tf_op jit(solution)/shard_map/ppermute | solution.py:664
  29.9 2.3 %copy-start = (bf16[2560,1024]{1,0:T(8,128)(2,1)}, bf16[2560,1024]{1,0:T(8,128)(2,1)S(1)}, u32[]{:S(2)}) copy-start(bf16[2560,1024]{1,0:T(8,128)(2,1)S(1)} %get-tuple-element.75.refs_3_.refs_13_.refs_2_.refs_4_.refs_6_) | copy-start | bytes 15728644
  32.2 2.7 %copy-start.3 = (f32[384,4096]{1,0:T(8,128)}, f32[384,4096]{1,0:T(8,128)S(1)}, u32[]{:S(2)}) copy-start(f32[384,4096]{1,0:T(8,128)S(1)} %get-tuple-element.71.refs_1_) | copy-start | bytes 18874372
  34.9 1.7 %copy-start.7 = (bf16[128,12288]{1,0:T(8,128)(2,1)}, bf16[128,12288]{1,0:T(8,128)(2,1)S(1)}, u32[]{:S(2)}) copy-start(bf16[128,12288]{1,0:T(8,128)(2,1)S(1)} %get-tuple-element.72.refs_2_) | copy-start | bytes 9437188
  36.5 1.6 %copy-start.9 = (bf16[128,12288]{1,0:T(8,128)(2,1)}, bf16[128,12288]{1,0:T(8,128)(2,1)S(1)}, u32[]{:S(2)}) copy-start(bf16[128,12288]{1,0:T(8,128)(2,1)S(1)} %get-tuple-element.73.refs_3_) | copy-start | bytes 9437188
  38.2 0.8 %copy-start.15 = (f32[2,128,512]{2,1,0:T(8,128)}, f32[2,128,512]{2,1,0:T(8,128)S(1)}, u32[]{:S(2)}) copy-start(f32[2,128,512]{2,1,0:T(8,128)S(1)} %get-tuple-element.76.refs_1_) | copy-start | bytes 1572868
  39.0 2.0 %collective-permute-start.4 = (bf16[2,128,512]{2,1,0:T(8,128)(2,1)}, bf16[2,128,512]{2,1,0:T(8,128)(2,1)}, u32[]{:S(2)}, u32[]{:S(2)}) collective-permute-start(bf16[2,128,512]{2,1,0:T(8,128)(2,1)} %get-tuple-element.77), channel_id=1, source_target_pairs={{0,1},{1,0},{2,3},{3,2},{4,5},{5,4},{6,7},{7,6},{8,9},{9,8},{10,11... | collective-permute-start | bytes 786440 | tf_op jit(solution)/shard_map/ppermute | solution.py:664
  39.1 22.7 %collective-permute-start.8 = (bf16[2,128,384]{2,1,0:T(8,128)(2,1)}, bf16[2,128,384]{2,1,0:T(8,128)(2,1)S(1)}, u32[]{:S(2)}, u32[]{:S(2)}) collective-permute-start(bf16[2,128,384]{2,1,0:T(8,128)(2,1)} %copy-done.23), channel_id=1, source_target_pairs={{0,1},{1,0},{2,3},{3,2},{4,5},{5,4},{6,7},{7,6},{8,9},{9,8},{10,11... | collective-permute-start | bytes 589832 | tf_op jit(solution)/shard_map/ppermute | solution.py:664
  39.5 22.3 %collective-permute-start.7 = (bf16[256,384]{1,0:T(8,128)(2,1)}, bf16[256,384]{1,0:T(8,128)(2,1)S(1)}, u32[]{:S(2)}, u32[]{:S(2)}) collective-permute-start(bf16[256,384]{1,0:T(8,128)(2,1)} %copy-done.13), channel_id=1, source_target_pairs={{0,2},{2,0},{1,3},{3,1},{4,6},{6,4},{5,7},{7,5},{8,10},{10,8},{9,1... | collective-permute-start | bytes 589832 | tf_op jit(solution)/shard_map/ppermute | solution.py:664
  41.0 2.5 %copy-start.1 = (bf16[2560,1024]{1,0:T(8,128)(2,1)S(1)}, bf16[2560,1024]{1,0:T(8,128)(2,1)}, u32[]{:S(2)}) copy-start(bf16[2560,1024]{1,0:T(8,128)(2,1)} %copy-done) | copy-start | bytes 15728644
  43.5 1.0 %copy-start.16 = (f32[2,128,512]{2,1,0:T(8,128)S(1)}, f32[2,128,512]{2,1,0:T(8,128)}, u32[]{:S(2)}) copy-start(f32[2,128,512]{2,1,0:T(8,128)} %copy-done.15) | copy-start | bytes 1572868
  44.5 4.5 %copy-start.2 = (bf16[2560,1024]{1,0:T(8,128)(2,1)S(1)}, bf16[2560,1024]{1,0:T(8,128)(2,1)}, u32[]{:S(2)}) copy-start(bf16[2560,1024]{1,0:T(8,128)(2,1)} %copy-done) | copy-start | bytes 15728644
  44.5 4.5 %copy-start.12 = (bf16[2,128,512]{2,1,0:T(8,128)(2,1)S(1)}, bf16[2,128,512]{2,1,0:T(8,128)(2,1)}, u32[]{:S(2)}) copy-start(bf16[2,128,512]{2,1,0:T(8,128)(2,1)} %copy-done.11) | copy-start | bytes 786436
  44.5 4.5 %copy-start.18 = (bf16[384,512]{1,0:T(8,128)(2,1)S(1)}, bf16[384,512]{1,0:T(8,128)(2,1)}, u32[]{:S(2)}) copy-start(bf16[384,512]{1,0:T(8,128)(2,1)} %copy-done.17) | copy-start | bytes 1179652
  45.7 17.1 %collective-permute-start.5 = (bf16[128,512]{1,0:T(8,128)(2,1)S(1)}, bf16[128,512]{1,0:T(8,128)(2,1)S(1)}, u32[]{:S(2)}, u32[]{:S(2)}) collective-permute-start(bf16[128,512]{1,0:T(8,128)(2,1)S(1)} %get-tuple-element.78.refs_14_), channel_id=1, source_target_pairs={{0,8},{4,12},{8,0},{12,4},{1,9},{5,13},{9,1},{13,5},{2,10},{6,14},... | collective-permute-start | bytes 393224 | tf_op jit(solution)/shard_map/ppermute | solution.py:664
  45.8 17.0 %collective-permute-start.6 = (bf16[128,512]{1,0:T(8,128)(2,1)S(1)}, bf16[128,512]{1,0:T(8,128)(2,1)S(1)}, u32[]{:S(2)}, u32[]{:S(2)}) collective-permute-start(bf16[128,512]{1,0:T(8,128)(2,1)S(1)} %get-tuple-element.83), channel_id=1, source_target_pairs={{0,4},{4,0},{8,12},{12,8},{1,5},{5,1},{9,13},{13,9},{2,6},{6,2},{1... | collective-permute-start | bytes 393224 | tf_op jit(solution)/shard_map/ppermute | solution.py:664
  49.0 2.8 %copy-start.4 = (f32[384,4096]{1,0:T(8,128)S(1)}, f32[384,4096]{1,0:T(8,128)}, u32[]{:S(2)}) copy-start(f32[384,4096]{1,0:T(8,128)} %copy-done.3) | copy-start | bytes 18874372
  51.8 1.9 %copy-start.6 = (bf16[384,4096]{1,0:T(8,128)(2,1)S(1)}, bf16[384,4096]{1,0:T(8,128)(2,1)}, u32[]{:S(2)}) copy-start(bf16[384,4096]{1,0:T(8,128)(2,1)} %copy-done.5) | copy-start | bytes 9437188
  53.7 1.9 %copy-start.8 = (bf16[128,12288]{1,0:T(8,128)(2,1)S(1)}, bf16[128,12288]{1,0:T(8,128)(2,1)}, u32[]{:S(2)}) copy-start(bf16[128,12288]{1,0:T(8,128)(2,1)} %copy-done.7) | copy-start | bytes 9437188
  55.6 1.9 %copy-start.10 = (bf16[128,12288]{1,0:T(8,128)(2,1)S(1)}, bf16[128,12288]{1,0:T(8,128)(2,1)}, u32[]{:S(2)}) copy-start(bf16[128,12288]{1,0:T(8,128)(2,1)} %copy-done.9) | copy-start | bytes 9437188
  57.4 1.0 %copy-start.20 = (bf16[384,512]{1,0:T(8,128)(2,1)S(1)}, bf16[384,512]{1,0:T(8,128)(2,1)}, u32[]{:S(2)}) copy-start(bf16[384,512]{1,0:T(8,128)(2,1)} %copy-done.19) | copy-start | bytes 1179652
  58.4 3.4 %copy-start.14 = (bf16[256,384]{1,0:T(8,128)(2,1)S(1)}, bf16[256,384]{1,0:T(8,128)(2,1)}, u32[]{:S(2)}) copy-start(bf16[256,384]{1,0:T(8,128)(2,1)} %copy-done.13) | copy-start | bytes 589828
  62.8 4.5 %copy-start.25 = (bf16[256,384]{1,0:T(8,128)(2,1)S(1)}, bf16[256,384]{1,0:T(8,128)(2,1)}, u32[]{:S(2)}) copy-start(bf16[256,384]{1,0:T(8,128)(2,1)} %copy-done.24) | copy-start | bytes 589828
  62.8 6.4 %collective-permute-start.9 = (bf16[128,512]{1,0:T(8,128)(2,1)S(1)}, bf16[128,512]{1,0:T(8,128)(2,1)S(1)}, u32[]{:S(2)}, u32[]{:S(2)}) collective-permute-start(bf16[128,512]{1,0:T(8,128)(2,1)S(1)} %get-tuple-element.87.refs_10_), channel_id=1, source_target_pairs={{0,4},{4,0},{8,12},{12,8},{1,5},{5,1},{9,13},{13,9},{2,6},{6,2},{1... | collective-permute-start | bytes 393224 | tf_op jit(solution)/shard_map/ppermute | solution.py:664
  62.9 4.3 %collective-permute-start.10 = (bf16[256,128]{1,0:T(8,128)(2,1)S(1)}, bf16[256,128]{1,0:T(8,128)(2,1)S(1)}, u32[]{:S(2)}, u32[]{:S(2)}) collective-permute-start(bf16[256,128]{1,0:T(8,128)(2,1)S(1)} %get-tuple-element.85.refs_4_.refs_9_), channel_id=1, source_target_pairs={{0,2},{2,0},{1,3},{3,1},{4,6},{6,4},{5,7},{7,5},{8,10},{10,8},{9,1... | collective-permute-start | bytes 196616 | tf_op jit(solution)/shard_map/ppermute | solution.py:664
  69.2 1.6 %copy-start.22 = (f32[2,128,384]{2,1,0:T(8,128)S(1)}, f32[2,128,384]{2,1,0:T(8,128)}, u32[]{:S(2)}) copy-start(f32[2,128,384]{2,1,0:T(8,128)} %copy-done.21) | copy-start | bytes 1179652
  69.3 1.5 %collective-permute-start.11 = (bf16[128,768]{1,0:T(8,128)(2,1)S(1)}, bf16[128,768]{1,0:T(8,128)(2,1)S(1)}, u32[]{:S(2)}, u32[]{:S(2)}) collective-permute-start(bf16[128,768]{1,0:T(8,128)(2,1)S(1)} %shard_map.132.refs_3_), channel_id=1, source_target_pairs={{0,1},{1,0},{2,3},{3,2},{4,5},{5,4},{6,7},{7,6},{8,9},{9,8},{10,11... | collective-permute-start | bytes 589832 | tf_op jit(solution)/shard_map/ppermute | solution.py:664
  70.9 5.6 %collective-permute-start.12 = (bf16[128,512]{1,0:T(8,128)(2,1)S(1)}, bf16[128,512]{1,0:T(8,128)(2,1)S(1)}, u32[]{:S(2)}, u32[]{:S(2)}) collective-permute-start(bf16[128,512]{1,0:T(8,128)(2,1)S(1)} %get-tuple-element.92.refs_3_.refs_6_), channel_id=1, source_target_pairs={{0,2},{2,0},{1,3},{3,1},{4,6},{6,4},{5,7},{7,5},{8,10},{10,8},{9,1... | collective-permute-start | bytes 393224 | tf_op jit(solution)/shard_map/ppermute | solution.py:664

commit v8 on v7

--- a/solution.py
+++ b/solution.py
@@ -60,32 +60,30 @@
 
 
 def kernel_call(body, facts, near, far, outs, scratch=(), aliases=None, after=(), cost=None,
-                limit=SMALL, hold=()):
+                limit=SMALL):
     smem = pl.BlockSpec(memory_space=pltpu.SMEM)
     vmem = pl.BlockSpec(memory_space=pltpu.VMEM)
     hbm = pl.BlockSpec(memory_space=pl.ANY)
     near = [pltpu.with_memory_space_constraint(a, pltpu.VMEM) for a in near]
-    hold = [pltpu.with_memory_space_constraint(a, pltpu.VMEM) for a in hold]
     place = {("near", i): 1 + i for i in range(len(near))}
     place |= {("far", i): 1 + len(near) + i for i in range(len(far))}
     used = 1 + len(near) + len(far)
 
     def kernel(*refs):
-        body(*refs[:used], *refs[used + len(hold) + len(after) :])
+        body(*refs[:used], *refs[used + len(after) :])
 
     return pl.pallas_call(
         kernel,
         out_shape=tuple(
             pltpu.VMEM(s, d) if inside else jax.ShapeDtypeStruct(s, d) for s, d, inside in outs
         ),
-        in_specs=[smem] + [vmem] * len(near) + [hbm] * len(far) + [vmem] * len(hold)
-        + [hbm] * len(after),
+        in_specs=[smem] + [vmem] * len(near) + [hbm] * (len(far) + len(after)),
         out_specs=tuple(vmem if inside else hbm for _, _, inside in outs),
         scratch_shapes=list(scratch),
         input_output_aliases={place[k]: v for k, v in (aliases or {}).items()},
         compiler_params=pltpu.CompilerParams(vmem_limit_bytes=limit),
         cost_estimate=cost or SLIGHT,
-    )(pltpu.with_memory_space_constraint(facts, pltpu.SMEM), *near, *far, *hold, *after)
+    )(pltpu.with_memory_space_constraint(facts, pltpu.SMEM), *near, *far, *after)
 
 
 def start(ids, counts, keys, values):
@@ -141,8 +139,8 @@
 
 
 class Head:
-    def __init__(self, kv, group, q, g, norms, deltas, en, ed):
-        self.kv, self.group, self.q, self.g, self.en, self.ed = kv, group, q, g, en, ed
+    def __init__(self, kv, group, norms, deltas, en, ed):
+        self.group = group
         self.heads = min(4, group)
         self.parts = group // self.heads
         self.tall = self.heads * PAGE
@@ -151,8 +149,8 @@
         ed[...] = row_terms(deltas[heads, :])
 
     def lanes(self, part, j):
-        at = self.kv * self.group * HD + part * (self.heads * HD) + j * HD
-        return pl.ds(pl.multiple_of(at, HD), HD)
+        at = (part * self.heads + j) * HD
+        return slice(at, at + HD)
 
     def stacked(self, ref, part, slots):
         return jnp.concatenate(
@@ -176,8 +174,8 @@
         return jnp.concatenate([stacked, jnp.concatenate(extra, axis=0)], axis=1)
 
     def turned_at(self, part, slot, count):
-        at = ((self.kv * self.parts + part) * SLOTS + slot) * self.tall
-        return pl.ds(pl.multiple_of(at, self.tall), self.tall * count)
+        at = (part * SLOTS + slot) * self.tall
+        return slice(at, at + self.tall * count)
 
     def put_queries(self, part, slot, rows_by_head, dq, add, stage):
         rows = slice(slot * PAGE, (slot + 1) * PAGE)
@@ -203,24 +201,23 @@
     return p.astype(BF16), (p * grads).astype(BF16)
 
 
-def attend(own, kvs, group, facts, inputs, pages, state, prior=(), after=(), w=None,
-           hold=()):
-    loading = "loaded" not in state
-    q, g, k, v, norms, deltas = inputs if loading else state["loaded"]
+def attend(own, kvs, group, facts, inputs, pages, state, prior=(), after=(), w=None):
+    loading = "k" not in state
+    q_all, k_all = inputs[0], inputs[2]
     count = len(kvs)
     parts = group // min(4, group)
     tall = min(4, group) * PAGE
     wide = min(4, group) * HD
     width = count * HD
     base = prior[0].shape[1] if prior else 0
-    kv_total = k.shape[1] // HD
-    fresh = [kv not in state["done"] for kv in kvs]
-    names = ["dq", "qt", "gt"] + ([] if all(fresh) else ["gq"])
-    turned = ((HD, kv_total * group * ROWS), BF16, True)
-    full = {"dq": (q.shape, F32, True), "qt": turned, "gt": turned, "gq": (q.shape, BF16, False)}
+    kv_total = k_all.shape[1] // HD
+    fresh = [("dq", kv) not in state for kv in kvs]
+    one_head = (ROWS, group * HD)
+    turned = ((HD, group * ROWS), BF16, True)
+    shapes = {"dq": (one_head, F32, True), "qt": turned, "gt": turned}
 
     near, far, aliases, outs = [], [], {}, []
-    at_near, at_far = {}, {}
+    at_near, at_far, at_out = {}, {}, {}
 
     def add_near(name, array):
         at_near[name] = len(near)
@@ -230,15 +227,21 @@
         at_far[name] = len(far)
         far.append(array)
 
-    for name in names:
-        outs.append(full[name])
-        if name in state:
-            if full[name][2]:
-                add_near(name, state[name])
-                aliases["near", at_near[name]] = len(outs) - 1
+    def add_out(name, out):
+        at_out[name] = len(outs)
+        outs.append(out)
+
+    for kv, is_fresh in zip(kvs, fresh):
+        for name, shape in shapes.items():
+            if is_fresh:
+                add_out((name, kv), shape)
             else:
-                add_far(name, state[name])
-                aliases["far", at_far[name]] = len(outs) - 1
+                add_near((name, kv), state[name, kv])
+    if not all(fresh):
+        add_out("gq", (q_all.shape, BF16, False))
+        if "gq" in state:
+            add_far("gq", state["gq"])
+            aliases["far", at_far["gq"]] = at_out["gq"]
     at_results = len(outs)
     if own:
         outs += [
@@ -253,14 +256,20 @@
             ((2, PAGE, width), BF16, True),
         ]
     at_loaded = len(outs)
-    in_names = ["q", "g", "k", "v", "norms", "deltas"]
-    in_arrays = [q, g, k, v, norms, deltas]
-    for name, array in zip(in_names, in_arrays):
-        if loading:
+    if loading:
+        for name, array in zip(("q", "g", "k", "v", "norms", "deltas"), inputs):
             add_far(name, array)
-            outs.append((array.shape, array.dtype, True))
-        else:
-            add_near(name, array)
+            if name in ("q", "g"):
+                for kv in range(kv_total):
+                    add_out((name, kv), (one_head, BF16, True))
+            else:
+                add_out(name, (array.shape, array.dtype, True))
+    else:
+        for name in ("k", "v", "norms", "deltas"):
+            add_near(name, state[name])
+        for kv in kvs:
+            for name in ("q", "g"):
+                add_near((name, kv), state[name, kv])
     at_end = len(outs)
     if w is not None:
         add_far("w", w)
@@ -288,33 +297,27 @@
         k_deep, v_deep, k_up, acc, en, ed, stage, sem, load_sem = refs[-len(scratch) :]
         near_ref = lambda name: ins[at_near[name]]
         far_ref = lambda name: ins[len(near) + at_far[name]]
-        held = dict(zip(names, out_refs))
+        held = lambda name: out_refs[at_out[name]] if name in at_out else near_ref(name)
         results = out_refs[at_results:at_loaded]
         copies = {}
         if loading:
-            into = dict(zip(in_names, out_refs[at_loaded:at_end]))
-
-            def load(key, name, columns=None):
-                src, dst = far_ref(name), into[name]
-                if columns is not None:
-                    src, dst = src.at[:, columns], dst.at[:, columns]
-                copies[key] = pltpu.make_async_copy(src, dst, load_sem.at[len(copies)])
+
+            def load(key, src):
+                copies[key] = pltpu.make_async_copy(src, held(key), load_sem.at[len(copies)])
                 copies[key].start()
 
-            for name in in_names[2:]:
-                load(name, name)
+            for name in ("k", "v", "norms", "deltas"):
+                load(name, far_ref(name))
             for kv in range(kv_total):
                 at = slice(kv * group * HD, (kv + 1) * group * HD)
-                load(("q", kv), "q", at)
-                load(("g", kv), "g", at)
-        else:
-            into = {name: near_ref(name) for name in in_names}
+                for name in ("q", "g"):
+                    load((name, kv), far_ref(name).at[:, at])
         if w is not None:
             w_copy = pltpu.make_async_copy(
                 far_ref("w"), out_refs[at_end], load_sem.at[2 * kv_total + 4]
             )
             w_copy.start()
-        q, g, k, v, norms, deltas = (into[name] for name in in_names)
+        k, v, norms, deltas = (held(name) for name in ("k", "v", "norms", "deltas"))
 
         def arrived(*keys):
             for key in keys:
@@ -357,20 +360,23 @@
                     set_keys(v_deep, None, j, jnp.where(leads, theirs, mine))
             acc[...] = jnp.zeros_like(acc)
 
-        def turned_rows(head, part, is_fresh, qs, gs, order):
+        def turned_rows(head, kv, part, is_fresh, qs, gs, order):
             if is_fresh:
                 for name, rows in (("qt", qs), ("gt", gs)):
                     for i, slot in enumerate(order):
-                        held[name][:, head.turned_at(part, slot, 1)] = rows[
+                        held((name, kv))[:, head.turned_at(part, slot, 1)] = rows[
                             i * tall : (i + 1) * tall
                         ].T
-            return lambda name, slot, slots: held[name][:, head.turned_at(part, slot, slots)]
-
-        def own_part(head, part, n, stage_ref):
+            return lambda name, slot, slots: held((name, kv))[
+                :, head.turned_at(part, slot, slots)
+            ]
+
+        def own_part(head, kv, part, n, stage_ref):
             order = (1, 2, 0)
-            qs, gs = head.stacked(q, part, order), head.stacked(g, part, order)
+            qs = head.stacked(held(("q", kv)), part, order)
+            gs = head.stacked(held(("g", kv)), part, order)
             qd, gd = head.deep(qs, en, part, order), head.deep(gs, ed, part, order)
-            turn = turned_rows(head, part, fresh[n], qs, gs, order)
+            turn = turned_rows(head, kv, part, fresh[n], qs, gs, order)
             low = lower(tall)
 
             def keep_first(p):
@@ -397,17 +403,18 @@
                 acc[i, :, cols(3, 4)] += dot_n(turn(name, 0, 1), b[tall:])
             first = dot_n(da, k_up[: 2 * PAGE])
             put = lambda slot, rows: head.put_queries(
-                part, slot, rows, held["dq"], not fresh[n], stage_ref
+                part, slot, rows, held(("dq", kv)), not fresh[n], stage_ref
             )
             put(1, first[:tall])
             put(2, first[tall:] + dot_n(db[:tall], k_up[cols(2, 3)]))
             put(0, dot_n(db[tall:], k_up[cols(3, 4)]))
 
-        def shared_part(head, part, n, stage_ref):
+        def shared_part(head, kv, part, n, stage_ref):
             order = (0, 1, 2)
-            qs, gs = head.stacked(q, part, order), head.stacked(g, part, order)
+            qs = head.stacked(held(("q", kv)), part, order)
+            gs = head.stacked(held(("g", kv)), part, order)
             qd, gd = head.deep(qs, en, part, order), head.deep(gs, ed, part, order)
-            turn = turned_rows(head, part, fresh[n], qs, gs, order)
+            turn = turned_rows(head, kv, part, fresh[n], qs, gs, order)
             column = lax.broadcasted_iota(I32, (tall, 2 * PAGE), 1)
             seen = column < facts[LIMIT]
 
@@ -420,7 +427,7 @@
             dq = dot_n(ds, k_up[...])
             for slot in range(SLOTS):
                 head.put_queries(
-                    part, slot, dq[slot * tall : (slot + 1) * tall], held["dq"], not fresh[n],
+                    part, slot, dq[slot * tall : (slot + 1) * tall], held(("dq", kv)), not fresh[n],
                     stage_ref,
                 )
 
@@ -451,30 +458,26 @@
         sends = []
         for n, kv in enumerate(kvs):
             arrived(("q", kv), ("g", kv))
-            head = Head(kv, group, q, g, norms, deltas, en, ed)
+            head = Head(kv, group, norms, deltas, en, ed)
             set_pages(n, kv)
 
-            def step(part, _, n=n, kv=kv, head=head):
+            for part in range(parts):
                 slot = n * parts + part
                 (own_part if own else shared_part)(
-                    head, part, n, None if fresh[n] else stage.at[slot]
+                    head, kv, part, n, None if fresh[n] else stage.at[slot]
                 )
                 if not fresh[n]:
-                    at = pl.multiple_of((kv * parts + part) * wide, wide)
-                    pltpu.make_async_copy(
-                        stage.at[slot], held["gq"].at[:, pl.ds(at, wide)], sem.at[slot]
-                    ).start()
-                return 0
-
-            for part in range(parts):
-                step(part, 0)
+                    at = (kv * parts + part) * wide
+                    sends.append(
+                        pltpu.make_async_copy(
+                            stage.at[slot], held("gq").at[:, at : at + wide], sem.at[slot]
+                        )
+                    )
+                    sends[-1].start()
+
             (put_own if own else put_shared)(n)
-            if not fresh[n]:
-                sends += [(n * parts + p, (kv * parts + p) * wide) for p in range(parts)]
-        for slot, at in sends:
-            pltpu.make_async_copy(
-                stage.at[slot], held["gq"].at[:, at : at + wide], sem.at[slot]
-            ).wait()
+        for c in sends:
+            c.wait()
         arrived(*list(copies))
         if w is not None:
             w_copy.wait()
@@ -485,13 +488,9 @@
             flops=240 * PAGE * PAGE * HD * group * count, bytes_accessed=1000, transcendentals=0
         ),
         LARGE,
-        hold,
     )
-    for name, array in zip(names, made):
-        state[name] = array
-    state["done"] = state["done"] | set(kvs)
-    if loading:
-        state["loaded"] = made[at_loaded:at_end]
+    for name, at in at_out.items():
+        state[name] = made[at]
     return list(made[at_results:at_loaded]) + list(made[at_end:])
 
 
@@ -702,7 +701,7 @@
     return mine, flipped(mine, "sub", 1)
 
 
-def over_cores(facts, kept, sent, hold):
+def over_cores(facts, kept, sent):
     width = kept.shape[-1]
 
     def body(_, near, away, total, root, next_one):
@@ -714,12 +713,12 @@
     page = ((PAGE, width), BF16, True)
     total, root, next_one = kernel_call(
         body, facts, [kept, flipped(sent, "sub", 1)], [],
-        [((2, PAGE, width), F32, True), page, page], hold=hold,
+        [((2, PAGE, width), F32, True), page, page],
     )
     return total, root, flipped(root, "leaf", 2), flipped(next_one, "leaf", 1)
 
 
-def over_halves(facts, total, root_far, next_far, after, hold):
+def over_halves(facts, total, root_far, next_far, after):
     width = total.shape[-1]
 
     def body(_, near, root_r, next_r, out, low):
@@ -731,12 +730,11 @@
     total, low = kernel_call(
         body, facts, [total, root_far, next_far], [],
         [((2, PAGE, width), F32, True), ((PAGE, width), BF16, True)], after=after,
-        hold=hold,
     )
     return total, low, flipped(low, "leaf", 1)
 
 
-def over_chips(facts, total, far, passenger, after, hold):
+def over_chips(facts, total, far, passenger, after):
     width = total.shape[-1]
     more = passenger.shape[-1]
 
@@ -748,12 +746,12 @@
 
     outs = [((PAGE, width + 2 * more), BF16, True)]
     (mine,) = kernel_call(
-        body, facts, [total, far, passenger], [], outs, after=after, hold=hold
+        body, facts, [total, far, passenger], [], outs, after=after
     )
     return mine, flipped(mine, "sub", 1)
 
 
-def finish_small_tree(facts, own0, mine, far, level2_far, hold):
+def finish_small_tree(facts, own0, mine, far, level2_far):
     width = sum(a.shape[-1] for a in own0)
 
     def body(facts, own_r, own_last, mine_r, far_r, low_r, dk, dv):
@@ -775,7 +773,7 @@
 
     page = ((PAGE, width), BF16, True)
     return kernel_call(
-        body, facts, [*own0, mine, far, level2_far], [], [page, page], hold=hold
+        body, facts, [*own0, mine, far, level2_far], [], [page, page]
     )
 
 
@@ -809,13 +807,13 @@
     two_sides = lax.axis_size("tensor") == 2
     inputs = [hbm(a) for a in (queries, grad_out, keys, values, log_norms, row_deltas)]
     facts, own = start(hbm(ancestors), hbm(counts), *inputs[2:4])
-    state = {"done": frozenset()}
-
-    def own_pages(kvs, pages, prior=(), after=(), hold=()):
-        return attend(True, kvs, group, facts, inputs, pages, state, prior, after, hold=hold)
-
-    def shared_pages(kvs, pages, after=(), w=None):
-        return attend(False, kvs, group, facts, inputs, pages, state, after=after, w=w)
+    state = {}
+
+    def own_pages(kvs, pages, prior=(), after=(), w=None):
+        return attend(True, kvs, group, facts, inputs, pages, state, prior, after, w)
+
+    def shared_pages(kvs, pages):
+        return attend(False, kvs, group, facts, inputs, pages, state)
 
     def spread(part):
         if two_sides:
@@ -840,17 +838,16 @@
         most = results[-1]
         far_v = [spread(most[1])]
         level2_far = flipped(most[3], "sub", 1)
-        kept, sent, w_near = shared_pages(kvs, shared, w=w)
-        hold = (w_near,)
-        total, root, root_far, next_far = over_cores(facts, kept, sent, hold)
-        last = own_pages(kvs[-1:], level2, after=(root,), hold=hold)
+        kept, sent = shared_pages(kvs, shared)
+        total, root, root_far, next_far = over_cores(facts, kept, sent)
+        *last, w_near = own_pages(kvs[-1:], level2, after=(root,), w=w)
         both = list(zip(most, last))
         begun = begin_input_grad(facts, side, w_near, both[1], (far_v[0], level2_far))
         far_v.append(spread(last[1]))
-        total, low, far = over_halves(facts, total, root_far, next_far, (begun,), hold)
+        total, low, far = over_halves(facts, total, root_far, next_far, (begun,))
         *grads, made = end_input_grad(facts, side, w_near, far_v, begun, both[:2], after=(low,))
-        mine, far = over_chips(facts, total, far, last[3], (made,), hold)
-        dk0, dv0 = finish_small_tree(facts, both[2], mine, far, level2_far, hold)
+        mine, far = over_chips(facts, total, far, last[3], (made,))
+        dk0, dv0 = finish_small_tree(facts, both[2], mine, far, level2_far)
         far_v = spread(dv0)
         begun = begin_input_grad(facts, side, w_near, [dv0])
         grads = end_input_grad(facts, side, w_near, [far_v], begun, ([dk0], [dv0]), grads)

time: 79.3 us -> 67.1 us (0.85)
  local copies, waits for them, and re-layouts: 22.1 us -> 9.78 us
    unnamed x52 -> x24, local copies, waits for them, and re-layouts: 22.1 us -> 9.78 us
  transfers between devices with their start and end apart: 13 -> 13, of which waited for: 6 -> 6; matrix products, arithmetic and copies ran while one was open for 0% -> 0% of each run, Pallas kernels for 22% -> 27%
where the time goes in v8:
time: 67.1 us; the launch traced here: 66.7 us
  Pallas kernels  29.6 us (44%)
  starting transfers between devices  13.8 us (21%)
  waiting for transfers between devices  12.5 us (19%)
  local copies, waits for them, and re-layouts  9.78 us (15%)
  between operations  1.02 us (2%)
    pallas_call x11, Pallas kernels, kernel_call(): pl.pallas_call(kernel, out_shape=tuple((pltpu.VMEM(s, d) if inside else j...  22.7 us
    ppermute x13, starting transfers between devices, flipped(): lax.ppermute(block, axis, [(i, i ^ bit) for i in range(count) if i ^ bit...  13.8 us
    ppermute x13, waiting for transfers between devices, flipped(): lax.ppermute(block, axis, [(i, i ^ bit) for i in range(count) if i ^ bit...  12.5 us
    unnamed x24, local copies, waits for them, and re-layouts  9.78 us
    pallas_call x2, Pallas kernels, end_input_grad(): pl.pallas_call(kernel, out_shape=(jax.ShapeDtypeStruct((ROWS, out_cols),...  4.17 us
    pallas_call x2, Pallas kernels, begin_input_grad(): pl.pallas_call(kernel, out_shape=pltpu.VMEM((out_cols, rows), F32), in_sp...  1.72 us
  transfers between devices with their start and end apart: 13, of which 6 were waited for; matrix products, arithmetic and copies ran while one was open for 0% of the time, Pallas kernels for 27%

profile of v8, /device:TPU:0, one launch (start us, length us, event | category | flops | bytes accessed | tf_op | source)
XLA Modules:
  0.0 66.7 jit_solution(3636979295237293758)
XLA Ops:
  0.6 1.0 %shard_map.120 = (s32[16]{0:T(128)S(4)}, bf16[2,128,512]{2,1,0:T(8,128)(2,1)S(1)}) custom-call(s32[1,5]{1,0:T(1,128)} %ids_ref.1, s32[1,3]{1,0:T(1,128)} %counts_ref.1, bf16[384,512]{1,0:T(8,128)(2,1)} %refs_5_.1, bf16[384,512]{1,0:T(8,128)(2,1)} %refs_6_.1), custom_call_target="tpu_custom_call" | custom-call | tf_op jit(solution)/shard_map/pallas_call | solution.py:116
  1.7 0.5 collective-permute-start
  2.2 1.2 %collective-permute-done.refs_2_.refs_10_.refs_11_ = bf16[2,128,512]{2,1,0:T(8,128)(2,1)S(1)} collective-permute-done((bf16[2,128,512]{2,1,0:T(8,128)(2,1)S(1)}, bf16[2,128,512]{2,1,0:T(8,128)(2,1)S(1)}, u32[]{:S(2)}, u32[]{:S(2)}) %collective-permute-start) | collective-permute-done | bytes 262176 | tf_op jit(solution)/shard_map/ppermute | solution.py:663
  3.4 3.0 %collective-permute-start.1 = (bf16[128,512]{1,0:T(8,128)(2,1)S(1)}, bf16[128,512]{1,0:T(8,128)(2,1)S(1)}, u32[]{:S(2)}, u32[]{:S(2)}) collective-permute-start(bf16[128,512]{1,0:T(8,128)(2,1)S(1)} %shard_map.121.refs_9_.refs_1_), channel_id=1, source_target_pairs={{0,4},{4,0},{8,12},{12,8},{1,5},{5,1},{9,13},{13,9},{2,6},{6,2},{1... | collective-permute-start | bytes 393224 | tf_op jit(solution)/shard_map/ppermute | solution.py:663
  6.4 4.3 %shard_map.122 = (f32[384,1024]{1,0:T(8,128)S(1)}, bf16[128,3072]{1,0:T(8,128)(2,1)S(1)}, bf16[128,3072]{1,0:T(8,128)(2,1)S(1)}, bf16[256,128]{1,0:T(8,128)(2,1)...) custom-call(s32[16]{0:T(128)S(4)} %get-tuple-element.61.refs_0_, ...), custom_call_target="tpu_custom_call" | custom-call | flops 4026531840 | bytes 1000 | tf_op jit(solution)/shard_map/pallas_call | solution.py:75
  10.7 0.0 copy-start.2
  10.7 0.0 copy-start.8
  10.7 0.0 copy-start.10
  10.7 0.0 collective-permute-done.1.refs_2_
  10.8 2.6 %collective-permute-start.2 = (bf16[128,512]{1,0:T(8,128)(2,1)S(1)}, bf16[128,512]{1,0:T(8,128)(2,1)S(1)}, u32[]{:S(2)}, u32[]{:S(2)}) collective-permute-start(bf16[128,512]{1,0:T(8,128)(2,1)S(1)} %shard_map.123.refs_15_.refs_3_), channel_id=1, source_target_pairs={{0,8},{4,12},{8,0},{12,4},{1,9},{5,13},{9,1},{13,5},{2,10},{6,14},... | collective-permute-start | bytes 393224 | tf_op jit(solution)/shard_map/ppermute | solution.py:663
  13.4 4.9 %shard_map.124 = (f32[384,1024]{1,0:T(8,128)S(1)}, bf16[128,3072]{1,0:T(8,128)(2,1)S(1)}, bf16[128,3072]{1,0:T(8,128)(2,1)S(1)}, f32[384,1024]{1,0:T(8,128)S(1)}...) custom-call(s32[16]{0:T(128)S(4)} %get-tuple-element.61.refs_0_, ...), custom_call_target="tpu_custom_call" | custom-call | flops 8053063680 | bytes 1000 | tf_op jit(solution)/shard_map/pallas_call | solution.py:75
  18.3 1.5 %collective-permute-done.2.refs_4_ = bf16[128,512]{1,0:T(8,128)(2,1)S(1)} collective-permute-done((bf16[128,512]{1,0:T(8,128)(2,1)S(1)}, bf16[128,512]{1,0:T(8,128)(2,1)S(1)}, u32[]{:S(2)}, u32[]{:S(2)}) %collective-permute-start.2) | collective-permute-done | bytes 131104 | tf_op jit(solution)/shard_map/ppermute | solution.py:663
  19.8 0.1 collective-permute-start.3
  19.9 1.5 %collective-permute-done.3.refs_23_ = bf16[2,128,512]{2,1,0:T(8,128)(2,1)S(1)} collective-permute-done((bf16[2,128,512]{2,1,0:T(8,128)(2,1)S(1)}, bf16[2,128,512]{2,1,0:T(8,128)(2,1)S(1)}, u32[]{:S(2)}, u32[]{:S(2)}) %collective-permute-start.3) | collective-permute-done | bytes 262176 | tf_op jit(solution)/shard_map/ppermute | solution.py:663
  21.4 0.0 copy-done.2
  21.4 0.0 copy-done.8
  21.4 0.0 copy-done.10
  21.4 8.2 %shard_map.126 = (f32[384,1024]{1,0:T(8,128)S(1)}, bf16[128,3072]{1,0:T(8,128)(2,1)S(1)}, bf16[128,3072]{1,0:T(8,128)(2,1)S(1)}, bf16[384,4096]{1,0:T(8,128)(2,1...) custom-call(s32[16]{0:T(128)S(4)} %get-tuple-element.61.refs_0_, ...), custom_call_target="tpu_custom_call" | custom-call | flops 16106127360 | bytes 1000 | tf_op jit(solution)/shard_map/pallas_call | solution.py:75
  29.6 0.0 copy-start
  29.6 1.1 %copy-done = f32[384,1024]{1,0:T(8,128)} copy-done((f32[384,1024]{1,0:T(8,128)}, f32[384,1024]{1,0:T(8,128)S(1)}, u32[]{:S(2)}) %copy-start) | copy-done | bytes 1572888
  30.8 0.0 copy-start.4
  30.8 0.9 %copy-done.4 = bf16[128,3072]{1,0:T(8,128)(2,1)} copy-done((bf16[128,3072]{1,0:T(8,128)(2,1)}, bf16[128,3072]{1,0:T(8,128)(2,1)S(1)}, u32[]{:S(2)}) %copy-start.4) | copy-done | bytes 786456
  31.7 0.0 copy-start.6
  31.7 0.9 %copy-done.6 = bf16[128,3072]{1,0:T(8,128)(2,1)} copy-done((bf16[128,3072]{1,0:T(8,128)(2,1)}, bf16[128,3072]{1,0:T(8,128)(2,1)S(1)}, u32[]{:S(2)}) %copy-start.6) | copy-done | bytes 786456
  32.6 0.1 collective-permute-start.4
  32.7 0.4 collective-permute-start.8
  33.1 1.5 %collective-permute-start.7 = (bf16[256,384]{1,0:T(8,128)(2,1)S(1)}, bf16[256,384]{1,0:T(8,128)(2,1)S(1)}, u32[]{:S(2)}, u32[]{:S(2)}) collective-permute-start(bf16[256,384]{1,0:T(8,128)(2,1)S(1)} %get-tuple-element.102.refs_3_.refs_8_), channel_id=1, source_target_pairs={{0,2},{2,0},{1,3},{3,1},{4,6},{6,4},{5,7},{7,5},{8,10},{10,8},{9,1... | collective-permute-start | bytes 589832 | tf_op jit(solution)/shard_map/ppermute | solution.py:663
  34.6 0.0 collective-permute-done.4.refs_2_
  34.6 0.1 shard_map.127
  34.7 0.1 collective-permute-start.5
  34.8 3.2 %collective-permute-start.6 = (bf16[128,512]{1,0:T(8,128)(2,1)S(1)}, bf16[128,512]{1,0:T(8,128)(2,1)S(1)}, u32[]{:S(2)}, u32[]{:S(2)}) collective-permute-start(bf16[128,512]{1,0:T(8,128)(2,1)S(1)} %get-tuple-element.101), channel_id=1, source_target_pairs={{0,4},{4,0},{8,12},{12,8},{1,5},{5,1},{9,13},{13,9},{2,6},{6,2},{1... | collective-permute-start | bytes 393224 | tf_op jit(solution)/shard_map/ppermute | solution.py:663
  38.0 0.0 copy-start.1
  38.0 1.4 %copy-done.1 = f32[384,1024]{1,0:T(8,128)S(1)} copy-done((f32[384,1024]{1,0:T(8,128)S(1)}, f32[384,1024]{1,0:T(8,128)}, u32[]{:S(2)}) %copy-start.1) | copy-done | bytes 1572888
  39.4 0.0 copy-start.3
  39.4 1.1 %copy-done.3 = bf16[384,1024]{1,0:T(8,128)(2,1)S(1)} copy-done((bf16[384,1024]{1,0:T(8,128)(2,1)S(1)}, bf16[384,1024]{1,0:T(8,128)(2,1)}, u32[]{:S(2)}) %copy-start.3) | copy-done | bytes 786456
  40.5 0.0 copy-start.5
  40.5 1.1 %copy-done.5 = bf16[128,3072]{1,0:T(8,128)(2,1)S(1)} copy-done((bf16[128,3072]{1,0:T(8,128)(2,1)S(1)}, bf16[128,3072]{1,0:T(8,128)(2,1)}, u32[]{:S(2)}) %copy-start.5) | copy-done | bytes 786456
  41.6 0.0 copy-start.7
  41.6 1.1 %copy-done.7 = bf16[128,3072]{1,0:T(8,128)(2,1)S(1)} copy-done((bf16[128,3072]{1,0:T(8,128)(2,1)S(1)}, bf16[128,3072]{1,0:T(8,128)(2,1)}, u32[]{:S(2)}) %copy-start.7) | copy-done | bytes 786456
  42.8 0.0 copy-start.9
  42.8 1.0 %copy-done.9 = bf16[384,512]{1,0:T(8,128)(2,1)S(1)} copy-done((bf16[384,512]{1,0:T(8,128)(2,1)S(1)}, bf16[384,512]{1,0:T(8,128)(2,1)}, u32[]{:S(2)}) %copy-start.9) | copy-done | bytes 393240
  43.8 0.0 copy-start.11
  43.8 1.0 %copy-done.11 = bf16[384,512]{1,0:T(8,128)(2,1)S(1)} copy-done((bf16[384,512]{1,0:T(8,128)(2,1)S(1)}, bf16[384,512]{1,0:T(8,128)(2,1)}, u32[]{:S(2)}) %copy-start.11) | copy-done | bytes 393240
  44.8 4.9 %shard_map.128 = (bf16[384,4096]{1,0:T(8,128)(2,1)}, bf16[256,128]{1,0:T(8,128)(2,1)S(1)}, bf16[256,128]{1,0:T(8,128)(2,1)S(1)}, f32[2,128,128]{2,1,0:T(8,128)S(...) custom-call(s32[16]{0:T(128)S(4)} %get-tuple-element.61.refs_0_, ...), custom_call_target="tpu_custom_call", output_to_operand_aliasing={{0}: (12, {})} | custom-call | flops 4026531840 | bytes 1000 | tf_op jit(solution)/shard_map/pallas_call | solution.py:75
  49.6 0.0 collective-permute-done.7.refs_5_.refs_4_
  49.7 0.0 collective-permute-done.8.refs_6_.refs_5_
  49.7 0.9 %shard_map.129.refs_4_.refs_3_ = f32[2560,256]{1,0:T(8,128)S(1)} custom-call(s32[16]{0:T(128)S(4)} %get-tuple-element.61.refs_0_, s32[1]{0:T(128)} %bitcast.refs_1_, bf16[2560,1024]{1,0:T(8,128)(2,1)S(1)} %get-tuple-element.97.refs_2_, bf16[256,384]{1,0:T(8,128)(2,1)S(1)} %get-tuple-element.102.refs_3_.refs_8_, ...), custom_call_target="tpu_custom_call" | custom-call | flops 1000 | bytes 1000 | tf_op jit(solution)/shard_map/pallas_call | solution.py:598
  50.6 0.0 collective-permute-done.5.refs_2_
  50.6 0.0 collective-permute-done.6.refs_3_
  50.6 0.1 shard_map.130
  50.7 0.1 collective-permute-start.9
  50.7 1.1 %collective-permute-start.10 = (bf16[256,128]{1,0:T(8,128)(2,1)S(1)}, bf16[256,128]{1,0:T(8,128)(2,1)S(1)}, u32[]{:S(2)}, u32[]{:S(2)}) collective-permute-start(bf16[256,128]{1,0:T(8,128)(2,1)S(1)} %get-tuple-element.103.refs_4_.refs_9_), channel_id=1, source_target_pairs={{0,2},{2,0},{1,3},{3,1},{4,6},{6,4},{5,7},{7,5},{8,10},{10,8},{9,1... | collective-permute-start | bytes 196616 | tf_op jit(solution)/shard_map/ppermute | solution.py:663
  51.8 3.3 %collective-permute-done.10.refs_5_ = bf16[256,128]{1,0:T(8,128)(2,1)S(1)} collective-permute-done((bf16[256,128]{1,0:T(8,128)(2,1)S(1)}, bf16[256,128]{1,0:T(8,128)(2,1)S(1)}, u32[]{:S(2)}, u32[]{:S(2)}) %collective-permute-start.10) | collective-permute-done | bytes 65568 | tf_op jit(solution)/shard_map/ppermute | solution.py:663
  55.1 1.9 %shard_map.131 = (bf16[384,2560]{1,0:T(8,128)(2,1)}, bf16[384,512]{1,0:T(8,128)(2,1)}, bf16[384,512]{1,0:T(8,128)(2,1)}, f32[8,128]{1,0:T(8,128)S(1)}) custom-call(s32[16]{0:T(128)S(4)} %get-tuple-element.61.refs_0_, s32[1]{0:T(128)} %bitcast.refs_1_, bf16[2560,1024]{1,0:T(8,128)(2,1)S(1)} %get-tuple-element.97.refs_2_, ...), custom_call_target="tpu_custom_call" | custom-call | flops 1000 | bytes 1000 | tf_op jit(solution)/shard_map/pallas_call | solution.py:644
  57.0 0.0 collective-permute-done.9.refs_2_
  57.0 0.1 shard_map.132.refs_3_
  57.0 0.1 collective-permute-start.11
  57.1 1.4 %collective-permute-done.11.refs_4_ = bf16[128,768]{1,0:T(8,128)(2,1)S(1)} collective-permute-done((bf16[128,768]{1,0:T(8,128)(2,1)S(1)}, bf16[128,768]{1,0:T(8,128)(2,1)S(1)}, u32[]{:S(2)}, u32[]{:S(2)}) %collective-permute-start.11) | collective-permute-done | bytes 196640 | tf_op jit(solution)/shard_map/ppermute | solution.py:663
  58.6 0.1 shard_map.133
  58.7 1.1 %collective-permute-start.12 = (bf16[128,512]{1,0:T(8,128)(2,1)S(1)}, bf16[128,512]{1,0:T(8,128)(2,1)S(1)}, u32[]{:S(2)}, u32[]{:S(2)}) collective-permute-start(bf16[128,512]{1,0:T(8,128)(2,1)S(1)} %get-tuple-element.110.refs_3_.refs_6_), channel_id=1, source_target_pairs={{0,2},{2,0},{1,3},{3,1},{4,6},{6,4},{5,7},{7,5},{8,10},{10,8},{9,1... | collective-permute-start | bytes 393224 | tf_op jit(solution)/shard_map/ppermute | solution.py:663
  59.8 0.8 %shard_map.134.refs_3_ = f32[2560,128]{1,0:T(8,128)S(1)} custom-call(s32[16]{0:T(128)S(4)} %get-tuple-element.61.refs_0_, s32[1]{0:T(128)} %bitcast.refs_1_, bf16[2560,1024]{1,0:T(8,128)(2,1)S(1)} %get-tuple-element.97.refs_2_, bf16[128,512]{1,0:T(8,128)(2,1)S(1)} %get-tuple-element.110.refs_3_.refs_6_), custom_call_target="tpu_custom_call" | custom-call | flops 1000 | bytes 1000 | tf_op jit(solution)/shard_map/pallas_call | solution.py:598
  60.6 3.7 %collective-permute-done.12.refs_4_ = bf16[128,512]{1,0:T(8,128)(2,1)S(1)} collective-permute-done((bf16[128,512]{1,0:T(8,128)(2,1)S(1)}, bf16[128,512]{1,0:T(8,128)(2,1)S(1)}, u32[]{:S(2)}, u32[]{:S(2)}) %collective-permute-start.12) | collective-permute-done | bytes 131104 | tf_op jit(solution)/shard_map/ppermute | solution.py:663
  64.3 2.3 %shard_map.135 = (bf16[384,2560]{1,0:T(8,128)(2,1)}, bf16[384,512]{1,0:T(8,128)(2,1)}, bf16[384,512]{1,0:T(8,128)(2,1)}, f32[8,128]{1,0:T(8,128)}) custom-call(s32[16]{0:T(128)S(4)} %get-tuple-element.61.refs_0_, s32[1]{0:T(128)} %bitcast.refs_1_, ...), custom_call_target="tpu_custom_call", output_to_operand_aliasing={{0}: (7, {}), {1}: (8, {}), {2}: (9, {})} | custom-call | flops 1000 | bytes 1000 | tf_op jit(solution)/shard_map/pallas_call | solution.py:644
  (3 shorter events, 0.1 us)
Async XLA Ops:
  1.7 1.7 %collective-permute-start = (bf16[2,128,512]{2,1,0:T(8,128)(2,1)S(1)}, bf16[2,128,512]{2,1,0:T(8,128)(2,1)S(1)}, u32[]{:S(2)}, u32[]{:S(2)}) collective-permute-start(bf16[2,128,512]{2,1,0:T(8,128)(2,1)S(1)} %get-tuple-element.62.refs_1_.refs_9_.refs_10_), channel_id=1, source_target_pairs={{0,1},{1,0},{2,3},{3,2},{4,5},{5,4},{6,7},{7,6},{8,9},{9,8},{10,11... | collective-permute-start | bytes 786440 | tf_op jit(solution)/shard_map/ppermute | solution.py:663
  3.4 7.3 %collective-permute-start.1 = (bf16[128,512]{1,0:T(8,128)(2,1)S(1)}, bf16[128,512]{1,0:T(8,128)(2,1)S(1)}, u32[]{:S(2)}, u32[]{:S(2)}) collective-permute-start(bf16[128,512]{1,0:T(8,128)(2,1)S(1)} %shard_map.121.refs_9_.refs_1_), channel_id=1, source_target_pairs={{0,4},{4,0},{8,12},{12,8},{1,5},{5,1},{9,13},{13,9},{2,6},{6,2},{1... | collective-permute-start | bytes 393224 | tf_op jit(solution)/shard_map/ppermute | solution.py:663
  10.7 10.7 %copy-start.2 = (bf16[384,1024]{1,0:T(8,128)(2,1)}, bf16[384,1024]{1,0:T(8,128)(2,1)S(1)}, u32[]{:S(2)}) copy-start(bf16[384,1024]{1,0:T(8,128)(2,1)S(1)} %get-tuple-element.87.refs_21_.refs_9_) | copy-start | bytes 2359300
  10.7 10.7 %copy-start.8 = (bf16[384,512]{1,0:T(8,128)(2,1)}, bf16[384,512]{1,0:T(8,128)(2,1)S(1)}, u32[]{:S(2)}) copy-start(bf16[384,512]{1,0:T(8,128)(2,1)S(1)} %get-tuple-element.66.refs_1_.refs_10_.refs_4_) | copy-start | bytes 1179652
  10.7 10.7 %copy-start.10 = (bf16[384,512]{1,0:T(8,128)(2,1)}, bf16[384,512]{1,0:T(8,128)(2,1)S(1)}, u32[]{:S(2)}) copy-start(bf16[384,512]{1,0:T(8,128)(2,1)S(1)} %get-tuple-element.67.refs_2_.refs_11_.refs_5_) | copy-start | bytes 1179652
  10.8 9.0 %collective-permute-start.2 = (bf16[128,512]{1,0:T(8,128)(2,1)S(1)}, bf16[128,512]{1,0:T(8,128)(2,1)S(1)}, u32[]{:S(2)}, u32[]{:S(2)}) collective-permute-start(bf16[128,512]{1,0:T(8,128)(2,1)S(1)} %shard_map.123.refs_15_.refs_3_), channel_id=1, source_target_pairs={{0,8},{4,12},{8,0},{12,4},{1,9},{5,13},{9,1},{13,5},{2,10},{6,14},... | collective-permute-start | bytes 393224 | tf_op jit(solution)/shard_map/ppermute | solution.py:663
  19.8 1.6 %collective-permute-start.3 = (bf16[2,128,512]{2,1,0:T(8,128)(2,1)S(1)}, bf16[2,128,512]{2,1,0:T(8,128)(2,1)S(1)}, u32[]{:S(2)}, u32[]{:S(2)}) collective-permute-start(bf16[2,128,512]{2,1,0:T(8,128)(2,1)S(1)} %shard_map.125.refs_22_), channel_id=1, source_target_pairs={{0,1},{1,0},{2,3},{3,2},{4,5},{5,4},{6,7},{7,6},{8,9},{9,8},{10,11... | collective-permute-start | bytes 786440 | tf_op jit(solution)/shard_map/ppermute | solution.py:663
  29.6 1.1 %copy-start = (f32[384,1024]{1,0:T(8,128)}, f32[384,1024]{1,0:T(8,128)S(1)}, u32[]{:S(2)}) copy-start(f32[384,1024]{1,0:T(8,128)S(1)} %get-tuple-element.89.refs_1_) | copy-start | bytes 4718596
  30.8 0.9 %copy-start.4 = (bf16[128,3072]{1,0:T(8,128)(2,1)}, bf16[128,3072]{1,0:T(8,128)(2,1)S(1)}, u32[]{:S(2)}) copy-start(bf16[128,3072]{1,0:T(8,128)(2,1)S(1)} %get-tuple-element.90.refs_2_) | copy-start | bytes 2359300
  31.7 0.9 %copy-start.6 = (bf16[128,3072]{1,0:T(8,128)(2,1)}, bf16[128,3072]{1,0:T(8,128)(2,1)S(1)}, u32[]{:S(2)}) copy-start(bf16[128,3072]{1,0:T(8,128)(2,1)S(1)} %get-tuple-element.91.refs_3_) | copy-start | bytes 2359300
  32.6 2.0 %collective-permute-start.4 = (bf16[2,128,512]{2,1,0:T(8,128)(2,1)S(1)}, bf16[2,128,512]{2,1,0:T(8,128)(2,1)S(1)}, u32[]{:S(2)}, u32[]{:S(2)}) collective-permute-start(bf16[2,128,512]{2,1,0:T(8,128)(2,1)S(1)} %get-tuple-element.94), channel_id=1, source_target_pairs={{0,1},{1,0},{2,3},{3,2},{4,5},{5,4},{6,7},{7,6},{8,9},{9,8},{10,11... | collective-permute-start | bytes 786440 | tf_op jit(solution)/shard_map/ppermute | solution.py:663
  32.7 16.9 %collective-permute-start.8 = (bf16[2,128,384]{2,1,0:T(8,128)(2,1)S(1)}, bf16[2,128,384]{2,1,0:T(8,128)(2,1)S(1)}, u32[]{:S(2)}, u32[]{:S(2)}) collective-permute-start(bf16[2,128,384]{2,1,0:T(8,128)(2,1)S(1)} %get-tuple-element.88.refs_5_), channel_id=1, source_target_pairs={{0,1},{1,0},{2,3},{3,2},{4,5},{5,4},{6,7},{7,6},{8,9},{9,8},{10,11... | collective-permute-start | bytes 589832 | tf_op jit(solution)/shard_map/ppermute | solution.py:663
  33.1 16.5 %collective-permute-start.7 = (bf16[256,384]{1,0:T(8,128)(2,1)S(1)}, bf16[256,384]{1,0:T(8,128)(2,1)S(1)}, u32[]{:S(2)}, u32[]{:S(2)}) collective-permute-start(bf16[256,384]{1,0:T(8,128)(2,1)S(1)} %get-tuple-element.102.refs_3_.refs_8_), channel_id=1, source_target_pairs={{0,2},{2,0},{1,3},{3,1},{4,6},{6,4},{5,7},{7,5},{8,10},{10,8},{9,1... | collective-permute-start | bytes 589832 | tf_op jit(solution)/shard_map/ppermute | solution.py:663
  34.7 15.9 %collective-permute-start.5 = (bf16[128,512]{1,0:T(8,128)(2,1)S(1)}, bf16[128,512]{1,0:T(8,128)(2,1)S(1)}, u32[]{:S(2)}, u32[]{:S(2)}) collective-permute-start(bf16[128,512]{1,0:T(8,128)(2,1)S(1)} %get-tuple-element.95.refs_14_), channel_id=1, source_target_pairs={{0,8},{4,12},{8,0},{12,4},{1,9},{5,13},{9,1},{13,5},{2,10},{6,14},... | collective-permute-start | bytes 393224 | tf_op jit(solution)/shard_map/ppermute | solution.py:663
  34.8 15.8 %collective-permute-start.6 = (bf16[128,512]{1,0:T(8,128)(2,1)S(1)}, bf16[128,512]{1,0:T(8,128)(2,1)S(1)}, u32[]{:S(2)}, u32[]{:S(2)}) collective-permute-start(bf16[128,512]{1,0:T(8,128)(2,1)S(1)} %get-tuple-element.101), channel_id=1, source_target_pairs={{0,4},{4,0},{8,12},{12,8},{1,5},{5,1},{9,13},{13,9},{2,6},{6,2},{1... | collective-permute-start | bytes 393224 | tf_op jit(solution)/shard_map/ppermute | solution.py:663
  38.0 1.4 %copy-start.1 = (f32[384,1024]{1,0:T(8,128)S(1)}, f32[384,1024]{1,0:T(8,128)}, u32[]{:S(2)}) copy-start(f32[384,1024]{1,0:T(8,128)} %copy-done) | copy-start | bytes 4718596
  39.4 1.1 %copy-start.3 = (bf16[384,1024]{1,0:T(8,128)(2,1)S(1)}, bf16[384,1024]{1,0:T(8,128)(2,1)}, u32[]{:S(2)}) copy-start(bf16[384,1024]{1,0:T(8,128)(2,1)} %copy-done.2) | copy-start | bytes 2359300
  40.5 1.1 %copy-start.5 = (bf16[128,3072]{1,0:T(8,128)(2,1)S(1)}, bf16[128,3072]{1,0:T(8,128)(2,1)}, u32[]{:S(2)}) copy-start(bf16[128,3072]{1,0:T(8,128)(2,1)} %copy-done.4) | copy-start | bytes 2359300
  41.6 1.1 %copy-start.7 = (bf16[128,3072]{1,0:T(8,128)(2,1)S(1)}, bf16[128,3072]{1,0:T(8,128)(2,1)}, u32[]{:S(2)}) copy-start(bf16[128,3072]{1,0:T(8,128)(2,1)} %copy-done.6) | copy-start | bytes 2359300
  42.8 1.0 %copy-start.9 = (bf16[384,512]{1,0:T(8,128)(2,1)S(1)}, bf16[384,512]{1,0:T(8,128)(2,1)}, u32[]{:S(2)}) copy-start(bf16[384,512]{1,0:T(8,128)(2,1)} %copy-done.8) | copy-start | bytes 1179652
  43.8 1.0 %copy-start.11 = (bf16[384,512]{1,0:T(8,128)(2,1)S(1)}, bf16[384,512]{1,0:T(8,128)(2,1)}, u32[]{:S(2)}) copy-start(bf16[384,512]{1,0:T(8,128)(2,1)} %copy-done.10) | copy-start | bytes 1179652
  50.7 6.3 %collective-permute-start.9 = (bf16[128,512]{1,0:T(8,128)(2,1)S(1)}, bf16[128,512]{1,0:T(8,128)(2,1)S(1)}, u32[]{:S(2)}, u32[]{:S(2)}) collective-permute-start(bf16[128,512]{1,0:T(8,128)(2,1)S(1)} %get-tuple-element.105.refs_10_), channel_id=1, source_target_pairs={{0,4},{4,0},{8,12},{12,8},{1,5},{5,1},{9,13},{13,9},{2,6},{6,2},{1... | collective-permute-start | bytes 393224 | tf_op jit(solution)/shard_map/ppermute | solution.py:663
  50.7 4.3 %collective-permute-start.10 = (bf16[256,128]{1,0:T(8,128)(2,1)S(1)}, bf16[256,128]{1,0:T(8,128)(2,1)S(1)}, u32[]{:S(2)}, u32[]{:S(2)}) collective-permute-start(bf16[256,128]{1,0:T(8,128)(2,1)S(1)} %get-tuple-element.103.refs_4_.refs_9_), channel_id=1, source_target_pairs={{0,2},{2,0},{1,3},{3,1},{4,6},{6,4},{5,7},{7,5},{8,10},{10,8},{9,1... | collective-permute-start | bytes 196616 | tf_op jit(solution)/shard_map/ppermute | solution.py:663
  57.0 1.5 %collective-permute-start.11 = (bf16[128,768]{1,0:T(8,128)(2,1)S(1)}, bf16[128,768]{1,0:T(8,128)(2,1)S(1)}, u32[]{:S(2)}, u32[]{:S(2)}) collective-permute-start(bf16[128,768]{1,0:T(8,128)(2,1)S(1)} %shard_map.132.refs_3_), channel_id=1, source_target_pairs={{0,1},{1,0},{2,3},{3,2},{4,5},{5,4},{6,7},{7,6},{8,9},{9,8},{10,11... | collective-permute-start | bytes 589832 | tf_op jit(solution)/shard_map/ppermute | solution.py:663
  58.7 5.6 %collective-permute-start.12 = (bf16[128,512]{1,0:T(8,128)(2,1)S(1)}, bf16[128,512]{1,0:T(8,128)(2,1)S(1)}, u32[]{:S(2)}, u32[]{:S(2)}) collective-permute-start(bf16[128,512]{1,0:T(8,128)(2,1)S(1)} %get-tuple-element.110.refs_3_.refs_6_), channel_id=1, source_target_pairs={{0,2},{2,0},{1,3},{3,1},{4,6},{6,4},{5,7},{7,5},{8,10},{10,8},{9,1... | collective-permute-start | bytes 393224 | tf_op jit(solution)/shard_map/ppermute | solution.py:663

commit v9 on v6

--- a/solution.py
+++ b/solution.py
@@ -563,68 +563,123 @@
     return copies
 
 
-def begin_input_grad(facts, side, w, own):
+def side_call(body, facts, side, near, far, outs, scratch, aliases=None, after=()):
+    smem = pl.BlockSpec(memory_space=pltpu.SMEM)
+    vmem = pl.BlockSpec(memory_space=pltpu.VMEM)
+    hbm = pl.BlockSpec(memory_space=pl.ANY)
+    near = [pltpu.with_memory_space_constraint(a, pltpu.VMEM) for a in near]
+    used = 2 + len(near) + len(far)
+
+    def kernel(*refs):
+        body(*refs[:used], *refs[used + len(after) :])
+
+    return pl.pallas_call(
+        kernel,
+        out_shape=tuple(
+            pltpu.VMEM(s, d) if inside else jax.ShapeDtypeStruct(s, d) for s, d, inside in outs
+        ),
+        in_specs=[smem] * 2 + [vmem] * len(near) + [hbm] * (len(far) + len(after)),
+        out_specs=tuple(vmem if inside else hbm for _, _, inside in outs),
+        scratch_shapes=list(scratch),
+        input_output_aliases={2 + len(near) + i: o for i, o in (aliases or {}).items()},
+        compiler_params=pltpu.CompilerParams(vmem_limit_bytes=LARGE),
+        cost_estimate=SLIGHT,
+    )(pltpu.with_memory_space_constraint(facts, pltpu.SMEM), side, *near, *far, *after)
+
+
+def half_columns(w, which):
+    half = w.shape[1] // 2
+    return pl.ds(pl.multiple_of(which * half, half), half)
+
+
+class Pieces:
+    def __init__(self, w_ref, which, into, sem, tiles):
+        self.copies = [
+            pltpu.make_async_copy(
+                w_ref.at[at, half_columns(w_ref, which)], into.at[at], sem.at[i]
+            )
+            for i, at in enumerate(tiles)
+        ]
+        for c in self.copies[:2]:
+            c.start()
+
+    def wait(self, i):
+        self.copies[i].wait()
+        if i + 2 < len(self.copies):
+            self.copies[i + 2].start()
+
+
+def begin_input_grad(facts, side, w, own, rest, after=()):
     out_cols, depth = w.shape
     tiles = width_tiles(w)
-    half = depth // 2
-
-    def body(facts, flag, own_r, w_ref, out, w_far, w_near, sem):
-        place = lambda which: pl.ds(pl.multiple_of(which * half, half), half)
-        loads = [
-            pltpu.make_async_copy(w_ref.at[at, place(flag[0])], w_near.at[at], sem.at[i])
-            for i, at in enumerate(tiles)
-        ]
-        rest = pltpu.make_async_copy(w_ref.at[:, place(1 - flag[0])], w_far, sem.at[len(tiles)])
-        for c in [*loads, rest]:
-            c.start()
+    count = len(own)
+    half = ((out_cols, depth // 2), BF16, True)
+
+    def body(facts, flag, *refs):
+        out, w_near, sem = refs[count + 1], refs[-2], refs[-1]
+        pieces = Pieces(refs[count], flag[0], w_near, sem, tiles)
+        mine = jnp.concatenate([r[...] for r in refs[:count]], axis=1)
         for i, at in enumerate(tiles):
-            loads[i].wait()
-            out[at] = dot_t(w_near[at], own_r[...])
-        rest.wait()
-
-    smem = pl.BlockSpec(memory_space=pltpu.SMEM)
-    vmem = pl.BlockSpec(memory_space=pltpu.VMEM)
-    return pl.pallas_call(
-        body,
-        out_shape=(pltpu.VMEM((out_cols, own.shape[0]), F32), pltpu.VMEM((out_cols, half), BF16)),
-        in_specs=[smem, smem, vmem, pl.BlockSpec(memory_space=pl.ANY)],
-        out_specs=(vmem, vmem),
-        scratch_shapes=[
-            pltpu.VMEM((out_cols, half), BF16), pltpu.SemaphoreType.DMA((len(tiles) + 1,))
-        ],
-        compiler_params=pltpu.CompilerParams(vmem_limit_bytes=LARGE),
-        cost_estimate=pl.CostEstimate(
-            flops=own.shape[0] * depth * out_cols, bytes_accessed=1000, transcendentals=0
-        ),
-    )(
-        pltpu.with_memory_space_constraint(facts, pltpu.SMEM), side,
-        pltpu.with_memory_space_constraint(own, pltpu.VMEM), w,
+            pieces.wait(i)
+            if rest and i + 3 == len(tiles):
+                other = pltpu.make_async_copy(
+                    refs[count].at[:, half_columns(refs[count], 1 - flag[0])], refs[count + 2],
+                    sem.at[len(tiles)],
+                )
+                other.start()
+            out[at] = dot_t(w_near[at], mine)
+        if rest:
+            other.wait()
+
+    return side_call(
+        body, facts, side, own, [w],
+        [((out_cols, own[0].shape[0]), F32, True)] + [half] * rest,
+        [pltpu.VMEM(half[0], BF16), pltpu.SemaphoreType.DMA((len(tiles) + 1,))], after=after,
     )
 
 
-def end_input_grad(facts, far, begun, w_far, grads, carry):
-    tiles = width_tiles(w_far)
+def end_input_grad(facts, side, w, far, begun, grads, carry=(), after=()):
+    tiles = width_tiles(w)
+    out_cols = w.shape[0]
     steps = len(tiles)
-    rows = far.shape[0]
-
-    def body(facts, far_r, begun_r, w_r, *refs):
-        out, dk, dv, stage, sem = refs[-5:]
-        copies = put_rows(refs[:2], dk, dv, 0, rows, sem, steps)
+    rows = far[0].shape[0]
+    top = 0 if carry else PAGE
+    width = sum(a.shape[1] for a in grads[0])
+    near = [begun, *far, *grads[0], *grads[1]] + ([w] if carry else [])
+    count = len(far)
+    half = (out_cols, width)
+
+    def body(facts, flag, begun_r, *refs):
+        far_r, grad_r = refs[:count], refs[count : count + 2 * len(grads[0])]
+        w_ref = refs[count + 2 * len(grads[0])]
+        out, dk, dv, made, stage, w_far, w_sem, sem = refs[-8:]
+        pieces = None if carry else Pieces(w_ref, 1 - flag[0], w_far, w_sem, tiles)
+        made[...] = jnp.zeros_like(made)
+        copies = put_rows(grad_r, dk, dv, top, rows, sem, steps)
+        other = jnp.concatenate([r[...] for r in far_r], axis=1)
         for i, at in enumerate(tiles):
-            stage[i] = (dot_t(w_r[at], far_r[...]) + begun_r[at]).astype(BF16).T
-            copies.append(pltpu.make_async_copy(stage.at[i], out.at[:rows, at], sem.at[i]))
+            if pieces:
+                pieces.wait(i)
+            product = dot_t((w_far if pieces else w_ref)[at], other)
+            stage[i] = (product + begun_r[at]).astype(BF16).T
+            copies.append(
+                pltpu.make_async_copy(stage.at[i], out.at[top : top + rows, at], sem.at[i])
+            )
             copies[-1].start()
         for c in copies:
             c.wait()
 
-    return kernel_call(
-        body, facts, [far, begun, w_far, *grads], carry,
-        [(a.shape, a.dtype, False) for a in carry],
+    full = ((ROWS, width), BF16, False)
+    return side_call(
+        body, facts, side, near, list(carry) if carry else [w],
+        [((ROWS, out_cols), BF16, False), full, full, ((8, HD), F32, True)],
         [
-            pltpu.VMEM((steps, rows, w_far.shape[0] // steps), BF16),
-            pltpu.SemaphoreType.DMA((steps + 2,)),
+            pltpu.VMEM((steps, rows, out_cols // steps), BF16),
+            pltpu.VMEM((8, HD) if carry else half, BF16),
+            pltpu.SemaphoreType.DMA((steps,)),
+            pltpu.SemaphoreType.DMA((steps + 2 * len(grads[0]),)),
         ],
-        {("far", i): i for i in range(len(carry))},
+        {i: i for i in range(len(carry))}, after,
     )
 
 
@@ -701,7 +756,7 @@
         body, facts, [total, root_far, next_far], [],
         [((2, PAGE, width), F32, True), ((PAGE, width), BF16, True)], after=after,
     )
-    return total, flipped(low, "leaf", 1)
+    return total, low, flipped(low, "leaf", 1)
 
 
 def over_chips(facts, total, far, passenger, after=()):
@@ -806,16 +861,17 @@
         level2_far = flipped(most[3], "sub", 1)
         kept, sent = shared_pages(kvs, shared)
         total, root, root_far, next_far = over_cores(facts, kept, sent)
-        last = own_pages(kvs[-1:], level2, after=(root, far_v[0], level2_far))
+        last = own_pages(kvs[-1:], level2, after=(root,))
+        both = list(zip(most, last))
+        begun, = begin_input_grad(facts, side, w, both[1], False, (far_v[0], level2_far))
         far_v.append(spread(last[1]))
-        total, far = over_halves(facts, total, root_far, next_far, (last[3],))
-        both = list(zip(most, last))
-        *grads, made = input_grad(facts, side, w, 2 * PAGE, both[1], far_v, both[:2])
+        total, low, far = over_halves(facts, total, root_far, next_far, (begun,))
+        *grads, made = end_input_grad(facts, side, w, far_v, begun, both[:2], after=(low,))
         mine, far = over_chips(facts, total, far, last[3], (made,))
         dk0, dv0 = finish_small_tree(facts, both[2], mine, far, level2_far)
         far_v = spread(dv0)
-        begun, w_far = begin_input_grad(facts, side, w, dv0)
-        grads = end_input_grad(facts, far_v, begun, w_far, [dk0, dv0], grads)
+        begun, w_far = begin_input_grad(facts, side, w, [dv0], True)
+        grads = end_input_grad(facts, side, w_far, [far_v], begun, ([dk0], [dv0]), grads)
         return (state["gq"], grads[1], grads[2], grads[0])
 
     first = lax.axis_index("sub") == 0

time: 60.3 us -> 82.8 us (1.37)
  local copies, waits for them, and re-layouts: 0 us -> 19.3 us
  Pallas kernels: 32.2 us -> 38.7 us
  waiting for transfers between devices: 13.4 us -> 8.5 us
  starting transfers between devices: 13.6 us -> 14.5 us
    unnamed x0 -> x46, local copies, waits for them, and re-layouts: none -> 19.3 us
    pallas_call x2 -> x4, Pallas kernels: 8.96 us -> 14.9 us  [side_call(): pl.pallas_call(kernel, out_shape=tuple((pltpu.VMEM(s, d) if inside else j...]
    ppermute x13, waiting for transfers between devices: 13.4 us -> 8.5 us  [flipped(): lax.ppermute(block, axis, [(i, i ^ bit) for i in range(count) if i ^ bit...]
    ppermute x13, starting transfers between devices: 13.6 us -> 14.5 us  [flipped(): lax.ppermute(block, axis, [(i, i ^ bit) for i in range(count) if i ^ bit...]
    pallas_call x12 -> x11, Pallas kernels: 22.2 us -> 22.8 us  [kernel_call(): pl.pallas_call(kernel, out_shape=tuple((pltpu.VMEM(s, d) if inside else j...]
  transfers between devices with their start and end apart: 13 -> 13, of which waited for: 9 -> 6; matrix products, arithmetic and copies ran while one was open for 0% -> 0% of each run, Pallas kernels for 36% -> 32%
where the time goes in v9:
time: 82.8 us; the launch traced here: 82.1 us
  Pallas kernels  38.7 us (47%)
  local copies, waits for them, and re-layouts  19.3 us (23%)
  starting transfers between devices  14.5 us (18%)
  waiting for transfers between devices  8.5 us (10%)
  between operations  1.11 us (1%)
    pallas_call x11, Pallas kernels, kernel_call(): pl.pallas_call(kernel, out_shape=tuple((pltpu.VMEM(s, d) if inside else j...  22.8 us
    unnamed x46, local copies, waits for them, and re-layouts  19.3 us
    pallas_call x4, Pallas kernels, side_call(): pl.pallas_call(kernel, out_shape=tuple((pltpu.VMEM(s, d) if inside else j...  14.9 us
    ppermute x13, starting transfers between devices, flipped(): lax.ppermute(block, axis, [(i, i ^ bit) for i in range(count) if i ^ bit...  14.5 us
    ppermute x13, waiting for transfers between devices, flipped(): lax.ppermute(block, axis, [(i, i ^ bit) for i in range(count) if i ^ bit...  8.5 us
  transfers between devices with their start and end apart: 13, of which 6 were waited for; matrix products, arithmetic and copies ran while one was open for 0% of the time, Pallas kernels for 32%

profile of v9, /device:TPU:0, one launch (start us, length us, event | category | flops | bytes accessed | tf_op | source)
XLA Modules:
  0.0 82.1 jit_solution(5486961514533045897)
XLA Ops:
  0.6 1.0 %shard_map.120 = (s32[16]{0:T(128)S(4)}, bf16[2,128,512]{2,1,0:T(8,128)(2,1)S(1)}) custom-call(s32[1,5]{1,0:T(1,128)} %ids_ref.1, s32[1,3]{1,0:T(1,128)} %counts_ref.1, bf16[384,512]{1,0:T(8,128)(2,1)} %refs_5_.1, bf16[384,512]{1,0:T(8,128)(2,1)} %refs_6_.1), custom_call_target="tpu_custom_call" | custom-call | tf_op jit(solution)/shard_map/pallas_call | solution.py:116
  1.7 0.5 collective-permute-start
  2.2 1.2 %collective-permute-done.refs_2_.refs_11_ = bf16[2,128,512]{2,1,0:T(8,128)(2,1)S(1)} collective-permute-done((bf16[2,128,512]{2,1,0:T(8,128)(2,1)S(1)}, bf16[2,128,512]{2,1,0:T(8,128)(2,1)S(1)}, u32[]{:S(2)}, u32[]{:S(2)}) %collective-permute-start) | collective-permute-done | bytes 262176 | tf_op jit(solution)/shard_map/ppermute | solution.py:688
  3.4 3.0 %collective-permute-start.1 = (bf16[128,512]{1,0:T(8,128)(2,1)S(1)}, bf16[128,512]{1,0:T(8,128)(2,1)S(1)}, u32[]{:S(2)}, u32[]{:S(2)}) collective-permute-start(bf16[128,512]{1,0:T(8,128)(2,1)S(1)} %shard_map.121.refs_9_.refs_1_), channel_id=1, source_target_pairs={{0,4},{4,0},{8,12},{12,8},{1,5},{5,1},{9,13},{13,9},{2,6},{6,2},{1... | collective-permute-start | bytes 393224 | tf_op jit(solution)/shard_map/ppermute | solution.py:688
  6.4 4.3 %shard_map.122 = (f32[384,4096]{1,0:T(8,128)S(1)}, bf16[128,12288]{1,0:T(8,128)(2,1)S(1)}, bf16[128,12288]{1,0:T(8,128)(2,1)S(1)}, bf16[256,128]{1,0:T(8,128)(2,...) custom-call(s32[16]{0:T(128)S(4)} %get-tuple-element.53.refs_0_, ...), custom_call_target="tpu_custom_call" | custom-call | flops 4026531840 | bytes 1000 | tf_op jit(solution)/shard_map/pallas_call | solution.py:75
  10.7 0.0 copy-start.2
  10.7 0.0 copy-start.16
  10.7 0.0 copy-start.18
  10.7 0.0 collective-permute-done.1.refs_2_
  10.7 2.7 %collective-permute-start.2 = (bf16[128,512]{1,0:T(8,128)(2,1)S(1)}, bf16[128,512]{1,0:T(8,128)(2,1)S(1)}, u32[]{:S(2)}, u32[]{:S(2)}) collective-permute-start(bf16[128,512]{1,0:T(8,128)(2,1)S(1)} %shard_map.123.refs_16_.refs_3_), channel_id=1, source_target_pairs={{0,8},{4,12},{8,0},{12,4},{1,9},{5,13},{9,1},{13,5},{2,10},{6,14},... | collective-permute-start | bytes 393224 | tf_op jit(solution)/shard_map/ppermute | solution.py:688
  13.4 0.0 copy-done.8
  13.4 4.9 %shard_map.124 = (f32[384,4096]{1,0:T(8,128)S(1)}, bf16[128,12288]{1,0:T(8,128)(2,1)S(1)}, bf16[128,12288]{1,0:T(8,128)(2,1)S(1)}, bf16[256,384]{1,0:T(8,128)(2,...) custom-call(s32[16]{0:T(128)S(4)} %get-tuple-element.53.refs_0_, ...), custom_call_target="tpu_custom_call", output_to_operand_aliasing={{0}: (1, {}), {1}: (2, {}), {2}: (3, {})} | custom-call | flops 8053063680 | bytes 1000 | tf_op jit(solution)/shard_map/pallas_call | solution.py:75
  18.3 0.0 copy-start.10
  18.3 0.0 copy-start.14
  18.3 0.0 copy-start.21
  18.3 0.0 copy-start.20
  18.3 1.4 %collective-permute-done.2.refs_4_ = bf16[128,512]{1,0:T(8,128)(2,1)S(1)} collective-permute-done((bf16[128,512]{1,0:T(8,128)(2,1)S(1)}, bf16[128,512]{1,0:T(8,128)(2,1)S(1)}, u32[]{:S(2)}, u32[]{:S(2)}) %collective-permute-start.2) | collective-permute-done | bytes 131104 | tf_op jit(solution)/shard_map/ppermute | solution.py:688
  19.8 0.1 collective-permute-start.3
  19.9 1.5 %collective-permute-done.3.refs_11_ = bf16[2,128,512]{2,1,0:T(8,128)(2,1)S(1)} collective-permute-done((bf16[2,128,512]{2,1,0:T(8,128)(2,1)S(1)}, bf16[2,128,512]{2,1,0:T(8,128)(2,1)S(1)}, u32[]{:S(2)}, u32[]{:S(2)}) %collective-permute-start.3) | collective-permute-done | bytes 262176 | tf_op jit(solution)/shard_map/ppermute | solution.py:688
  21.4 0.0 copy-done.10
  21.4 0.0 copy-done.14
  21.4 0.0 copy-done.2
  21.4 0.0 copy-done.16
  21.4 0.0 copy-done.18
  21.4 8.9 %shard_map.126 = (f32[384,4096]{1,0:T(8,128)S(1)}, bf16[128,12288]{1,0:T(8,128)(2,1)S(1)}, bf16[128,12288]{1,0:T(8,128)(2,1)S(1)}, bf16[384,4096]{1,0:T(8,128)(2...) custom-call(s32[16]{0:T(128)S(4)} %get-tuple-element.53.refs_0_, ...), custom_call_target="tpu_custom_call", output_to_operand_aliasing={{0}: (1, {}), {1}: (2, {}), {2}: (3, {})} | custom-call | flops 16106127360 | bytes 1000 | tf_op jit(solution)/shard_map/pallas_call | solution.py:75
  30.4 2.7 %copy-done = f32[384,4096]{1,0:T(8,128)} copy-done((f32[384,4096]{1,0:T(8,128)}, f32[384,4096]{1,0:T(8,128)S(1)}, u32[]{:S(2)}) %copy-start) | copy-done | bytes 6291480
  33.1 1.7 %copy-done.4 = bf16[128,12288]{1,0:T(8,128)(2,1)} copy-done((bf16[128,12288]{1,0:T(8,128)(2,1)}, bf16[128,12288]{1,0:T(8,128)(2,1)S(1)}, u32[]{:S(2)}) %copy-start.4) | copy-done | bytes 3145752
  34.8 1.6 %copy-done.6 = bf16[128,12288]{1,0:T(8,128)(2,1)} copy-done((bf16[128,12288]{1,0:T(8,128)(2,1)}, bf16[128,12288]{1,0:T(8,128)(2,1)S(1)}, u32[]{:S(2)}) %copy-start.6) | copy-done | bytes 3145752
  36.4 0.8 copy-done.12
  37.2 0.1 collective-permute-start.4
  37.3 0.4 collective-permute-start.8
  37.7 1.5 %collective-permute-start.7 = (bf16[256,384]{1,0:T(8,128)(2,1)}, bf16[256,384]{1,0:T(8,128)(2,1)S(1)}, u32[]{:S(2)}, u32[]{:S(2)}) collective-permute-start(bf16[256,384]{1,0:T(8,128)(2,1)} %copy-done.10), channel_id=1, source_target_pairs={{0,2},{2,0},{1,3},{3,1},{4,6},{6,4},{5,7},{7,5},{8,10},{10,8},{9,1... | collective-permute-start | bytes 589832 | tf_op jit(solution)/shard_map/ppermute | solution.py:688
  39.2 0.0 collective-permute-done.4.refs_2_
  39.2 1.0 %copy-done.13 = f32[2,128,512]{2,1,0:T(8,128)S(1)} copy-done((f32[2,128,512]{2,1,0:T(8,128)S(1)}, f32[2,128,512]{2,1,0:T(8,128)}, u32[]{:S(2)}) %copy-start.13) | copy-done | bytes 524312
  40.3 1.0 %shard_map.127 = (f32[2,128,512]{2,1,0:T(8,128)S(1)}, bf16[128,512]{1,0:T(8,128)(2,1)S(1)}, bf16[128,512]{1,0:T(8,128)(2,1)S(1)}) custom-call(s32[16]{0:T(128)S(4)} %get-tuple-element.53.refs_0_, f32[2,128,512]{2,1,0:T(8,128)S(1)} %copy-done.13, bf16[2,128,512]{2,1,0:T(8,128)(2,1)} %collective-permute-done.4.refs_2_), custom_call_target="tpu_custom_call" | custom-call | flops 1000 | bytes 1000 | tf_op jit(solution)/shard_map/pallas_call | solution.py:75
  41.3 0.1 collective-permute-start.5
  41.4 3.2 %collective-permute-start.6 = (bf16[128,512]{1,0:T(8,128)(2,1)S(1)}, bf16[128,512]{1,0:T(8,128)(2,1)S(1)}, u32[]{:S(2)}, u32[]{:S(2)}) collective-permute-start(bf16[128,512]{1,0:T(8,128)(2,1)S(1)} %get-tuple-element.83), channel_id=1, source_target_pairs={{0,4},{4,0},{8,12},{12,8},{1,5},{5,1},{9,13},{13,9},{2,6},{6,2},{1... | collective-permute-start | bytes 393224 | tf_op jit(solution)/shard_map/ppermute | solution.py:688
  44.5 2.8 %copy-done.1 = f32[384,4096]{1,0:T(8,128)S(1)} copy-done((f32[384,4096]{1,0:T(8,128)S(1)}, f32[384,4096]{1,0:T(8,128)}, u32[]{:S(2)}) %copy-start.1) | copy-done | bytes 6291480
  47.3 1.9 %copy-done.3 = bf16[384,4096]{1,0:T(8,128)(2,1)S(1)} copy-done((bf16[384,4096]{1,0:T(8,128)(2,1)S(1)}, bf16[384,4096]{1,0:T(8,128)(2,1)}, u32[]{:S(2)}) %copy-start.3) | copy-done | bytes 3145752
  49.2 1.9 %copy-done.5 = bf16[128,12288]{1,0:T(8,128)(2,1)S(1)} copy-done((bf16[128,12288]{1,0:T(8,128)(2,1)S(1)}, bf16[128,12288]{1,0:T(8,128)(2,1)}, u32[]{:S(2)}) %copy-start.5) | copy-done | bytes 3145752
  51.1 1.9 %copy-done.7 = bf16[128,12288]{1,0:T(8,128)(2,1)S(1)} copy-done((bf16[128,12288]{1,0:T(8,128)(2,1)S(1)}, bf16[128,12288]{1,0:T(8,128)(2,1)}, u32[]{:S(2)}) %copy-start.7) | copy-done | bytes 3145752
  53.0 0.9 %copy-done.9 = bf16[2,128,512]{2,1,0:T(8,128)(2,1)S(1)} copy-done((bf16[2,128,512]{2,1,0:T(8,128)(2,1)S(1)}, bf16[2,128,512]{2,1,0:T(8,128)(2,1)}, u32[]{:S(2)}) %copy-start.9) | copy-done | bytes 262168
  54.0 1.0 %copy-done.17 = bf16[384,512]{1,0:T(8,128)(2,1)S(1)} copy-done((bf16[384,512]{1,0:T(8,128)(2,1)S(1)}, bf16[384,512]{1,0:T(8,128)(2,1)}, u32[]{:S(2)}) %copy-start.17) | copy-done | bytes 393240
  55.0 1.0 %copy-done.19 = bf16[384,512]{1,0:T(8,128)(2,1)S(1)} copy-done((bf16[384,512]{1,0:T(8,128)(2,1)S(1)}, bf16[384,512]{1,0:T(8,128)(2,1)}, u32[]{:S(2)}) %copy-start.19) | copy-done | bytes 393240
  55.9 3.4 %shard_map.128 = (f32[384,4096]{1,0:T(8,128)S(1)}, bf16[128,12288]{1,0:T(8,128)(2,1)S(1)}, bf16[128,12288]{1,0:T(8,128)(2,1)S(1)}, bf16[384,4096]{1,0:T(8,128)(2...) custom-call(s32[16]{0:T(128)S(4)} %get-tuple-element.53.refs_0_, ...), custom_call_target="tpu_custom_call", output_to_operand_aliasing={{0}: (1, {}), {1}: (2, {}), {2}: (3, {}), {3}: (12, {})} | custom-call | flops 4026531840 | bytes 1000 | tf_op jit(solution)/shard_map/pallas_call | solution.py:75
  59.3 0.0 collective-permute-done.7.refs_5_.refs_3_
  59.3 0.0 collective-permute-done.8.refs_6_.refs_5_
  59.4 0.0 copy-done.11
  59.4 3.7 %shard_map.129.refs_4_.refs_2_ = f32[2560,256]{1,0:T(8,128)S(1)} custom-call(s32[16]{0:T(128)S(4)} %get-tuple-element.53.refs_0_, s32[1]{0:T(128)} %bitcast.refs_1_, bf16[256,384]{1,0:T(8,128)(2,1)S(1)} %copy-done.11, bf16[256,128]{1,0:T(8,128)(2,1)S(1)} %get-tuple-element.85.refs_3_.refs_8_, bf16[2560,1024]{1,0:T(8,128)(2,1)} %refs_3_.3, ...), custom_call_target="tpu_custom_call" | custom-call | flops 1000 | bytes 1000 | tf_op jit(solution)/shard_map/pallas_call | solution.py:576
  63.1 0.0 collective-permute-done.5.refs_2_
  63.1 0.0 collective-permute-done.6.refs_3_
  63.1 0.1 shard_map.130
  63.2 0.1 collective-permute-start.9
  63.3 1.4 %collective-permute-start.10 = (bf16[256,128]{1,0:T(8,128)(2,1)S(1)}, bf16[256,128]{1,0:T(8,128)(2,1)S(1)}, u32[]{:S(2)}, u32[]{:S(2)}) collective-permute-start(bf16[256,128]{1,0:T(8,128)(2,1)S(1)} %get-tuple-element.85.refs_3_.refs_8_), channel_id=1, source_target_pairs={{0,2},{2,0},{1,3},{3,1},{4,6},{6,4},{5,7},{7,5},{8,10},{10,8},{9,1... | collective-permute-start | bytes 196616 | tf_op jit(solution)/shard_map/ppermute | solution.py:688
  64.7 2.9 %collective-permute-done.10.refs_4_ = bf16[256,128]{1,0:T(8,128)(2,1)S(1)} collective-permute-done((bf16[256,128]{1,0:T(8,128)(2,1)S(1)}, bf16[256,128]{1,0:T(8,128)(2,1)S(1)}, u32[]{:S(2)}, u32[]{:S(2)}) %collective-permute-start.10) | collective-permute-done | bytes 65568 | tf_op jit(solution)/shard_map/ppermute | solution.py:688
  67.6 4.8 %shard_map.131 = (bf16[384,2560]{1,0:T(8,128)(2,1)}, bf16[384,512]{1,0:T(8,128)(2,1)}, bf16[384,512]{1,0:T(8,128)(2,1)}, f32[8,128]{1,0:T(8,128)S(1)}) custom-call(s32[16]{0:T(128)S(4)} %get-tuple-element.53.refs_0_, s32[1]{0:T(128)} %bitcast.refs_1_, f32[2560,256]{1,0:T(8,128)S(1)} %shard_map.129.refs_4_.refs_2_, ...), custom_call_target="tpu_custom_call" | custom-call | flops 1000 | bytes 1000 | tf_op jit(solution)/shard_map/pallas_call | solution.py:576
  72.3 0.0 collective-permute-done.9.refs_2_
  72.4 0.1 collective-permute-start.11
  72.5 1.4 %collective-permute-done.11.refs_4_ = bf16[128,768]{1,0:T(8,128)(2,1)S(1)} collective-permute-done((bf16[128,768]{1,0:T(8,128)(2,1)S(1)}, bf16[128,768]{1,0:T(8,128)(2,1)S(1)}, u32[]{:S(2)}, u32[]{:S(2)}) %collective-permute-start.11) | collective-permute-done | bytes 196640 | tf_op jit(solution)/shard_map/ppermute | solution.py:688
  73.9 0.1 shard_map.133
  74.0 1.4 %collective-permute-start.12 = (bf16[128,512]{1,0:T(8,128)(2,1)S(1)}, bf16[128,512]{1,0:T(8,128)(2,1)S(1)}, u32[]{:S(2)}, u32[]{:S(2)}) collective-permute-start(bf16[128,512]{1,0:T(8,128)(2,1)S(1)} %get-tuple-element.92.refs_2_.refs_5_), channel_id=1, source_target_pairs={{0,2},{2,0},{1,3},{3,1},{4,6},{6,4},{5,7},{7,5},{8,10},{10,8},{9,1... | collective-permute-start | bytes 393224 | tf_op jit(solution)/shard_map/ppermute | solution.py:688
  75.5 4.1 %shard_map.134 = (f32[2560,128]{1,0:T(8,128)S(1)}, bf16[2560,512]{1,0:T(8,128)(2,1)S(1)}) custom-call(s32[16]{0:T(128)S(4)} %get-tuple-element.53.refs_0_, s32[1]{0:T(128)} %bitcast.refs_1_, bf16[128,512]{1,0:T(8,128)(2,1)S(1)} %get-tuple-element.92.refs_2_.refs_5_, bf16[2560,1024]{1,0:T(8,128)(2,1)} %refs_3_.3), custom_call_target="tpu_custom_call" | custom-call | flops 1000 | bytes 1000 | tf_op jit(solution)/shard_map/pallas_call | solution.py:576
  79.6 0.1 collective-permute-done.12.refs_3_
  79.7 2.3 %shard_map.135 = (bf16[384,2560]{1,0:T(8,128)(2,1)}, bf16[384,512]{1,0:T(8,128)(2,1)}, bf16[384,512]{1,0:T(8,128)(2,1)}, f32[8,128]{1,0:T(8,128)}) custom-call(s32[16]{0:T(128)S(4)} %get-tuple-element.53.refs_0_, s32[1]{0:T(128)} %bitcast.refs_1_, ...), custom_call_target="tpu_custom_call", output_to_operand_aliasing={{0}: (7, {}), {1}: (8, {}), {2}: (9, {})} | custom-call | flops 1000 | bytes 1000 | tf_op jit(solution)/shard_map/pallas_call | solution.py:576
  (24 shorter events, 0.2 us)
Async XLA Ops:
  1.7 1.7 %collective-permute-start = (bf16[2,128,512]{2,1,0:T(8,128)(2,1)S(1)}, bf16[2,128,512]{2,1,0:T(8,128)(2,1)S(1)}, u32[]{:S(2)}, u32[]{:S(2)}) collective-permute-start(bf16[2,128,512]{2,1,0:T(8,128)(2,1)S(1)} %get-tuple-element.54.refs_1_.refs_10_), channel_id=1, source_target_pairs={{0,1},{1,0},{2,3},{3,2},{4,5},{5,4},{6,7},{7,6},{8,9},{9,8},{10,11... | collective-permute-start | bytes 786440 | tf_op jit(solution)/shard_map/ppermute | solution.py:688
  3.3 10.1 %copy-start.8 = (bf16[2,128,512]{2,1,0:T(8,128)(2,1)}, bf16[2,128,512]{2,1,0:T(8,128)(2,1)S(1)}, u32[]{:S(2)}) copy-start(bf16[2,128,512]{2,1,0:T(8,128)(2,1)S(1)} %collective-permute-done.refs_2_.refs_11_) | copy-start | bytes 786436
  3.4 7.3 %collective-permute-start.1 = (bf16[128,512]{1,0:T(8,128)(2,1)S(1)}, bf16[128,512]{1,0:T(8,128)(2,1)S(1)}, u32[]{:S(2)}, u32[]{:S(2)}) collective-permute-start(bf16[128,512]{1,0:T(8,128)(2,1)S(1)} %shard_map.121.refs_9_.refs_1_), channel_id=1, source_target_pairs={{0,4},{4,0},{8,12},{12,8},{1,5},{5,1},{9,13},{13,9},{2,6},{6,2},{1... | collective-permute-start | bytes 393224 | tf_op jit(solution)/shard_map/ppermute | solution.py:688
  10.7 10.7 %copy-start.2 = (bf16[384,4096]{1,0:T(8,128)(2,1)}, bf16[384,4096]{1,0:T(8,128)(2,1)S(1)}, u32[]{:S(2)}) copy-start(bf16[384,4096]{1,0:T(8,128)(2,1)S(1)} %get-tuple-element.59.refs_5_) | copy-start | bytes 9437188
  10.7 10.7 %copy-start.16 = (bf16[384,512]{1,0:T(8,128)(2,1)}, bf16[384,512]{1,0:T(8,128)(2,1)S(1)}, u32[]{:S(2)}) copy-start(bf16[384,512]{1,0:T(8,128)(2,1)S(1)} %get-tuple-element.60.refs_6_) | copy-start | bytes 1179652
  10.7 10.7 %copy-start.18 = (bf16[384,512]{1,0:T(8,128)(2,1)}, bf16[384,512]{1,0:T(8,128)(2,1)S(1)}, u32[]{:S(2)}) copy-start(bf16[384,512]{1,0:T(8,128)(2,1)S(1)} %get-tuple-element.61.refs_7_) | copy-start | bytes 1179652
  10.7 9.0 %collective-permute-start.2 = (bf16[128,512]{1,0:T(8,128)(2,1)S(1)}, bf16[128,512]{1,0:T(8,128)(2,1)S(1)}, u32[]{:S(2)}, u32[]{:S(2)}) collective-permute-start(bf16[128,512]{1,0:T(8,128)(2,1)S(1)} %shard_map.123.refs_16_.refs_3_), channel_id=1, source_target_pairs={{0,8},{4,12},{8,0},{12,4},{1,9},{5,13},{9,1},{13,5},{2,10},{6,14},... | collective-permute-start | bytes 393224 | tf_op jit(solution)/shard_map/ppermute | solution.py:688
  18.3 3.1 %copy-start.10 = (bf16[256,384]{1,0:T(8,128)(2,1)}, bf16[256,384]{1,0:T(8,128)(2,1)S(1)}, u32[]{:S(2)}) copy-start(bf16[256,384]{1,0:T(8,128)(2,1)S(1)} %get-tuple-element.84.refs_2_.refs_7_) | copy-start | bytes 589828
  18.3 3.1 %copy-start.14 = (f32[2,128,384]{2,1,0:T(8,128)}, f32[2,128,384]{2,1,0:T(8,128)S(1)}, u32[]{:S(2)}) copy-start(f32[2,128,384]{2,1,0:T(8,128)S(1)} %get-tuple-element.80.refs_1_) | copy-start | bytes 1179652
  18.3 3.1 %copy-start.21 = (bf16[256,384]{1,0:T(8,128)(2,1)}, bf16[256,384]{1,0:T(8,128)(2,1)S(1)}, u32[]{:S(2)}) copy-start(bf16[256,384]{1,0:T(8,128)(2,1)S(1)} %get-tuple-element.89.refs_5_) | copy-start | bytes 589828
  18.3 12.0 %copy-start.20 = (bf16[2,128,384]{2,1,0:T(8,128)(2,1)}, bf16[2,128,384]{2,1,0:T(8,128)(2,1)S(1)}, u32[]{:S(2)}) copy-start(bf16[2,128,384]{2,1,0:T(8,128)(2,1)S(1)} %get-tuple-element.71.refs_5_) | copy-start | bytes 589828
  19.8 1.6 %collective-permute-start.3 = (bf16[2,128,512]{2,1,0:T(8,128)(2,1)S(1)}, bf16[2,128,512]{2,1,0:T(8,128)(2,1)S(1)}, u32[]{:S(2)}, u32[]{:S(2)}) collective-permute-start(bf16[2,128,512]{2,1,0:T(8,128)(2,1)S(1)} %shard_map.125.refs_10_), channel_id=1, source_target_pairs={{0,1},{1,0},{2,3},{3,2},{4,5},{5,4},{6,7},{7,6},{8,9},{9,8},{10,11... | collective-permute-start | bytes 786440 | tf_op jit(solution)/shard_map/ppermute | solution.py:688
  30.4 2.7 %copy-start = (f32[384,4096]{1,0:T(8,128)}, f32[384,4096]{1,0:T(8,128)S(1)}, u32[]{:S(2)}) copy-start(f32[384,4096]{1,0:T(8,128)S(1)} %get-tuple-element.72.refs_1_) | copy-start | bytes 18874372
  33.1 1.7 %copy-start.4 = (bf16[128,12288]{1,0:T(8,128)(2,1)}, bf16[128,12288]{1,0:T(8,128)(2,1)S(1)}, u32[]{:S(2)}) copy-start(bf16[128,12288]{1,0:T(8,128)(2,1)S(1)} %get-tuple-element.73.refs_2_) | copy-start | bytes 9437188
  34.8 1.6 %copy-start.6 = (bf16[128,12288]{1,0:T(8,128)(2,1)}, bf16[128,12288]{1,0:T(8,128)(2,1)S(1)}, u32[]{:S(2)}) copy-start(bf16[128,12288]{1,0:T(8,128)(2,1)S(1)} %get-tuple-element.74.refs_3_) | copy-start | bytes 9437188
  36.4 0.8 copy-start.12
  37.2 2.0 %collective-permute-start.4 = (bf16[2,128,512]{2,1,0:T(8,128)(2,1)}, bf16[2,128,512]{2,1,0:T(8,128)(2,1)}, u32[]{:S(2)}, u32[]{:S(2)}) collective-permute-start(bf16[2,128,512]{2,1,0:T(8,128)(2,1)} %get-tuple-element.77), channel_id=1, source_target_pairs={{0,1},{1,0},{2,3},{3,2},{4,5},{5,4},{6,7},{7,6},{8,9},{9,8},{10,11... | collective-permute-start | bytes 786440 | tf_op jit(solution)/shard_map/ppermute | solution.py:688
  37.3 22.0 %collective-permute-start.8 = (bf16[2,128,384]{2,1,0:T(8,128)(2,1)}, bf16[2,128,384]{2,1,0:T(8,128)(2,1)S(1)}, u32[]{:S(2)}, u32[]{:S(2)}) collective-permute-start(bf16[2,128,384]{2,1,0:T(8,128)(2,1)} %copy-done.20), channel_id=1, source_target_pairs={{0,1},{1,0},{2,3},{3,2},{4,5},{5,4},{6,7},{7,6},{8,9},{9,8},{10,11... | collective-permute-start | bytes 589832 | tf_op jit(solution)/shard_map/ppermute | solution.py:688
  37.7 21.6 %collective-permute-start.7 = (bf16[256,384]{1,0:T(8,128)(2,1)}, bf16[256,384]{1,0:T(8,128)(2,1)S(1)}, u32[]{:S(2)}, u32[]{:S(2)}) collective-permute-start(bf16[256,384]{1,0:T(8,128)(2,1)} %copy-done.10), channel_id=1, source_target_pairs={{0,2},{2,0},{1,3},{3,1},{4,6},{6,4},{5,7},{7,5},{8,10},{10,8},{9,1... | collective-permute-start | bytes 589832 | tf_op jit(solution)/shard_map/ppermute | solution.py:688
  39.2 1.0 %copy-start.13 = (f32[2,128,512]{2,1,0:T(8,128)S(1)}, f32[2,128,512]{2,1,0:T(8,128)}, u32[]{:S(2)}) copy-start(f32[2,128,512]{2,1,0:T(8,128)} %copy-done.12) | copy-start | bytes 1572868
  41.3 21.8 %collective-permute-start.5 = (bf16[128,512]{1,0:T(8,128)(2,1)S(1)}, bf16[128,512]{1,0:T(8,128)(2,1)S(1)}, u32[]{:S(2)}, u32[]{:S(2)}) collective-permute-start(bf16[128,512]{1,0:T(8,128)(2,1)S(1)} %get-tuple-element.78.refs_13_), channel_id=1, source_target_pairs={{0,8},{4,12},{8,0},{12,4},{1,9},{5,13},{9,1},{13,5},{2,10},{6,14},... | collective-permute-start | bytes 393224 | tf_op jit(solution)/shard_map/ppermute | solution.py:688
  41.4 21.8 %collective-permute-start.6 = (bf16[128,512]{1,0:T(8,128)(2,1)S(1)}, bf16[128,512]{1,0:T(8,128)(2,1)S(1)}, u32[]{:S(2)}, u32[]{:S(2)}) collective-permute-start(bf16[128,512]{1,0:T(8,128)(2,1)S(1)} %get-tuple-element.83), channel_id=1, source_target_pairs={{0,4},{4,0},{8,12},{12,8},{1,5},{5,1},{9,13},{13,9},{2,6},{6,2},{1... | collective-permute-start | bytes 393224 | tf_op jit(solution)/shard_map/ppermute | solution.py:688
  44.5 2.8 %copy-start.1 = (f32[384,4096]{1,0:T(8,128)S(1)}, f32[384,4096]{1,0:T(8,128)}, u32[]{:S(2)}) copy-start(f32[384,4096]{1,0:T(8,128)} %copy-done) | copy-start | bytes 18874372
  47.3 1.9 %copy-start.3 = (bf16[384,4096]{1,0:T(8,128)(2,1)S(1)}, bf16[384,4096]{1,0:T(8,128)(2,1)}, u32[]{:S(2)}) copy-start(bf16[384,4096]{1,0:T(8,128)(2,1)} %copy-done.2) | copy-start | bytes 9437188
  49.2 1.9 %copy-start.5 = (bf16[128,12288]{1,0:T(8,128)(2,1)S(1)}, bf16[128,12288]{1,0:T(8,128)(2,1)}, u32[]{:S(2)}) copy-start(bf16[128,12288]{1,0:T(8,128)(2,1)} %copy-done.4) | copy-start | bytes 9437188
  51.1 1.9 %copy-start.7 = (bf16[128,12288]{1,0:T(8,128)(2,1)S(1)}, bf16[128,12288]{1,0:T(8,128)(2,1)}, u32[]{:S(2)}) copy-start(bf16[128,12288]{1,0:T(8,128)(2,1)} %copy-done.6) | copy-start | bytes 9437188
  53.0 0.9 %copy-start.9 = (bf16[2,128,512]{2,1,0:T(8,128)(2,1)S(1)}, bf16[2,128,512]{2,1,0:T(8,128)(2,1)}, u32[]{:S(2)}) copy-start(bf16[2,128,512]{2,1,0:T(8,128)(2,1)} %copy-done.8) | copy-start | bytes 786436
  54.0 1.0 %copy-start.17 = (bf16[384,512]{1,0:T(8,128)(2,1)S(1)}, bf16[384,512]{1,0:T(8,128)(2,1)}, u32[]{:S(2)}) copy-start(bf16[384,512]{1,0:T(8,128)(2,1)} %copy-done.16) | copy-start | bytes 1179652
  54.9 1.0 %copy-start.19 = (bf16[384,512]{1,0:T(8,128)(2,1)S(1)}, bf16[384,512]{1,0:T(8,128)(2,1)}, u32[]{:S(2)}) copy-start(bf16[384,512]{1,0:T(8,128)(2,1)} %copy-done.18) | copy-start | bytes 1179652
  55.9 3.4 %copy-start.11 = (bf16[256,384]{1,0:T(8,128)(2,1)S(1)}, bf16[256,384]{1,0:T(8,128)(2,1)}, u32[]{:S(2)}) copy-start(bf16[256,384]{1,0:T(8,128)(2,1)} %copy-done.10) | copy-start | bytes 589828
  63.1 4.5 %copy-start.22 = (bf16[256,384]{1,0:T(8,128)(2,1)S(1)}, bf16[256,384]{1,0:T(8,128)(2,1)}, u32[]{:S(2)}) copy-start(bf16[256,384]{1,0:T(8,128)(2,1)} %copy-done.21) | copy-start | bytes 589828
  63.2 9.2 %collective-permute-start.9 = (bf16[128,512]{1,0:T(8,128)(2,1)S(1)}, bf16[128,512]{1,0:T(8,128)(2,1)S(1)}, u32[]{:S(2)}, u32[]{:S(2)}) collective-permute-start(bf16[128,512]{1,0:T(8,128)(2,1)S(1)} %get-tuple-element.87.refs_10_), channel_id=1, source_target_pairs={{0,4},{4,0},{8,12},{12,8},{1,5},{5,1},{9,13},{13,9},{2,6},{6,2},{1... | collective-permute-start | bytes 393224 | tf_op jit(solution)/shard_map/ppermute | solution.py:688
  63.3 4.3 %collective-permute-start.10 = (bf16[256,128]{1,0:T(8,128)(2,1)S(1)}, bf16[256,128]{1,0:T(8,128)(2,1)S(1)}, u32[]{:S(2)}, u32[]{:S(2)}) collective-permute-start(bf16[256,128]{1,0:T(8,128)(2,1)S(1)} %get-tuple-element.85.refs_3_.refs_8_), channel_id=1, source_target_pairs={{0,2},{2,0},{1,3},{3,1},{4,6},{6,4},{5,7},{7,5},{8,10},{10,8},{9,1... | collective-permute-start | bytes 196616 | tf_op jit(solution)/shard_map/ppermute | solution.py:688
  67.6 6.3 %copy-start.15 = (f32[2,128,384]{2,1,0:T(8,128)S(1)}, f32[2,128,384]{2,1,0:T(8,128)}, u32[]{:S(2)}) copy-start(f32[2,128,384]{2,1,0:T(8,128)} %copy-done.14) | copy-start | bytes 1179652
  72.4 1.5 %collective-permute-start.11 = (bf16[128,768]{1,0:T(8,128)(2,1)S(1)}, bf16[128,768]{1,0:T(8,128)(2,1)S(1)}, u32[]{:S(2)}, u32[]{:S(2)}) collective-permute-start(bf16[128,768]{1,0:T(8,128)(2,1)S(1)} %shard_map.132.refs_3_), channel_id=1, source_target_pairs={{0,1},{1,0},{2,3},{3,2},{4,5},{5,4},{6,7},{7,6},{8,9},{9,8},{10,11... | collective-permute-start | bytes 589832 | tf_op jit(solution)/shard_map/ppermute | solution.py:688
  74.0 5.6 %collective-permute-start.12 = (bf16[128,512]{1,0:T(8,128)(2,1)S(1)}, bf16[128,512]{1,0:T(8,128)(2,1)S(1)}, u32[]{:S(2)}, u32[]{:S(2)}) collective-permute-start(bf16[128,512]{1,0:T(8,128)(2,1)S(1)} %get-tuple-element.92.refs_2_.refs_5_), channel_id=1, source_target_pairs={{0,2},{2,0},{1,3},{3,1},{4,6},{6,4},{5,7},{7,5},{8,10},{10,8},{9,1... | collective-permute-start | bytes 393224 | tf_op jit(solution)/shard_map/ppermute | solution.py:688

commit v10 on v8

--- a/solution.py
+++ b/solution.py
@@ -32,10 +32,10 @@
 
 
 FACTS = 16
-N0, N1, N2, OWNS2, LIMIT, LEADS, ROOT_IN_CHIP, ROOT_IN_PAIR, NEXT_IN_CHIP = range(9)
-
-
-def write_facts(facts, ids, counts):
+N0, N1, N2, OWNS2, LIMIT, LEADS, ROOT_IN_CHIP, ROOT_IN_PAIR, NEXT_IN_CHIP, SIDE = range(10)
+
+
+def write_facts(facts, ids, counts, side):
     page = [ids[0, j] for j in range(INNER + 1)]
     own = page[INNER] - 1
     leaf = own // SLOTS
@@ -51,7 +51,8 @@
     facts[ROOT_IN_CHIP] = number(same(0, 1))
     facts[ROOT_IN_PAIR] = number(same(0, 2))
     facts[NEXT_IN_CHIP] = number(same(1, 1))
-    for i in range(NEXT_IN_CHIP + 1, FACTS):
+    facts[SIDE] = side
+    for i in range(SIDE + 1, FACTS):
         facts[i] = 0
 
 
@@ -86,10 +87,10 @@
     )(pltpu.with_memory_space_constraint(facts, pltpu.SMEM), *near, *far, *after)
 
 
-def start(ids, counts, keys, values):
+def start(side, ids, counts, keys, values):
     width = keys.shape[1]
 
-    def body(ids_ref, counts_ref, k_ref, v_ref, facts, out, held, ids_s, counts_s, sem):
+    def body(side_ref, ids_ref, counts_ref, k_ref, v_ref, facts, out, held, ids_s, counts_s, sem):
         copies = [
             pltpu.make_async_copy(src, dst, sem.at[i])
             for i, (src, dst) in enumerate(
@@ -105,7 +106,7 @@
             c.start()
         copies[0].wait()
         copies[1].wait()
-        write_facts(facts, ids_s, counts_s)
+        write_facts(facts, ids_s, counts_s, side_ref[0])
         ok = row_ok(counts_s[0, 0], PAGE, width)
         for i in range(2):
             copies[2 + i].wait()
@@ -116,7 +117,7 @@
     return pl.pallas_call(
         body,
         out_shape=(pltpu.SMEM((FACTS,), I32), pltpu.VMEM((2, PAGE, width), BF16)),
-        in_specs=[hbm] * 4,
+        in_specs=[smem] + [hbm] * 4,
         out_specs=(smem, pl.BlockSpec(memory_space=pltpu.VMEM)),
         scratch_shapes=[
             pltpu.VMEM((2, PAGE, width), BF16),
@@ -125,7 +126,7 @@
             pltpu.SemaphoreType.DMA((4,)),
         ],
         compiler_params=pltpu.CompilerParams(vmem_limit_bytes=SMALL),
-    )(ids, counts, keys, values)
+    )(side, ids, counts, keys, values)
 
 
 def row_terms(rows):
@@ -499,7 +500,7 @@
     return [slice(i, i + tile) for i in range(0, w.shape[0], tile)]
 
 
-def input_grad(facts, side, w, rows, own, far, grads, carry=None):
+def input_grad(facts, w, rows, own, far, grads, carry=None):
     out_cols, depth = w.shape
     tiles = width_tiles(w)
     top = 0 if rows == PAGE else PAGE
@@ -509,7 +510,7 @@
     count = len(grads[0])
     carry = list(carry or [])
 
-    def body(facts, flag, *refs):
+    def body(facts, *refs):
         own_r, refs = refs[: len(own)], refs[len(own) :]
         far_r, refs = refs[: len(far)], refs[len(far) :]
         grad_r, w_ref = refs[: 2 * count], refs[2 * count]
@@ -524,7 +525,7 @@
         columns = lambda rs: jnp.concatenate([r[...] for r in rs], axis=1)
         full = columns(own_r)
         if far:
-            other, leads = columns(far_r), flag[0] == 0
+            other, leads = columns(far_r), facts[SIDE] == 0
             full = jnp.concatenate(
                 [jnp.where(leads, full, other), jnp.where(leads, other, full)], axis=1
             )
@@ -549,7 +550,7 @@
         out_shape=(
             jax.ShapeDtypeStruct((ROWS, out_cols), BF16), kept, kept, pltpu.VMEM((8, HD), F32)
         ),
-        in_specs=[smem] * 2 + [vmem] * len(arrays) + [hbm] * (1 + len(carry)),
+        in_specs=[smem] + [vmem] * len(arrays) + [hbm] * (1 + len(carry)),
         out_specs=(hbm, hbm, hbm, vmem),
         scratch_shapes=[
             pltpu.VMEM(w.shape, BF16),
@@ -557,10 +558,10 @@
             pltpu.SemaphoreType.DMA((steps,)),
             pltpu.SemaphoreType.DMA((steps + 2 * count,)),
         ],
-        input_output_aliases={3 + len(arrays) + i: i for i in range(len(carry))},
+        input_output_aliases={2 + len(arrays) + i: i for i in range(len(carry))},
         compiler_params=pltpu.CompilerParams(vmem_limit_bytes=LARGE),
         cost_estimate=SLIGHT,
-    )(pltpu.with_memory_space_constraint(facts, pltpu.SMEM), side, *arrays, w, *carry)
+    )(pltpu.with_memory_space_constraint(facts, pltpu.SMEM), *arrays, w, *carry)
 
 
 def put_rows(pieces, dk, dv, top, rows, sem, first):
@@ -576,15 +577,15 @@
     return copies
 
 
-def begin_input_grad(facts, side, w, own, after=()):
+def begin_input_grad(facts, w, own, after=()):
     out_cols, depth = w.shape
     half = depth // 2
     rows = own[0].shape[0]
     count = len(own)
 
-    def body(facts, flag, w_ref, *refs):
+    def body(facts, w_ref, *refs):
         mine, out = jnp.concatenate([r[...] for r in refs[:count]], axis=1), refs[-1]
-        where = pl.ds(pl.multiple_of(flag[0] * half, half), half)
+        where = pl.ds(pl.multiple_of(facts[SIDE] * half, half), half)
         for at in width_tiles(w):
             out[at] = dot_t(w_ref[at, where], mine)
 
@@ -593,19 +594,19 @@
     near = [pltpu.with_memory_space_constraint(a, pltpu.VMEM) for a in (w, *own)]
 
     def kernel(*refs):
-        body(*refs[: 3 + count], refs[-1])
+        body(*refs[: 2 + count], refs[-1])
 
     return pl.pallas_call(
         kernel,
         out_shape=pltpu.VMEM((out_cols, rows), F32),
-        in_specs=[smem, smem] + [vmem] * len(near) + [pl.BlockSpec(memory_space=pl.ANY)] * len(after),
+        in_specs=[smem] + [vmem] * len(near) + [pl.BlockSpec(memory_space=pl.ANY)] * len(after),
         out_specs=vmem,
         compiler_params=pltpu.CompilerParams(vmem_limit_bytes=LARGE),
         cost_estimate=SLIGHT,
-    )(pltpu.with_memory_space_constraint(facts, pltpu.SMEM), side, *near, *after)
-
-
-def end_input_grad(facts, side, w, far, begun, grads, carry=None, after=()):
+    )(pltpu.with_memory_space_constraint(facts, pltpu.SMEM), *near, *after)
+
+
+def end_input_grad(facts, w, far, begun, grads, carry=None, after=()):
     tiles = width_tiles(w)
     out_cols, depth = w.shape
     half = depth // 2
@@ -616,13 +617,13 @@
     near = [w, begun, *far, *grads[0], *grads[1]]
     carry = list(carry or [])
 
-    def body(facts, flag, w_r, begun_r, *refs):
+    def body(facts, w_r, begun_r, *refs):
         far_r, grad_r = refs[: len(far)], refs[len(far) : len(near) - 2]
         out, dk, dv, made, stage, sem = refs[-6:]
         made[...] = jnp.zeros_like(made)
         copies = put_rows(grad_r, dk, dv, top, rows, sem, steps)
         other = jnp.concatenate([r[...] for r in far_r], axis=1)
-        where = pl.ds(pl.multiple_of((1 - flag[0]) * half, half), half)
+        where = pl.ds(pl.multiple_of((1 - facts[SIDE]) * half, half), half)
         for i, at in enumerate(tiles):
             stage[i] = (dot_t(w_r[at, where], other) + begun_r[at]).astype(BF16).T
             copies.append(
@@ -639,23 +640,23 @@
     kept = jax.ShapeDtypeStruct((ROWS, width), BF16)
 
     def kernel(*refs):
-        body(*refs[: 2 + len(near)], *refs[2 + len(near) + len(carry) + len(after) :])
+        body(*refs[: 1 + len(near)], *refs[1 + len(near) + len(carry) + len(after) :])
 
     return pl.pallas_call(
         kernel,
         out_shape=(
             jax.ShapeDtypeStruct((ROWS, out_cols), BF16), kept, kept, pltpu.VMEM((8, HD), F32)
         ),
-        in_specs=[smem, smem] + [vmem] * len(near) + [hbm] * (len(carry) + len(after)),
+        in_specs=[smem] + [vmem] * len(near) + [hbm] * (len(carry) + len(after)),
         out_specs=(hbm, hbm, hbm, vmem),
         scratch_shapes=[
             pltpu.VMEM((steps, rows, out_cols // steps), BF16),
             pltpu.SemaphoreType.DMA((steps + 2 * len(grads[0]),)),
         ],
-        input_output_aliases={2 + len(near) + i: i for i in range(len(carry))},
+        input_output_aliases={1 + len(near) + i: i for i in range(len(carry))},
         compiler_params=pltpu.CompilerParams(vmem_limit_bytes=LARGE),
         cost_estimate=SLIGHT,
-    )(pltpu.with_memory_space_constraint(facts, pltpu.SMEM), side, *near, *carry, *after)
+    )(pltpu.with_memory_space_constraint(facts, pltpu.SMEM), *near, *carry, *after)
 
 
 def flipped(block, axis, bit):
@@ -806,7 +807,7 @@
     side = lax.axis_index("tensor").astype(I32).reshape(1)
     two_sides = lax.axis_size("tensor") == 2
     inputs = [hbm(a) for a in (queries, grad_out, keys, values, log_norms, row_deltas)]
-    facts, own = start(hbm(ancestors), hbm(counts), *inputs[2:4])
+    facts, own = start(side, hbm(ancestors), hbm(counts), *inputs[2:4])
     state = {}
 
     def own_pages(kvs, pages, prior=(), after=(), w=None):
@@ -842,15 +843,15 @@
         total, root, root_far, next_far = over_cores(facts, kept, sent)
         *last, w_near = own_pages(kvs[-1:], level2, after=(root,), w=w)
         both = list(zip(most, last))
-        begun = begin_input_grad(facts, side, w_near, both[1], (far_v[0], level2_far))
+        begun = begin_input_grad(facts, w_near, both[1], (far_v[0], level2_far))
         far_v.append(spread(last[1]))
         total, low, far = over_halves(facts, total, root_far, next_far, (begun,))
-        *grads, made = end_input_grad(facts, side, w_near, far_v, begun, both[:2], after=(low,))
+        *grads, made = end_input_grad(facts, w_near, far_v, begun, both[:2], after=(low,))
         mine, far = over_chips(facts, total, far, last[3], (made,))
         dk0, dv0 = finish_small_tree(facts, both[2], mine, far, level2_far)
         far_v = spread(dv0)
-        begun = begin_input_grad(facts, side, w_near, [dv0])
-        grads = end_input_grad(facts, side, w_near, [far_v], begun, ([dk0], [dv0]), grads)
+        begun = begin_input_grad(facts, w_near, [dv0])
+        grads = end_input_grad(facts, w_near, [far_v], begun, ([dk0], [dv0]), grads)
         return (state["gq"], grads[1], grads[2], grads[0])
 
     first = lax.axis_index("sub") == 0
@@ -876,8 +877,8 @@
         pair = lambda part: ([part], [spread(part)])
     else:
         pair = lambda part: ([spread(part)], [])
-    *grads, _ = input_grad(facts, side, w, 2 * PAGE, *pair(dv12), ([dk12], [dv12]))
-    grads = input_grad(facts, side, w, PAGE, *pair(dv0), ([dk0], [dv0]), grads)
+    *grads, _ = input_grad(facts, w, 2 * PAGE, *pair(dv12), ([dk12], [dv12]))
+    grads = input_grad(facts, w, PAGE, *pair(dv0), ([dk0], [dv0]), grads)
     return (state["gq"], grads[1], grads[2], grads[0])
 
 

time: 67.1 us -> 57.2 us (0.85)
  local copies, waits for them, and re-layouts: 9.78 us -> 0 us
  starting transfers between devices: 13.8 us -> 14.5 us
    unnamed x24 -> x0, local copies, waits for them, and re-layouts: 9.78 us -> none
  transfers between devices with their start and end apart: 13 -> 13, of which waited for: 6 -> 7; matrix products, arithmetic and copies ran while one was open for 0% -> 0% of each run, Pallas kernels for 27% -> 31%
where the time goes in v10:
time: 57.2 us; the launch traced here: 57 us
  Pallas kernels  29.5 us (52%)
  starting transfers between devices  14.5 us (25%)
  waiting for transfers between devices  12.1 us (21%)
  between operations  0.97 us (2%)
    pallas_call x11, Pallas kernels, kernel_call(): pl.pallas_call(kernel, out_shape=tuple((pltpu.VMEM(s, d) if inside else j...  22.6 us
    ppermute x13, starting transfers between devices, flipped(): lax.ppermute(block, axis, [(i, i ^ bit) for i in range(count) if i ^ bit...  14.5 us
    ppermute x13, waiting for transfers between devices, flipped(): lax.ppermute(block, axis, [(i, i ^ bit) for i in range(count) if i ^ bit...  12.1 us
    pallas_call x2, Pallas kernels, end_input_grad(): pl.pallas_call(kernel, out_shape=(jax.ShapeDtypeStruct((ROWS, out_cols),...  4.2 us
    pallas_call x2, Pallas kernels, begin_input_grad(): pl.pallas_call(kernel, out_shape=pltpu.VMEM((out_cols, rows), F32), in_sp...  1.71 us
  transfers between devices with their start and end apart: 13, of which 7 were waited for; matrix products, arithmetic and copies ran while one was open for 0% of the time, Pallas kernels for 31%

profile of v10, /device:TPU:0, one launch (start us, length us, event | category | flops | bytes accessed | tf_op | source)
XLA Modules:
  0.0 57.0 jit_solution(1983704684990810491)
XLA Ops:
  0.6 1.0 %shard_map.120 = (s32[16]{0:T(128)S(4)}, bf16[2,128,512]{2,1,0:T(8,128)(2,1)S(1)}) custom-call(s32[1]{0:T(128)} %bitcast.side_ref, s32[1,5]{1,0:T(1,128)} %ids_ref.1, s32[1,3]{1,0:T(1,128)} %counts_ref.1, bf16[384,512]{1,0:T(8,128)(2,1)} %refs_5_.1, bf16[384,512]{1,0:T(8,128)(2,1)} %refs_6_.1), custom_call_target="tpu_custom_call" | custom-call | tf_op jit(solution)/shard_map/pallas_call | solution.py:117
  1.7 0.5 collective-permute-start
  2.2 1.2 %collective-permute-done.refs_2_.refs_10_.refs_11_ = bf16[2,128,512]{2,1,0:T(8,128)(2,1)S(1)} collective-permute-done((bf16[2,128,512]{2,1,0:T(8,128)(2,1)S(1)}, bf16[2,128,512]{2,1,0:T(8,128)(2,1)S(1)}, u32[]{:S(2)}, u32[]{:S(2)}) %collective-permute-start) | collective-permute-done | bytes 262176 | tf_op jit(solution)/shard_map/ppermute | solution.py:664
  3.4 3.0 %collective-permute-start.1 = (bf16[128,512]{1,0:T(8,128)(2,1)S(1)}, bf16[128,512]{1,0:T(8,128)(2,1)S(1)}, u32[]{:S(2)}, u32[]{:S(2)}) collective-permute-start(bf16[128,512]{1,0:T(8,128)(2,1)S(1)} %shard_map.121.refs_9_.refs_1_), channel_id=1, source_target_pairs={{0,4},{4,0},{8,12},{12,8},{1,5},{5,1},{9,13},{13,9},{2,6},{6,2},{1... | collective-permute-start | bytes 393224 | tf_op jit(solution)/shard_map/ppermute | solution.py:664
  6.4 4.3 %shard_map.122 = (f32[384,1024]{1,0:T(8,128)S(1)}, bf16[128,3072]{1,0:T(8,128)(2,1)S(1)}, bf16[128,3072]{1,0:T(8,128)(2,1)S(1)}, bf16[256,128]{1,0:T(8,128)(2,1)...) custom-call(s32[16]{0:T(128)S(4)} %get-tuple-element.61.refs_0_, ...), custom_call_target="tpu_custom_call" | custom-call | flops 4026531840 | bytes 1000 | tf_op jit(solution)/shard_map/pallas_call | solution.py:76
  10.7 0.0 collective-permute-done.1.refs_2_
  10.7 2.6 %collective-permute-start.2 = (bf16[128,512]{1,0:T(8,128)(2,1)S(1)}, bf16[128,512]{1,0:T(8,128)(2,1)S(1)}, u32[]{:S(2)}, u32[]{:S(2)}) collective-permute-start(bf16[128,512]{1,0:T(8,128)(2,1)S(1)} %shard_map.123.refs_15_.refs_3_), channel_id=1, source_target_pairs={{0,8},{4,12},{8,0},{12,4},{1,9},{5,13},{9,1},{13,5},{2,10},{6,14},... | collective-permute-start | bytes 393224 | tf_op jit(solution)/shard_map/ppermute | solution.py:664
  13.4 4.9 %shard_map.124 = (f32[384,1024]{1,0:T(8,128)S(1)}, bf16[128,3072]{1,0:T(8,128)(2,1)S(1)}, bf16[128,3072]{1,0:T(8,128)(2,1)S(1)}, f32[384,1024]{1,0:T(8,128)S(1)}...) custom-call(s32[16]{0:T(128)S(4)} %get-tuple-element.61.refs_0_, ...), custom_call_target="tpu_custom_call" | custom-call | flops 8053063680 | bytes 1000 | tf_op jit(solution)/shard_map/pallas_call | solution.py:76
  18.3 1.5 %collective-permute-done.2.refs_4_ = bf16[128,512]{1,0:T(8,128)(2,1)S(1)} collective-permute-done((bf16[128,512]{1,0:T(8,128)(2,1)S(1)}, bf16[128,512]{1,0:T(8,128)(2,1)S(1)}, u32[]{:S(2)}, u32[]{:S(2)}) %collective-permute-start.2) | collective-permute-done | bytes 131104 | tf_op jit(solution)/shard_map/ppermute | solution.py:664
  19.8 0.1 collective-permute-start.3
  19.8 1.5 %collective-permute-done.3.refs_23_ = bf16[2,128,512]{2,1,0:T(8,128)(2,1)S(1)} collective-permute-done((bf16[2,128,512]{2,1,0:T(8,128)(2,1)S(1)}, bf16[2,128,512]{2,1,0:T(8,128)(2,1)S(1)}, u32[]{:S(2)}, u32[]{:S(2)}) %collective-permute-start.3) | collective-permute-done | bytes 262176 | tf_op jit(solution)/shard_map/ppermute | solution.py:664
  21.4 8.2 %shard_map.126 = (f32[384,1024]{1,0:T(8,128)S(1)}, bf16[128,3072]{1,0:T(8,128)(2,1)S(1)}, bf16[128,3072]{1,0:T(8,128)(2,1)S(1)}, bf16[384,4096]{1,0:T(8,128)(2,1...) custom-call(s32[16]{0:T(128)S(4)} %get-tuple-element.61.refs_0_, ...), custom_call_target="tpu_custom_call" | custom-call | flops 16106127360 | bytes 1000 | tf_op jit(solution)/shard_map/pallas_call | solution.py:76
  29.6 0.2 collective-permute-start.4
  29.8 0.4 collective-permute-start.8
  30.1 1.5 %collective-permute-start.7 = (bf16[256,384]{1,0:T(8,128)(2,1)S(1)}, bf16[256,384]{1,0:T(8,128)(2,1)S(1)}, u32[]{:S(2)}, u32[]{:S(2)}) collective-permute-start(bf16[256,384]{1,0:T(8,128)(2,1)S(1)} %get-tuple-element.102.refs_2_.refs_7_), channel_id=1, source_target_pairs={{0,2},{2,0},{1,3},{3,1},{4,6},{6,4},{5,7},{7,5},{8,10},{10,8},{9,1... | collective-permute-start | bytes 589832 | tf_op jit(solution)/shard_map/ppermute | solution.py:664
  31.6 0.0 collective-permute-done.4.refs_2_
  31.6 0.1 shard_map.127
  31.7 0.1 collective-permute-start.5
  31.8 3.2 %collective-permute-start.6 = (bf16[128,512]{1,0:T(8,128)(2,1)S(1)}, bf16[128,512]{1,0:T(8,128)(2,1)S(1)}, u32[]{:S(2)}, u32[]{:S(2)}) collective-permute-start(bf16[128,512]{1,0:T(8,128)(2,1)S(1)} %get-tuple-element.101), channel_id=1, source_target_pairs={{0,4},{4,0},{8,12},{12,8},{1,5},{5,1},{9,13},{13,9},{2,6},{6,2},{1... | collective-permute-start | bytes 393224 | tf_op jit(solution)/shard_map/ppermute | solution.py:664
  35.0 4.9 %shard_map.128 = (bf16[384,4096]{1,0:T(8,128)(2,1)}, bf16[256,128]{1,0:T(8,128)(2,1)S(1)}, bf16[256,128]{1,0:T(8,128)(2,1)S(1)}, f32[2,128,128]{2,1,0:T(8,128)S(...) custom-call(s32[16]{0:T(128)S(4)} %get-tuple-element.61.refs_0_, ...), custom_call_target="tpu_custom_call", output_to_operand_aliasing={{0}: (12, {})} | custom-call | flops 4026531840 | bytes 1000 | tf_op jit(solution)/shard_map/pallas_call | solution.py:76
  39.9 0.0 collective-permute-done.7.refs_4_.refs_3_
  39.9 0.0 collective-permute-done.8.refs_5_
  39.9 0.9 %shard_map.129.refs_4_.refs_2_ = f32[2560,256]{1,0:T(8,128)S(1)} custom-call(s32[16]{0:T(128)S(4)} %get-tuple-element.61.refs_0_, bf16[2560,1024]{1,0:T(8,128)(2,1)S(1)} %get-tuple-element.97.refs_1_, bf16[256,384]{1,0:T(8,128)(2,1)S(1)} %get-tuple-element.102.refs_2_.refs_7_, bf16[256,128]{1,0:T(8,128)(2,1)S(1)} %get-tuple-element.103.refs_3_.refs_8_, ...), custom_call_target="tpu_custom_call" | custom-call | flops 1000 | bytes 1000 | tf_op jit(solution)/shard_map/pallas_call | solution.py:599
  40.8 0.0 collective-permute-done.5.refs_2_
  40.8 0.1 collective-permute-done.6.refs_3_
  40.9 0.1 shard_map.130
  41.0 0.1 collective-permute-start.9
  41.0 1.4 %collective-permute-start.10 = (bf16[256,128]{1,0:T(8,128)(2,1)S(1)}, bf16[256,128]{1,0:T(8,128)(2,1)S(1)}, u32[]{:S(2)}, u32[]{:S(2)}) collective-permute-start(bf16[256,128]{1,0:T(8,128)(2,1)S(1)} %get-tuple-element.103.refs_3_.refs_8_), channel_id=1, source_target_pairs={{0,2},{2,0},{1,3},{3,1},{4,6},{6,4},{5,7},{7,5},{8,10},{10,8},{9,1... | collective-permute-start | bytes 196616 | tf_op jit(solution)/shard_map/ppermute | solution.py:664
  42.4 3.0 %collective-permute-done.10.refs_4_ = bf16[256,128]{1,0:T(8,128)(2,1)S(1)} collective-permute-done((bf16[256,128]{1,0:T(8,128)(2,1)S(1)}, bf16[256,128]{1,0:T(8,128)(2,1)S(1)}, u32[]{:S(2)}, u32[]{:S(2)}) %collective-permute-start.10) | collective-permute-done | bytes 65568 | tf_op jit(solution)/shard_map/ppermute | solution.py:664
  45.4 1.9 %shard_map.131 = (bf16[384,2560]{1,0:T(8,128)(2,1)}, bf16[384,512]{1,0:T(8,128)(2,1)}, bf16[384,512]{1,0:T(8,128)(2,1)}, f32[8,128]{1,0:T(8,128)S(1)}) custom-call(s32[16]{0:T(128)S(4)} %get-tuple-element.61.refs_0_, bf16[2560,1024]{1,0:T(8,128)(2,1)S(1)} %get-tuple-element.97.refs_1_, f32[2560,256]{1,0:T(8,128)S(1)} %shard_map.129.refs_4_.refs_2_, ...), custom_call_target="tpu_custom_call" | custom-call | flops 1000 | bytes 1000 | tf_op jit(solution)/shard_map/pallas_call | solution.py:645
  47.3 0.0 collective-permute-done.9.refs_2_
  47.4 0.1 collective-permute-start.11
  47.5 1.4 %collective-permute-done.11.refs_4_ = bf16[128,768]{1,0:T(8,128)(2,1)S(1)} collective-permute-done((bf16[128,768]{1,0:T(8,128)(2,1)S(1)}, bf16[128,768]{1,0:T(8,128)(2,1)S(1)}, u32[]{:S(2)}, u32[]{:S(2)}) %collective-permute-start.11) | collective-permute-done | bytes 196640 | tf_op jit(solution)/shard_map/ppermute | solution.py:664
  48.9 0.1 shard_map.133
  49.0 1.4 %collective-permute-start.12 = (bf16[128,512]{1,0:T(8,128)(2,1)S(1)}, bf16[128,512]{1,0:T(8,128)(2,1)S(1)}, u32[]{:S(2)}, u32[]{:S(2)}) collective-permute-start(bf16[128,512]{1,0:T(8,128)(2,1)S(1)} %get-tuple-element.110.refs_2_.refs_5_), channel_id=1, source_target_pairs={{0,2},{2,0},{1,3},{3,1},{4,6},{6,4},{5,7},{7,5},{8,10},{10,8},{9,1... | collective-permute-start | bytes 393224 | tf_op jit(solution)/shard_map/ppermute | solution.py:664
  50.4 0.8 %shard_map.134.refs_2_ = f32[2560,128]{1,0:T(8,128)S(1)} custom-call(s32[16]{0:T(128)S(4)} %get-tuple-element.61.refs_0_, bf16[2560,1024]{1,0:T(8,128)(2,1)S(1)} %get-tuple-element.97.refs_1_, bf16[128,512]{1,0:T(8,128)(2,1)S(1)} %get-tuple-element.110.refs_2_.refs_5_), custom_call_target="tpu_custom_call" | custom-call | flops 1000 | bytes 1000 | tf_op jit(solution)/shard_map/pallas_call | solution.py:599
  51.2 3.4 %collective-permute-done.12.refs_3_ = bf16[128,512]{1,0:T(8,128)(2,1)S(1)} collective-permute-done((bf16[128,512]{1,0:T(8,128)(2,1)S(1)}, bf16[128,512]{1,0:T(8,128)(2,1)S(1)}, u32[]{:S(2)}, u32[]{:S(2)}) %collective-permute-start.12) | collective-permute-done | bytes 131104 | tf_op jit(solution)/shard_map/ppermute | solution.py:664
  54.6 2.3 %shard_map.135 = (bf16[384,2560]{1,0:T(8,128)(2,1)}, bf16[384,512]{1,0:T(8,128)(2,1)}, bf16[384,512]{1,0:T(8,128)(2,1)}, f32[8,128]{1,0:T(8,128)}) custom-call(s32[16]{0:T(128)S(4)} %get-tuple-element.61.refs_0_, bf16[2560,1024]{1,0:T(8,128)(2,1)S(1)} %get-tuple-element.97.refs_1_, ...), custom_call_target="tpu_custom_call", output_to_operand_aliasing={{0}: (6, {}), {1}: (7, {}), {2}: (8, {})} | custom-call | flops 1000 | bytes 1000 | tf_op jit(solution)/shard_map/pallas_call | solution.py:645
  (4 shorter events, 0.1 us)
Async XLA Ops:
  1.7 1.7 %collective-permute-start = (bf16[2,128,512]{2,1,0:T(8,128)(2,1)S(1)}, bf16[2,128,512]{2,1,0:T(8,128)(2,1)S(1)}, u32[]{:S(2)}, u32[]{:S(2)}) collective-permute-start(bf16[2,128,512]{2,1,0:T(8,128)(2,1)S(1)} %get-tuple-element.62.refs_1_.refs_9_.refs_10_), channel_id=1, source_target_pairs={{0,1},{1,0},{2,3},{3,2},{4,5},{5,4},{6,7},{7,6},{8,9},{9,8},{10,11... | collective-permute-start | bytes 786440 | tf_op jit(solution)/shard_map/ppermute | solution.py:664
  3.4 7.3 %collective-permute-start.1 = (bf16[128,512]{1,0:T(8,128)(2,1)S(1)}, bf16[128,512]{1,0:T(8,128)(2,1)S(1)}, u32[]{:S(2)}, u32[]{:S(2)}) collective-permute-start(bf16[128,512]{1,0:T(8,128)(2,1)S(1)} %shard_map.121.refs_9_.refs_1_), channel_id=1, source_target_pairs={{0,4},{4,0},{8,12},{12,8},{1,5},{5,1},{9,13},{13,9},{2,6},{6,2},{1... | collective-permute-start | bytes 393224 | tf_op jit(solution)/shard_map/ppermute | solution.py:664
  10.7 9.0 %collective-permute-start.2 = (bf16[128,512]{1,0:T(8,128)(2,1)S(1)}, bf16[128,512]{1,0:T(8,128)(2,1)S(1)}, u32[]{:S(2)}, u32[]{:S(2)}) collective-permute-start(bf16[128,512]{1,0:T(8,128)(2,1)S(1)} %shard_map.123.refs_15_.refs_3_), channel_id=1, source_target_pairs={{0,8},{4,12},{8,0},{12,4},{1,9},{5,13},{9,1},{13,5},{2,10},{6,14},... | collective-permute-start | bytes 393224 | tf_op jit(solution)/shard_map/ppermute | solution.py:664
  19.8 1.6 %collective-permute-start.3 = (bf16[2,128,512]{2,1,0:T(8,128)(2,1)S(1)}, bf16[2,128,512]{2,1,0:T(8,128)(2,1)S(1)}, u32[]{:S(2)}, u32[]{:S(2)}) collective-permute-start(bf16[2,128,512]{2,1,0:T(8,128)(2,1)S(1)} %shard_map.125.refs_22_), channel_id=1, source_target_pairs={{0,1},{1,0},{2,3},{3,2},{4,5},{5,4},{6,7},{7,6},{8,9},{9,8},{10,11... | collective-permute-start | bytes 786440 | tf_op jit(solution)/shard_map/ppermute | solution.py:664
  29.6 2.1 %collective-permute-start.4 = (bf16[2,128,512]{2,1,0:T(8,128)(2,1)S(1)}, bf16[2,128,512]{2,1,0:T(8,128)(2,1)S(1)}, u32[]{:S(2)}, u32[]{:S(2)}) collective-permute-start(bf16[2,128,512]{2,1,0:T(8,128)(2,1)S(1)} %get-tuple-element.94), channel_id=1, source_target_pairs={{0,1},{1,0},{2,3},{3,2},{4,5},{5,4},{6,7},{7,6},{8,9},{9,8},{10,11... | collective-permute-start | bytes 786440 | tf_op jit(solution)/shard_map/ppermute | solution.py:664
  29.8 10.2 %collective-permute-start.8 = (bf16[2,128,384]{2,1,0:T(8,128)(2,1)S(1)}, bf16[2,128,384]{2,1,0:T(8,128)(2,1)S(1)}, u32[]{:S(2)}, u32[]{:S(2)}) collective-permute-start(bf16[2,128,384]{2,1,0:T(8,128)(2,1)S(1)} %get-tuple-element.88.refs_5_), channel_id=1, source_target_pairs={{0,1},{1,0},{2,3},{3,2},{4,5},{5,4},{6,7},{7,6},{8,9},{9,8},{10,11... | collective-permute-start | bytes 589832 | tf_op jit(solution)/shard_map/ppermute | solution.py:664
  30.1 9.8 %collective-permute-start.7 = (bf16[256,384]{1,0:T(8,128)(2,1)S(1)}, bf16[256,384]{1,0:T(8,128)(2,1)S(1)}, u32[]{:S(2)}, u32[]{:S(2)}) collective-permute-start(bf16[256,384]{1,0:T(8,128)(2,1)S(1)} %get-tuple-element.102.refs_2_.refs_7_), channel_id=1, source_target_pairs={{0,2},{2,0},{1,3},{3,1},{4,6},{6,4},{5,7},{7,5},{8,10},{10,8},{9,1... | collective-permute-start | bytes 589832 | tf_op jit(solution)/shard_map/ppermute | solution.py:664
  31.7 9.1 %collective-permute-start.5 = (bf16[128,512]{1,0:T(8,128)(2,1)S(1)}, bf16[128,512]{1,0:T(8,128)(2,1)S(1)}, u32[]{:S(2)}, u32[]{:S(2)}) collective-permute-start(bf16[128,512]{1,0:T(8,128)(2,1)S(1)} %get-tuple-element.95.refs_14_), channel_id=1, source_target_pairs={{0,8},{4,12},{8,0},{12,4},{1,9},{5,13},{9,1},{13,5},{2,10},{6,14},... | collective-permute-start | bytes 393224 | tf_op jit(solution)/shard_map/ppermute | solution.py:664
  31.8 9.1 %collective-permute-start.6 = (bf16[128,512]{1,0:T(8,128)(2,1)S(1)}, bf16[128,512]{1,0:T(8,128)(2,1)S(1)}, u32[]{:S(2)}, u32[]{:S(2)}) collective-permute-start(bf16[128,512]{1,0:T(8,128)(2,1)S(1)} %get-tuple-element.101), channel_id=1, source_target_pairs={{0,4},{4,0},{8,12},{12,8},{1,5},{5,1},{9,13},{13,9},{2,6},{6,2},{1... | collective-permute-start | bytes 393224 | tf_op jit(solution)/shard_map/ppermute | solution.py:664
  41.0 6.4 %collective-permute-start.9 = (bf16[128,512]{1,0:T(8,128)(2,1)S(1)}, bf16[128,512]{1,0:T(8,128)(2,1)S(1)}, u32[]{:S(2)}, u32[]{:S(2)}) collective-permute-start(bf16[128,512]{1,0:T(8,128)(2,1)S(1)} %get-tuple-element.105.refs_9_), channel_id=1, source_target_pairs={{0,4},{4,0},{8,12},{12,8},{1,5},{5,1},{9,13},{13,9},{2,6},{6,2},{1... | collective-permute-start | bytes 393224 | tf_op jit(solution)/shard_map/ppermute | solution.py:664
  41.0 4.3 %collective-permute-start.10 = (bf16[256,128]{1,0:T(8,128)(2,1)S(1)}, bf16[256,128]{1,0:T(8,128)(2,1)S(1)}, u32[]{:S(2)}, u32[]{:S(2)}) collective-permute-start(bf16[256,128]{1,0:T(8,128)(2,1)S(1)} %get-tuple-element.103.refs_3_.refs_8_), channel_id=1, source_target_pairs={{0,2},{2,0},{1,3},{3,1},{4,6},{6,4},{5,7},{7,5},{8,10},{10,8},{9,1... | collective-permute-start | bytes 196616 | tf_op jit(solution)/shard_map/ppermute | solution.py:664
  47.4 1.5 %collective-permute-start.11 = (bf16[128,768]{1,0:T(8,128)(2,1)S(1)}, bf16[128,768]{1,0:T(8,128)(2,1)S(1)}, u32[]{:S(2)}, u32[]{:S(2)}) collective-permute-start(bf16[128,768]{1,0:T(8,128)(2,1)S(1)} %shard_map.132.refs_3_), channel_id=1, source_target_pairs={{0,1},{1,0},{2,3},{3,2},{4,5},{5,4},{6,7},{7,6},{8,9},{9,8},{10,11... | collective-permute-start | bytes 589832 | tf_op jit(solution)/shard_map/ppermute | solution.py:664
  49.0 5.6 %collective-permute-start.12 = (bf16[128,512]{1,0:T(8,128)(2,1)S(1)}, bf16[128,512]{1,0:T(8,128)(2,1)S(1)}, u32[]{:S(2)}, u32[]{:S(2)}) collective-permute-start(bf16[128,512]{1,0:T(8,128)(2,1)S(1)} %get-tuple-element.110.refs_2_.refs_5_), channel_id=1, source_target_pairs={{0,2},{2,0},{1,3},{3,1},{4,6},{6,4},{5,7},{7,5},{8,10},{10,8},{9,1... | collective-permute-start | bytes 393224 | tf_op jit(solution)/shard_map/ppermute | solution.py:664

commit v11 on v10

--- a/solution.py
+++ b/solution.py
@@ -236,9 +236,11 @@
         for name, shape in shapes.items():
             if is_fresh:
                 add_out((name, kv), shape)
-            else:
+            elif own or name != "dq":
                 add_near((name, kv), state[name, kv])
-    if not all(fresh):
+        if not own and not is_fresh:
+            add_out(("ds", kv), ((group * ROWS, 2 * PAGE), BF16, True))
+    if own and not all(fresh):
         add_out("gq", (q_all.shape, BF16, False))
         if "gq" in state:
             add_far("gq", state["gq"])
@@ -425,6 +427,9 @@
             p, ds = weigh(dot_n(qd, k_deep[...]), dot_n(gd, v_deep[...]), keep)
             acc[0] += dot_n(turn("qt", 0, SLOTS), ds)
             acc[1] += dot_n(turn("gt", 0, SLOTS), p)
+            if not fresh[n]:
+                held(("ds", kv))[part * SLOTS * tall : (part + 1) * SLOTS * tall] = ds
+                return
             dq = dot_n(ds, k_up[...])
             for slot in range(SLOTS):
                 head.put_queries(
@@ -465,9 +470,9 @@
             for part in range(parts):
                 slot = n * parts + part
                 (own_part if own else shared_part)(
-                    head, kv, part, n, None if fresh[n] else stage.at[slot]
+                    head, kv, part, n, stage.at[slot] if own and not fresh[n] else None
                 )
-                if not fresh[n]:
+                if own and not fresh[n]:
                     at = (kv * parts + part) * wide
                     sends.append(
                         pltpu.make_async_copy(
@@ -498,6 +503,55 @@
 def width_tiles(w):
     tile = next(t for t in (512, 640, 320, 128, w.shape[0]) if w.shape[0] % t == 0)
     return [slice(i, i + tile) for i in range(0, w.shape[0], tile)]
+
+
+def finish_queries(kvs, group, facts, pages, state, after=()):
+    parts = group // min(4, group)
+    heads = group // parts
+    tall = heads * PAGE
+    wide = heads * HD
+    near = list(pages)
+    for kv in kvs:
+        near += [state["ds", kv], state["dq", kv]]
+
+    def body(facts, mine, theirs, *refs):
+        gq, made, stage, sem = refs[-4:]
+        made[...] = jnp.zeros_like(made)
+        leads = facts[LEADS] == 1
+        sends = []
+        for n, kv in enumerate(kvs):
+            ds, dq = refs[2 * n : 2 * n + 2]
+            lane = slice(kv * HD, (kv + 1) * HD)
+            keys = jnp.concatenate(
+                [jnp.where(leads, mine[j, :, lane], theirs[j, :, lane]) for j in range(2)], axis=0
+            )
+            for part in range(parts):
+                at = n * parts + part
+                gained = dot_n(ds[part * SLOTS * tall : (part + 1) * SLOTS * tall], keys)
+                for i in range(SLOTS * heads):
+                    slot, j = divmod(i, heads)
+                    rows = slice(slot * PAGE, (slot + 1) * PAGE)
+                    value = gained[i * PAGE : (i + 1) * PAGE] + dq[
+                        rows, part * wide + j * HD : part * wide + (j + 1) * HD
+                    ]
+                    stage[at, rows, j * HD : (j + 1) * HD] = (value * SCALE).astype(BF16)
+                to = (kv * parts + part) * wide
+                sends.append(
+                    pltpu.make_async_copy(stage.at[at], gq.at[:, to : to + wide], sem.at[at])
+                )
+                sends[-1].start()
+        for c in sends:
+            c.wait()
+
+    count = len(kvs) * parts
+    far = [state["gq"]] if "gq" in state else []
+    shape = (ROWS, state["k"].shape[1] * group)
+    state["gq"], made = kernel_call(
+        body, facts, near, far, [(shape, BF16, False), ((8, HD), F32, True)],
+        [pltpu.VMEM((count, ROWS, wide), BF16), pltpu.SemaphoreType.DMA((count,))],
+        {("far", 0): 0} if far else {}, after, limit=LARGE,
+    )
+    return made
 
 
 def input_grad(facts, w, rows, own, far, grads, carry=None):
@@ -846,25 +900,25 @@
         begun = begin_input_grad(facts, w_near, both[1], (far_v[0], level2_far))
         far_v.append(spread(last[1]))
         total, low, far = over_halves(facts, total, root_far, next_far, (begun,))
-        *grads, made = end_input_grad(facts, w_near, far_v, begun, both[:2], after=(low,))
-        mine, far = over_chips(facts, total, far, last[3], (made,))
+        made = finish_queries(kvs[:-1], group, facts, shared, state, (low,))
+        mine, far = over_chips(facts, total, far, last[3], (made, far_v[1]))
         dk0, dv0 = finish_small_tree(facts, both[2], mine, far, level2_far)
-        far_v = spread(dv0)
-        begun = begin_input_grad(facts, w_near, [dv0])
-        grads = end_input_grad(facts, w_near, [far_v], begun, ([dk0], [dv0]), grads)
+        far_0 = spread(dv0)
+        begun_0 = begin_input_grad(facts, w_near, [dv0])
+        *grads, _ = end_input_grad(facts, w_near, far_v, begun, both[:2], after=(begun_0,))
+        grads = end_input_grad(facts, w_near, [far_0], begun_0, ([dk0], [dv0]), grads)
         return (state["gq"], grads[1], grads[2], grads[0])
 
     first = lax.axis_index("sub") == 0
     path_ids = ancestors[0]
     pages = gather_tree(path_ids, own)
     dk12, dv12, own0, send2 = own_pages(kvs, (pages[2], pages[2]))
-    kept, sent = shared_pages(
-        kvs,
-        (
-            jnp.where(first, pages[:2, 0], pages[:2, 1]),
-            jnp.where(first, pages[:2, 1], pages[:2, 0]),
-        ),
+    shared = (
+        jnp.where(first, pages[:2, 0], pages[:2, 1]),
+        jnp.where(first, pages[:2, 1], pages[:2, 0]),
     )
+    kept, sent = shared_pages(kvs, shared)
+    finish_queries(kvs, group, facts, shared, state)
     sent = sent.astype(F32)
     upper = jnp.stack([jnp.where(first, kept, sent), jnp.where(first, sent, kept)], axis=1)
     low = send2.astype(F32)

time: 57.2 us -> 54.6 us (0.955)
  waiting for transfers between devices: 12.1 us -> 7.95 us
  Pallas kernels: 29.5 us -> 31 us
    ppermute x13, waiting for transfers between devices: 12.1 us -> 7.95 us  [flipped(): lax.ppermute(block, axis, [(i, i ^ bit) for i in range(count) if i ^ bit...]
    pallas_call x11 -> x12, Pallas kernels: 22.6 us -> 23.6 us  [kernel_call(): pl.pallas_call(kernel, out_shape=tuple((pltpu.VMEM(s, d) if inside else j...]
  transfers between devices with their start and end apart: 13 -> 13, of which waited for: 7 -> 8; matrix products, arithmetic and copies ran while one was open for 0% -> 0% of each run, Pallas kernels for 31% -> 38%
where the time goes in v11:
time: 54.6 us; the launch traced here: 54.4 us
  Pallas kernels  31 us (57%)
  starting transfers between devices  14.5 us (27%)
  waiting for transfers between devices  7.95 us (15%)
  between operations  0.96 us (2%)
    pallas_call x12, Pallas kernels, kernel_call(): pl.pallas_call(kernel, out_shape=tuple((pltpu.VMEM(s, d) if inside else j...  23.6 us
    ppermute x13, starting transfers between devices, flipped(): lax.ppermute(block, axis, [(i, i ^ bit) for i in range(count) if i ^ bit...  14.5 us
    ppermute x13, waiting for transfers between devices, flipped(): lax.ppermute(block, axis, [(i, i ^ bit) for i in range(count) if i ^ bit...  7.95 us
    pallas_call x2, Pallas kernels, end_input_grad(): pl.pallas_call(kernel, out_shape=(jax.ShapeDtypeStruct((ROWS, out_cols),...  4.7 us
    pallas_call x2, Pallas kernels, begin_input_grad(): pl.pallas_call(kernel, out_shape=pltpu.VMEM((out_cols, rows), F32), in_sp...  1.72 us
  transfers between devices with their start and end apart: 13, of which 8 were waited for; matrix products, arithmetic and copies ran while one was open for 0% of the time, Pallas kernels for 38%

profile of v11, /device:TPU:0, one launch (start us, length us, event | category | flops | bytes accessed | tf_op | source)
XLA Modules:
  0.0 54.4 jit_solution(3674159552347455845)
XLA Ops:
  0.6 1.0 %shard_map.120 = (s32[16]{0:T(128)S(4)}, bf16[2,128,512]{2,1,0:T(8,128)(2,1)S(1)}) custom-call(s32[1]{0:T(128)} %bitcast.side_ref, s32[1,5]{1,0:T(1,128)} %ids_ref.1, s32[1,3]{1,0:T(1,128)} %counts_ref.1, bf16[384,512]{1,0:T(8,128)(2,1)} %refs_5_.1, bf16[384,512]{1,0:T(8,128)(2,1)} %refs_6_.1), custom_call_target="tpu_custom_call" | custom-call | tf_op jit(solution)/shard_map/pallas_call | solution.py:117
  1.7 0.5 collective-permute-start
  2.2 1.2 %collective-permute-done.refs_2_.refs_10_.refs_11_ = bf16[2,128,512]{2,1,0:T(8,128)(2,1)S(1)} collective-permute-done((bf16[2,128,512]{2,1,0:T(8,128)(2,1)S(1)}, bf16[2,128,512]{2,1,0:T(8,128)(2,1)S(1)}, u32[]{:S(2)}, u32[]{:S(2)}) %collective-permute-start) | collective-permute-done | bytes 262176 | tf_op jit(solution)/shard_map/ppermute | solution.py:718
  3.4 3.0 %collective-permute-start.1 = (bf16[128,512]{1,0:T(8,128)(2,1)S(1)}, bf16[128,512]{1,0:T(8,128)(2,1)S(1)}, u32[]{:S(2)}, u32[]{:S(2)}) collective-permute-start(bf16[128,512]{1,0:T(8,128)(2,1)S(1)} %shard_map.121.refs_9_.refs_1_), channel_id=1, source_target_pairs={{0,4},{4,0},{8,12},{12,8},{1,5},{5,1},{9,13},{13,9},{2,6},{6,2},{1... | collective-permute-start | bytes 393224 | tf_op jit(solution)/shard_map/ppermute | solution.py:718
  6.4 4.3 %shard_map.122 = (f32[384,1024]{1,0:T(8,128)S(1)}, bf16[128,3072]{1,0:T(8,128)(2,1)S(1)}, bf16[128,3072]{1,0:T(8,128)(2,1)S(1)}, bf16[256,128]{1,0:T(8,128)(2,1)...) custom-call(s32[16]{0:T(128)S(4)} %get-tuple-element.64.refs_0_, ...), custom_call_target="tpu_custom_call" | custom-call | flops 4026531840 | bytes 1000 | tf_op jit(solution)/shard_map/pallas_call | solution.py:76
  10.7 0.0 collective-permute-done.1.refs_2_
  10.8 2.7 %collective-permute-start.2 = (bf16[128,512]{1,0:T(8,128)(2,1)S(1)}, bf16[128,512]{1,0:T(8,128)(2,1)S(1)}, u32[]{:S(2)}, u32[]{:S(2)}) collective-permute-start(bf16[128,512]{1,0:T(8,128)(2,1)S(1)} %shard_map.123.refs_15_.refs_3_), channel_id=1, source_target_pairs={{0,8},{4,12},{8,0},{12,4},{1,9},{5,13},{9,1},{13,5},{2,10},{6,14},... | collective-permute-start | bytes 393224 | tf_op jit(solution)/shard_map/ppermute | solution.py:718
  13.4 4.9 %shard_map.124 = (f32[384,1024]{1,0:T(8,128)S(1)}, bf16[128,3072]{1,0:T(8,128)(2,1)S(1)}, bf16[128,3072]{1,0:T(8,128)(2,1)S(1)}, f32[384,1024]{1,0:T(8,128)S(1)}...) custom-call(s32[16]{0:T(128)S(4)} %get-tuple-element.64.refs_0_, ...), custom_call_target="tpu_custom_call" | custom-call | flops 8053063680 | bytes 1000 | tf_op jit(solution)/shard_map/pallas_call | solution.py:76
  18.3 1.4 %collective-permute-done.2.refs_4_ = bf16[128,512]{1,0:T(8,128)(2,1)S(1)} collective-permute-done((bf16[128,512]{1,0:T(8,128)(2,1)S(1)}, bf16[128,512]{1,0:T(8,128)(2,1)S(1)}, u32[]{:S(2)}, u32[]{:S(2)}) %collective-permute-start.2) | collective-permute-done | bytes 131104 | tf_op jit(solution)/shard_map/ppermute | solution.py:718
  19.8 0.1 collective-permute-start.3
  19.9 1.5 %collective-permute-done.3.refs_20_.refs_2_ = bf16[2,128,512]{2,1,0:T(8,128)(2,1)S(1)} collective-permute-done((bf16[2,128,512]{2,1,0:T(8,128)(2,1)S(1)}, bf16[2,128,512]{2,1,0:T(8,128)(2,1)S(1)}, u32[]{:S(2)}, u32[]{:S(2)}) %collective-permute-start.3) | collective-permute-done | bytes 262176 | tf_op jit(solution)/shard_map/ppermute | solution.py:718
  21.4 6.5 %shard_map.126 = (bf16[3072,256]{1,0:T(8,128)(2,1)S(1)}, bf16[3072,256]{1,0:T(8,128)(2,1)S(1)}, bf16[3072,256]{1,0:T(8,128)(2,1)S(1)}, f32[384,1024]{1,0:T(8,128...) custom-call(s32[16]{0:T(128)S(4)} %get-tuple-element.64.refs_0_, ...), custom_call_target="tpu_custom_call" | custom-call | flops 16106127360 | bytes 1000 | tf_op jit(solution)/shard_map/pallas_call | solution.py:76
  28.0 0.2 collective-permute-start.4
  28.2 0.4 collective-permute-start.8
  28.5 1.5 %collective-permute-start.7 = (bf16[256,384]{1,0:T(8,128)(2,1)S(1)}, bf16[256,384]{1,0:T(8,128)(2,1)S(1)}, u32[]{:S(2)}, u32[]{:S(2)}) collective-permute-start(bf16[256,384]{1,0:T(8,128)(2,1)S(1)} %get-tuple-element.105.refs_2_.refs_7_), channel_id=1, source_target_pairs={{0,2},{2,0},{1,3},{3,1},{4,6},{6,4},{5,7},{7,5},{8,10},{10,8},{9,1... | collective-permute-start | bytes 589832 | tf_op jit(solution)/shard_map/ppermute | solution.py:718
  30.0 0.0 collective-permute-done.4.refs_2_
  30.0 0.1 shard_map.127
  30.1 0.1 collective-permute-start.5
  30.2 3.2 %collective-permute-start.6 = (bf16[128,512]{1,0:T(8,128)(2,1)S(1)}, bf16[128,512]{1,0:T(8,128)(2,1)S(1)}, u32[]{:S(2)}, u32[]{:S(2)}) collective-permute-start(bf16[128,512]{1,0:T(8,128)(2,1)S(1)} %get-tuple-element.103), channel_id=1, source_target_pairs={{0,4},{4,0},{8,12},{12,8},{1,5},{5,1},{9,13},{13,9},{2,6},{6,2},{1... | collective-permute-start | bytes 393224 | tf_op jit(solution)/shard_map/ppermute | solution.py:718
  33.4 4.9 %shard_map.128 = (bf16[384,4096]{1,0:T(8,128)(2,1)}, bf16[256,128]{1,0:T(8,128)(2,1)S(1)}, bf16[256,128]{1,0:T(8,128)(2,1)S(1)}, f32[2,128,128]{2,1,0:T(8,128)S(...) custom-call(s32[16]{0:T(128)S(4)} %get-tuple-element.64.refs_0_, ...), custom_call_target="tpu_custom_call" | custom-call | flops 4026531840 | bytes 1000 | tf_op jit(solution)/shard_map/pallas_call | solution.py:76
  38.3 0.0 collective-permute-done.7.refs_4_.refs_3_
  38.3 0.0 collective-permute-done.8.refs_5_
  38.3 0.9 %shard_map.129.refs_4_.refs_2_ = f32[2560,256]{1,0:T(8,128)S(1)} custom-call(s32[16]{0:T(128)S(4)} %get-tuple-element.64.refs_0_, bf16[2560,1024]{1,0:T(8,128)(2,1)S(1)} %get-tuple-element.104.refs_1_, bf16[256,384]{1,0:T(8,128)(2,1)S(1)} %get-tuple-element.105.refs_2_.refs_7_, bf16[256,128]{1,0:T(8,128)(2,1)S(1)} %get-tuple-element.106.refs_3_.refs_8_, ...), custom_call_target="tpu_custom_call" | custom-call | flops 1000 | bytes 1000 | tf_op jit(solution)/shard_map/pallas_call | solution.py:653
  39.2 0.0 collective-permute-done.5.refs_2_
  39.2 0.2 collective-permute-done.6.refs_3_
  39.4 0.1 shard_map.130
  39.5 0.1 collective-permute-start.9
  39.5 1.4 %collective-permute-start.10 = (bf16[256,128]{1,0:T(8,128)(2,1)S(1)}, bf16[256,128]{1,0:T(8,128)(2,1)S(1)}, u32[]{:S(2)}, u32[]{:S(2)}) collective-permute-start(bf16[256,128]{1,0:T(8,128)(2,1)S(1)} %get-tuple-element.106.refs_3_.refs_8_), channel_id=1, source_target_pairs={{0,2},{2,0},{1,3},{3,1},{4,6},{6,4},{5,7},{7,5},{8,10},{10,8},{9,1... | collective-permute-start | bytes 196616 | tf_op jit(solution)/shard_map/ppermute | solution.py:718
  40.9 2.6 %shard_map.131 = (bf16[384,4096]{1,0:T(8,128)(2,1)}, f32[8,128]{1,0:T(8,128)S(1)}) custom-call(s32[16]{0:T(128)S(4)} %get-tuple-element.64.refs_0_, bf16[2,128,512]{2,1,0:T(8,128)(2,1)S(1)} %shard_map.125.refs_19_.refs_1_, bf16[2,128,512]{2,1,0:T(8,128)(2,1)S(1)} %collective-permute-done.3.refs_20_.refs_2_, ...), custom_call_target="tpu_custom_call", output_to_operand_aliasing={{0}: (9, {})} | custom-call | flops 1000 | bytes 1000 | tf_op jit(solution)/shard_map/pallas_call | solution.py:76
  43.5 0.4 collective-permute-done.10.refs_5_.refs_4_
  43.9 0.9 %collective-permute-done.9.refs_2_ = bf16[128,512]{1,0:T(8,128)(2,1)S(1)} collective-permute-done((bf16[128,512]{1,0:T(8,128)(2,1)S(1)}, bf16[128,512]{1,0:T(8,128)(2,1)S(1)}, u32[]{:S(2)}, u32[]{:S(2)}) %collective-permute-start.9) | collective-permute-done | bytes 131104 | tf_op jit(solution)/shard_map/ppermute | solution.py:718
  44.8 0.1 collective-permute-start.11
  44.8 1.4 %collective-permute-done.11.refs_4_ = bf16[128,768]{1,0:T(8,128)(2,1)S(1)} collective-permute-done((bf16[128,768]{1,0:T(8,128)(2,1)S(1)}, bf16[128,768]{1,0:T(8,128)(2,1)S(1)}, u32[]{:S(2)}, u32[]{:S(2)}) %collective-permute-start.11) | collective-permute-done | bytes 196640 | tf_op jit(solution)/shard_map/ppermute | solution.py:718
  46.3 0.1 shard_map.133
  46.4 1.4 %collective-permute-start.12 = (bf16[128,512]{1,0:T(8,128)(2,1)S(1)}, bf16[128,512]{1,0:T(8,128)(2,1)S(1)}, u32[]{:S(2)}, u32[]{:S(2)}) collective-permute-start(bf16[128,512]{1,0:T(8,128)(2,1)S(1)} %get-tuple-element.114.refs_2_.refs_5_), channel_id=1, source_target_pairs={{0,2},{2,0},{1,3},{3,1},{4,6},{6,4},{5,7},{7,5},{8,10},{10,8},{9,1... | collective-permute-start | bytes 393224 | tf_op jit(solution)/shard_map/ppermute | solution.py:718
  47.8 0.8 %shard_map.134.refs_9_.refs_2_ = f32[2560,128]{1,0:T(8,128)S(1)} custom-call(s32[16]{0:T(128)S(4)} %get-tuple-element.64.refs_0_, bf16[2560,1024]{1,0:T(8,128)(2,1)S(1)} %get-tuple-element.104.refs_1_, bf16[128,512]{1,0:T(8,128)(2,1)S(1)} %get-tuple-element.114.refs_2_.refs_5_), custom_call_target="tpu_custom_call" | custom-call | flops 1000 | bytes 1000 | tf_op jit(solution)/shard_map/pallas_call | solution.py:653
  48.6 2.4 %shard_map.135 = (bf16[384,2560]{1,0:T(8,128)(2,1)}, bf16[384,512]{1,0:T(8,128)(2,1)}, bf16[384,512]{1,0:T(8,128)(2,1)}, f32[8,128]{1,0:T(8,128)}) custom-call(s32[16]{0:T(128)S(4)} %get-tuple-element.64.refs_0_, bf16[2560,1024]{1,0:T(8,128)(2,1)S(1)} %get-tuple-element.104.refs_1_, f32[2560,256]{1,0:T(8,128)S(1)} %shard_map.129.refs_4_.refs_2_, ...), custom_call_target="tpu_custom_call" | custom-call | flops 1000 | bytes 1000 | tf_op jit(solution)/shard_map/pallas_call | solution.py:699
  51.1 0.9 %collective-permute-done.12.refs_3_ = bf16[128,512]{1,0:T(8,128)(2,1)S(1)} collective-permute-done((bf16[128,512]{1,0:T(8,128)(2,1)S(1)}, bf16[128,512]{1,0:T(8,128)(2,1)S(1)}, u32[]{:S(2)}, u32[]{:S(2)}) %collective-permute-start.12) | collective-permute-done | bytes 131104 | tf_op jit(solution)/shard_map/ppermute | solution.py:718
  52.0 2.3 %shard_map.136 = (bf16[384,2560]{1,0:T(8,128)(2,1)}, bf16[384,512]{1,0:T(8,128)(2,1)}, bf16[384,512]{1,0:T(8,128)(2,1)}, f32[8,128]{1,0:T(8,128)}) custom-call(s32[16]{0:T(128)S(4)} %get-tuple-element.64.refs_0_, bf16[2560,1024]{1,0:T(8,128)(2,1)S(1)} %get-tuple-element.104.refs_1_, ...), custom_call_target="tpu_custom_call", output_to_operand_aliasing={{0}: (6, {}), {1}: (7, {}), {2}: (8, {})} | custom-call | flops 1000 | bytes 1000 | tf_op jit(solution)/shard_map/pallas_call | solution.py:699
  (4 shorter events, 0.1 us)
Async XLA Ops:
  1.7 1.7 %collective-permute-start = (bf16[2,128,512]{2,1,0:T(8,128)(2,1)S(1)}, bf16[2,128,512]{2,1,0:T(8,128)(2,1)S(1)}, u32[]{:S(2)}, u32[]{:S(2)}) collective-permute-start(bf16[2,128,512]{2,1,0:T(8,128)(2,1)S(1)} %get-tuple-element.65.refs_1_.refs_9_.refs_10_), channel_id=1, source_target_pairs={{0,1},{1,0},{2,3},{3,2},{4,5},{5,4},{6,7},{7,6},{8,9},{9,8},{10,11... | collective-permute-start | bytes 786440 | tf_op jit(solution)/shard_map/ppermute | solution.py:718
  3.4 7.4 %collective-permute-start.1 = (bf16[128,512]{1,0:T(8,128)(2,1)S(1)}, bf16[128,512]{1,0:T(8,128)(2,1)S(1)}, u32[]{:S(2)}, u32[]{:S(2)}) collective-permute-start(bf16[128,512]{1,0:T(8,128)(2,1)S(1)} %shard_map.121.refs_9_.refs_1_), channel_id=1, source_target_pairs={{0,4},{4,0},{8,12},{12,8},{1,5},{5,1},{9,13},{13,9},{2,6},{6,2},{1... | collective-permute-start | bytes 393224 | tf_op jit(solution)/shard_map/ppermute | solution.py:718
  10.8 9.0 %collective-permute-start.2 = (bf16[128,512]{1,0:T(8,128)(2,1)S(1)}, bf16[128,512]{1,0:T(8,128)(2,1)S(1)}, u32[]{:S(2)}, u32[]{:S(2)}) collective-permute-start(bf16[128,512]{1,0:T(8,128)(2,1)S(1)} %shard_map.123.refs_15_.refs_3_), channel_id=1, source_target_pairs={{0,8},{4,12},{8,0},{12,4},{1,9},{5,13},{9,1},{13,5},{2,10},{6,14},... | collective-permute-start | bytes 393224 | tf_op jit(solution)/shard_map/ppermute | solution.py:718
  19.8 1.6 %collective-permute-start.3 = (bf16[2,128,512]{2,1,0:T(8,128)(2,1)S(1)}, bf16[2,128,512]{2,1,0:T(8,128)(2,1)S(1)}, u32[]{:S(2)}, u32[]{:S(2)}) collective-permute-start(bf16[2,128,512]{2,1,0:T(8,128)(2,1)S(1)} %shard_map.125.refs_19_.refs_1_), channel_id=1, source_target_pairs={{0,1},{1,0},{2,3},{3,2},{4,5},{5,4},{6,7},{7,6},{8,9},{9,8},{10,11... | collective-permute-start | bytes 786440 | tf_op jit(solution)/shard_map/ppermute | solution.py:718
  28.0 2.1 %collective-permute-start.4 = (bf16[2,128,512]{2,1,0:T(8,128)(2,1)S(1)}, bf16[2,128,512]{2,1,0:T(8,128)(2,1)S(1)}, u32[]{:S(2)}, u32[]{:S(2)}) collective-permute-start(bf16[2,128,512]{2,1,0:T(8,128)(2,1)S(1)} %get-tuple-element.99), channel_id=1, source_target_pairs={{0,1},{1,0},{2,3},{3,2},{4,5},{5,4},{6,7},{7,6},{8,9},{9,8},{10,11... | collective-permute-start | bytes 786440 | tf_op jit(solution)/shard_map/ppermute | solution.py:718
  28.2 10.1 %collective-permute-start.8 = (bf16[2,128,384]{2,1,0:T(8,128)(2,1)S(1)}, bf16[2,128,384]{2,1,0:T(8,128)(2,1)S(1)}, u32[]{:S(2)}, u32[]{:S(2)}) collective-permute-start(bf16[2,128,384]{2,1,0:T(8,128)(2,1)S(1)} %get-tuple-element.78.refs_5_), channel_id=1, source_target_pairs={{0,1},{1,0},{2,3},{3,2},{4,5},{5,4},{6,7},{7,6},{8,9},{9,8},{10,11... | collective-permute-start | bytes 589832 | tf_op jit(solution)/shard_map/ppermute | solution.py:718
  28.5 9.7 %collective-permute-start.7 = (bf16[256,384]{1,0:T(8,128)(2,1)S(1)}, bf16[256,384]{1,0:T(8,128)(2,1)S(1)}, u32[]{:S(2)}, u32[]{:S(2)}) collective-permute-start(bf16[256,384]{1,0:T(8,128)(2,1)S(1)} %get-tuple-element.105.refs_2_.refs_7_), channel_id=1, source_target_pairs={{0,2},{2,0},{1,3},{3,1},{4,6},{6,4},{5,7},{7,5},{8,10},{10,8},{9,1... | collective-permute-start | bytes 589832 | tf_op jit(solution)/shard_map/ppermute | solution.py:718
  30.1 9.1 %collective-permute-start.5 = (bf16[128,512]{1,0:T(8,128)(2,1)S(1)}, bf16[128,512]{1,0:T(8,128)(2,1)S(1)}, u32[]{:S(2)}, u32[]{:S(2)}) collective-permute-start(bf16[128,512]{1,0:T(8,128)(2,1)S(1)} %get-tuple-element.100.refs_13_), channel_id=1, source_target_pairs={{0,8},{4,12},{8,0},{12,4},{1,9},{5,13},{9,1},{13,5},{2,10},{6,14},... | collective-permute-start | bytes 393224 | tf_op jit(solution)/shard_map/ppermute | solution.py:718
  30.2 9.2 %collective-permute-start.6 = (bf16[128,512]{1,0:T(8,128)(2,1)S(1)}, bf16[128,512]{1,0:T(8,128)(2,1)S(1)}, u32[]{:S(2)}, u32[]{:S(2)}) collective-permute-start(bf16[128,512]{1,0:T(8,128)(2,1)S(1)} %get-tuple-element.103), channel_id=1, source_target_pairs={{0,4},{4,0},{8,12},{12,8},{1,5},{5,1},{9,13},{13,9},{2,6},{6,2},{1... | collective-permute-start | bytes 393224 | tf_op jit(solution)/shard_map/ppermute | solution.py:718
  39.5 5.3 %collective-permute-start.9 = (bf16[128,512]{1,0:T(8,128)(2,1)S(1)}, bf16[128,512]{1,0:T(8,128)(2,1)S(1)}, u32[]{:S(2)}, u32[]{:S(2)}) collective-permute-start(bf16[128,512]{1,0:T(8,128)(2,1)S(1)} %get-tuple-element.107.refs_10_), channel_id=1, source_target_pairs={{0,4},{4,0},{8,12},{12,8},{1,5},{5,1},{9,13},{13,9},{2,6},{6,2},{1... | collective-permute-start | bytes 393224 | tf_op jit(solution)/shard_map/ppermute | solution.py:718
  39.5 4.3 %collective-permute-start.10 = (bf16[256,128]{1,0:T(8,128)(2,1)S(1)}, bf16[256,128]{1,0:T(8,128)(2,1)S(1)}, u32[]{:S(2)}, u32[]{:S(2)}) collective-permute-start(bf16[256,128]{1,0:T(8,128)(2,1)S(1)} %get-tuple-element.106.refs_3_.refs_8_), channel_id=1, source_target_pairs={{0,2},{2,0},{1,3},{3,1},{4,6},{6,4},{5,7},{7,5},{8,10},{10,8},{9,1... | collective-permute-start | bytes 196616 | tf_op jit(solution)/shard_map/ppermute | solution.py:718
  44.8 1.5 %collective-permute-start.11 = (bf16[128,768]{1,0:T(8,128)(2,1)S(1)}, bf16[128,768]{1,0:T(8,128)(2,1)S(1)}, u32[]{:S(2)}, u32[]{:S(2)}) collective-permute-start(bf16[128,768]{1,0:T(8,128)(2,1)S(1)} %shard_map.132.refs_3_), channel_id=1, source_target_pairs={{0,1},{1,0},{2,3},{3,2},{4,5},{5,4},{6,7},{7,6},{8,9},{9,8},{10,11... | collective-permute-start | bytes 589832 | tf_op jit(solution)/shard_map/ppermute | solution.py:718
  46.4 5.6 %collective-permute-start.12 = (bf16[128,512]{1,0:T(8,128)(2,1)S(1)}, bf16[128,512]{1,0:T(8,128)(2,1)S(1)}, u32[]{:S(2)}, u32[]{:S(2)}) collective-permute-start(bf16[128,512]{1,0:T(8,128)(2,1)S(1)} %get-tuple-element.114.refs_2_.refs_5_), channel_id=1, source_target_pairs={{0,2},{2,0},{1,3},{3,1},{4,6},{6,4},{5,7},{7,5},{8,10},{10,8},{9,1... | collective-permute-start | bytes 393224 | tf_op jit(solution)/shard_map/ppermute | solution.py:718

commit v12 on v11

--- a/solution.py
+++ b/solution.py
@@ -32,10 +32,33 @@
 
 
 FACTS = 16
-N0, N1, N2, OWNS2, LIMIT, LEADS, ROOT_IN_CHIP, ROOT_IN_PAIR, NEXT_IN_CHIP, SIDE = range(10)
-
-
-def write_facts(facts, ids, counts, side):
+N0, N1, N2, OWNS2, LIMIT, LEADS, ROOT_IN_CHIP, ROOT_IN_PAIR, NEXT_IN_CHIP, SIDE, SWAP = range(11)
+
+
+class Order:
+    def __init__(self, crossed, heads):
+        self.crossed, self.heads = crossed, heads
+        self.half = heads // 2 if crossed else heads
+
+    def at(self, facts, head, unit):
+        if not self.crossed:
+            return head * unit
+        step = ((head ^ self.half) - head) * unit
+        return pl.multiple_of(facts[SWAP] * step + head * unit, unit)
+
+    def runs(self, first, last):
+        cuts = [first, *(h for h in range(first + 1, last) if h % self.half == 0), last]
+        return list(zip(cuts[:-1], cuts[1:]))
+
+    def real(self, facts, rows):
+        if not self.crossed:
+            return rows
+        width = self.half * HD
+        turned = jnp.concatenate([rows[:, width:], rows[:, :width]], axis=1)
+        return jnp.where(facts[SWAP] == 1, turned, rows)
+
+
+def write_facts(facts, ids, counts, side, order):
     page = [ids[0, j] for j in range(INNER + 1)]
     own = page[INNER] - 1
     leaf = own // SLOTS
@@ -52,7 +75,8 @@
     facts[ROOT_IN_PAIR] = number(same(0, 2))
     facts[NEXT_IN_CHIP] = number(same(1, 1))
     facts[SIDE] = side
-    for i in range(SIDE + 1, FACTS):
+    facts[SWAP] = lax.rem(leaf, 2) if order.crossed else 0
+    for i in range(SWAP + 1, FACTS):
         facts[i] = 0
 
 
@@ -87,7 +111,7 @@
     )(pltpu.with_memory_space_constraint(facts, pltpu.SMEM), *near, *far, *after)
 
 
-def start(side, ids, counts, keys, values):
+def start(order, side, ids, counts, keys, values):
     width = keys.shape[1]
 
     def body(side_ref, ids_ref, counts_ref, k_ref, v_ref, facts, out, held, ids_s, counts_s, sem):
@@ -106,7 +130,7 @@
             c.start()
         copies[0].wait()
         copies[1].wait()
-        write_facts(facts, ids_s, counts_s, side_ref[0])
+        write_facts(facts, ids_s, counts_s, side_ref[0], order)
         ok = row_ok(counts_s[0, 0], PAGE, width)
         for i in range(2):
             copies[2 + i].wait()
@@ -202,7 +226,8 @@
     return p.astype(BF16), (p * grads).astype(BF16)
 
 
-def attend(own, kvs, group, facts, inputs, pages, state, prior=(), after=(), w=None):
+def attend(own, kvs, group, order, facts, inputs, pages, state, prior=(), after=(), w=None,
+           ride=None):
     loading = "k" not in state
     q_all, k_all = inputs[0], inputs[2]
     count = len(kvs)
@@ -255,8 +280,7 @@
         ]
     else:
         outs += [
-            ((2, PAGE, width), F32, True),
-            ((2, PAGE, width), BF16, True),
+            ((4, PAGE, width), F32, True) if ride is None else ((7, PAGE, width), BF16, True),
         ]
     at_loaded = len(outs)
     if loading:
@@ -281,6 +305,8 @@
         add_near(("page", i), page)
     for i, array in enumerate(prior):
         add_near(("prior", i), array)
+    if ride is not None:
+        add_near("ride", ride)
     key_pages = 4 if own else 2
     scratch = [
         pltpu.VMEM((2 * HD, key_pages * PAGE), BF16),
@@ -291,7 +317,7 @@
         pltpu.VMEM((ROWS, HD), BF16),
         pltpu.VMEM((count * parts, ROWS, wide), BF16),
         pltpu.SemaphoreType.DMA((count * parts,)),
-        pltpu.SemaphoreType.DMA((2 * kv_total + 5,)),
+        pltpu.SemaphoreType.DMA((2 * kv_total + 9,)),
     ]
     cols = lambda a, b: slice(a * PAGE, b * PAGE)
 
@@ -305,19 +331,27 @@
         copies = {}
         if loading:
 
-            def load(key, src):
-                copies[key] = pltpu.make_async_copy(src, held(key), load_sem.at[len(copies)])
+            def load(key, src, dst):
+                copies[key] = pltpu.make_async_copy(src, dst, load_sem.at[len(copies)])
                 copies[key].start()
 
-            for name in ("k", "v", "norms", "deltas"):
-                load(name, far_ref(name))
+            for lo, hi in order.runs(0, kv_total):
+                for name in ("k", "v"):
+                    at = pl.ds(order.at(facts, lo, HD), (hi - lo) * HD)
+                    here = slice(lo * HD, hi * HD)
+                    load((name, lo), far_ref(name).at[:, at], held(name).at[:, here])
+                for name in ("norms", "deltas"):
+                    at = pl.ds(order.at(facts, lo, group), (hi - lo) * group)
+                    here = slice(lo * group, hi * group)
+                    load((name, lo), far_ref(name).at[at], held(name).at[here])
+            shared_loads = list(copies)
             for kv in range(kv_total):
-                at = slice(kv * group * HD, (kv + 1) * group * HD)
+                at = pl.ds(order.at(facts, kv, group * HD), group * HD)
                 for name in ("q", "g"):
-                    load((name, kv), far_ref(name).at[:, at])
+                    load((name, kv), far_ref(name).at[:, at], held((name, kv)))
         if w is not None:
             w_copy = pltpu.make_async_copy(
-                far_ref("w"), out_refs[at_end], load_sem.at[2 * kv_total + 4]
+                far_ref("w"), out_refs[at_end], load_sem.at[2 * kv_total + 8]
             )
             w_copy.start()
         k, v, norms, deltas = (held(name) for name in ("k", "v", "norms", "deltas"))
@@ -331,9 +365,15 @@
         v_deep[HD:] = jnp.full((HD, key_pages * PAGE), -1.0, BF16)
         for out, i in zip(results, range(len(prior))):
             out[..., :base] = near_ref(("prior", i))[...]
-        owns2, leads = facts[OWNS2] == 1, facts[LEADS] == 1
+        if ride is not None:
+            (out,), more = results, near_ref("ride")
+            for kind in range(2):
+                out[4 + kind] = more[kind, :, :width]
+                spare = slice(kind * HD, (kind + 1) * HD)
+                out[6, :, spare] = more[kind, :, width:]
+        owns2 = facts[OWNS2] == 1
         if loading:
-            arrived("norms", "deltas", "k", "v")
+            arrived(*shared_loads)
             lane = lax.broadcasted_iota(I32, norms.shape, 1)
             limit = jnp.where(
                 lane < PAGE, facts[N0], jnp.where(lane < 2 * PAGE, facts[N1], facts[N2])
@@ -345,8 +385,8 @@
 
         def set_pages(n, kv):
             lane = slice(kv * HD, (kv + 1) * HD)
-            first, second = (near_ref(("page", i)) for i in range(2))
             if own:
+                first, second = (near_ref(("page", i)) for i in range(2))
                 zero = jnp.zeros((), BF16)
                 for slot, (at, c) in enumerate(((3, N0), (0, N1), (2, N2))):
                     ok = row_ok(facts[c], PAGE, HD)
@@ -354,13 +394,20 @@
                     set_keys(k_deep, k_up, at, jnp.where(ok, k[rows, lane], zero))
                     set_keys(v_deep, None, at, jnp.where(ok, v[rows, lane], zero))
                 level2 = [jnp.where(owns2, first[i, :, lane], second[i, :, lane]) for i in (0, 1)]
+                if order.crossed:
+                    at = (kv ^ order.half) * HD
+                    lane = slice(at, at + HD)
+                    for i in range(2):
+                        other = jnp.where(owns2, first[i, :, lane], second[i, :, lane])
+                        level2[i] = jnp.where(facts[SWAP] == 1, other, level2[i])
                 set_keys(k_deep, k_up, 1, level2[0])
                 set_keys(v_deep, None, 1, level2[1])
             else:
+                page = near_ref(("page", 0))
                 for j in range(2):
-                    mine, theirs = first[j, :, lane], second[j, :, lane]
-                    set_keys(k_deep, k_up, j, jnp.where(leads, mine, theirs))
-                    set_keys(v_deep, None, j, jnp.where(leads, theirs, mine))
+                    here = slice(n * HD, (n + 1) * HD)
+                    set_keys(k_deep, k_up, j, page[j, 0, :, here])
+                    set_keys(v_deep, None, j, page[j, 1, :, here])
             acc[...] = jnp.zeros_like(acc)
 
         def turned_rows(head, kv, part, is_fresh, qs, gs, order):
@@ -453,13 +500,12 @@
                 send2[kind, :, here] = level2.astype(BF16)
 
         def put_shared(n):
-            kept, sent = results
+            (out,) = results
             here = slice(n * HD, (n + 1) * HD)
-            grad_k, grad_v = acc[0].T * SCALE, acc[1].T
+            grads = acc[0].T * SCALE, acc[1].T
             for j in range(2):
-                a, b = grad_k[cols(j, j + 1)], grad_v[cols(j, j + 1)]
-                kept[j, :, here] = jnp.where(leads, a, b)
-                sent[j, :, here] = jnp.where(leads, b, a).astype(BF16)
+                for kind in range(2):
+                    out[2 * j + kind, :, here] = grads[kind][cols(j, j + 1)].astype(out.dtype)
 
         sends = []
         for n, kv in enumerate(kvs):
@@ -473,10 +519,12 @@
                     head, kv, part, n, stage.at[slot] if own and not fresh[n] else None
                 )
                 if own and not fresh[n]:
-                    at = (kv * parts + part) * wide
+                    at = order.at(facts, kv, group * HD) + part * wide
                     sends.append(
                         pltpu.make_async_copy(
-                            stage.at[slot], held("gq").at[:, at : at + wide], sem.at[slot]
+                            stage.at[slot],
+                            held("gq").at[:, pl.ds(pl.multiple_of(at, wide), wide)],
+                            sem.at[slot],
                         )
                     )
                     sends[-1].start()
@@ -500,12 +548,12 @@
     return list(made[at_results:at_loaded]) + list(made[at_end:])
 
 
-def width_tiles(w):
-    tile = next(t for t in (512, 640, 320, 128, w.shape[0]) if w.shape[0] % t == 0)
+def width_tiles(w, sizes=(512, 640, 320, 128)):
+    tile = next(t for t in (*sizes, w.shape[0]) if w.shape[0] % t == 0)
     return [slice(i, i + tile) for i in range(0, w.shape[0], tile)]
 
 
-def finish_queries(kvs, group, facts, pages, state, after=()):
+def finish_queries(kvs, group, order, facts, pages, state, after=()):
     parts = group // min(4, group)
     heads = group // parts
     tall = heads * PAGE
@@ -514,17 +562,14 @@
     for kv in kvs:
         near += [state["ds", kv], state["dq", kv]]
 
-    def body(facts, mine, theirs, *refs):
+    def body(facts, *refs):
         gq, made, stage, sem = refs[-4:]
         made[...] = jnp.zeros_like(made)
-        leads = facts[LEADS] == 1
         sends = []
         for n, kv in enumerate(kvs):
-            ds, dq = refs[2 * n : 2 * n + 2]
-            lane = slice(kv * HD, (kv + 1) * HD)
-            keys = jnp.concatenate(
-                [jnp.where(leads, mine[j, :, lane], theirs[j, :, lane]) for j in range(2)], axis=0
-            )
+            ds, dq = refs[len(pages) + 2 * n : len(pages) + 2 * n + 2]
+            page, at = refs[kv // order.half], kv % order.half * HD
+            keys = jnp.concatenate([page[j, 0, :, at : at + HD] for j in range(2)], axis=0)
             for part in range(parts):
                 at = n * parts + part
                 gained = dot_n(ds[part * SLOTS * tall : (part + 1) * SLOTS * tall], keys)
@@ -535,9 +580,9 @@
                         rows, part * wide + j * HD : part * wide + (j + 1) * HD
                     ]
                     stage[at, rows, j * HD : (j + 1) * HD] = (value * SCALE).astype(BF16)
-                to = (kv * parts + part) * wide
+                to = pl.multiple_of(order.at(facts, kv, group * HD) + part * wide, wide)
                 sends.append(
-                    pltpu.make_async_copy(stage.at[at], gq.at[:, to : to + wide], sem.at[at])
+                    pltpu.make_async_copy(stage.at[at], gq.at[:, pl.ds(to, wide)], sem.at[at])
                 )
                 sends[-1].start()
         for c in sends:
@@ -554,7 +599,7 @@
     return made
 
 
-def input_grad(facts, w, rows, own, far, grads, carry=None):
+def input_grad(order, facts, w, rows, own, far, grads, carry=None):
     out_cols, depth = w.shape
     tiles = width_tiles(w)
     top = 0 if rows == PAGE else PAGE
@@ -583,7 +628,7 @@
             full = jnp.concatenate(
                 [jnp.where(leads, full, other), jnp.where(leads, other, full)], axis=1
             )
-        copies = put_rows(grad_r, dk, dv, top, rows, sem, steps)
+        copies = put_rows(order, facts, grad_r, dk, dv, top, rows, sem, steps)
         for i, at in enumerate(tiles):
             loads[i].wait()
             stage[i] = dot_t(w_near[at], full).astype(BF16).T
@@ -610,7 +655,7 @@
             pltpu.VMEM(w.shape, BF16),
             pltpu.VMEM((steps, rows, out_cols // steps), BF16),
             pltpu.SemaphoreType.DMA((steps,)),
-            pltpu.SemaphoreType.DMA((steps + 2 * count,)),
+            pltpu.SemaphoreType.DMA((steps + 2 * order.heads,)),
         ],
         input_output_aliases={2 + len(arrays) + i: i for i in range(len(carry))},
         compiler_params=pltpu.CompilerParams(vmem_limit_bytes=LARGE),
@@ -618,20 +663,27 @@
     )(pltpu.with_memory_space_constraint(facts, pltpu.SMEM), *arrays, w, *carry)
 
 
-def put_rows(pieces, dk, dv, top, rows, sem, first):
+def put_rows(order, facts, pieces, dk, dv, top, rows, sem, first):
     copies = []
     count = len(pieces) // 2
     for dst, mine in ((dk, pieces[:count]), (dv, pieces[count:])):
-        at = 0
+        head = 0
         for src in mine:
-            here = dst.at[top : top + rows, at : at + src.shape[1]]
-            copies.append(pltpu.make_async_copy(src, here, sem.at[first + len(copies)]))
-            copies[-1].start()
-            at += src.shape[1]
+            more = src.shape[1] // HD
+            for lo, hi in order.runs(head, head + more):
+                copies.append(
+                    pltpu.make_async_copy(
+                        src.at[:, (lo - head) * HD : (hi - head) * HD],
+                        dst.at[top : top + rows, pl.ds(order.at(facts, lo, HD), (hi - lo) * HD)],
+                        sem.at[first + len(copies)],
+                    )
+                )
+                copies[-1].start()
+            head += more
     return copies
 
 
-def begin_input_grad(facts, w, own, after=()):
+def begin_input_grad(order, facts, w, own, after=()):
     out_cols, depth = w.shape
     half = depth // 2
     rows = own[0].shape[0]
@@ -639,6 +691,7 @@
 
     def body(facts, w_ref, *refs):
         mine, out = jnp.concatenate([r[...] for r in refs[:count]], axis=1), refs[-1]
+        mine = order.real(facts, mine)
         where = pl.ds(pl.multiple_of(facts[SIDE] * half, half), half)
         for at in width_tiles(w):
             out[at] = dot_t(w_ref[at, where], mine)
@@ -660,8 +713,8 @@
     )(pltpu.with_memory_space_constraint(facts, pltpu.SMEM), *near, *after)
 
 
-def end_input_grad(facts, w, far, begun, grads, carry=None, after=()):
-    tiles = width_tiles(w)
+def end_input_grad(order, facts, w, far, begun, grads, carry=None, after=()):
+    tiles = width_tiles(w, (1280, 640, 320, 128))
     out_cols, depth = w.shape
     half = depth // 2
     steps = len(tiles)
@@ -675,8 +728,8 @@
         far_r, grad_r = refs[: len(far)], refs[len(far) : len(near) - 2]
         out, dk, dv, made, stage, sem = refs[-6:]
         made[...] = jnp.zeros_like(made)
-        copies = put_rows(grad_r, dk, dv, top, rows, sem, steps)
-        other = jnp.concatenate([r[...] for r in far_r], axis=1)
+        copies = put_rows(order, facts, grad_r, dk, dv, top, rows, sem, steps)
+        other = order.real(facts, jnp.concatenate([r[...] for r in far_r], axis=1))
         where = pl.ds(pl.multiple_of((1 - facts[SIDE]) * half, half), half)
         for i, at in enumerate(tiles):
             stage[i] = (dot_t(w_r[at, where], other) + begun_r[at]).astype(BF16).T
@@ -705,7 +758,7 @@
         out_specs=(hbm, hbm, hbm, vmem),
         scratch_shapes=[
             pltpu.VMEM((steps, rows, out_cols // steps), BF16),
-            pltpu.SemaphoreType.DMA((steps + 2 * len(grads[0]),)),
+            pltpu.SemaphoreType.DMA((steps + 2 * order.heads,)),
         ],
         input_output_aliases={1 + len(near) + i: i for i in range(len(carry))},
         compiler_params=pltpu.CompilerParams(vmem_limit_bytes=LARGE),
@@ -723,17 +776,19 @@
 
 
 def gather_small_tree(facts, own, beside_pair, beside_half):
-    two = (own.shape, BF16, True)
-    page = (own.shape[1:], BF16, True)
+    width = own.shape[-1] // 2
+    page = ((2, PAGE, width), BF16, True)
     from_core = flipped(own, "sub", 1)
 
     def choose_chip(facts, own_ref, far_ref, out):
-        for kind in range(2):
+        for swap in range(2):
             for mine in range(2):
 
-                @pl.when((facts[LEADS] != kind) & (facts[OWNS2] != mine))
-                def _copy(kind=kind, mine=mine):
-                    out[...] = (own_ref if mine else far_ref)[kind]
+                @pl.when((facts[SWAP] == swap) & (facts[OWNS2] != mine))
+                def _copy(swap=swap, mine=mine):
+                    out[...] = (own_ref if mine else far_ref)[
+                        :, :, swap * width : (swap + 1) * width
+                    ]
 
     (chip,) = kernel_call(choose_chip, facts, [own, from_core], [], [page])
     from_pair = flipped(chip, "leaf", 1)
@@ -751,24 +806,24 @@
 
     after = beside_half(pair)
     (mine,) = kernel_call(
-        choose_all, facts, [chip, from_pair, pair, from_half], [], [two], after=after
+        choose_all, facts, [chip, from_pair, pair, from_half], [],
+        [((2, *page[0]), BF16, True)], after=after,
     )
     return mine, flipped(mine, "sub", 1)
 
 
-def over_cores(facts, kept, sent):
+def over_cores(facts, kept, far):
     width = kept.shape[-1]
 
     def body(_, near, away, total, root, next_one):
-        for j, low in enumerate((root, next_one)):
-            value = near[j] + away[j].astype(F32)
-            total[j] = value
-            low[...] = value.astype(BF16)
-
-    page = ((PAGE, width), BF16, True)
+        for i in range(4):
+            value = near[i] + away[i].astype(F32)
+            total[i] = value
+            (root, next_one)[i // 2][i % 2] = value.astype(BF16)
+
+    pages = ((2, PAGE, width), BF16, True)
     total, root, next_one = kernel_call(
-        body, facts, [kept, flipped(sent, "sub", 1)], [],
-        [((2, PAGE, width), F32, True), page, page],
+        body, facts, [kept, far], [], [((4, PAGE, width), F32, True), pages, pages]
     )
     return total, root, flipped(root, "leaf", 2), flipped(next_one, "leaf", 1)
 
@@ -777,58 +832,57 @@
     width = total.shape[-1]
 
     def body(_, near, root_r, next_r, out, low):
-        root = near[0] + root_r[...].astype(F32)
-        out[0] = root
+        root = near[:2] + root_r[...].astype(F32)
+        out[:2] = root
         low[...] = root.astype(BF16)
-        out[1] = near[1] + next_r[...].astype(F32)
+        out[2:] = near[2:] + next_r[...].astype(F32)
 
     total, low = kernel_call(
         body, facts, [total, root_far, next_far], [],
-        [((2, PAGE, width), F32, True), ((PAGE, width), BF16, True)], after=after,
+        [((4, PAGE, width), F32, True), ((2, PAGE, width), BF16, True)], after=after,
     )
     return total, low, flipped(low, "leaf", 1)
 
 
-def over_chips(facts, total, far, passenger, after):
+def over_chips(facts, total, far, level2, after):
     width = total.shape[-1]
-    more = passenger.shape[-1]
 
     def body(facts, near, away, extra, out):
-        root = near[0] + away[...].astype(F32)
-        out[:, :width] = jnp.where(facts[ROOT_IN_CHIP] == 1, root, near[1]).astype(BF16)
-        for kind in range(2):
-            out[:, width + kind * more : width + (kind + 1) * more] = extra[kind]
-
-    outs = [((PAGE, width + 2 * more), BF16, True)]
-    (mine,) = kernel_call(
-        body, facts, [total, far, passenger], [], outs, after=after
-    )
+        root = near[:2] + away[...].astype(F32)
+        out[:, :, :width] = jnp.where(facts[ROOT_IN_CHIP] == 1, root, near[2:]).astype(BF16)
+        out[:, :, width:] = extra[:, :, extra.shape[-1] - HD :]
+
+    outs = [((2, PAGE, width + HD), BF16, True)]
+    (mine,) = kernel_call(body, facts, [total, far, level2], [], outs, after=after)
     return mine, flipped(mine, "sub", 1)
 
 
-def finish_small_tree(facts, own0, mine, far, level2_far):
-    width = sum(a.shape[-1] for a in own0)
-
-    def body(facts, own_r, own_last, mine_r, far_r, low_r, dk, dv):
-        owns2, leads = facts[OWNS2] == 1, facts[LEADS] == 1
+def finish_small_tree(order, facts, own0, mine, far, level2_far, after):
+    width = own0.shape[-1]
+    part = order.half * HD
+
+    def body(facts, own_r, mine_r, far_r, low_r, dk, dv):
+        owns2 = facts[OWNS2] == 1
         ok = row_ok(facts[N0], PAGE, HD)
-        for at in range(0, width, HD):
-            c = slice(at, at + HD)
-            last = at + HD == width
-            near, away = mine_r[:, c], far_r[:, c]
-            gained = [jnp.where(leads, near, away), jnp.where(leads, away, near)]
+        for head in range(order.heads):
+            c = slice(head * HD, (head + 1) * HD)
+            at = head % order.half * HD
+            here = slice(at, at + HD)
+            theirs = head ^ order.half
             for kind, out in enumerate((dk, dv)):
-                if last:
-                    level2 = far_r[:, width + kind * HD : width + (kind + 1) * HD]
+                gained = (far_r if head < order.half else mine_r)[kind, :, here]
+                if theirs < order.half:
+                    level2 = low_r[4 + kind, :, theirs * HD : (theirs + 1) * HD]
+                elif theirs + 1 < order.heads:
+                    level2 = low_r[6, :, kind * HD : (kind + 1) * HD]
                 else:
-                    level2 = low_r[kind, :, c]
-                more = jnp.where(owns2, level2, gained[kind]).astype(F32)
-                base = own_last[kind] if last else own_r[kind, :, c]
-                out[:, c] = jnp.where(ok, base + more, 0.0).astype(BF16)
+                    level2 = far_r[kind, :, part : part + HD]
+                more = jnp.where(owns2, level2, gained).astype(F32)
+                out[:, c] = jnp.where(ok, own_r[kind, :, c] + more, 0.0).astype(BF16)
 
     page = ((PAGE, width), BF16, True)
     return kernel_call(
-        body, facts, [*own0, mine, far, level2_far], [], [page, page]
+        body, facts, [own0, mine, far, level2_far], [], [page, page], after=after
     )
 
 
@@ -861,14 +915,18 @@
     side = lax.axis_index("tensor").astype(I32).reshape(1)
     two_sides = lax.axis_size("tensor") == 2
     inputs = [hbm(a) for a in (queries, grad_out, keys, values, log_norms, row_deltas)]
-    facts, own = start(side, hbm(ancestors), hbm(counts), *inputs[2:4])
+    fast = leaves == 8 and lax.axis_size("sub") == 2 and kv == 4 and two_sides
+    order = Order(fast, kv)
+    facts, own = start(order, side, hbm(ancestors), hbm(counts), *inputs[2:4])
     state = {}
 
     def own_pages(kvs, pages, prior=(), after=(), w=None):
-        return attend(True, kvs, group, facts, inputs, pages, state, prior, after, w)
-
-    def shared_pages(kvs, pages):
-        return attend(False, kvs, group, facts, inputs, pages, state)
+        return attend(
+            True, kvs, group, order, facts, inputs, pages, state, prior, after, w
+        )
+
+    def shared_pages(kvs, page, ride=None):
+        return attend(False, kvs, group, order, facts, inputs, [page], state, ride=ride)[0]
 
     def spread(part):
         if two_sides:
@@ -877,7 +935,7 @@
 
     kvs = tuple(range(kv))
     w = hbm(w_value)
-    if leaves == 8 and lax.axis_size("sub") == 2 and kv >= 3 and two_sides:
+    if fast:
         level2, results = [], []
 
         def beside_pair(from_core, chip):
@@ -886,43 +944,39 @@
             return (results[-1][3],)
 
         def beside_half(pair):
-            results.append(own_pages(kvs[1:-1], level2, results[-1], (pair,)))
+            results.append(own_pages(kvs[1:3], level2, results[-1], (pair,)))
             return (results[-1][3],)
 
-        shared = gather_small_tree(facts, own, beside_pair, beside_half)
-        most = results[-1]
-        far_v = [spread(most[1])]
-        level2_far = flipped(most[3], "sub", 1)
-        kept, sent = shared_pages(kvs, shared)
+        mine, theirs = gather_small_tree(facts, own, beside_pair, beside_half)
+        sent = flipped(shared_pages(kvs[:2], mine, results[-1][3]), "sub", 1)
+        kept = shared_pages(kvs[2:], theirs)
         total, root, root_far, next_far = over_cores(facts, kept, sent)
-        *last, w_near = own_pages(kvs[-1:], level2, after=(root,), w=w)
-        both = list(zip(most, last))
-        begun = begin_input_grad(facts, w_near, both[1], (far_v[0], level2_far))
-        far_v.append(spread(last[1]))
+        dk12, dv12, own0, send2, w_near = own_pages(
+            kvs[3:], level2, results[-1], (root,), w
+        )
+        begun = begin_input_grad(order, facts, w_near, [dv12])
+        far_v = spread(dv12)
         total, low, far = over_halves(facts, total, root_far, next_far, (begun,))
-        made = finish_queries(kvs[:-1], group, facts, shared, state, (low,))
-        mine, far = over_chips(facts, total, far, last[3], (made, far_v[1]))
-        dk0, dv0 = finish_small_tree(facts, both[2], mine, far, level2_far)
+        made = finish_queries(kvs[:3], group, order, facts, (mine, theirs), state, (low,))
+        near, far = over_chips(facts, total, far, send2, (made,))
+        dk0, dv0 = finish_small_tree(order, facts, own0, near, far, sent, (far_v,))
         far_0 = spread(dv0)
-        begun_0 = begin_input_grad(facts, w_near, [dv0])
-        *grads, _ = end_input_grad(facts, w_near, far_v, begun, both[:2], after=(begun_0,))
-        grads = end_input_grad(facts, w_near, [far_0], begun_0, ([dk0], [dv0]), grads)
+        begun_0 = begin_input_grad(order, facts, w_near, [dv0])
+        *grads, _ = end_input_grad(
+            order, facts, w_near, [far_v], begun, ([dk12], [dv12]), after=(begun_0,)
+        )
+        grads = end_input_grad(
+            order, facts, w_near, [far_0], begun_0, ([dk0], [dv0]), grads
+        )
         return (state["gq"], grads[1], grads[2], grads[0])
 
-    first = lax.axis_index("sub") == 0
     path_ids = ancestors[0]
     pages = gather_tree(path_ids, own)
     dk12, dv12, own0, send2 = own_pages(kvs, (pages[2], pages[2]))
-    shared = (
-        jnp.where(first, pages[:2, 0], pages[:2, 1]),
-        jnp.where(first, pages[:2, 1], pages[:2, 0]),
-    )
-    kept, sent = shared_pages(kvs, shared)
-    finish_queries(kvs, group, facts, shared, state)
-    sent = sent.astype(F32)
-    upper = jnp.stack([jnp.where(first, kept, sent), jnp.where(first, sent, kept)], axis=1)
+    grads = shared_pages(kvs, pages[:2])
+    finish_queries(kvs, group, order, facts, (pages[:2],), state)
     low = send2.astype(F32)
-    total = reduce_tree(path_ids, jnp.concatenate([upper, low[None]]))
+    total = reduce_tree(path_ids, jnp.concatenate([grads.reshape(2, 2, *grads.shape[1:]), low[None]]))
     total += own0 - jnp.where(path_ids[2] == path_ids[INNER] - 1, low, 0.0)
     has = jnp.any(path_ids[:INNER] == path_ids[INNER] - 1)
     ok = (jnp.arange(PAGE) < jnp.where(has, counts[0, 0], 0))[:, None]
@@ -931,8 +985,8 @@
         pair = lambda part: ([part], [spread(part)])
     else:
         pair = lambda part: ([spread(part)], [])
-    *grads, _ = input_grad(facts, w, 2 * PAGE, *pair(dv12), ([dk12], [dv12]))
-    grads = input_grad(facts, w, PAGE, *pair(dv0), ([dk0], [dv0]), grads)
+    *grads, _ = input_grad(order, facts, w, 2 * PAGE, *pair(dv12), ([dk12], [dv12]))
+    grads = input_grad(order, facts, w, PAGE, *pair(dv0), ([dk0], [dv0]), grads)
     return (state["gq"], grads[1], grads[2], grads[0])
 
 

time: 54.6 us -> 53.5 us (0.980)
  Pallas kernels: 31 us -> 32.4 us
  waiting for transfers between devices: 7.95 us -> 6.69 us
  starting transfers between devices: 14.5 us -> 13.3 us
    ppermute x13 -> x11, waiting for transfers between devices: 7.95 us -> 6.69 us  [flipped(): lax.ppermute(block, axis, [(i, i ^ bit) for i in range(count) if i ^ bit...]
    ppermute x13 -> x11, starting transfers between devices: 14.5 us -> 13.3 us  [flipped(): lax.ppermute(block, axis, [(i, i ^ bit) for i in range(count) if i ^ bit...]
    pallas_call x12 -> x13, Pallas kernels: 23.6 us -> 24.5 us  [kernel_call(): pl.pallas_call(kernel, out_shape=tuple((pltpu.VMEM(s, d) if inside else j...]
  transfers between devices with their start and end apart: 13 -> 11, of which waited for: 8 -> 6; matrix products, arithmetic and copies ran while one was open for 0% -> 0% of each run, Pallas kernels for 38% -> 54%
where the time goes in v12:
time: 53.5 us; the launch traced here: 53.4 us
  Pallas kernels  32.4 us (61%)
  starting transfers between devices  13.3 us (25%)
  waiting for transfers between devices  6.69 us (13%)
  between operations  0.95 us (2%)
    pallas_call x13, Pallas kernels, kernel_call(): pl.pallas_call(kernel, out_shape=tuple((pltpu.VMEM(s, d) if inside else j...  24.5 us
    ppermute x11, starting transfers between devices, flipped(): lax.ppermute(block, axis, [(i, i ^ bit) for i in range(count) if i ^ bit...  13.3 us
    ppermute x11, waiting for transfers between devices, flipped(): lax.ppermute(block, axis, [(i, i ^ bit) for i in range(count) if i ^ bit...  6.69 us
    pallas_call x2, Pallas kernels, end_input_grad(): pl.pallas_call(kernel, out_shape=(jax.ShapeDtypeStruct((ROWS, out_cols),...  5.18 us
    pallas_call x2, Pallas kernels, begin_input_grad(): pl.pallas_call(kernel, out_shape=pltpu.VMEM((out_cols, rows), F32), in_sp...  1.72 us
  transfers between devices with their start and end apart: 11, of which 6 were waited for; matrix products, arithmetic and copies ran while one was open for 0% of the time, Pallas kernels for 54%

profile of v12, /device:TPU:0, one launch (start us, length us, event | category | flops | bytes accessed | tf_op | source)
XLA Modules:
  0.0 53.4 jit_solution(3656978617547716459)
XLA Ops:
  0.6 1.0 %shard_map.120 = (s32[16]{0:T(128)S(4)}, bf16[2,128,512]{2,1,0:T(8,128)(2,1)S(1)}) custom-call(s32[1]{0:T(128)} %bitcast.side_ref, s32[1,5]{1,0:T(1,128)} %ids_ref.1, s32[1,3]{1,0:T(1,128)} %counts_ref.1, bf16[384,512]{1,0:T(8,128)(2,1)} %refs_5_.1, bf16[384,512]{1,0:T(8,128)(2,1)} %refs_6_.1), custom_call_target="tpu_custom_call" | custom-call | tf_op jit(solution)/shard_map/pallas_call | solution.py:141
  1.7 0.5 collective-permute-start
  2.2 1.2 %collective-permute-done.refs_2_.refs_10_.refs_11_ = bf16[2,128,512]{2,1,0:T(8,128)(2,1)S(1)} collective-permute-done((bf16[2,128,512]{2,1,0:T(8,128)(2,1)S(1)}, bf16[2,128,512]{2,1,0:T(8,128)(2,1)S(1)}, u32[]{:S(2)}, u32[]{:S(2)}) %collective-permute-start) | collective-permute-done | bytes 262176 | tf_op jit(solution)/shard_map/ppermute | solution.py:771
  3.4 3.0 %collective-permute-start.1 = (bf16[2,128,256]{2,1,0:T(8,128)(2,1)S(1)}, bf16[2,128,256]{2,1,0:T(8,128)(2,1)S(1)}, u32[]{:S(2)}, u32[]{:S(2)}) collective-permute-start(bf16[2,128,256]{2,1,0:T(8,128)(2,1)S(1)} %shard_map.121.refs_9_.refs_1_), channel_id=1, source_target_pairs={{0,4},{4,0},{8,12},{12,8},{1,5},{5,1},{9,13},{13,9},{2,6},{6,2},{1... | collective-permute-start | bytes 393224 | tf_op jit(solution)/shard_map/ppermute | solution.py:771
  6.4 4.6 %shard_map.122 = (f32[384,1024]{1,0:T(8,128)S(1)}, bf16[128,3072]{1,0:T(8,128)(2,1)S(1)}, bf16[128,3072]{1,0:T(8,128)(2,1)S(1)}, bf16[256,128]{1,0:T(8,128)(2,1)...) custom-call(s32[16]{0:T(128)S(4)} %get-tuple-element.64.refs_0_, ...), custom_call_target="tpu_custom_call" | custom-call | flops 4026531840 | bytes 1000 | tf_op jit(solution)/shard_map/pallas_call | solution.py:100
  11.0 0.0 collective-permute-done.1.refs_2_
  11.0 2.7 %collective-permute-start.2 = (bf16[2,128,256]{2,1,0:T(8,128)(2,1)S(1)}, bf16[2,128,256]{2,1,0:T(8,128)(2,1)S(1)}, u32[]{:S(2)}, u32[]{:S(2)}) collective-permute-start(bf16[2,128,256]{2,1,0:T(8,128)(2,1)S(1)} %shard_map.123.refs_15_.refs_3_), channel_id=1, source_target_pairs={{0,8},{4,12},{8,0},{12,4},{1,9},{5,13},{9,1},{13,5},{2,10},{6,14},... | collective-permute-start | bytes 393224 | tf_op jit(solution)/shard_map/ppermute | solution.py:771
  13.6 5.0 %shard_map.124 = (f32[384,1024]{1,0:T(8,128)S(1)}, bf16[128,3072]{1,0:T(8,128)(2,1)S(1)}, bf16[128,3072]{1,0:T(8,128)(2,1)S(1)}, f32[384,1024]{1,0:T(8,128)S(1)}...) custom-call(s32[16]{0:T(128)S(4)} %get-tuple-element.64.refs_0_, ...), custom_call_target="tpu_custom_call" | custom-call | flops 8053063680 | bytes 1000 | tf_op jit(solution)/shard_map/pallas_call | solution.py:100
  18.6 1.2 %collective-permute-done.2.refs_4_ = bf16[2,128,256]{2,1,0:T(8,128)(2,1)S(1)} collective-permute-done((bf16[2,128,256]{2,1,0:T(8,128)(2,1)S(1)}, bf16[2,128,256]{2,1,0:T(8,128)(2,1)S(1)}, u32[]{:S(2)}, u32[]{:S(2)}) %collective-permute-start.2) | collective-permute-done | bytes 131104 | tf_op jit(solution)/shard_map/ppermute | solution.py:771
  19.9 0.1 collective-permute-start.3
  19.9 3.3 %shard_map.126 = (bf16[3072,256]{1,0:T(8,128)(2,1)S(1)}, bf16[3072,256]{1,0:T(8,128)(2,1)S(1)}, bf16[7,128,256]{2,1,0:T(8,128)(2,1)S(1)}) custom-call(s32[16]{0:T(128)S(4)} %get-tuple-element.64.refs_0_, bf16[128,3072]{1,0:T(8,128)(2,1)S(1)} %get-tuple-element.79.refs_1_, bf16[128,3072]{1,0:T(8,128)(2,1)S(1)} %get-tuple-element.80.refs_2_, ...), custom_call_target="tpu_custom_call" | custom-call | flops 8053063680 | bytes 1000 | tf_op jit(solution)/shard_map/pallas_call | solution.py:100
  23.3 0.6 %collective-permute-start.4 = (bf16[7,128,256]{2,1,0:T(8,128)(2,1)S(1)}, bf16[7,128,256]{2,1,0:T(8,128)(2,1)S(1)}, u32[]{:S(2)}, u32[]{:S(2)}) collective-permute-start(bf16[7,128,256]{2,1,0:T(8,128)(2,1)S(1)} %get-tuple-element.102), channel_id=1, source_target_pairs={{0,1},{1,0},{2,3},{3,2},{4,5},{5,4},{6,7},{7,6},{8,9},{9,8},{10,11... | collective-permute-start | bytes 1376264 | tf_op jit(solution)/shard_map/ppermute | solution.py:771
  23.8 0.0 collective-permute-done.3.refs_11_.refs_2_
  23.8 3.9 %shard_map.127 = (bf16[3072,256]{1,0:T(8,128)(2,1)S(1)}, f32[384,1024]{1,0:T(8,128)S(1)}, bf16[128,3072]{1,0:T(8,128)(2,1)S(1)}, bf16[128,3072]{1,0:T(8,128)(2,1)S(1)}, f32[4,128,256]{2,1,0:T(8,128)S(1)}) custom-call(s32[16]{0:T(128)S(4)} %get-tuple-element.64.refs_0_, bf16[128,3072]{1,0:T(8,128)(2,1)S(1)} %get-tuple-element.89.refs_1_, ...), custom_call_target="tpu_custom_call" | custom-call | flops 8053063680 | bytes 1000 | tf_op jit(solution)/shard_map/pallas_call | solution.py:100
  27.7 0.0 collective-permute-done.4.refs_2_.refs_4_
  27.7 0.1 shard_map.128
  27.8 0.1 collective-permute-start.5
  27.9 3.2 %collective-permute-start.6 = (bf16[2,128,256]{2,1,0:T(8,128)(2,1)S(1)}, bf16[2,128,256]{2,1,0:T(8,128)(2,1)S(1)}, u32[]{:S(2)}, u32[]{:S(2)}) collective-permute-start(bf16[2,128,256]{2,1,0:T(8,128)(2,1)S(1)} %get-tuple-element.106), channel_id=1, source_target_pairs={{0,4},{4,0},{8,12},{12,8},{1,5},{5,1},{9,13},{13,9},{2,6},{6,2},{1... | collective-permute-start | bytes 393224 | tf_op jit(solution)/shard_map/ppermute | solution.py:771
  31.1 4.8 %shard_map.129 = (bf16[384,4096]{1,0:T(8,128)(2,1)}, bf16[256,512]{1,0:T(8,128)(2,1)S(1)}, bf16[256,512]{1,0:T(8,128)(2,1)S(1)}, f32[2,128,512]{2,1,0:T(8,128)S(...) custom-call(s32[16]{0:T(128)S(4)} %get-tuple-element.64.refs_0_, ...), custom_call_target="tpu_custom_call" | custom-call | flops 4026531840 | bytes 1000 | tf_op jit(solution)/shard_map/pallas_call | solution.py:100
  35.8 0.9 %shard_map.130.refs_4_.refs_2_ = f32[2560,256]{1,0:T(8,128)S(1)} custom-call(s32[16]{0:T(128)S(4)} %get-tuple-element.64.refs_0_, bf16[2560,1024]{1,0:T(8,128)(2,1)S(1)} %get-tuple-element.107.refs_1_, bf16[256,512]{1,0:T(8,128)(2,1)S(1)} %get-tuple-element.108.refs_2_.refs_5_), custom_call_target="tpu_custom_call" | custom-call | flops 1000 | bytes 1000 | tf_op jit(solution)/shard_map/pallas_call | solution.py:706
  36.7 0.4 collective-permute-done.5.refs_2_
  37.1 0.2 collective-permute-done.6.refs_3_
  37.3 0.1 shard_map.131
  37.3 0.1 collective-permute-start.7
  37.4 1.6 %collective-permute-start.9 = (bf16[256,512]{1,0:T(8,128)(2,1)S(1)}, bf16[256,512]{1,0:T(8,128)(2,1)S(1)}, u32[]{:S(2)}, u32[]{:S(2)}) collective-permute-start(bf16[256,512]{1,0:T(8,128)(2,1)S(1)} %get-tuple-element.108.refs_2_.refs_5_), channel_id=1, source_target_pairs={{0,2},{2,0},{1,3},{3,1},{4,6},{6,4},{5,7},{7,5},{8,10},{10,8},{9,1... | collective-permute-start | bytes 786440 | tf_op jit(solution)/shard_map/ppermute | solution.py:771
  39.0 2.6 %shard_map.132 = (bf16[384,4096]{1,0:T(8,128)(2,1)}, f32[8,128]{1,0:T(8,128)S(1)}) custom-call(s32[16]{0:T(128)S(4)} %get-tuple-element.64.refs_0_, bf16[2,2,128,256]{3,2,1,0:T(8,128)(2,1)S(1)} %shard_map.125.refs_13_.refs_1_, bf16[2,2,128,256]{3,2,1,0:T(8,128)(2,1)S(1)} %collective-permute-done.3.refs_11_.refs_2_, ...), custom_call_target="tpu_custom_call", output_to_operand_aliasing={{0}: (9, {})} | custom-call | flops 1000 | bytes 1000 | tf_op jit(solution)/shard_map/pallas_call | solution.py:100
  41.6 1.0 %collective-permute-done.7.refs_2_ = bf16[2,128,256]{2,1,0:T(8,128)(2,1)S(1)} collective-permute-done((bf16[2,128,256]{2,1,0:T(8,128)(2,1)S(1)}, bf16[2,128,256]{2,1,0:T(8,128)(2,1)S(1)}, u32[]{:S(2)}, u32[]{:S(2)}) %collective-permute-start.7) | collective-permute-done | bytes 131104 | tf_op jit(solution)/shard_map/ppermute | solution.py:771
  42.6 0.1 collective-permute-start.8
  42.7 2.8 %collective-permute-done.9.refs_5_.refs_3_ = bf16[256,512]{1,0:T(8,128)(2,1)S(1)} collective-permute-done((bf16[256,512]{1,0:T(8,128)(2,1)S(1)}, bf16[256,512]{1,0:T(8,128)(2,1)S(1)}, u32[]{:S(2)}, u32[]{:S(2)}) %collective-permute-start.9) | collective-permute-done | bytes 262176 | tf_op jit(solution)/shard_map/ppermute | solution.py:771
  45.5 0.0 collective-permute-done.8.refs_3_
  45.5 0.1 shard_map.134
  45.6 1.6 %collective-permute-start.10 = (bf16[128,512]{1,0:T(8,128)(2,1)S(1)}, bf16[128,512]{1,0:T(8,128)(2,1)S(1)}, u32[]{:S(2)}, u32[]{:S(2)}) collective-permute-start(bf16[128,512]{1,0:T(8,128)(2,1)S(1)} %get-tuple-element.115.refs_2_.refs_5_), channel_id=1, source_target_pairs={{0,2},{2,0},{1,3},{3,1},{4,6},{6,4},{5,7},{7,5},{8,10},{10,8},{9,1... | collective-permute-start | bytes 393224 | tf_op jit(solution)/shard_map/ppermute | solution.py:771
  47.2 0.8 %shard_map.135.refs_6_.refs_2_ = f32[2560,128]{1,0:T(8,128)S(1)} custom-call(s32[16]{0:T(128)S(4)} %get-tuple-element.64.refs_0_, bf16[2560,1024]{1,0:T(8,128)(2,1)S(1)} %get-tuple-element.107.refs_1_, bf16[128,512]{1,0:T(8,128)(2,1)S(1)} %get-tuple-element.115.refs_2_.refs_5_), custom_call_target="tpu_custom_call" | custom-call | flops 1000 | bytes 1000 | tf_op jit(solution)/shard_map/pallas_call | solution.py:706
  48.0 2.7 %shard_map.136 = (bf16[384,2560]{1,0:T(8,128)(2,1)}, bf16[384,512]{1,0:T(8,128)(2,1)}, bf16[384,512]{1,0:T(8,128)(2,1)}, f32[8,128]{1,0:T(8,128)}) custom-call(s32[16]{0:T(128)S(4)} %get-tuple-element.64.refs_0_, bf16[2560,1024]{1,0:T(8,128)(2,1)S(1)} %get-tuple-element.107.refs_1_, f32[2560,256]{1,0:T(8,128)S(1)} %shard_map.130.refs_4_.refs_2_, ...), custom_call_target="tpu_custom_call" | custom-call | flops 1000 | bytes 1000 | tf_op jit(solution)/shard_map/pallas_call | solution.py:752
  50.8 0.0 collective-permute-done.10.refs_3_
  50.8 2.4 %shard_map.137 = (bf16[384,2560]{1,0:T(8,128)(2,1)}, bf16[384,512]{1,0:T(8,128)(2,1)}, bf16[384,512]{1,0:T(8,128)(2,1)}, f32[8,128]{1,0:T(8,128)}) custom-call(s32[16]{0:T(128)S(4)} %get-tuple-element.64.refs_0_, bf16[2560,1024]{1,0:T(8,128)(2,1)S(1)} %get-tuple-element.107.refs_1_, ...), custom_call_target="tpu_custom_call", output_to_operand_aliasing={{0}: (6, {}), {1}: (7, {}), {2}: (8, {})} | custom-call | flops 1000 | bytes 1000 | tf_op jit(solution)/shard_map/pallas_call | solution.py:752
  (4 shorter events, 0.1 us)
Async XLA Ops:
  1.7 1.7 %collective-permute-start = (bf16[2,128,512]{2,1,0:T(8,128)(2,1)S(1)}, bf16[2,128,512]{2,1,0:T(8,128)(2,1)S(1)}, u32[]{:S(2)}, u32[]{:S(2)}) collective-permute-start(bf16[2,128,512]{2,1,0:T(8,128)(2,1)S(1)} %get-tuple-element.65.refs_1_.refs_9_.refs_10_), channel_id=1, source_target_pairs={{0,1},{1,0},{2,3},{3,2},{4,5},{5,4},{6,7},{7,6},{8,9},{9,8},{10,11... | collective-permute-start | bytes 786440 | tf_op jit(solution)/shard_map/ppermute | solution.py:771
  3.4 7.6 %collective-permute-start.1 = (bf16[2,128,256]{2,1,0:T(8,128)(2,1)S(1)}, bf16[2,128,256]{2,1,0:T(8,128)(2,1)S(1)}, u32[]{:S(2)}, u32[]{:S(2)}) collective-permute-start(bf16[2,128,256]{2,1,0:T(8,128)(2,1)S(1)} %shard_map.121.refs_9_.refs_1_), channel_id=1, source_target_pairs={{0,4},{4,0},{8,12},{12,8},{1,5},{5,1},{9,13},{13,9},{2,6},{6,2},{1... | collective-permute-start | bytes 393224 | tf_op jit(solution)/shard_map/ppermute | solution.py:771
  11.0 8.8 %collective-permute-start.2 = (bf16[2,128,256]{2,1,0:T(8,128)(2,1)S(1)}, bf16[2,128,256]{2,1,0:T(8,128)(2,1)S(1)}, u32[]{:S(2)}, u32[]{:S(2)}) collective-permute-start(bf16[2,128,256]{2,1,0:T(8,128)(2,1)S(1)} %shard_map.123.refs_15_.refs_3_), channel_id=1, source_target_pairs={{0,8},{4,12},{8,0},{12,4},{1,9},{5,13},{9,1},{13,5},{2,10},{6,14},... | collective-permute-start | bytes 393224 | tf_op jit(solution)/shard_map/ppermute | solution.py:771
  19.9 3.9 %collective-permute-start.3 = (bf16[2,2,128,256]{3,2,1,0:T(8,128)(2,1)S(1)}, bf16[2,2,128,256]{3,2,1,0:T(8,128)(2,1)S(1)}, u32[]{:S(2)}, u32[]{:S(2)}) collective-permute-start(bf16[2,2,128,256]{3,2,1,0:T(8,128)(2,1)S(1)} %shard_map.125.refs_13_.refs_1_), channel_id=1, source_target_pairs={{0,1},{1,0},{2,3},{3,2},{4,5},{5,4},{6,7},{7,6},{8,9},{9,8},{10,11... | collective-permute-start | bytes 786440 | tf_op jit(solution)/shard_map/ppermute | solution.py:771
  23.3 4.5 %collective-permute-start.4 = (bf16[7,128,256]{2,1,0:T(8,128)(2,1)S(1)}, bf16[7,128,256]{2,1,0:T(8,128)(2,1)S(1)}, u32[]{:S(2)}, u32[]{:S(2)}) collective-permute-start(bf16[7,128,256]{2,1,0:T(8,128)(2,1)S(1)} %get-tuple-element.102), channel_id=1, source_target_pairs={{0,1},{1,0},{2,3},{3,2},{4,5},{5,4},{6,7},{7,6},{8,9},{9,8},{10,11... | collective-permute-start | bytes 1376264 | tf_op jit(solution)/shard_map/ppermute | solution.py:771
  27.8 9.3 %collective-permute-start.5 = (bf16[2,128,256]{2,1,0:T(8,128)(2,1)S(1)}, bf16[2,128,256]{2,1,0:T(8,128)(2,1)S(1)}, u32[]{:S(2)}, u32[]{:S(2)}) collective-permute-start(bf16[2,128,256]{2,1,0:T(8,128)(2,1)S(1)} %get-tuple-element.103.refs_17_), channel_id=1, source_target_pairs={{0,8},{4,12},{8,0},{12,4},{1,9},{5,13},{9,1},{13,5},{2,10},{6,14},... | collective-permute-start | bytes 393224 | tf_op jit(solution)/shard_map/ppermute | solution.py:771
  27.9 9.3 %collective-permute-start.6 = (bf16[2,128,256]{2,1,0:T(8,128)(2,1)S(1)}, bf16[2,128,256]{2,1,0:T(8,128)(2,1)S(1)}, u32[]{:S(2)}, u32[]{:S(2)}) collective-permute-start(bf16[2,128,256]{2,1,0:T(8,128)(2,1)S(1)} %get-tuple-element.106), channel_id=1, source_target_pairs={{0,4},{4,0},{8,12},{12,8},{1,5},{5,1},{9,13},{13,9},{2,6},{6,2},{1... | collective-permute-start | bytes 393224 | tf_op jit(solution)/shard_map/ppermute | solution.py:771
  37.3 5.3 %collective-permute-start.7 = (bf16[2,128,256]{2,1,0:T(8,128)(2,1)S(1)}, bf16[2,128,256]{2,1,0:T(8,128)(2,1)S(1)}, u32[]{:S(2)}, u32[]{:S(2)}) collective-permute-start(bf16[2,128,256]{2,1,0:T(8,128)(2,1)S(1)} %get-tuple-element.109.refs_10_), channel_id=1, source_target_pairs={{0,4},{4,0},{8,12},{12,8},{1,5},{5,1},{9,13},{13,9},{2,6},{6,2},{1... | collective-permute-start | bytes 393224 | tf_op jit(solution)/shard_map/ppermute | solution.py:771
  37.4 8.1 %collective-permute-start.9 = (bf16[256,512]{1,0:T(8,128)(2,1)S(1)}, bf16[256,512]{1,0:T(8,128)(2,1)S(1)}, u32[]{:S(2)}, u32[]{:S(2)}) collective-permute-start(bf16[256,512]{1,0:T(8,128)(2,1)S(1)} %get-tuple-element.108.refs_2_.refs_5_), channel_id=1, source_target_pairs={{0,2},{2,0},{1,3},{3,1},{4,6},{6,4},{5,7},{7,5},{8,10},{10,8},{9,1... | collective-permute-start | bytes 786440 | tf_op jit(solution)/shard_map/ppermute | solution.py:771
  42.6 2.8 %collective-permute-start.8 = (bf16[2,128,384]{2,1,0:T(8,128)(2,1)S(1)}, bf16[2,128,384]{2,1,0:T(8,128)(2,1)S(1)}, u32[]{:S(2)}, u32[]{:S(2)}) collective-permute-start(bf16[2,128,384]{2,1,0:T(8,128)(2,1)S(1)} %shard_map.133.refs_2_), channel_id=1, source_target_pairs={{0,1},{1,0},{2,3},{3,2},{4,5},{5,4},{6,7},{7,6},{8,9},{9,8},{10,11... | collective-permute-start | bytes 589832 | tf_op jit(solution)/shard_map/ppermute | solution.py:771
  45.6 5.2 %collective-permute-start.10 = (bf16[128,512]{1,0:T(8,128)(2,1)S(1)}, bf16[128,512]{1,0:T(8,128)(2,1)S(1)}, u32[]{:S(2)}, u32[]{:S(2)}) collective-permute-start(bf16[128,512]{1,0:T(8,128)(2,1)S(1)} %get-tuple-element.115.refs_2_.refs_5_), channel_id=1, source_target_pairs={{0,2},{2,0},{1,3},{3,1},{4,6},{6,4},{5,7},{7,5},{8,10},{10,8},{9,1... | collective-permute-start | bytes 393224 | tf_op jit(solution)/shard_map/ppermute | solution.py:771

commit v13 on v12

--- a/solution.py
+++ b/solution.py
@@ -305,8 +305,8 @@
         add_near(("page", i), page)
     for i, array in enumerate(prior):
         add_near(("prior", i), array)
-    if ride is not None:
-        add_near("ride", ride)
+    for i, array in enumerate(ride or ()):
+        add_near(("ride", i), array)
     key_pages = 4 if own else 2
     scratch = [
         pltpu.VMEM((2 * HD, key_pages * PAGE), BF16),
@@ -366,11 +366,10 @@
         for out, i in zip(results, range(len(prior))):
             out[..., :base] = near_ref(("prior", i))[...]
         if ride is not None:
-            (out,), more = results, near_ref("ride")
+            (out,) = results
             for kind in range(2):
-                out[4 + kind] = more[kind, :, :width]
-                spare = slice(kind * HD, (kind + 1) * HD)
-                out[6, :, spare] = more[kind, :, width:]
+                out[4 + kind] = near_ref(("ride", 0))[kind]
+                out[6, :, kind * HD : (kind + 1) * HD] = near_ref(("ride", 1))[kind]
         owns2 = facts[OWNS2] == 1
         if loading:
             arrived(*shared_loads)
@@ -548,8 +547,8 @@
     return list(made[at_results:at_loaded]) + list(made[at_end:])
 
 
-def width_tiles(w, sizes=(512, 640, 320, 128)):
-    tile = next(t for t in (*sizes, w.shape[0]) if w.shape[0] % t == 0)
+def width_tiles(w):
+    tile = next(t for t in (512, 640, 320, 128, w.shape[0]) if w.shape[0] % t == 0)
     return [slice(i, i + tile) for i in range(0, w.shape[0], tile)]
 
 
@@ -714,7 +713,7 @@
 
 
 def end_input_grad(order, facts, w, far, begun, grads, carry=None, after=()):
-    tiles = width_tiles(w, (1280, 640, 320, 128))
+    tiles = width_tiles(w)
     out_cols, depth = w.shape
     half = depth // 2
     steps = len(tiles)
@@ -857,11 +856,11 @@
     return mine, flipped(mine, "sub", 1)
 
 
-def finish_small_tree(order, facts, own0, mine, far, level2_far, after):
-    width = own0.shape[-1]
+def finish_small_tree(order, facts, own0, mine, far, level2_far):
     part = order.half * HD
-
-    def body(facts, own_r, mine_r, far_r, low_r, dk, dv):
+    width = 2 * part
+
+    def body(facts, own_first, own_second, mine_r, far_r, low_r, dk, dv):
         owns2 = facts[OWNS2] == 1
         ok = row_ok(facts[N0], PAGE, HD)
         for head in range(order.heads):
@@ -870,7 +869,9 @@
             here = slice(at, at + HD)
             theirs = head ^ order.half
             for kind, out in enumerate((dk, dv)):
-                gained = (far_r if head < order.half else mine_r)[kind, :, here]
+                first = head < order.half
+                gained = (far_r if first else mine_r)[kind, :, here]
+                base = (own_first if first else own_second)[kind, :, here]
                 if theirs < order.half:
                     level2 = low_r[4 + kind, :, theirs * HD : (theirs + 1) * HD]
                 elif theirs + 1 < order.heads:
@@ -878,12 +879,10 @@
                 else:
                     level2 = far_r[kind, :, part : part + HD]
                 more = jnp.where(owns2, level2, gained).astype(F32)
-                out[:, c] = jnp.where(ok, own_r[kind, :, c] + more, 0.0).astype(BF16)
+                out[:, c] = jnp.where(ok, base + more, 0.0).astype(BF16)
 
     page = ((PAGE, width), BF16, True)
-    return kernel_call(
-        body, facts, [own0, mine, far, level2_far], [], [page, page], after=after
-    )
+    return kernel_call(body, facts, [*own0, mine, far, level2_far], [], [page, page])
 
 
 def gather_tree(ids, own):
@@ -925,8 +924,10 @@
             True, kvs, group, order, facts, inputs, pages, state, prior, after, w
         )
 
-    def shared_pages(kvs, page, ride=None):
-        return attend(False, kvs, group, order, facts, inputs, [page], state, ride=ride)[0]
+    def shared_pages(kvs, page, ride=None, after=()):
+        return attend(
+            False, kvs, group, order, facts, inputs, [page], state, after=after, ride=ride
+        )[0]
 
     def spread(part):
         if two_sides:
@@ -936,34 +937,37 @@
     kvs = tuple(range(kv))
     w = hbm(w_value)
     if fast:
-        level2, results = [], []
+        level2, by_head, far_v = [], [], []
 
         def beside_pair(from_core, chip):
             level2.extend((own, from_core))
-            results.append(own_pages(kvs[:1], level2, after=(chip,)))
-            return (results[-1][3],)
+            by_head.append(own_pages(kvs[:1], level2, after=(chip,)))
+            return (by_head[0][3],)
 
         def beside_half(pair):
-            results.append(own_pages(kvs[1:3], level2, results[-1], (pair,)))
-            return (results[-1][3],)
+            by_head.append(own_pages(kvs[1:2], level2, by_head[0], (pair,)))
+            far_v.append(spread(by_head[1][1]))
+            by_head.append(own_pages(kvs[2:3], level2, after=(by_head[1][3],)))
+            return (by_head[2][3],)
 
         mine, theirs = gather_small_tree(facts, own, beside_pair, beside_half)
-        sent = flipped(shared_pages(kvs[:2], mine, results[-1][3]), "sub", 1)
+        first, third = by_head[1:]
+        sent = shared_pages(kvs[:2], mine, (first[3], third[3]), far_v)
+        sent = flipped(sent, "sub", 1)
         kept = shared_pages(kvs[2:], theirs)
         total, root, root_far, next_far = over_cores(facts, kept, sent)
-        dk12, dv12, own0, send2, w_near = own_pages(
-            kvs[3:], level2, results[-1], (root,), w
-        )
-        begun = begin_input_grad(order, facts, w_near, [dv12])
-        far_v = spread(dv12)
+        *second, w_near = own_pages(kvs[3:], level2, third, (root,), w)
+        both = list(zip(first, second))
+        begun = begin_input_grad(order, facts, w_near, both[1])
+        far_v.append(spread(second[1]))
         total, low, far = over_halves(facts, total, root_far, next_far, (begun,))
         made = finish_queries(kvs[:3], group, order, facts, (mine, theirs), state, (low,))
-        near, far = over_chips(facts, total, far, send2, (made,))
-        dk0, dv0 = finish_small_tree(order, facts, own0, near, far, sent, (far_v,))
+        near, far = over_chips(facts, total, far, second[3], (made, far_v[1]))
+        dk0, dv0 = finish_small_tree(order, facts, both[2], near, far, sent)
         far_0 = spread(dv0)
         begun_0 = begin_input_grad(order, facts, w_near, [dv0])
         *grads, _ = end_input_grad(
-            order, facts, w_near, [far_v], begun, ([dk12], [dv12]), after=(begun_0,)
+            order, facts, w_near, far_v, begun, both[:2], after=(begun_0,)
         )
         grads = end_input_grad(
             order, facts, w_near, [far_0], begun_0, ([dk0], [dv0]), grads

time: 53.5 us -> 53.6 us (level)
  Pallas kernels: 32.4 us -> 31.1 us
  waiting for transfers between devices: 6.69 us -> 7.88 us
    ppermute x11 -> x12, waiting for transfers between devices: 6.69 us -> 7.88 us  [flipped(): lax.ppermute(block, axis, [(i, i ^ bit) for i in range(count) if i ^ bit...]
    pallas_call x13 -> x14, Pallas kernels: 24.5 us -> 23.6 us  [kernel_call(): pl.pallas_call(kernel, out_shape=tuple((pltpu.VMEM(s, d) if inside else j...]
    ppermute x11 -> x12, starting transfers between devices: 13.3 us -> 13.4 us  [flipped(): lax.ppermute(block, axis, [(i, i ^ bit) for i in range(count) if i ^ bit...]
  transfers between devices with their start and end apart: 11 -> 12, of which waited for: 6 -> 6; matrix products, arithmetic and copies ran while one was open for 0% -> 0% of each run, Pallas kernels for 54% -> 52%
where the time goes in v13:
time: 53.6 us; the launch traced here: 53.4 us
  Pallas kernels  31.1 us (58%)
  starting transfers between devices  13.4 us (25%)
  waiting for transfers between devices  7.88 us (15%)
  between operations  0.99 us (2%)
    pallas_call x14, Pallas kernels, kernel_call(): pl.pallas_call(kernel, out_shape=tuple((pltpu.VMEM(s, d) if inside else j...  23.6 us
    ppermute x12, starting transfers between devices, flipped(): lax.ppermute(block, axis, [(i, i ^ bit) for i in range(count) if i ^ bit...  13.4 us
    ppermute x12, waiting for transfers between devices, flipped(): lax.ppermute(block, axis, [(i, i ^ bit) for i in range(count) if i ^ bit...  7.88 us
    pallas_call x2, Pallas kernels, end_input_grad(): pl.pallas_call(kernel, out_shape=(jax.ShapeDtypeStruct((ROWS, out_cols),...  4.8 us
    pallas_call x2, Pallas kernels, begin_input_grad(): pl.pallas_call(kernel, out_shape=pltpu.VMEM((out_cols, rows), F32), in_sp...  1.72 us
  transfers between devices with their start and end apart: 12, of which 6 were waited for; matrix products, arithmetic and copies ran while one was open for 0% of the time, Pallas kernels for 52%

profile of v13, /device:TPU:0, one launch (start us, length us, event | category | flops | bytes accessed | tf_op | source)
XLA Modules:
  0.0 53.4 jit_solution(17558566774799937288)
XLA Ops:
  0.6 1.0 %shard_map.120 = (s32[16]{0:T(128)S(4)}, bf16[2,128,512]{2,1,0:T(8,128)(2,1)S(1)}) custom-call(s32[1]{0:T(128)} %bitcast.side_ref, s32[1,5]{1,0:T(1,128)} %ids_ref.1, s32[1,3]{1,0:T(1,128)} %counts_ref.1, bf16[384,512]{1,0:T(8,128)(2,1)} %refs_5_.1, bf16[384,512]{1,0:T(8,128)(2,1)} %refs_6_.1), custom_call_target="tpu_custom_call" | custom-call | tf_op jit(solution)/shard_map/pallas_call | solution.py:141
  1.7 0.5 collective-permute-start
  2.2 1.2 %collective-permute-done.refs_2_.refs_8_.refs_11_ = bf16[2,128,512]{2,1,0:T(8,128)(2,1)S(1)} collective-permute-done((bf16[2,128,512]{2,1,0:T(8,128)(2,1)S(1)}, bf16[2,128,512]{2,1,0:T(8,128)(2,1)S(1)}, u32[]{:S(2)}, u32[]{:S(2)}) %collective-permute-start) | collective-permute-done | bytes 262176 | tf_op jit(solution)/shard_map/ppermute | solution.py:770
  3.4 3.0 %collective-permute-start.1 = (bf16[2,128,256]{2,1,0:T(8,128)(2,1)S(1)}, bf16[2,128,256]{2,1,0:T(8,128)(2,1)S(1)}, u32[]{:S(2)}, u32[]{:S(2)}) collective-permute-start(bf16[2,128,256]{2,1,0:T(8,128)(2,1)S(1)} %shard_map.121.refs_9_.refs_1_), channel_id=1, source_target_pairs={{0,4},{4,0},{8,12},{12,8},{1,5},{5,1},{9,13},{13,9},{2,6},{6,2},{1... | collective-permute-start | bytes 393224 | tf_op jit(solution)/shard_map/ppermute | solution.py:770
  6.4 4.6 %shard_map.122 = (f32[384,1024]{1,0:T(8,128)S(1)}, bf16[128,3072]{1,0:T(8,128)(2,1)S(1)}, bf16[128,3072]{1,0:T(8,128)(2,1)S(1)}, bf16[256,128]{1,0:T(8,128)(2,1)...) custom-call(s32[16]{0:T(128)S(4)} %get-tuple-element.68.refs_0_, ...), custom_call_target="tpu_custom_call" | custom-call | flops 4026531840 | bytes 1000 | tf_op jit(solution)/shard_map/pallas_call | solution.py:100
  11.0 0.0 collective-permute-done.1.refs_2_
  11.0 2.6 %collective-permute-start.2 = (bf16[2,128,256]{2,1,0:T(8,128)(2,1)S(1)}, bf16[2,128,256]{2,1,0:T(8,128)(2,1)S(1)}, u32[]{:S(2)}, u32[]{:S(2)}) collective-permute-start(bf16[2,128,256]{2,1,0:T(8,128)(2,1)S(1)} %shard_map.123.refs_13_.refs_3_), channel_id=1, source_target_pairs={{0,8},{4,12},{8,0},{12,4},{1,9},{5,13},{9,1},{13,5},{2,10},{6,14},... | collective-permute-start | bytes 393224 | tf_op jit(solution)/shard_map/ppermute | solution.py:770
  13.7 2.7 %shard_map.124 = (f32[384,1024]{1,0:T(8,128)S(1)}, bf16[128,3072]{1,0:T(8,128)(2,1)S(1)}, bf16[128,3072]{1,0:T(8,128)(2,1)S(1)}, bf16[256,256]{1,0:T(8,128)(2,1)...) custom-call(s32[16]{0:T(128)S(4)} %get-tuple-element.68.refs_0_, ...), custom_call_target="tpu_custom_call" | custom-call | flops 4026531840 | bytes 1000 | tf_op jit(solution)/shard_map/pallas_call | solution.py:100
  16.4 1.6 %collective-permute-start.4 = (bf16[256,256]{1,0:T(8,128)(2,1)S(1)}, bf16[256,256]{1,0:T(8,128)(2,1)S(1)}, u32[]{:S(2)}, u32[]{:S(2)}) collective-permute-start(bf16[256,256]{1,0:T(8,128)(2,1)S(1)} %get-tuple-element.90.refs_2_.refs_7_), channel_id=1, source_target_pairs={{0,2},{2,0},{1,3},{3,1},{4,6},{6,4},{5,7},{7,5},{8,10},{10,8},{9,1... | collective-permute-start | bytes 393224 | tf_op jit(solution)/shard_map/ppermute | solution.py:770
  17.9 2.7 %shard_map.125 = (f32[384,1024]{1,0:T(8,128)S(1)}, bf16[128,3072]{1,0:T(8,128)(2,1)S(1)}, bf16[128,3072]{1,0:T(8,128)(2,1)S(1)}, bf16[256,128]{1,0:T(8,128)(2,1)...) custom-call(s32[16]{0:T(128)S(4)} %get-tuple-element.68.refs_0_, ...), custom_call_target="tpu_custom_call" | custom-call | flops 4026531840 | bytes 1000 | tf_op jit(solution)/shard_map/pallas_call | solution.py:100
  20.6 0.0 collective-permute-done.2.refs_4_
  20.7 0.1 collective-permute-start.3
  20.8 0.7 %collective-permute-done.4.refs_16_.refs_3_ = bf16[256,256]{1,0:T(8,128)(2,1)S(1)} collective-permute-done((bf16[256,256]{1,0:T(8,128)(2,1)S(1)}, bf16[256,256]{1,0:T(8,128)(2,1)S(1)}, u32[]{:S(2)}, u32[]{:S(2)}) %collective-permute-start.4) | collective-permute-done | bytes 131104 | tf_op jit(solution)/shard_map/ppermute | solution.py:770
  21.4 3.2 %shard_map.127 = (bf16[3072,256]{1,0:T(8,128)(2,1)S(1)}, bf16[3072,256]{1,0:T(8,128)(2,1)S(1)}, bf16[7,128,256]{2,1,0:T(8,128)(2,1)S(1)}) custom-call(s32[16]{0:T(128)S(4)} %get-tuple-element.68.refs_0_, bf16[128,3072]{1,0:T(8,128)(2,1)S(1)} %get-tuple-element.84.refs_1_, bf16[128,3072]{1,0:T(8,128)(2,1)S(1)} %get-tuple-element.85.refs_2_, ...), custom_call_target="tpu_custom_call" | custom-call | flops 8053063680 | bytes 1000 | tf_op jit(solution)/shard_map/pallas_call | solution.py:100
  24.7 0.1 collective-permute-start.5
  24.8 0.0 collective-permute-done.3.refs_11_.refs_2_
  24.8 3.9 %shard_map.128 = (bf16[3072,256]{1,0:T(8,128)(2,1)S(1)}, f32[384,1024]{1,0:T(8,128)S(1)}, bf16[128,3072]{1,0:T(8,128)(2,1)S(1)}, bf16[128,3072]{1,0:T(8,128)(2,1)S(1)}, f32[4,128,256]{2,1,0:T(8,128)S(1)}) custom-call(s32[16]{0:T(128)S(4)} %get-tuple-element.68.refs_0_, bf16[128,3072]{1,0:T(8,128)(2,1)S(1)} %get-tuple-element.95.refs_1_, ...), custom_call_target="tpu_custom_call" | custom-call | flops 8053063680 | bytes 1000 | tf_op jit(solution)/shard_map/pallas_call | solution.py:100
  28.7 0.0 collective-permute-done.5.refs_2_.refs_5_
  28.7 0.1 shard_map.129
  28.8 0.4 collective-permute-start.6
  29.2 1.9 %collective-permute-start.7 = (bf16[2,128,256]{2,1,0:T(8,128)(2,1)S(1)}, bf16[2,128,256]{2,1,0:T(8,128)(2,1)S(1)}, u32[]{:S(2)}, u32[]{:S(2)}) collective-permute-start(bf16[2,128,256]{2,1,0:T(8,128)(2,1)S(1)} %get-tuple-element.112), channel_id=1, source_target_pairs={{0,4},{4,0},{8,12},{12,8},{1,5},{5,1},{9,13},{13,9},{2,6},{6,2},{1... | collective-permute-start | bytes 393224 | tf_op jit(solution)/shard_map/ppermute | solution.py:770
  31.0 3.5 %shard_map.130 = (bf16[384,4096]{1,0:T(8,128)(2,1)}, bf16[256,256]{1,0:T(8,128)(2,1)S(1)}, bf16[256,256]{1,0:T(8,128)(2,1)S(1)}, f32[2,128,256]{2,1,0:T(8,128)S(...) custom-call(s32[16]{0:T(128)S(4)} %get-tuple-element.68.refs_0_, ...), custom_call_target="tpu_custom_call" | custom-call | flops 4026531840 | bytes 1000 | tf_op jit(solution)/shard_map/pallas_call | solution.py:100
  34.5 1.6 %collective-permute-start.9 = (bf16[256,256]{1,0:T(8,128)(2,1)S(1)}, bf16[256,256]{1,0:T(8,128)(2,1)S(1)}, u32[]{:S(2)}, u32[]{:S(2)}) collective-permute-start(bf16[256,256]{1,0:T(8,128)(2,1)S(1)} %get-tuple-element.114.refs_3_.refs_8_), channel_id=1, source_target_pairs={{0,2},{2,0},{1,3},{3,1},{4,6},{6,4},{5,7},{7,5},{8,10},{10,8},{9,1... | collective-permute-start | bytes 393224 | tf_op jit(solution)/shard_map/ppermute | solution.py:770
  36.1 0.9 %shard_map.131.refs_4_.refs_2_ = f32[2560,256]{1,0:T(8,128)S(1)} custom-call(s32[16]{0:T(128)S(4)} %get-tuple-element.68.refs_0_, bf16[2560,1024]{1,0:T(8,128)(2,1)S(1)} %get-tuple-element.113.refs_1_, bf16[256,256]{1,0:T(8,128)(2,1)S(1)} %get-tuple-element.90.refs_2_.refs_7_, bf16[256,256]{1,0:T(8,128)(2,1)S(1)} %get-tuple-element.114.refs_3_.refs_8_), custom_call_target="tpu_custom_call" | custom-call | flops 1000 | bytes 1000 | tf_op jit(solution)/shard_map/pallas_call | solution.py:705
  37.0 1.4 %collective-permute-done.6.refs_2_ = bf16[2,128,256]{2,1,0:T(8,128)(2,1)S(1)} collective-permute-done((bf16[2,128,256]{2,1,0:T(8,128)(2,1)S(1)}, bf16[2,128,256]{2,1,0:T(8,128)(2,1)S(1)}, u32[]{:S(2)}, u32[]{:S(2)}) %collective-permute-start.6) | collective-permute-done | bytes 131104 | tf_op jit(solution)/shard_map/ppermute | solution.py:770
  38.4 0.0 collective-permute-done.7.refs_3_
  38.4 0.1 shard_map.132
  38.5 0.1 collective-permute-start.8
  38.6 2.6 %shard_map.133 = (bf16[384,4096]{1,0:T(8,128)(2,1)}, f32[8,128]{1,0:T(8,128)S(1)}) custom-call(s32[16]{0:T(128)S(4)} %get-tuple-element.68.refs_0_, bf16[2,2,128,256]{3,2,1,0:T(8,128)(2,1)S(1)} %shard_map.126.refs_13_.refs_1_, bf16[2,2,128,256]{3,2,1,0:T(8,128)(2,1)S(1)} %collective-permute-done.3.refs_11_.refs_2_, ...), custom_call_target="tpu_custom_call", output_to_operand_aliasing={{0}: (9, {})} | custom-call | flops 1000 | bytes 1000 | tf_op jit(solution)/shard_map/pallas_call | solution.py:100
  41.2 0.0 collective-permute-done.9.refs_5_.refs_4_
  41.2 2.5 %collective-permute-done.8.refs_2_ = bf16[2,128,256]{2,1,0:T(8,128)(2,1)S(1)} collective-permute-done((bf16[2,128,256]{2,1,0:T(8,128)(2,1)S(1)}, bf16[2,128,256]{2,1,0:T(8,128)(2,1)S(1)}, u32[]{:S(2)}, u32[]{:S(2)}) %collective-permute-start.8) | collective-permute-done | bytes 131104 | tf_op jit(solution)/shard_map/ppermute | solution.py:770
  43.7 0.1 collective-permute-start.10
  43.8 1.4 %collective-permute-done.10.refs_4_ = bf16[2,128,384]{2,1,0:T(8,128)(2,1)S(1)} collective-permute-done((bf16[2,128,384]{2,1,0:T(8,128)(2,1)S(1)}, bf16[2,128,384]{2,1,0:T(8,128)(2,1)S(1)}, u32[]{:S(2)}, u32[]{:S(2)}) %collective-permute-start.10) | collective-permute-done | bytes 196640 | tf_op jit(solution)/shard_map/ppermute | solution.py:770
  45.2 0.1 shard_map.135
  45.3 1.6 %collective-permute-start.11 = (bf16[128,512]{1,0:T(8,128)(2,1)S(1)}, bf16[128,512]{1,0:T(8,128)(2,1)S(1)}, u32[]{:S(2)}, u32[]{:S(2)}) collective-permute-start(bf16[128,512]{1,0:T(8,128)(2,1)S(1)} %get-tuple-element.122.refs_2_.refs_5_), channel_id=1, source_target_pairs={{0,2},{2,0},{1,3},{3,1},{4,6},{6,4},{5,7},{7,5},{8,10},{10,8},{9,1... | collective-permute-start | bytes 393224 | tf_op jit(solution)/shard_map/ppermute | solution.py:770
  46.9 0.8 %shard_map.136.refs_9_.refs_2_ = f32[2560,128]{1,0:T(8,128)S(1)} custom-call(s32[16]{0:T(128)S(4)} %get-tuple-element.68.refs_0_, bf16[2560,1024]{1,0:T(8,128)(2,1)S(1)} %get-tuple-element.113.refs_1_, bf16[128,512]{1,0:T(8,128)(2,1)S(1)} %get-tuple-element.122.refs_2_.refs_5_), custom_call_target="tpu_custom_call" | custom-call | flops 1000 | bytes 1000 | tf_op jit(solution)/shard_map/pallas_call | solution.py:705
  47.8 2.5 %shard_map.137 = (bf16[384,2560]{1,0:T(8,128)(2,1)}, bf16[384,512]{1,0:T(8,128)(2,1)}, bf16[384,512]{1,0:T(8,128)(2,1)}, f32[8,128]{1,0:T(8,128)}) custom-call(s32[16]{0:T(128)S(4)} %get-tuple-element.68.refs_0_, bf16[2560,1024]{1,0:T(8,128)(2,1)S(1)} %get-tuple-element.113.refs_1_, f32[2560,256]{1,0:T(8,128)S(1)} %shard_map.131.refs_4_.refs_2_, ...), custom_call_target="tpu_custom_call" | custom-call | flops 1000 | bytes 1000 | tf_op jit(solution)/shard_map/pallas_call | solution.py:751
  50.3 0.7 %collective-permute-done.11.refs_3_ = bf16[128,512]{1,0:T(8,128)(2,1)S(1)} collective-permute-done((bf16[128,512]{1,0:T(8,128)(2,1)S(1)}, bf16[128,512]{1,0:T(8,128)(2,1)S(1)}, u32[]{:S(2)}, u32[]{:S(2)}) %collective-permute-start.11) | collective-permute-done | bytes 131104 | tf_op jit(solution)/shard_map/ppermute | solution.py:770
  51.0 2.3 %shard_map.138 = (bf16[384,2560]{1,0:T(8,128)(2,1)}, bf16[384,512]{1,0:T(8,128)(2,1)}, bf16[384,512]{1,0:T(8,128)(2,1)}, f32[8,128]{1,0:T(8,128)}) custom-call(s32[16]{0:T(128)S(4)} %get-tuple-element.68.refs_0_, bf16[2560,1024]{1,0:T(8,128)(2,1)S(1)} %get-tuple-element.113.refs_1_, ...), custom_call_target="tpu_custom_call", output_to_operand_aliasing={{0}: (6, {}), {1}: (7, {}), {2}: (8, {})} | custom-call | flops 1000 | bytes 1000 | tf_op jit(solution)/shard_map/pallas_call | solution.py:751
  (4 shorter events, 0.1 us)
Async XLA Ops:
  1.7 1.7 %collective-permute-start = (bf16[2,128,512]{2,1,0:T(8,128)(2,1)S(1)}, bf16[2,128,512]{2,1,0:T(8,128)(2,1)S(1)}, u32[]{:S(2)}, u32[]{:S(2)}) collective-permute-start(bf16[2,128,512]{2,1,0:T(8,128)(2,1)S(1)} %get-tuple-element.69.refs_1_.refs_7_.refs_10_), channel_id=1, source_target_pairs={{0,1},{1,0},{2,3},{3,2},{4,5},{5,4},{6,7},{7,6},{8,9},{9,8},{10,11... | collective-permute-start | bytes 786440 | tf_op jit(solution)/shard_map/ppermute | solution.py:770
  3.4 7.6 %collective-permute-start.1 = (bf16[2,128,256]{2,1,0:T(8,128)(2,1)S(1)}, bf16[2,128,256]{2,1,0:T(8,128)(2,1)S(1)}, u32[]{:S(2)}, u32[]{:S(2)}) collective-permute-start(bf16[2,128,256]{2,1,0:T(8,128)(2,1)S(1)} %shard_map.121.refs_9_.refs_1_), channel_id=1, source_target_pairs={{0,4},{4,0},{8,12},{12,8},{1,5},{5,1},{9,13},{13,9},{2,6},{6,2},{1... | collective-permute-start | bytes 393224 | tf_op jit(solution)/shard_map/ppermute | solution.py:770
  11.0 9.6 %collective-permute-start.2 = (bf16[2,128,256]{2,1,0:T(8,128)(2,1)S(1)}, bf16[2,128,256]{2,1,0:T(8,128)(2,1)S(1)}, u32[]{:S(2)}, u32[]{:S(2)}) collective-permute-start(bf16[2,128,256]{2,1,0:T(8,128)(2,1)S(1)} %shard_map.123.refs_13_.refs_3_), channel_id=1, source_target_pairs={{0,8},{4,12},{8,0},{12,4},{1,9},{5,13},{9,1},{13,5},{2,10},{6,14},... | collective-permute-start | bytes 393224 | tf_op jit(solution)/shard_map/ppermute | solution.py:770
  16.4 5.0 %collective-permute-start.4 = (bf16[256,256]{1,0:T(8,128)(2,1)S(1)}, bf16[256,256]{1,0:T(8,128)(2,1)S(1)}, u32[]{:S(2)}, u32[]{:S(2)}) collective-permute-start(bf16[256,256]{1,0:T(8,128)(2,1)S(1)} %get-tuple-element.90.refs_2_.refs_7_), channel_id=1, source_target_pairs={{0,2},{2,0},{1,3},{3,1},{4,6},{6,4},{5,7},{7,5},{8,10},{10,8},{9,1... | collective-permute-start | bytes 393224 | tf_op jit(solution)/shard_map/ppermute | solution.py:770
  20.7 4.1 %collective-permute-start.3 = (bf16[2,2,128,256]{3,2,1,0:T(8,128)(2,1)S(1)}, bf16[2,2,128,256]{3,2,1,0:T(8,128)(2,1)S(1)}, u32[]{:S(2)}, u32[]{:S(2)}) collective-permute-start(bf16[2,2,128,256]{3,2,1,0:T(8,128)(2,1)S(1)} %shard_map.126.refs_13_.refs_1_), channel_id=1, source_target_pairs={{0,1},{1,0},{2,3},{3,2},{4,5},{5,4},{6,7},{7,6},{8,9},{9,8},{10,11... | collective-permute-start | bytes 786440 | tf_op jit(solution)/shard_map/ppermute | solution.py:770
  24.7 4.0 %collective-permute-start.5 = (bf16[7,128,256]{2,1,0:T(8,128)(2,1)S(1)}, bf16[7,128,256]{2,1,0:T(8,128)(2,1)S(1)}, u32[]{:S(2)}, u32[]{:S(2)}) collective-permute-start(bf16[7,128,256]{2,1,0:T(8,128)(2,1)S(1)} %get-tuple-element.108), channel_id=1, source_target_pairs={{0,1},{1,0},{2,3},{3,2},{4,5},{5,4},{6,7},{7,6},{8,9},{9,8},{10,11... | collective-permute-start | bytes 1376264 | tf_op jit(solution)/shard_map/ppermute | solution.py:770
  28.8 9.7 %collective-permute-start.6 = (bf16[2,128,256]{2,1,0:T(8,128)(2,1)S(1)}, bf16[2,128,256]{2,1,0:T(8,128)(2,1)S(1)}, u32[]{:S(2)}, u32[]{:S(2)}) collective-permute-start(bf16[2,128,256]{2,1,0:T(8,128)(2,1)S(1)} %get-tuple-element.109.refs_17_), channel_id=1, source_target_pairs={{0,8},{4,12},{8,0},{12,4},{1,9},{5,13},{9,1},{13,5},{2,10},{6,14},... | collective-permute-start | bytes 393224 | tf_op jit(solution)/shard_map/ppermute | solution.py:770
  29.2 9.3 %collective-permute-start.7 = (bf16[2,128,256]{2,1,0:T(8,128)(2,1)S(1)}, bf16[2,128,256]{2,1,0:T(8,128)(2,1)S(1)}, u32[]{:S(2)}, u32[]{:S(2)}) collective-permute-start(bf16[2,128,256]{2,1,0:T(8,128)(2,1)S(1)} %get-tuple-element.112), channel_id=1, source_target_pairs={{0,4},{4,0},{8,12},{12,8},{1,5},{5,1},{9,13},{13,9},{2,6},{6,2},{1... | collective-permute-start | bytes 393224 | tf_op jit(solution)/shard_map/ppermute | solution.py:770
  34.5 6.7 %collective-permute-start.9 = (bf16[256,256]{1,0:T(8,128)(2,1)S(1)}, bf16[256,256]{1,0:T(8,128)(2,1)S(1)}, u32[]{:S(2)}, u32[]{:S(2)}) collective-permute-start(bf16[256,256]{1,0:T(8,128)(2,1)S(1)} %get-tuple-element.114.refs_3_.refs_8_), channel_id=1, source_target_pairs={{0,2},{2,0},{1,3},{3,1},{4,6},{6,4},{5,7},{7,5},{8,10},{10,8},{9,1... | collective-permute-start | bytes 393224 | tf_op jit(solution)/shard_map/ppermute | solution.py:770
  38.5 5.2 %collective-permute-start.8 = (bf16[2,128,256]{2,1,0:T(8,128)(2,1)S(1)}, bf16[2,128,256]{2,1,0:T(8,128)(2,1)S(1)}, u32[]{:S(2)}, u32[]{:S(2)}) collective-permute-start(bf16[2,128,256]{2,1,0:T(8,128)(2,1)S(1)} %get-tuple-element.115.refs_10_), channel_id=1, source_target_pairs={{0,4},{4,0},{8,12},{12,8},{1,5},{5,1},{9,13},{13,9},{2,6},{6,2},{1... | collective-permute-start | bytes 393224 | tf_op jit(solution)/shard_map/ppermute | solution.py:770
  43.7 1.5 %collective-permute-start.10 = (bf16[2,128,384]{2,1,0:T(8,128)(2,1)S(1)}, bf16[2,128,384]{2,1,0:T(8,128)(2,1)S(1)}, u32[]{:S(2)}, u32[]{:S(2)}) collective-permute-start(bf16[2,128,384]{2,1,0:T(8,128)(2,1)S(1)} %shard_map.134.refs_3_), channel_id=1, source_target_pairs={{0,1},{1,0},{2,3},{3,2},{4,5},{5,4},{6,7},{7,6},{8,9},{9,8},{10,11... | collective-permute-start | bytes 589832 | tf_op jit(solution)/shard_map/ppermute | solution.py:770
  45.3 5.6 %collective-permute-start.11 = (bf16[128,512]{1,0:T(8,128)(2,1)S(1)}, bf16[128,512]{1,0:T(8,128)(2,1)S(1)}, u32[]{:S(2)}, u32[]{:S(2)}) collective-permute-start(bf16[128,512]{1,0:T(8,128)(2,1)S(1)} %get-tuple-element.122.refs_2_.refs_5_), channel_id=1, source_target_pairs={{0,2},{2,0},{1,3},{3,1},{4,6},{6,4},{5,7},{7,5},{8,10},{10,8},{9,1... | collective-permute-start | bytes 393224 | tf_op jit(solution)/shard_map/ppermute | solution.py:770

commit v14 on v13

--- a/solution.py
+++ b/solution.py
@@ -368,8 +368,11 @@
         if ride is not None:
             (out,) = results
             for kind in range(2):
-                out[4 + kind] = near_ref(("ride", 0))[kind]
-                out[6, :, kind * HD : (kind + 1) * HD] = near_ref(("ride", 1))[kind]
+                more = jnp.concatenate(
+                    [near_ref(("ride", i))[kind] for i in range(len(ride))], axis=1
+                )
+                out[4 + kind] = more[:, :width]
+                out[6, :, kind * HD : (kind + 1) * HD] = more[:, width:]
         owns2 = facts[OWNS2] == 1
         if loading:
             arrived(*shared_loads)
@@ -860,8 +863,10 @@
     part = order.half * HD
     width = 2 * part
 
-    def body(facts, own_first, own_second, mine_r, far_r, low_r, dk, dv):
+    def body(facts, *refs):
+        mine_r, far_r, low_r, dk, dv = refs[len(own0) :]
         owns2 = facts[OWNS2] == 1
+        own_r = [(r, at) for r in refs[: len(own0)] for at in range(0, r.shape[-1], HD)]
         ok = row_ok(facts[N0], PAGE, HD)
         for head in range(order.heads):
             c = slice(head * HD, (head + 1) * HD)
@@ -869,9 +874,9 @@
             here = slice(at, at + HD)
             theirs = head ^ order.half
             for kind, out in enumerate((dk, dv)):
-                first = head < order.half
-                gained = (far_r if first else mine_r)[kind, :, here]
-                base = (own_first if first else own_second)[kind, :, here]
+                gained = (far_r if head < order.half else mine_r)[kind, :, here]
+                ref, start_at = own_r[head]
+                base = ref[kind, :, start_at : start_at + HD]
                 if theirs < order.half:
                     level2 = low_r[4 + kind, :, theirs * HD : (theirs + 1) * HD]
                 elif theirs + 1 < order.heads:
@@ -945,24 +950,22 @@
             return (by_head[0][3],)
 
         def beside_half(pair):
-            by_head.append(own_pages(kvs[1:2], level2, by_head[0], (pair,)))
-            far_v.append(spread(by_head[1][1]))
-            by_head.append(own_pages(kvs[2:3], level2, after=(by_head[1][3],)))
-            return (by_head[2][3],)
+            by_head.append(own_pages(kvs[1:3], level2, by_head[0], (pair,)))
+            return (by_head[1][3],)
 
         mine, theirs = gather_small_tree(facts, own, beside_pair, beside_half)
-        first, third = by_head[1:]
-        sent = shared_pages(kvs[:2], mine, (first[3], third[3]), far_v)
+        most = by_head[1]
+        sent = shared_pages(kvs[:2], mine, (most[3],))
         sent = flipped(sent, "sub", 1)
         kept = shared_pages(kvs[2:], theirs)
         total, root, root_far, next_far = over_cores(facts, kept, sent)
-        *second, w_near = own_pages(kvs[3:], level2, third, (root,), w)
-        both = list(zip(first, second))
+        *last, w_near = own_pages(kvs[3:], level2, most, (root,), w)
+        both = [[piece] for piece in last]
         begun = begin_input_grad(order, facts, w_near, both[1])
-        far_v.append(spread(second[1]))
+        far_v.append(spread(last[1]))
         total, low, far = over_halves(facts, total, root_far, next_far, (begun,))
         made = finish_queries(kvs[:3], group, order, facts, (mine, theirs), state, (low,))
-        near, far = over_chips(facts, total, far, second[3], (made, far_v[1]))
+        near, far = over_chips(facts, total, far, last[3], (made, *far_v))
         dk0, dv0 = finish_small_tree(order, facts, both[2], near, far, sent)
         far_0 = spread(dv0)
         begun_0 = begin_input_grad(order, facts, w_near, [dv0])

time: 53.6 us -> 53.5 us (level)
  Pallas kernels: 31.1 us -> 32 us
  waiting for transfers between devices: 7.88 us -> 6.99 us
    ppermute x12 -> x11, waiting for transfers between devices: 7.88 us -> 6.99 us  [flipped(): lax.ppermute(block, axis, [(i, i ^ bit) for i in range(count) if i ^ bit...]
    pallas_call x14 -> x13, Pallas kernels: 23.6 us -> 24.5 us  [kernel_call(): pl.pallas_call(kernel, out_shape=tuple((pltpu.VMEM(s, d) if inside else j...]
    ppermute x12 -> x11, starting transfers between devices: 13.4 us -> 13.3 us  [flipped(): lax.ppermute(block, axis, [(i, i ^ bit) for i in range(count) if i ^ bit...]
  transfers between devices with their start and end apart: 12 -> 11, of which waited for: 6 -> 6; matrix products, arithmetic and copies ran while one was open for 0% -> 0% of each run, Pallas kernels for 52% -> 53%
where the time goes in v14:
time: 53.5 us; the launch traced here: 53.3 us
  Pallas kernels  32 us (60%)
  starting transfers between devices  13.3 us (25%)
  waiting for transfers between devices  6.99 us (13%)
  between operations  0.95 us (2%)
    pallas_call x13, Pallas kernels, kernel_call(): pl.pallas_call(kernel, out_shape=tuple((pltpu.VMEM(s, d) if inside else j...  24.5 us
    ppermute x11, starting transfers between devices, flipped(): lax.ppermute(block, axis, [(i, i ^ bit) for i in range(count) if i ^ bit...  13.3 us
    ppermute x11, waiting for transfers between devices, flipped(): lax.ppermute(block, axis, [(i, i ^ bit) for i in range(count) if i ^ bit...  6.99 us
    pallas_call x2, Pallas kernels, end_input_grad(): pl.pallas_call(kernel, out_shape=(jax.ShapeDtypeStruct((ROWS, out_cols),...  4.82 us
    pallas_call x2, Pallas kernels, begin_input_grad(): pl.pallas_call(kernel, out_shape=pltpu.VMEM((out_cols, rows), F32), in_sp...  1.73 us
  transfers between devices with their start and end apart: 11, of which 6 were waited for; matrix products, arithmetic and copies ran while one was open for 0% of the time, Pallas kernels for 53%

profile of v14, /device:TPU:0, one launch (start us, length us, event | category | flops | bytes accessed | tf_op | source)
XLA Modules:
  0.0 53.3 jit_solution(12667839003247164632)
XLA Ops:
  0.6 1.0 %shard_map.120 = (s32[16]{0:T(128)S(4)}, bf16[2,128,512]{2,1,0:T(8,128)(2,1)S(1)}) custom-call(s32[1]{0:T(128)} %bitcast.side_ref, s32[1,5]{1,0:T(1,128)} %ids_ref.1, s32[1,3]{1,0:T(1,128)} %counts_ref.1, bf16[384,512]{1,0:T(8,128)(2,1)} %refs_5_.1, bf16[384,512]{1,0:T(8,128)(2,1)} %refs_6_.1), custom_call_target="tpu_custom_call" | custom-call | tf_op jit(solution)/shard_map/pallas_call | solution.py:141
  1.7 0.5 collective-permute-start
  2.2 1.2 %collective-permute-done.refs_2_.refs_10_.refs_11_ = bf16[2,128,512]{2,1,0:T(8,128)(2,1)S(1)} collective-permute-done((bf16[2,128,512]{2,1,0:T(8,128)(2,1)S(1)}, bf16[2,128,512]{2,1,0:T(8,128)(2,1)S(1)}, u32[]{:S(2)}, u32[]{:S(2)}) %collective-permute-start) | collective-permute-done | bytes 262176 | tf_op jit(solution)/shard_map/ppermute | solution.py:773
  3.4 3.0 %collective-permute-start.1 = (bf16[2,128,256]{2,1,0:T(8,128)(2,1)S(1)}, bf16[2,128,256]{2,1,0:T(8,128)(2,1)S(1)}, u32[]{:S(2)}, u32[]{:S(2)}) collective-permute-start(bf16[2,128,256]{2,1,0:T(8,128)(2,1)S(1)} %shard_map.121.refs_9_.refs_1_), channel_id=1, source_target_pairs={{0,4},{4,0},{8,12},{12,8},{1,5},{5,1},{9,13},{13,9},{2,6},{6,2},{1... | collective-permute-start | bytes 393224 | tf_op jit(solution)/shard_map/ppermute | solution.py:773
  6.4 4.6 %shard_map.122 = (f32[384,1024]{1,0:T(8,128)S(1)}, bf16[128,3072]{1,0:T(8,128)(2,1)S(1)}, bf16[128,3072]{1,0:T(8,128)(2,1)S(1)}, bf16[256,128]{1,0:T(8,128)(2,1)...) custom-call(s32[16]{0:T(128)S(4)} %get-tuple-element.64.refs_0_, ...), custom_call_target="tpu_custom_call" | custom-call | flops 4026531840 | bytes 1000 | tf_op jit(solution)/shard_map/pallas_call | solution.py:100
  11.0 0.0 collective-permute-done.1.refs_2_
  11.0 2.7 %collective-permute-start.2 = (bf16[2,128,256]{2,1,0:T(8,128)(2,1)S(1)}, bf16[2,128,256]{2,1,0:T(8,128)(2,1)S(1)}, u32[]{:S(2)}, u32[]{:S(2)}) collective-permute-start(bf16[2,128,256]{2,1,0:T(8,128)(2,1)S(1)} %shard_map.123.refs_15_.refs_3_), channel_id=1, source_target_pairs={{0,8},{4,12},{8,0},{12,4},{1,9},{5,13},{9,1},{13,5},{2,10},{6,14},... | collective-permute-start | bytes 393224 | tf_op jit(solution)/shard_map/ppermute | solution.py:773
  13.6 5.0 %shard_map.124 = (f32[384,1024]{1,0:T(8,128)S(1)}, bf16[128,3072]{1,0:T(8,128)(2,1)S(1)}, bf16[128,3072]{1,0:T(8,128)(2,1)S(1)}, f32[384,1024]{1,0:T(8,128)S(1)}...) custom-call(s32[16]{0:T(128)S(4)} %get-tuple-element.64.refs_0_, ...), custom_call_target="tpu_custom_call" | custom-call | flops 8053063680 | bytes 1000 | tf_op jit(solution)/shard_map/pallas_call | solution.py:100
  18.6 1.2 %collective-permute-done.2.refs_4_ = bf16[2,128,256]{2,1,0:T(8,128)(2,1)S(1)} collective-permute-done((bf16[2,128,256]{2,1,0:T(8,128)(2,1)S(1)}, bf16[2,128,256]{2,1,0:T(8,128)(2,1)S(1)}, u32[]{:S(2)}, u32[]{:S(2)}) %collective-permute-start.2) | collective-permute-done | bytes 131104 | tf_op jit(solution)/shard_map/ppermute | solution.py:773
  19.9 0.1 collective-permute-start.3
  19.9 3.3 %shard_map.126 = (bf16[3072,256]{1,0:T(8,128)(2,1)S(1)}, bf16[3072,256]{1,0:T(8,128)(2,1)S(1)}, bf16[7,128,256]{2,1,0:T(8,128)(2,1)S(1)}) custom-call(s32[16]{0:T(128)S(4)} %get-tuple-element.64.refs_0_, bf16[128,3072]{1,0:T(8,128)(2,1)S(1)} %get-tuple-element.79.refs_1_, bf16[128,3072]{1,0:T(8,128)(2,1)S(1)} %get-tuple-element.80.refs_2_, ...), custom_call_target="tpu_custom_call" | custom-call | flops 8053063680 | bytes 1000 | tf_op jit(solution)/shard_map/pallas_call | solution.py:100
  23.3 0.5 %collective-permute-start.4 = (bf16[7,128,256]{2,1,0:T(8,128)(2,1)S(1)}, bf16[7,128,256]{2,1,0:T(8,128)(2,1)S(1)}, u32[]{:S(2)}, u32[]{:S(2)}) collective-permute-start(bf16[7,128,256]{2,1,0:T(8,128)(2,1)S(1)} %get-tuple-element.102), channel_id=1, source_target_pairs={{0,1},{1,0},{2,3},{3,2},{4,5},{5,4},{6,7},{7,6},{8,9},{9,8},{10,11... | collective-permute-start | bytes 1376264 | tf_op jit(solution)/shard_map/ppermute | solution.py:773
  23.8 0.0 collective-permute-done.3.refs_11_.refs_2_
  23.8 3.9 %shard_map.127 = (bf16[3072,256]{1,0:T(8,128)(2,1)S(1)}, f32[384,1024]{1,0:T(8,128)S(1)}, bf16[128,3072]{1,0:T(8,128)(2,1)S(1)}, bf16[128,3072]{1,0:T(8,128)(2,1)S(1)}, f32[4,128,256]{2,1,0:T(8,128)S(1)}) custom-call(s32[16]{0:T(128)S(4)} %get-tuple-element.64.refs_0_, bf16[128,3072]{1,0:T(8,128)(2,1)S(1)} %get-tuple-element.89.refs_1_, ...), custom_call_target="tpu_custom_call" | custom-call | flops 8053063680 | bytes 1000 | tf_op jit(solution)/shard_map/pallas_call | solution.py:100
  27.7 0.0 collective-permute-done.4.refs_2_.refs_4_
  27.7 0.1 shard_map.128
  27.8 0.1 collective-permute-start.5
  27.9 3.2 %collective-permute-start.6 = (bf16[2,128,256]{2,1,0:T(8,128)(2,1)S(1)}, bf16[2,128,256]{2,1,0:T(8,128)(2,1)S(1)}, u32[]{:S(2)}, u32[]{:S(2)}) collective-permute-start(bf16[2,128,256]{2,1,0:T(8,128)(2,1)S(1)} %get-tuple-element.106), channel_id=1, source_target_pairs={{0,4},{4,0},{8,12},{12,8},{1,5},{5,1},{9,13},{13,9},{2,6},{6,2},{1... | collective-permute-start | bytes 393224 | tf_op jit(solution)/shard_map/ppermute | solution.py:773
  31.1 4.8 %shard_map.129 = (bf16[384,4096]{1,0:T(8,128)(2,1)}, bf16[256,512]{1,0:T(8,128)(2,1)S(1)}, bf16[256,512]{1,0:T(8,128)(2,1)S(1)}, f32[2,128,512]{2,1,0:T(8,128)S(...) custom-call(s32[16]{0:T(128)S(4)} %get-tuple-element.64.refs_0_, ...), custom_call_target="tpu_custom_call" | custom-call | flops 4026531840 | bytes 1000 | tf_op jit(solution)/shard_map/pallas_call | solution.py:100
  35.8 1.6 %collective-permute-start.8 = (bf16[256,512]{1,0:T(8,128)(2,1)S(1)}, bf16[256,512]{1,0:T(8,128)(2,1)S(1)}, u32[]{:S(2)}, u32[]{:S(2)}) collective-permute-start(bf16[256,512]{1,0:T(8,128)(2,1)S(1)} %get-tuple-element.108.refs_2_.refs_5_), channel_id=1, source_target_pairs={{0,2},{2,0},{1,3},{3,1},{4,6},{6,4},{5,7},{7,5},{8,10},{10,8},{9,1... | collective-permute-start | bytes 786440 | tf_op jit(solution)/shard_map/ppermute | solution.py:773
  37.4 0.9 %shard_map.130.refs_4_.refs_2_ = f32[2560,256]{1,0:T(8,128)S(1)} custom-call(s32[16]{0:T(128)S(4)} %get-tuple-element.64.refs_0_, bf16[2560,1024]{1,0:T(8,128)(2,1)S(1)} %get-tuple-element.107.refs_1_, bf16[256,512]{1,0:T(8,128)(2,1)S(1)} %get-tuple-element.108.refs_2_.refs_5_), custom_call_target="tpu_custom_call" | custom-call | flops 1000 | bytes 1000 | tf_op jit(solution)/shard_map/pallas_call | solution.py:708
  38.3 0.0 collective-permute-done.5.refs_2_
  38.3 0.0 collective-permute-done.6.refs_3_
  38.3 0.1 shard_map.131
  38.4 0.1 collective-permute-start.7
  38.5 2.6 %shard_map.132 = (bf16[384,4096]{1,0:T(8,128)(2,1)}, f32[8,128]{1,0:T(8,128)S(1)}) custom-call(s32[16]{0:T(128)S(4)} %get-tuple-element.64.refs_0_, bf16[2,2,128,256]{3,2,1,0:T(8,128)(2,1)S(1)} %shard_map.125.refs_13_.refs_1_, bf16[2,2,128,256]{3,2,1,0:T(8,128)(2,1)S(1)} %collective-permute-done.3.refs_11_.refs_2_, ...), custom_call_target="tpu_custom_call", output_to_operand_aliasing={{0}: (9, {})} | custom-call | flops 1000 | bytes 1000 | tf_op jit(solution)/shard_map/pallas_call | solution.py:100
  41.1 2.3 %collective-permute-done.7.refs_2_ = bf16[2,128,256]{2,1,0:T(8,128)(2,1)S(1)} collective-permute-done((bf16[2,128,256]{2,1,0:T(8,128)(2,1)S(1)}, bf16[2,128,256]{2,1,0:T(8,128)(2,1)S(1)}, u32[]{:S(2)}, u32[]{:S(2)}) %collective-permute-start.7) | collective-permute-done | bytes 131104 | tf_op jit(solution)/shard_map/ppermute | solution.py:773
  43.4 0.2 collective-permute-done.8.refs_5_.refs_3_
  43.6 0.1 collective-permute-start.9
  43.7 1.4 %collective-permute-done.9.refs_3_ = bf16[2,128,384]{2,1,0:T(8,128)(2,1)S(1)} collective-permute-done((bf16[2,128,384]{2,1,0:T(8,128)(2,1)S(1)}, bf16[2,128,384]{2,1,0:T(8,128)(2,1)S(1)}, u32[]{:S(2)}, u32[]{:S(2)}) %collective-permute-start.9) | collective-permute-done | bytes 196640 | tf_op jit(solution)/shard_map/ppermute | solution.py:773
  45.1 0.1 shard_map.134
  45.2 1.6 %collective-permute-start.10 = (bf16[128,512]{1,0:T(8,128)(2,1)S(1)}, bf16[128,512]{1,0:T(8,128)(2,1)S(1)}, u32[]{:S(2)}, u32[]{:S(2)}) collective-permute-start(bf16[128,512]{1,0:T(8,128)(2,1)S(1)} %get-tuple-element.115.refs_2_.refs_5_), channel_id=1, source_target_pairs={{0,2},{2,0},{1,3},{3,1},{4,6},{6,4},{5,7},{7,5},{8,10},{10,8},{9,1... | collective-permute-start | bytes 393224 | tf_op jit(solution)/shard_map/ppermute | solution.py:773
  46.8 0.8 %shard_map.135.refs_6_.refs_2_ = f32[2560,128]{1,0:T(8,128)S(1)} custom-call(s32[16]{0:T(128)S(4)} %get-tuple-element.64.refs_0_, bf16[2560,1024]{1,0:T(8,128)(2,1)S(1)} %get-tuple-element.107.refs_1_, bf16[128,512]{1,0:T(8,128)(2,1)S(1)} %get-tuple-element.115.refs_2_.refs_5_), custom_call_target="tpu_custom_call" | custom-call | flops 1000 | bytes 1000 | tf_op jit(solution)/shard_map/pallas_call | solution.py:708
  47.6 2.5 %shard_map.136 = (bf16[384,2560]{1,0:T(8,128)(2,1)}, bf16[384,512]{1,0:T(8,128)(2,1)}, bf16[384,512]{1,0:T(8,128)(2,1)}, f32[8,128]{1,0:T(8,128)}) custom-call(s32[16]{0:T(128)S(4)} %get-tuple-element.64.refs_0_, bf16[2560,1024]{1,0:T(8,128)(2,1)S(1)} %get-tuple-element.107.refs_1_, f32[2560,256]{1,0:T(8,128)S(1)} %shard_map.130.refs_4_.refs_2_, ...), custom_call_target="tpu_custom_call" | custom-call | flops 1000 | bytes 1000 | tf_op jit(solution)/shard_map/pallas_call | solution.py:754
  50.2 0.7 %collective-permute-done.10.refs_3_ = bf16[128,512]{1,0:T(8,128)(2,1)S(1)} collective-permute-done((bf16[128,512]{1,0:T(8,128)(2,1)S(1)}, bf16[128,512]{1,0:T(8,128)(2,1)S(1)}, u32[]{:S(2)}, u32[]{:S(2)}) %collective-permute-start.10) | collective-permute-done | bytes 131104 | tf_op jit(solution)/shard_map/ppermute | solution.py:773
  50.9 2.3 %shard_map.137 = (bf16[384,2560]{1,0:T(8,128)(2,1)}, bf16[384,512]{1,0:T(8,128)(2,1)}, bf16[384,512]{1,0:T(8,128)(2,1)}, f32[8,128]{1,0:T(8,128)}) custom-call(s32[16]{0:T(128)S(4)} %get-tuple-element.64.refs_0_, bf16[2560,1024]{1,0:T(8,128)(2,1)S(1)} %get-tuple-element.107.refs_1_, ...), custom_call_target="tpu_custom_call", output_to_operand_aliasing={{0}: (6, {}), {1}: (7, {}), {2}: (8, {})} | custom-call | flops 1000 | bytes 1000 | tf_op jit(solution)/shard_map/pallas_call | solution.py:754
  (4 shorter events, 0.1 us)
Async XLA Ops:
  1.7 1.7 %collective-permute-start = (bf16[2,128,512]{2,1,0:T(8,128)(2,1)S(1)}, bf16[2,128,512]{2,1,0:T(8,128)(2,1)S(1)}, u32[]{:S(2)}, u32[]{:S(2)}) collective-permute-start(bf16[2,128,512]{2,1,0:T(8,128)(2,1)S(1)} %get-tuple-element.65.refs_1_.refs_9_.refs_10_), channel_id=1, source_target_pairs={{0,1},{1,0},{2,3},{3,2},{4,5},{5,4},{6,7},{7,6},{8,9},{9,8},{10,11... | collective-permute-start | bytes 786440 | tf_op jit(solution)/shard_map/ppermute | solution.py:773
  3.4 7.6 %collective-permute-start.1 = (bf16[2,128,256]{2,1,0:T(8,128)(2,1)S(1)}, bf16[2,128,256]{2,1,0:T(8,128)(2,1)S(1)}, u32[]{:S(2)}, u32[]{:S(2)}) collective-permute-start(bf16[2,128,256]{2,1,0:T(8,128)(2,1)S(1)} %shard_map.121.refs_9_.refs_1_), channel_id=1, source_target_pairs={{0,4},{4,0},{8,12},{12,8},{1,5},{5,1},{9,13},{13,9},{2,6},{6,2},{1... | collective-permute-start | bytes 393224 | tf_op jit(solution)/shard_map/ppermute | solution.py:773
  11.0 8.8 %collective-permute-start.2 = (bf16[2,128,256]{2,1,0:T(8,128)(2,1)S(1)}, bf16[2,128,256]{2,1,0:T(8,128)(2,1)S(1)}, u32[]{:S(2)}, u32[]{:S(2)}) collective-permute-start(bf16[2,128,256]{2,1,0:T(8,128)(2,1)S(1)} %shard_map.123.refs_15_.refs_3_), channel_id=1, source_target_pairs={{0,8},{4,12},{8,0},{12,4},{1,9},{5,13},{9,1},{13,5},{2,10},{6,14},... | collective-permute-start | bytes 393224 | tf_op jit(solution)/shard_map/ppermute | solution.py:773
  19.9 3.9 %collective-permute-start.3 = (bf16[2,2,128,256]{3,2,1,0:T(8,128)(2,1)S(1)}, bf16[2,2,128,256]{3,2,1,0:T(8,128)(2,1)S(1)}, u32[]{:S(2)}, u32[]{:S(2)}) collective-permute-start(bf16[2,2,128,256]{3,2,1,0:T(8,128)(2,1)S(1)} %shard_map.125.refs_13_.refs_1_), channel_id=1, source_target_pairs={{0,1},{1,0},{2,3},{3,2},{4,5},{5,4},{6,7},{7,6},{8,9},{9,8},{10,11... | collective-permute-start | bytes 786440 | tf_op jit(solution)/shard_map/ppermute | solution.py:773
  23.3 4.5 %collective-permute-start.4 = (bf16[7,128,256]{2,1,0:T(8,128)(2,1)S(1)}, bf16[7,128,256]{2,1,0:T(8,128)(2,1)S(1)}, u32[]{:S(2)}, u32[]{:S(2)}) collective-permute-start(bf16[7,128,256]{2,1,0:T(8,128)(2,1)S(1)} %get-tuple-element.102), channel_id=1, source_target_pairs={{0,1},{1,0},{2,3},{3,2},{4,5},{5,4},{6,7},{7,6},{8,9},{9,8},{10,11... | collective-permute-start | bytes 1376264 | tf_op jit(solution)/shard_map/ppermute | solution.py:773
  27.8 10.5 %collective-permute-start.5 = (bf16[2,128,256]{2,1,0:T(8,128)(2,1)S(1)}, bf16[2,128,256]{2,1,0:T(8,128)(2,1)S(1)}, u32[]{:S(2)}, u32[]{:S(2)}) collective-permute-start(bf16[2,128,256]{2,1,0:T(8,128)(2,1)S(1)} %get-tuple-element.103.refs_17_), channel_id=1, source_target_pairs={{0,8},{4,12},{8,0},{12,4},{1,9},{5,13},{9,1},{13,5},{2,10},{6,14},... | collective-permute-start | bytes 393224 | tf_op jit(solution)/shard_map/ppermute | solution.py:773
  27.9 10.4 %collective-permute-start.6 = (bf16[2,128,256]{2,1,0:T(8,128)(2,1)S(1)}, bf16[2,128,256]{2,1,0:T(8,128)(2,1)S(1)}, u32[]{:S(2)}, u32[]{:S(2)}) collective-permute-start(bf16[2,128,256]{2,1,0:T(8,128)(2,1)S(1)} %get-tuple-element.106), channel_id=1, source_target_pairs={{0,4},{4,0},{8,12},{12,8},{1,5},{5,1},{9,13},{13,9},{2,6},{6,2},{1... | collective-permute-start | bytes 393224 | tf_op jit(solution)/shard_map/ppermute | solution.py:773
  35.8 7.7 %collective-permute-start.8 = (bf16[256,512]{1,0:T(8,128)(2,1)S(1)}, bf16[256,512]{1,0:T(8,128)(2,1)S(1)}, u32[]{:S(2)}, u32[]{:S(2)}) collective-permute-start(bf16[256,512]{1,0:T(8,128)(2,1)S(1)} %get-tuple-element.108.refs_2_.refs_5_), channel_id=1, source_target_pairs={{0,2},{2,0},{1,3},{3,1},{4,6},{6,4},{5,7},{7,5},{8,10},{10,8},{9,1... | collective-permute-start | bytes 786440 | tf_op jit(solution)/shard_map/ppermute | solution.py:773
  38.4 5.0 %collective-permute-start.7 = (bf16[2,128,256]{2,1,0:T(8,128)(2,1)S(1)}, bf16[2,128,256]{2,1,0:T(8,128)(2,1)S(1)}, u32[]{:S(2)}, u32[]{:S(2)}) collective-permute-start(bf16[2,128,256]{2,1,0:T(8,128)(2,1)S(1)} %get-tuple-element.109.refs_10_), channel_id=1, source_target_pairs={{0,4},{4,0},{8,12},{12,8},{1,5},{5,1},{9,13},{13,9},{2,6},{6,2},{1... | collective-permute-start | bytes 393224 | tf_op jit(solution)/shard_map/ppermute | solution.py:773
  43.6 1.5 %collective-permute-start.9 = (bf16[2,128,384]{2,1,0:T(8,128)(2,1)S(1)}, bf16[2,128,384]{2,1,0:T(8,128)(2,1)S(1)}, u32[]{:S(2)}, u32[]{:S(2)}) collective-permute-start(bf16[2,128,384]{2,1,0:T(8,128)(2,1)S(1)} %shard_map.133.refs_2_), channel_id=1, source_target_pairs={{0,1},{1,0},{2,3},{3,2},{4,5},{5,4},{6,7},{7,6},{8,9},{9,8},{10,11... | collective-permute-start | bytes 589832 | tf_op jit(solution)/shard_map/ppermute | solution.py:773
  45.2 5.6 %collective-permute-start.10 = (bf16[128,512]{1,0:T(8,128)(2,1)S(1)}, bf16[128,512]{1,0:T(8,128)(2,1)S(1)}, u32[]{:S(2)}, u32[]{:S(2)}) collective-permute-start(bf16[128,512]{1,0:T(8,128)(2,1)S(1)} %get-tuple-element.115.refs_2_.refs_5_), channel_id=1, source_target_pairs={{0,2},{2,0},{1,3},{3,1},{4,6},{6,4},{5,7},{7,5},{8,10},{10,8},{9,1... | collective-permute-start | bytes 393224 | tf_op jit(solution)/shard_map/ppermute | solution.py:773

commit v15 on v14

--- a/solution.py
+++ b/solution.py
@@ -226,7 +226,7 @@
     return p.astype(BF16), (p * grads).astype(BF16)
 
 
-def attend(own, kvs, group, order, facts, inputs, pages, state, prior=(), after=(), w=None,
+def attend(own, kvs, group, order, facts, inputs, pages, state, prior=(), after=(),
            ride=None):
     loading = "k" not in state
     q_all, k_all = inputs[0], inputs[2]
@@ -297,10 +297,6 @@
         for kv in kvs:
             for name in ("q", "g"):
                 add_near((name, kv), state[name, kv])
-    at_end = len(outs)
-    if w is not None:
-        add_far("w", w)
-        outs.append((w.shape, w.dtype, True))
     for i, page in enumerate(pages):
         add_near(("page", i), page)
     for i, array in enumerate(prior):
@@ -317,7 +313,7 @@
         pltpu.VMEM((ROWS, HD), BF16),
         pltpu.VMEM((count * parts, ROWS, wide), BF16),
         pltpu.SemaphoreType.DMA((count * parts,)),
-        pltpu.SemaphoreType.DMA((2 * kv_total + 9,)),
+        pltpu.SemaphoreType.DMA((2 * kv_total + 8,)),
     ]
     cols = lambda a, b: slice(a * PAGE, b * PAGE)
 
@@ -349,11 +345,6 @@
                 at = pl.ds(order.at(facts, kv, group * HD), group * HD)
                 for name in ("q", "g"):
                     load((name, kv), far_ref(name).at[:, at], held((name, kv)))
-        if w is not None:
-            w_copy = pltpu.make_async_copy(
-                far_ref("w"), out_refs[at_end], load_sem.at[2 * kv_total + 8]
-            )
-            w_copy.start()
         k, v, norms, deltas = (held(name) for name in ("k", "v", "norms", "deltas"))
 
         def arrived(*keys):
@@ -535,8 +526,6 @@
         for c in sends:
             c.wait()
         arrived(*list(copies))
-        if w is not None:
-            w_copy.wait()
 
     made = kernel_call(
         body, facts, near, far, outs, scratch, aliases, after,
@@ -547,7 +536,7 @@
     )
     for name, at in at_out.items():
         state[name] = made[at]
-    return list(made[at_results:at_loaded]) + list(made[at_end:])
+    return list(made[at_results:at_loaded])
 
 
 def width_tiles(w):
@@ -555,7 +544,7 @@
     return [slice(i, i + tile) for i in range(0, w.shape[0], tile)]
 
 
-def finish_queries(kvs, group, order, facts, pages, state, after=()):
+def finish_queries(kvs, group, order, facts, pages, state, after=(), w=None):
     parts = group // min(4, group)
     heads = group // parts
     tall = heads * PAGE
@@ -565,7 +554,13 @@
         near += [state["ds", kv], state["dq", kv]]
 
     def body(facts, *refs):
-        gq, made, stage, sem = refs[-4:]
+        stage, sem = refs[-2:]
+        if w is not None:
+            gq, made, w_near = refs[-5:-2]
+            w_copy = pltpu.make_async_copy(refs[-6], w_near, sem.at[len(kvs) * parts])
+            w_copy.start()
+        else:
+            gq, made = refs[-4:-2]
         made[...] = jnp.zeros_like(made)
         sends = []
         for n, kv in enumerate(kvs):
@@ -589,51 +584,63 @@
                 sends[-1].start()
         for c in sends:
             c.wait()
+        if w is not None:
+            w_copy.wait()
 
     count = len(kvs) * parts
     far = [state["gq"]] if "gq" in state else []
+    aliases = {("far", 0): 0} if far else {}
     shape = (ROWS, state["k"].shape[1] * group)
-    state["gq"], made = kernel_call(
-        body, facts, near, far, [(shape, BF16, False), ((8, HD), F32, True)],
-        [pltpu.VMEM((count, ROWS, wide), BF16), pltpu.SemaphoreType.DMA((count,))],
-        {("far", 0): 0} if far else {}, after, limit=LARGE,
+    outs = [(shape, BF16, False), ((8, HD), F32, True)]
+    if w is not None:
+        far = far + [w]
+        outs.append((w.shape, w.dtype, True))
+    state["gq"], *made = kernel_call(
+        body, facts, near, far, outs,
+        [pltpu.VMEM((count, ROWS, wide), BF16), pltpu.SemaphoreType.DMA((count + 1,))],
+        aliases, after, limit=LARGE,
     )
     return made
 
 
-def input_grad(order, facts, w, rows, own, far, grads, carry=None):
+def input_grad(order, facts, w, rows, own, far, grads, carry=None, near_w=False, after=()):
     out_cols, depth = w.shape
     tiles = width_tiles(w)
     top = 0 if rows == PAGE else PAGE
     steps = len(tiles)
     width = sum(a.shape[1] for a in grads[0])
-    arrays = [*own, *far, *grads[0], *grads[1]]
+    arrays = [*own, *far, *grads[0], *grads[1]] + [w] * near_w
     count = len(grads[0])
     carry = list(carry or [])
+    lead = [] if near_w else [w]
+    rest = [*lead, *carry, *after]
 
     def body(facts, *refs):
         own_r, refs = refs[: len(own)], refs[len(own) :]
         far_r, refs = refs[: len(far)], refs[len(far) :]
         grad_r, w_ref = refs[: 2 * count], refs[2 * count]
         out, dk, dv, made, w_near, stage, w_sem, sem = refs[-8:]
-        loads = [
-            pltpu.make_async_copy(w_ref.at[at], w_near.at[at], w_sem.at[i])
-            for i, at in enumerate(tiles)
-        ]
+        loads = []
+        if not near_w:
+            loads = [
+                pltpu.make_async_copy(w_ref.at[at], w_near.at[at], w_sem.at[i])
+                for i, at in enumerate(tiles)
+            ]
         for c in loads:
             c.start()
         made[...] = jnp.zeros_like(made)
         columns = lambda rs: jnp.concatenate([r[...] for r in rs], axis=1)
-        full = columns(own_r)
+        full = order.real(facts, columns(own_r))
         if far:
-            other, leads = columns(far_r), facts[SIDE] == 0
+            other, first = order.real(facts, columns(far_r)), facts[SIDE] == 0
             full = jnp.concatenate(
-                [jnp.where(leads, full, other), jnp.where(leads, other, full)], axis=1
+                [jnp.where(first, full, other), jnp.where(first, other, full)], axis=1
             )
         copies = put_rows(order, facts, grad_r, dk, dv, top, rows, sem, steps)
         for i, at in enumerate(tiles):
-            loads[i].wait()
-            stage[i] = dot_t(w_near[at], full).astype(BF16).T
+            if loads:
+                loads[i].wait()
+            stage[i] = dot_t((w_ref if near_w else w_near)[at], full).astype(BF16).T
             copies.append(
                 pltpu.make_async_copy(stage.at[i], out.at[top : top + rows, at], sem.at[i])
             )
@@ -651,18 +658,20 @@
         out_shape=(
             jax.ShapeDtypeStruct((ROWS, out_cols), BF16), kept, kept, pltpu.VMEM((8, HD), F32)
         ),
-        in_specs=[smem] + [vmem] * len(arrays) + [hbm] * (1 + len(carry)),
+        in_specs=[smem] + [vmem] * len(arrays) + [hbm] * len(rest),
         out_specs=(hbm, hbm, hbm, vmem),
         scratch_shapes=[
-            pltpu.VMEM(w.shape, BF16),
+            pltpu.VMEM((8, HD) if near_w else w.shape, BF16),
             pltpu.VMEM((steps, rows, out_cols // steps), BF16),
             pltpu.SemaphoreType.DMA((steps,)),
             pltpu.SemaphoreType.DMA((steps + 2 * order.heads,)),
         ],
-        input_output_aliases={2 + len(arrays) + i: i for i in range(len(carry))},
+        input_output_aliases={
+            1 + len(arrays) + len(lead) + i: i for i in range(len(carry))
+        },
         compiler_params=pltpu.CompilerParams(vmem_limit_bytes=LARGE),
         cost_estimate=SLIGHT,
-    )(pltpu.with_memory_space_constraint(facts, pltpu.SMEM), *arrays, w, *carry)
+    )(pltpu.with_memory_space_constraint(facts, pltpu.SMEM), *arrays, *rest)
 
 
 def put_rows(order, facts, pieces, dk, dv, top, rows, sem, first):
@@ -924,10 +933,8 @@
     facts, own = start(order, side, hbm(ancestors), hbm(counts), *inputs[2:4])
     state = {}
 
-    def own_pages(kvs, pages, prior=(), after=(), w=None):
-        return attend(
-            True, kvs, group, order, facts, inputs, pages, state, prior, after, w
-        )
+    def own_pages(kvs, pages, prior=(), after=()):
+        return attend(True, kvs, group, order, facts, inputs, pages, state, prior, after)
 
     def shared_pages(kvs, page, ride=None, after=()):
         return attend(
@@ -942,7 +949,7 @@
     kvs = tuple(range(kv))
     w = hbm(w_value)
     if fast:
-        level2, by_head, far_v = [], [], []
+        level2, by_head = [], []
 
         def beside_pair(from_core, chip):
             level2.extend((own, from_core))
@@ -959,22 +966,21 @@
         sent = flipped(sent, "sub", 1)
         kept = shared_pages(kvs[2:], theirs)
         total, root, root_far, next_far = over_cores(facts, kept, sent)
-        *last, w_near = own_pages(kvs[3:], level2, most, (root,), w)
-        both = [[piece] for piece in last]
-        begun = begin_input_grad(order, facts, w_near, both[1])
-        far_v.append(spread(last[1]))
-        total, low, far = over_halves(facts, total, root_far, next_far, (begun,))
-        made = finish_queries(kvs[:3], group, order, facts, (mine, theirs), state, (low,))
-        near, far = over_chips(facts, total, far, last[3], (made, *far_v))
-        dk0, dv0 = finish_small_tree(order, facts, both[2], near, far, sent)
+        dk12, dv12, own0, send2 = own_pages(kvs[3:], level2, most, (root,))
+        far_v = spread(dv12)
+        total, low, far = over_halves(facts, total, root_far, next_far, (send2,))
+        made, w_near = finish_queries(
+            kvs[:3], group, order, facts, (mine, theirs), state, (low,), w
+        )
+        near, far = over_chips(facts, total, far, send2, (made, far_v))
+        dk0, dv0 = finish_small_tree(order, facts, [own0], near, far, sent)
         far_0 = spread(dv0)
-        begun_0 = begin_input_grad(order, facts, w_near, [dv0])
-        *grads, _ = end_input_grad(
-            order, facts, w_near, far_v, begun, both[:2], after=(begun_0,)
+        begun = begin_input_grad(order, facts, w_near, [dv0])
+        *grads, _ = input_grad(
+            order, facts, w_near, 2 * PAGE, [dv12], [far_v], ([dk12], [dv12]), near_w=True,
+            after=(begun,),
         )
-        grads = end_input_grad(
-            order, facts, w_near, [far_0], begun_0, ([dk0], [dv0]), grads
-        )
+        grads = end_input_grad(order, facts, w_near, [far_0], begun, ([dk0], [dv0]), grads)
         return (state["gq"], grads[1], grads[2], grads[0])
 
     path_ids = ancestors[0]

time: 53.5 us -> 52.3 us (0.978)
  waiting for transfers between devices: 6.99 us -> 6.15 us
  Pallas kernels: 32 us -> 31.4 us
    pallas_call x0 -> x1, Pallas kernels: none -> 3.19 us  [input_grad(): pl.pallas_call(body, out_shape=(jax.ShapeDtypeStruct((ROWS, out_cols), BF...]
    pallas_call x2 -> x1, Pallas kernels: 4.82 us -> 2.33 us  [end_input_grad(): pl.pallas_call(kernel, out_shape=(jax.ShapeDtypeStruct((ROWS, out_cols),...]
    pallas_call x2 -> x1, Pallas kernels: 1.73 us -> 0.84 us  [begin_input_grad(): pl.pallas_call(kernel, out_shape=pltpu.VMEM((out_cols, rows), F32), in_sp...]
    ppermute x11, waiting for transfers between devices: 6.99 us -> 6.15 us  [flipped(): lax.ppermute(block, axis, [(i, i ^ bit) for i in range(count) if i ^ bit...]
  transfers between devices with their start and end apart: 11 -> 11, of which waited for: 6 -> 5; matrix products, arithmetic and copies ran while one was open for 0% -> 0% of each run, Pallas kernels for 53% -> 53%
where the time goes in v15:
time: 52.3 us; the launch traced here: 52.1 us
  Pallas kernels  31.4 us (60%)
  starting transfers between devices  13.7 us (26%)
  waiting for transfers between devices  6.15 us (12%)
  between operations  0.95 us (2%)
    pallas_call x13, Pallas kernels, kernel_call(): pl.pallas_call(kernel, out_shape=tuple((pltpu.VMEM(s, d) if inside else j...  24 us
    ppermute x11, starting transfers between devices, flipped(): lax.ppermute(block, axis, [(i, i ^ bit) for i in range(count) if i ^ bit...  13.7 us
    ppermute x11, waiting for transfers between devices, flipped(): lax.ppermute(block, axis, [(i, i ^ bit) for i in range(count) if i ^ bit...  6.15 us
    pallas_call x1, Pallas kernels, input_grad(): pl.pallas_call(body, out_shape=(jax.ShapeDtypeStruct((ROWS, out_cols), BF...  3.19 us
    pallas_call x1, Pallas kernels, end_input_grad(): pl.pallas_call(kernel, out_shape=(jax.ShapeDtypeStruct((ROWS, out_cols),...  2.33 us
  transfers between devices with their start and end apart: 11, of which 5 were waited for; matrix products, arithmetic and copies ran while one was open for 0% of the time, Pallas kernels for 53%

profile of v15, /device:TPU:0, one launch (start us, length us, event | category | flops | bytes accessed | tf_op | source)
XLA Modules:
  0.0 52.1 jit_solution(1826569071047574050)
XLA Ops:
  0.6 1.0 %shard_map.120 = (s32[16]{0:T(128)S(4)}, bf16[2,128,512]{2,1,0:T(8,128)(2,1)S(1)}) custom-call(s32[1]{0:T(128)} %bitcast.side_ref, s32[1,5]{1,0:T(1,128)} %ids_ref.1, s32[1,3]{1,0:T(1,128)} %counts_ref.1, bf16[384,512]{1,0:T(8,128)(2,1)} %refs_5_.1, bf16[384,512]{1,0:T(8,128)(2,1)} %refs_6_.1), custom_call_target="tpu_custom_call" | custom-call | tf_op jit(solution)/shard_map/pallas_call | solution.py:141
  1.7 0.5 collective-permute-start
  2.2 1.2 %collective-permute-done.refs_2_.refs_10_.refs_11_ = bf16[2,128,512]{2,1,0:T(8,128)(2,1)S(1)} collective-permute-done((bf16[2,128,512]{2,1,0:T(8,128)(2,1)S(1)}, bf16[2,128,512]{2,1,0:T(8,128)(2,1)S(1)}, u32[]{:S(2)}, u32[]{:S(2)}) %collective-permute-start) | collective-permute-done | bytes 262176 | tf_op jit(solution)/shard_map/ppermute | solution.py:782
  3.4 3.0 %collective-permute-start.1 = (bf16[2,128,256]{2,1,0:T(8,128)(2,1)S(1)}, bf16[2,128,256]{2,1,0:T(8,128)(2,1)S(1)}, u32[]{:S(2)}, u32[]{:S(2)}) collective-permute-start(bf16[2,128,256]{2,1,0:T(8,128)(2,1)S(1)} %shard_map.121.refs_9_.refs_1_), channel_id=1, source_target_pairs={{0,4},{4,0},{8,12},{12,8},{1,5},{5,1},{9,13},{13,9},{2,6},{6,2},{1... | collective-permute-start | bytes 393224 | tf_op jit(solution)/shard_map/ppermute | solution.py:782
  6.4 4.5 %shard_map.122 = (f32[384,1024]{1,0:T(8,128)S(1)}, bf16[128,3072]{1,0:T(8,128)(2,1)S(1)}, bf16[128,3072]{1,0:T(8,128)(2,1)S(1)}, bf16[256,128]{1,0:T(8,128)(2,1)...) custom-call(s32[16]{0:T(128)S(4)} %get-tuple-element.64.refs_0_.fact, ...), custom_call_target="tpu_custom_call" | custom-call | flops 4026531840 | bytes 1000 | tf_op jit(solution)/shard_map/pallas_call | solution.py:100
  10.9 0.0 collective-permute-done.1.refs_2_
  11.0 2.7 %collective-permute-start.2 = (bf16[2,128,256]{2,1,0:T(8,128)(2,1)S(1)}, bf16[2,128,256]{2,1,0:T(8,128)(2,1)S(1)}, u32[]{:S(2)}, u32[]{:S(2)}) collective-permute-start(bf16[2,128,256]{2,1,0:T(8,128)(2,1)S(1)} %shard_map.123.refs_15_.refs_3_), channel_id=1, source_target_pairs={{0,8},{4,12},{8,0},{12,4},{1,9},{5,13},{9,1},{13,5},{2,10},{6,14},... | collective-permute-start | bytes 393224 | tf_op jit(solution)/shard_map/ppermute | solution.py:782
  13.6 5.0 %shard_map.124 = (f32[384,1024]{1,0:T(8,128)S(1)}, bf16[128,3072]{1,0:T(8,128)(2,1)S(1)}, bf16[128,3072]{1,0:T(8,128)(2,1)S(1)}, f32[384,1024]{1,0:T(8,128)S(1)}...) custom-call(s32[16]{0:T(128)S(4)} %get-tuple-element.64.refs_0_.fact, ...), custom_call_target="tpu_custom_call" | custom-call | flops 8053063680 | bytes 1000 | tf_op jit(solution)/shard_map/pallas_call | solution.py:100
  18.6 1.2 %collective-permute-done.2.refs_4_ = bf16[2,128,256]{2,1,0:T(8,128)(2,1)S(1)} collective-permute-done((bf16[2,128,256]{2,1,0:T(8,128)(2,1)S(1)}, bf16[2,128,256]{2,1,0:T(8,128)(2,1)S(1)}, u32[]{:S(2)}, u32[]{:S(2)}) %collective-permute-start.2) | collective-permute-done | bytes 131104 | tf_op jit(solution)/shard_map/ppermute | solution.py:782
  19.8 0.1 collective-permute-start.3
  19.9 3.2 %shard_map.126 = (bf16[3072,256]{1,0:T(8,128)(2,1)S(1)}, bf16[3072,256]{1,0:T(8,128)(2,1)S(1)}, bf16[7,128,256]{2,1,0:T(8,128)(2,1)S(1)}) custom-call(s32[16]{0:T(128)S(4)} %get-tuple-element.64.refs_0_.facts, bf16[128,3072]{1,0:T(8,128)(2,1)S(1)} %get-tuple-element.79.refs_1_, bf16[128,3072]{1,0:T(8,128)(2,1)S(1)} %get-tuple-element.80.refs_2_, ...), custom_call_target="tpu_custom_call" | custom-call | flops 8053063680 | bytes 1000 | tf_op jit(solution)/shard_map/pallas_call | solution.py:100
  23.2 0.5 %collective-permute-start.4 = (bf16[7,128,256]{2,1,0:T(8,128)(2,1)S(1)}, bf16[7,128,256]{2,1,0:T(8,128)(2,1)S(1)}, u32[]{:S(2)}, u32[]{:S(2)}) collective-permute-start(bf16[7,128,256]{2,1,0:T(8,128)(2,1)S(1)} %get-tuple-element.102), channel_id=1, source_target_pairs={{0,1},{1,0},{2,3},{3,2},{4,5},{5,4},{6,7},{7,6},{8,9},{9,8},{10,11... | collective-permute-start | bytes 1376264 | tf_op jit(solution)/shard_map/ppermute | solution.py:782
  23.7 0.0 collective-permute-done.3.refs_11_.refs_2_
  23.7 3.9 %shard_map.127 = (bf16[3072,256]{1,0:T(8,128)(2,1)S(1)}, f32[384,1024]{1,0:T(8,128)S(1)}, bf16[128,3072]{1,0:T(8,128)(2,1)S(1)}, bf16[128,3072]{1,0:T(8,128)(2,1)S(1)}, f32[4,128,256]{2,1,0:T(8,128)S(1)}) custom-call(s32[16]{0:T(128)S(4)} %get-tuple-element.64.refs_0_.facts, bf16[128,3072]{1,0:T(8,128)(2,1)S(1)} %get-tuple-element.89.refs_1_, ...), custom_call_target="tpu_custom_call" | custom-call | flops 8053063680 | bytes 1000 | tf_op jit(solution)/shard_map/pallas_call | solution.py:100
  27.7 0.0 collective-permute-done.4.refs_2_.refs_4_
  27.7 0.1 shard_map.128
  27.7 0.1 collective-permute-start.6
  27.8 3.2 %collective-permute-start.5 = (bf16[2,128,256]{2,1,0:T(8,128)(2,1)S(1)}, bf16[2,128,256]{2,1,0:T(8,128)(2,1)S(1)}, u32[]{:S(2)}, u32[]{:S(2)}) collective-permute-start(bf16[2,128,256]{2,1,0:T(8,128)(2,1)S(1)} %get-tuple-element.103.refs_16_), channel_id=1, source_target_pairs={{0,8},{4,12},{8,0},{12,4},{1,9},{5,13},{9,1},{13,5},{2,10},{6,14},... | collective-permute-start | bytes 393224 | tf_op jit(solution)/shard_map/ppermute | solution.py:782
  31.0 3.5 %shard_map.129 = (bf16[384,4096]{1,0:T(8,128)(2,1)}, bf16[256,512]{1,0:T(8,128)(2,1)S(1)}, bf16[256,512]{1,0:T(8,128)(2,1)S(1)}, f32[2,128,512]{2,1,0:T(8,128)S(1)}, bf16[2,128,512]{2,1,0:T(8,128)(2,1)S(1)}) custom-call(s32[16]{0:T(128)S(4)} %get-tuple-element.64.refs_0_.facts, f32[384,1024]{1,0:T(8,128)S(1)} %get-tuple-element.95.refs_1_, ...), custom_call_target="tpu_custom_call" | custom-call | flops 4026531840 | bytes 1000 | tf_op jit(solution)/shard_map/pallas_call | solution.py:100
  34.6 1.6 %collective-permute-start.8 = (bf16[256,512]{1,0:T(8,128)(2,1)S(1)}, bf16[256,512]{1,0:T(8,128)(2,1)S(1)}, u32[]{:S(2)}, u32[]{:S(2)}) collective-permute-start(bf16[256,512]{1,0:T(8,128)(2,1)S(1)} %get-tuple-element.114.refs_0_.refs_3_), channel_id=1, source_target_pairs={{0,2},{2,0},{1,3},{3,1},{4,6},{6,4},{5,7},{7,5},{8,10},{10,8},{9,1... | collective-permute-start | bytes 786440 | tf_op jit(solution)/shard_map/ppermute | solution.py:782
  36.1 0.0 collective-permute-done.6.refs_3_
  36.1 1.2 %collective-permute-done.5.refs_2_ = bf16[2,128,256]{2,1,0:T(8,128)(2,1)S(1)} collective-permute-done((bf16[2,128,256]{2,1,0:T(8,128)(2,1)S(1)}, bf16[2,128,256]{2,1,0:T(8,128)(2,1)S(1)}, u32[]{:S(2)}, u32[]{:S(2)}) %collective-permute-start.5) | collective-permute-done | bytes 131104 | tf_op jit(solution)/shard_map/ppermute | solution.py:782
  37.3 0.1 shard_map.130
  37.3 0.4 collective-permute-start.7
  37.7 3.4 %shard_map.131 = (bf16[384,4096]{1,0:T(8,128)(2,1)}, f32[8,128]{1,0:T(8,128)S(1)}, bf16[2560,1024]{1,0:T(8,128)(2,1)S(1)}) custom-call(s32[16]{0:T(128)S(4)} %get-tuple-element.64.refs_0_.facts, bf16[2,2,128,256]{3,2,1,0:T(8,128)(2,1)S(1)} %shard_map.125.refs_13_.refs_1_, ...), custom_call_target="tpu_custom_call", output_to_operand_aliasing={{0}: (9, {})} | custom-call | flops 1000 | bytes 1000 | tf_op jit(solution)/shard_map/pallas_call | solution.py:100
  41.2 1.2 %collective-permute-done.7.refs_2_ = bf16[2,128,256]{2,1,0:T(8,128)(2,1)S(1)} collective-permute-done((bf16[2,128,256]{2,1,0:T(8,128)(2,1)S(1)}, bf16[2,128,256]{2,1,0:T(8,128)(2,1)S(1)}, u32[]{:S(2)}, u32[]{:S(2)}) %collective-permute-start.7) | collective-permute-done | bytes 131104 | tf_op jit(solution)/shard_map/ppermute | solution.py:782
  42.4 0.0 collective-permute-done.8.refs_5_.refs_1_
  42.4 0.1 collective-permute-start.9
  42.5 1.4 %collective-permute-done.9.refs_3_ = bf16[2,128,384]{2,1,0:T(8,128)(2,1)S(1)} collective-permute-done((bf16[2,128,384]{2,1,0:T(8,128)(2,1)S(1)}, bf16[2,128,384]{2,1,0:T(8,128)(2,1)S(1)}, u32[]{:S(2)}, u32[]{:S(2)}) %collective-permute-start.9) | collective-permute-done | bytes 196640 | tf_op jit(solution)/shard_map/ppermute | solution.py:782
  43.9 0.1 shard_map.133
  44.0 1.6 %collective-permute-start.10 = (bf16[128,512]{1,0:T(8,128)(2,1)S(1)}, bf16[128,512]{1,0:T(8,128)(2,1)S(1)}, u32[]{:S(2)}, u32[]{:S(2)}) collective-permute-start(bf16[128,512]{1,0:T(8,128)(2,1)S(1)} %get-tuple-element.115.refs_2_.refs_5_), channel_id=1, source_target_pairs={{0,2},{2,0},{1,3},{3,1},{4,6},{6,4},{5,7},{7,5},{8,10},{10,8},{9,1... | collective-permute-start | bytes 393224 | tf_op jit(solution)/shard_map/ppermute | solution.py:782
  45.6 0.8 %shard_map.134.refs_5_.refs_2_ = f32[2560,128]{1,0:T(8,128)S(1)} custom-call(s32[16]{0:T(128)S(4)} %get-tuple-element.64.refs_0_.facts, bf16[2560,1024]{1,0:T(8,128)(2,1)S(1)} %get-tuple-element.110.refs_1_.refs_4_, bf16[128,512]{1,0:T(8,128)(2,1)S(1)} %get-tuple-element.115.refs_2_.refs_5_), custom_call_target="tpu_custom_call" | custom-call | flops 1000 | bytes 1000 | tf_op jit(solution)/shard_map/pallas_call | solution.py:717
  46.4 3.2 %shard_map.135 = (bf16[384,2560]{1,0:T(8,128)(2,1)}, bf16[384,512]{1,0:T(8,128)(2,1)}, bf16[384,512]{1,0:T(8,128)(2,1)}, f32[8,128]{1,0:T(8,128)}) custom-call(s32[16]{0:T(128)S(4)} %get-tuple-element.64.refs_0_.facts, bf16[256,512]{1,0:T(8,128)(2,1)S(1)} %get-tuple-element.114.refs_0_.refs_3_, bf16[256,512]{1,0:T(8,128)(2,1)S(1)} %collective-permute-done.8.refs_5_.refs_1_, ...), custom_call_target="tpu_custom_call" | custom-call | flops 1000 | bytes 1000 | tf_op jit(solution)/shard_map/pallas_call | solution.py:656
  49.6 0.0 collective-permute-done.10.refs_3_
  49.7 2.3 %shard_map.136 = (bf16[384,2560]{1,0:T(8,128)(2,1)}, bf16[384,512]{1,0:T(8,128)(2,1)}, bf16[384,512]{1,0:T(8,128)(2,1)}, f32[8,128]{1,0:T(8,128)}) custom-call(s32[16]{0:T(128)S(4)} %get-tuple-element.64.refs_0_.facts, bf16[2560,1024]{1,0:T(8,128)(2,1)S(1)} %get-tuple-element.110.refs_1_.refs_4_, ...), custom_call_target="tpu_custom_call", output_to_operand_aliasing={{0}: (6, {}), {1}: (7, {}), {2}: (8, {})} | custom-call | flops 1000 | bytes 1000 | tf_op jit(solution)/shard_map/pallas_call | solution.py:763
  (4 shorter events, 0.1 us)
Async XLA Ops:
  1.7 1.7 %collective-permute-start = (bf16[2,128,512]{2,1,0:T(8,128)(2,1)S(1)}, bf16[2,128,512]{2,1,0:T(8,128)(2,1)S(1)}, u32[]{:S(2)}, u32[]{:S(2)}) collective-permute-start(bf16[2,128,512]{2,1,0:T(8,128)(2,1)S(1)} %get-tuple-element.65.refs_1_.refs_9_.refs_10_), channel_id=1, source_target_pairs={{0,1},{1,0},{2,3},{3,2},{4,5},{5,4},{6,7},{7,6},{8,9},{9,8},{10,11... | collective-permute-start | bytes 786440 | tf_op jit(solution)/shard_map/ppermute | solution.py:782
  3.4 7.6 %collective-permute-start.1 = (bf16[2,128,256]{2,1,0:T(8,128)(2,1)S(1)}, bf16[2,128,256]{2,1,0:T(8,128)(2,1)S(1)}, u32[]{:S(2)}, u32[]{:S(2)}) collective-permute-start(bf16[2,128,256]{2,1,0:T(8,128)(2,1)S(1)} %shard_map.121.refs_9_.refs_1_), channel_id=1, source_target_pairs={{0,4},{4,0},{8,12},{12,8},{1,5},{5,1},{9,13},{13,9},{2,6},{6,2},{1... | collective-permute-start | bytes 393224 | tf_op jit(solution)/shard_map/ppermute | solution.py:782
  11.0 8.8 %collective-permute-start.2 = (bf16[2,128,256]{2,1,0:T(8,128)(2,1)S(1)}, bf16[2,128,256]{2,1,0:T(8,128)(2,1)S(1)}, u32[]{:S(2)}, u32[]{:S(2)}) collective-permute-start(bf16[2,128,256]{2,1,0:T(8,128)(2,1)S(1)} %shard_map.123.refs_15_.refs_3_), channel_id=1, source_target_pairs={{0,8},{4,12},{8,0},{12,4},{1,9},{5,13},{9,1},{13,5},{2,10},{6,14},... | collective-permute-start | bytes 393224 | tf_op jit(solution)/shard_map/ppermute | solution.py:782
  19.8 3.9 %collective-permute-start.3 = (bf16[2,2,128,256]{3,2,1,0:T(8,128)(2,1)S(1)}, bf16[2,2,128,256]{3,2,1,0:T(8,128)(2,1)S(1)}, u32[]{:S(2)}, u32[]{:S(2)}) collective-permute-start(bf16[2,2,128,256]{3,2,1,0:T(8,128)(2,1)S(1)} %shard_map.125.refs_13_.refs_1_), channel_id=1, source_target_pairs={{0,1},{1,0},{2,3},{3,2},{4,5},{5,4},{6,7},{7,6},{8,9},{9,8},{10,11... | collective-permute-start | bytes 786440 | tf_op jit(solution)/shard_map/ppermute | solution.py:782
  23.2 4.5 %collective-permute-start.4 = (bf16[7,128,256]{2,1,0:T(8,128)(2,1)S(1)}, bf16[7,128,256]{2,1,0:T(8,128)(2,1)S(1)}, u32[]{:S(2)}, u32[]{:S(2)}) collective-permute-start(bf16[7,128,256]{2,1,0:T(8,128)(2,1)S(1)} %get-tuple-element.102), channel_id=1, source_target_pairs={{0,1},{1,0},{2,3},{3,2},{4,5},{5,4},{6,7},{7,6},{8,9},{9,8},{10,11... | collective-permute-start | bytes 1376264 | tf_op jit(solution)/shard_map/ppermute | solution.py:782
  27.7 8.4 %collective-permute-start.6 = (bf16[2,128,256]{2,1,0:T(8,128)(2,1)S(1)}, bf16[2,128,256]{2,1,0:T(8,128)(2,1)S(1)}, u32[]{:S(2)}, u32[]{:S(2)}) collective-permute-start(bf16[2,128,256]{2,1,0:T(8,128)(2,1)S(1)} %get-tuple-element.106), channel_id=1, source_target_pairs={{0,4},{4,0},{8,12},{12,8},{1,5},{5,1},{9,13},{13,9},{2,6},{6,2},{1... | collective-permute-start | bytes 393224 | tf_op jit(solution)/shard_map/ppermute | solution.py:782
  27.8 9.5 %collective-permute-start.5 = (bf16[2,128,256]{2,1,0:T(8,128)(2,1)S(1)}, bf16[2,128,256]{2,1,0:T(8,128)(2,1)S(1)}, u32[]{:S(2)}, u32[]{:S(2)}) collective-permute-start(bf16[2,128,256]{2,1,0:T(8,128)(2,1)S(1)} %get-tuple-element.103.refs_16_), channel_id=1, source_target_pairs={{0,8},{4,12},{8,0},{12,4},{1,9},{5,13},{9,1},{13,5},{2,10},{6,14},... | collective-permute-start | bytes 393224 | tf_op jit(solution)/shard_map/ppermute | solution.py:782
  34.6 7.8 %collective-permute-start.8 = (bf16[256,512]{1,0:T(8,128)(2,1)S(1)}, bf16[256,512]{1,0:T(8,128)(2,1)S(1)}, u32[]{:S(2)}, u32[]{:S(2)}) collective-permute-start(bf16[256,512]{1,0:T(8,128)(2,1)S(1)} %get-tuple-element.114.refs_0_.refs_3_), channel_id=1, source_target_pairs={{0,2},{2,0},{1,3},{3,1},{4,6},{6,4},{5,7},{7,5},{8,10},{10,8},{9,1... | collective-permute-start | bytes 786440 | tf_op jit(solution)/shard_map/ppermute | solution.py:782
  37.3 5.0 %collective-permute-start.7 = (bf16[2,128,256]{2,1,0:T(8,128)(2,1)S(1)}, bf16[2,128,256]{2,1,0:T(8,128)(2,1)S(1)}, u32[]{:S(2)}, u32[]{:S(2)}) collective-permute-start(bf16[2,128,256]{2,1,0:T(8,128)(2,1)S(1)} %get-tuple-element.108.refs_11_), channel_id=1, source_target_pairs={{0,4},{4,0},{8,12},{12,8},{1,5},{5,1},{9,13},{13,9},{2,6},{6,2},{1... | collective-permute-start | bytes 393224 | tf_op jit(solution)/shard_map/ppermute | solution.py:782
  42.4 1.5 %collective-permute-start.9 = (bf16[2,128,384]{2,1,0:T(8,128)(2,1)S(1)}, bf16[2,128,384]{2,1,0:T(8,128)(2,1)S(1)}, u32[]{:S(2)}, u32[]{:S(2)}) collective-permute-start(bf16[2,128,384]{2,1,0:T(8,128)(2,1)S(1)} %shard_map.132.refs_2_), channel_id=1, source_target_pairs={{0,1},{1,0},{2,3},{3,2},{4,5},{5,4},{6,7},{7,6},{8,9},{9,8},{10,11... | collective-permute-start | bytes 589832 | tf_op jit(solution)/shard_map/ppermute | solution.py:782
  44.0 5.6 %collective-permute-start.10 = (bf16[128,512]{1,0:T(8,128)(2,1)S(1)}, bf16[128,512]{1,0:T(8,128)(2,1)S(1)}, u32[]{:S(2)}, u32[]{:S(2)}) collective-permute-start(bf16[128,512]{1,0:T(8,128)(2,1)S(1)} %get-tuple-element.115.refs_2_.refs_5_), channel_id=1, source_target_pairs={{0,2},{2,0},{1,3},{3,1},{4,6},{6,4},{5,7},{7,5},{8,10},{10,8},{9,1... | collective-permute-start | bytes 393224 | tf_op jit(solution)/shard_map/ppermute | solution.py:782

commit v16 on v15

--- a/solution.py
+++ b/solution.py
@@ -280,7 +280,7 @@
         ]
     else:
         outs += [
-            ((4, PAGE, width), F32, True) if ride is None else ((7, PAGE, width), BF16, True),
+            ((4, PAGE, width), F32, True) if ride is None else ((8, PAGE, width), BF16, True),
         ]
     at_loaded = len(outs)
     if loading:
@@ -301,8 +301,8 @@
         add_near(("page", i), page)
     for i, array in enumerate(prior):
         add_near(("prior", i), array)
-    for i, array in enumerate(ride or ()):
-        add_near(("ride", i), array)
+    if ride is not None:
+        add_near("ride", ride)
     key_pages = 4 if own else 2
     scratch = [
         pltpu.VMEM((2 * HD, key_pages * PAGE), BF16),
@@ -357,13 +357,10 @@
         for out, i in zip(results, range(len(prior))):
             out[..., :base] = near_ref(("prior", i))[...]
         if ride is not None:
-            (out,) = results
+            (out,), more = results, near_ref("ride")
             for kind in range(2):
-                more = jnp.concatenate(
-                    [near_ref(("ride", i))[kind] for i in range(len(ride))], axis=1
-                )
-                out[4 + kind] = more[:, :width]
-                out[6, :, kind * HD : (kind + 1) * HD] = more[:, width:]
+                out[4 + kind] = more[kind, :, :width]
+                out[6 + kind] = more[kind, :, width:]
         owns2 = facts[OWNS2] == 1
         if loading:
             arrived(*shared_loads)
@@ -724,57 +721,37 @@
     )(pltpu.with_memory_space_constraint(facts, pltpu.SMEM), *near, *after)
 
 
-def end_input_grad(order, facts, w, far, begun, grads, carry=None, after=()):
+def end_input_grad(order, facts, w, base, across, corner, begun, grads, carry):
     tiles = width_tiles(w)
     out_cols, depth = w.shape
     half = depth // 2
     steps = len(tiles)
-    rows = far[0].shape[0]
-    top = 0 if rows == PAGE else PAGE
-    width = sum(a.shape[1] for a in grads[0])
-    near = [w, begun, *far, *grads[0], *grads[1]]
-    carry = list(carry or [])
-
-    def body(facts, w_r, begun_r, *refs):
-        far_r, grad_r = refs[: len(far)], refs[len(far) : len(near) - 2]
-        out, dk, dv, made, stage, sem = refs[-6:]
-        made[...] = jnp.zeros_like(made)
-        copies = put_rows(order, facts, grad_r, dk, dv, top, rows, sem, steps)
-        other = order.real(facts, jnp.concatenate([r[...] for r in far_r], axis=1))
+    rows = base.shape[0]
+
+    def body(facts, w_r, begun_r, base_r, across_r, corner_r, *refs):
+        out, dk, dv, stage, sem = refs[-5:]
+        copies = put_rows(order, facts, refs[:2], dk, dv, 0, rows, sem, steps)
+        gained = jnp.concatenate([corner_r[...], across_r[...]], axis=1).astype(F32)
+        known = base_r[...]
+        more = jnp.where(row_ok(facts[N0], rows, half), known.astype(F32) + gained, 0.0)
+        other = order.real(facts, jnp.where(facts[OWNS2] == 1, known, more.astype(BF16)))
         where = pl.ds(pl.multiple_of((1 - facts[SIDE]) * half, half), half)
         for i, at in enumerate(tiles):
             stage[i] = (dot_t(w_r[at, where], other) + begun_r[at]).astype(BF16).T
-            copies.append(
-                pltpu.make_async_copy(stage.at[i], out.at[top : top + rows, at], sem.at[i])
-            )
+            copies.append(pltpu.make_async_copy(stage.at[i], out.at[:rows, at], sem.at[i]))
             copies[-1].start()
         for c in copies:
             c.wait()
 
-    smem = pl.BlockSpec(memory_space=pltpu.SMEM)
-    vmem = pl.BlockSpec(memory_space=pltpu.VMEM)
-    hbm = pl.BlockSpec(memory_space=pl.ANY)
-    near = [pltpu.with_memory_space_constraint(a, pltpu.VMEM) for a in near]
-    kept = jax.ShapeDtypeStruct((ROWS, width), BF16)
-
-    def kernel(*refs):
-        body(*refs[: 1 + len(near)], *refs[1 + len(near) + len(carry) + len(after) :])
-
-    return pl.pallas_call(
-        kernel,
-        out_shape=(
-            jax.ShapeDtypeStruct((ROWS, out_cols), BF16), kept, kept, pltpu.VMEM((8, HD), F32)
-        ),
-        in_specs=[smem] + [vmem] * len(near) + [hbm] * (len(carry) + len(after)),
-        out_specs=(hbm, hbm, hbm, vmem),
-        scratch_shapes=[
+    return kernel_call(
+        body, facts, [w, begun, base, across, corner, *grads], list(carry),
+        [(a.shape, a.dtype, False) for a in carry],
+        [
             pltpu.VMEM((steps, rows, out_cols // steps), BF16),
             pltpu.SemaphoreType.DMA((steps + 2 * order.heads,)),
         ],
-        input_output_aliases={1 + len(near) + i: i for i in range(len(carry))},
-        compiler_params=pltpu.CompilerParams(vmem_limit_bytes=LARGE),
-        cost_estimate=SLIGHT,
-    )(pltpu.with_memory_space_constraint(facts, pltpu.SMEM), *near, *carry, *after)
+        {("far", i): i for i in range(len(carry))},
+    )
 
 
 def flipped(block, axis, bit):
@@ -855,48 +832,58 @@
     return total, low, flipped(low, "leaf", 1)
 
 
-def over_chips(facts, total, far, level2, after):
+def over_chips(facts, total, far, after):
     width = total.shape[-1]
 
-    def body(facts, near, away, extra, out):
+    def body(facts, near, away, out, values):
         root = near[:2] + away[...].astype(F32)
-        out[:, :, :width] = jnp.where(facts[ROOT_IN_CHIP] == 1, root, near[2:]).astype(BF16)
-        out[:, :, width:] = extra[:, :, extra.shape[-1] - HD :]
-
-    outs = [((2, PAGE, width + HD), BF16, True)]
-    (mine,) = kernel_call(body, facts, [total, far, level2], [], outs, after=after)
-    return mine, flipped(mine, "sub", 1)
+        picked = jnp.where(facts[ROOT_IN_CHIP] == 1, root, near[2:]).astype(BF16)
+        out[...] = picked
+        values[...] = picked[1]
+
+    outs = [((2, PAGE, width), BF16, True), ((PAGE, width), BF16, True)]
+    mine, values = kernel_call(body, facts, [total, far], [], outs, after=after)
+    across = flipped(values, "tensor", 1)
+    corner = lax.ppermute(values, ("tensor", "sub"), [(i, 3 - i) for i in range(4)])
+    return mine, flipped(mine, "sub", 1), across, corner
+
+
+def other_level2(order, head, kind, ref):
+    theirs = head ^ order.half
+    at = theirs % order.half * HD
+    return ref[4 + 2 * (theirs // order.half) + kind, :, at : at + HD]
+
+
+def begin_values(order, facts, own0, level2_far):
+    def body(facts, own_r, low_r, out):
+        ok = row_ok(facts[N0], PAGE, HD)
+        for head in range(order.heads):
+            c = slice(head * HD, (head + 1) * HD)
+            low = other_level2(order, head, 1, low_r).astype(F32)
+            value = own_r[1, :, c] + jnp.where(facts[OWNS2] == 1, low, 0.0)
+            out[:, c] = jnp.where(ok, value, 0.0).astype(BF16)
+
+    outs = [((PAGE, own0.shape[-1]), BF16, True)]
+    return kernel_call(body, facts, [own0, level2_far], [], outs)[0]
 
 
 def finish_small_tree(order, facts, own0, mine, far, level2_far):
-    part = order.half * HD
-    width = 2 * part
-
-    def body(facts, *refs):
-        mine_r, far_r, low_r, dk, dv = refs[len(own0) :]
+    width = own0.shape[-1]
+
+    def body(facts, own_r, mine_r, far_r, low_r, dk, dv):
         owns2 = facts[OWNS2] == 1
-        own_r = [(r, at) for r in refs[: len(own0)] for at in range(0, r.shape[-1], HD)]
         ok = row_ok(facts[N0], PAGE, HD)
         for head in range(order.heads):
             c = slice(head * HD, (head + 1) * HD)
             at = head % order.half * HD
-            here = slice(at, at + HD)
-            theirs = head ^ order.half
             for kind, out in enumerate((dk, dv)):
-                gained = (far_r if head < order.half else mine_r)[kind, :, here]
-                ref, start_at = own_r[head]
-                base = ref[kind, :, start_at : start_at + HD]
-                if theirs < order.half:
-                    level2 = low_r[4 + kind, :, theirs * HD : (theirs + 1) * HD]
-                elif theirs + 1 < order.heads:
-                    level2 = low_r[6, :, kind * HD : (kind + 1) * HD]
-                else:
-                    level2 = far_r[kind, :, part : part + HD]
+                gained = (far_r if head < order.half else mine_r)[kind, :, at : at + HD]
+                level2 = other_level2(order, head, kind, low_r)
                 more = jnp.where(owns2, level2, gained).astype(F32)
-                out[:, c] = jnp.where(ok, base + more, 0.0).astype(BF16)
+                out[:, c] = jnp.where(ok, own_r[kind, :, c] + more, 0.0).astype(BF16)
 
     page = ((PAGE, width), BF16, True)
-    return kernel_call(body, facts, [*own0, mine, far, level2_far], [], [page, page])
+    return kernel_call(body, facts, [own0, mine, far, level2_far], [], [page, page])
 
 
 def gather_tree(ids, own):
@@ -949,38 +936,39 @@
     kvs = tuple(range(kv))
     w = hbm(w_value)
     if fast:
-        level2, by_head = [], []
+        level2, halves = [], []
 
         def beside_pair(from_core, chip):
             level2.extend((own, from_core))
-            by_head.append(own_pages(kvs[:1], level2, after=(chip,)))
-            return (by_head[0][3],)
+            halves.append(own_pages(kvs[:2], level2, after=(chip,)))
+            return (halves[0][3],)
 
         def beside_half(pair):
-            by_head.append(own_pages(kvs[1:3], level2, by_head[0], (pair,)))
-            return (by_head[1][3],)
+            halves.append(own_pages(kvs[2:], level2, halves[0], (pair,)))
+            return (halves[1][3],)
 
         mine, theirs = gather_small_tree(facts, own, beside_pair, beside_half)
-        most = by_head[1]
-        sent = shared_pages(kvs[:2], mine, (most[3],))
-        sent = flipped(sent, "sub", 1)
+        dk12, dv12, own0, send2 = halves[1]
+        sent = flipped(shared_pages(kvs[:2], mine, send2), "sub", 1)
         kept = shared_pages(kvs[2:], theirs)
         total, root, root_far, next_far = over_cores(facts, kept, sent)
-        dk12, dv12, own0, send2 = own_pages(kvs[3:], level2, most, (root,))
         far_v = spread(dv12)
-        total, low, far = over_halves(facts, total, root_far, next_far, (send2,))
+        base = begin_values(order, facts, own0, sent)
         made, w_near = finish_queries(
-            kvs[:3], group, order, facts, (mine, theirs), state, (low,), w
+            kvs, group, order, facts, (mine, theirs), state, (root, base), w
         )
-        near, far = over_chips(facts, total, far, send2, (made, far_v))
-        dk0, dv0 = finish_small_tree(order, facts, [own0], near, far, sent)
-        far_0 = spread(dv0)
+        total, low, far = over_halves(facts, total, root_far, next_far, (made,))
+        base_far = spread(base)
+        *grads, made = input_grad(
+            order, facts, w_near, 2 * PAGE, [dv12], [far_v], ([dk12], [dv12]), near_w=True,
+            after=(low,),
+        )
+        near, far, across, corner = over_chips(facts, total, far, (made, base_far))
+        dk0, dv0 = finish_small_tree(order, facts, own0, near, far, sent)
         begun = begin_input_grad(order, facts, w_near, [dv0])
-        *grads, _ = input_grad(
-            order, facts, w_near, 2 * PAGE, [dv12], [far_v], ([dk12], [dv12]), near_w=True,
-            after=(begun,),
+        grads = end_input_grad(
+            order, facts, w_near, base_far, across, corner, begun, [dk0, dv0], grads
         )
-        grads = end_input_grad(order, facts, w_near, [far_0], begun, ([dk0], [dv0]), grads)
         return (state["gq"], grads[1], grads[2], grads[0])
 
     path_ids = ancestors[0]

time: 52.3 us -> 52.8 us (level)
  Pallas kernels: 31.4 us -> 29.1 us
  waiting for transfers between devices: 6.15 us -> 7.49 us
  starting transfers between devices: 13.7 us -> 15 us
    pallas_call x1 -> x0, Pallas kernels: 2.33 us -> none  [end_input_grad(): pl.pallas_call(kernel, out_shape=(jax.ShapeDtypeStruct((ROWS, out_cols),...]
    ppermute x0 -> x1, starting transfers between devices: none -> 1.26 us  [over_chips(): lax.ppermute(values, ('tensor', 'sub'), [(i, 3 - i) for i in range(4)])]
    ppermute x0 -> x1, waiting for transfers between devices: none -> 0.79 us  [over_chips(): lax.ppermute(values, ('tensor', 'sub'), [(i, 3 - i) for i in range(4)])]
    pallas_call x13 -> x14, Pallas kernels: 24 us -> 24.6 us  [kernel_call(): pl.pallas_call(kernel, out_shape=tuple((pltpu.VMEM(s, d) if inside else j...]
    ppermute x11 -> x12, waiting for transfers between devices: 6.15 us -> 6.7 us  [flipped(): lax.ppermute(block, axis, [(i, i ^ bit) for i in range(count) if i ^ bit...]
    pallas_call x1, Pallas kernels: 3.19 us -> 2.64 us  [input_grad(): pl.pallas_call(body, out_shape=(jax.ShapeDtypeStruct((ROWS, out_cols), BF...]
    ppermute x11 -> x12, starting transfers between devices: 13.7 us -> 13.8 us  [flipped(): lax.ppermute(block, axis, [(i, i ^ bit) for i in range(count) if i ^ bit...]
  transfers between devices with their start and end apart: 11 -> 13, of which waited for: 5 -> 5; matrix products, arithmetic and copies ran while one was open for 0% -> 0% of each run, Pallas kernels for 53% -> 50%
where the time goes in v16:
time: 52.8 us; the launch traced here: 52.6 us
  Pallas kernels  29.1 us (55%)
  starting transfers between devices  15 us (28%)
  waiting for transfers between devices  7.49 us (14%)
  between operations  0.97 us (2%)
    pallas_call x14, Pallas kernels, kernel_call(): pl.pallas_call(kernel, out_shape=tuple((pltpu.VMEM(s, d) if inside else j...  24.6 us
    ppermute x12, starting transfers between devices, flipped(): lax.ppermute(block, axis, [(i, i ^ bit) for i in range(count) if i ^ bit...  13.8 us
    ppermute x12, waiting for transfers between devices, flipped(): lax.ppermute(block, axis, [(i, i ^ bit) for i in range(count) if i ^ bit...  6.7 us
    pallas_call x1, Pallas kernels, input_grad(): pl.pallas_call(body, out_shape=(jax.ShapeDtypeStruct((ROWS, out_cols), BF...  2.64 us
    ppermute x1, starting transfers between devices, over_chips(): lax.ppermute(values, ('tensor', 'sub'), [(i, 3 - i) for i in range(4)])  1.26 us
  transfers between devices with their start and end apart: 13, of which 5 were waited for; matrix products, arithmetic and copies ran while one was open for 0% of the time, Pallas kernels for 50%

profile of v16, /device:TPU:0, one launch (start us, length us, event | category | flops | bytes accessed | tf_op | source)
XLA Modules:
  0.0 52.6 jit_solution(10426097037174637548)
XLA Ops:
  0.6 1.0 %shard_map.120 = (s32[16]{0:T(128)S(4)}, bf16[2,128,512]{2,1,0:T(8,128)(2,1)S(1)}) custom-call(s32[1]{0:T(128)} %bitcast.side_ref, s32[1,5]{1,0:T(1,128)} %ids_ref.1, s32[1,3]{1,0:T(1,128)} %counts_ref.1, bf16[384,512]{1,0:T(8,128)(2,1)} %refs_5_.1, bf16[384,512]{1,0:T(8,128)(2,1)} %refs_6_.1), custom_call_target="tpu_custom_call" | custom-call | tf_op jit(solution)/shard_map/pallas_call | solution.py:141
  1.7 0.5 collective-permute-start
  2.2 1.2 %collective-permute-done.refs_2_.refs_10_ = bf16[2,128,512]{2,1,0:T(8,128)(2,1)S(1)} collective-permute-done((bf16[2,128,512]{2,1,0:T(8,128)(2,1)S(1)}, bf16[2,128,512]{2,1,0:T(8,128)(2,1)S(1)}, u32[]{:S(2)}, u32[]{:S(2)}) %collective-permute-start) | collective-permute-done | bytes 262176 | tf_op jit(solution)/shard_map/ppermute | solution.py:759
  3.4 3.0 %collective-permute-start.1 = (bf16[2,128,256]{2,1,0:T(8,128)(2,1)S(1)}, bf16[2,128,256]{2,1,0:T(8,128)(2,1)S(1)}, u32[]{:S(2)}, u32[]{:S(2)}) collective-permute-start(bf16[2,128,256]{2,1,0:T(8,128)(2,1)S(1)} %shard_map.121.refs_9_.refs_1_), channel_id=1, source_target_pairs={{0,4},{4,0},{8,12},{12,8},{1,5},{5,1},{9,13},{13,9},{2,6},{6,2},{1... | collective-permute-start | bytes 393224 | tf_op jit(solution)/shard_map/ppermute | solution.py:759
  6.4 7.0 %shard_map.122 = (f32[384,1024]{1,0:T(8,128)S(1)}, bf16[128,3072]{1,0:T(8,128)(2,1)S(1)}, bf16[128,3072]{1,0:T(8,128)(2,1)S(1)}, f32[384,1024]{1,0:T(8,128)S(1)}...) custom-call(s32[16]{0:T(128)S(4)} %get-tuple-element.63.refs_0_.fact, ...), custom_call_target="tpu_custom_call" | custom-call | flops 8053063680 | bytes 1000 | tf_op jit(solution)/shard_map/pallas_call | solution.py:100
  13.4 0.0 collective-permute-done.1.refs_2_
  13.5 2.7 %collective-permute-start.2 = (bf16[2,128,256]{2,1,0:T(8,128)(2,1)S(1)}, bf16[2,128,256]{2,1,0:T(8,128)(2,1)S(1)}, u32[]{:S(2)}, u32[]{:S(2)}) collective-permute-start(bf16[2,128,256]{2,1,0:T(8,128)(2,1)S(1)} %shard_map.123.refs_15_.refs_3_), channel_id=1, source_target_pairs={{0,8},{4,12},{8,0},{12,4},{1,9},{5,13},{9,1},{13,5},{2,10},{6,14},... | collective-permute-start | bytes 393224 | tf_op jit(solution)/shard_map/ppermute | solution.py:759
  16.1 5.1 %shard_map.124 = (f32[384,1024]{1,0:T(8,128)S(1)}, bf16[128,3072]{1,0:T(8,128)(2,1)S(1)}, bf16[128,3072]{1,0:T(8,128)(2,1)S(1)}, f32[384,1024]{1,0:T(8,128)S(1)}...) custom-call(s32[16]{0:T(128)S(4)} %get-tuple-element.63.refs_0_.fact, ...), custom_call_target="tpu_custom_call" | custom-call | flops 8053063680 | bytes 1000 | tf_op jit(solution)/shard_map/pallas_call | solution.py:100
  21.2 1.6 %collective-permute-start.8 = (bf16[256,512]{1,0:T(8,128)(2,1)S(1)}, bf16[256,512]{1,0:T(8,128)(2,1)S(1)}, u32[]{:S(2)}, u32[]{:S(2)}) collective-permute-start(bf16[256,512]{1,0:T(8,128)(2,1)S(1)} %get-tuple-element.109.refs_0_.refs_3_), channel_id=1, source_target_pairs={{0,2},{2,0},{1,3},{3,1},{4,6},{6,4},{5,7},{7,5},{8,10},{10,8},{9,1... | collective-permute-start | bytes 786440 | tf_op jit(solution)/shard_map/ppermute | solution.py:759
  22.8 0.0 collective-permute-done.2.refs_4_
  22.8 0.1 collective-permute-start.3
  22.9 3.4 %shard_map.126 = (bf16[3072,256]{1,0:T(8,128)(2,1)S(1)}, bf16[3072,256]{1,0:T(8,128)(2,1)S(1)}, bf16[8,128,256]{2,1,0:T(8,128)(2,1)S(1)}) custom-call(s32[16]{0:T(128)S(4)} %get-tuple-element.63.refs_0_.facts, bf16[128,3072]{1,0:T(8,128)(2,1)S(1)} %get-tuple-element.78.refs_1_, bf16[128,3072]{1,0:T(8,128)(2,1)S(1)} %get-tuple-element.79.refs_2_, ...), custom_call_target="tpu_custom_call" | custom-call | flops 8053063680 | bytes 1000 | tf_op jit(solution)/shard_map/pallas_call | solution.py:100
  26.3 0.6 %collective-permute-start.4 = (bf16[8,128,256]{2,1,0:T(8,128)(2,1)S(1)}, bf16[8,128,256]{2,1,0:T(8,128)(2,1)S(1)}, u32[]{:S(2)}, u32[]{:S(2)}) collective-permute-start(bf16[8,128,256]{2,1,0:T(8,128)(2,1)S(1)} %get-tuple-element.99), channel_id=1, source_target_pairs={{0,1},{1,0},{2,3},{3,2},{4,5},{5,4},{6,7},{7,6},{8,9},{9,8},{10,11... | collective-permute-start | bytes 1572872 | tf_op jit(solution)/shard_map/ppermute | solution.py:759
  26.8 0.0 collective-permute-done.3.refs_13_.refs_2_
  26.8 3.3 %shard_map.127 = (bf16[3072,256]{1,0:T(8,128)(2,1)S(1)}, bf16[3072,256]{1,0:T(8,128)(2,1)S(1)}, f32[4,128,256]{2,1,0:T(8,128)S(1)}) custom-call(s32[16]{0:T(128)S(4)} %get-tuple-element.63.refs_0_.facts, bf16[128,3072]{1,0:T(8,128)(2,1)S(1)} %get-tuple-element.90.refs_1_, bf16[128,3072]{1,0:T(8,128)(2,1)S(1)} %get-tuple-element.91.refs_2_, ...), custom_call_target="tpu_custom_call" | custom-call | flops 8053063680 | bytes 1000 | tf_op jit(solution)/shard_map/pallas_call | solution.py:100
  30.1 0.0 collective-permute-done.4.refs_2_.refs_4_
  30.1 0.1 shard_map.128
  30.2 0.5 collective-permute-start.6
  30.7 2.3 %collective-permute-start.5 = (bf16[2,128,256]{2,1,0:T(8,128)(2,1)S(1)}, bf16[2,128,256]{2,1,0:T(8,128)(2,1)S(1)}, u32[]{:S(2)}, u32[]{:S(2)}) collective-permute-start(bf16[2,128,256]{2,1,0:T(8,128)(2,1)S(1)} %get-tuple-element.100.refs_12_), channel_id=1, source_target_pairs={{0,8},{4,12},{8,0},{12,4},{1,9},{5,13},{9,1},{13,5},{2,10},{6,14},... | collective-permute-start | bytes 393224 | tf_op jit(solution)/shard_map/ppermute | solution.py:759
  33.0 0.1 shard_map.129.refs_13_
  33.1 1.6 %collective-permute-start.9 = (bf16[128,512]{1,0:T(8,128)(2,1)S(1)}, bf16[128,512]{1,0:T(8,128)(2,1)S(1)}, u32[]{:S(2)}, u32[]{:S(2)}) collective-permute-start(bf16[128,512]{1,0:T(8,128)(2,1)S(1)} %shard_map.129.refs_13_), channel_id=1, source_target_pairs={{0,2},{2,0},{1,3},{3,1},{4,6},{6,4},{5,7},{7,5},{8,10},{10,8},{9,1... | collective-permute-start | bytes 393224 | tf_op jit(solution)/shard_map/ppermute | solution.py:759
  34.6 3.7 %shard_map.130 = (bf16[384,4096]{1,0:T(8,128)(2,1)}, f32[8,128]{1,0:T(8,128)S(1)}, bf16[2560,1024]{1,0:T(8,128)(2,1)S(1)}) custom-call(s32[16]{0:T(128)S(4)} %get-tuple-element.63.refs_0_.facts, bf16[2,2,128,256]{3,2,1,0:T(8,128)(2,1)S(1)} %shard_map.125.refs_13_.refs_1_, bf16[2,2,128,256]{3,2,1,0:T(8,128)(2,1)S(1)} %collective-permute-done.3.refs_13_.refs_2_, ...), custom_call_target="tpu_custom_call" | custom-call | flops 1000 | bytes 1000 | tf_op jit(solution)/shard_map/pallas_call | solution.py:100
  38.4 0.0 collective-permute-done.6.refs_3_
  38.4 1.3 %collective-permute-done.5.refs_2_ = bf16[2,128,256]{2,1,0:T(8,128)(2,1)S(1)} collective-permute-done((bf16[2,128,256]{2,1,0:T(8,128)(2,1)S(1)}, bf16[2,128,256]{2,1,0:T(8,128)(2,1)S(1)}, u32[]{:S(2)}, u32[]{:S(2)}) %collective-permute-start.5) | collective-permute-done | bytes 131104 | tf_op jit(solution)/shard_map/ppermute | solution.py:759
  39.6 0.1 shard_map.131
  39.7 0.1 collective-permute-start.7
  39.8 0.0 collective-permute-done.8.refs_1_
  39.8 2.6 %shard_map.132 = (bf16[384,2560]{1,0:T(8,128)(2,1)}, bf16[384,512]{1,0:T(8,128)(2,1)}, bf16[384,512]{1,0:T(8,128)(2,1)}, f32[8,128]{1,0:T(8,128)S(1)}) custom-call(s32[16]{0:T(128)S(4)} %get-tuple-element.63.refs_0_.facts, bf16[256,512]{1,0:T(8,128)(2,1)S(1)} %get-tuple-element.109.refs_0_.refs_3_, bf16[256,512]{1,0:T(8,128)(2,1)S(1)} %collective-permute-done.8.refs_1_, ...), custom_call_target="tpu_custom_call" | custom-call | flops 1000 | bytes 1000 | tf_op jit(solution)/shard_map/pallas_call | solution.py:653
  42.4 0.0 collective-permute-done.9.refs_4_.refs_3_
  42.4 2.3 %collective-permute-done.7.refs_2_ = bf16[2,128,256]{2,1,0:T(8,128)(2,1)S(1)} collective-permute-done((bf16[2,128,256]{2,1,0:T(8,128)(2,1)S(1)}, bf16[2,128,256]{2,1,0:T(8,128)(2,1)S(1)}, u32[]{:S(2)}, u32[]{:S(2)}) %collective-permute-start.7) | collective-permute-done | bytes 131104 | tf_op jit(solution)/shard_map/ppermute | solution.py:759
  44.7 0.1 collective-permute-start.10
  44.8 1.3 %collective-permute-start.12 = (bf16[128,256]{1,0:T(8,128)(2,1)S(1)}, bf16[128,256]{1,0:T(8,128)(2,1)S(1)}, u32[]{:S(2)}, u32[]{:S(2)}) collective-permute-start(bf16[128,256]{1,0:T(8,128)(2,1)S(1)} %get-tuple-element.114), channel_id=1, source_target_pairs={{0,3},{1,2},{2,1},{3,0},{4,7},{5,6},{6,5},{7,4},{8,11},{9,10},{10,... | collective-permute-start | bytes 196616 | tf_op jit(solution)/shard_map/ppermute | solution.py:847
  46.1 0.9 %collective-permute-start.11 = (bf16[128,256]{1,0:T(8,128)(2,1)S(1)}, bf16[128,256]{1,0:T(8,128)(2,1)S(1)}, u32[]{:S(2)}, u32[]{:S(2)}) collective-permute-start(bf16[128,256]{1,0:T(8,128)(2,1)S(1)} %get-tuple-element.114), channel_id=1, source_target_pairs={{0,2},{2,0},{1,3},{3,1},{4,6},{6,4},{5,7},{7,5},{8,10},{10,8},{9,1... | collective-permute-start | bytes 196616 | tf_op jit(solution)/shard_map/ppermute | solution.py:759
  47.0 0.0 collective-permute-done.10.refs_3_
  47.0 0.1 shard_map.134
  47.1 0.8 %shard_map.135.refs_2_ = f32[2560,128]{1,0:T(8,128)S(1)} custom-call(s32[16]{0:T(128)S(4)} %get-tuple-element.63.refs_0_.facts, bf16[2560,1024]{1,0:T(8,128)(2,1)S(1)} %get-tuple-element.103.refs_4_.refs_1_, bf16[128,512]{1,0:T(8,128)(2,1)S(1)} %get-tuple-element.113.refs_2_.refs_7_), custom_call_target="tpu_custom_call" | custom-call | flops 1000 | bytes 1000 | tf_op jit(solution)/shard_map/pallas_call | solution.py:714
  47.9 0.8 %collective-permute-done.12.refs_5_ = bf16[128,256]{1,0:T(8,128)(2,1)S(1)} collective-permute-done((bf16[128,256]{1,0:T(8,128)(2,1)S(1)}, bf16[128,256]{1,0:T(8,128)(2,1)S(1)}, u32[]{:S(2)}, u32[]{:S(2)}) %collective-permute-start.12) | collective-permute-done | bytes 65568 | tf_op jit(solution)/shard_map/ppermute | solution.py:847
  48.7 2.0 %collective-permute-done.11.refs_4_ = bf16[128,256]{1,0:T(8,128)(2,1)S(1)} collective-permute-done((bf16[128,256]{1,0:T(8,128)(2,1)S(1)}, bf16[128,256]{1,0:T(8,128)(2,1)S(1)}, u32[]{:S(2)}, u32[]{:S(2)}) %collective-permute-start.11) | collective-permute-done | bytes 65568 | tf_op jit(solution)/shard_map/ppermute | solution.py:759
  50.7 1.7 %shard_map.136 = (bf16[384,2560]{1,0:T(8,128)(2,1)}, bf16[384,512]{1,0:T(8,128)(2,1)}, bf16[384,512]{1,0:T(8,128)(2,1)}) custom-call(s32[16]{0:T(128)S(4)} %get-tuple-element.63.refs_0_.facts, bf16[2560,1024]{1,0:T(8,128)(2,1)S(1)} %get-tuple-element.103.refs_4_.refs_1_, ...), custom_call_target="tpu_custom_call", output_to_operand_aliasing={{0}: (8, {}), {1}: (9, {}), {2}: (10, {})} | custom-call | flops 1000 | bytes 1000 | tf_op jit(solution)/shard_map/pallas_call | solution.py:100
  (4 shorter events, 0.1 us)
Async XLA Ops:
  1.7 1.7 %collective-permute-start = (bf16[2,128,512]{2,1,0:T(8,128)(2,1)S(1)}, bf16[2,128,512]{2,1,0:T(8,128)(2,1)S(1)}, u32[]{:S(2)}, u32[]{:S(2)}) collective-permute-start(bf16[2,128,512]{2,1,0:T(8,128)(2,1)S(1)} %get-tuple-element.64.refs_1_.refs_9_), channel_id=1, source_target_pairs={{0,1},{1,0},{2,3},{3,2},{4,5},{5,4},{6,7},{7,6},{8,9},{9,8},{10,11... | collective-permute-start | bytes 786440 | tf_op jit(solution)/shard_map/ppermute | solution.py:759
  3.4 10.1 %collective-permute-start.1 = (bf16[2,128,256]{2,1,0:T(8,128)(2,1)S(1)}, bf16[2,128,256]{2,1,0:T(8,128)(2,1)S(1)}, u32[]{:S(2)}, u32[]{:S(2)}) collective-permute-start(bf16[2,128,256]{2,1,0:T(8,128)(2,1)S(1)} %shard_map.121.refs_9_.refs_1_), channel_id=1, source_target_pairs={{0,4},{4,0},{8,12},{12,8},{1,5},{5,1},{9,13},{13,9},{2,6},{6,2},{1... | collective-permute-start | bytes 393224 | tf_op jit(solution)/shard_map/ppermute | solution.py:759
  13.5 9.3 %collective-permute-start.2 = (bf16[2,128,256]{2,1,0:T(8,128)(2,1)S(1)}, bf16[2,128,256]{2,1,0:T(8,128)(2,1)S(1)}, u32[]{:S(2)}, u32[]{:S(2)}) collective-permute-start(bf16[2,128,256]{2,1,0:T(8,128)(2,1)S(1)} %shard_map.123.refs_15_.refs_3_), channel_id=1, source_target_pairs={{0,8},{4,12},{8,0},{12,4},{1,9},{5,13},{9,1},{13,5},{2,10},{6,14},... | collective-permute-start | bytes 393224 | tf_op jit(solution)/shard_map/ppermute | solution.py:759
  21.2 18.6 %collective-permute-start.8 = (bf16[256,512]{1,0:T(8,128)(2,1)S(1)}, bf16[256,512]{1,0:T(8,128)(2,1)S(1)}, u32[]{:S(2)}, u32[]{:S(2)}) collective-permute-start(bf16[256,512]{1,0:T(8,128)(2,1)S(1)} %get-tuple-element.109.refs_0_.refs_3_), channel_id=1, source_target_pairs={{0,2},{2,0},{1,3},{3,1},{4,6},{6,4},{5,7},{7,5},{8,10},{10,8},{9,1... | collective-permute-start | bytes 786440 | tf_op jit(solution)/shard_map/ppermute | solution.py:759
  22.8 4.0 %collective-permute-start.3 = (bf16[2,2,128,256]{3,2,1,0:T(8,128)(2,1)S(1)}, bf16[2,2,128,256]{3,2,1,0:T(8,128)(2,1)S(1)}, u32[]{:S(2)}, u32[]{:S(2)}) collective-permute-start(bf16[2,2,128,256]{3,2,1,0:T(8,128)(2,1)S(1)} %shard_map.125.refs_13_.refs_1_), channel_id=1, source_target_pairs={{0,1},{1,0},{2,3},{3,2},{4,5},{5,4},{6,7},{7,6},{8,9},{9,8},{10,11... | collective-permute-start | bytes 786440 | tf_op jit(solution)/shard_map/ppermute | solution.py:759
  26.3 3.9 %collective-permute-start.4 = (bf16[8,128,256]{2,1,0:T(8,128)(2,1)S(1)}, bf16[8,128,256]{2,1,0:T(8,128)(2,1)S(1)}, u32[]{:S(2)}, u32[]{:S(2)}) collective-permute-start(bf16[8,128,256]{2,1,0:T(8,128)(2,1)S(1)} %get-tuple-element.99), channel_id=1, source_target_pairs={{0,1},{1,0},{2,3},{3,2},{4,5},{5,4},{6,7},{7,6},{8,9},{9,8},{10,11... | collective-permute-start | bytes 1572872 | tf_op jit(solution)/shard_map/ppermute | solution.py:759
  30.2 8.2 %collective-permute-start.6 = (bf16[2,128,256]{2,1,0:T(8,128)(2,1)S(1)}, bf16[2,128,256]{2,1,0:T(8,128)(2,1)S(1)}, u32[]{:S(2)}, u32[]{:S(2)}) collective-permute-start(bf16[2,128,256]{2,1,0:T(8,128)(2,1)S(1)} %get-tuple-element.105), channel_id=1, source_target_pairs={{0,4},{4,0},{8,12},{12,8},{1,5},{5,1},{9,13},{13,9},{2,6},{6,2},{1... | collective-permute-start | bytes 393224 | tf_op jit(solution)/shard_map/ppermute | solution.py:759
  30.7 8.9 %collective-permute-start.5 = (bf16[2,128,256]{2,1,0:T(8,128)(2,1)S(1)}, bf16[2,128,256]{2,1,0:T(8,128)(2,1)S(1)}, u32[]{:S(2)}, u32[]{:S(2)}) collective-permute-start(bf16[2,128,256]{2,1,0:T(8,128)(2,1)S(1)} %get-tuple-element.100.refs_12_), channel_id=1, source_target_pairs={{0,8},{4,12},{8,0},{12,4},{1,9},{5,13},{9,1},{13,5},{2,10},{6,14},... | collective-permute-start | bytes 393224 | tf_op jit(solution)/shard_map/ppermute | solution.py:759
  33.1 9.3 %collective-permute-start.9 = (bf16[128,512]{1,0:T(8,128)(2,1)S(1)}, bf16[128,512]{1,0:T(8,128)(2,1)S(1)}, u32[]{:S(2)}, u32[]{:S(2)}) collective-permute-start(bf16[128,512]{1,0:T(8,128)(2,1)S(1)} %shard_map.129.refs_13_), channel_id=1, source_target_pairs={{0,2},{2,0},{1,3},{3,1},{4,6},{6,4},{5,7},{7,5},{8,10},{10,8},{9,1... | collective-permute-start | bytes 393224 | tf_op jit(solution)/shard_map/ppermute | solution.py:759
  39.7 5.0 %collective-permute-start.7 = (bf16[2,128,256]{2,1,0:T(8,128)(2,1)S(1)}, bf16[2,128,256]{2,1,0:T(8,128)(2,1)S(1)}, u32[]{:S(2)}, u32[]{:S(2)}) collective-permute-start(bf16[2,128,256]{2,1,0:T(8,128)(2,1)S(1)} %get-tuple-element.108.refs_5_), channel_id=1, source_target_pairs={{0,4},{4,0},{8,12},{12,8},{1,5},{5,1},{9,13},{13,9},{2,6},{6,2},{1... | collective-permute-start | bytes 393224 | tf_op jit(solution)/shard_map/ppermute | solution.py:759
  44.7 2.2 %collective-permute-start.10 = (bf16[2,128,256]{2,1,0:T(8,128)(2,1)S(1)}, bf16[2,128,256]{2,1,0:T(8,128)(2,1)S(1)}, u32[]{:S(2)}, u32[]{:S(2)}) collective-permute-start(bf16[2,128,256]{2,1,0:T(8,128)(2,1)S(1)} %get-tuple-element.112.refs_2_), channel_id=1, source_target_pairs={{0,1},{1,0},{2,3},{3,2},{4,5},{5,4},{6,7},{7,6},{8,9},{9,8},{10,11... | collective-permute-start | bytes 393224 | tf_op jit(solution)/shard_map/ppermute | solution.py:759
  44.8 3.9 %collective-permute-start.12 = (bf16[128,256]{1,0:T(8,128)(2,1)S(1)}, bf16[128,256]{1,0:T(8,128)(2,1)S(1)}, u32[]{:S(2)}, u32[]{:S(2)}) collective-permute-start(bf16[128,256]{1,0:T(8,128)(2,1)S(1)} %get-tuple-element.114), channel_id=1, source_target_pairs={{0,3},{1,2},{2,1},{3,0},{4,7},{5,6},{6,5},{7,4},{8,11},{9,10},{10,... | collective-permute-start | bytes 196616 | tf_op jit(solution)/shard_map/ppermute | solution.py:847
  46.1 4.6 %collective-permute-start.11 = (bf16[128,256]{1,0:T(8,128)(2,1)S(1)}, bf16[128,256]{1,0:T(8,128)(2,1)S(1)}, u32[]{:S(2)}, u32[]{:S(2)}) collective-permute-start(bf16[128,256]{1,0:T(8,128)(2,1)S(1)} %get-tuple-element.114), channel_id=1, source_target_pairs={{0,2},{2,0},{1,3},{3,1},{4,6},{6,4},{5,7},{7,5},{8,10},{10,8},{9,1... | collective-permute-start | bytes 196616 | tf_op jit(solution)/shard_map/ppermute | solution.py:759

commit v17 on v16

--- a/solution.py
+++ b/solution.py
@@ -329,7 +329,6 @@
 
             def load(key, src, dst):
                 copies[key] = pltpu.make_async_copy(src, dst, load_sem.at[len(copies)])
-                copies[key].start()
 
             for lo, hi in order.runs(0, kv_total):
                 for name in ("k", "v"):
@@ -340,11 +339,15 @@
                     at = pl.ds(order.at(facts, lo, group), (hi - lo) * group)
                     here = slice(lo * group, hi * group)
                     load((name, lo), far_ref(name).at[at], held(name).at[here])
-            shared_loads = list(copies)
             for kv in range(kv_total):
                 at = pl.ds(order.at(facts, kv, group * HD), group * HD)
                 for name in ("q", "g"):
                     load((name, kv), far_ref(name).at[:, at], held((name, kv)))
+            rows_of = [(name, 0) for name in ("k", "v", "norms", "deltas")]
+            first = [*rows_of, ("q", kvs[0]), ("g", kvs[0])]
+            rest = [key for key in copies if key not in first]
+            for key in first:
+                copies[key].start()
         k, v, norms, deltas = (held(name) for name in ("k", "v", "norms", "deltas"))
 
         def arrived(*keys):
@@ -362,13 +365,21 @@
                 out[4 + kind] = more[kind, :, :width]
                 out[6 + kind] = more[kind, :, width:]
         owns2 = facts[OWNS2] == 1
-        if loading:
-            arrived(*shared_loads)
-            lane = lax.broadcasted_iota(I32, norms.shape, 1)
+
+        def set_norms(lo, hi):
+            rows = slice(lo * group, hi * group)
+            lane = lax.broadcasted_iota(I32, ((hi - lo) * group, ROWS), 1)
             limit = jnp.where(
                 lane < PAGE, facts[N0], jnp.where(lane < 2 * PAGE, facts[N1], facts[N2])
             )
-            norms[...] = jnp.where(lane % PAGE < limit, norms[...] * (1.0 / SCALE), BLOCKED)
+            norms[rows] = jnp.where(lane % PAGE < limit, norms[rows] * (1.0 / SCALE), BLOCKED)
+
+        if loading:
+            arrived(*first)
+            for key in rest:
+                copies[key].start()
+            ready, *later = order.runs(0, kv_total)
+            set_norms(*ready)
         lower = lambda rows: lax.broadcasted_iota(I32, (rows, PAGE), 1) <= (
             lax.broadcasted_iota(I32, (rows, PAGE), 0) % PAGE
         )
@@ -522,7 +533,10 @@
             (put_own if own else put_shared)(n)
         for c in sends:
             c.wait()
-        arrived(*list(copies))
+        if loading:
+            arrived(*list(copies))
+            for heads in later:
+                set_norms(*heads)
 
     made = kernel_call(
         body, facts, near, far, outs, scratch, aliases, after,

time: 52.8 us -> 53.5 us (1.013)
  Pallas kernels: 29.1 us -> 29.8 us
    pallas_call x14, Pallas kernels: 24.6 us -> 25.3 us  [kernel_call(): pl.pallas_call(kernel, out_shape=tuple((pltpu.VMEM(s, d) if inside else j...]
  transfers between devices with their start and end apart: 13 -> 13, of which waited for: 5 -> 5; matrix products, arithmetic and copies ran while one was open for 0% -> 0% of each run, Pallas kernels for 50% -> 51%
where the time goes in v17:
time: 53.5 us; the launch traced here: 53.3 us
  Pallas kernels  29.8 us (56%)
  starting transfers between devices  15 us (28%)
  waiting for transfers between devices  7.49 us (14%)
  between operations  0.97 us (2%)
    pallas_call x14, Pallas kernels, kernel_call(): pl.pallas_call(kernel, out_shape=tuple((pltpu.VMEM(s, d) if inside else j...  25.3 us
    ppermute x12, starting transfers between devices, flipped(): lax.ppermute(block, axis, [(i, i ^ bit) for i in range(count) if i ^ bit...  13.8 us
    ppermute x12, waiting for transfers between devices, flipped(): lax.ppermute(block, axis, [(i, i ^ bit) for i in range(count) if i ^ bit...  6.7 us
    pallas_call x1, Pallas kernels, input_grad(): pl.pallas_call(body, out_shape=(jax.ShapeDtypeStruct((ROWS, out_cols), BF...  2.65 us
    ppermute x1, starting transfers between devices, over_chips(): lax.ppermute(values, ('tensor', 'sub'), [(i, 3 - i) for i in range(4)])  1.26 us
  transfers between devices with their start and end apart: 13, of which 5 were waited for; matrix products, arithmetic and copies ran while one was open for 0% of the time, Pallas kernels for 51%

profile of v17, /device:TPU:0, one launch (start us, length us, event | category | flops | bytes accessed | tf_op | source)
XLA Modules:
  0.0 53.3 jit_solution(9071480833328138185)
XLA Ops:
  0.6 1.0 %shard_map.120 = (s32[16]{0:T(128)S(4)}, bf16[2,128,512]{2,1,0:T(8,128)(2,1)S(1)}) custom-call(s32[1]{0:T(128)} %bitcast.side_ref, s32[1,5]{1,0:T(1,128)} %ids_ref.1, s32[1,3]{1,0:T(1,128)} %counts_ref.1, bf16[384,512]{1,0:T(8,128)(2,1)} %refs_5_.1, bf16[384,512]{1,0:T(8,128)(2,1)} %refs_6_.1), custom_call_target="tpu_custom_call" | custom-call | tf_op jit(solution)/shard_map/pallas_call | solution.py:141
  1.7 0.5 collective-permute-start
  2.2 1.2 %collective-permute-done.refs_2_.refs_10_ = bf16[2,128,512]{2,1,0:T(8,128)(2,1)S(1)} collective-permute-done((bf16[2,128,512]{2,1,0:T(8,128)(2,1)S(1)}, bf16[2,128,512]{2,1,0:T(8,128)(2,1)S(1)}, u32[]{:S(2)}, u32[]{:S(2)}) %collective-permute-start) | collective-permute-done | bytes 262176 | tf_op jit(solution)/shard_map/ppermute | solution.py:773
  3.4 3.0 %collective-permute-start.1 = (bf16[2,128,256]{2,1,0:T(8,128)(2,1)S(1)}, bf16[2,128,256]{2,1,0:T(8,128)(2,1)S(1)}, u32[]{:S(2)}, u32[]{:S(2)}) collective-permute-start(bf16[2,128,256]{2,1,0:T(8,128)(2,1)S(1)} %shard_map.121.refs_9_.refs_1_), channel_id=1, source_target_pairs={{0,4},{4,0},{8,12},{12,8},{1,5},{5,1},{9,13},{13,9},{2,6},{6,2},{1... | collective-permute-start | bytes 393224 | tf_op jit(solution)/shard_map/ppermute | solution.py:773
  6.4 7.7 %shard_map.122 = (f32[384,1024]{1,0:T(8,128)S(1)}, bf16[128,3072]{1,0:T(8,128)(2,1)S(1)}, bf16[128,3072]{1,0:T(8,128)(2,1)S(1)}, f32[384,1024]{1,0:T(8,128)S(1)}...) custom-call(s32[16]{0:T(128)S(4)} %get-tuple-element.63.refs_0_.fact, ...), custom_call_target="tpu_custom_call" | custom-call | flops 8053063680 | bytes 1000 | tf_op jit(solution)/shard_map/pallas_call | solution.py:100
  14.1 0.0 collective-permute-done.1.refs_2_
  14.2 2.7 %collective-permute-start.2 = (bf16[2,128,256]{2,1,0:T(8,128)(2,1)S(1)}, bf16[2,128,256]{2,1,0:T(8,128)(2,1)S(1)}, u32[]{:S(2)}, u32[]{:S(2)}) collective-permute-start(bf16[2,128,256]{2,1,0:T(8,128)(2,1)S(1)} %shard_map.123.refs_15_.refs_3_), channel_id=1, source_target_pairs={{0,8},{4,12},{8,0},{12,4},{1,9},{5,13},{9,1},{13,5},{2,10},{6,14},... | collective-permute-start | bytes 393224 | tf_op jit(solution)/shard_map/ppermute | solution.py:773
  16.8 5.1 %shard_map.124 = (f32[384,1024]{1,0:T(8,128)S(1)}, bf16[128,3072]{1,0:T(8,128)(2,1)S(1)}, bf16[128,3072]{1,0:T(8,128)(2,1)S(1)}, f32[384,1024]{1,0:T(8,128)S(1)}...) custom-call(s32[16]{0:T(128)S(4)} %get-tuple-element.63.refs_0_.fact, ...), custom_call_target="tpu_custom_call" | custom-call | flops 8053063680 | bytes 1000 | tf_op jit(solution)/shard_map/pallas_call | solution.py:100
  21.9 1.6 %collective-permute-start.8 = (bf16[256,512]{1,0:T(8,128)(2,1)S(1)}, bf16[256,512]{1,0:T(8,128)(2,1)S(1)}, u32[]{:S(2)}, u32[]{:S(2)}) collective-permute-start(bf16[256,512]{1,0:T(8,128)(2,1)S(1)} %get-tuple-element.109.refs_0_.refs_3_), channel_id=1, source_target_pairs={{0,2},{2,0},{1,3},{3,1},{4,6},{6,4},{5,7},{7,5},{8,10},{10,8},{9,1... | collective-permute-start | bytes 786440 | tf_op jit(solution)/shard_map/ppermute | solution.py:773
  23.4 0.0 collective-permute-done.2.refs_4_
  23.5 0.1 collective-permute-start.3
  23.6 3.4 %shard_map.126 = (bf16[3072,256]{1,0:T(8,128)(2,1)S(1)}, bf16[3072,256]{1,0:T(8,128)(2,1)S(1)}, bf16[8,128,256]{2,1,0:T(8,128)(2,1)S(1)}) custom-call(s32[16]{0:T(128)S(4)} %get-tuple-element.63.refs_0_.facts, bf16[128,3072]{1,0:T(8,128)(2,1)S(1)} %get-tuple-element.78.refs_1_, bf16[128,3072]{1,0:T(8,128)(2,1)S(1)} %get-tuple-element.79.refs_2_, ...), custom_call_target="tpu_custom_call" | custom-call | flops 8053063680 | bytes 1000 | tf_op jit(solution)/shard_map/pallas_call | solution.py:100
  27.0 0.5 %collective-permute-start.4 = (bf16[8,128,256]{2,1,0:T(8,128)(2,1)S(1)}, bf16[8,128,256]{2,1,0:T(8,128)(2,1)S(1)}, u32[]{:S(2)}, u32[]{:S(2)}) collective-permute-start(bf16[8,128,256]{2,1,0:T(8,128)(2,1)S(1)} %get-tuple-element.99), channel_id=1, source_target_pairs={{0,1},{1,0},{2,3},{3,2},{4,5},{5,4},{6,7},{7,6},{8,9},{9,8},{10,11... | collective-permute-start | bytes 1572872 | tf_op jit(solution)/shard_map/ppermute | solution.py:773
  27.5 0.0 collective-permute-done.3.refs_13_.refs_2_
  27.5 3.3 %shard_map.127 = (bf16[3072,256]{1,0:T(8,128)(2,1)S(1)}, bf16[3072,256]{1,0:T(8,128)(2,1)S(1)}, f32[4,128,256]{2,1,0:T(8,128)S(1)}) custom-call(s32[16]{0:T(128)S(4)} %get-tuple-element.63.refs_0_.facts, bf16[128,3072]{1,0:T(8,128)(2,1)S(1)} %get-tuple-element.90.refs_1_, bf16[128,3072]{1,0:T(8,128)(2,1)S(1)} %get-tuple-element.91.refs_2_, ...), custom_call_target="tpu_custom_call" | custom-call | flops 8053063680 | bytes 1000 | tf_op jit(solution)/shard_map/pallas_call | solution.py:100
  30.8 0.0 collective-permute-done.4.refs_2_.refs_4_
  30.8 0.1 shard_map.128
  30.9 0.5 collective-permute-start.6
  31.4 2.3 %collective-permute-start.5 = (bf16[2,128,256]{2,1,0:T(8,128)(2,1)S(1)}, bf16[2,128,256]{2,1,0:T(8,128)(2,1)S(1)}, u32[]{:S(2)}, u32[]{:S(2)}) collective-permute-start(bf16[2,128,256]{2,1,0:T(8,128)(2,1)S(1)} %get-tuple-element.100.refs_12_), channel_id=1, source_target_pairs={{0,8},{4,12},{8,0},{12,4},{1,9},{5,13},{9,1},{13,5},{2,10},{6,14},... | collective-permute-start | bytes 393224 | tf_op jit(solution)/shard_map/ppermute | solution.py:773
  33.7 0.1 shard_map.129.refs_13_
  33.8 1.6 %collective-permute-start.9 = (bf16[128,512]{1,0:T(8,128)(2,1)S(1)}, bf16[128,512]{1,0:T(8,128)(2,1)S(1)}, u32[]{:S(2)}, u32[]{:S(2)}) collective-permute-start(bf16[128,512]{1,0:T(8,128)(2,1)S(1)} %shard_map.129.refs_13_), channel_id=1, source_target_pairs={{0,2},{2,0},{1,3},{3,1},{4,6},{6,4},{5,7},{7,5},{8,10},{10,8},{9,1... | collective-permute-start | bytes 393224 | tf_op jit(solution)/shard_map/ppermute | solution.py:773
  35.3 3.7 %shard_map.130 = (bf16[384,4096]{1,0:T(8,128)(2,1)}, f32[8,128]{1,0:T(8,128)S(1)}, bf16[2560,1024]{1,0:T(8,128)(2,1)S(1)}) custom-call(s32[16]{0:T(128)S(4)} %get-tuple-element.63.refs_0_.facts, bf16[2,2,128,256]{3,2,1,0:T(8,128)(2,1)S(1)} %shard_map.125.refs_13_.refs_1_, bf16[2,2,128,256]{3,2,1,0:T(8,128)(2,1)S(1)} %collective-permute-done.3.refs_13_.refs_2_, ...), custom_call_target="tpu_custom_call" | custom-call | flops 1000 | bytes 1000 | tf_op jit(solution)/shard_map/pallas_call | solution.py:100
  39.0 0.0 collective-permute-done.6.refs_3_
  39.0 1.3 %collective-permute-done.5.refs_2_ = bf16[2,128,256]{2,1,0:T(8,128)(2,1)S(1)} collective-permute-done((bf16[2,128,256]{2,1,0:T(8,128)(2,1)S(1)}, bf16[2,128,256]{2,1,0:T(8,128)(2,1)S(1)}, u32[]{:S(2)}, u32[]{:S(2)}) %collective-permute-start.5) | collective-permute-done | bytes 131104 | tf_op jit(solution)/shard_map/ppermute | solution.py:773
  40.3 0.1 shard_map.131
  40.4 0.1 collective-permute-start.7
  40.4 0.0 collective-permute-done.8.refs_1_
  40.5 2.6 %shard_map.132 = (bf16[384,2560]{1,0:T(8,128)(2,1)}, bf16[384,512]{1,0:T(8,128)(2,1)}, bf16[384,512]{1,0:T(8,128)(2,1)}, f32[8,128]{1,0:T(8,128)S(1)}) custom-call(s32[16]{0:T(128)S(4)} %get-tuple-element.63.refs_0_.facts, bf16[256,512]{1,0:T(8,128)(2,1)S(1)} %get-tuple-element.109.refs_0_.refs_3_, bf16[256,512]{1,0:T(8,128)(2,1)S(1)} %collective-permute-done.8.refs_1_, ...), custom_call_target="tpu_custom_call" | custom-call | flops 1000 | bytes 1000 | tf_op jit(solution)/shard_map/pallas_call | solution.py:667
  43.1 0.0 collective-permute-done.9.refs_4_.refs_3_
  43.1 2.3 %collective-permute-done.7.refs_2_ = bf16[2,128,256]{2,1,0:T(8,128)(2,1)S(1)} collective-permute-done((bf16[2,128,256]{2,1,0:T(8,128)(2,1)S(1)}, bf16[2,128,256]{2,1,0:T(8,128)(2,1)S(1)}, u32[]{:S(2)}, u32[]{:S(2)}) %collective-permute-start.7) | collective-permute-done | bytes 131104 | tf_op jit(solution)/shard_map/ppermute | solution.py:773
  45.4 0.1 collective-permute-start.10
  45.5 1.3 %collective-permute-start.12 = (bf16[128,256]{1,0:T(8,128)(2,1)S(1)}, bf16[128,256]{1,0:T(8,128)(2,1)S(1)}, u32[]{:S(2)}, u32[]{:S(2)}) collective-permute-start(bf16[128,256]{1,0:T(8,128)(2,1)S(1)} %get-tuple-element.114), channel_id=1, source_target_pairs={{0,3},{1,2},{2,1},{3,0},{4,7},{5,6},{6,5},{7,4},{8,11},{9,10},{10,... | collective-permute-start | bytes 196616 | tf_op jit(solution)/shard_map/ppermute | solution.py:861
  46.8 0.9 %collective-permute-start.11 = (bf16[128,256]{1,0:T(8,128)(2,1)S(1)}, bf16[128,256]{1,0:T(8,128)(2,1)S(1)}, u32[]{:S(2)}, u32[]{:S(2)}) collective-permute-start(bf16[128,256]{1,0:T(8,128)(2,1)S(1)} %get-tuple-element.114), channel_id=1, source_target_pairs={{0,2},{2,0},{1,3},{3,1},{4,6},{6,4},{5,7},{7,5},{8,10},{10,8},{9,1... | collective-permute-start | bytes 196616 | tf_op jit(solution)/shard_map/ppermute | solution.py:773
  47.7 0.0 collective-permute-done.10.refs_3_
  47.7 0.1 shard_map.134
  47.8 0.8 %shard_map.135.refs_2_ = f32[2560,128]{1,0:T(8,128)S(1)} custom-call(s32[16]{0:T(128)S(4)} %get-tuple-element.63.refs_0_.facts, bf16[2560,1024]{1,0:T(8,128)(2,1)S(1)} %get-tuple-element.103.refs_4_.refs_1_, bf16[128,512]{1,0:T(8,128)(2,1)S(1)} %get-tuple-element.113.refs_2_.refs_7_), custom_call_target="tpu_custom_call" | custom-call | flops 1000 | bytes 1000 | tf_op jit(solution)/shard_map/pallas_call | solution.py:728
  48.6 0.8 %collective-permute-done.12.refs_5_ = bf16[128,256]{1,0:T(8,128)(2,1)S(1)} collective-permute-done((bf16[128,256]{1,0:T(8,128)(2,1)S(1)}, bf16[128,256]{1,0:T(8,128)(2,1)S(1)}, u32[]{:S(2)}, u32[]{:S(2)}) %collective-permute-start.12) | collective-permute-done | bytes 65568 | tf_op jit(solution)/shard_map/ppermute | solution.py:861
  49.4 2.0 %collective-permute-done.11.refs_4_ = bf16[128,256]{1,0:T(8,128)(2,1)S(1)} collective-permute-done((bf16[128,256]{1,0:T(8,128)(2,1)S(1)}, bf16[128,256]{1,0:T(8,128)(2,1)S(1)}, u32[]{:S(2)}, u32[]{:S(2)}) %collective-permute-start.11) | collective-permute-done | bytes 65568 | tf_op jit(solution)/shard_map/ppermute | solution.py:773
  51.4 1.7 %shard_map.136 = (bf16[384,2560]{1,0:T(8,128)(2,1)}, bf16[384,512]{1,0:T(8,128)(2,1)}, bf16[384,512]{1,0:T(8,128)(2,1)}) custom-call(s32[16]{0:T(128)S(4)} %get-tuple-element.63.refs_0_.facts, bf16[2560,1024]{1,0:T(8,128)(2,1)S(1)} %get-tuple-element.103.refs_4_.refs_1_, ...), custom_call_target="tpu_custom_call", output_to_operand_aliasing={{0}: (8, {}), {1}: (9, {}), {2}: (10, {})} | custom-call | flops 1000 | bytes 1000 | tf_op jit(solution)/shard_map/pallas_call | solution.py:100
  (4 shorter events, 0.1 us)
Async XLA Ops:
  1.7 1.7 %collective-permute-start = (bf16[2,128,512]{2,1,0:T(8,128)(2,1)S(1)}, bf16[2,128,512]{2,1,0:T(8,128)(2,1)S(1)}, u32[]{:S(2)}, u32[]{:S(2)}) collective-permute-start(bf16[2,128,512]{2,1,0:T(8,128)(2,1)S(1)} %get-tuple-element.64.refs_1_.refs_9_), channel_id=1, source_target_pairs={{0,1},{1,0},{2,3},{3,2},{4,5},{5,4},{6,7},{7,6},{8,9},{9,8},{10,11... | collective-permute-start | bytes 786440 | tf_op jit(solution)/shard_map/ppermute | solution.py:773
  3.4 10.7 %collective-permute-start.1 = (bf16[2,128,256]{2,1,0:T(8,128)(2,1)S(1)}, bf16[2,128,256]{2,1,0:T(8,128)(2,1)S(1)}, u32[]{:S(2)}, u32[]{:S(2)}) collective-permute-start(bf16[2,128,256]{2,1,0:T(8,128)(2,1)S(1)} %shard_map.121.refs_9_.refs_1_), channel_id=1, source_target_pairs={{0,4},{4,0},{8,12},{12,8},{1,5},{5,1},{9,13},{13,9},{2,6},{6,2},{1... | collective-permute-start | bytes 393224 | tf_op jit(solution)/shard_map/ppermute | solution.py:773
  14.2 9.3 %collective-permute-start.2 = (bf16[2,128,256]{2,1,0:T(8,128)(2,1)S(1)}, bf16[2,128,256]{2,1,0:T(8,128)(2,1)S(1)}, u32[]{:S(2)}, u32[]{:S(2)}) collective-permute-start(bf16[2,128,256]{2,1,0:T(8,128)(2,1)S(1)} %shard_map.123.refs_15_.refs_3_), channel_id=1, source_target_pairs={{0,8},{4,12},{8,0},{12,4},{1,9},{5,13},{9,1},{13,5},{2,10},{6,14},... | collective-permute-start | bytes 393224 | tf_op jit(solution)/shard_map/ppermute | solution.py:773
  21.9 18.6 %collective-permute-start.8 = (bf16[256,512]{1,0:T(8,128)(2,1)S(1)}, bf16[256,512]{1,0:T(8,128)(2,1)S(1)}, u32[]{:S(2)}, u32[]{:S(2)}) collective-permute-start(bf16[256,512]{1,0:T(8,128)(2,1)S(1)} %get-tuple-element.109.refs_0_.refs_3_), channel_id=1, source_target_pairs={{0,2},{2,0},{1,3},{3,1},{4,6},{6,4},{5,7},{7,5},{8,10},{10,8},{9,1... | collective-permute-start | bytes 786440 | tf_op jit(solution)/shard_map/ppermute | solution.py:773
  23.5 4.0 %collective-permute-start.3 = (bf16[2,2,128,256]{3,2,1,0:T(8,128)(2,1)S(1)}, bf16[2,2,128,256]{3,2,1,0:T(8,128)(2,1)S(1)}, u32[]{:S(2)}, u32[]{:S(2)}) collective-permute-start(bf16[2,2,128,256]{3,2,1,0:T(8,128)(2,1)S(1)} %shard_map.125.refs_13_.refs_1_), channel_id=1, source_target_pairs={{0,1},{1,0},{2,3},{3,2},{4,5},{5,4},{6,7},{7,6},{8,9},{9,8},{10,11... | collective-permute-start | bytes 786440 | tf_op jit(solution)/shard_map/ppermute | solution.py:773
  27.0 3.9 %collective-permute-start.4 = (bf16[8,128,256]{2,1,0:T(8,128)(2,1)S(1)}, bf16[8,128,256]{2,1,0:T(8,128)(2,1)S(1)}, u32[]{:S(2)}, u32[]{:S(2)}) collective-permute-start(bf16[8,128,256]{2,1,0:T(8,128)(2,1)S(1)} %get-tuple-element.99), channel_id=1, source_target_pairs={{0,1},{1,0},{2,3},{3,2},{4,5},{5,4},{6,7},{7,6},{8,9},{9,8},{10,11... | collective-permute-start | bytes 1572872 | tf_op jit(solution)/shard_map/ppermute | solution.py:773
  30.9 8.2 %collective-permute-start.6 = (bf16[2,128,256]{2,1,0:T(8,128)(2,1)S(1)}, bf16[2,128,256]{2,1,0:T(8,128)(2,1)S(1)}, u32[]{:S(2)}, u32[]{:S(2)}) collective-permute-start(bf16[2,128,256]{2,1,0:T(8,128)(2,1)S(1)} %get-tuple-element.105), channel_id=1, source_target_pairs={{0,4},{4,0},{8,12},{12,8},{1,5},{5,1},{9,13},{13,9},{2,6},{6,2},{1... | collective-permute-start | bytes 393224 | tf_op jit(solution)/shard_map/ppermute | solution.py:773
  31.4 8.9 %collective-permute-start.5 = (bf16[2,128,256]{2,1,0:T(8,128)(2,1)S(1)}, bf16[2,128,256]{2,1,0:T(8,128)(2,1)S(1)}, u32[]{:S(2)}, u32[]{:S(2)}) collective-permute-start(bf16[2,128,256]{2,1,0:T(8,128)(2,1)S(1)} %get-tuple-element.100.refs_12_), channel_id=1, source_target_pairs={{0,8},{4,12},{8,0},{12,4},{1,9},{5,13},{9,1},{13,5},{2,10},{6,14},... | collective-permute-start | bytes 393224 | tf_op jit(solution)/shard_map/ppermute | solution.py:773
  33.8 9.4 %collective-permute-start.9 = (bf16[128,512]{1,0:T(8,128)(2,1)S(1)}, bf16[128,512]{1,0:T(8,128)(2,1)S(1)}, u32[]{:S(2)}, u32[]{:S(2)}) collective-permute-start(bf16[128,512]{1,0:T(8,128)(2,1)S(1)} %shard_map.129.refs_13_), channel_id=1, source_target_pairs={{0,2},{2,0},{1,3},{3,1},{4,6},{6,4},{5,7},{7,5},{8,10},{10,8},{9,1... | collective-permute-start | bytes 393224 | tf_op jit(solution)/shard_map/ppermute | solution.py:773
  40.4 5.0 %collective-permute-start.7 = (bf16[2,128,256]{2,1,0:T(8,128)(2,1)S(1)}, bf16[2,128,256]{2,1,0:T(8,128)(2,1)S(1)}, u32[]{:S(2)}, u32[]{:S(2)}) collective-permute-start(bf16[2,128,256]{2,1,0:T(8,128)(2,1)S(1)} %get-tuple-element.108.refs_5_), channel_id=1, source_target_pairs={{0,4},{4,0},{8,12},{12,8},{1,5},{5,1},{9,13},{13,9},{2,6},{6,2},{1... | collective-permute-start | bytes 393224 | tf_op jit(solution)/shard_map/ppermute | solution.py:773
  45.4 2.2 %collective-permute-start.10 = (bf16[2,128,256]{2,1,0:T(8,128)(2,1)S(1)}, bf16[2,128,256]{2,1,0:T(8,128)(2,1)S(1)}, u32[]{:S(2)}, u32[]{:S(2)}) collective-permute-start(bf16[2,128,256]{2,1,0:T(8,128)(2,1)S(1)} %get-tuple-element.112.refs_2_), channel_id=1, source_target_pairs={{0,1},{1,0},{2,3},{3,2},{4,5},{5,4},{6,7},{7,6},{8,9},{9,8},{10,11... | collective-permute-start | bytes 393224 | tf_op jit(solution)/shard_map/ppermute | solution.py:773
  45.5 3.9 %collective-permute-start.12 = (bf16[128,256]{1,0:T(8,128)(2,1)S(1)}, bf16[128,256]{1,0:T(8,128)(2,1)S(1)}, u32[]{:S(2)}, u32[]{:S(2)}) collective-permute-start(bf16[128,256]{1,0:T(8,128)(2,1)S(1)} %get-tuple-element.114), channel_id=1, source_target_pairs={{0,3},{1,2},{2,1},{3,0},{4,7},{5,6},{6,5},{7,4},{8,11},{9,10},{10,... | collective-permute-start | bytes 196616 | tf_op jit(solution)/shard_map/ppermute | solution.py:861
  46.8 4.6 %collective-permute-start.11 = (bf16[128,256]{1,0:T(8,128)(2,1)S(1)}, bf16[128,256]{1,0:T(8,128)(2,1)S(1)}, u32[]{:S(2)}, u32[]{:S(2)}) collective-permute-start(bf16[128,256]{1,0:T(8,128)(2,1)S(1)} %get-tuple-element.114), channel_id=1, source_target_pairs={{0,2},{2,0},{1,3},{3,1},{4,6},{6,4},{5,7},{7,5},{8,10},{10,8},{9,1... | collective-permute-start | bytes 196616 | tf_op jit(solution)/shard_map/ppermute | solution.py:773

commit v18 on v16

--- a/solution.py
+++ b/solution.py
@@ -854,8 +854,9 @@
     return ref[4 + 2 * (theirs // order.half) + kind, :, at : at + HD]
 
 
-def begin_values(order, facts, own0, level2_far):
-    def body(facts, own_r, low_r, out):
+def begin_values(order, facts, own0, level2_far, handed):
+    def body(facts, own_r, low_r, handed_r, out, handed_out):
+        handed_out[...] = handed_r[...]
         ok = row_ok(facts[N0], PAGE, HD)
         for head in range(order.heads):
             c = slice(head * HD, (head + 1) * HD)
@@ -863,8 +864,8 @@
             value = own_r[1, :, c] + jnp.where(facts[OWNS2] == 1, low, 0.0)
             out[:, c] = jnp.where(ok, value, 0.0).astype(BF16)
 
-    outs = [((PAGE, own0.shape[-1]), BF16, True)]
-    return kernel_call(body, facts, [own0, level2_far], [], outs)[0]
+    outs = [((PAGE, own0.shape[-1]), BF16, True), (handed.shape, handed.dtype, True)]
+    return kernel_call(body, facts, [own0, level2_far, handed], [], outs)
 
 
 def finish_small_tree(order, facts, own0, mine, far, level2_far):
@@ -936,24 +937,24 @@
     kvs = tuple(range(kv))
     w = hbm(w_value)
     if fast:
-        level2, halves = [], []
+        level2, calls = [], []
 
         def beside_pair(from_core, chip):
             level2.extend((own, from_core))
-            halves.append(own_pages(kvs[:2], level2, after=(chip,)))
-            return (halves[0][3],)
+            calls.append(own_pages(kvs[:1], level2, after=(chip,)))
+            return (calls[0][3],)
 
         def beside_half(pair):
-            halves.append(own_pages(kvs[2:], level2, halves[0], (pair,)))
-            return (halves[1][3],)
+            calls.append(own_pages(kvs[1:], level2, calls[0], (pair,)))
+            return (calls[1][3],)
 
         mine, theirs = gather_small_tree(facts, own, beside_pair, beside_half)
-        dk12, dv12, own0, send2 = halves[1]
+        dk12, dv12, own0, send2 = calls[1]
         sent = flipped(shared_pages(kvs[:2], mine, send2), "sub", 1)
         kept = shared_pages(kvs[2:], theirs)
         total, root, root_far, next_far = over_cores(facts, kept, sent)
+        base, dv12 = begin_values(order, facts, own0, sent, dv12)
         far_v = spread(dv12)
-        base = begin_values(order, facts, own0, sent)
         made, w_near = finish_queries(
             kvs, group, order, facts, (mine, theirs), state, (root, base), w
         )

time: 52.8 us -> 51.6 us (0.977)
  starting transfers between devices: 15 us -> 13.1 us
  waiting for transfers between devices: 7.49 us -> 8.24 us
    ppermute x12, starting transfers between devices: 13.8 us -> 11.5 us  [flipped(): lax.ppermute(block, axis, [(i, i ^ bit) for i in range(count) if i ^ bit...]
    ppermute x12, waiting for transfers between devices: 6.7 us -> 7.32 us  [flipped(): lax.ppermute(block, axis, [(i, i ^ bit) for i in range(count) if i ^ bit...]
  transfers between devices with their start and end apart: 13 -> 13, of which waited for: 5 -> 6; matrix products, arithmetic and copies ran while one was open for 0% -> 0% of each run, Pallas kernels for 50% -> 51%
where the time goes in v18:
time: 51.6 us; the launch traced here: 51.4 us
  Pallas kernels  29.1 us (56%)
  starting transfers between devices  13.1 us (25%)
  waiting for transfers between devices  8.24 us (16%)
  between operations  0.98 us (2%)
    pallas_call x14, Pallas kernels, kernel_call(): pl.pallas_call(kernel, out_shape=tuple((pltpu.VMEM(s, d) if inside else j...  24.6 us
    ppermute x12, starting transfers between devices, flipped(): lax.ppermute(block, axis, [(i, i ^ bit) for i in range(count) if i ^ bit...  11.5 us
    ppermute x12, waiting for transfers between devices, flipped(): lax.ppermute(block, axis, [(i, i ^ bit) for i in range(count) if i ^ bit...  7.32 us
    pallas_call x1, Pallas kernels, input_grad(): pl.pallas_call(body, out_shape=(jax.ShapeDtypeStruct((ROWS, out_cols), BF...  2.63 us
    ppermute x1, starting transfers between devices, over_chips(): lax.ppermute(values, ('tensor', 'sub'), [(i, 3 - i) for i in range(4)])  1.61 us
  transfers between devices with their start and end apart: 13, of which 6 were waited for; matrix products, arithmetic and copies ran while one was open for 0% of the time, Pallas kernels for 51%

profile of v18, /device:TPU:0, one launch (start us, length us, event | category | flops | bytes accessed | tf_op | source)
XLA Modules:
  0.0 51.4 jit_solution(7047023879868403452)
XLA Ops:
  0.6 1.0 %shard_map.120 = (s32[16]{0:T(128)S(4)}, bf16[2,128,512]{2,1,0:T(8,128)(2,1)S(1)}) custom-call(s32[1]{0:T(128)} %bitcast.side_ref, s32[1,5]{1,0:T(1,128)} %ids_ref.1, s32[1,3]{1,0:T(1,128)} %counts_ref.1, bf16[384,512]{1,0:T(8,128)(2,1)} %refs_5_.1, bf16[384,512]{1,0:T(8,128)(2,1)} %refs_6_.1), custom_call_target="tpu_custom_call" | custom-call | tf_op jit(solution)/shard_map/pallas_call | solution.py:141
  1.7 0.5 %collective-permute-start = (bf16[2,128,512]{2,1,0:T(8,128)(2,1)S(1)}, bf16[2,128,512]{2,1,0:T(8,128)(2,1)S(1)}, u32[]{:S(2)}, u32[]{:S(2)}) collective-permute-start(bf16[2,128,512]{2,1,0:T(8,128)(2,1)S(1)} %get-tuple-element.66.refs_1_.refs_11_), channel_id=1, source_target_pairs={{0,1},{1,0},{2,3},{3,2},{4,5},{5,4},{6,7},{7,6},{8,9},{9,8},{10,11... | collective-permute-start | bytes 786440 | tf_op jit(solution)/shard_map/ppermute | solution.py:759
  2.2 1.2 %collective-permute-done.refs_2_.refs_12_ = bf16[2,128,512]{2,1,0:T(8,128)(2,1)S(1)} collective-permute-done((bf16[2,128,512]{2,1,0:T(8,128)(2,1)S(1)}, bf16[2,128,512]{2,1,0:T(8,128)(2,1)S(1)}, u32[]{:S(2)}, u32[]{:S(2)}) %collective-permute-start) | collective-permute-done | bytes 262176 | tf_op jit(solution)/shard_map/ppermute | solution.py:759
  3.4 3.0 %collective-permute-start.1 = (bf16[2,128,256]{2,1,0:T(8,128)(2,1)S(1)}, bf16[2,128,256]{2,1,0:T(8,128)(2,1)S(1)}, u32[]{:S(2)}, u32[]{:S(2)}) collective-permute-start(bf16[2,128,256]{2,1,0:T(8,128)(2,1)S(1)} %shard_map.121.refs_9_.refs_1_), channel_id=1, source_target_pairs={{0,4},{4,0},{8,12},{12,8},{1,5},{5,1},{9,13},{13,9},{2,6},{6,2},{1... | collective-permute-start | bytes 393224 | tf_op jit(solution)/shard_map/ppermute | solution.py:759
  6.4 4.5 %shard_map.122 = (f32[384,1024]{1,0:T(8,128)S(1)}, bf16[128,3072]{1,0:T(8,128)(2,1)S(1)}, bf16[128,3072]{1,0:T(8,128)(2,1)S(1)}, bf16[256,128]{1,0:T(8,128)(2,1)...) custom-call(s32[16]{0:T(128)S(4)} %get-tuple-element.65.refs_0_.fact, ...), custom_call_target="tpu_custom_call" | custom-call | flops 4026531840 | bytes 1000 | tf_op jit(solution)/shard_map/pallas_call | solution.py:100
  10.9 0.0 collective-permute-done.1.refs_2_
  11.0 2.7 %collective-permute-start.2 = (bf16[2,128,256]{2,1,0:T(8,128)(2,1)S(1)}, bf16[2,128,256]{2,1,0:T(8,128)(2,1)S(1)}, u32[]{:S(2)}, u32[]{:S(2)}) collective-permute-start(bf16[2,128,256]{2,1,0:T(8,128)(2,1)S(1)} %shard_map.123.refs_17_.refs_3_), channel_id=1, source_target_pairs={{0,8},{4,12},{8,0},{12,4},{1,9},{5,13},{9,1},{13,5},{2,10},{6,14},... | collective-permute-start | bytes 393224 | tf_op jit(solution)/shard_map/ppermute | solution.py:759
  13.6 7.5 %shard_map.124 = (f32[384,1024]{1,0:T(8,128)S(1)}, bf16[128,3072]{1,0:T(8,128)(2,1)S(1)}, bf16[128,3072]{1,0:T(8,128)(2,1)S(1)}, f32[384,1024]{1,0:T(8,128)S(1)}...) custom-call(s32[16]{0:T(128)S(4)} %get-tuple-element.65.refs_0_.fact, ...), custom_call_target="tpu_custom_call" | custom-call | flops 12079595520 | bytes 1000 | tf_op jit(solution)/shard_map/pallas_call | solution.py:100
  21.1 0.0 collective-permute-done.2.refs_4_
  21.1 0.1 collective-permute-start.3
  21.2 3.5 %shard_map.126 = (bf16[3072,256]{1,0:T(8,128)(2,1)S(1)}, bf16[3072,256]{1,0:T(8,128)(2,1)S(1)}, bf16[8,128,256]{2,1,0:T(8,128)(2,1)S(1)}) custom-call(s32[16]{0:T(128)S(4)} %get-tuple-element.65.refs_0_.facts, bf16[128,3072]{1,0:T(8,128)(2,1)S(1)} %get-tuple-element.82.refs_1_, bf16[128,3072]{1,0:T(8,128)(2,1)S(1)} %get-tuple-element.83.refs_2_, ...), custom_call_target="tpu_custom_call" | custom-call | flops 8053063680 | bytes 1000 | tf_op jit(solution)/shard_map/pallas_call | solution.py:100
  24.7 0.5 %collective-permute-start.4 = (bf16[8,128,256]{2,1,0:T(8,128)(2,1)S(1)}, bf16[8,128,256]{2,1,0:T(8,128)(2,1)S(1)}, u32[]{:S(2)}, u32[]{:S(2)}) collective-permute-start(bf16[8,128,256]{2,1,0:T(8,128)(2,1)S(1)} %get-tuple-element.101), channel_id=1, source_target_pairs={{0,1},{1,0},{2,3},{3,2},{4,5},{5,4},{6,7},{7,6},{8,9},{9,8},{10,11... | collective-permute-start | bytes 1572872 | tf_op jit(solution)/shard_map/ppermute | solution.py:759
  25.3 0.0 collective-permute-done.3.refs_13_.refs_2_
  25.3 3.2 %shard_map.127 = (bf16[3072,256]{1,0:T(8,128)(2,1)S(1)}, bf16[3072,256]{1,0:T(8,128)(2,1)S(1)}, f32[4,128,256]{2,1,0:T(8,128)S(1)}) custom-call(s32[16]{0:T(128)S(4)} %get-tuple-element.65.refs_0_.facts, bf16[128,3072]{1,0:T(8,128)(2,1)S(1)} %get-tuple-element.92.refs_1_, bf16[128,3072]{1,0:T(8,128)(2,1)S(1)} %get-tuple-element.93.refs_2_, ...), custom_call_target="tpu_custom_call" | custom-call | flops 8053063680 | bytes 1000 | tf_op jit(solution)/shard_map/pallas_call | solution.py:100
  28.5 0.0 collective-permute-done.4.refs_2_.refs_4_
  28.5 0.1 shard_map.128
  28.6 1.0 %collective-permute-start.6 = (bf16[2,128,256]{2,1,0:T(8,128)(2,1)S(1)}, bf16[2,128,256]{2,1,0:T(8,128)(2,1)S(1)}, u32[]{:S(2)}, u32[]{:S(2)}) collective-permute-start(bf16[2,128,256]{2,1,0:T(8,128)(2,1)S(1)} %get-tuple-element.109), channel_id=1, source_target_pairs={{0,4},{4,0},{8,12},{12,8},{1,5},{5,1},{9,13},{13,9},{2,6},{6,2},{1... | collective-permute-start | bytes 393224 | tf_op jit(solution)/shard_map/ppermute | solution.py:759
  29.6 1.0 %collective-permute-start.5 = (bf16[2,128,256]{2,1,0:T(8,128)(2,1)S(1)}, bf16[2,128,256]{2,1,0:T(8,128)(2,1)S(1)}, u32[]{:S(2)}, u32[]{:S(2)}) collective-permute-start(bf16[2,128,256]{2,1,0:T(8,128)(2,1)S(1)} %get-tuple-element.102.refs_12_), channel_id=1, source_target_pairs={{0,8},{4,12},{8,0},{12,4},{1,9},{5,13},{9,1},{13,5},{2,10},{6,14},... | collective-permute-start | bytes 393224 | tf_op jit(solution)/shard_map/ppermute | solution.py:759
  30.5 0.1 shard_map.129
  30.6 1.6 %collective-permute-start.8 = (bf16[256,512]{1,0:T(8,128)(2,1)S(1)}, bf16[256,512]{1,0:T(8,128)(2,1)S(1)}, u32[]{:S(2)}, u32[]{:S(2)}) collective-permute-start(bf16[256,512]{1,0:T(8,128)(2,1)S(1)} %get-tuple-element.113.refs_0_.refs_3_), channel_id=1, source_target_pairs={{0,2},{2,0},{1,3},{3,1},{4,6},{6,4},{5,7},{7,5},{8,10},{10,8},{9,1... | collective-permute-start | bytes 786440 | tf_op jit(solution)/shard_map/ppermute | solution.py:759
  32.2 0.5 %collective-permute-start.9 = (bf16[128,512]{1,0:T(8,128)(2,1)S(1)}, bf16[128,512]{1,0:T(8,128)(2,1)S(1)}, u32[]{:S(2)}, u32[]{:S(2)}) collective-permute-start(bf16[128,512]{1,0:T(8,128)(2,1)S(1)} %get-tuple-element.105.refs_13_), channel_id=1, source_target_pairs={{0,2},{2,0},{1,3},{3,1},{4,6},{6,4},{5,7},{7,5},{8,10},{10,8},{9,1... | collective-permute-start | bytes 393224 | tf_op jit(solution)/shard_map/ppermute | solution.py:759
  32.7 3.7 %shard_map.130 = (bf16[384,4096]{1,0:T(8,128)(2,1)}, f32[8,128]{1,0:T(8,128)S(1)}, bf16[2560,1024]{1,0:T(8,128)(2,1)S(1)}) custom-call(s32[16]{0:T(128)S(4)} %get-tuple-element.65.refs_0_.facts, bf16[2,2,128,256]{3,2,1,0:T(8,128)(2,1)S(1)} %shard_map.125.refs_13_.refs_1_, bf16[2,2,128,256]{3,2,1,0:T(8,128)(2,1)S(1)} %collective-permute-done.3.refs_13_.refs_2_, ...), custom_call_target="tpu_custom_call" | custom-call | flops 1000 | bytes 1000 | tf_op jit(solution)/shard_map/pallas_call | solution.py:100
  36.4 0.0 collective-permute-done.6.refs_3_
  36.4 2.0 %collective-permute-done.5.refs_2_ = bf16[2,128,256]{2,1,0:T(8,128)(2,1)S(1)} collective-permute-done((bf16[2,128,256]{2,1,0:T(8,128)(2,1)S(1)}, bf16[2,128,256]{2,1,0:T(8,128)(2,1)S(1)}, u32[]{:S(2)}, u32[]{:S(2)}) %collective-permute-start.5) | collective-permute-done | bytes 131104 | tf_op jit(solution)/shard_map/ppermute | solution.py:759
  38.4 0.1 shard_map.131
  38.5 0.1 collective-permute-start.7
  38.6 1.2 %collective-permute-done.8.refs_1_ = bf16[256,512]{1,0:T(8,128)(2,1)S(1)} collective-permute-done((bf16[256,512]{1,0:T(8,128)(2,1)S(1)}, bf16[256,512]{1,0:T(8,128)(2,1)S(1)}, u32[]{:S(2)}, u32[]{:S(2)}) %collective-permute-start.8) | collective-permute-done | bytes 262176 | tf_op jit(solution)/shard_map/ppermute | solution.py:759
  39.8 2.6 %shard_map.132 = (bf16[384,2560]{1,0:T(8,128)(2,1)}, bf16[384,512]{1,0:T(8,128)(2,1)}, bf16[384,512]{1,0:T(8,128)(2,1)}, f32[8,128]{1,0:T(8,128)S(1)}) custom-call(s32[16]{0:T(128)S(4)} %get-tuple-element.65.refs_0_.facts, bf16[256,512]{1,0:T(8,128)(2,1)S(1)} %get-tuple-element.113.refs_0_.refs_3_, bf16[256,512]{1,0:T(8,128)(2,1)S(1)} %collective-permute-done.8.refs_1_, ...), custom_call_target="tpu_custom_call" | custom-call | flops 1000 | bytes 1000 | tf_op jit(solution)/shard_map/pallas_call | solution.py:653
  42.4 0.0 collective-permute-done.9.refs_4_.refs_3_
  42.4 1.1 %collective-permute-done.7.refs_2_ = bf16[2,128,256]{2,1,0:T(8,128)(2,1)S(1)} collective-permute-done((bf16[2,128,256]{2,1,0:T(8,128)(2,1)S(1)}, bf16[2,128,256]{2,1,0:T(8,128)(2,1)S(1)}, u32[]{:S(2)}, u32[]{:S(2)}) %collective-permute-start.7) | collective-permute-done | bytes 131104 | tf_op jit(solution)/shard_map/ppermute | solution.py:759
  43.6 0.1 collective-permute-start.10
  43.6 1.6 %collective-permute-start.12 = (bf16[128,256]{1,0:T(8,128)(2,1)S(1)}, bf16[128,256]{1,0:T(8,128)(2,1)S(1)}, u32[]{:S(2)}, u32[]{:S(2)}) collective-permute-start(bf16[128,256]{1,0:T(8,128)(2,1)S(1)} %get-tuple-element.118), channel_id=1, source_target_pairs={{0,3},{1,2},{2,1},{3,0},{4,7},{5,6},{6,5},{7,4},{8,11},{9,10},{10,... | collective-permute-start | bytes 196616 | tf_op jit(solution)/shard_map/ppermute | solution.py:847
  45.3 0.5 %collective-permute-start.11 = (bf16[128,256]{1,0:T(8,128)(2,1)S(1)}, bf16[128,256]{1,0:T(8,128)(2,1)S(1)}, u32[]{:S(2)}, u32[]{:S(2)}) collective-permute-start(bf16[128,256]{1,0:T(8,128)(2,1)S(1)} %get-tuple-element.118), channel_id=1, source_target_pairs={{0,2},{2,0},{1,3},{3,1},{4,6},{6,4},{5,7},{7,5},{8,10},{10,8},{9,1... | collective-permute-start | bytes 196616 | tf_op jit(solution)/shard_map/ppermute | solution.py:759
  45.8 0.0 collective-permute-done.10.refs_3_
  45.8 0.1 shard_map.134
  45.9 0.8 %shard_map.135.refs_2_ = f32[2560,128]{1,0:T(8,128)S(1)} custom-call(s32[16]{0:T(128)S(4)} %get-tuple-element.65.refs_0_.facts, bf16[2560,1024]{1,0:T(8,128)(2,1)S(1)} %get-tuple-element.107.refs_4_.refs_1_, bf16[128,512]{1,0:T(8,128)(2,1)S(1)} %get-tuple-element.117.refs_2_.refs_7_), custom_call_target="tpu_custom_call" | custom-call | flops 1000 | bytes 1000 | tf_op jit(solution)/shard_map/pallas_call | solution.py:714
  46.8 0.9 %collective-permute-done.12.refs_5_ = bf16[128,256]{1,0:T(8,128)(2,1)S(1)} collective-permute-done((bf16[128,256]{1,0:T(8,128)(2,1)S(1)}, bf16[128,256]{1,0:T(8,128)(2,1)S(1)}, u32[]{:S(2)}, u32[]{:S(2)}) %collective-permute-start.12) | collective-permute-done | bytes 65568 | tf_op jit(solution)/shard_map/ppermute | solution.py:847
  47.7 1.8 %collective-permute-done.11.refs_4_ = bf16[128,256]{1,0:T(8,128)(2,1)S(1)} collective-permute-done((bf16[128,256]{1,0:T(8,128)(2,1)S(1)}, bf16[128,256]{1,0:T(8,128)(2,1)S(1)}, u32[]{:S(2)}, u32[]{:S(2)}) %collective-permute-start.11) | collective-permute-done | bytes 65568 | tf_op jit(solution)/shard_map/ppermute | solution.py:759
  49.5 1.7 %shard_map.136 = (bf16[384,2560]{1,0:T(8,128)(2,1)}, bf16[384,512]{1,0:T(8,128)(2,1)}, bf16[384,512]{1,0:T(8,128)(2,1)}) custom-call(s32[16]{0:T(128)S(4)} %get-tuple-element.65.refs_0_.facts, bf16[2560,1024]{1,0:T(8,128)(2,1)S(1)} %get-tuple-element.107.refs_4_.refs_1_, ...), custom_call_target="tpu_custom_call", output_to_operand_aliasing={{0}: (8, {}), {1}: (9, {}), {2}: (10, {})} | custom-call | flops 1000 | bytes 1000 | tf_op jit(solution)/shard_map/pallas_call | solution.py:100
  (4 shorter events, 0.1 us)
Async XLA Ops:
  1.7 1.7 %collective-permute-start = (bf16[2,128,512]{2,1,0:T(8,128)(2,1)S(1)}, bf16[2,128,512]{2,1,0:T(8,128)(2,1)S(1)}, u32[]{:S(2)}, u32[]{:S(2)}) collective-permute-start(bf16[2,128,512]{2,1,0:T(8,128)(2,1)S(1)} %get-tuple-element.66.refs_1_.refs_11_), channel_id=1, source_target_pairs={{0,1},{1,0},{2,3},{3,2},{4,5},{5,4},{6,7},{7,6},{8,9},{9,8},{10,11... | collective-permute-start | bytes 786440 | tf_op jit(solution)/shard_map/ppermute | solution.py:759
  3.4 7.6 %collective-permute-start.1 = (bf16[2,128,256]{2,1,0:T(8,128)(2,1)S(1)}, bf16[2,128,256]{2,1,0:T(8,128)(2,1)S(1)}, u32[]{:S(2)}, u32[]{:S(2)}) collective-permute-start(bf16[2,128,256]{2,1,0:T(8,128)(2,1)S(1)} %shard_map.121.refs_9_.refs_1_), channel_id=1, source_target_pairs={{0,4},{4,0},{8,12},{12,8},{1,5},{5,1},{9,13},{13,9},{2,6},{6,2},{1... | collective-permute-start | bytes 393224 | tf_op jit(solution)/shard_map/ppermute | solution.py:759
  11.0 10.1 %collective-permute-start.2 = (bf16[2,128,256]{2,1,0:T(8,128)(2,1)S(1)}, bf16[2,128,256]{2,1,0:T(8,128)(2,1)S(1)}, u32[]{:S(2)}, u32[]{:S(2)}) collective-permute-start(bf16[2,128,256]{2,1,0:T(8,128)(2,1)S(1)} %shard_map.123.refs_17_.refs_3_), channel_id=1, source_target_pairs={{0,8},{4,12},{8,0},{12,4},{1,9},{5,13},{9,1},{13,5},{2,10},{6,14},... | collective-permute-start | bytes 393224 | tf_op jit(solution)/shard_map/ppermute | solution.py:759
  21.1 4.1 %collective-permute-start.3 = (bf16[2,2,128,256]{3,2,1,0:T(8,128)(2,1)S(1)}, bf16[2,2,128,256]{3,2,1,0:T(8,128)(2,1)S(1)}, u32[]{:S(2)}, u32[]{:S(2)}) collective-permute-start(bf16[2,2,128,256]{3,2,1,0:T(8,128)(2,1)S(1)} %shard_map.125.refs_13_.refs_1_), channel_id=1, source_target_pairs={{0,1},{1,0},{2,3},{3,2},{4,5},{5,4},{6,7},{7,6},{8,9},{9,8},{10,11... | collective-permute-start | bytes 786440 | tf_op jit(solution)/shard_map/ppermute | solution.py:759
  24.7 3.8 %collective-permute-start.4 = (bf16[8,128,256]{2,1,0:T(8,128)(2,1)S(1)}, bf16[8,128,256]{2,1,0:T(8,128)(2,1)S(1)}, u32[]{:S(2)}, u32[]{:S(2)}) collective-permute-start(bf16[8,128,256]{2,1,0:T(8,128)(2,1)S(1)} %get-tuple-element.101), channel_id=1, source_target_pairs={{0,1},{1,0},{2,3},{3,2},{4,5},{5,4},{6,7},{7,6},{8,9},{9,8},{10,11... | collective-permute-start | bytes 1572872 | tf_op jit(solution)/shard_map/ppermute | solution.py:759
  28.6 7.9 %collective-permute-start.6 = (bf16[2,128,256]{2,1,0:T(8,128)(2,1)S(1)}, bf16[2,128,256]{2,1,0:T(8,128)(2,1)S(1)}, u32[]{:S(2)}, u32[]{:S(2)}) collective-permute-start(bf16[2,128,256]{2,1,0:T(8,128)(2,1)S(1)} %get-tuple-element.109), channel_id=1, source_target_pairs={{0,4},{4,0},{8,12},{12,8},{1,5},{5,1},{9,13},{13,9},{2,6},{6,2},{1... | collective-permute-start | bytes 393224 | tf_op jit(solution)/shard_map/ppermute | solution.py:759
  29.6 8.8 %collective-permute-start.5 = (bf16[2,128,256]{2,1,0:T(8,128)(2,1)S(1)}, bf16[2,128,256]{2,1,0:T(8,128)(2,1)S(1)}, u32[]{:S(2)}, u32[]{:S(2)}) collective-permute-start(bf16[2,128,256]{2,1,0:T(8,128)(2,1)S(1)} %get-tuple-element.102.refs_12_), channel_id=1, source_target_pairs={{0,8},{4,12},{8,0},{12,4},{1,9},{5,13},{9,1},{13,5},{2,10},{6,14},... | collective-permute-start | bytes 393224 | tf_op jit(solution)/shard_map/ppermute | solution.py:759
  30.6 9.2 %collective-permute-start.8 = (bf16[256,512]{1,0:T(8,128)(2,1)S(1)}, bf16[256,512]{1,0:T(8,128)(2,1)S(1)}, u32[]{:S(2)}, u32[]{:S(2)}) collective-permute-start(bf16[256,512]{1,0:T(8,128)(2,1)S(1)} %get-tuple-element.113.refs_0_.refs_3_), channel_id=1, source_target_pairs={{0,2},{2,0},{1,3},{3,1},{4,6},{6,4},{5,7},{7,5},{8,10},{10,8},{9,1... | collective-permute-start | bytes 786440 | tf_op jit(solution)/shard_map/ppermute | solution.py:759
  32.2 10.2 %collective-permute-start.9 = (bf16[128,512]{1,0:T(8,128)(2,1)S(1)}, bf16[128,512]{1,0:T(8,128)(2,1)S(1)}, u32[]{:S(2)}, u32[]{:S(2)}) collective-permute-start(bf16[128,512]{1,0:T(8,128)(2,1)S(1)} %get-tuple-element.105.refs_13_), channel_id=1, source_target_pairs={{0,2},{2,0},{1,3},{3,1},{4,6},{6,4},{5,7},{7,5},{8,10},{10,8},{9,1... | collective-permute-start | bytes 393224 | tf_op jit(solution)/shard_map/ppermute | solution.py:759
  38.5 5.0 %collective-permute-start.7 = (bf16[2,128,256]{2,1,0:T(8,128)(2,1)S(1)}, bf16[2,128,256]{2,1,0:T(8,128)(2,1)S(1)}, u32[]{:S(2)}, u32[]{:S(2)}) collective-permute-start(bf16[2,128,256]{2,1,0:T(8,128)(2,1)S(1)} %get-tuple-element.112.refs_5_), channel_id=1, source_target_pairs={{0,4},{4,0},{8,12},{12,8},{1,5},{5,1},{9,13},{13,9},{2,6},{6,2},{1... | collective-permute-start | bytes 393224 | tf_op jit(solution)/shard_map/ppermute | solution.py:759
  43.6 2.2 %collective-permute-start.10 = (bf16[2,128,256]{2,1,0:T(8,128)(2,1)S(1)}, bf16[2,128,256]{2,1,0:T(8,128)(2,1)S(1)}, u32[]{:S(2)}, u32[]{:S(2)}) collective-permute-start(bf16[2,128,256]{2,1,0:T(8,128)(2,1)S(1)} %get-tuple-element.116.refs_2_), channel_id=1, source_target_pairs={{0,1},{1,0},{2,3},{3,2},{4,5},{5,4},{6,7},{7,6},{8,9},{9,8},{10,11... | collective-permute-start | bytes 393224 | tf_op jit(solution)/shard_map/ppermute | solution.py:759
  43.6 4.0 %collective-permute-start.12 = (bf16[128,256]{1,0:T(8,128)(2,1)S(1)}, bf16[128,256]{1,0:T(8,128)(2,1)S(1)}, u32[]{:S(2)}, u32[]{:S(2)}) collective-permute-start(bf16[128,256]{1,0:T(8,128)(2,1)S(1)} %get-tuple-element.118), channel_id=1, source_target_pairs={{0,3},{1,2},{2,1},{3,0},{4,7},{5,6},{6,5},{7,4},{8,11},{9,10},{10,... | collective-permute-start | bytes 196616 | tf_op jit(solution)/shard_map/ppermute | solution.py:847
  45.3 4.3 %collective-permute-start.11 = (bf16[128,256]{1,0:T(8,128)(2,1)S(1)}, bf16[128,256]{1,0:T(8,128)(2,1)S(1)}, u32[]{:S(2)}, u32[]{:S(2)}) collective-permute-start(bf16[128,256]{1,0:T(8,128)(2,1)S(1)} %get-tuple-element.118), channel_id=1, source_target_pairs={{0,2},{2,0},{1,3},{3,1},{4,6},{6,4},{5,7},{7,5},{8,10},{10,8},{9,1... | collective-permute-start | bytes 196616 | tf_op jit(solution)/shard_map/ppermute | solution.py:759

commit v19 on v18

--- a/solution.py
+++ b/solution.py
@@ -202,17 +202,6 @@
         at = (part * SLOTS + slot) * self.tall
         return slice(at, at + self.tall * count)
 
-    def put_queries(self, part, slot, rows_by_head, dq, add, stage):
-        rows = slice(slot * PAGE, (slot + 1) * PAGE)
-        for j in range(self.heads):
-            value = rows_by_head[j * PAGE : (j + 1) * PAGE]
-            if stage is None:
-                dq[rows, self.lanes(part, j)] = value
-            else:
-                if add:
-                    value = value + dq[rows, self.lanes(part, j)]
-                stage[rows, j * HD : (j + 1) * HD] = (value * SCALE).astype(BF16)
-
 
 def set_keys(deep, upright, at, page):
     where = slice(at * PAGE, (at + 1) * PAGE)
@@ -233,14 +222,20 @@
     count = len(kvs)
     parts = group // min(4, group)
     tall = min(4, group) * PAGE
-    wide = min(4, group) * HD
     width = count * HD
     base = prior[0].shape[1] if prior else 0
     kv_total = k_all.shape[1] // HD
-    fresh = [("dq", kv) not in state for kv in kvs]
+    fresh = [("qt", kv) not in state for kv in kvs]
     one_head = (ROWS, group * HD)
     turned = ((HD, group * ROWS), BF16, True)
-    shapes = {"dq": (one_head, F32, True), "qt": turned, "gt": turned}
+    low = lambda rows, columns: ((rows, columns), BF16, True)
+    shapes = {
+        "da": low(2 * group * PAGE, 2 * PAGE),
+        "db": low(2 * group * PAGE, PAGE),
+        "ku": low(4 * PAGE, HD),
+        "qt": turned,
+        "gt": turned,
+    }
 
     near, far, aliases, outs = [], [], {}, []
     at_near, at_far, at_out = {}, {}, {}
@@ -261,15 +256,10 @@
         for name, shape in shapes.items():
             if is_fresh:
                 add_out((name, kv), shape)
-            elif own or name != "dq":
+            elif name in ("qt", "gt"):
                 add_near((name, kv), state[name, kv])
         if not own and not is_fresh:
             add_out(("ds", kv), ((group * ROWS, 2 * PAGE), BF16, True))
-    if own and not all(fresh):
-        add_out("gq", (q_all.shape, BF16, False))
-        if "gq" in state:
-            add_far("gq", state["gq"])
-            aliases["far", at_far["gq"]] = at_out["gq"]
     at_results = len(outs)
     if own:
         outs += [
@@ -311,15 +301,13 @@
         pltpu.VMEM((2, HD, key_pages * PAGE), F32),
         pltpu.VMEM((ROWS, HD), BF16),
         pltpu.VMEM((ROWS, HD), BF16),
-        pltpu.VMEM((count * parts, ROWS, wide), BF16),
-        pltpu.SemaphoreType.DMA((count * parts,)),
         pltpu.SemaphoreType.DMA((2 * kv_total + 8,)),
     ]
     cols = lambda a, b: slice(a * PAGE, b * PAGE)
 
     def body(facts, *refs):
         ins, out_refs = refs[: len(near) + len(far)], refs[len(near) + len(far) : -len(scratch)]
-        k_deep, v_deep, k_up, acc, en, ed, stage, sem, load_sem = refs[-len(scratch) :]
+        k_deep, v_deep, k_up, acc, en, ed, load_sem = refs[-len(scratch) :]
         near_ref = lambda name: ins[at_near[name]]
         far_ref = lambda name: ins[len(near) + at_far[name]]
         held = lambda name: out_refs[at_out[name]] if name in at_out else near_ref(name)
@@ -411,7 +399,7 @@
                 :, head.turned_at(part, slot, slots)
             ]
 
-        def own_part(head, kv, part, n, stage_ref):
+        def own_part(head, kv, part, n):
             order = (1, 2, 0)
             qs = head.stacked(held(("q", kv)), part, order)
             gs = head.stacked(held(("g", kv)), part, order)
@@ -441,15 +429,11 @@
                 acc[i, :, : 2 * PAGE] += dot_n(turn(name, 1, 2), a)
                 acc[i, :, cols(2, 3)] += dot_n(turn(name, 2, 1), b[:tall])
                 acc[i, :, cols(3, 4)] += dot_n(turn(name, 0, 1), b[tall:])
-            first = dot_n(da, k_up[: 2 * PAGE])
-            put = lambda slot, rows: head.put_queries(
-                part, slot, rows, held(("dq", kv)), not fresh[n], stage_ref
-            )
-            put(1, first[:tall])
-            put(2, first[tall:] + dot_n(db[:tall], k_up[cols(2, 3)]))
-            put(0, dot_n(db[tall:], k_up[cols(3, 4)]))
-
-        def shared_part(head, kv, part, n, stage_ref):
+            here = slice(part * 2 * tall, (part + 1) * 2 * tall)
+            held(("da", kv))[here] = da
+            held(("db", kv))[here] = db
+
+        def shared_part(head, kv, part, n):
             order = (0, 1, 2)
             qs = head.stacked(held(("q", kv)), part, order)
             gs = head.stacked(held(("g", kv)), part, order)
@@ -464,15 +448,7 @@
             p, ds = weigh(dot_n(qd, k_deep[...]), dot_n(gd, v_deep[...]), keep)
             acc[0] += dot_n(turn("qt", 0, SLOTS), ds)
             acc[1] += dot_n(turn("gt", 0, SLOTS), p)
-            if not fresh[n]:
-                held(("ds", kv))[part * SLOTS * tall : (part + 1) * SLOTS * tall] = ds
-                return
-            dq = dot_n(ds, k_up[...])
-            for slot in range(SLOTS):
-                head.put_queries(
-                    part, slot, dq[slot * tall : (slot + 1) * tall], held(("dq", kv)), not fresh[n],
-                    stage_ref,
-                )
+            held(("ds", kv))[part * SLOTS * tall : (part + 1) * SLOTS * tall] = ds
 
         def put_own(n):
             dk12, dv12, own0, send2 = results
@@ -497,31 +473,16 @@
                 for kind in range(2):
                     out[2 * j + kind, :, here] = grads[kind][cols(j, j + 1)].astype(out.dtype)
 
-        sends = []
         for n, kv in enumerate(kvs):
             arrived(("q", kv), ("g", kv))
             head = Head(kv, group, norms, deltas, en, ed)
             set_pages(n, kv)
 
             for part in range(parts):
-                slot = n * parts + part
-                (own_part if own else shared_part)(
-                    head, kv, part, n, stage.at[slot] if own and not fresh[n] else None
-                )
-                if own and not fresh[n]:
-                    at = order.at(facts, kv, group * HD) + part * wide
-                    sends.append(
-                        pltpu.make_async_copy(
-                            stage.at[slot],
-                            held("gq").at[:, pl.ds(pl.multiple_of(at, wide), wide)],
-                            sem.at[slot],
-                        )
-                    )
-                    sends[-1].start()
-
+                (own_part if own else shared_part)(head, kv, part, n)
+            if own:
+                held(("ku", kv))[...] = k_up[...]
             (put_own if own else put_shared)(n)
-        for c in sends:
-            c.wait()
         arrived(*list(copies))
 
     made = kernel_call(
@@ -547,8 +508,9 @@
     tall = heads * PAGE
     wide = heads * HD
     near = list(pages)
+    names = ("ds", "da", "db", "ku")
     for kv in kvs:
-        near += [state["ds", kv], state["dq", kv]]
+        near += [state[name, kv] for name in names]
 
     def body(facts, *refs):
         stage, sem = refs[-2:]
@@ -561,18 +523,26 @@
         made[...] = jnp.zeros_like(made)
         sends = []
         for n, kv in enumerate(kvs):
-            ds, dq = refs[len(pages) + 2 * n : len(pages) + 2 * n + 2]
+            first = len(pages) + len(names) * n
+            ds, da, db, ku = refs[first : first + len(names)]
             page, at = refs[kv // order.half], kv % order.half * HD
             keys = jnp.concatenate([page[j, 0, :, at : at + HD] for j in range(2)], axis=0)
             for part in range(parts):
                 at = n * parts + part
                 gained = dot_n(ds[part * SLOTS * tall : (part + 1) * SLOTS * tall], keys)
+                here = part * 2 * tall
+                wide_part = dot_n(da[here : here + 2 * tall], ku[: 2 * PAGE])
+                own2 = dot_n(db[here : here + tall], ku[2 * PAGE : 3 * PAGE])
+                own0 = dot_n(db[here + tall : here + 2 * tall], ku[3 * PAGE :])
+                by_slot = (
+                    gained[:tall] + own0,
+                    gained[tall : 2 * tall] + wide_part[:tall],
+                    gained[2 * tall :] + (wide_part[tall:] + own2),
+                )
                 for i in range(SLOTS * heads):
                     slot, j = divmod(i, heads)
                     rows = slice(slot * PAGE, (slot + 1) * PAGE)
-                    value = gained[i * PAGE : (i + 1) * PAGE] + dq[
-                        rows, part * wide + j * HD : part * wide + (j + 1) * HD
-                    ]
+                    value = by_slot[slot][j * PAGE : (j + 1) * PAGE]
                     stage[at, rows, j * HD : (j + 1) * HD] = (value * SCALE).astype(BF16)
                 to = pl.multiple_of(order.at(facts, kv, group * HD) + part * wide, wide)
                 sends.append(

time: 51.6 us -> 50.3 us (0.975)
  starting transfers between devices: 13.1 us -> 14.7 us
  waiting for transfers between devices: 8.24 us -> 6.68 us
  Pallas kernels: 29.1 us -> 27.8 us
    ppermute x12, waiting for transfers between devices: 7.32 us -> 5.75 us  [flipped(): lax.ppermute(block, axis, [(i, i ^ bit) for i in range(count) if i ^ bit...]
    ppermute x12, starting transfers between devices: 11.5 us -> 13.1 us  [flipped(): lax.ppermute(block, axis, [(i, i ^ bit) for i in range(count) if i ^ bit...]
    pallas_call x14, Pallas kernels: 24.6 us -> 23.4 us  [kernel_call(): pl.pallas_call(kernel, out_shape=tuple((pltpu.VMEM(s, d) if inside else j...]
  transfers between devices with their start and end apart: 13 -> 13, of which waited for: 6 -> 6; matrix products, arithmetic and copies ran while one was open for 0% -> 0% of each run, Pallas kernels for 51% -> 50%
where the time goes in v19:
time: 50.3 us; the launch traced here: 50.2 us
  Pallas kernels  27.8 us (55%)
  starting transfers between devices  14.7 us (29%)
  waiting for transfers between devices  6.68 us (13%)
  between operations  0.97 us (2%)
    pallas_call x14, Pallas kernels, kernel_call(): pl.pallas_call(kernel, out_shape=tuple((pltpu.VMEM(s, d) if inside else j...  23.4 us
    ppermute x12, starting transfers between devices, flipped(): lax.ppermute(block, axis, [(i, i ^ bit) for i in range(count) if i ^ bit...  13.1 us
    ppermute x12, waiting for transfers between devices, flipped(): lax.ppermute(block, axis, [(i, i ^ bit) for i in range(count) if i ^ bit...  5.75 us
    pallas_call x1, Pallas kernels, input_grad(): pl.pallas_call(body, out_shape=(jax.ShapeDtypeStruct((ROWS, out_cols), BF...  2.64 us
    ppermute x1, starting transfers between devices, over_chips(): lax.ppermute(values, ('tensor', 'sub'), [(i, 3 - i) for i in range(4)])  1.6 us
    pallas_call x1, Pallas kernels, start(): pl.pallas_call(body, out_shape=(pltpu.SMEM((FACTS,), I32), pltpu.VMEM((2,...  1.02 us
  transfers between devices with their start and end apart: 13, of which 6 were waited for; matrix products, arithmetic and copies ran while one was open for 0% of the time, Pallas kernels for 50%

profile of v19, /device:TPU:0, one launch (start us, length us, event | category | flops | bytes accessed | tf_op | source)
XLA Modules:
  0.0 50.2 jit_solution(10532517227287619016)
XLA Ops:
  0.6 1.0 %shard_map.120 = (s32[16]{0:T(128)S(4)}, bf16[2,128,512]{2,1,0:T(8,128)(2,1)S(1)}) custom-call(s32[1]{0:T(128)} %bitcast.side_ref, s32[1,5]{1,0:T(1,128)} %ids_ref.1, s32[1,3]{1,0:T(1,128)} %counts_ref.1, bf16[384,512]{1,0:T(8,128)(2,1)} %refs_5_.1, bf16[384,512]{1,0:T(8,128)(2,1)} %refs_6_.1), custom_call_target="tpu_custom_call" | custom-call | tf_op jit(solution)/shard_map/pallas_call | solution.py:141
  1.7 0.5 %collective-permute-start = (bf16[2,128,512]{2,1,0:T(8,128)(2,1)S(1)}, bf16[2,128,512]{2,1,0:T(8,128)(2,1)S(1)}, u32[]{:S(2)}, u32[]{:S(2)}) collective-permute-start(bf16[2,128,512]{2,1,0:T(8,128)(2,1)S(1)} %get-tuple-element.74.refs_1_.refs_11_), channel_id=1, source_target_pairs={{0,1},{1,0},{2,3},{3,2},{4,5},{5,4},{6,7},{7,6},{8,9},{9,8},{10,11... | collective-permute-start | bytes 786440 | tf_op jit(solution)/shard_map/ppermute | solution.py:729
  2.2 1.2 %collective-permute-done.refs_2_.refs_12_ = bf16[2,128,512]{2,1,0:T(8,128)(2,1)S(1)} collective-permute-done((bf16[2,128,512]{2,1,0:T(8,128)(2,1)S(1)}, bf16[2,128,512]{2,1,0:T(8,128)(2,1)S(1)}, u32[]{:S(2)}, u32[]{:S(2)}) %collective-permute-start) | collective-permute-done | bytes 262176 | tf_op jit(solution)/shard_map/ppermute | solution.py:729
  3.4 3.0 %collective-permute-start.1 = (bf16[2,128,256]{2,1,0:T(8,128)(2,1)S(1)}, bf16[2,128,256]{2,1,0:T(8,128)(2,1)S(1)}, u32[]{:S(2)}, u32[]{:S(2)}) collective-permute-start(bf16[2,128,256]{2,1,0:T(8,128)(2,1)S(1)} %shard_map.121.refs_9_.refs_1_), channel_id=1, source_target_pairs={{0,4},{4,0},{8,12},{12,8},{1,5},{5,1},{9,13},{13,9},{2,6},{6,2},{1... | collective-permute-start | bytes 393224 | tf_op jit(solution)/shard_map/ppermute | solution.py:729
  6.4 4.1 %shard_map.122 = (bf16[2048,256]{1,0:T(8,128)(2,1)S(1)}, bf16[2048,128]{1,0:T(8,128)(2,1)S(1)}, bf16[512,128]{1,0:T(8,128)(2,1)S(1)}, bf16[128,3072]{1,0:T(8,128...) custom-call(s32[16]{0:T(128)S(4)} %get-tuple-element.73.refs_0_.fact, ...), custom_call_target="tpu_custom_call" | custom-call | flops 4026531840 | bytes 1000 | tf_op jit(solution)/shard_map/pallas_call | solution.py:100
  10.5 0.0 collective-permute-done.1.refs_2_
  10.5 2.7 %collective-permute-start.2 = (bf16[2,128,256]{2,1,0:T(8,128)(2,1)S(1)}, bf16[2,128,256]{2,1,0:T(8,128)(2,1)S(1)}, u32[]{:S(2)}, u32[]{:S(2)}) collective-permute-start(bf16[2,128,256]{2,1,0:T(8,128)(2,1)S(1)} %shard_map.123.refs_17_.refs_3_), channel_id=1, source_target_pairs={{0,8},{4,12},{8,0},{12,4},{1,9},{5,13},{9,1},{13,5},{2,10},{6,14},... | collective-permute-start | bytes 393224 | tf_op jit(solution)/shard_map/ppermute | solution.py:729
  13.2 6.2 %shard_map.124 = (bf16[2048,256]{1,0:T(8,128)(2,1)S(1)}, bf16[2048,128]{1,0:T(8,128)(2,1)S(1)}, bf16[512,128]{1,0:T(8,128)(2,1)S(1)}, bf16[128,3072]{1,0:T(8,128...) custom-call(s32[16]{0:T(128)S(4)} %get-tuple-element.73.refs_0_.fact, ...), custom_call_target="tpu_custom_call" | custom-call | flops 12079595520 | bytes 1000 | tf_op jit(solution)/shard_map/pallas_call | solution.py:100
  19.4 0.2 collective-permute-done.2.refs_4_
  19.6 0.1 collective-permute-start.3
  19.7 3.2 %shard_map.126 = (bf16[3072,256]{1,0:T(8,128)(2,1)S(1)}, bf16[3072,256]{1,0:T(8,128)(2,1)S(1)}, bf16[8,128,256]{2,1,0:T(8,128)(2,1)S(1)}) custom-call(s32[16]{0:T(128)S(4)} %get-tuple-element.73.refs_0_.facts, bf16[128,3072]{1,0:T(8,128)(2,1)S(1)} %get-tuple-element.90.refs_1_, bf16[128,3072]{1,0:T(8,128)(2,1)S(1)} %get-tuple-element.91.refs_2_, ...), custom_call_target="tpu_custom_call" | custom-call | flops 8053063680 | bytes 1000 | tf_op jit(solution)/shard_map/pallas_call | solution.py:100
  22.9 0.6 %collective-permute-start.4 = (bf16[8,128,256]{2,1,0:T(8,128)(2,1)S(1)}, bf16[8,128,256]{2,1,0:T(8,128)(2,1)S(1)}, u32[]{:S(2)}, u32[]{:S(2)}) collective-permute-start(bf16[8,128,256]{2,1,0:T(8,128)(2,1)S(1)} %get-tuple-element.117), channel_id=1, source_target_pairs={{0,1},{1,0},{2,3},{3,2},{4,5},{5,4},{6,7},{7,6},{8,9},{9,8},{10,11... | collective-permute-start | bytes 1572872 | tf_op jit(solution)/shard_map/ppermute | solution.py:729
  23.5 0.0 collective-permute-done.3.refs_13_.refs_2_
  23.5 3.3 %shard_map.127 = (bf16[3072,256]{1,0:T(8,128)(2,1)S(1)}, bf16[3072,256]{1,0:T(8,128)(2,1)S(1)}, f32[4,128,256]{2,1,0:T(8,128)S(1)}) custom-call(s32[16]{0:T(128)S(4)} %get-tuple-element.73.refs_0_.facts, bf16[128,3072]{1,0:T(8,128)(2,1)S(1)} %get-tuple-element.104.refs_1_, bf16[128,3072]{1,0:T(8,128)(2,1)S(1)} %get-tuple-element.105.refs_2_, ...), custom_call_target="tpu_custom_call" | custom-call | flops 8053063680 | bytes 1000 | tf_op jit(solution)/shard_map/pallas_call | solution.py:100
  26.8 0.0 collective-permute-done.4.refs_2_.refs_4_
  26.8 0.1 shard_map.128
  26.9 1.3 %collective-permute-start.6 = (bf16[2,128,256]{2,1,0:T(8,128)(2,1)S(1)}, bf16[2,128,256]{2,1,0:T(8,128)(2,1)S(1)}, u32[]{:S(2)}, u32[]{:S(2)}) collective-permute-start(bf16[2,128,256]{2,1,0:T(8,128)(2,1)S(1)} %get-tuple-element.125), channel_id=1, source_target_pairs={{0,4},{4,0},{8,12},{12,8},{1,5},{5,1},{9,13},{13,9},{2,6},{6,2},{1... | collective-permute-start | bytes 393224 | tf_op jit(solution)/shard_map/ppermute | solution.py:729
  28.2 2.2 %collective-permute-start.5 = (bf16[2,128,256]{2,1,0:T(8,128)(2,1)S(1)}, bf16[2,128,256]{2,1,0:T(8,128)(2,1)S(1)}, u32[]{:S(2)}, u32[]{:S(2)}) collective-permute-start(bf16[2,128,256]{2,1,0:T(8,128)(2,1)S(1)} %get-tuple-element.118.refs_20_), channel_id=1, source_target_pairs={{0,8},{4,12},{8,0},{12,4},{1,9},{5,13},{9,1},{13,5},{2,10},{6,14},... | collective-permute-start | bytes 393224 | tf_op jit(solution)/shard_map/ppermute | solution.py:729
  30.4 0.1 shard_map.129
  30.5 1.6 %collective-permute-start.8 = (bf16[256,512]{1,0:T(8,128)(2,1)S(1)}, bf16[256,512]{1,0:T(8,128)(2,1)S(1)}, u32[]{:S(2)}, u32[]{:S(2)}) collective-permute-start(bf16[256,512]{1,0:T(8,128)(2,1)S(1)} %get-tuple-element.129.refs_0_.refs_3_), channel_id=1, source_target_pairs={{0,2},{2,0},{1,3},{3,1},{4,6},{6,4},{5,7},{7,5},{8,10},{10,8},{9,1... | collective-permute-start | bytes 786440 | tf_op jit(solution)/shard_map/ppermute | solution.py:729
  32.0 0.5 %collective-permute-start.9 = (bf16[128,512]{1,0:T(8,128)(2,1)S(1)}, bf16[128,512]{1,0:T(8,128)(2,1)S(1)}, u32[]{:S(2)}, u32[]{:S(2)}) collective-permute-start(bf16[128,512]{1,0:T(8,128)(2,1)S(1)} %get-tuple-element.121.refs_21_), channel_id=1, source_target_pairs={{0,2},{2,0},{1,3},{3,1},{4,6},{6,4},{5,7},{7,5},{8,10},{10,8},{9,1... | collective-permute-start | bytes 393224 | tf_op jit(solution)/shard_map/ppermute | solution.py:729
  32.6 4.4 %shard_map.130 = (bf16[384,4096]{1,0:T(8,128)(2,1)}, f32[8,128]{1,0:T(8,128)S(1)}, bf16[2560,1024]{1,0:T(8,128)(2,1)S(1)}) custom-call(s32[16]{0:T(128)S(4)} %get-tuple-element.73.refs_0_.facts, bf16[2,2,128,256]{3,2,1,0:T(8,128)(2,1)S(1)} %shard_map.125.refs_13_.refs_1_, bf16[2,2,128,256]{3,2,1,0:T(8,128)(2,1)S(1)} %collective-permute-done.3.refs_13_.refs_2_, ...), custom_call_target="tpu_custom_call" | custom-call | flops 1000 | bytes 1000 | tf_op jit(solution)/shard_map/pallas_call | solution.py:100
  36.9 0.0 collective-permute-done.6.refs_3_
  36.9 0.1 collective-permute-done.5.refs_2_
  37.1 0.1 shard_map.131
  37.1 0.1 collective-permute-start.7
  37.2 2.4 %collective-permute-done.8.refs_1_ = bf16[256,512]{1,0:T(8,128)(2,1)S(1)} collective-permute-done((bf16[256,512]{1,0:T(8,128)(2,1)S(1)}, bf16[256,512]{1,0:T(8,128)(2,1)S(1)}, u32[]{:S(2)}, u32[]{:S(2)}) %collective-permute-start.8) | collective-permute-done | bytes 262176 | tf_op jit(solution)/shard_map/ppermute | solution.py:729
  39.6 2.6 %shard_map.132 = (bf16[384,2560]{1,0:T(8,128)(2,1)}, bf16[384,512]{1,0:T(8,128)(2,1)}, bf16[384,512]{1,0:T(8,128)(2,1)}, f32[8,128]{1,0:T(8,128)S(1)}) custom-call(s32[16]{0:T(128)S(4)} %get-tuple-element.73.refs_0_.facts, bf16[256,512]{1,0:T(8,128)(2,1)S(1)} %get-tuple-element.129.refs_0_.refs_3_, bf16[256,512]{1,0:T(8,128)(2,1)S(1)} %collective-permute-done.8.refs_1_, ...), custom_call_target="tpu_custom_call" | custom-call | flops 1000 | bytes 1000 | tf_op jit(solution)/shard_map/pallas_call | solution.py:623
  42.3 0.0 collective-permute-done.9.refs_4_.refs_3_
  42.3 0.0 collective-permute-done.7.refs_2_
  42.3 0.1 collective-permute-start.10
  42.4 1.6 %collective-permute-start.12 = (bf16[128,256]{1,0:T(8,128)(2,1)S(1)}, bf16[128,256]{1,0:T(8,128)(2,1)S(1)}, u32[]{:S(2)}, u32[]{:S(2)}) collective-permute-start(bf16[128,256]{1,0:T(8,128)(2,1)S(1)} %get-tuple-element.134), channel_id=1, source_target_pairs={{0,3},{1,2},{2,1},{3,0},{4,7},{5,6},{6,5},{7,4},{8,11},{9,10},{10,... | collective-permute-start | bytes 196616 | tf_op jit(solution)/shard_map/ppermute | solution.py:817
  44.0 0.5 %collective-permute-start.11 = (bf16[128,256]{1,0:T(8,128)(2,1)S(1)}, bf16[128,256]{1,0:T(8,128)(2,1)S(1)}, u32[]{:S(2)}, u32[]{:S(2)}) collective-permute-start(bf16[128,256]{1,0:T(8,128)(2,1)S(1)} %get-tuple-element.134), channel_id=1, source_target_pairs={{0,2},{2,0},{1,3},{3,1},{4,6},{6,4},{5,7},{7,5},{8,10},{10,8},{9,1... | collective-permute-start | bytes 196616 | tf_op jit(solution)/shard_map/ppermute | solution.py:729
  44.5 0.0 collective-permute-done.10.refs_3_
  44.5 0.1 shard_map.134
  44.7 0.8 %shard_map.135.refs_2_ = f32[2560,128]{1,0:T(8,128)S(1)} custom-call(s32[16]{0:T(128)S(4)} %get-tuple-element.73.refs_0_.facts, bf16[2560,1024]{1,0:T(8,128)(2,1)S(1)} %get-tuple-element.123.refs_4_.refs_1_, bf16[128,512]{1,0:T(8,128)(2,1)S(1)} %get-tuple-element.133.refs_2_.refs_7_), custom_call_target="tpu_custom_call" | custom-call | flops 1000 | bytes 1000 | tf_op jit(solution)/shard_map/pallas_call | solution.py:684
  45.5 0.9 %collective-permute-done.12.refs_5_ = bf16[128,256]{1,0:T(8,128)(2,1)S(1)} collective-permute-done((bf16[128,256]{1,0:T(8,128)(2,1)S(1)}, bf16[128,256]{1,0:T(8,128)(2,1)S(1)}, u32[]{:S(2)}, u32[]{:S(2)}) %collective-permute-start.12) | collective-permute-done | bytes 65568 | tf_op jit(solution)/shard_map/ppermute | solution.py:817
  46.4 1.8 %collective-permute-done.11.refs_4_ = bf16[128,256]{1,0:T(8,128)(2,1)S(1)} collective-permute-done((bf16[128,256]{1,0:T(8,128)(2,1)S(1)}, bf16[128,256]{1,0:T(8,128)(2,1)S(1)}, u32[]{:S(2)}, u32[]{:S(2)}) %collective-permute-start.11) | collective-permute-done | bytes 65568 | tf_op jit(solution)/shard_map/ppermute | solution.py:729
  48.3 1.7 %shard_map.136 = (bf16[384,2560]{1,0:T(8,128)(2,1)}, bf16[384,512]{1,0:T(8,128)(2,1)}, bf16[384,512]{1,0:T(8,128)(2,1)}) custom-call(s32[16]{0:T(128)S(4)} %get-tuple-element.73.refs_0_.facts, bf16[2560,1024]{1,0:T(8,128)(2,1)S(1)} %get-tuple-element.123.refs_4_.refs_1_, ...), custom_call_target="tpu_custom_call", output_to_operand_aliasing={{0}: (8, {}), {1}: (9, {}), {2}: (10, {})} | custom-call | flops 1000 | bytes 1000 | tf_op jit(solution)/shard_map/pallas_call | solution.py:100
  (4 shorter events, 0.1 us)
Async XLA Ops:
  1.7 1.7 %collective-permute-start = (bf16[2,128,512]{2,1,0:T(8,128)(2,1)S(1)}, bf16[2,128,512]{2,1,0:T(8,128)(2,1)S(1)}, u32[]{:S(2)}, u32[]{:S(2)}) collective-permute-start(bf16[2,128,512]{2,1,0:T(8,128)(2,1)S(1)} %get-tuple-element.74.refs_1_.refs_11_), channel_id=1, source_target_pairs={{0,1},{1,0},{2,3},{3,2},{4,5},{5,4},{6,7},{7,6},{8,9},{9,8},{10,11... | collective-permute-start | bytes 786440 | tf_op jit(solution)/shard_map/ppermute | solution.py:729
  3.4 7.1 %collective-permute-start.1 = (bf16[2,128,256]{2,1,0:T(8,128)(2,1)S(1)}, bf16[2,128,256]{2,1,0:T(8,128)(2,1)S(1)}, u32[]{:S(2)}, u32[]{:S(2)}) collective-permute-start(bf16[2,128,256]{2,1,0:T(8,128)(2,1)S(1)} %shard_map.121.refs_9_.refs_1_), channel_id=1, source_target_pairs={{0,4},{4,0},{8,12},{12,8},{1,5},{5,1},{9,13},{13,9},{2,6},{6,2},{1... | collective-permute-start | bytes 393224 | tf_op jit(solution)/shard_map/ppermute | solution.py:729
  10.5 9.0 %collective-permute-start.2 = (bf16[2,128,256]{2,1,0:T(8,128)(2,1)S(1)}, bf16[2,128,256]{2,1,0:T(8,128)(2,1)S(1)}, u32[]{:S(2)}, u32[]{:S(2)}) collective-permute-start(bf16[2,128,256]{2,1,0:T(8,128)(2,1)S(1)} %shard_map.123.refs_17_.refs_3_), channel_id=1, source_target_pairs={{0,8},{4,12},{8,0},{12,4},{1,9},{5,13},{9,1},{13,5},{2,10},{6,14},... | collective-permute-start | bytes 393224 | tf_op jit(solution)/shard_map/ppermute | solution.py:729
  19.6 3.9 %collective-permute-start.3 = (bf16[2,2,128,256]{3,2,1,0:T(8,128)(2,1)S(1)}, bf16[2,2,128,256]{3,2,1,0:T(8,128)(2,1)S(1)}, u32[]{:S(2)}, u32[]{:S(2)}) collective-permute-start(bf16[2,2,128,256]{3,2,1,0:T(8,128)(2,1)S(1)} %shard_map.125.refs_13_.refs_1_), channel_id=1, source_target_pairs={{0,1},{1,0},{2,3},{3,2},{4,5},{5,4},{6,7},{7,6},{8,9},{9,8},{10,11... | collective-permute-start | bytes 786440 | tf_op jit(solution)/shard_map/ppermute | solution.py:729
  22.9 3.9 %collective-permute-start.4 = (bf16[8,128,256]{2,1,0:T(8,128)(2,1)S(1)}, bf16[8,128,256]{2,1,0:T(8,128)(2,1)S(1)}, u32[]{:S(2)}, u32[]{:S(2)}) collective-permute-start(bf16[8,128,256]{2,1,0:T(8,128)(2,1)S(1)} %get-tuple-element.117), channel_id=1, source_target_pairs={{0,1},{1,0},{2,3},{3,2},{4,5},{5,4},{6,7},{7,6},{8,9},{9,8},{10,11... | collective-permute-start | bytes 1572872 | tf_op jit(solution)/shard_map/ppermute | solution.py:729
  26.9 10.0 %collective-permute-start.6 = (bf16[2,128,256]{2,1,0:T(8,128)(2,1)S(1)}, bf16[2,128,256]{2,1,0:T(8,128)(2,1)S(1)}, u32[]{:S(2)}, u32[]{:S(2)}) collective-permute-start(bf16[2,128,256]{2,1,0:T(8,128)(2,1)S(1)} %get-tuple-element.125), channel_id=1, source_target_pairs={{0,4},{4,0},{8,12},{12,8},{1,5},{5,1},{9,13},{13,9},{2,6},{6,2},{1... | collective-permute-start | bytes 393224 | tf_op jit(solution)/shard_map/ppermute | solution.py:729
  28.2 8.9 %collective-permute-start.5 = (bf16[2,128,256]{2,1,0:T(8,128)(2,1)S(1)}, bf16[2,128,256]{2,1,0:T(8,128)(2,1)S(1)}, u32[]{:S(2)}, u32[]{:S(2)}) collective-permute-start(bf16[2,128,256]{2,1,0:T(8,128)(2,1)S(1)} %get-tuple-element.118.refs_20_), channel_id=1, source_target_pairs={{0,8},{4,12},{8,0},{12,4},{1,9},{5,13},{9,1},{13,5},{2,10},{6,14},... | collective-permute-start | bytes 393224 | tf_op jit(solution)/shard_map/ppermute | solution.py:729
  30.5 9.1 %collective-permute-start.8 = (bf16[256,512]{1,0:T(8,128)(2,1)S(1)}, bf16[256,512]{1,0:T(8,128)(2,1)S(1)}, u32[]{:S(2)}, u32[]{:S(2)}) collective-permute-start(bf16[256,512]{1,0:T(8,128)(2,1)S(1)} %get-tuple-element.129.refs_0_.refs_3_), channel_id=1, source_target_pairs={{0,2},{2,0},{1,3},{3,1},{4,6},{6,4},{5,7},{7,5},{8,10},{10,8},{9,1... | collective-permute-start | bytes 786440 | tf_op jit(solution)/shard_map/ppermute | solution.py:729
  32.0 10.2 %collective-permute-start.9 = (bf16[128,512]{1,0:T(8,128)(2,1)S(1)}, bf16[128,512]{1,0:T(8,128)(2,1)S(1)}, u32[]{:S(2)}, u32[]{:S(2)}) collective-permute-start(bf16[128,512]{1,0:T(8,128)(2,1)S(1)} %get-tuple-element.121.refs_21_), channel_id=1, source_target_pairs={{0,2},{2,0},{1,3},{3,1},{4,6},{6,4},{5,7},{7,5},{8,10},{10,8},{9,1... | collective-permute-start | bytes 393224 | tf_op jit(solution)/shard_map/ppermute | solution.py:729
  37.1 5.1 %collective-permute-start.7 = (bf16[2,128,256]{2,1,0:T(8,128)(2,1)S(1)}, bf16[2,128,256]{2,1,0:T(8,128)(2,1)S(1)}, u32[]{:S(2)}, u32[]{:S(2)}) collective-permute-start(bf16[2,128,256]{2,1,0:T(8,128)(2,1)S(1)} %get-tuple-element.128.refs_5_), channel_id=1, source_target_pairs={{0,4},{4,0},{8,12},{12,8},{1,5},{5,1},{9,13},{13,9},{2,6},{6,2},{1... | collective-permute-start | bytes 393224 | tf_op jit(solution)/shard_map/ppermute | solution.py:729
  42.3 2.2 %collective-permute-start.10 = (bf16[2,128,256]{2,1,0:T(8,128)(2,1)S(1)}, bf16[2,128,256]{2,1,0:T(8,128)(2,1)S(1)}, u32[]{:S(2)}, u32[]{:S(2)}) collective-permute-start(bf16[2,128,256]{2,1,0:T(8,128)(2,1)S(1)} %get-tuple-element.132.refs_2_), channel_id=1, source_target_pairs={{0,1},{1,0},{2,3},{3,2},{4,5},{5,4},{6,7},{7,6},{8,9},{9,8},{10,11... | collective-permute-start | bytes 393224 | tf_op jit(solution)/shard_map/ppermute | solution.py:729
  42.4 4.0 %collective-permute-start.12 = (bf16[128,256]{1,0:T(8,128)(2,1)S(1)}, bf16[128,256]{1,0:T(8,128)(2,1)S(1)}, u32[]{:S(2)}, u32[]{:S(2)}) collective-permute-start(bf16[128,256]{1,0:T(8,128)(2,1)S(1)} %get-tuple-element.134), channel_id=1, source_target_pairs={{0,3},{1,2},{2,1},{3,0},{4,7},{5,6},{6,5},{7,4},{8,11},{9,10},{10,... | collective-permute-start | bytes 196616 | tf_op jit(solution)/shard_map/ppermute | solution.py:817
  44.0 4.3 %collective-permute-start.11 = (bf16[128,256]{1,0:T(8,128)(2,1)S(1)}, bf16[128,256]{1,0:T(8,128)(2,1)S(1)}, u32[]{:S(2)}, u32[]{:S(2)}) collective-permute-start(bf16[128,256]{1,0:T(8,128)(2,1)S(1)} %get-tuple-element.134), channel_id=1, source_target_pairs={{0,2},{2,0},{1,3},{3,1},{4,6},{6,4},{5,7},{7,5},{8,10},{10,8},{9,1... | collective-permute-start | bytes 196616 | tf_op jit(solution)/shard_map/ppermute | solution.py:729

commit v20 on v19

--- a/solution.py
+++ b/solution.py
@@ -691,7 +691,7 @@
     )(pltpu.with_memory_space_constraint(facts, pltpu.SMEM), *near, *after)
 
 
-def end_input_grad(order, facts, w, base, across, corner, begun, grads, carry):
+def end_input_grad(order, facts, w, base, across, corner, begun, grads, carry, after):
     tiles = width_tiles(w)
     out_cols, depth = w.shape
     half = depth // 2
@@ -720,7 +720,7 @@
             pltpu.VMEM((steps, rows, out_cols // steps), BF16),
             pltpu.SemaphoreType.DMA((steps + 2 * order.heads,)),
         ],
-        {("far", i): i for i in range(len(carry))},
+        {("far", i): i for i in range(len(carry))}, after,
     )
 
 
@@ -926,7 +926,7 @@
         base, dv12 = begin_values(order, facts, own0, sent, dv12)
         far_v = spread(dv12)
         made, w_near = finish_queries(
-            kvs, group, order, facts, (mine, theirs), state, (root, base), w
+            kvs[:3], group, order, facts, (mine, theirs), state, (root, base), w
         )
         total, low, far = over_halves(facts, total, root_far, next_far, (made,))
         base_far = spread(base)
@@ -937,8 +937,11 @@
         near, far, across, corner = over_chips(facts, total, far, (made, base_far))
         dk0, dv0 = finish_small_tree(order, facts, own0, near, far, sent)
         begun = begin_input_grad(order, facts, w_near, [dv0])
+        made = finish_queries(
+            kvs[3:], group, order, facts, (mine, theirs), state, (begun,)
+        )
         grads = end_input_grad(
-            order, facts, w_near, base_far, across, corner, begun, [dk0, dv0], grads
+            order, facts, w_near, base_far, across, corner, begun, [dk0, dv0], grads, made
         )
         return (state["gq"], grads[1], grads[2], grads[0])
 

time: 50.3 us -> 50.2 us (level)
  waiting for transfers between devices: 6.68 us -> 5.82 us
  Pallas kernels: 27.8 us -> 28.5 us
    ppermute x1, waiting for transfers between devices: 0.94 us -> 0.01 us  [over_chips(): lax.ppermute(values, ('tensor', 'sub'), [(i, 3 - i) for i in range(4)])]
    pallas_call x14 -> x15, Pallas kernels: 23.4 us -> 24 us  [kernel_call(): pl.pallas_call(kernel, out_shape=tuple((pltpu.VMEM(s, d) if inside else j...]
  transfers between devices with their start and end apart: 13 -> 13, of which waited for: 6 -> 5; matrix products, arithmetic and copies ran while one was open for 0% -> 0% of each run, Pallas kernels for 50% -> 51%
where the time goes in v20:
time: 50.2 us; the launch traced here: 50 us
  Pallas kernels  28.5 us (57%)
  starting transfers between devices  14.7 us (29%)
  waiting for transfers between devices  5.82 us (12%)
  between operations  0.99 us (2%)
    pallas_call x15, Pallas kernels, kernel_call(): pl.pallas_call(kernel, out_shape=tuple((pltpu.VMEM(s, d) if inside else j...  24 us
    ppermute x12, starting transfers between devices, flipped(): lax.ppermute(block, axis, [(i, i ^ bit) for i in range(count) if i ^ bit...  13.1 us
    ppermute x12, waiting for transfers between devices, flipped(): lax.ppermute(block, axis, [(i, i ^ bit) for i in range(count) if i ^ bit...  5.82 us
    pallas_call x1, Pallas kernels, input_grad(): pl.pallas_call(body, out_shape=(jax.ShapeDtypeStruct((ROWS, out_cols), BF...  2.62 us
    ppermute x1, starting transfers between devices, over_chips(): lax.ppermute(values, ('tensor', 'sub'), [(i, 3 - i) for i in range(4)])  1.61 us
    pallas_call x1, Pallas kernels, start(): pl.pallas_call(body, out_shape=(pltpu.SMEM((FACTS,), I32), pltpu.VMEM((2,...  1.02 us
  transfers between devices with their start and end apart: 13, of which 5 were waited for; matrix products, arithmetic and copies ran while one was open for 0% of the time, Pallas kernels for 51%

profile of v20, /device:TPU:0, one launch (start us, length us, event | category | flops | bytes accessed | tf_op | source)
XLA Modules:
  0.0 50.0 jit_solution(7188437977853073465)
XLA Ops:
  0.6 1.0 %shard_map.120 = (s32[16]{0:T(128)S(4)}, bf16[2,128,512]{2,1,0:T(8,128)(2,1)S(1)}) custom-call(s32[1]{0:T(128)} %bitcast.side_ref, s32[1,5]{1,0:T(1,128)} %ids_ref.1, s32[1,3]{1,0:T(1,128)} %counts_ref.1, bf16[384,512]{1,0:T(8,128)(2,1)} %refs_5_.1, bf16[384,512]{1,0:T(8,128)(2,1)} %refs_6_.1), custom_call_target="tpu_custom_call" | custom-call | tf_op jit(solution)/shard_map/pallas_call | solution.py:141
  1.7 0.5 %collective-permute-start = (bf16[2,128,512]{2,1,0:T(8,128)(2,1)S(1)}, bf16[2,128,512]{2,1,0:T(8,128)(2,1)S(1)}, u32[]{:S(2)}, u32[]{:S(2)}) collective-permute-start(bf16[2,128,512]{2,1,0:T(8,128)(2,1)S(1)} %get-tuple-element.76.refs_1_.refs_11_), channel_id=1, source_target_pairs={{0,1},{1,0},{2,3},{3,2},{4,5},{5,4},{6,7},{7,6},{8,9},{9,8},{10,11... | collective-permute-start | bytes 786440 | tf_op jit(solution)/shard_map/ppermute | solution.py:729
  2.2 1.2 %collective-permute-done.refs_2_.refs_12_ = bf16[2,128,512]{2,1,0:T(8,128)(2,1)S(1)} collective-permute-done((bf16[2,128,512]{2,1,0:T(8,128)(2,1)S(1)}, bf16[2,128,512]{2,1,0:T(8,128)(2,1)S(1)}, u32[]{:S(2)}, u32[]{:S(2)}) %collective-permute-start) | collective-permute-done | bytes 262176 | tf_op jit(solution)/shard_map/ppermute | solution.py:729
  3.4 3.0 %collective-permute-start.1 = (bf16[2,128,256]{2,1,0:T(8,128)(2,1)S(1)}, bf16[2,128,256]{2,1,0:T(8,128)(2,1)S(1)}, u32[]{:S(2)}, u32[]{:S(2)}) collective-permute-start(bf16[2,128,256]{2,1,0:T(8,128)(2,1)S(1)} %shard_map.121.refs_9_.refs_1_), channel_id=1, source_target_pairs={{0,4},{4,0},{8,12},{12,8},{1,5},{5,1},{9,13},{13,9},{2,6},{6,2},{1... | collective-permute-start | bytes 393224 | tf_op jit(solution)/shard_map/ppermute | solution.py:729
  6.4 4.1 %shard_map.122 = (bf16[2048,256]{1,0:T(8,128)(2,1)S(1)}, bf16[2048,128]{1,0:T(8,128)(2,1)S(1)}, bf16[512,128]{1,0:T(8,128)(2,1)S(1)}, bf16[128,3072]{1,0:T(8,128...) custom-call(s32[16]{0:T(128)S(4)} %get-tuple-element.75.refs_0_.fact, ...), custom_call_target="tpu_custom_call" | custom-call | flops 4026531840 | bytes 1000 | tf_op jit(solution)/shard_map/pallas_call | solution.py:100
  10.5 0.0 collective-permute-done.1.refs_2_
  10.5 2.7 %collective-permute-start.2 = (bf16[2,128,256]{2,1,0:T(8,128)(2,1)S(1)}, bf16[2,128,256]{2,1,0:T(8,128)(2,1)S(1)}, u32[]{:S(2)}, u32[]{:S(2)}) collective-permute-start(bf16[2,128,256]{2,1,0:T(8,128)(2,1)S(1)} %shard_map.123.refs_17_.refs_3_), channel_id=1, source_target_pairs={{0,8},{4,12},{8,0},{12,4},{1,9},{5,13},{9,1},{13,5},{2,10},{6,14},... | collective-permute-start | bytes 393224 | tf_op jit(solution)/shard_map/ppermute | solution.py:729
  13.1 6.1 %shard_map.124 = (bf16[2048,256]{1,0:T(8,128)(2,1)S(1)}, bf16[2048,128]{1,0:T(8,128)(2,1)S(1)}, bf16[512,128]{1,0:T(8,128)(2,1)S(1)}, bf16[128,3072]{1,0:T(8,128...) custom-call(s32[16]{0:T(128)S(4)} %get-tuple-element.75.refs_0_.fact, ...), custom_call_target="tpu_custom_call" | custom-call | flops 12079595520 | bytes 1000 | tf_op jit(solution)/shard_map/pallas_call | solution.py:100
  19.3 0.2 collective-permute-done.2.refs_4_
  19.5 0.1 collective-permute-start.3
  19.6 3.1 %shard_map.127 = (bf16[3072,256]{1,0:T(8,128)(2,1)S(1)}, bf16[3072,256]{1,0:T(8,128)(2,1)S(1)}, bf16[8,128,256]{2,1,0:T(8,128)(2,1)S(1)}) custom-call(s32[16]{0:T(128)S(4)} %get-tuple-element.75.refs_0_.facts, bf16[128,3072]{1,0:T(8,128)(2,1)S(1)} %get-tuple-element.100.refs_1_, bf16[128,3072]{1,0:T(8,128)(2,1)S(1)} %get-tuple-element.101.refs_2_, ...), custom_call_target="tpu_custom_call" | custom-call | flops 8053063680 | bytes 1000 | tf_op jit(solution)/shard_map/pallas_call | solution.py:100
  22.8 0.6 %collective-permute-start.4 = (bf16[8,128,256]{2,1,0:T(8,128)(2,1)S(1)}, bf16[8,128,256]{2,1,0:T(8,128)(2,1)S(1)}, u32[]{:S(2)}, u32[]{:S(2)}) collective-permute-start(bf16[8,128,256]{2,1,0:T(8,128)(2,1)S(1)} %get-tuple-element.119), channel_id=1, source_target_pairs={{0,1},{1,0},{2,3},{3,2},{4,5},{5,4},{6,7},{7,6},{8,9},{9,8},{10,11... | collective-permute-start | bytes 1572872 | tf_op jit(solution)/shard_map/ppermute | solution.py:729
  23.3 0.0 collective-permute-done.3.refs_13_.refs_2_
  23.3 3.3 %shard_map.126 = (bf16[3072,256]{1,0:T(8,128)(2,1)S(1)}, bf16[3072,256]{1,0:T(8,128)(2,1)S(1)}, f32[4,128,256]{2,1,0:T(8,128)S(1)}) custom-call(s32[16]{0:T(128)S(4)} %get-tuple-element.75.refs_0_.facts, bf16[128,3072]{1,0:T(8,128)(2,1)S(1)} %get-tuple-element.92.refs_1_, bf16[128,3072]{1,0:T(8,128)(2,1)S(1)} %get-tuple-element.93.refs_2_, ...), custom_call_target="tpu_custom_call" | custom-call | flops 8053063680 | bytes 1000 | tf_op jit(solution)/shard_map/pallas_call | solution.py:100
  26.7 0.0 collective-permute-done.4.refs_2_.refs_4_
  26.7 0.1 shard_map.128
  26.7 1.3 %collective-permute-start.6 = (bf16[2,128,256]{2,1,0:T(8,128)(2,1)S(1)}, bf16[2,128,256]{2,1,0:T(8,128)(2,1)S(1)}, u32[]{:S(2)}, u32[]{:S(2)}) collective-permute-start(bf16[2,128,256]{2,1,0:T(8,128)(2,1)S(1)} %get-tuple-element.127), channel_id=1, source_target_pairs={{0,4},{4,0},{8,12},{12,8},{1,5},{5,1},{9,13},{13,9},{2,6},{6,2},{1... | collective-permute-start | bytes 393224 | tf_op jit(solution)/shard_map/ppermute | solution.py:729
  28.0 2.3 %collective-permute-start.5 = (bf16[2,128,256]{2,1,0:T(8,128)(2,1)S(1)}, bf16[2,128,256]{2,1,0:T(8,128)(2,1)S(1)}, u32[]{:S(2)}, u32[]{:S(2)}) collective-permute-start(bf16[2,128,256]{2,1,0:T(8,128)(2,1)S(1)} %get-tuple-element.120.refs_16_), channel_id=1, source_target_pairs={{0,8},{4,12},{8,0},{12,4},{1,9},{5,13},{9,1},{13,5},{2,10},{6,14},... | collective-permute-start | bytes 393224 | tf_op jit(solution)/shard_map/ppermute | solution.py:729
  30.3 0.1 shard_map.129
  30.3 1.6 %collective-permute-start.8 = (bf16[256,512]{1,0:T(8,128)(2,1)S(1)}, bf16[256,512]{1,0:T(8,128)(2,1)S(1)}, u32[]{:S(2)}, u32[]{:S(2)}) collective-permute-start(bf16[256,512]{1,0:T(8,128)(2,1)S(1)} %get-tuple-element.131.refs_0_.refs_3_), channel_id=1, source_target_pairs={{0,2},{2,0},{1,3},{3,1},{4,6},{6,4},{5,7},{7,5},{8,10},{10,8},{9,1... | collective-permute-start | bytes 786440 | tf_op jit(solution)/shard_map/ppermute | solution.py:729
  31.9 0.5 %collective-permute-start.9 = (bf16[128,512]{1,0:T(8,128)(2,1)S(1)}, bf16[128,512]{1,0:T(8,128)(2,1)S(1)}, u32[]{:S(2)}, u32[]{:S(2)}) collective-permute-start(bf16[128,512]{1,0:T(8,128)(2,1)S(1)} %get-tuple-element.123.refs_17_), channel_id=1, source_target_pairs={{0,2},{2,0},{1,3},{3,1},{4,6},{6,4},{5,7},{7,5},{8,10},{10,8},{9,1... | collective-permute-start | bytes 393224 | tf_op jit(solution)/shard_map/ppermute | solution.py:729
  32.4 3.5 %shard_map.130 = (bf16[384,4096]{1,0:T(8,128)(2,1)}, f32[8,128]{1,0:T(8,128)S(1)}, bf16[2560,1024]{1,0:T(8,128)(2,1)S(1)}) custom-call(s32[16]{0:T(128)S(4)} %get-tuple-element.75.refs_0_.facts, bf16[2,2,128,256]{3,2,1,0:T(8,128)(2,1)S(1)} %shard_map.125.refs_13_.refs_1_, bf16[2,2,128,256]{3,2,1,0:T(8,128)(2,1)S(1)} %collective-permute-done.3.refs_13_.refs_2_, ...), custom_call_target="tpu_custom_call" | custom-call | flops 1000 | bytes 1000 | tf_op jit(solution)/shard_map/pallas_call | solution.py:100
  35.9 0.0 collective-permute-done.6.refs_3_
  35.9 1.0 %collective-permute-done.5.refs_2_ = bf16[2,128,256]{2,1,0:T(8,128)(2,1)S(1)} collective-permute-done((bf16[2,128,256]{2,1,0:T(8,128)(2,1)S(1)}, bf16[2,128,256]{2,1,0:T(8,128)(2,1)S(1)}, u32[]{:S(2)}, u32[]{:S(2)}) %collective-permute-start.5) | collective-permute-done | bytes 131104 | tf_op jit(solution)/shard_map/ppermute | solution.py:729
  36.9 0.1 shard_map.131
  37.0 0.1 collective-permute-start.7
  37.0 2.4 %collective-permute-done.8.refs_1_ = bf16[256,512]{1,0:T(8,128)(2,1)S(1)} collective-permute-done((bf16[256,512]{1,0:T(8,128)(2,1)S(1)}, bf16[256,512]{1,0:T(8,128)(2,1)S(1)}, u32[]{:S(2)}, u32[]{:S(2)}) %collective-permute-start.8) | collective-permute-done | bytes 262176 | tf_op jit(solution)/shard_map/ppermute | solution.py:729
  39.5 2.6 %shard_map.132 = (bf16[384,2560]{1,0:T(8,128)(2,1)}, bf16[384,512]{1,0:T(8,128)(2,1)}, bf16[384,512]{1,0:T(8,128)(2,1)}, f32[8,128]{1,0:T(8,128)S(1)}) custom-call(s32[16]{0:T(128)S(4)} %get-tuple-element.75.refs_0_.facts, bf16[256,512]{1,0:T(8,128)(2,1)S(1)} %get-tuple-element.131.refs_0_.refs_3_, bf16[256,512]{1,0:T(8,128)(2,1)S(1)} %collective-permute-done.8.refs_1_, ...), custom_call_target="tpu_custom_call" | custom-call | flops 1000 | bytes 1000 | tf_op jit(solution)/shard_map/pallas_call | solution.py:623
  42.1 0.0 collective-permute-done.9.refs_4_.refs_3_
  42.1 0.0 collective-permute-done.7.refs_2_
  42.2 0.1 collective-permute-start.10
  42.3 1.6 %collective-permute-start.12 = (bf16[128,256]{1,0:T(8,128)(2,1)S(1)}, bf16[128,256]{1,0:T(8,128)(2,1)S(1)}, u32[]{:S(2)}, u32[]{:S(2)}) collective-permute-start(bf16[128,256]{1,0:T(8,128)(2,1)S(1)} %get-tuple-element.137), channel_id=1, source_target_pairs={{0,3},{1,2},{2,1},{3,0},{4,7},{5,6},{6,5},{7,4},{8,11},{9,10},{10,... | collective-permute-start | bytes 196616 | tf_op jit(solution)/shard_map/ppermute | solution.py:817
  43.9 0.5 %collective-permute-start.11 = (bf16[128,256]{1,0:T(8,128)(2,1)S(1)}, bf16[128,256]{1,0:T(8,128)(2,1)S(1)}, u32[]{:S(2)}, u32[]{:S(2)}) collective-permute-start(bf16[128,256]{1,0:T(8,128)(2,1)S(1)} %get-tuple-element.137), channel_id=1, source_target_pairs={{0,2},{2,0},{1,3},{3,1},{4,6},{6,4},{5,7},{7,5},{8,10},{10,8},{9,1... | collective-permute-start | bytes 196616 | tf_op jit(solution)/shard_map/ppermute | solution.py:729
  44.4 0.0 collective-permute-done.10.refs_3_
  44.4 0.1 shard_map.134
  44.5 0.8 %shard_map.135.refs_8_.refs_2_ = f32[2560,128]{1,0:T(8,128)S(1)} custom-call(s32[16]{0:T(128)S(4)} %get-tuple-element.75.refs_0_.facts, bf16[2560,1024]{1,0:T(8,128)(2,1)S(1)} %get-tuple-element.125.refs_4_.refs_1_, bf16[128,512]{1,0:T(8,128)(2,1)S(1)} %get-tuple-element.135.refs_2_.refs_7_), custom_call_target="tpu_custom_call" | custom-call | flops 1000 | bytes 1000 | tf_op jit(solution)/shard_map/pallas_call | solution.py:684
  45.4 1.8 %shard_map.136 = (bf16[384,4096]{1,0:T(8,128)(2,1)}, f32[8,128]{1,0:T(8,128)S(1)}) custom-call(s32[16]{0:T(128)S(4)} %get-tuple-element.75.refs_0_.facts, bf16[2,2,128,256]{3,2,1,0:T(8,128)(2,1)S(1)} %shard_map.125.refs_13_.refs_1_, bf16[2,2,128,256]{3,2,1,0:T(8,128)(2,1)S(1)} %collective-permute-done.3.refs_13_.refs_2_, ...), custom_call_target="tpu_custom_call", output_to_operand_aliasing={{0}: (7, {})} | custom-call | flops 1000 | bytes 1000 | tf_op jit(solution)/shard_map/pallas_call | solution.py:100
  47.2 0.0 collective-permute-done.12.refs_5_
  47.2 1.0 %collective-permute-done.11.refs_4_ = bf16[128,256]{1,0:T(8,128)(2,1)S(1)} collective-permute-done((bf16[128,256]{1,0:T(8,128)(2,1)S(1)}, bf16[128,256]{1,0:T(8,128)(2,1)S(1)}, u32[]{:S(2)}, u32[]{:S(2)}) %collective-permute-start.11) | collective-permute-done | bytes 65568 | tf_op jit(solution)/shard_map/ppermute | solution.py:729
  48.1 1.7 %shard_map.137 = (bf16[384,2560]{1,0:T(8,128)(2,1)}, bf16[384,512]{1,0:T(8,128)(2,1)}, bf16[384,512]{1,0:T(8,128)(2,1)}) custom-call(s32[16]{0:T(128)S(4)} %get-tuple-element.75.refs_0_.facts, bf16[2560,1024]{1,0:T(8,128)(2,1)S(1)} %get-tuple-element.125.refs_4_.refs_1_, ...), custom_call_target="tpu_custom_call", output_to_operand_aliasing={{0}: (8, {}), {1}: (9, {}), {2}: (10, {})} | custom-call | flops 1000 | bytes 1000 | tf_op jit(solution)/shard_map/pallas_call | solution.py:100
  (4 shorter events, 0.1 us)
Async XLA Ops:
  1.7 1.7 %collective-permute-start = (bf16[2,128,512]{2,1,0:T(8,128)(2,1)S(1)}, bf16[2,128,512]{2,1,0:T(8,128)(2,1)S(1)}, u32[]{:S(2)}, u32[]{:S(2)}) collective-permute-start(bf16[2,128,512]{2,1,0:T(8,128)(2,1)S(1)} %get-tuple-element.76.refs_1_.refs_11_), channel_id=1, source_target_pairs={{0,1},{1,0},{2,3},{3,2},{4,5},{5,4},{6,7},{7,6},{8,9},{9,8},{10,11... | collective-permute-start | bytes 786440 | tf_op jit(solution)/shard_map/ppermute | solution.py:729
  3.4 7.1 %collective-permute-start.1 = (bf16[2,128,256]{2,1,0:T(8,128)(2,1)S(1)}, bf16[2,128,256]{2,1,0:T(8,128)(2,1)S(1)}, u32[]{:S(2)}, u32[]{:S(2)}) collective-permute-start(bf16[2,128,256]{2,1,0:T(8,128)(2,1)S(1)} %shard_map.121.refs_9_.refs_1_), channel_id=1, source_target_pairs={{0,4},{4,0},{8,12},{12,8},{1,5},{5,1},{9,13},{13,9},{2,6},{6,2},{1... | collective-permute-start | bytes 393224 | tf_op jit(solution)/shard_map/ppermute | solution.py:729
  10.5 9.0 %collective-permute-start.2 = (bf16[2,128,256]{2,1,0:T(8,128)(2,1)S(1)}, bf16[2,128,256]{2,1,0:T(8,128)(2,1)S(1)}, u32[]{:S(2)}, u32[]{:S(2)}) collective-permute-start(bf16[2,128,256]{2,1,0:T(8,128)(2,1)S(1)} %shard_map.123.refs_17_.refs_3_), channel_id=1, source_target_pairs={{0,8},{4,12},{8,0},{12,4},{1,9},{5,13},{9,1},{13,5},{2,10},{6,14},... | collective-permute-start | bytes 393224 | tf_op jit(solution)/shard_map/ppermute | solution.py:729
  19.5 3.8 %collective-permute-start.3 = (bf16[2,2,128,256]{3,2,1,0:T(8,128)(2,1)S(1)}, bf16[2,2,128,256]{3,2,1,0:T(8,128)(2,1)S(1)}, u32[]{:S(2)}, u32[]{:S(2)}) collective-permute-start(bf16[2,2,128,256]{3,2,1,0:T(8,128)(2,1)S(1)} %shard_map.125.refs_13_.refs_1_), channel_id=1, source_target_pairs={{0,1},{1,0},{2,3},{3,2},{4,5},{5,4},{6,7},{7,6},{8,9},{9,8},{10,11... | collective-permute-start | bytes 786440 | tf_op jit(solution)/shard_map/ppermute | solution.py:729
  22.8 3.9 %collective-permute-start.4 = (bf16[8,128,256]{2,1,0:T(8,128)(2,1)S(1)}, bf16[8,128,256]{2,1,0:T(8,128)(2,1)S(1)}, u32[]{:S(2)}, u32[]{:S(2)}) collective-permute-start(bf16[8,128,256]{2,1,0:T(8,128)(2,1)S(1)} %get-tuple-element.119), channel_id=1, source_target_pairs={{0,1},{1,0},{2,3},{3,2},{4,5},{5,4},{6,7},{7,6},{8,9},{9,8},{10,11... | collective-permute-start | bytes 1572872 | tf_op jit(solution)/shard_map/ppermute | solution.py:729
  26.7 9.2 %collective-permute-start.6 = (bf16[2,128,256]{2,1,0:T(8,128)(2,1)S(1)}, bf16[2,128,256]{2,1,0:T(8,128)(2,1)S(1)}, u32[]{:S(2)}, u32[]{:S(2)}) collective-permute-start(bf16[2,128,256]{2,1,0:T(8,128)(2,1)S(1)} %get-tuple-element.127), channel_id=1, source_target_pairs={{0,4},{4,0},{8,12},{12,8},{1,5},{5,1},{9,13},{13,9},{2,6},{6,2},{1... | collective-permute-start | bytes 393224 | tf_op jit(solution)/shard_map/ppermute | solution.py:729
  28.0 8.9 %collective-permute-start.5 = (bf16[2,128,256]{2,1,0:T(8,128)(2,1)S(1)}, bf16[2,128,256]{2,1,0:T(8,128)(2,1)S(1)}, u32[]{:S(2)}, u32[]{:S(2)}) collective-permute-start(bf16[2,128,256]{2,1,0:T(8,128)(2,1)S(1)} %get-tuple-element.120.refs_16_), channel_id=1, source_target_pairs={{0,8},{4,12},{8,0},{12,4},{1,9},{5,13},{9,1},{13,5},{2,10},{6,14},... | collective-permute-start | bytes 393224 | tf_op jit(solution)/shard_map/ppermute | solution.py:729
  30.3 9.1 %collective-permute-start.8 = (bf16[256,512]{1,0:T(8,128)(2,1)S(1)}, bf16[256,512]{1,0:T(8,128)(2,1)S(1)}, u32[]{:S(2)}, u32[]{:S(2)}) collective-permute-start(bf16[256,512]{1,0:T(8,128)(2,1)S(1)} %get-tuple-element.131.refs_0_.refs_3_), channel_id=1, source_target_pairs={{0,2},{2,0},{1,3},{3,1},{4,6},{6,4},{5,7},{7,5},{8,10},{10,8},{9,1... | collective-permute-start | bytes 786440 | tf_op jit(solution)/shard_map/ppermute | solution.py:729
  31.9 10.2 %collective-permute-start.9 = (bf16[128,512]{1,0:T(8,128)(2,1)S(1)}, bf16[128,512]{1,0:T(8,128)(2,1)S(1)}, u32[]{:S(2)}, u32[]{:S(2)}) collective-permute-start(bf16[128,512]{1,0:T(8,128)(2,1)S(1)} %get-tuple-element.123.refs_17_), channel_id=1, source_target_pairs={{0,2},{2,0},{1,3},{3,1},{4,6},{6,4},{5,7},{7,5},{8,10},{10,8},{9,1... | collective-permute-start | bytes 393224 | tf_op jit(solution)/shard_map/ppermute | solution.py:729
  37.0 5.2 %collective-permute-start.7 = (bf16[2,128,256]{2,1,0:T(8,128)(2,1)S(1)}, bf16[2,128,256]{2,1,0:T(8,128)(2,1)S(1)}, u32[]{:S(2)}, u32[]{:S(2)}) collective-permute-start(bf16[2,128,256]{2,1,0:T(8,128)(2,1)S(1)} %get-tuple-element.130.refs_5_), channel_id=1, source_target_pairs={{0,4},{4,0},{8,12},{12,8},{1,5},{5,1},{9,13},{13,9},{2,6},{6,2},{1... | collective-permute-start | bytes 393224 | tf_op jit(solution)/shard_map/ppermute | solution.py:729
  42.2 2.2 %collective-permute-start.10 = (bf16[2,128,256]{2,1,0:T(8,128)(2,1)S(1)}, bf16[2,128,256]{2,1,0:T(8,128)(2,1)S(1)}, u32[]{:S(2)}, u32[]{:S(2)}) collective-permute-start(bf16[2,128,256]{2,1,0:T(8,128)(2,1)S(1)} %get-tuple-element.134.refs_2_), channel_id=1, source_target_pairs={{0,1},{1,0},{2,3},{3,2},{4,5},{5,4},{6,7},{7,6},{8,9},{9,8},{10,11... | collective-permute-start | bytes 393224 | tf_op jit(solution)/shard_map/ppermute | solution.py:729
  42.3 4.9 %collective-permute-start.12 = (bf16[128,256]{1,0:T(8,128)(2,1)S(1)}, bf16[128,256]{1,0:T(8,128)(2,1)S(1)}, u32[]{:S(2)}, u32[]{:S(2)}) collective-permute-start(bf16[128,256]{1,0:T(8,128)(2,1)S(1)} %get-tuple-element.137), channel_id=1, source_target_pairs={{0,3},{1,2},{2,1},{3,0},{4,7},{5,6},{6,5},{7,4},{8,11},{9,10},{10,... | collective-permute-start | bytes 196616 | tf_op jit(solution)/shard_map/ppermute | solution.py:817
  43.9 4.3 %collective-permute-start.11 = (bf16[128,256]{1,0:T(8,128)(2,1)S(1)}, bf16[128,256]{1,0:T(8,128)(2,1)S(1)}, u32[]{:S(2)}, u32[]{:S(2)}) collective-permute-start(bf16[128,256]{1,0:T(8,128)(2,1)S(1)} %get-tuple-element.137), channel_id=1, source_target_pairs={{0,2},{2,0},{1,3},{3,1},{4,6},{6,4},{5,7},{7,5},{8,10},{10,8},{9,1... | collective-permute-start | bytes 196616 | tf_op jit(solution)/shard_map/ppermute | solution.py:729

commit v21 on v19

--- a/solution.py
+++ b/solution.py
@@ -930,13 +930,13 @@
         )
         total, low, far = over_halves(facts, total, root_far, next_far, (made,))
         base_far = spread(base)
-        *grads, made = input_grad(
-            order, facts, w_near, 2 * PAGE, [dv12], [far_v], ([dk12], [dv12]), near_w=True,
-            after=(low,),
-        )
-        near, far, across, corner = over_chips(facts, total, far, (made, base_far))
+        near, far, across, corner = over_chips(facts, total, far, (low, base_far, far_v))
         dk0, dv0 = finish_small_tree(order, facts, own0, near, far, sent)
         begun = begin_input_grad(order, facts, w_near, [dv0])
+        *grads, _ = input_grad(
+            order, facts, w_near, 2 * PAGE, [dv12], [far_v], ([dk12], [dv12]), near_w=True,
+            after=(begun,),
+        )
         grads = end_input_grad(
             order, facts, w_near, base_far, across, corner, begun, [dk0, dv0], grads
         )

time: 50.3 us -> 50.8 us (level)
  Pallas kernels: 27.8 us -> 28.5 us
    ppermute x1, waiting for transfers between devices: 0.94 us -> 0.01 us  [over_chips(): lax.ppermute(values, ('tensor', 'sub'), [(i, 3 - i) for i in range(4)])]
    ppermute x12, waiting for transfers between devices: 5.75 us -> 6.48 us  [flipped(): lax.ppermute(block, axis, [(i, i ^ bit) for i in range(count) if i ^ bit...]
    pallas_call x1, Pallas kernels: 2.64 us -> 3.19 us  [input_grad(): pl.pallas_call(body, out_shape=(jax.ShapeDtypeStruct((ROWS, out_cols), BF...]
  transfers between devices with their start and end apart: 13 -> 13, of which waited for: 6 -> 5; matrix products, arithmetic and copies ran while one was open for 0% -> 0% of each run, Pallas kernels for 50% -> 51%
where the time goes in v21:
time: 50.8 us; the launch traced here: 50.6 us
  Pallas kernels  28.5 us (56%)
  starting transfers between devices  14.7 us (29%)
  waiting for transfers between devices  6.48 us (13%)
  between operations  0.97 us (2%)
    pallas_call x14, Pallas kernels, kernel_call(): pl.pallas_call(kernel, out_shape=tuple((pltpu.VMEM(s, d) if inside else j...  23.5 us
    ppermute x12, starting transfers between devices, flipped(): lax.ppermute(block, axis, [(i, i ^ bit) for i in range(count) if i ^ bit...  13.1 us
    ppermute x12, waiting for transfers between devices, flipped(): lax.ppermute(block, axis, [(i, i ^ bit) for i in range(count) if i ^ bit...  6.48 us
    pallas_call x1, Pallas kernels, input_grad(): pl.pallas_call(body, out_shape=(jax.ShapeDtypeStruct((ROWS, out_cols), BF...  3.19 us
    ppermute x1, starting transfers between devices, over_chips(): lax.ppermute(values, ('tensor', 'sub'), [(i, 3 - i) for i in range(4)])  1.62 us
  transfers between devices with their start and end apart: 13, of which 5 were waited for; matrix products, arithmetic and copies ran while one was open for 0% of the time, Pallas kernels for 51%

profile of v21, /device:TPU:0, one launch (start us, length us, event | category | flops | bytes accessed | tf_op | source)
XLA Modules:
  0.0 50.6 jit_solution(265152362169917790)
XLA Ops:
  0.6 1.0 %shard_map.120 = (s32[16]{0:T(128)S(4)}, bf16[2,128,512]{2,1,0:T(8,128)(2,1)S(1)}) custom-call(s32[1]{0:T(128)} %bitcast.side_ref, s32[1,5]{1,0:T(1,128)} %ids_ref.1, s32[1,3]{1,0:T(1,128)} %counts_ref.1, bf16[384,512]{1,0:T(8,128)(2,1)} %refs_5_.1, bf16[384,512]{1,0:T(8,128)(2,1)} %refs_6_.1), custom_call_target="tpu_custom_call" | custom-call | tf_op jit(solution)/shard_map/pallas_call | solution.py:141
  1.7 0.5 %collective-permute-start = (bf16[2,128,512]{2,1,0:T(8,128)(2,1)S(1)}, bf16[2,128,512]{2,1,0:T(8,128)(2,1)S(1)}, u32[]{:S(2)}, u32[]{:S(2)}) collective-permute-start(bf16[2,128,512]{2,1,0:T(8,128)(2,1)S(1)} %get-tuple-element.73.refs_1_.refs_11_), channel_id=1, source_target_pairs={{0,1},{1,0},{2,3},{3,2},{4,5},{5,4},{6,7},{7,6},{8,9},{9,8},{10,11... | collective-permute-start | bytes 786440 | tf_op jit(solution)/shard_map/ppermute | solution.py:729
  2.2 1.2 %collective-permute-done.refs_2_.refs_12_ = bf16[2,128,512]{2,1,0:T(8,128)(2,1)S(1)} collective-permute-done((bf16[2,128,512]{2,1,0:T(8,128)(2,1)S(1)}, bf16[2,128,512]{2,1,0:T(8,128)(2,1)S(1)}, u32[]{:S(2)}, u32[]{:S(2)}) %collective-permute-start) | collective-permute-done | bytes 262176 | tf_op jit(solution)/shard_map/ppermute | solution.py:729
  3.4 3.0 %collective-permute-start.1 = (bf16[2,128,256]{2,1,0:T(8,128)(2,1)S(1)}, bf16[2,128,256]{2,1,0:T(8,128)(2,1)S(1)}, u32[]{:S(2)}, u32[]{:S(2)}) collective-permute-start(bf16[2,128,256]{2,1,0:T(8,128)(2,1)S(1)} %shard_map.121.refs_9_.refs_1_), channel_id=1, source_target_pairs={{0,4},{4,0},{8,12},{12,8},{1,5},{5,1},{9,13},{13,9},{2,6},{6,2},{1... | collective-permute-start | bytes 393224 | tf_op jit(solution)/shard_map/ppermute | solution.py:729
  6.4 4.1 %shard_map.122 = (bf16[2048,256]{1,0:T(8,128)(2,1)S(1)}, bf16[2048,128]{1,0:T(8,128)(2,1)S(1)}, bf16[512,128]{1,0:T(8,128)(2,1)S(1)}, bf16[128,3072]{1,0:T(8,128...) custom-call(s32[16]{0:T(128)S(4)} %get-tuple-element.72.refs_0_.fact, ...), custom_call_target="tpu_custom_call" | custom-call | flops 4026531840 | bytes 1000 | tf_op jit(solution)/shard_map/pallas_call | solution.py:100
  10.5 0.0 collective-permute-done.1.refs_2_
  10.5 2.7 %collective-permute-start.2 = (bf16[2,128,256]{2,1,0:T(8,128)(2,1)S(1)}, bf16[2,128,256]{2,1,0:T(8,128)(2,1)S(1)}, u32[]{:S(2)}, u32[]{:S(2)}) collective-permute-start(bf16[2,128,256]{2,1,0:T(8,128)(2,1)S(1)} %shard_map.123.refs_17_.refs_3_), channel_id=1, source_target_pairs={{0,8},{4,12},{8,0},{12,4},{1,9},{5,13},{9,1},{13,5},{2,10},{6,14},... | collective-permute-start | bytes 393224 | tf_op jit(solution)/shard_map/ppermute | solution.py:729
  13.2 6.2 %shard_map.124 = (bf16[2048,256]{1,0:T(8,128)(2,1)S(1)}, bf16[2048,128]{1,0:T(8,128)(2,1)S(1)}, bf16[512,128]{1,0:T(8,128)(2,1)S(1)}, bf16[128,3072]{1,0:T(8,128...) custom-call(s32[16]{0:T(128)S(4)} %get-tuple-element.72.refs_0_.fact, ...), custom_call_target="tpu_custom_call" | custom-call | flops 12079595520 | bytes 1000 | tf_op jit(solution)/shard_map/pallas_call | solution.py:100
  19.4 0.2 collective-permute-done.2.refs_4_
  19.6 0.1 collective-permute-start.3
  19.7 3.2 %shard_map.126 = (bf16[3072,256]{1,0:T(8,128)(2,1)S(1)}, bf16[3072,256]{1,0:T(8,128)(2,1)S(1)}, bf16[8,128,256]{2,1,0:T(8,128)(2,1)S(1)}) custom-call(s32[16]{0:T(128)S(4)} %get-tuple-element.72.refs_0_.facts, bf16[128,3072]{1,0:T(8,128)(2,1)S(1)} %get-tuple-element.89.refs_1_, bf16[128,3072]{1,0:T(8,128)(2,1)S(1)} %get-tuple-element.90.refs_2_, ...), custom_call_target="tpu_custom_call" | custom-call | flops 8053063680 | bytes 1000 | tf_op jit(solution)/shard_map/pallas_call | solution.py:100
  22.9 0.6 %collective-permute-start.4 = (bf16[8,128,256]{2,1,0:T(8,128)(2,1)S(1)}, bf16[8,128,256]{2,1,0:T(8,128)(2,1)S(1)}, u32[]{:S(2)}, u32[]{:S(2)}) collective-permute-start(bf16[8,128,256]{2,1,0:T(8,128)(2,1)S(1)} %get-tuple-element.116), channel_id=1, source_target_pairs={{0,1},{1,0},{2,3},{3,2},{4,5},{5,4},{6,7},{7,6},{8,9},{9,8},{10,11... | collective-permute-start | bytes 1572872 | tf_op jit(solution)/shard_map/ppermute | solution.py:729
  23.5 0.0 collective-permute-done.3.refs_13_.refs_2_
  23.5 3.4 %shard_map.127 = (bf16[3072,256]{1,0:T(8,128)(2,1)S(1)}, bf16[3072,256]{1,0:T(8,128)(2,1)S(1)}, f32[4,128,256]{2,1,0:T(8,128)S(1)}) custom-call(s32[16]{0:T(128)S(4)} %get-tuple-element.72.refs_0_.facts, bf16[128,3072]{1,0:T(8,128)(2,1)S(1)} %get-tuple-element.103.refs_1_, bf16[128,3072]{1,0:T(8,128)(2,1)S(1)} %get-tuple-element.104.refs_2_, ...), custom_call_target="tpu_custom_call" | custom-call | flops 8053063680 | bytes 1000 | tf_op jit(solution)/shard_map/pallas_call | solution.py:100
  26.9 0.0 collective-permute-done.4.refs_2_.refs_4_
  26.9 0.1 shard_map.128
  26.9 1.3 %collective-permute-start.6 = (bf16[2,128,256]{2,1,0:T(8,128)(2,1)S(1)}, bf16[2,128,256]{2,1,0:T(8,128)(2,1)S(1)}, u32[]{:S(2)}, u32[]{:S(2)}) collective-permute-start(bf16[2,128,256]{2,1,0:T(8,128)(2,1)S(1)} %get-tuple-element.124), channel_id=1, source_target_pairs={{0,4},{4,0},{8,12},{12,8},{1,5},{5,1},{9,13},{13,9},{2,6},{6,2},{1... | collective-permute-start | bytes 393224 | tf_op jit(solution)/shard_map/ppermute | solution.py:729
  28.3 2.2 %collective-permute-start.5 = (bf16[2,128,256]{2,1,0:T(8,128)(2,1)S(1)}, bf16[2,128,256]{2,1,0:T(8,128)(2,1)S(1)}, u32[]{:S(2)}, u32[]{:S(2)}) collective-permute-start(bf16[2,128,256]{2,1,0:T(8,128)(2,1)S(1)} %get-tuple-element.117.refs_20_), channel_id=1, source_target_pairs={{0,8},{4,12},{8,0},{12,4},{1,9},{5,13},{9,1},{13,5},{2,10},{6,14},... | collective-permute-start | bytes 393224 | tf_op jit(solution)/shard_map/ppermute | solution.py:729
  30.4 0.1 shard_map.129
  30.5 1.6 %collective-permute-start.9 = (bf16[256,512]{1,0:T(8,128)(2,1)S(1)}, bf16[256,512]{1,0:T(8,128)(2,1)S(1)}, u32[]{:S(2)}, u32[]{:S(2)}) collective-permute-start(bf16[256,512]{1,0:T(8,128)(2,1)S(1)} %get-tuple-element.128.refs_0_.refs_3_), channel_id=1, source_target_pairs={{0,2},{2,0},{1,3},{3,1},{4,6},{6,4},{5,7},{7,5},{8,10},{10,8},{9,1... | collective-permute-start | bytes 786440 | tf_op jit(solution)/shard_map/ppermute | solution.py:729
  32.1 0.5 %collective-permute-start.8 = (bf16[128,512]{1,0:T(8,128)(2,1)S(1)}, bf16[128,512]{1,0:T(8,128)(2,1)S(1)}, u32[]{:S(2)}, u32[]{:S(2)}) collective-permute-start(bf16[128,512]{1,0:T(8,128)(2,1)S(1)} %get-tuple-element.120.refs_21_), channel_id=1, source_target_pairs={{0,2},{2,0},{1,3},{3,1},{4,6},{6,4},{5,7},{7,5},{8,10},{10,8},{9,1... | collective-permute-start | bytes 393224 | tf_op jit(solution)/shard_map/ppermute | solution.py:729
  32.6 4.4 %shard_map.130 = (bf16[384,4096]{1,0:T(8,128)(2,1)}, f32[8,128]{1,0:T(8,128)S(1)}, bf16[2560,1024]{1,0:T(8,128)(2,1)S(1)}) custom-call(s32[16]{0:T(128)S(4)} %get-tuple-element.72.refs_0_.facts, bf16[2,2,128,256]{3,2,1,0:T(8,128)(2,1)S(1)} %shard_map.125.refs_13_.refs_1_, bf16[2,2,128,256]{3,2,1,0:T(8,128)(2,1)S(1)} %collective-permute-done.3.refs_13_.refs_2_, ...), custom_call_target="tpu_custom_call" | custom-call | flops 1000 | bytes 1000 | tf_op jit(solution)/shard_map/pallas_call | solution.py:100
  37.0 0.0 collective-permute-done.6.refs_3_
  37.0 0.2 collective-permute-done.5.refs_2_
  37.2 0.1 shard_map.131
  37.2 0.1 collective-permute-start.7
  37.3 3.8 %collective-permute-done.8.refs_4_.refs_3_ = bf16[128,512]{1,0:T(8,128)(2,1)S(1)} collective-permute-done((bf16[128,512]{1,0:T(8,128)(2,1)S(1)}, bf16[128,512]{1,0:T(8,128)(2,1)S(1)}, u32[]{:S(2)}, u32[]{:S(2)}) %collective-permute-start.8) | collective-permute-done | bytes 131104 | tf_op jit(solution)/shard_map/ppermute | solution.py:729
  41.1 1.2 %collective-permute-done.7.refs_2_ = bf16[2,128,256]{2,1,0:T(8,128)(2,1)S(1)} collective-permute-done((bf16[2,128,256]{2,1,0:T(8,128)(2,1)S(1)}, bf16[2,128,256]{2,1,0:T(8,128)(2,1)S(1)}, u32[]{:S(2)}, u32[]{:S(2)}) %collective-permute-start.7) | collective-permute-done | bytes 131104 | tf_op jit(solution)/shard_map/ppermute | solution.py:729
  42.3 0.0 collective-permute-done.9.refs_5_.refs_1_
  42.3 0.1 collective-permute-start.10
  42.4 1.6 %collective-permute-start.12 = (bf16[128,256]{1,0:T(8,128)(2,1)S(1)}, bf16[128,256]{1,0:T(8,128)(2,1)S(1)}, u32[]{:S(2)}, u32[]{:S(2)}) collective-permute-start(bf16[128,256]{1,0:T(8,128)(2,1)S(1)} %get-tuple-element.131), channel_id=1, source_target_pairs={{0,3},{1,2},{2,1},{3,0},{4,7},{5,6},{6,5},{7,4},{8,11},{9,10},{10,... | collective-permute-start | bytes 196616 | tf_op jit(solution)/shard_map/ppermute | solution.py:817
  44.0 0.5 %collective-permute-start.11 = (bf16[128,256]{1,0:T(8,128)(2,1)S(1)}, bf16[128,256]{1,0:T(8,128)(2,1)S(1)}, u32[]{:S(2)}, u32[]{:S(2)}) collective-permute-start(bf16[128,256]{1,0:T(8,128)(2,1)S(1)} %get-tuple-element.131), channel_id=1, source_target_pairs={{0,2},{2,0},{1,3},{3,1},{4,6},{6,4},{5,7},{7,5},{8,10},{10,8},{9,1... | collective-permute-start | bytes 196616 | tf_op jit(solution)/shard_map/ppermute | solution.py:729
  44.5 0.0 collective-permute-done.10.refs_3_
  44.5 0.1 shard_map.133
  44.7 0.8 %shard_map.134.refs_5_.refs_2_ = f32[2560,128]{1,0:T(8,128)S(1)} custom-call(s32[16]{0:T(128)S(4)} %get-tuple-element.72.refs_0_.facts, bf16[2560,1024]{1,0:T(8,128)(2,1)S(1)} %get-tuple-element.122.refs_1_.refs_4_, bf16[128,512]{1,0:T(8,128)(2,1)S(1)} %get-tuple-element.130.refs_2_.refs_7_), custom_call_target="tpu_custom_call" | custom-call | flops 1000 | bytes 1000 | tf_op jit(solution)/shard_map/pallas_call | solution.py:684
  45.5 3.2 %shard_map.135 = (bf16[384,2560]{1,0:T(8,128)(2,1)}, bf16[384,512]{1,0:T(8,128)(2,1)}, bf16[384,512]{1,0:T(8,128)(2,1)}, f32[8,128]{1,0:T(8,128)}) custom-call(s32[16]{0:T(128)S(4)} %get-tuple-element.72.refs_0_.facts, bf16[256,512]{1,0:T(8,128)(2,1)S(1)} %get-tuple-element.128.refs_0_.refs_3_, bf16[256,512]{1,0:T(8,128)(2,1)S(1)} %collective-permute-done.9.refs_5_.refs_1_, ...), custom_call_target="tpu_custom_call" | custom-call | flops 1000 | bytes 1000 | tf_op jit(solution)/shard_map/pallas_call | solution.py:623
  48.7 0.0 collective-permute-done.12.refs_5_
  48.7 0.0 collective-permute-done.11.refs_4_
  48.7 1.7 %shard_map.136 = (bf16[384,2560]{1,0:T(8,128)(2,1)}, bf16[384,512]{1,0:T(8,128)(2,1)}, bf16[384,512]{1,0:T(8,128)(2,1)}) custom-call(s32[16]{0:T(128)S(4)} %get-tuple-element.72.refs_0_.facts, bf16[2560,1024]{1,0:T(8,128)(2,1)S(1)} %get-tuple-element.122.refs_1_.refs_4_, ...), custom_call_target="tpu_custom_call", output_to_operand_aliasing={{0}: (8, {}), {1}: (9, {}), {2}: (10, {})} | custom-call | flops 1000 | bytes 1000 | tf_op jit(solution)/shard_map/pallas_call | solution.py:100
  (4 shorter events, 0.1 us)
Async XLA Ops:
  1.7 1.7 %collective-permute-start = (bf16[2,128,512]{2,1,0:T(8,128)(2,1)S(1)}, bf16[2,128,512]{2,1,0:T(8,128)(2,1)S(1)}, u32[]{:S(2)}, u32[]{:S(2)}) collective-permute-start(bf16[2,128,512]{2,1,0:T(8,128)(2,1)S(1)} %get-tuple-element.73.refs_1_.refs_11_), channel_id=1, source_target_pairs={{0,1},{1,0},{2,3},{3,2},{4,5},{5,4},{6,7},{7,6},{8,9},{9,8},{10,11... | collective-permute-start | bytes 786440 | tf_op jit(solution)/shard_map/ppermute | solution.py:729
  3.4 7.1 %collective-permute-start.1 = (bf16[2,128,256]{2,1,0:T(8,128)(2,1)S(1)}, bf16[2,128,256]{2,1,0:T(8,128)(2,1)S(1)}, u32[]{:S(2)}, u32[]{:S(2)}) collective-permute-start(bf16[2,128,256]{2,1,0:T(8,128)(2,1)S(1)} %shard_map.121.refs_9_.refs_1_), channel_id=1, source_target_pairs={{0,4},{4,0},{8,12},{12,8},{1,5},{5,1},{9,13},{13,9},{2,6},{6,2},{1... | collective-permute-start | bytes 393224 | tf_op jit(solution)/shard_map/ppermute | solution.py:729
  10.5 9.0 %collective-permute-start.2 = (bf16[2,128,256]{2,1,0:T(8,128)(2,1)S(1)}, bf16[2,128,256]{2,1,0:T(8,128)(2,1)S(1)}, u32[]{:S(2)}, u32[]{:S(2)}) collective-permute-start(bf16[2,128,256]{2,1,0:T(8,128)(2,1)S(1)} %shard_map.123.refs_17_.refs_3_), channel_id=1, source_target_pairs={{0,8},{4,12},{8,0},{12,4},{1,9},{5,13},{9,1},{13,5},{2,10},{6,14},... | collective-permute-start | bytes 393224 | tf_op jit(solution)/shard_map/ppermute | solution.py:729
  19.6 3.9 %collective-permute-start.3 = (bf16[2,2,128,256]{3,2,1,0:T(8,128)(2,1)S(1)}, bf16[2,2,128,256]{3,2,1,0:T(8,128)(2,1)S(1)}, u32[]{:S(2)}, u32[]{:S(2)}) collective-permute-start(bf16[2,2,128,256]{3,2,1,0:T(8,128)(2,1)S(1)} %shard_map.125.refs_13_.refs_1_), channel_id=1, source_target_pairs={{0,1},{1,0},{2,3},{3,2},{4,5},{5,4},{6,7},{7,6},{8,9},{9,8},{10,11... | collective-permute-start | bytes 786440 | tf_op jit(solution)/shard_map/ppermute | solution.py:729
  22.9 3.9 %collective-permute-start.4 = (bf16[8,128,256]{2,1,0:T(8,128)(2,1)S(1)}, bf16[8,128,256]{2,1,0:T(8,128)(2,1)S(1)}, u32[]{:S(2)}, u32[]{:S(2)}) collective-permute-start(bf16[8,128,256]{2,1,0:T(8,128)(2,1)S(1)} %get-tuple-element.116), channel_id=1, source_target_pairs={{0,1},{1,0},{2,3},{3,2},{4,5},{5,4},{6,7},{7,6},{8,9},{9,8},{10,11... | collective-permute-start | bytes 1572872 | tf_op jit(solution)/shard_map/ppermute | solution.py:729
  26.9 10.0 %collective-permute-start.6 = (bf16[2,128,256]{2,1,0:T(8,128)(2,1)S(1)}, bf16[2,128,256]{2,1,0:T(8,128)(2,1)S(1)}, u32[]{:S(2)}, u32[]{:S(2)}) collective-permute-start(bf16[2,128,256]{2,1,0:T(8,128)(2,1)S(1)} %get-tuple-element.124), channel_id=1, source_target_pairs={{0,4},{4,0},{8,12},{12,8},{1,5},{5,1},{9,13},{13,9},{2,6},{6,2},{1... | collective-permute-start | bytes 393224 | tf_op jit(solution)/shard_map/ppermute | solution.py:729
  28.3 8.9 %collective-permute-start.5 = (bf16[2,128,256]{2,1,0:T(8,128)(2,1)S(1)}, bf16[2,128,256]{2,1,0:T(8,128)(2,1)S(1)}, u32[]{:S(2)}, u32[]{:S(2)}) collective-permute-start(bf16[2,128,256]{2,1,0:T(8,128)(2,1)S(1)} %get-tuple-element.117.refs_20_), channel_id=1, source_target_pairs={{0,8},{4,12},{8,0},{12,4},{1,9},{5,13},{9,1},{13,5},{2,10},{6,14},... | collective-permute-start | bytes 393224 | tf_op jit(solution)/shard_map/ppermute | solution.py:729
  30.5 11.7 %collective-permute-start.9 = (bf16[256,512]{1,0:T(8,128)(2,1)S(1)}, bf16[256,512]{1,0:T(8,128)(2,1)S(1)}, u32[]{:S(2)}, u32[]{:S(2)}) collective-permute-start(bf16[256,512]{1,0:T(8,128)(2,1)S(1)} %get-tuple-element.128.refs_0_.refs_3_), channel_id=1, source_target_pairs={{0,2},{2,0},{1,3},{3,1},{4,6},{6,4},{5,7},{7,5},{8,10},{10,8},{9,1... | collective-permute-start | bytes 786440 | tf_op jit(solution)/shard_map/ppermute | solution.py:729
  32.1 9.0 %collective-permute-start.8 = (bf16[128,512]{1,0:T(8,128)(2,1)S(1)}, bf16[128,512]{1,0:T(8,128)(2,1)S(1)}, u32[]{:S(2)}, u32[]{:S(2)}) collective-permute-start(bf16[128,512]{1,0:T(8,128)(2,1)S(1)} %get-tuple-element.120.refs_21_), channel_id=1, source_target_pairs={{0,2},{2,0},{1,3},{3,1},{4,6},{6,4},{5,7},{7,5},{8,10},{10,8},{9,1... | collective-permute-start | bytes 393224 | tf_op jit(solution)/shard_map/ppermute | solution.py:729
  37.2 5.0 %collective-permute-start.7 = (bf16[2,128,256]{2,1,0:T(8,128)(2,1)S(1)}, bf16[2,128,256]{2,1,0:T(8,128)(2,1)S(1)}, u32[]{:S(2)}, u32[]{:S(2)}) collective-permute-start(bf16[2,128,256]{2,1,0:T(8,128)(2,1)S(1)} %get-tuple-element.127.refs_3_), channel_id=1, source_target_pairs={{0,4},{4,0},{8,12},{12,8},{1,5},{5,1},{9,13},{13,9},{2,6},{6,2},{1... | collective-permute-start | bytes 393224 | tf_op jit(solution)/shard_map/ppermute | solution.py:729
  42.3 2.2 %collective-permute-start.10 = (bf16[2,128,256]{2,1,0:T(8,128)(2,1)S(1)}, bf16[2,128,256]{2,1,0:T(8,128)(2,1)S(1)}, u32[]{:S(2)}, u32[]{:S(2)}) collective-permute-start(bf16[2,128,256]{2,1,0:T(8,128)(2,1)S(1)} %get-tuple-element.129.refs_2_), channel_id=1, source_target_pairs={{0,1},{1,0},{2,3},{3,2},{4,5},{5,4},{6,7},{7,6},{8,9},{9,8},{10,11... | collective-permute-start | bytes 393224 | tf_op jit(solution)/shard_map/ppermute | solution.py:729
  42.4 6.3 %collective-permute-start.12 = (bf16[128,256]{1,0:T(8,128)(2,1)S(1)}, bf16[128,256]{1,0:T(8,128)(2,1)S(1)}, u32[]{:S(2)}, u32[]{:S(2)}) collective-permute-start(bf16[128,256]{1,0:T(8,128)(2,1)S(1)} %get-tuple-element.131), channel_id=1, source_target_pairs={{0,3},{1,2},{2,1},{3,0},{4,7},{5,6},{6,5},{7,4},{8,11},{9,10},{10,... | collective-permute-start | bytes 196616 | tf_op jit(solution)/shard_map/ppermute | solution.py:817
  44.0 4.7 %collective-permute-start.11 = (bf16[128,256]{1,0:T(8,128)(2,1)S(1)}, bf16[128,256]{1,0:T(8,128)(2,1)S(1)}, u32[]{:S(2)}, u32[]{:S(2)}) collective-permute-start(bf16[128,256]{1,0:T(8,128)(2,1)S(1)} %get-tuple-element.131), channel_id=1, source_target_pairs={{0,2},{2,0},{1,3},{3,1},{4,6},{6,4},{5,7},{7,5},{8,10},{10,8},{9,1... | collective-permute-start | bytes 196616 | tf_op jit(solution)/shard_map/ppermute | solution.py:729
